TPU v7x, 32 devices: a whole 2x2x4 slice. The times are simulated.
32 devices in a mesh: rep: 2 (over y), tp: 4 (over z), sec: 4 (over x, core).
Axes of the slice: x: 2, y: 2, z: 4, core: 2. Of those that a mesh axis runs over, the one named last changes fastest.
Arguments:
- prompt_key_values: bfloat16 [64, 2, 1024, 512], P(('rep', 'sec'), None, 'tp'), parts along dimension 0, may hold values from -16 to 16
- queries: bfloat16 [8, 8, 4, 4096], P(('rep', 'sec')), parts along dimension 0, may hold values from -8 to 8
- routing: int32 [64, 1], P('rep'), parts along dimension 0, may hold values from 0 to 3; in each aligned block of 8 rows (0 to 7, 8 to 15, ...) at most 2 rows name the same one
- lengths: int32 [64], P('rep'), parts along dimension 0, may hold values from 128 to 1024, as said below
- out_weight: bfloat16 [4096, 8192], P(None, 'tp'), may hold values from -0.375 to 0.375
Outputs:
- layer_out: bfloat16 [64, 4, 8192], P(('rep', 'sec'), None, 'tp'), parts along dimension 0
- decode_group_cache: bfloat16 [8, 8, 2, 1024, 512], P(('rep', 'sec'), None, None, 'tp'), parts along dimension 0
There are 2 independent parts, one for each index of `rep`. A program takes and returns all parts, laid end to end along the dimension named above; an argument that names none is the same for every part. Nothing has to cross between parts.
Inputs may be any that keep to these rules, and one draw needn't show every extreme that they name: `routing`: among the 8 prompts of one prefill group, no decode group is named more than 2 times, and in some groups one is named exactly 2 times. `lengths`: some prompt has exactly 1024 positions.
All inputs are finite; a program needn't handle non-finite values.
Results may differ from a plain program's by a relative error of at most 0.008.
Values may be sent and summed in bfloat16 or wider, within the bound.
No kernel may reach another device: no remote copies, remote signals or barrier semaphores. Data moves between devices by JAX's collectives and lax.ppermute only.
A program may use at most 128 MiB of HBM per device.

v0:
```python
import jax
import jax.numpy as jnp
from jax import lax
from jax.sharding import PartitionSpec as P

HEAD_SIZE = 128
KEY_VALUE_HEADS = 4
REQ_GRP = 8
CAP = 2


def combined_all(value, axis, combine):
    everything = jax.tree.map(lambda part: lax.all_gather(part, axis), value)
    first = jax.tree.map(lambda part: part[0], everything)

    def lap(k, so_far):
        return combine(so_far, jax.tree.map(lambda part: part[k], everything))

    return lax.fori_loop(1, lax.axis_size(axis), lap, first)


def slot_numbers(target_output, group_size, capacity):
    request_count = target_output.shape[0]
    ordinal = jnp.arange(request_count, dtype=jnp.int32)
    source = ordinal // group_size
    earlier = (
        (source[:, None] == source[None, :])
        & (target_output[:, None] == target_output[None, :])
        & (ordinal[None, :] < ordinal[:, None])
    )
    position = jnp.sum(earlier.astype(jnp.int32), axis=1)
    return (source * capacity + position, target_output * capacity + position)


def join_parts(left_part, right_part):
    summit = jnp.maximum(left_part[1], right_part[1])
    left_scale = jnp.exp(left_part[1] - summit)
    right_scale = jnp.exp(right_part[1] - summit)
    numerator = left_part[0] * left_scale[..., None] + right_part[0] * right_scale[..., None]
    return (numerator, summit, left_part[2] * left_scale + right_part[2] * right_scale)


def body(prompt_key_values, queries, routing, lengths, out_weight):
    section = lax.axis_index("sec")
    tp_index = lax.axis_index("tp")
    group_slot_total = queries.shape[1]
    sample_rows = queries.shape[2]
    local_length = prompt_key_values.shape[2]
    head_total = queries.shape[3] // HEAD_SIZE
    decode_groups = head_total // KEY_VALUE_HEADS
    target_output = routing[:, 0]
    arrival_order, depart = slot_numbers(target_output, REQ_GRP, CAP)
    own_depart = lax.dynamic_slice_in_dim(depart, section * REQ_GRP, REQ_GRP)
    slot_ids = jnp.arange(group_slot_total, dtype=jnp.int32)
    chosen = own_depart[None, :] == slot_ids[:, None]
    filled = jnp.any(chosen, axis=1)
    source_row = jnp.sum(
        jnp.where(chosen, jnp.arange(REQ_GRP, dtype=jnp.int32)[None, :], 0), axis=1
    )
    outgoing = jnp.where(
        filled[:, None, None, None],
        jnp.take(prompt_key_values, source_row, axis=0),
        jnp.zeros((), jnp.bfloat16),
    )
    arrived_cache = lax.all_to_all(outgoing, "sec", split_axis=0, concat_axis=0, tiled=True)
    landed = (target_output == section)[None, :] & (arrival_order[None, :] == slot_ids[:, None])
    slot_length = jnp.maximum(jnp.sum(jnp.where(landed, lengths[None, :], 0), axis=1), 1)
    positions = tp_index * local_length + jnp.arange(local_length, dtype=jnp.int32)
    visible = positions[None, :] < slot_length[:, None]
    query_matrix = queries[0].reshape(
        group_slot_total, sample_rows, KEY_VALUE_HEADS, decode_groups, HEAD_SIZE
    )
    key_matrix = arrived_cache[:, 0].reshape(
        group_slot_total, local_length, KEY_VALUE_HEADS, HEAD_SIZE
    )
    value_matrix = arrived_cache[:, 1].reshape(
        group_slot_total, local_length, KEY_VALUE_HEADS, HEAD_SIZE
    )
    scores = jnp.einsum(
        "asknd,alkd->asknl", query_matrix, key_matrix, preferred_element_type=jnp.float32
    ) * HEAD_SIZE ** (-0.5)
    cover_mask = visible[:, None, None, None, :]
    scores = jnp.where(cover_mask, scores, -1e30)
    peak_score = jnp.max(scores, axis=-1)
    weights = jnp.where(cover_mask, jnp.exp(scores - peak_score[..., None]), 0.0)
    weight_sum = jnp.sum(weights, axis=-1)
    numerator = jnp.einsum("asknl,alkd->asknd", weights, value_matrix.astype(jnp.float32))
    row_count = group_slot_total * sample_rows
    numerator = numerator.reshape(row_count, head_total, HEAD_SIZE)
    peak_score = peak_score.reshape(row_count, head_total)
    weight_sum = weight_sum.reshape(row_count, head_total)
    numerator, peak_score, weight_sum = combined_all(
        (numerator, peak_score, weight_sum), "tp", join_parts
    )
    attended = (
        (numerator / weight_sum[..., None])
        .reshape(row_count, head_total * HEAD_SIZE)
        .astype(jnp.bfloat16)
    )
    projected = jnp.dot(attended, out_weight, preferred_element_type=jnp.float32)
    outgoing_rows = projected.astype(jnp.bfloat16).reshape(
        group_slot_total, sample_rows, out_weight.shape[1]
    )
    returned = lax.all_to_all(outgoing_rows, "sec", split_axis=0, concat_axis=0, tiled=True)
    layer_out = jnp.take(returned, own_depart, axis=0)
    return (layer_out, arrived_cache[None])


def solution(mesh):
    placed = (
        P(("rep", "sec"), None, "tp", None),
        P(("rep", "sec"), None, None, None),
        P("rep", None),
        P("rep"),
        P(None, "tp"),
    )
    return jax.shard_map(
        body,
        mesh=mesh,
        in_specs=placed,
        out_specs=(P(("rep", "sec"), None, "tp"), P(("rep", "sec"), None, None, "tp", None)),
        check_vma=False,
    )
```

profile of v0, /device:TPU:0, one launch (start us, length us, event | category | flops | bytes accessed | tf_op | source)
XLA Modules:
  0.0 170.5 jit_solution(10769992331043194088)
XLA Ops:
  7.2 0.9 convert_reduce_fusion
  8.1 0.7 multiply_add_fusion
  9.0 0.1 fusion.13
  9.1 5.0 %gather_fusion = bf16[8,2,256,512]{3,2,1,0:T(8,128)(2,1)} fusion(bf16[8,2,256,512]{3,2,1,0:T(8,128)(2,1)} %param.7, s32[1024]{0:T(1024)S(1)} %pad_clamp_fusion.1), kind=kCustom, calls=%fused_computation | custom fusion | bytes 8388640 | tf_op jit(solution)/shard_map/jit(_take)/gather | solution.py:62
  14.1 4.7 %select_select_fusion = bf16[8,2,256,512]{3,2,1,0:T(8,128)(2,1)} fusion(bf16[8,2,256,512]{3,2,1,0:T(8,128)(2,1)} %gather_fusion, pred[8]{0:T(512)(128)(4,1)S(1)} %compare_and_fusion, pred[8]{0:T(512)(128)(4,1)S(1)} %fusion.13), kind=kLoop, calls=%fused_computation.10 | loop fusion | flops 4194304 | bytes 8388624 | tf_op jit(solution)/shard_map/jit(_where)/select_n | solution.py:60
  18.8 5.0 %all-to-all-start = ((bf16[8,2,256,512]{3,2,1,0:T(8,128)(2,1)}), bf16[8,2,256,512]{3,2,1,0:T(8,128)(2,1)}, u32[]{:S(2)}, u32[]{:S(2)}) async-start(bf16[8,2,256,512]{3,2,1,0:T(8,128)(2,1)} %select_select_fusion), calls=%async_computation | async-start | bytes 8388608 | tf_op jit(solution)/shard_map/all_to_all | solution.py:65
  23.9 0.3 reshape_squeeze.11
  24.3 0.1 select_reduce_fusion
  24.5 48.2 %all-to-all-done = bf16[8,2,256,512]{3,2,1,0:T(8,128)(2,1)} async-done(((bf16[8,2,256,512]{3,2,1,0:T(8,128)(2,1)}), bf16[8,2,256,512]{3,2,1,0:T(8,128)(2,1)}, u32[]{:S(2)}, u32[]{:S(2)}) %all-to-all-start) | async-done | bytes 4194336 | tf_op jit(solution)/shard_map/all_to_all | solution.py:65
  72.7 3.9 %fusion.18 = (bf16[8,1,256,512]{3,2,1,0:T(8,128)(2,1)S(1)}, bf16[8,1,256,512]{3,2,1,0:T(8,128)(2,1)}) fusion(bf16[8,2,256,512]{3,2,1,0:T(8,128)(2,1)} %all-to-all-done), kind=kLoop, calls=%fused_computation.57 | loop fusion | bytes 8388608 | tf_op jit(solution)/shard_map/slice | solution.py:73
  76.6 2.4 %copy.38 = bf16[8,1,256,512]{2,3,0,1:T(8,128)(2,1)} copy(bf16[8,1,256,512]{3,2,1,0:T(8,128)(2,1)S(1)} %get-tuple-element.203) | data formatting | bytes 4194304 | tf_op jit(solution)/shard_map/slice | solution.py:73
  79.0 2.8 %copy.37 = bf16[8,1,256,512]{2,3,0,1:T(8,128)(2,1)S(1)} copy(bf16[8,1,256,512]{3,2,1,0:T(8,128)(2,1)} %get-tuple-element.204) | data formatting | bytes 4194304 | tf_op jit(solution)/shard_map/slice | solution.py:76
  81.8 2.1 %fusion.19 = (f32[8,4,4,8]{3,1,2,0:T(4,128)S(1)}, f32[8,4,4,8,256]{4,3,1,2,0:T(8,128)S(1)}) fusion(bf16[8,256,4,128,1]{1,3,4,2,0:T(8,128)(2,1)} %bitcast.56, bf16[8,4,4,8,128]{4,3,2,1,0:T(8,128)(2,1)S(1)} %reshape_squeeze.11, pred[8,256]{1,0:T(8,128)(4,1)S(1)} %broadcast_compare_fusion), kind=kOutput, calls=%fused_computation.58 | convolution fusion | flops 67894272 | bytes 3414016 | tf_op jit(solution)/shard_map/asknd,alkd->asknl/dot_general | solution.py:79
  84.0 0.8 convolution_bitcast_fusion
  84.8 0.9 copy.42
  85.7 0.5 fusion.5
  86.4 14.3 %all_gather.11 = f32[4,32,32]{2,1,0:T(8,128)S(1)} all-gather(f32[1,32,32]{2,1,0:T(8,128)S(1)} %all_gather_reshape.11), channel_id=1, replica_groups=mesh['rep'=2,'tp'=4,'sec'=4] {'tp'}, dimensions={0}, use_global_device_ids=true | all-gather | bytes 20480 | tf_op jit(solution)/shard_map/all_gather | solution.py:13
  100.7 13.6 %all_gather.10 = f32[4,32,32]{2,1,0:T(8,128)S(1)} all-gather(f32[1,32,32]{2,1,0:T(8,128)S(1)} %all_gather_reshape.10), channel_id=1, replica_groups=mesh['rep'=2,'tp'=4,'sec'=4] {'tp'}, dimensions={0}, use_global_device_ids=true | all-gather | bytes 20480 | tf_op jit(solution)/shard_map/all_gather | solution.py:13
  114.3 19.7 %all-gather.2.cloned.1.call-done = f32[4,32,32,128]{3,2,1,0:T(8,128)} async-done(((f32[1,32,32,128]{3,2,1,0:T(8,128)}), f32[4,32,32,128]{3,2,1,0:T(8,128)}) %all-gather.2.cloned.1.call-update) | async-done | bytes 2097168 | tf_op jit(solution)/shard_map/all_gather | solution.py:13
  134.1 1.1 slice_bitcast_fusion
  135.2 4.8 %while.19 = (s32[]{:T(128)}, f32[32,32,128]{2,1,0:T(8,128)S(1)}, f32[32,32]{1,0:T(8,128)S(1)}, f32[32,32]{1,0:T(8,128)S(1)}, f32[4,32,32]{2,1,0:T(8,128)S(1)}, /...) while((s32[]{:T(128)}, f32[32,32,128]{2,1,0:T(8,128)S(1)}, ...), condition=%wide.region_7.8_spmd, body=%wide.region_6.7_spmd.sunk | while | flops 399365 | bytes 1613975 | solution.py:19
  135.2 1.5 fusion.26
  136.8 1.5 fusion.26
  138.4 1.5 fusion.26
  140.0 0.2 divide_convert_fusion
  140.2 8.8 %convolution_convert_fusion = bf16[32,2048]{1,0:T(8,128)(2,1)S(1)} fusion(bf16[4096,2048]{1,0:T(8,128)(2,1)} %param.11, bf16[4,8,32,128]{3,2,1,0:T(8,128)(2,1)S(1)} %bitcast.58), kind=kOutput, calls=%fused_computation.11 | convolution fusion | flops 536936448 | bytes 17170432 | tf_op jit(solution)/shard_map/dot_general | solution.py:100
  149.0 0.7 reshape.107
  149.7 3.3 %all-to-all-start.1 = ((bf16[8,4,2048]{2,1,0:T(4,128)(2,1)}), bf16[8,4,2048]{2,1,0:T(4,128)(2,1)S(1)}, u32[]{:S(2)}, u32[]{:S(2)}) async-start(bf16[8,4,2048]{2,1,0:T(4,128)(2,1)} %reshape.107), calls=%async_computation.1 | async-start | bytes 262144 | tf_op jit(solution)/shard_map/all_to_all | solution.py:104
  153.0 4.6 %all-to-all-done.1 = bf16[8,4,2048]{2,1,0:T(4,128)(2,1)S(1)} async-done(((bf16[8,4,2048]{2,1,0:T(4,128)(2,1)}), bf16[8,4,2048]{2,1,0:T(4,128)(2,1)S(1)}, u32[]{:S(2)}, u32[]{:S(2)}) %all-to-all-start.1) | async-done | bytes 131104 | tf_op jit(solution)/shard_map/all_to_all | solution.py:104
  157.6 0.7 gather_fusion.1
  158.3 0.8 broadcast_select_fusion
  159.1 4.6 %copy.73 = bf16[1,8,2,256,512]{4,3,2,1,0:T(8,128)(2,1)} copy(bf16[1,8,2,256,512]{4,3,2,1,0:T(8,128)(2,1)} %bitcast.16) | data formatting | bytes 8388608
  (29 shorter events, 0.7 us)
Async XLA Ops:
  18.8 5.1 %copy-start = (bf16[1,8,4,4096]{3,2,1,0:T(4,128)(2,1)S(1)}, bf16[1,8,4,4096]{3,2,1,0:T(4,128)(2,1)}, u32[]{:S(2)}) copy-start(bf16[1,8,4,4096]{3,2,1,0:T(4,128)(2,1)} %param.8) | copy-start | bytes 786436
  18.8 5.4 %copy-start.1 = (s32[32,1]{0,1:T(1,128)S(1)}, s32[32,1]{0,1:T(1,128)}, u32[]{:S(2)}) copy-start(s32[32,1]{0,1:T(1,128)} %param.9) | copy-start | bytes 388
  18.8 5.4 %copy-start.2 = (s32[32]{0:T(128)S(1)}, s32[32]{0:T(128)}, u32[]{:S(2)}) copy-start(s32[32]{0:T(128)} %param.10) | copy-start | bytes 388
  18.8 53.8 %all-to-all-start = ((bf16[8,2,256,512]{3,2,1,0:T(8,128)(2,1)}), bf16[8,2,256,512]{3,2,1,0:T(8,128)(2,1)}, u32[]{:S(2)}, u32[]{:S(2)}) async-start(bf16[8,2,256,512]{3,2,1,0:T(8,128)(2,1)} %select_select_fusion), calls=%async_computation | async-start | bytes 8388608 | tf_op jit(solution)/shard_map/all_to_all | solution.py:65
  23.8 110.2 %all-gather.2.cloned.1.call-start = ((), (), s32[]{:S(2)}) async-start(), calls=%async_computation.2 | async-start | bytes 2621440 | tf_op jit(solution)/shard_map/all_gather | solution.py:13
  149.7 7.9 %all-to-all-start.1 = ((bf16[8,4,2048]{2,1,0:T(4,128)(2,1)}), bf16[8,4,2048]{2,1,0:T(4,128)(2,1)S(1)}, u32[]{:S(2)}, u32[]{:S(2)}) async-start(bf16[8,4,2048]{2,1,0:T(4,128)(2,1)} %reshape.107), calls=%async_computation.1 | async-start | bytes 262144 | tf_op jit(solution)/shard_map/all_to_all | solution.py:104
Sparse Core Ops, SparseCore 0:
  85.8 48.2 all-gather.1
where the time goes:
time: 171 us; the launch traced here: 170 us
  waiting for transfers between devices  72.6 us (42%)
  blocking collectives  27.9 us (16%)
  local copies, waits for them, and re-layouts  22.6 us (13%)
  between operations  14.2 us (8%)
  other arithmetic  13 us (8%)
  matrix products  11.7 us (7%)
  starting transfers between devices  8.36 us (5%)
    all_to_all x1, waiting for transfers between devices, body(): lax.all_to_all(outgoing, 'sec', split_axis=0, concat_axis=0, tiled=True)  48.2 us
    all_gather x2, blocking collectives, combined_all(): everything = jax.tree.map(lambda part: lax.all_gather(part, axis), value)  27.9 us
    all_gather x1, waiting for transfers between devices, combined_all(): everything = jax.tree.map(lambda part: lax.all_gather(part, axis), value)  19.7 us
    dot_general x1, matrix products, body(): jnp.dot(attended, out_weight, preferred_element_type=jnp.float32)  8.78 us
    slice x2, local copies, waits for them, and re-layouts, body(): arrived_cache[:, 0]  6.3 us
    gather x1, local copies, waits for them, and re-layouts, body(): jnp.take(prompt_key_values, source_row, axis=0)  5.02 us
    all_to_all x1, starting transfers between devices, body(): lax.all_to_all(outgoing, 'sec', split_axis=0, concat_axis=0, tiled=True)  4.99 us
    select_n x1, other arithmetic, body(): jnp.where(filled[:, None, None, None], jnp.take(prompt_key_values, source...  4.72 us
  transfers between devices with their start and end apart: 3, of which 3 were waited for; matrix products, arithmetic and copies ran while one was open for 1% of the time, Pallas kernels for 0%

commit v1 on v0

v1 whole, which is shorter than its diff:
```python
import functools

import jax
import jax.numpy as jnp
from jax import lax
from jax.experimental import pallas as pl
from jax.experimental.pallas import tpu as pltpu
from jax.sharding import PartitionSpec as P

HEAD_SIZE = 128
KEY_VALUE_HEADS = 4
REQ_GRP = 8
CAP = 2
HIDDEN = -1e30

ANY = pl.BlockSpec(memory_space=pl.ANY)
VMEM = pl.BlockSpec(memory_space=pltpu.VMEM)
SMEM = pl.BlockSpec(memory_space=pltpu.SMEM)


def swap(value, axis, offset):
    count = lax.axis_size(axis)
    return lax.ppermute(value, axis, [(i, i ^ offset) for i in range(count)])


def own_slots(routing_ref, section, used, visit):
    for t in range(used.shape[0]):
        used[t] = 0
    for i in range(REQ_GRP):
        target = routing_ref[section * REQ_GRP + i]
        order = used[target]
        used[target] = order + 1
        visit(i, target, order)


def pack_kernel(offsets, section_count, routing_ref, cache_ref, *refs):
    out_refs, (source, used, zeros, sem) = refs[:-4], refs[-4:]
    section = lax.axis_index("sec")
    full = section_count * CAP == REQ_GRP

    def note(i, target, order):
        source[target * CAP + order] = i

    own_slots(routing_ref, section, used, note)
    if not full:
        zeros[...] = jnp.zeros_like(zeros)
    copies = []
    for n, offset in enumerate(offsets):
        target = section ^ offset
        for order in range(CAP):
            if offset == 0:
                place = out_refs[n * CAP].at[0, section * CAP + order]
            else:
                place = out_refs[n * CAP + order].at[0]
            row = source[target * CAP + order]
            slot_sem = sem.at[n * CAP + order]
            if full:
                copy = pltpu.make_async_copy(cache_ref.at[row], place, slot_sem)
                copy.start()
                copies.append(copy)
            else:
                filled = order < used[target]

                @pl.when(filled)
                def _():
                    pltpu.make_async_copy(cache_ref.at[row], place, slot_sem).start()

                @pl.when(jnp.logical_not(filled))
                def _():
                    pltpu.make_async_copy(zeros, place, slot_sem).start()

                copies.append(pltpu.make_async_copy(zeros, place, slot_sem))
    for copy in copies:
        copy.wait()


def pack(routing, cache, offsets, section_count):
    row_shape = cache.shape[1:]
    full = section_count * CAP == REQ_GRP
    shapes = []
    for offset in offsets:
        if offset == 0:
            shapes.append(jax.ShapeDtypeStruct((1, section_count * CAP) + row_shape, cache.dtype))
        else:
            shapes.extend([jax.ShapeDtypeStruct((1,) + row_shape, cache.dtype)] * CAP)
    return pl.pallas_call(
        functools.partial(pack_kernel, offsets, section_count),
        out_shape=shapes,
        in_specs=[SMEM, ANY],
        out_specs=[ANY] * len(shapes),
        scratch_shapes=[
            pltpu.SMEM((section_count * CAP,), jnp.int32),
            pltpu.SMEM((section_count,), jnp.int32),
            pltpu.VMEM((8, 128) if full else row_shape, cache.dtype),
            pltpu.SemaphoreType.DMA((len(offsets) * CAP,)),
        ],
        cost_estimate=pl.CostEstimate(
            flops=0, bytes_accessed=2 * len(offsets) * CAP * 2 * row_shape[1] * row_shape[2] * 2, transcendentals=0
        ),
        name="pack_cache",
    )(routing, cache)


def place_kernel(offsets, *refs):
    count = len(offsets)
    part_refs, out_ref, sem = refs[1 : 1 + count], refs[1 + count], refs[2 + count]
    section = lax.axis_index("sec")
    copies = []
    for n, (offset, first) in enumerate(offsets):
        length = part_refs[n].shape[0]
        slots = out_ref.at[0, pl.ds((section ^ offset) * CAP + first, length)]
        copy = pltpu.make_async_copy(part_refs[n], slots, sem.at[n])
        copy.start()
        copies.append(copy)
    for copy in copies:
        copy.wait()


def place(whole, parts, offsets):
    return pl.pallas_call(
        functools.partial(place_kernel, offsets),
        out_shape=jax.ShapeDtypeStruct(whole.shape, whole.dtype),
        in_specs=[ANY] * (1 + len(parts)),
        out_specs=ANY,
        scratch_shapes=[pltpu.SemaphoreType.DMA((len(parts),))],
        input_output_aliases={0: 0},
        cost_estimate=pl.CostEstimate(
            flops=0, bytes_accessed=sum(4 * part.size for part in parts), transcendentals=0
        ),
        name="place_cache",
    )(whole, *parts)


def attend_kernel(section_count, tp_count, routing_ref, lengths_ref, cache_ref, *refs):
    query_refs, message_refs = refs[:section_count], refs[section_count : section_count + tp_count]
    slot_of, used, held, queries, stats, messages, sem = refs[section_count + tp_count :]
    section = lax.axis_index("sec")
    tp_index = lax.axis_index("tp")
    samples, _, heads, _ = query_refs[0].shape[1:]
    rows = samples * heads
    local = cache_ref.shape[2]
    groups = REQ_GRP * KEY_VALUE_HEADS // tp_count

    def fetch(i):
        return pltpu.make_async_copy(cache_ref.at[i], held.at[i], sem.at[i])

    for i in range(REQ_GRP):
        fetch(i).start()

    def note(i, target, order):
        slot_of[i] = (target ^ section) * CAP + order

    own_slots(routing_ref, section, used, note)
    for offset in range(section_count):
        for order in range(CAP):
            for k in range(KEY_VALUE_HEADS):
                block = query_refs[offset][order, :, k].astype(jnp.float32)
                queries[offset * CAP + order, k] = block.reshape(rows, HEAD_SIZE).astype(jnp.bfloat16)
    stats[...] = jnp.zeros_like(stats)
    lane = lax.broadcasted_iota(jnp.int32, (rows, HEAD_SIZE), 1)
    position = lax.broadcasted_iota(jnp.int32, (rows, local), 1) + tp_index * local

    @pl.loop(0, REQ_GRP)
    def _(i):
        fetch(i).wait()
        visible = position < lengths_ref[section * REQ_GRP + i]
        for k in range(KEY_VALUE_HEADS):
            columns = pl.ds(k * HEAD_SIZE, HEAD_SIZE)
            score = lax.dot_general(
                queries[slot_of[i], k],
                held[i, 0, :, columns],
                (((1,), (1,)), ((), ())),
                preferred_element_type=jnp.float32,
            ) * HEAD_SIZE ** (-0.5)
            score = jnp.where(visible, score, HIDDEN)
            peak = jnp.max(score, axis=1, keepdims=True)
            weight = jnp.where(visible, jnp.exp(score - peak), 0.0)
            total = jnp.sum(weight, axis=1, keepdims=True)
            mixed = jnp.dot(
                weight.astype(jnp.bfloat16), held[i, 1, :, columns], preferred_element_type=jnp.float32
            )
            some = total > 0.0
            safe = jnp.where(some, total, 1.0)
            group = i * KEY_VALUE_HEADS + k
            device, inner = group // groups, group % groups
            messages[device, inner] = (mixed / safe).astype(jnp.bfloat16)
            level = jnp.where(some, peak + jnp.log(safe), HIDDEN)
            stats[device] = jnp.where(lane == inner, level, stats[device])

    for offset in range(tp_count):
        device = tp_index ^ offset
        message_refs[offset][0:groups] = messages[device]
        level = stats[device]
        high = level.astype(jnp.bfloat16).astype(jnp.float32)
        rest = level - high
        middle = rest.astype(jnp.bfloat16).astype(jnp.float32)
        low = rest - middle
        packed = high + pltpu.roll(middle, groups, 1) + pltpu.roll(low, 2 * groups, 1)
        message_refs[offset][groups] = packed.astype(jnp.bfloat16)


def attend(routing, lengths, cache, queries, tp_count):
    section_count = len(queries)
    samples, _, heads, _ = queries[0].shape[1:]
    rows = samples * heads
    groups = REQ_GRP * KEY_VALUE_HEADS // tp_count
    message = jax.ShapeDtypeStruct((groups + 1, rows, HEAD_SIZE), jnp.bfloat16)
    multiplies = REQ_GRP * rows * KEY_VALUE_HEADS * HEAD_SIZE * cache.shape[2]
    return pl.pallas_call(
        functools.partial(attend_kernel, section_count, tp_count),
        out_shape=[message] * tp_count,
        in_specs=[SMEM, SMEM, ANY] + [VMEM] * section_count,
        out_specs=[VMEM] * tp_count,
        scratch_shapes=[
            pltpu.SMEM((REQ_GRP,), jnp.int32),
            pltpu.SMEM((section_count,), jnp.int32),
            pltpu.VMEM(cache.shape, cache.dtype),
            pltpu.VMEM((section_count * CAP, KEY_VALUE_HEADS, rows, HEAD_SIZE), jnp.bfloat16),
            pltpu.VMEM((tp_count, rows, HEAD_SIZE), jnp.float32),
            pltpu.VMEM((tp_count, groups, rows, HEAD_SIZE), jnp.bfloat16),
            pltpu.SemaphoreType.DMA((REQ_GRP,)),
        ],
        compiler_params=pltpu.CompilerParams(vmem_limit_bytes=24 << 20),
        cost_estimate=pl.CostEstimate(
            flops=4 * multiplies, bytes_accessed=2 * cache.size, transcendentals=multiplies // HEAD_SIZE
        ),
        name="attend",
    )(routing, lengths, cache, *queries)


def join_kernel(samples, *refs):
    message_refs, out_ref, joined = refs[:-2], refs[-2], refs[-1]
    groups = message_refs[0].shape[0] - 1
    rows = message_refs[0].shape[1]
    heads = rows // samples
    levels = []
    for ref in message_refs:
        packed = ref[groups].astype(jnp.float32)
        span = HEAD_SIZE
        levels.append(
            packed + pltpu.roll(packed, span - groups, 1) + pltpu.roll(packed, span - 2 * groups, 1)
        )
    summit = functools.reduce(jnp.maximum, levels)
    scales = [jnp.exp(level - summit) for level in levels]
    total = functools.reduce(jnp.add, scales)
    scales = [scale / total for scale in scales]
    for inner in range(groups):
        terms = [
            ref[inner].astype(jnp.float32) * scale[:, inner : inner + 1]
            for ref, scale in zip(message_refs, scales)
        ]
        joined[inner] = functools.reduce(jnp.add, terms)
    for inner in range(groups):
        for head in range(heads):
            block = joined[inner, pl.ds(head, samples, stride=heads), :]
            if len(out_ref.shape) == 2:
                row = inner // KEY_VALUE_HEADS * samples
                column = (inner % KEY_VALUE_HEADS * heads + head) * HEAD_SIZE
                out_ref[row : row + samples, column : column + HEAD_SIZE] = block
            else:
                out_ref[inner, :, head * HEAD_SIZE : (head + 1) * HEAD_SIZE] = block


def join(messages, samples):
    groups = messages[0].shape[0] - 1
    rows = messages[0].shape[1]
    width = rows // samples * HEAD_SIZE
    if groups % KEY_VALUE_HEADS == 0:
        shape = (groups // KEY_VALUE_HEADS * samples, KEY_VALUE_HEADS * width)
    else:
        shape = (groups, samples, width)
    return pl.pallas_call(
        functools.partial(join_kernel, samples),
        out_shape=jax.ShapeDtypeStruct(shape, jnp.float32),
        in_specs=[VMEM] * len(messages),
        out_specs=VMEM,
        scratch_shapes=[pltpu.VMEM((groups, rows, HEAD_SIZE), jnp.float32)],
        cost_estimate=pl.CostEstimate(
            flops=4 * len(messages) * messages[0].size,
            bytes_accessed=2 * len(messages) * messages[0].size,
            transcendentals=0,
        ),
        name="join",
    )(*messages).astype(jnp.bfloat16)


def project_kernel(count, *refs):
    part_refs, weight_ref, out_ref = refs[:count], refs[count], refs[count + 1]
    tp_index = lax.axis_index("tp")
    left = jnp.concatenate([ref[...].astype(jnp.float32) for ref in part_refs], axis=0)
    result = jnp.dot(left.astype(jnp.bfloat16), weight_ref[...], preferred_element_type=jnp.float32)
    samples = out_ref.shape[1]
    share = out_ref.shape[0] // count
    for offset in range(count):
        first = (tp_index ^ offset) * share
        for n in range(share):
            row = (offset * share + n) * samples
            out_ref[first + n] = result[row : row + samples].astype(out_ref.dtype)


def project(parts, weight, samples):
    count = len(parts)
    prompts = sum(part.shape[0] for part in parts) // samples
    depth, width = weight.shape
    tile = min(512, width)
    return pl.pallas_call(
        functools.partial(project_kernel, count),
        grid=(width // tile,),
        out_shape=jax.ShapeDtypeStruct((prompts, samples, width), jnp.bfloat16),
        in_specs=[pl.BlockSpec(part.shape, lambda n: (0, 0)) for part in parts]
        + [pl.BlockSpec((depth, tile), lambda n: (0, n))],
        out_specs=pl.BlockSpec((prompts, samples, tile), lambda n: (0, 0, n)),
        compiler_params=pltpu.CompilerParams(vmem_limit_bytes=24 << 20),
        cost_estimate=pl.CostEstimate(
            flops=2 * prompts * samples * depth * width, bytes_accessed=2 * depth * width, transcendentals=0
        ),
        name="project",
    )(*parts, weight)


def body(prompt_key_values, queries, routing, lengths, out_weight):
    section_count = lax.axis_size("sec")
    tp_count = lax.axis_size("tp")
    section = lax.axis_index("sec")
    slot_count, samples, query_width = queries.shape[1:]
    heads = query_width // HEAD_SIZE // KEY_VALUE_HEADS
    routing = routing.reshape(-1)
    blocks = queries.reshape(section_count, CAP, samples, KEY_VALUE_HEADS, heads, HEAD_SIZE)
    own_queries = []
    for offset in range(section_count):
        block = lax.dynamic_index_in_dim(blocks, section ^ offset, 0, keepdims=False)
        own_queries.append(swap(block, "sec", offset) if offset else block)

    far = [offset for offset in range(2, section_count)]
    outgoing = pack(routing, prompt_key_values, far, section_count)
    arrived = [
        (offset, order, swap(outgoing[n * CAP + order], "sec", offset))
        for order in range(CAP)
        for n, offset in enumerate(far)
    ]
    *near, whole = pack(routing, prompt_key_values, [1, 0], section_count)
    whole = place(whole, [swap(part, "sec", 1) for part in near], [(1, order) for order in range(CAP)])

    messages = attend(routing, lengths, prompt_key_values, own_queries, tp_count)
    messages = [swap(part, "tp", offset) if offset else part for offset, part in enumerate(messages)]
    share = join(messages, samples)
    shares = [swap(share, "tp", offset) if offset else share for offset in range(tp_count)]
    if share.ndim == 3:
        tp_index = lax.axis_index("tp")
        stacked = jnp.stack(shares)[jnp.arange(tp_count) ^ tp_index]
        stacked = stacked.reshape(REQ_GRP, KEY_VALUE_HEADS, samples, -1).transpose(0, 2, 1, 3)
        attended = stacked.reshape(REQ_GRP * samples, query_width)
        layer_out = jnp.dot(attended, out_weight, preferred_element_type=jnp.float32)
        layer_out = layer_out.astype(jnp.bfloat16).reshape(REQ_GRP, samples, -1)
    else:
        layer_out = project(shares, out_weight, samples)

    half = len(arrived) // 2
    for some in (arrived[:half], arrived[half:]):
        whole = place(whole, [part for _, _, part in some], [(offset, order) for offset, order, _ in some])
    return (layer_out, whole)


def solution(mesh):
    placed = (
        P(("rep", "sec"), None, "tp", None),
        P(("rep", "sec"), None, None, None),
        P("rep", None),
        P("rep"),
        P(None, "tp"),
    )
    return jax.shard_map(
        body,
        mesh=mesh,
        in_specs=placed,
        out_specs=(P(("rep", "sec"), None, "tp"), P(("rep", "sec"), None, None, "tp", None)),
        check_vma=False,
    )
```

time: 171 us -> 289 us (1.69)
  Pallas kernels: 0 us -> 248 us
  waiting for transfers between devices: 72.6 us -> 10.4 us
  blocking collectives: 27.9 us -> 0 us
  between operations: 14.2 us -> 0.82 us
  other arithmetic: 13 us -> 0.91 us
  matrix products: 11.7 us -> 0 us
  local copies, waits for them, and re-layouts: 22.6 us -> 12.7 us
  starting transfers between devices: 8.36 us -> 15.9 us
    pallas_call x0 -> x8, Pallas kernels: none -> 248 us  [the longest x2 131 us: pack(): pl.pallas_call(functools.partial(pack_kernel, offsets, section_count), ou...]
    all_to_all x2 -> x0, waiting for transfers between devices: 52.8 us -> none  [the longest x1 48.2 us: body(): lax.all_to_all(outgoing, 'sec', split_axis=0, concat_axis=0, tiled=True)]
    all_gather x2 -> x0, blocking collectives: 27.9 us -> none  [combined_all(): everything = jax.tree.map(lambda part: lax.all_gather(part, axis), value)]
    all_gather x1 -> x0, waiting for transfers between devices: 19.7 us -> none  [combined_all(): everything = jax.tree.map(lambda part: lax.all_gather(part, axis), value)]
    ppermute x0 -> x15, starting transfers between devices: none -> 15.9 us  [swap(): return lax.ppermute(value, axis, [(i, i ^ offset) for i in range(count)])]
    dot_general x3 -> x0, matrix products: 11.7 us -> none  [the longest x1 8.78 us: body(): jnp.dot(attended, out_weight, preferred_element_type=jnp.float32)]
    ppermute x0 -> x15, waiting for transfers between devices: none -> 10.4 us  [swap(): return lax.ppermute(value, axis, [(i, i ^ offset) for i in range(count)])]
    slice x3 -> x0, local copies, waits for them, and re-layouts: 9.15 us -> none  [the longest x2 6.3 us: body(): arrived_cache[:, 0]]
  transfers between devices with their start and end apart: 3 -> 15, of which waited for: 3 -> 4; matrix products, arithmetic and copies ran while one was open for 1% -> 0% of each run, Pallas kernels for 0% -> 52%
where the time goes in v1:
time: 289 us
  Pallas kernels  248 us (86%)
  starting transfers between devices  15.9 us (6%)
  local copies, waits for them, and re-layouts  12.7 us (4%)
  waiting for transfers between devices  10.4 us (4%)
    pallas_call x2, Pallas kernels, pack(): pl.pallas_call(functools.partial(pack_kernel, offsets, section_count), ou...  131 us
    pallas_call x3, Pallas kernels, place(): pl.pallas_call(functools.partial(place_kernel, offsets), out_shape=jax.Sh...  98.6 us
    ppermute x15, starting transfers between devices, swap(): return lax.ppermute(value, axis, [(i, i ^ offset) for i in range(count)])  15.9 us
    unnamed x30, local copies, waits for them, and re-layouts  12.4 us
    ppermute x15, waiting for transfers between devices, swap(): return lax.ppermute(value, axis, [(i, i ^ offset) for i in range(count)])  10.4 us
    pallas_call x1, Pallas kernels, attend(): pl.pallas_call(functools.partial(attend_kernel, section_count, tp_count),...  9.62 us
    pallas_call x1, Pallas kernels, project(): pl.pallas_call(functools.partial(project_kernel, count), grid=(width // t...  6.62 us
  transfers between devices with their start and end apart: 15, of which 4 were waited for; matrix products, arithmetic and copies ran while one was open for 0% of the time, Pallas kernels for 52%

profile of v1, /device:TPU:0, one launch (start us, length us, event | category | flops | bytes accessed | tf_op | source)
XLA Modules:
  0.0 288.5 jit_solution(25465091817357081)
XLA Ops:
  0.7 65.5 %pack_cache.2 = (bf16[1,2,256,512]{3,2,1,0:T(8,128)(2,1)}, bf16[1,2,256,512]{3,2,1,0:T(8,128)(2,1)}, bf16[1,8,2,256,512]{4,3,2,1,0:T(8,128)(2,1)}) custom-call(s32[32]{0:T(128)} %bitcast.9, bf16[8,2,256,512]{3,2,1,0:T(8,128)(2,1)} %cache_ref.5), custom_call_target="tpu_custom_call" | custom-call | bytes 4194304 | tf_op jit(solution)/shard_map/pack_cache/pallas_call | solution.py:86
  66.2 0.5 collective-permute-start.10
  67.2 2.9 %collective-permute-start.1 = (bf16[2,4,4,8,128]{4,3,2,1,0:T(8,128)(2,1)S(1)}, bf16[2,4,4,8,128]{4,3,2,1,0:T(8,128)(2,1)S(1)}, u32[]{:S(2)}, u32[]{:S(2)}) collective-permute-start(bf16[2,4,4,8,128]{4,3,2,1,0:T(8,128)(2,1)S(1)} %get-tuple-element.25), channel_id=1, source_target_pairs={{0,2},{1,3},{2,0},{3,1},{4,6},{5,7},{6,4},{7,5},{8,10},{9,11},{10,... | collective-permute-start | bytes 196616 | tf_op jit(solution)/shard_map/ppermute | solution.py:23
  70.1 2.3 collective-permute-done.1.refs_2_
  72.4 2.0 collective-permute-done.2.refs_3_
  74.5 2.2 copy-done
  76.7 9.6 %attend.1 = (bf16[9,32,128]{2,1,0:T(8,128)(2,1)S(1)}, bf16[9,32,128]{2,1,0:T(8,128)(2,1)S(1)}, bf16[9,32,128]{2,1,0:T(8,128)(2,1)S(1)}, bf16[9,32,128]{2,1,0:T(8,128)(2,1)S(1)}) custom-call(s32[32]{0:T(128)S(1)} %bitcast.11, s32[32]{0:T(128)S(1)} %copy-done.4, bf16[8,2,256,512]{3,2,1,0:T(8,128)(2,1)S(1)} %copy-done, ...), custom_call_target="tpu_custom_call" | custom-call | flops 134217728 | bytes 4194304 | tf_op jit(solution)/shard_map/attend/pallas_call | solution.py:209
  86.3 0.6 copy-done.2
  86.9 1.6 collective-permute-start.3
  88.5 2.6 collective-permute-start.4
  91.3 5.2 %collective-permute-done.4.refs_2_ = bf16[9,32,128]{2,1,0:T(8,128)(2,1)S(1)} collective-permute-done((bf16[9,32,128]{2,1,0:T(8,128)(2,1)S(1)}, bf16[9,32,128]{2,1,0:T(8,128)(2,1)S(1)}, u32[]{:S(2)}, u32[]{:S(2)}) %collective-permute-start.4) | collective-permute-done | bytes 73760 | tf_op jit(solution)/shard_map/ppermute | solution.py:23
  96.6 0.8 collective-permute-done.5.refs_3_
  97.4 0.6 copy-done.13
  98.0 2.0 join.1
  100.0 0.9 convert_element_type.3.refs_0_
  100.9 1.4 collective-permute-start.6
  102.3 1.7 collective-permute-start.7
  104.0 1.3 collective-permute-start.8
  105.3 65.4 %pack_cache.3 = (bf16[1,2,256,512]{3,2,1,0:T(8,128)(2,1)}, bf16[1,2,256,512]{3,2,1,0:T(8,128)(2,1)}, bf16[1,2,256,512]{3,2,1,0:T(8,128)(2,1)}, bf16[1,2,256,512]{3,2,1,0:T(8,128)(2,1)}) custom-call(s32[32]{0:T(128)} %bitcast.10, bf16[8,2,256,512]{3,2,1,0:T(8,128)(2,1)} %cache_ref.5), custom_call_target="tpu_custom_call" | custom-call | bytes 4194304 | tf_op jit(solution)/shard_map/pack_cache/pallas_call | solution.py:86
  170.7 0.8 collective-permute-start.11
  171.4 1.2 collective-permute-start.12
  172.6 0.7 collective-permute-start.13
  173.3 0.9 collective-permute-start.14
  174.2 5.8 %copy-done.1 = bf16[4096,2048]{1,0:T(8,128)(2,1)S(1)} copy-done((bf16[4096,2048]{1,0:T(8,128)(2,1)S(1)}, bf16[4096,2048]{1,0:T(8,128)(2,1)}, u32[]{:S(2)}) %copy-start.1) | copy-done | bytes 16777240
  180.0 6.6 %project.1 = bf16[8,4,2048]{2,1,0:T(4,128)(2,1)} custom-call(bf16[8,4096]{1,0:T(8,128)(2,1)S(1)} %convert_element_type.3.refs_0_, bf16[8,4096]{1,0:T(8,128)(2,1)S(1)} %collective-permute-done.6.refs_1_, bf16[8,4096]{1,0:T(8,128)(2,1)S(1)} %collective-permute-done.7.refs_2_, bf16[8,4096]{1,0:T(8,128)(2,1)S(1)} %collective-permute-done.8.refs_3_, ...), custom_call_target="tpu_custom_call" | custom-call | flops 536870912 | bytes 16777216 | tf_op jit(solution)/shard_map/project/pallas_call | solution.py:306
  186.6 0.8 copy-done.6
  187.4 32.9 %place_cache.3.refs_0_ = bf16[1,8,2,256,512]{4,3,2,1,0:T(8,128)(2,1)} custom-call(bf16[1,8,2,256,512]{4,3,2,1,0:T(8,128)(2,1)} %get-tuple-element.17.refs_0_, bf16[1,2,256,512]{3,2,1,0:T(8,128)(2,1)} %copy-done.6, bf16[1,2,256,512]{3,2,1,0:T(8,128)(2,1)} %copy-done.5), custom_call_target="tpu_custom_call", output_to_operand_aliasing={{}: (0, {})} | custom-call | bytes 2097152 | tf_op jit(solution)/shard_map/place_cache/pallas_call | solution.py:120
  220.4 0.8 copy-done.7
  221.2 0.8 copy-done.9
  221.9 32.9 %place_cache.4.refs_0_ = bf16[1,8,2,256,512]{4,3,2,1,0:T(8,128)(2,1)} custom-call(bf16[1,8,2,256,512]{4,3,2,1,0:T(8,128)(2,1)} %place_cache.3.refs_0_, bf16[1,2,256,512]{3,2,1,0:T(8,128)(2,1)} %copy-done.7, bf16[1,2,256,512]{3,2,1,0:T(8,128)(2,1)} %copy-done.9), custom_call_target="tpu_custom_call", output_to_operand_aliasing={{}: (0, {})} | custom-call | bytes 2097152 | tf_op jit(solution)/shard_map/place_cache/pallas_call | solution.py:120
  254.9 0.8 copy-done.8
  255.6 32.9 %place_cache.5 = bf16[1,8,2,256,512]{4,3,2,1,0:T(8,128)(2,1)} custom-call(bf16[1,8,2,256,512]{4,3,2,1,0:T(8,128)(2,1)} %place_cache.4.refs_0_, bf16[1,2,256,512]{3,2,1,0:T(8,128)(2,1)} %copy-done.8, bf16[1,2,256,512]{3,2,1,0:T(8,128)(2,1)} %collective-permute-done.14.refs_2_), custom_call_target="tpu_custom_call", output_to_operand_aliasing={{}: (0, {})} | custom-call | bytes 2097152 | tf_op jit(solution)/shard_map/place_cache/pallas_call | solution.py:120
  (39 shorter events, 0.7 us)
Async XLA Ops:
  0.6 73.9 %copy-start.3 = (s32[32,1]{0,1:T(1,128)S(1)}, s32[32,1]{0,1:T(1,128)}, u32[]{:S(2)}) copy-start(s32[32,1]{0,1:T(1,128)} %param.7) | copy-start | bytes 388
  0.6 66.1 %copy-start.10 = (bf16[1,8,4,4096]{3,2,1,0:T(4,128)(2,1)S(1)}, bf16[1,8,4,4096]{3,2,1,0:T(4,128)(2,1)}, u32[]{:S(2)}) copy-start(bf16[1,8,4,4096]{3,2,1,0:T(4,128)(2,1)} %param.6) | copy-start | bytes 786436
  0.7 73.8 %copy-start.4 = (s32[32]{0:T(128)S(1)}, s32[32]{0:T(128)}, u32[]{:S(2)}) copy-start(s32[32]{0:T(128)} %lengths_ref.1) | copy-start | bytes 388
  66.2 39.1 %copy-start.14 = (bf16[1,2,256,512]{3,2,1,0:T(8,128)(2,1)S(1)}, bf16[1,2,256,512]{3,2,1,0:T(8,128)(2,1)}, u32[]{:S(2)}) copy-start(bf16[1,2,256,512]{3,2,1,0:T(8,128)(2,1)} %get-tuple-element.18) | copy-start | bytes 1572868
  66.2 107.1 %collective-permute-start.10 = (bf16[1,2,256,512]{3,2,1,0:T(8,128)(2,1)}, bf16[1,2,256,512]{3,2,1,0:T(8,128)(2,1)S(1)}, u32[]{:S(2)}, u32[]{:S(2)}) collective-permute-start(bf16[1,2,256,512]{3,2,1,0:T(8,128)(2,1)} %get-tuple-element.19), channel_id=1, source_target_pairs={{0,1},{1,0},{2,3},{3,2},{4,5},{5,4},{6,7},{7,6},{8,9},{9,8},{10,11... | collective-permute-start | bytes 1572872 | tf_op jit(solution)/shard_map/ppermute | solution.py:23
  67.1 3.1 %collective-permute-start = (bf16[2,4,4,8,128]{4,3,2,1,0:T(8,128)(2,1)S(1)}, bf16[2,4,4,8,128]{4,3,2,1,0:T(8,128)(2,1)S(1)}, u32[]{:S(2)}, u32[]{:S(2)}) collective-permute-start(bf16[2,4,4,8,128]{4,3,2,1,0:T(8,128)(2,1)S(1)} %get-tuple-element.26), channel_id=1, source_target_pairs={{0,1},{1,0},{2,3},{3,2},{4,5},{5,4},{6,7},{7,6},{8,9},{9,8},{10,11... | collective-permute-start | bytes 196616 | tf_op jit(solution)/shard_map/ppermute | solution.py:23
  67.2 5.3 %collective-permute-start.1 = (bf16[2,4,4,8,128]{4,3,2,1,0:T(8,128)(2,1)S(1)}, bf16[2,4,4,8,128]{4,3,2,1,0:T(8,128)(2,1)S(1)}, u32[]{:S(2)}, u32[]{:S(2)}) collective-permute-start(bf16[2,4,4,8,128]{4,3,2,1,0:T(8,128)(2,1)S(1)} %get-tuple-element.25), channel_id=1, source_target_pairs={{0,2},{1,3},{2,0},{3,1},{4,6},{5,7},{6,4},{7,5},{8,10},{9,11},{10,... | collective-permute-start | bytes 196616 | tf_op jit(solution)/shard_map/ppermute | solution.py:23
  70.1 4.4 %collective-permute-start.2 = (bf16[2,4,4,8,128]{4,3,2,1,0:T(8,128)(2,1)S(1)}, bf16[2,4,4,8,128]{4,3,2,1,0:T(8,128)(2,1)S(1)}, u32[]{:S(2)}, u32[]{:S(2)}) collective-permute-start(bf16[2,4,4,8,128]{4,3,2,1,0:T(8,128)(2,1)S(1)} %get-tuple-element.24), channel_id=1, source_target_pairs={{0,3},{1,2},{2,1},{3,0},{4,7},{5,6},{6,5},{7,4},{8,11},{9,10},{10,... | collective-permute-start | bytes 196616 | tf_op jit(solution)/shard_map/ppermute | solution.py:23
  74.5 2.2 copy-start
  86.3 0.6 copy-start.2
  86.9 4.4 %collective-permute-start.3 = (bf16[9,32,128]{2,1,0:T(8,128)(2,1)S(1)}, bf16[9,32,128]{2,1,0:T(8,128)(2,1)S(1)}, u32[]{:S(2)}, u32[]{:S(2)}) collective-permute-start(bf16[9,32,128]{2,1,0:T(8,128)(2,1)S(1)} %get-tuple-element.14), channel_id=1, source_target_pairs={{0,4},{4,0},{8,12},{12,8},{1,5},{5,1},{9,13},{13,9},{2,6},{6,2},{1... | collective-permute-start | bytes 221192 | tf_op jit(solution)/shard_map/ppermute | solution.py:23
  88.5 8.0 %collective-permute-start.4 = (bf16[9,32,128]{2,1,0:T(8,128)(2,1)S(1)}, bf16[9,32,128]{2,1,0:T(8,128)(2,1)S(1)}, u32[]{:S(2)}, u32[]{:S(2)}) collective-permute-start(bf16[9,32,128]{2,1,0:T(8,128)(2,1)S(1)} %get-tuple-element.15), channel_id=1, source_target_pairs={{0,8},{4,12},{8,0},{12,4},{1,9},{5,13},{9,1},{13,5},{2,10},{6,14},... | collective-permute-start | bytes 221192 | tf_op jit(solution)/shard_map/ppermute | solution.py:23
  91.1 6.3 %collective-permute-start.5 = (bf16[9,32,128]{2,1,0:T(8,128)(2,1)S(1)}, bf16[9,32,128]{2,1,0:T(8,128)(2,1)S(1)}, u32[]{:S(2)}, u32[]{:S(2)}) collective-permute-start(bf16[9,32,128]{2,1,0:T(8,128)(2,1)S(1)} %get-tuple-element.16), channel_id=1, source_target_pairs={{0,12},{4,8},{8,4},{12,0},{1,13},{5,9},{9,5},{13,1},{2,14},{6,10},... | collective-permute-start | bytes 221192 | tf_op jit(solution)/shard_map/ppermute | solution.py:23
  91.3 6.0 %copy-start.11 = (bf16[9,32,128]{2,1,0:T(8,128)(2,1)}, bf16[9,32,128]{2,1,0:T(8,128)(2,1)S(1)}, u32[]{:S(2)}) copy-start(bf16[9,32,128]{2,1,0:T(8,128)(2,1)S(1)} %collective-permute-done.3.refs_1_) | copy-start | bytes 221188
  96.6 0.8 copy-start.12
  97.4 0.6 copy-start.13
  100.9 69.8 %collective-permute-start.6 = (bf16[8,4096]{1,0:T(8,128)(2,1)S(1)}, bf16[8,4096]{1,0:T(8,128)(2,1)S(1)}, u32[]{:S(2)}, u32[]{:S(2)}) collective-permute-start(bf16[8,4096]{1,0:T(8,128)(2,1)S(1)} %convert_element_type.3.refs_0_), channel_id=1, source_target_pairs={{0,4},{4,0},{8,12},{12,8},{1,5},{5,1},{9,13},{13,9},{2,6},{6,2},{1... | collective-permute-start | bytes 196616 | tf_op jit(solution)/shard_map/ppermute | solution.py:23
  102.3 69.2 %collective-permute-start.7 = (bf16[8,4096]{1,0:T(8,128)(2,1)S(1)}, bf16[8,4096]{1,0:T(8,128)(2,1)S(1)}, u32[]{:S(2)}, u32[]{:S(2)}) collective-permute-start(bf16[8,4096]{1,0:T(8,128)(2,1)S(1)} %convert_element_type.3.refs_0_), channel_id=1, source_target_pairs={{0,8},{4,12},{8,0},{12,4},{1,9},{5,13},{9,1},{13,5},{2,10},{6,14},... | collective-permute-start | bytes 196616 | tf_op jit(solution)/shard_map/ppermute | solution.py:23
  104.0 68.7 %collective-permute-start.8 = (bf16[8,4096]{1,0:T(8,128)(2,1)S(1)}, bf16[8,4096]{1,0:T(8,128)(2,1)S(1)}, u32[]{:S(2)}, u32[]{:S(2)}) collective-permute-start(bf16[8,4096]{1,0:T(8,128)(2,1)S(1)} %convert_element_type.3.refs_0_), channel_id=1, source_target_pairs={{0,12},{4,8},{8,4},{12,0},{1,13},{5,9},{9,5},{13,1},{2,14},{6,10},... | collective-permute-start | bytes 196616 | tf_op jit(solution)/shard_map/ppermute | solution.py:23
  105.3 81.4 %collective-permute-start.9 = (bf16[1,2,256,512]{3,2,1,0:T(8,128)(2,1)S(1)}, bf16[1,2,256,512]{3,2,1,0:T(8,128)(2,1)S(1)}, u32[]{:S(2)}, u32[]{:S(2)}) collective-permute-start(bf16[1,2,256,512]{3,2,1,0:T(8,128)(2,1)S(1)} %copy-done.14), channel_id=1, source_target_pairs={{0,1},{1,0},{2,3},{3,2},{4,5},{5,4},{6,7},{7,6},{8,9},{9,8},{10,11... | collective-permute-start | bytes 1572872 | tf_op jit(solution)/shard_map/ppermute | solution.py:23
  170.7 49.7 %collective-permute-start.11 = (bf16[1,2,256,512]{3,2,1,0:T(8,128)(2,1)}, bf16[1,2,256,512]{3,2,1,0:T(8,128)(2,1)S(1)}, u32[]{:S(2)}, u32[]{:S(2)}) collective-permute-start(bf16[1,2,256,512]{3,2,1,0:T(8,128)(2,1)} %get-tuple-element.20), channel_id=1, source_target_pairs={{0,2},{1,3},{2,0},{3,1},{4,6},{5,7},{6,4},{7,5},{8,10},{9,11},{10,... | collective-permute-start | bytes 1572872 | tf_op jit(solution)/shard_map/ppermute | solution.py:23
  171.4 48.9 %collective-permute-start.12 = (bf16[1,2,256,512]{3,2,1,0:T(8,128)(2,1)}, bf16[1,2,256,512]{3,2,1,0:T(8,128)(2,1)S(1)}, u32[]{:S(2)}, u32[]{:S(2)}) collective-permute-start(bf16[1,2,256,512]{3,2,1,0:T(8,128)(2,1)} %get-tuple-element.21), channel_id=1, source_target_pairs={{0,3},{1,2},{2,1},{3,0},{4,7},{5,6},{6,5},{7,4},{8,11},{9,10},{10,... | collective-permute-start | bytes 1572872 | tf_op jit(solution)/shard_map/ppermute | solution.py:23
  172.6 82.2 %collective-permute-start.13 = (bf16[1,2,256,512]{3,2,1,0:T(8,128)(2,1)}, bf16[1,2,256,512]{3,2,1,0:T(8,128)(2,1)S(1)}, u32[]{:S(2)}, u32[]{:S(2)}) collective-permute-start(bf16[1,2,256,512]{3,2,1,0:T(8,128)(2,1)} %get-tuple-element.22), channel_id=1, source_target_pairs={{0,2},{1,3},{2,0},{3,1},{4,6},{5,7},{6,4},{7,5},{8,10},{9,11},{10,... | collective-permute-start | bytes 1572872 | tf_op jit(solution)/shard_map/ppermute | solution.py:23
  173.3 13.3 %copy-start.5 = (bf16[1,2,256,512]{3,2,1,0:T(8,128)(2,1)}, bf16[1,2,256,512]{3,2,1,0:T(8,128)(2,1)S(1)}, u32[]{:S(2)}) copy-start(bf16[1,2,256,512]{3,2,1,0:T(8,128)(2,1)S(1)} %collective-permute-done.10.refs_2_) | copy-start | bytes 1572868
  173.3 81.5 %collective-permute-start.14 = (bf16[1,2,256,512]{3,2,1,0:T(8,128)(2,1)}, bf16[1,2,256,512]{3,2,1,0:T(8,128)(2,1)}, u32[]{:S(2)}, u32[]{:S(2)}) collective-permute-start(bf16[1,2,256,512]{3,2,1,0:T(8,128)(2,1)} %get-tuple-element.23), channel_id=1, source_target_pairs={{0,3},{1,2},{2,1},{3,0},{4,7},{5,6},{6,5},{7,4},{8,11},{9,10},{10,... | collective-permute-start | bytes 1572872 | tf_op jit(solution)/shard_map/ppermute | solution.py:23
  174.2 5.8 %copy-start.1 = (bf16[4096,2048]{1,0:T(8,128)(2,1)S(1)}, bf16[4096,2048]{1,0:T(8,128)(2,1)}, u32[]{:S(2)}) copy-start(bf16[4096,2048]{1,0:T(8,128)(2,1)} %refs_4_.1) | copy-start | bytes 50331652
  186.6 0.8 copy-start.6
  220.3 0.8 copy-start.7
  221.1 0.8 copy-start.9
  254.8 0.8 copy-start.8

commit v2 on v0

v2 whole, which is shorter than its diff:
```python
import functools

import jax
import jax.numpy as jnp
from jax import lax
from jax.experimental import pallas as pl
from jax.experimental.pallas import tpu as pltpu
from jax.sharding import PartitionSpec as P

HEAD_SIZE = 128
KEY_VALUE_HEADS = 4
REQ_GRP = 8
CAP = 2
HIDDEN = -1e30

HBM = pl.BlockSpec(memory_space=pltpu.HBM)
VMEM = pl.BlockSpec(memory_space=pltpu.VMEM)
SMEM = pl.BlockSpec(memory_space=pltpu.SMEM)


def limit(mebibytes):
    return pltpu.CompilerParams(vmem_limit_bytes=mebibytes << 20)


def cost(flops, bytes_accessed, transcendentals=0):
    return pl.CostEstimate(flops=flops, bytes_accessed=bytes_accessed, transcendentals=transcendentals)


def swap(value, axis, offset):
    count = lax.axis_size(axis)
    return lax.ppermute(value, axis, [(i, i ^ offset) for i in range(count)])


def scatter(value, axis):
    return lax.all_to_all(value, axis, split_axis=0, concat_axis=0, tiled=True)


def own_slots(routing_ref, section, used, source):
    for t in range(used.shape[0]):
        used[t] = 0
    for i in range(REQ_GRP):
        target = routing_ref[section * REQ_GRP + i]
        order = used[target]
        used[target] = order + 1
        source[target * CAP + order] = i


def pack_kernel(section_count, routing_ref, cache_ref, *refs):
    out_refs, (source, used, sem) = refs[:-3], refs[-3:]
    section = lax.axis_index("sec")
    full = section_count * CAP == REQ_GRP
    own_slots(routing_ref, section, used, source)

    def copy(n, row):
        return pltpu.make_async_copy(cache_ref.at[row], out_refs[n].at[0], sem.at[n])

    for n in reversed(range(section_count * CAP)):
        slot = (section ^ (n // CAP)) * CAP + n % CAP
        if full:
            copy(n, source[slot]).start()
        else:
            filled = n % CAP < used[slot // CAP]

            @pl.when(filled)
            def _():
                copy(n, source[slot]).start()

            @pl.when(jnp.logical_not(filled))
            def _():
                out_refs[n][...] = jnp.zeros_like(out_refs[n])

    for n in reversed(range(section_count * CAP)):
        if full:
            copy(n, 0).wait()
        else:
            slot = (section ^ (n // CAP)) * CAP + n % CAP

            @pl.when(n % CAP < used[slot // CAP])
            def _():
                copy(n, 0).wait()


def pack(routing, cache, section_count):
    slots = section_count * CAP
    return pl.pallas_call(
        functools.partial(pack_kernel, section_count),
        out_shape=[jax.ShapeDtypeStruct((1,) + cache.shape[1:], cache.dtype)] * slots,
        in_specs=[SMEM, HBM],
        out_specs=[VMEM] * slots,
        scratch_shapes=[
            pltpu.SMEM((slots,), jnp.int32),
            pltpu.SMEM((section_count,), jnp.int32),
            pltpu.SemaphoreType.DMA((slots,)),
        ],
        compiler_params=limit(8),
        cost_estimate=cost(0, 4 * cache.size),
        name="pack_cache",
    )(routing, cache)


def place_kernel(slots, *refs):
    count = len(slots)
    part_refs, out_ref, sem = refs[-2 - count : -2], refs[-2], refs[-1]
    section = lax.axis_index("sec")
    copies = []
    for n, (offset, order) in enumerate(slots):
        slot = out_ref.at[0, (section ^ offset) * CAP + order]
        copy = pltpu.make_async_copy(part_refs[n].at[0], slot, sem.at[n])
        copy.start()
        copies.append(copy)
    for copy in copies:
        copy.wait()


def place(whole, parts, slots, slot_count):
    given = [] if whole is None else [whole]
    part = parts[0]
    return pl.pallas_call(
        functools.partial(place_kernel, slots),
        out_shape=jax.ShapeDtypeStruct((1, slot_count) + part.shape[1:], part.dtype),
        in_specs=[HBM] * len(given) + [VMEM] * len(parts),
        out_specs=HBM,
        scratch_shapes=[pltpu.SemaphoreType.DMA((len(parts),))],
        input_output_aliases={0: 0} if given else {},
        compiler_params=limit(8),
        cost_estimate=cost(0, 4 * len(parts) * part.size),
        name="place_cache",
    )(*given, *parts)


def attend_kernel(section_count, routing_ref, lengths_ref, query_ref, *refs):
    slots = section_count * CAP
    cache_refs, message_ref = refs[:slots], refs[slots]
    source, used, stats = refs[slots + 1 :]
    section = lax.axis_index("sec")
    tp_index = lax.axis_index("tp")
    samples, _, heads, _ = query_ref.shape[2:]
    rows = samples * heads
    local = cache_refs[0].shape[2]
    groups = message_ref.shape[1] - 1
    full = slots == REQ_GRP
    own_slots(routing_ref, section, used, source)
    stats[...] = jnp.zeros_like(stats)
    lane = lax.broadcasted_iota(jnp.int32, (rows, HEAD_SIZE), 1)
    position = lax.broadcasted_iota(jnp.int32, (rows, local), 1) + tp_index * local

    def partial(n, k, row):
        columns = pl.ds(pl.multiple_of(k * HEAD_SIZE, HEAD_SIZE), HEAD_SIZE)
        target = section ^ (n // CAP)
        visible = position < lengths_ref[section * REQ_GRP + row]
        query = query_ref[target, n % CAP, :, k].astype(jnp.float32).reshape(rows, HEAD_SIZE)
        score = lax.dot_general(
            query.astype(jnp.bfloat16),
            cache_refs[n][0, 0, :, columns],
            (((1,), (1,)), ((), ())),
            preferred_element_type=jnp.float32,
        ) * HEAD_SIZE ** (-0.5)
        score = jnp.where(visible, score, HIDDEN)
        peak = jnp.max(score, axis=1, keepdims=True)
        weight = jnp.where(visible, jnp.exp(score - peak), 0.0)
        total = jnp.sum(weight, axis=1, keepdims=True)
        mixed = jnp.dot(
            weight.astype(jnp.bfloat16), cache_refs[n][0, 1, :, columns], preferred_element_type=jnp.float32
        )
        some = total > 0.0
        safe = jnp.where(some, total, 1.0)
        return (mixed / safe).astype(jnp.bfloat16), jnp.where(some, peak + jnp.log(safe), HIDDEN)

    def store(k, row, result):
        mixed, level = result
        group = row * KEY_VALUE_HEADS + k
        device, inner = group // groups, group % groups
        message_ref[device, inner] = mixed
        stats[device] = jnp.where(lane == inner, level, stats[device])

    @pl.loop(0, KEY_VALUE_HEADS)
    def _(k):
        if full:
            numbers = [source[(section ^ (n // CAP)) * CAP + n % CAP] for n in range(slots)]
            results = [partial(n, k, row) for n, row in enumerate(numbers)]
            for row, result in zip(numbers, results):
                store(k, row, result)
        else:
            for n in range(slots):
                target = section ^ (n // CAP)

                @pl.when(n % CAP < used[target])
                def _():
                    row = source[target * CAP + n % CAP]
                    store(k, row, partial(n, k, row))

    for device in range(message_ref.shape[0]):
        level = stats[device]
        high = level.astype(jnp.bfloat16).astype(jnp.float32)
        rest = level - high
        middle = rest.astype(jnp.bfloat16).astype(jnp.float32)
        low = rest - middle
        packed = high + pltpu.roll(middle, groups, 1) + pltpu.roll(low, 2 * groups, 1)
        message_ref[device, groups] = packed.astype(jnp.bfloat16)


def attend(routing, lengths, queries, caches, tp_count):
    section_count, _, samples, _, heads, _ = queries.shape
    rows = samples * heads
    groups = REQ_GRP * KEY_VALUE_HEADS // tp_count
    multiplies = REQ_GRP * rows * KEY_VALUE_HEADS * HEAD_SIZE * caches[0].shape[2]
    return pl.pallas_call(
        functools.partial(attend_kernel, section_count),
        out_shape=jax.ShapeDtypeStruct((tp_count, groups + 1, rows, HEAD_SIZE), jnp.bfloat16),
        in_specs=[SMEM, SMEM] + [VMEM] * (1 + len(caches)),
        out_specs=VMEM,
        scratch_shapes=[
            pltpu.SMEM((section_count * CAP,), jnp.int32),
            pltpu.SMEM((section_count,), jnp.int32),
            pltpu.VMEM((tp_count, rows, HEAD_SIZE), jnp.float32),
        ],
        compiler_params=limit(12),
        cost_estimate=cost(4 * multiplies, 2 * len(caches) * caches[0].size, multiplies // HEAD_SIZE),
        name="attend",
    )(routing, lengths, queries, *caches)


def join_kernel(message_ref, out_ref, joined, flat):
    count, groups, rows, span = message_ref.shape
    groups -= 1
    samples = flat.shape[-2] if len(flat.shape) == 3 else flat.shape[0] // (groups // KEY_VALUE_HEADS)
    heads = rows // samples
    levels = []
    for n in range(count):
        packed = message_ref[n, groups].astype(jnp.float32)
        levels.append(packed + pltpu.roll(packed, span - groups, 1) + pltpu.roll(packed, span - 2 * groups, 1))
    summit = functools.reduce(jnp.maximum, levels)
    scales = [jnp.exp(level - summit) for level in levels]
    total = functools.reduce(jnp.add, scales)
    scales = [scale / total for scale in scales]
    for inner in range(groups):
        terms = [message_ref[n, inner].astype(jnp.float32) * scales[n][:, inner : inner + 1] for n in range(count)]
        joined[inner] = functools.reduce(jnp.add, terms)
    for inner in range(groups):
        for head in range(heads):
            block = joined[inner, pl.ds(head, samples, stride=heads), :]
            if len(flat.shape) == 2:
                row = inner // KEY_VALUE_HEADS * samples
                column = (inner % KEY_VALUE_HEADS * heads + head) * HEAD_SIZE
                flat[row : row + samples, column : column + HEAD_SIZE] = block
            else:
                flat[inner, :, head * HEAD_SIZE : (head + 1) * HEAD_SIZE] = block
    rounded = flat[...].astype(jnp.bfloat16)
    for n in range(count):
        out_ref[n] = rounded


def join(messages, samples):
    count, groups, rows, _ = messages.shape
    groups -= 1
    width = rows // samples * HEAD_SIZE
    if groups % KEY_VALUE_HEADS == 0:
        shape = (groups // KEY_VALUE_HEADS * samples, KEY_VALUE_HEADS * width)
    else:
        shape = (groups, samples, width)
    return pl.pallas_call(
        join_kernel,
        out_shape=jax.ShapeDtypeStruct((count,) + shape, jnp.bfloat16),
        in_specs=[VMEM],
        out_specs=VMEM,
        scratch_shapes=[
            pltpu.VMEM((groups, rows, HEAD_SIZE), jnp.float32),
            pltpu.VMEM(shape, jnp.float32),
        ],
        compiler_params=limit(8),
        cost_estimate=cost(4 * messages.size, 2 * messages.size),
        name="join",
    )(messages)


def project_kernel(left_ref, weight_ref, out_ref):
    count, share, depth = left_ref.shape
    left = left_ref[...].astype(jnp.float32).reshape(count * share, depth).astype(jnp.bfloat16)
    result = jnp.dot(left, weight_ref[...], preferred_element_type=jnp.float32)
    prompts, samples, _ = out_ref.shape
    for n in range(prompts):
        out_ref[n] = result[n * samples : (n + 1) * samples].astype(out_ref.dtype)


def project(left, weight, samples):
    count, share, depth = left.shape
    prompts = count * share // samples
    width = weight.shape[1]
    tile = min(256, width)
    return pl.pallas_call(
        project_kernel,
        grid=(width // tile,),
        out_shape=jax.ShapeDtypeStruct((prompts, samples, width), jnp.bfloat16),
        in_specs=[
            pl.BlockSpec(left.shape, lambda n: (0, 0, 0)),
            pl.BlockSpec((depth, tile), lambda n: (0, n)),
        ],
        out_specs=pl.BlockSpec((prompts, samples, tile), lambda n: (0, 0, n)),
        compiler_params=limit(16),
        cost_estimate=cost(2 * left.size * width, 2 * depth * width),
        name="project",
    )(left, weight)


def body(prompt_key_values, queries, routing, lengths, out_weight):
    section_count = lax.axis_size("sec")
    tp_count = lax.axis_size("tp")
    slot_count, samples, query_width = queries.shape[1:]
    heads = query_width // HEAD_SIZE // KEY_VALUE_HEADS
    routing = routing.reshape(-1)
    own_queries = scatter(
        queries.reshape(section_count, CAP, samples, KEY_VALUE_HEADS, heads, HEAD_SIZE), "sec"
    )

    packed = pack(routing, prompt_key_values, section_count)
    slots = [(n // CAP, n % CAP) for n in range(slot_count)]
    arrived = {
        (offset, order): swap(part, "sec", offset) if offset else part
        for (offset, order), part in zip(slots, packed)
    }

    messages = attend(routing, lengths, own_queries, packed, tp_count)
    shares = scatter(join(scatter(messages, "tp"), samples), "tp")
    if shares.ndim == 4:
        attended = shares.reshape(REQ_GRP, KEY_VALUE_HEADS, samples, -1).transpose(0, 2, 1, 3)
        attended = attended.reshape(REQ_GRP * samples, query_width)
        layer_out = jnp.dot(attended, out_weight, preferred_element_type=jnp.float32)
        layer_out = layer_out.astype(jnp.bfloat16).reshape(REQ_GRP, samples, -1)
    else:
        layer_out = project(shares, out_weight, samples)

    whole = None
    for stage in (
        [slot for slot in slots if slot[0] < 2],
        [slot for slot in slots if slot[0] >= 2 and slot[1] == 0],
        [slot for slot in slots if slot[0] >= 2 and slot[1] == 1],
    ):
        whole = place(whole, [arrived[slot] for slot in stage], stage, slot_count)
    return (layer_out, whole)


def solution(mesh):
    placed = (
        P(("rep", "sec"), None, "tp", None),
        P(("rep", "sec"), None, None, None),
        P("rep", None),
        P("rep"),
        P(None, "tp"),
    )
    return jax.shard_map(
        body,
        mesh=mesh,
        in_specs=placed,
        out_specs=(P(("rep", "sec"), None, "tp"), P(("rep", "sec"), None, None, "tp", None)),
        check_vma=False,
    )
```

time: 171 us -> 98.5 us (0.58)
  waiting for transfers between devices: 72.6 us -> 36.5 us
  Pallas kernels: 0 us -> 25 us
  blocking collectives: 27.9 us -> 9.71 us
  between operations: 14.2 us -> 0.77 us
  other arithmetic: 13 us -> 0 us
  matrix products: 11.7 us -> 0 us
  local copies, waits for them, and re-layouts: 22.6 us -> 13.6 us
  starting transfers between devices: 8.36 us -> 12.3 us
    all_to_all x2, waiting for transfers between devices: 52.8 us -> 5.63 us  [scatter(): return lax.all_to_all(value, axis, split_axis=0, concat_axis=0, tiled=True)]
    ppermute x0 -> x6, waiting for transfers between devices: none -> 30.8 us  [swap(): return lax.ppermute(value, axis, [(i, i ^ offset) for i in range(count)])]
    all_gather x2 -> x0, blocking collectives: 27.9 us -> none  [combined_all(): everything = jax.tree.map(lambda part: lax.all_gather(part, axis), value)]
    pallas_call x0 -> x7, Pallas kernels: none -> 25 us  [the longest x1 9.95 us: attend(): pl.pallas_call(functools.partial(attend_kernel, section_count), out_shape...]
    all_gather x1 -> x0, waiting for transfers between devices: 19.7 us -> none  [combined_all(): everything = jax.tree.map(lambda part: lax.all_gather(part, axis), value)]
    dot_general x3 -> x0, matrix products: 11.7 us -> none  [the longest x1 8.78 us: body(): jnp.dot(attended, out_weight, preferred_element_type=jnp.float32)]
    all_to_all x0 -> x1, blocking collectives: none -> 9.71 us  [scatter(): return lax.all_to_all(value, axis, split_axis=0, concat_axis=0, tiled=True)]
    slice x3 -> x0, local copies, waits for them, and re-layouts: 9.15 us -> none  [the longest x2 6.3 us: body(): arrived_cache[:, 0]]
  transfers between devices with their start and end apart: 3 -> 8, of which waited for: 3 -> 4; matrix products, arithmetic and copies ran while one was open for 1% -> 1% of each run, Pallas kernels for 0% -> 17%
where the time goes in v2:
time: 98.5 us; the launch traced here: 97.9 us
  waiting for transfers between devices  36.5 us (37%)
  Pallas kernels  25 us (25%)
  local copies, waits for them, and re-layouts  13.6 us (14%)
  starting transfers between devices  12.3 us (12%)
  blocking collectives  9.71 us (10%)
    ppermute x6, waiting for transfers between devices, swap(): return lax.ppermute(value, axis, [(i, i ^ offset) for i in range(count)])  30.8 us
    unnamed x24, local copies, waits for them, and re-layouts  12.3 us
    pallas_call x1, Pallas kernels, attend(): pl.pallas_call(functools.partial(attend_kernel, section_count), out_shape...  9.95 us
    all_to_all x1, blocking collectives, scatter(): return lax.all_to_all(value, axis, split_axis=0, concat_axis=0, tiled=True)  9.71 us
    all_to_all x2, starting transfers between devices, scatter(): return lax.all_to_all(value, axis, split_axis=0, concat_axis=0, tiled=True)  8.27 us
    pallas_call x1, Pallas kernels, project(): pl.pallas_call(project_kernel, grid=(width // tile,), out_shape=jax.Shape...  6.85 us
    all_to_all x2, waiting for transfers between devices, scatter(): return lax.all_to_all(value, axis, split_axis=0, concat_axis=0, tiled=True)  5.63 us
    pallas_call x3, Pallas kernels, place(): pl.pallas_call(functools.partial(place_kernel, slots), out_shape=jax.Shap...  5.39 us
  transfers between devices with their start and end apart: 8, of which 4 were waited for; matrix products, arithmetic and copies ran while one was open for 1% of the time, Pallas kernels for 17%

profile of v2, /device:TPU:0, one launch (start us, length us, event | category | flops | bytes accessed | tf_op | source)
XLA Modules:
  0.0 97.9 jit_solution(5878013113767699414)
XLA Ops:
  0.7 2.2 %copy-done.1 = bf16[8,2,256,512]{3,2,1,0:T(8,128)(2,1)S(1)} copy-done((bf16[8,2,256,512]{3,2,1,0:T(8,128)(2,1)S(1)}, bf16[8,2,256,512]{3,2,1,0:T(8,128)(2,1)}, u32[]{:S(2)}) %copy-start.1) | copy-done | bytes 4194328
  2.9 0.7 copy-done.9
  3.5 1.8 %pack_cache.1 = (bf16[1,2,256,512]{3,2,1,0:T(8,128)(2,1)S(1)}, bf16[1,2,256,512]{3,2,1,0:T(8,128)(2,1)S(1)}, bf16[1,2,256,512]{3,2,1,0:T(8,128)(2,1)}, bf16[1,2,...) custom-call(s32[32]{0:T(128)S(1)} %bitcast.1, ...), custom_call_target="tpu_custom_call" | custom-call | bytes 8388608 | tf_op jit(solution)/shard_map/pack_cache/pallas_call | solution.py:85
  5.3 0.8 copy-done.5
  6.1 0.8 copy-done.7
  6.9 0.5 collective-permute-start
  7.4 1.3 %reshape.11 = bf16[4,2,4,4,8,128]{5,4,3,2,1,0:T(8,128)(2,1)S(1)} reshape(bf16[1,8,4,4096]{3,2,1,0:T(4,128)(2,1)} %param.6) | data formatting | bytes 524288 | tf_op jit(solution)/shard_map/reshape | solution.py:312
  8.7 9.7 %all_to_all.15.query_ref = bf16[4,2,4,4,8,128]{5,4,3,2,1,0:T(8,128)(2,1)S(1)} all-to-all(bf16[4,2,4,4,8,128]{5,4,3,2,1,0:T(8,128)(2,1)S(1)} %reshape.11), channel_id=1, replica_groups=mesh['rep'=2,'tp'=4,'sec'=4] {'sec'}, dimensions={0} | all-to-all | bytes 524288 | tf_op jit(solution)/shard_map/all_to_all | solution.py:35
  18.4 1.0 %copy-done.6 = bf16[1,2,256,512]{3,2,1,0:T(8,128)(2,1)S(1)} copy-done((bf16[1,2,256,512]{3,2,1,0:T(8,128)(2,1)S(1)}, bf16[1,2,256,512]{3,2,1,0:T(8,128)(2,1)}, u32[]{:S(2)}) %copy-start.6) | copy-done | bytes 524312
  19.4 1.0 %copy-done.8 = bf16[1,2,256,512]{3,2,1,0:T(8,128)(2,1)S(1)} copy-done((bf16[1,2,256,512]{3,2,1,0:T(8,128)(2,1)S(1)}, bf16[1,2,256,512]{3,2,1,0:T(8,128)(2,1)}, u32[]{:S(2)}) %copy-start.8) | copy-done | bytes 524312
  20.5 9.9 %attend.1 = bf16[4,9,32,128]{3,2,1,0:T(8,128)(2,1)} custom-call(s32[32]{0:T(128)S(1)} %bitcast.2, s32[32]{0:T(128)S(1)} %copy-done.11, bf16[4,2,4,4,8,128]{5,4,3,2,1,0:T(8,128)(2,1)S(1)} %all_to_all.15.query_ref, bf16[1,2,256,512]{3,2,1,0:T(8,128)(2,1)S(1)} %get-tuple-element.10.refs_0_, bf16[1,2,256,512]{3,2,1,0:T(8,128)(2,1)S(1)} %get-tuple-element.11.refs_1_, ...), custom_call_target="tpu_custom_call" | custom-call | flops 134217728 | bytes 4194304 | tf_op jit(solution)/shard_map/attend/pallas_call | solution.py:207
  30.4 4.9 %all-to-all-start.1 = ((bf16[4,9,32,128]{3,2,1,0:T(8,128)(2,1)}), bf16[4,9,32,128]{3,2,1,0:T(8,128)(2,1)S(1)}, u32[]{:S(2)}, u32[]{:S(2)}) async-start(bf16[4,9,32,128]{3,2,1,0:T(8,128)(2,1)} %attend.1), calls=%async_computation.1 | async-start | bytes 589824 | tf_op jit(solution)/shard_map/all_to_all | solution.py:35
  35.3 0.0 collective-permute-start.1
  35.3 0.4 collective-permute-start.2
  35.7 1.4 %collective-permute-start.3 = (bf16[1,2,256,512]{3,2,1,0:T(8,128)(2,1)}, bf16[1,2,256,512]{3,2,1,0:T(8,128)(2,1)S(1)}, u32[]{:S(2)}, u32[]{:S(2)}) collective-permute-start(bf16[1,2,256,512]{3,2,1,0:T(8,128)(2,1)} %copy-done.4), channel_id=1, source_target_pairs={{0,3},{1,2},{2,1},{3,0},{4,7},{5,6},{6,5},{7,4},{8,11},{9,10},{10,... | collective-permute-start | bytes 1572872 | tf_op jit(solution)/shard_map/ppermute | solution.py:31
  37.2 0.4 collective-permute-start.4
  37.5 0.0 collective-permute-done.refs_2_
  37.5 1.3 %collective-permute-start.5 = (bf16[1,2,256,512]{3,2,1,0:T(8,128)(2,1)}, bf16[1,2,256,512]{3,2,1,0:T(8,128)(2,1)}, u32[]{:S(2)}, u32[]{:S(2)}) collective-permute-start(bf16[1,2,256,512]{3,2,1,0:T(8,128)(2,1)} %copy-done.2), channel_id=1, source_target_pairs={{0,3},{1,2},{2,1},{3,0},{4,7},{5,6},{6,5},{7,4},{8,11},{9,10},{10,... | collective-permute-start | bytes 1572872 | tf_op jit(solution)/shard_map/ppermute | solution.py:31
  38.9 5.6 %all-to-all-done.1.message_ref = bf16[4,9,32,128]{3,2,1,0:T(8,128)(2,1)S(1)} async-done(((bf16[4,9,32,128]{3,2,1,0:T(8,128)(2,1)}), bf16[4,9,32,128]{3,2,1,0:T(8,128)(2,1)S(1)}, u32[]{:S(2)}, u32[]{:S(2)}) %all-to-all-start.1) | async-done | bytes 294944 | tf_op jit(solution)/shard_map/all_to_all | solution.py:35
  44.5 1.1 %join.1 = bf16[4,8,4096]{2,1,0:T(8,128)(2,1)} custom-call(bf16[4,9,32,128]{3,2,1,0:T(8,128)(2,1)S(1)} %all-to-all-done.1.message_ref), custom_call_target="tpu_custom_call" | custom-call | flops 589824 | bytes 294912 | tf_op jit(solution)/shard_map/join/pallas_call | solution.py:261
  45.6 3.4 %all-to-all-start.2 = ((bf16[4,8,4096]{2,1,0:T(8,128)(2,1)}), bf16[4,8,4096]{2,1,0:T(8,128)(2,1)S(1)}, u32[]{:S(2)}, u32[]{:S(2)}) async-start(bf16[4,8,4096]{2,1,0:T(8,128)(2,1)} %join.1), calls=%async_computation.2 | async-start | bytes 524288 | tf_op jit(solution)/shard_map/all_to_all | solution.py:35
  49.0 0.0 collective-permute-done.1.refs_3_
  49.0 2.4 %place_cache.3.refs_0_ = bf16[1,8,2,256,512]{4,3,2,1,0:T(8,128)(2,1)} custom-call(bf16[1,2,256,512]{3,2,1,0:T(8,128)(2,1)S(1)} %get-tuple-element.10.refs_0_, bf16[1,2,256,512]{3,2,1,0:T(8,128)(2,1)S(1)} %get-tuple-element.11.refs_1_, bf16[1,2,256,512]{3,2,1,0:T(8,128)(2,1)S(1)} %collective-permute-done.refs_2_, ...), custom_call_target="tpu_custom_call" | custom-call | bytes 4194304 | tf_op jit(solution)/shard_map/place_cache/pallas_call | solution.py:118
  51.4 9.2 %collective-permute-done.3.refs_2_ = bf16[1,2,256,512]{3,2,1,0:T(8,128)(2,1)S(1)} collective-permute-done((bf16[1,2,256,512]{3,2,1,0:T(8,128)(2,1)}, bf16[1,2,256,512]{3,2,1,0:T(8,128)(2,1)S(1)}, u32[]{:S(2)}, u32[]{:S(2)}) %collective-permute-start.3) | collective-permute-done | bytes 524320 | tf_op jit(solution)/shard_map/ppermute | solution.py:31
  60.6 1.0 %place_cache.4.refs_0_ = bf16[1,8,2,256,512]{4,3,2,1,0:T(8,128)(2,1)} custom-call(bf16[1,8,2,256,512]{4,3,2,1,0:T(8,128)(2,1)} %place_cache.3.refs_0_, bf16[1,2,256,512]{3,2,1,0:T(8,128)(2,1)S(1)} %collective-permute-done.2.refs_1_, bf16[1,2,256,512]{3,2,1,0:T(8,128)(2,1)S(1)} %collective-permute-done.3.refs_2_), custom_call_target="tpu_custom_call", output_to_operand_aliasing={{}: (0, {})} | custom-call | bytes 2097152 | tf_op jit(solution)/shard_map/place_cache/pallas_call | solution.py:118
  61.6 11.2 %collective-permute-done.4.refs_1_ = bf16[1,2,256,512]{3,2,1,0:T(8,128)(2,1)S(1)} collective-permute-done((bf16[1,2,256,512]{3,2,1,0:T(8,128)(2,1)}, bf16[1,2,256,512]{3,2,1,0:T(8,128)(2,1)S(1)}, u32[]{:S(2)}, u32[]{:S(2)}) %collective-permute-start.4) | collective-permute-done | bytes 524320 | tf_op jit(solution)/shard_map/ppermute | solution.py:31
  72.8 10.4 %collective-permute-done.5.refs_2_ = bf16[1,2,256,512]{3,2,1,0:T(8,128)(2,1)} collective-permute-done((bf16[1,2,256,512]{3,2,1,0:T(8,128)(2,1)}, bf16[1,2,256,512]{3,2,1,0:T(8,128)(2,1)}, u32[]{:S(2)}, u32[]{:S(2)}) %collective-permute-start.5) | collective-permute-done | bytes 524320 | tf_op jit(solution)/shard_map/ppermute | solution.py:31
  83.2 2.0 %place_cache.5 = bf16[1,8,2,256,512]{4,3,2,1,0:T(8,128)(2,1)} custom-call(bf16[1,8,2,256,512]{4,3,2,1,0:T(8,128)(2,1)} %place_cache.4.refs_0_, bf16[1,2,256,512]{3,2,1,0:T(8,128)(2,1)S(1)} %collective-permute-done.4.refs_1_, bf16[1,2,256,512]{3,2,1,0:T(8,128)(2,1)} %collective-permute-done.5.refs_2_), custom_call_target="tpu_custom_call", output_to_operand_aliasing={{}: (0, {})} | custom-call | bytes 2097152 | tf_op jit(solution)/shard_map/place_cache/pallas_call | solution.py:118
  85.3 0.0 all-to-all-done.2.left_ref
  85.3 0.0 copy-start
  85.3 5.8 %copy-done = bf16[4096,2048]{1,0:T(8,128)(2,1)S(1)} copy-done((bf16[4096,2048]{1,0:T(8,128)(2,1)S(1)}, bf16[4096,2048]{1,0:T(8,128)(2,1)}, u32[]{:S(2)}) %copy-start) | copy-done | bytes 16777240
  91.0 6.9 %project.1 = bf16[8,4,2048]{2,1,0:T(4,128)(2,1)} custom-call(bf16[4,8,4096]{2,1,0:T(8,128)(2,1)S(1)} %all-to-all-done.2.left_ref, bf16[4096,2048]{1,0:T(8,128)(2,1)S(1)} %copy-done), custom_call_target="tpu_custom_call" | custom-call | flops 536870912 | bytes 16777216 | tf_op jit(solution)/shard_map/project/pallas_call | solution.py:290
  (17 shorter events, 0.0 us)
Async XLA Ops:
  0.6 17.8 %copy-start.10 = (s32[32,1]{0,1:T(1,128)S(1)}, s32[32,1]{0,1:T(1,128)}, u32[]{:S(2)}) copy-start(s32[32,1]{0,1:T(1,128)} %param.7) | copy-start | bytes 388
  0.6 17.8 %copy-start.11 = (s32[32]{0:T(128)S(1)}, s32[32]{0:T(128)}, u32[]{:S(2)}) copy-start(s32[32]{0:T(128)} %lengths_ref.1) | copy-start | bytes 388
  0.6 2.2 %copy-start.1 = (bf16[8,2,256,512]{3,2,1,0:T(8,128)(2,1)S(1)}, bf16[8,2,256,512]{3,2,1,0:T(8,128)(2,1)}, u32[]{:S(2)}) copy-start(bf16[8,2,256,512]{3,2,1,0:T(8,128)(2,1)} %cache_ref.1) | copy-start | bytes 12582916
  2.9 0.7 copy-start.9
  5.3 0.8 copy-start.5
  6.1 0.8 copy-start.7
  6.9 28.4 %copy-start.3 = (bf16[1,2,256,512]{3,2,1,0:T(8,128)(2,1)}, bf16[1,2,256,512]{3,2,1,0:T(8,128)(2,1)S(1)}, u32[]{:S(2)}) copy-start(bf16[1,2,256,512]{3,2,1,0:T(8,128)(2,1)S(1)} %get-tuple-element.15.refs_5_) | copy-start | bytes 1572868
  6.9 28.4 %copy-start.4 = (bf16[1,2,256,512]{3,2,1,0:T(8,128)(2,1)}, bf16[1,2,256,512]{3,2,1,0:T(8,128)(2,1)S(1)}, u32[]{:S(2)}) copy-start(bf16[1,2,256,512]{3,2,1,0:T(8,128)(2,1)S(1)} %get-tuple-element.16.refs_6_) | copy-start | bytes 1572868
  6.9 28.8 %copy-start.2 = (bf16[1,2,256,512]{3,2,1,0:T(8,128)(2,1)}, bf16[1,2,256,512]{3,2,1,0:T(8,128)(2,1)S(1)}, u32[]{:S(2)}) copy-start(bf16[1,2,256,512]{3,2,1,0:T(8,128)(2,1)S(1)} %get-tuple-element.17.refs_7_) | copy-start | bytes 1572868
  6.9 30.6 %collective-permute-start = (bf16[1,2,256,512]{3,2,1,0:T(8,128)(2,1)}, bf16[1,2,256,512]{3,2,1,0:T(8,128)(2,1)S(1)}, u32[]{:S(2)}, u32[]{:S(2)}) collective-permute-start(bf16[1,2,256,512]{3,2,1,0:T(8,128)(2,1)} %get-tuple-element.12.refs_2_), channel_id=1, source_target_pairs={{0,1},{1,0},{2,3},{3,2},{4,5},{5,4},{6,7},{7,6},{8,9},{9,8},{10,11... | collective-permute-start | bytes 1572872 | tf_op jit(solution)/shard_map/ppermute | solution.py:31
  18.4 1.0 %copy-start.6 = (bf16[1,2,256,512]{3,2,1,0:T(8,128)(2,1)S(1)}, bf16[1,2,256,512]{3,2,1,0:T(8,128)(2,1)}, u32[]{:S(2)}) copy-start(bf16[1,2,256,512]{3,2,1,0:T(8,128)(2,1)} %copy-done.5) | copy-start | bytes 1572868
  19.4 1.0 %copy-start.8 = (bf16[1,2,256,512]{3,2,1,0:T(8,128)(2,1)S(1)}, bf16[1,2,256,512]{3,2,1,0:T(8,128)(2,1)}, u32[]{:S(2)}) copy-start(bf16[1,2,256,512]{3,2,1,0:T(8,128)(2,1)} %copy-done.7) | copy-start | bytes 1572868
  30.4 14.1 %all-to-all-start.1 = ((bf16[4,9,32,128]{3,2,1,0:T(8,128)(2,1)}), bf16[4,9,32,128]{3,2,1,0:T(8,128)(2,1)S(1)}, u32[]{:S(2)}, u32[]{:S(2)}) async-start(bf16[4,9,32,128]{3,2,1,0:T(8,128)(2,1)} %attend.1), calls=%async_computation.1 | async-start | bytes 589824 | tf_op jit(solution)/shard_map/all_to_all | solution.py:35
  35.3 13.7 %collective-permute-start.1 = (bf16[1,2,256,512]{3,2,1,0:T(8,128)(2,1)}, bf16[1,2,256,512]{3,2,1,0:T(8,128)(2,1)}, u32[]{:S(2)}, u32[]{:S(2)}) collective-permute-start(bf16[1,2,256,512]{3,2,1,0:T(8,128)(2,1)} %copy-done.7), channel_id=1, source_target_pairs={{0,1},{1,0},{2,3},{3,2},{4,5},{5,4},{6,7},{7,6},{8,9},{9,8},{10,11... | collective-permute-start | bytes 1572872 | tf_op jit(solution)/shard_map/ppermute | solution.py:31
  35.3 16.1 %collective-permute-start.2 = (bf16[1,2,256,512]{3,2,1,0:T(8,128)(2,1)}, bf16[1,2,256,512]{3,2,1,0:T(8,128)(2,1)S(1)}, u32[]{:S(2)}, u32[]{:S(2)}) collective-permute-start(bf16[1,2,256,512]{3,2,1,0:T(8,128)(2,1)} %copy-done.5), channel_id=1, source_target_pairs={{0,2},{1,3},{2,0},{3,1},{4,6},{5,7},{6,4},{7,5},{8,10},{9,11},{10,... | collective-permute-start | bytes 1572872 | tf_op jit(solution)/shard_map/ppermute | solution.py:31
  35.7 24.9 %collective-permute-start.3 = (bf16[1,2,256,512]{3,2,1,0:T(8,128)(2,1)}, bf16[1,2,256,512]{3,2,1,0:T(8,128)(2,1)S(1)}, u32[]{:S(2)}, u32[]{:S(2)}) collective-permute-start(bf16[1,2,256,512]{3,2,1,0:T(8,128)(2,1)} %copy-done.4), channel_id=1, source_target_pairs={{0,3},{1,2},{2,1},{3,0},{4,7},{5,6},{6,5},{7,4},{8,11},{9,10},{10,... | collective-permute-start | bytes 1572872 | tf_op jit(solution)/shard_map/ppermute | solution.py:31
  37.2 35.6 %collective-permute-start.4 = (bf16[1,2,256,512]{3,2,1,0:T(8,128)(2,1)}, bf16[1,2,256,512]{3,2,1,0:T(8,128)(2,1)S(1)}, u32[]{:S(2)}, u32[]{:S(2)}) collective-permute-start(bf16[1,2,256,512]{3,2,1,0:T(8,128)(2,1)} %copy-done.3), channel_id=1, source_target_pairs={{0,2},{1,3},{2,0},{3,1},{4,6},{5,7},{6,4},{7,5},{8,10},{9,11},{10,... | collective-permute-start | bytes 1572872 | tf_op jit(solution)/shard_map/ppermute | solution.py:31
  37.5 45.7 %collective-permute-start.5 = (bf16[1,2,256,512]{3,2,1,0:T(8,128)(2,1)}, bf16[1,2,256,512]{3,2,1,0:T(8,128)(2,1)}, u32[]{:S(2)}, u32[]{:S(2)}) collective-permute-start(bf16[1,2,256,512]{3,2,1,0:T(8,128)(2,1)} %copy-done.2), channel_id=1, source_target_pairs={{0,3},{1,2},{2,1},{3,0},{4,7},{5,6},{6,5},{7,4},{8,11},{9,10},{10,... | collective-permute-start | bytes 1572872 | tf_op jit(solution)/shard_map/ppermute | solution.py:31
  45.6 39.7 %all-to-all-start.2 = ((bf16[4,8,4096]{2,1,0:T(8,128)(2,1)}), bf16[4,8,4096]{2,1,0:T(8,128)(2,1)S(1)}, u32[]{:S(2)}, u32[]{:S(2)}) async-start(bf16[4,8,4096]{2,1,0:T(8,128)(2,1)} %join.1), calls=%async_computation.2 | async-start | bytes 524288 | tf_op jit(solution)/shard_map/all_to_all | solution.py:35
  85.3 5.8 %copy-start = (bf16[4096,2048]{1,0:T(8,128)(2,1)S(1)}, bf16[4096,2048]{1,0:T(8,128)(2,1)}, u32[]{:S(2)}) copy-start(bf16[4096,2048]{1,0:T(8,128)(2,1)} %weight_ref.1) | copy-start | bytes 50331652

commit v3 on v2

v3 whole, which is shorter than its diff:
```python
import functools

import jax
import jax.numpy as jnp
from jax import lax
from jax.experimental import pallas as pl
from jax.experimental.pallas import tpu as pltpu
from jax.sharding import PartitionSpec as P

HEAD_SIZE = 128
KEY_VALUE_HEADS = 4
REQ_GRP = 8
CAP = 2
HIDDEN = -1e30
SPLIT_LIMIT = 8
PACK_LIMIT = 48
FETCH_LIMIT = 36

ANY = pl.BlockSpec(memory_space=pl.ANY)
HBM = pl.BlockSpec(memory_space=pltpu.HBM)
VMEM = pl.BlockSpec(memory_space=pltpu.VMEM)
SMEM = pl.BlockSpec(memory_space=pltpu.SMEM)


def limit(mebibytes):
    return pltpu.CompilerParams(vmem_limit_bytes=mebibytes << 20)


def cost(flops, bytes_accessed, transcendentals=0):
    return pl.CostEstimate(flops=flops, bytes_accessed=bytes_accessed, transcendentals=transcendentals)


def swap(value, axis, offset):
    if offset == 0:
        return value
    count = lax.axis_size(axis)
    return lax.ppermute(value, axis, [(i, i ^ offset) for i in range(count)])


def own_slots(routing_ref, section, used, source):
    for t in range(used.shape[0]):
        used[t] = 0
    for i in range(REQ_GRP):
        target = routing_ref[section * REQ_GRP + i]
        order = used[target]
        used[target] = order + 1
        source[target * CAP + order] = i


def split_kernel(section_count, query_ref, *refs):
    out_refs, sem = refs[:section_count], refs[section_count]
    section = lax.axis_index("sec")
    copies = []
    for offset in range(section_count):
        part = query_ref.at[0, pl.ds((section ^ offset) * CAP, CAP)]
        copies.append(pltpu.make_async_copy(part, out_refs[offset], sem.at[offset]))
        copies[-1].start()
    for copy in copies:
        copy.wait()


def split(queries, section_count):
    part = jax.ShapeDtypeStruct((CAP,) + queries.shape[2:], queries.dtype)
    return pl.pallas_call(
        functools.partial(split_kernel, section_count),
        out_shape=[part] * section_count,
        in_specs=[HBM],
        out_specs=[VMEM] * section_count,
        scratch_shapes=[pltpu.SemaphoreType.DMA((section_count,))],
        compiler_params=limit(SPLIT_LIMIT),
        cost_estimate=cost(0, 4 * queries.size),
        name="split",
    )(queries)


def pack_kernel(section_count, routing_ref, cache_ref, *refs):
    cache_out, (source, used, sem) = refs[-3 - section_count : -3], refs[-3:]
    section = lax.axis_index("sec")
    full = section_count * CAP == REQ_GRP
    own_slots(routing_ref, section, used, source)
    slots = [(offset, order) for offset in reversed(range(section_count)) for order in range(CAP)]

    def copy(offset, order, row):
        return pltpu.make_async_copy(
            cache_ref.at[row], cache_out[offset].at[order], sem.at[offset * CAP + order]
        )

    for offset, order in slots:
        target = section ^ offset
        if full:
            copy(offset, order, source[target * CAP + order]).start()
        else:

            @pl.when(order < used[target])
            def _():
                copy(offset, order, source[target * CAP + order]).start()

            @pl.when(order >= used[target])
            def _():
                cache_out[offset][order] = jnp.zeros_like(cache_out[offset][order])

    for offset, order in slots:
        if full:
            copy(offset, order, 0).wait()
        else:

            @pl.when(order < used[section ^ offset])
            def _():
                copy(offset, order, 0).wait()


def pack(routing, cache, others, section_count):
    slots = section_count * CAP
    cache_part = jax.ShapeDtypeStruct((CAP,) + cache.shape[1:], cache.dtype)
    return pl.pallas_call(
        functools.partial(pack_kernel, section_count),
        out_shape=[cache_part] * section_count,
        in_specs=[SMEM, HBM] + [ANY] * len(others),
        out_specs=[VMEM] * section_count,
        scratch_shapes=[
            pltpu.SMEM((slots,), jnp.int32),
            pltpu.SMEM((section_count,), jnp.int32),
            pltpu.SemaphoreType.DMA((slots,)),
        ],
        compiler_params=limit(PACK_LIMIT),
        cost_estimate=cost(0, 4 * cache.size),
        name="pack",
    )(routing, cache, *others)


def gate_kernel(*refs):
    pass


def gate(values, others):
    count = len(values)
    return pl.pallas_call(
        gate_kernel,
        out_shape=[jax.ShapeDtypeStruct(value.shape, value.dtype) for value in values],
        in_specs=[ANY] * (count + len(others)),
        out_specs=[ANY] * count,
        input_output_aliases={n: n for n in range(count)},
        compiler_params=limit(1),
        cost_estimate=cost(0, 0),
        name="gate",
    )(*values, *others)


def place_kernel(offsets, *refs):
    count = len(offsets)
    part_refs, out_ref, sem = refs[-2 - count : -2], refs[-2], refs[-1]
    section = lax.axis_index("sec")
    copies = []
    for n, offset in enumerate(offsets):
        for order in range(CAP):
            slot = out_ref.at[0, (section ^ offset) * CAP + order]
            copy = pltpu.make_async_copy(part_refs[n].at[order], slot, sem.at[n * CAP + order])
            copy.start()
            copies.append(copy)
    for copy in copies:
        copy.wait()


def place(given, parts, offsets, slot_count):
    part = parts[0]
    return pl.pallas_call(
        functools.partial(place_kernel, offsets),
        out_shape=jax.ShapeDtypeStruct((1, slot_count) + part.shape[1:], part.dtype),
        in_specs=[HBM] * len(given) + [VMEM] * len(parts),
        out_specs=HBM,
        scratch_shapes=[pltpu.SemaphoreType.DMA((len(parts) * CAP,))],
        input_output_aliases={0: 0} if given else {},
        compiler_params=limit(8),
        cost_estimate=cost(0, 4 * len(parts) * part.size),
        name="place",
    )(*given, *parts)


def attend_kernel(section_count, tp_count, routing_ref, lengths_ref, *refs):
    cache_refs, query_refs = refs[:section_count], refs[section_count : 2 * section_count]
    message_refs = refs[-5 - tp_count : -5]
    source, used, messages, stats, stacked = refs[-5:]
    section = lax.axis_index("sec")
    tp_index = lax.axis_index("tp")
    local = cache_refs[0].shape[2]
    groups, rows, _ = messages.shape[1:]
    span = KEY_VALUE_HEADS * rows
    prompts = max(1, groups // KEY_VALUE_HEADS)
    full = section_count * CAP == REQ_GRP
    own_slots(routing_ref, section, used, source)
    position = lax.broadcasted_iota(jnp.int32, (local, span), 0) + tp_index * local
    owner = lax.broadcasted_iota(jnp.int32, (HEAD_SIZE, span), 1) // rows

    def prompt(offset, order):
        row = source[(section ^ offset) * CAP + order]
        visible = position < lengths_ref[section * REQ_GRP + row]
        values = query_refs[offset][order].astype(jnp.float32)
        samples = values.shape[0]
        slot = offset * CAP + order
        for head in range(span // samples):
            stacked[slot, head * samples : (head + 1) * samples] = values[:, head * HEAD_SIZE : (head + 1) * HEAD_SIZE]
        query = stacked[slot].T.astype(jnp.bfloat16)
        query = [jnp.where(owner == k, query, jnp.zeros_like(query)) for k in range(KEY_VALUE_HEADS)]
        score = jnp.dot(
            cache_refs[offset][order, 0], jnp.concatenate(query, axis=0), preferred_element_type=jnp.float32
        ) * HEAD_SIZE ** (-0.5)
        score = jnp.where(visible, score, HIDDEN)
        peak = jnp.max(score, axis=0, keepdims=True)
        weight = jnp.where(visible, jnp.exp(score - peak), 0.0)
        total = jnp.sum(weight, axis=0, keepdims=True)
        some = total > 0.0
        safe = jnp.where(some, total, 1.0)
        stats[pl.ds(row, 1)] = jnp.where(some, peak + jnp.log(safe), HIDDEN)
        weight = (weight * (1.0 / safe)).T.astype(jnp.bfloat16)
        for k in range(KEY_VALUE_HEADS):
            mixed = jnp.dot(
                weight[k * rows : (k + 1) * rows],
                cache_refs[offset][order, 1, :, k * HEAD_SIZE : (k + 1) * HEAD_SIZE],
                preferred_element_type=jnp.float32,
            )
            group = row * KEY_VALUE_HEADS + k
            messages[group // groups, group % groups] = mixed.astype(jnp.bfloat16)

    for offset in range(section_count):
        for order in range(CAP):
            if full:
                prompt(offset, order)
            else:
                pl.when(order < used[section ^ offset])(functools.partial(prompt, offset, order))

    level = stats[...]
    high = level.astype(jnp.bfloat16).astype(jnp.float32)
    rest = level - high
    middle = rest.astype(jnp.bfloat16).astype(jnp.float32)
    stats[...] = high
    stats_middle, stats_low = middle, rest - middle
    for offset in range(tp_count):
        device = tp_index ^ offset
        message_refs[offset][0:groups] = messages[device]
        message_refs[offset][groups] = jnp.zeros((rows, HEAD_SIZE), jnp.bfloat16)
    for part, values in enumerate((high, stats_middle, stats_low)):
        stats[...] = values
        for offset in range(tp_count):
            first = (tp_index ^ offset) * groups // KEY_VALUE_HEADS
            block = jnp.concatenate(
                [stats[pl.ds(first + n, 1)] for n in range(prompts)]
                + [jnp.zeros((16 - prompts, span), jnp.float32)],
                axis=0,
            )
            if part < 2:
                message_refs[offset][groups, part * 16 : part * 16 + 16] = block.astype(jnp.bfloat16)
            else:
                message_refs[offset][groups + 1] = jnp.concatenate([block, jnp.zeros_like(block)], axis=0).astype(
                    jnp.bfloat16
                )


def attend(routing, lengths, caches, queries, others, tp_count):
    section_count = len(caches)
    samples, width = queries[0].shape[1:]
    span = width // HEAD_SIZE * samples
    rows = span // KEY_VALUE_HEADS
    groups = REQ_GRP * KEY_VALUE_HEADS // tp_count
    multiplies = REQ_GRP * span * HEAD_SIZE * caches[0].shape[2]
    return pl.pallas_call(
        functools.partial(attend_kernel, section_count, tp_count),
        out_shape=[jax.ShapeDtypeStruct((groups + 2, rows, HEAD_SIZE), jnp.bfloat16)] * tp_count,
        in_specs=[SMEM, SMEM] + [VMEM] * (2 * section_count) + [ANY] * len(others),
        out_specs=[VMEM] * tp_count,
        scratch_shapes=[
            pltpu.SMEM((section_count * CAP,), jnp.int32),
            pltpu.SMEM((section_count,), jnp.int32),
            pltpu.VMEM((tp_count, groups, rows, HEAD_SIZE), jnp.bfloat16),
            pltpu.VMEM((REQ_GRP, span), jnp.float32),
            pltpu.VMEM((section_count * CAP, span, HEAD_SIZE), jnp.float32),
        ],
        compiler_params=limit(12),
        cost_estimate=cost(4 * multiplies, 2 * section_count * caches[0].size, multiplies // HEAD_SIZE),
        name="attend",
    )(routing, lengths, *caches, *queries, *others)


def join_kernel(count, samples, *refs):
    message_refs, (out_ref, scaling, flat) = refs[:count], refs[-3:]
    groups, rows, _ = message_refs[0].shape
    groups -= 2
    heads = rows // samples
    tp_index = lax.axis_index("tp")
    levels = []
    for ref in message_refs:
        upper = ref[groups].astype(jnp.float32)
        lower = ref[groups + 1].astype(jnp.float32)
        levels.append(upper[0:8] + upper[16:24] + lower[0:8])
    summit = functools.reduce(jnp.maximum, levels)
    scales = [jnp.exp(level - summit) for level in levels]
    total = functools.reduce(jnp.add, scales)
    for n, scale in enumerate(scales):
        scaling[n] = (scale / total).T
    for inner in range(groups):
        if groups % KEY_VALUE_HEADS:
            first = (tp_index * groups + inner) % KEY_VALUE_HEADS * rows
            part = pl.ds(pl.multiple_of(first, rows), rows)
        else:
            part = pl.ds(inner % KEY_VALUE_HEADS * rows, rows)
        prompt = inner // KEY_VALUE_HEADS
        terms = [
            ref[inner].astype(jnp.float32) * scaling[n, part, prompt : prompt + 1]
            for n, ref in enumerate(message_refs)
        ]
        joined = functools.reduce(jnp.add, terms)
        for head in range(heads):
            block = joined[head * samples : (head + 1) * samples]
            if len(flat.shape) == 2:
                row = prompt * samples
                column = (inner % KEY_VALUE_HEADS * heads + head) * HEAD_SIZE
                flat[row : row + samples, column : column + HEAD_SIZE] = block
            else:
                flat[inner, :, head * HEAD_SIZE : (head + 1) * HEAD_SIZE] = block
    out_ref[...] = flat[...].astype(jnp.bfloat16)


def join(messages, others, samples):
    groups, rows, _ = messages[0].shape
    groups -= 2
    width = rows // samples * HEAD_SIZE
    if groups % KEY_VALUE_HEADS == 0:
        shape = (groups // KEY_VALUE_HEADS * samples, KEY_VALUE_HEADS * width)
    else:
        shape = (groups, samples, width)
    count = len(messages)
    return pl.pallas_call(
        functools.partial(join_kernel, count, samples),
        out_shape=jax.ShapeDtypeStruct(shape, jnp.bfloat16),
        in_specs=[VMEM] * count + [ANY] * len(others),
        out_specs=VMEM,
        scratch_shapes=[
            pltpu.VMEM((count, KEY_VALUE_HEADS * rows, 8), jnp.float32),
            pltpu.VMEM(shape, jnp.float32),
        ],
        compiler_params=limit(8),
        cost_estimate=cost(4 * count * messages[0].size, 2 * count * messages[0].size),
        name="join",
    )(*messages, *others)


def fetch_kernel(weight_ref, *refs):
    out_ref, sem = refs[-2:]
    copies = []
    step = weight_ref.shape[0] // sem.shape[0]
    for n in range(sem.shape[0]):
        part = pl.ds(n * step, step)
        copies.append(pltpu.make_async_copy(weight_ref.at[part], out_ref.at[part], sem.at[n]))
        copies[-1].start()
    for copy in copies:
        copy.wait()


def fetch(weight, others):
    return pl.pallas_call(
        fetch_kernel,
        out_shape=jax.ShapeDtypeStruct(weight.shape, weight.dtype),
        in_specs=[HBM] + [ANY] * len(others),
        out_specs=VMEM,
        scratch_shapes=[pltpu.SemaphoreType.DMA((8,))],
        compiler_params=limit(FETCH_LIMIT),
        cost_estimate=cost(0, 4 * weight.size),
        name="fetch",
    )(weight, *others)


def project_kernel(count, tile, *refs):
    part_refs, weight_ref, out_ref = refs[:count], refs[count], refs[count + 1]
    tp_index = lax.axis_index("tp")
    prompts, samples, width = out_ref.shape
    share = prompts // count
    left = jnp.concatenate([ref[...].astype(jnp.float32) for ref in part_refs], axis=0).astype(jnp.bfloat16)
    for first in range(0, width, tile):
        result = jnp.dot(left, weight_ref[:, first : first + tile], preferred_element_type=jnp.float32)
        for offset in range(count):
            for n in range(share):
                row = (offset * share + n) * samples
                block = result[row : row + samples].astype(out_ref.dtype)
                out_ref[(tp_index ^ offset) * share + n, :, first : first + tile] = block


def project(parts, weight, samples):
    count = len(parts)
    depth, width = weight.shape
    total = count * parts[0].shape[0]
    return pl.pallas_call(
        functools.partial(project_kernel, count, min(256, width)),
        out_shape=jax.ShapeDtypeStruct((total // samples, samples, width), jnp.bfloat16),
        in_specs=[VMEM] * (count + 1),
        out_specs=VMEM,
        compiler_params=limit(24),
        cost_estimate=cost(2 * total * depth * width, 2 * depth * width),
        name="project",
    )(*parts, weight)


def body(prompt_key_values, queries, routing, lengths, out_weight):
    section_count = lax.axis_size("sec")
    tp_count = lax.axis_size("tp")
    slot_count, samples, query_width = queries.shape[1:]
    routing = routing.reshape(-1)

    query_parts = split(queries, section_count)
    own_queries = [swap(part, "sec", offset) for offset, part in enumerate(query_parts)]
    caches = pack(routing, prompt_key_values, query_parts[:1], section_count)
    caches = caches[:1] + gate(caches[1:], own_queries[1:])
    arrived = [swap(part, "sec", offset) for offset, part in enumerate(caches)]
    messages = attend(routing, lengths, caches, own_queries, arrived[1:2], tp_count)
    partials = [swap(part, "tp", offset) for offset, part in enumerate(messages)]
    held_weight = fetch(out_weight, messages[:1])
    share = join(partials, [held_weight], samples)
    shares = [swap(share, "tp", offset) for offset in range(tp_count)]
    if share.ndim == 3:
        attended = jnp.stack(shares)[jnp.arange(tp_count) ^ lax.axis_index("tp")]
        attended = attended.reshape(REQ_GRP, KEY_VALUE_HEADS, samples, -1).transpose(0, 2, 1, 3)
        attended = attended.reshape(REQ_GRP * samples, query_width)
        layer_out = jnp.dot(attended, out_weight, preferred_element_type=jnp.float32)
        layer_out = layer_out.astype(jnp.bfloat16).reshape(REQ_GRP, samples, -1)
    else:
        layer_out = project(shares, held_weight, samples)

    whole = place([], arrived[:2], [0, 1], slot_count)
    for offset in range(2, section_count):
        whole = place([whole, layer_out], arrived[offset : offset + 1], [offset], slot_count)
    return (layer_out, whole)


def solution(mesh):
    placed = (
        P(("rep", "sec"), None, "tp", None),
        P(("rep", "sec"), None, None, None),
        P("rep", None),
        P("rep"),
        P(None, "tp"),
    )
    return jax.shard_map(
        body,
        mesh=mesh,
        in_specs=placed,
        out_specs=(P(("rep", "sec"), None, "tp"), P(("rep", "sec"), None, None, "tp", None)),
        check_vma=False,
    )
```

time: 98.5 us -> 57.7 us (0.59)
  waiting for transfers between devices: 36.5 us -> 20.2 us
  local copies, waits for them, and re-layouts: 13.6 us -> 2.51 us
  blocking collectives: 9.71 us -> 0 us
  Pallas kernels: 25 us -> 20.2 us
  starting transfers between devices: 12.3 us -> 13.9 us
    ppermute x6 -> x12, waiting for transfers between devices: 30.8 us -> 20.2 us  [swap(): return lax.ppermute(value, axis, [(i, i ^ offset) for i in range(count)])]
    ppermute x6 -> x12, starting transfers between devices: 4.01 us -> 13.9 us  [swap(): return lax.ppermute(value, axis, [(i, i ^ offset) for i in range(count)])]
    unnamed x24 -> x8, local copies, waits for them, and re-layouts: 12.3 us -> 2.51 us
    all_to_all x1 -> x0, blocking collectives: 9.71 us -> none  [scatter(): return lax.all_to_all(value, axis, split_axis=0, concat_axis=0, tiled=True)]
    all_to_all x2 -> x0, starting transfers between devices: 8.27 us -> none  [scatter(): return lax.all_to_all(value, axis, split_axis=0, concat_axis=0, tiled=True)]
    pallas_call x6 -> x9, Pallas kernels: 23.3 us -> 17.4 us  [the longest x1 5.92 us: fetch(): pl.pallas_call(fetch_kernel, out_shape=jax.ShapeDtypeStruct(weight.shape,...]
    all_to_all x2 -> x0, waiting for transfers between devices: 5.63 us -> none  [scatter(): return lax.all_to_all(value, axis, split_axis=0, concat_axis=0, tiled=True)]
    reshape x1 -> x0, local copies, waits for them, and re-layouts: 1.32 us -> none  [body(): queries.reshape(section_count, CAP, samples, KEY_VALUE_HEADS, heads, HEAD...]
  transfers between devices with their start and end apart: 8 -> 12, of which waited for: 4 -> 6; matrix products, arithmetic and copies ran while one was open for 1% -> 0% of each run, Pallas kernels for 17% -> 33%
where the time goes in v3:
time: 57.7 us; the launch traced here: 57.5 us
  Pallas kernels  20.2 us (35%)
  waiting for transfers between devices  20.2 us (35%)
  starting transfers between devices  13.9 us (24%)
  local copies, waits for them, and re-layouts  2.51 us (4%)
  between operations  0.74 us (1%)
    ppermute x12, waiting for transfers between devices, swap(): return lax.ppermute(value, axis, [(i, i ^ offset) for i in range(count)])  20.2 us
    ppermute x12, starting transfers between devices, swap(): return lax.ppermute(value, axis, [(i, i ^ offset) for i in range(count)])  13.9 us
    pallas_call x1, Pallas kernels, fetch(): pl.pallas_call(fetch_kernel, out_shape=jax.ShapeDtypeStruct(weight.shape,...  5.92 us
    pallas_call x1, Pallas kernels, attend(): pl.pallas_call(functools.partial(attend_kernel, section_count, tp_count),...  3.78 us
    pallas_call x1, Pallas kernels, project(): pl.pallas_call(functools.partial(project_kernel, count, min(256, width)),...  3.64 us
    pallas_call x3, Pallas kernels, place(): pl.pallas_call(functools.partial(place_kernel, offsets), out_shape=jax.Sh...  3.31 us
    pallas_call x1, Pallas kernels, pack(): pl.pallas_call(functools.partial(pack_kernel, section_count), out_shape=[...  2.81 us
    unnamed x8, local copies, waits for them, and re-layouts  2.51 us
  transfers between devices with their start and end apart: 12, of which 6 were waited for; matrix products, arithmetic and copies ran while one was open for 0% of the time, Pallas kernels for 33%

profile of v3, /device:TPU:0, one launch (start us, length us, event | category | flops | bytes accessed | tf_op | source)
XLA Modules:
  0.0 57.5 jit_solution(431132988198075759)
XLA Ops:
  0.6 0.9 %copy-done.1 = bf16[1,8,4,4096]{3,2,1,0:T(4,128)(2,1)S(1)} copy-done((bf16[1,8,4,4096]{3,2,1,0:T(4,128)(2,1)S(1)}, bf16[1,8,4,4096]{3,2,1,0:T(4,128)(2,1)}, u32[]{:S(2)}) %copy-start.1) | copy-done | bytes 262168
  1.6 0.4 split.1
  1.9 0.5 collective-permute-start
  2.5 2.6 %collective-permute-start.1 = (bf16[2,4,4096]{2,1,0:T(4,128)(2,1)S(1)}, bf16[2,4,4096]{2,1,0:T(4,128)(2,1)S(1)}, u32[]{:S(2)}, u32[]{:S(2)}) collective-permute-start(bf16[2,4,4096]{2,1,0:T(4,128)(2,1)S(1)} %get-tuple-element.23), channel_id=1, source_target_pairs={{0,2},{1,3},{2,0},{3,1},{4,6},{5,7},{6,4},{7,5},{8,10},{9,11},{10,... | collective-permute-start | bytes 196616 | tf_op jit(solution)/shard_map/ppermute | solution.py:37
  5.0 0.1 collective-permute-start.2
  5.1 0.7 %copy-done.2 = s32[32,1]{0,1:T(1,128)S(1)} copy-done((s32[32,1]{0,1:T(1,128)S(1)}, s32[32,1]{0,1:T(1,128)}, u32[]{:S(2)}) %copy-start.2) | copy-done | bytes 152
  5.8 2.8 %pack.1 = (bf16[2,2,256,512]{3,2,1,0:T(8,128)(2,1)S(1)}, bf16[2,2,256,512]{3,2,1,0:T(8,128)(2,1)S(1)}, bf16[2,2,256,512]{3,2,1,0:T(8,128)(2,1)S(1)}, bf16[2,2,256,512]{3,2,1,0:T(8,128)(2,1)S(1)}) custom-call(s32[32]{0:T(128)S(1)} %bitcast.1, bf16[8,2,256,512]{3,2,1,0:T(8,128)(2,1)} %cache_ref.1, bf16[2,4,4096]{2,1,0:T(4,128)(2,1)S(1)} %get-tuple-element.17.refs_0_.refs_4_), custom_call_target="tpu_custom_call" | custom-call | bytes 8388608 | tf_op jit(solution)/shard_map/pack/pallas_call | solution.py:115
  8.6 0.5 collective-permute-done.2.refs_5_.refs_7_
  9.1 0.2 collective-permute-start.3
  9.2 1.5 %collective-permute-start.10 = (bf16[2,2,256,512]{3,2,1,0:T(8,128)(2,1)S(1)}, bf16[2,2,256,512]{3,2,1,0:T(8,128)(2,1)S(1)}, u32[]{:S(2)}, u32[]{:S(2)}) collective-permute-start(bf16[2,2,256,512]{3,2,1,0:T(8,128)(2,1)S(1)} %get-tuple-element.26.refs_2_), channel_id=1, source_target_pairs={{0,2},{1,3},{2,0},{3,1},{4,6},{5,7},{6,4},{7,5},{8,10},{9,11},{10,... | collective-permute-start | bytes 3145736 | tf_op jit(solution)/shard_map/ppermute | solution.py:37
  10.8 0.2 collective-permute-start.11
  10.9 0.8 %collective-permute-done.3.refs_8_.refs_1_ = bf16[2,2,256,512]{3,2,1,0:T(8,128)(2,1)S(1)} collective-permute-done((bf16[2,2,256,512]{3,2,1,0:T(8,128)(2,1)S(1)}, bf16[2,2,256,512]{3,2,1,0:T(8,128)(2,1)S(1)}, u32[]{:S(2)}, u32[]{:S(2)}) %collective-permute-start.3) | collective-permute-done | bytes 1048608 | tf_op jit(solution)/shard_map/ppermute | solution.py:37
  11.7 3.8 %attend.1 = (bf16[10,32,128]{2,1,0:T(8,128)(2,1)S(1)}, bf16[10,32,128]{2,1,0:T(8,128)(2,1)S(1)}, bf16[10,32,128]{2,1,0:T(8,128)(2,1)S(1)}, bf16[10,32,128]{2,1,0:T(8,128)(2,1)S(1)}) custom-call(s32[32]{0:T(128)S(1)} %bitcast.2, s32[32]{0:T(128)S(1)} %copy-done.3, bf16[2,2,256,512]{3,2,1,0:T(8,128)(2,1)S(1)} %get-tuple-element.18.refs_0_, ...), custom_call_target="tpu_custom_call" | custom-call | flops 134217728 | bytes 4194304 | tf_op jit(solution)/shard_map/attend/pallas_call | solution.py:265
  15.5 1.6 %collective-permute-start.4 = (bf16[10,32,128]{2,1,0:T(8,128)(2,1)S(1)}, bf16[10,32,128]{2,1,0:T(8,128)(2,1)S(1)}, u32[]{:S(2)}, u32[]{:S(2)}) collective-permute-start(bf16[10,32,128]{2,1,0:T(8,128)(2,1)S(1)} %get-tuple-element.29), channel_id=1, source_target_pairs={{0,4},{4,0},{8,12},{12,8},{1,5},{5,1},{9,13},{13,9},{2,6},{6,2},{1... | collective-permute-start | bytes 245768 | tf_op jit(solution)/shard_map/ppermute | solution.py:37
  17.2 2.6 %collective-permute-start.5 = (bf16[10,32,128]{2,1,0:T(8,128)(2,1)S(1)}, bf16[10,32,128]{2,1,0:T(8,128)(2,1)S(1)}, u32[]{:S(2)}, u32[]{:S(2)}) collective-permute-start(bf16[10,32,128]{2,1,0:T(8,128)(2,1)S(1)} %get-tuple-element.30), channel_id=1, source_target_pairs={{0,8},{4,12},{8,0},{12,4},{1,9},{5,13},{9,1},{13,5},{2,10},{6,14},... | collective-permute-start | bytes 245768 | tf_op jit(solution)/shard_map/ppermute | solution.py:37
  19.8 0.2 collective-permute-start.6
  20.0 5.9 %fetch.1.refs_4_ = bf16[4096,2048]{1,0:T(8,128)(2,1)S(1)} custom-call(bf16[4096,2048]{1,0:T(8,128)(2,1)} %weight_ref.1, bf16[10,32,128]{2,1,0:T(8,128)(2,1)S(1)} %get-tuple-element.28.refs_0_), custom_call_target="tpu_custom_call" | custom-call | bytes 33554432 | tf_op jit(solution)/shard_map/fetch/pallas_call | solution.py:359
  25.9 0.0 collective-permute-done.4.refs_1_
  25.9 0.7 %collective-permute-done.5.refs_2_ = bf16[10,32,128]{2,1,0:T(8,128)(2,1)S(1)} collective-permute-done((bf16[10,32,128]{2,1,0:T(8,128)(2,1)S(1)}, bf16[10,32,128]{2,1,0:T(8,128)(2,1)S(1)}, u32[]{:S(2)}, u32[]{:S(2)}) %collective-permute-start.5) | collective-permute-done | bytes 81952 | tf_op jit(solution)/shard_map/ppermute | solution.py:37
  26.7 0.0 collective-permute-done.6.refs_3_
  26.7 0.4 join.1.refs_0_
  27.1 1.6 %collective-permute-start.7 = (bf16[8,4096]{1,0:T(8,128)(2,1)S(1)}, bf16[8,4096]{1,0:T(8,128)(2,1)S(1)}, u32[]{:S(2)}, u32[]{:S(2)}) collective-permute-start(bf16[8,4096]{1,0:T(8,128)(2,1)S(1)} %join.1.refs_0_), channel_id=1, source_target_pairs={{0,4},{4,0},{8,12},{12,8},{1,5},{5,1},{9,13},{13,9},{2,6},{6,2},{1... | collective-permute-start | bytes 196616 | tf_op jit(solution)/shard_map/ppermute | solution.py:37
  28.7 1.9 %collective-permute-start.8 = (bf16[8,4096]{1,0:T(8,128)(2,1)S(1)}, bf16[8,4096]{1,0:T(8,128)(2,1)S(1)}, u32[]{:S(2)}, u32[]{:S(2)}) collective-permute-start(bf16[8,4096]{1,0:T(8,128)(2,1)S(1)} %join.1.refs_0_), channel_id=1, source_target_pairs={{0,8},{4,12},{8,0},{12,4},{1,9},{5,13},{9,1},{13,5},{2,10},{6,14},... | collective-permute-start | bytes 196616 | tf_op jit(solution)/shard_map/ppermute | solution.py:37
  30.6 0.9 %collective-permute-start.9 = (bf16[8,4096]{1,0:T(8,128)(2,1)S(1)}, bf16[8,4096]{1,0:T(8,128)(2,1)S(1)}, u32[]{:S(2)}, u32[]{:S(2)}) collective-permute-start(bf16[8,4096]{1,0:T(8,128)(2,1)S(1)} %join.1.refs_0_), channel_id=1, source_target_pairs={{0,12},{4,8},{8,4},{12,0},{1,13},{5,9},{9,5},{13,1},{2,14},{6,10},... | collective-permute-start | bytes 196616 | tf_op jit(solution)/shard_map/ppermute | solution.py:37
  31.5 1.3 %place.3.refs_0_ = bf16[1,8,2,256,512]{4,3,2,1,0:T(8,128)(2,1)} custom-call(bf16[2,2,256,512]{3,2,1,0:T(8,128)(2,1)S(1)} %get-tuple-element.18.refs_0_, bf16[2,2,256,512]{3,2,1,0:T(8,128)(2,1)S(1)} %collective-permute-done.3.refs_8_.refs_1_), custom_call_target="tpu_custom_call" | custom-call | bytes 4194304 | tf_op jit(solution)/shard_map/place/pallas_call | solution.py:166
  32.9 2.6 %collective-permute-done.8.refs_2_ = bf16[8,4096]{1,0:T(8,128)(2,1)S(1)} collective-permute-done((bf16[8,4096]{1,0:T(8,128)(2,1)S(1)}, bf16[8,4096]{1,0:T(8,128)(2,1)S(1)}, u32[]{:S(2)}, u32[]{:S(2)}) %collective-permute-start.8) | collective-permute-done | bytes 65568 | tf_op jit(solution)/shard_map/ppermute | solution.py:37
  35.5 1.3 %collective-permute-done.9.refs_3_ = bf16[8,4096]{1,0:T(8,128)(2,1)S(1)} collective-permute-done((bf16[8,4096]{1,0:T(8,128)(2,1)S(1)}, bf16[8,4096]{1,0:T(8,128)(2,1)S(1)}, u32[]{:S(2)}, u32[]{:S(2)}) %collective-permute-start.9) | collective-permute-done | bytes 65568 | tf_op jit(solution)/shard_map/ppermute | solution.py:37
  36.8 3.6 %project.1.refs_1_ = bf16[8,4,2048]{2,1,0:T(4,128)(2,1)} custom-call(bf16[8,4096]{1,0:T(8,128)(2,1)S(1)} %join.1.refs_0_, bf16[8,4096]{1,0:T(8,128)(2,1)S(1)} %collective-permute-done.7.refs_1_, bf16[8,4096]{1,0:T(8,128)(2,1)S(1)} %collective-permute-done.8.refs_2_, bf16[8,4096]{1,0:T(8,128)(2,1)S(1)} %collective-permute-done.9.refs_3_, ...), custom_call_target="tpu_custom_call" | custom-call | flops 536870912 | bytes 16777216 | tf_op jit(solution)/shard_map/project/pallas_call | solution.py:390
  40.4 0.9 %copy-done = bf16[8,4,2048]{2,1,0:T(4,128)(2,1)S(1)} copy-done((bf16[8,4,2048]{2,1,0:T(4,128)(2,1)S(1)}, bf16[8,4,2048]{2,1,0:T(4,128)(2,1)}, u32[]{:S(2)}) %copy-start) | copy-done | bytes 131096
  41.3 1.0 %place.4.refs_0_ = bf16[1,8,2,256,512]{4,3,2,1,0:T(8,128)(2,1)} custom-call(bf16[1,8,2,256,512]{4,3,2,1,0:T(8,128)(2,1)} %place.3.refs_0_, bf16[8,4,2048]{2,1,0:T(4,128)(2,1)S(1)} %copy-done, bf16[2,2,256,512]{3,2,1,0:T(8,128)(2,1)S(1)} %collective-permute-done.10.refs_2_), custom_call_target="tpu_custom_call", output_to_operand_aliasing={{}: (0, {})} | custom-call | bytes 2097152 | tf_op jit(solution)/shard_map/place/pallas_call | solution.py:166
  42.3 14.3 %collective-permute-done.11.refs_2_ = bf16[2,2,256,512]{3,2,1,0:T(8,128)(2,1)S(1)} collective-permute-done((bf16[2,2,256,512]{3,2,1,0:T(8,128)(2,1)S(1)}, bf16[2,2,256,512]{3,2,1,0:T(8,128)(2,1)S(1)}, u32[]{:S(2)}, u32[]{:S(2)}) %collective-permute-start.11) | collective-permute-done | bytes 1048608 | tf_op jit(solution)/shard_map/ppermute | solution.py:37
  56.5 1.0 %place.5 = bf16[1,8,2,256,512]{4,3,2,1,0:T(8,128)(2,1)} custom-call(bf16[1,8,2,256,512]{4,3,2,1,0:T(8,128)(2,1)} %place.4.refs_0_, bf16[8,4,2048]{2,1,0:T(4,128)(2,1)S(1)} %copy-done, bf16[2,2,256,512]{3,2,1,0:T(8,128)(2,1)S(1)} %collective-permute-done.11.refs_2_), custom_call_target="tpu_custom_call", output_to_operand_aliasing={{}: (0, {})} | custom-call | bytes 2097152 | tf_op jit(solution)/shard_map/place/pallas_call | solution.py:166
  (10 shorter events, 0.0 us)
Async XLA Ops:
  0.6 1.0 %copy-start.1 = (bf16[1,8,4,4096]{3,2,1,0:T(4,128)(2,1)S(1)}, bf16[1,8,4,4096]{3,2,1,0:T(4,128)(2,1)}, u32[]{:S(2)}) copy-start(bf16[1,8,4,4096]{3,2,1,0:T(4,128)(2,1)} %query_ref.1) | copy-start | bytes 786436
  1.6 10.2 %copy-start.3 = (s32[32]{0:T(128)S(1)}, s32[32]{0:T(128)}, u32[]{:S(2)}) copy-start(s32[32]{0:T(128)} %lengths_ref.1) | copy-start | bytes 388
  1.9 6.6 %collective-permute-start = (bf16[2,4,4096]{2,1,0:T(4,128)(2,1)S(1)}, bf16[2,4,4096]{2,1,0:T(4,128)(2,1)S(1)}, u32[]{:S(2)}, u32[]{:S(2)}) collective-permute-start(bf16[2,4,4096]{2,1,0:T(4,128)(2,1)S(1)} %get-tuple-element.22), channel_id=1, source_target_pairs={{0,1},{1,0},{2,3},{3,2},{4,5},{5,4},{6,7},{7,6},{8,9},{9,8},{10,11... | collective-permute-start | bytes 196616 | tf_op jit(solution)/shard_map/ppermute | solution.py:37
  2.5 6.1 %collective-permute-start.1 = (bf16[2,4,4096]{2,1,0:T(4,128)(2,1)S(1)}, bf16[2,4,4096]{2,1,0:T(4,128)(2,1)S(1)}, u32[]{:S(2)}, u32[]{:S(2)}) collective-permute-start(bf16[2,4,4096]{2,1,0:T(4,128)(2,1)S(1)} %get-tuple-element.23), channel_id=1, source_target_pairs={{0,2},{1,3},{2,0},{3,1},{4,6},{5,7},{6,4},{7,5},{8,10},{9,11},{10,... | collective-permute-start | bytes 196616 | tf_op jit(solution)/shard_map/ppermute | solution.py:37
  5.0 4.0 %collective-permute-start.2 = (bf16[2,4,4096]{2,1,0:T(4,128)(2,1)S(1)}, bf16[2,4,4096]{2,1,0:T(4,128)(2,1)S(1)}, u32[]{:S(2)}, u32[]{:S(2)}) collective-permute-start(bf16[2,4,4096]{2,1,0:T(4,128)(2,1)S(1)} %get-tuple-element.24), channel_id=1, source_target_pairs={{0,3},{1,2},{2,1},{3,0},{4,7},{5,6},{6,5},{7,4},{8,11},{9,10},{10,... | collective-permute-start | bytes 196616 | tf_op jit(solution)/shard_map/ppermute | solution.py:37
  5.1 0.7 %copy-start.2 = (s32[32,1]{0,1:T(1,128)S(1)}, s32[32,1]{0,1:T(1,128)}, u32[]{:S(2)}) copy-start(s32[32,1]{0,1:T(1,128)} %param.7) | copy-start | bytes 388
  9.1 2.7 %collective-permute-start.3 = (bf16[2,2,256,512]{3,2,1,0:T(8,128)(2,1)S(1)}, bf16[2,2,256,512]{3,2,1,0:T(8,128)(2,1)S(1)}, u32[]{:S(2)}, u32[]{:S(2)}) collective-permute-start(bf16[2,2,256,512]{3,2,1,0:T(8,128)(2,1)S(1)} %get-tuple-element.25.refs_1_), channel_id=1, source_target_pairs={{0,1},{1,0},{2,3},{3,2},{4,5},{5,4},{6,7},{7,6},{8,9},{9,8},{10,11... | collective-permute-start | bytes 3145736 | tf_op jit(solution)/shard_map/ppermute | solution.py:37
  9.2 31.1 %collective-permute-start.10 = (bf16[2,2,256,512]{3,2,1,0:T(8,128)(2,1)S(1)}, bf16[2,2,256,512]{3,2,1,0:T(8,128)(2,1)S(1)}, u32[]{:S(2)}, u32[]{:S(2)}) collective-permute-start(bf16[2,2,256,512]{3,2,1,0:T(8,128)(2,1)S(1)} %get-tuple-element.26.refs_2_), channel_id=1, source_target_pairs={{0,2},{1,3},{2,0},{3,1},{4,6},{5,7},{6,4},{7,5},{8,10},{9,11},{10,... | collective-permute-start | bytes 3145736 | tf_op jit(solution)/shard_map/ppermute | solution.py:37
  10.8 45.8 %collective-permute-start.11 = (bf16[2,2,256,512]{3,2,1,0:T(8,128)(2,1)S(1)}, bf16[2,2,256,512]{3,2,1,0:T(8,128)(2,1)S(1)}, u32[]{:S(2)}, u32[]{:S(2)}) collective-permute-start(bf16[2,2,256,512]{3,2,1,0:T(8,128)(2,1)S(1)} %get-tuple-element.27.refs_3_), channel_id=1, source_target_pairs={{0,3},{1,2},{2,1},{3,0},{4,7},{5,6},{6,5},{7,4},{8,11},{9,10},{10,... | collective-permute-start | bytes 3145736 | tf_op jit(solution)/shard_map/ppermute | solution.py:37
  15.5 10.4 %collective-permute-start.4 = (bf16[10,32,128]{2,1,0:T(8,128)(2,1)S(1)}, bf16[10,32,128]{2,1,0:T(8,128)(2,1)S(1)}, u32[]{:S(2)}, u32[]{:S(2)}) collective-permute-start(bf16[10,32,128]{2,1,0:T(8,128)(2,1)S(1)} %get-tuple-element.29), channel_id=1, source_target_pairs={{0,4},{4,0},{8,12},{12,8},{1,5},{5,1},{9,13},{13,9},{2,6},{6,2},{1... | collective-permute-start | bytes 245768 | tf_op jit(solution)/shard_map/ppermute | solution.py:37
  17.2 9.5 %collective-permute-start.5 = (bf16[10,32,128]{2,1,0:T(8,128)(2,1)S(1)}, bf16[10,32,128]{2,1,0:T(8,128)(2,1)S(1)}, u32[]{:S(2)}, u32[]{:S(2)}) collective-permute-start(bf16[10,32,128]{2,1,0:T(8,128)(2,1)S(1)} %get-tuple-element.30), channel_id=1, source_target_pairs={{0,8},{4,12},{8,0},{12,4},{1,9},{5,13},{9,1},{13,5},{2,10},{6,14},... | collective-permute-start | bytes 245768 | tf_op jit(solution)/shard_map/ppermute | solution.py:37
  19.8 6.9 %collective-permute-start.6 = (bf16[10,32,128]{2,1,0:T(8,128)(2,1)S(1)}, bf16[10,32,128]{2,1,0:T(8,128)(2,1)S(1)}, u32[]{:S(2)}, u32[]{:S(2)}) collective-permute-start(bf16[10,32,128]{2,1,0:T(8,128)(2,1)S(1)} %get-tuple-element.31), channel_id=1, source_target_pairs={{0,12},{4,8},{8,4},{12,0},{1,13},{5,9},{9,5},{13,1},{2,14},{6,10},... | collective-permute-start | bytes 245768 | tf_op jit(solution)/shard_map/ppermute | solution.py:37
  27.1 5.8 %collective-permute-start.7 = (bf16[8,4096]{1,0:T(8,128)(2,1)S(1)}, bf16[8,4096]{1,0:T(8,128)(2,1)S(1)}, u32[]{:S(2)}, u32[]{:S(2)}) collective-permute-start(bf16[8,4096]{1,0:T(8,128)(2,1)S(1)} %join.1.refs_0_), channel_id=1, source_target_pairs={{0,4},{4,0},{8,12},{12,8},{1,5},{5,1},{9,13},{13,9},{2,6},{6,2},{1... | collective-permute-start | bytes 196616 | tf_op jit(solution)/shard_map/ppermute | solution.py:37
  28.7 6.8 %collective-permute-start.8 = (bf16[8,4096]{1,0:T(8,128)(2,1)S(1)}, bf16[8,4096]{1,0:T(8,128)(2,1)S(1)}, u32[]{:S(2)}, u32[]{:S(2)}) collective-permute-start(bf16[8,4096]{1,0:T(8,128)(2,1)S(1)} %join.1.refs_0_), channel_id=1, source_target_pairs={{0,8},{4,12},{8,0},{12,4},{1,9},{5,13},{9,1},{13,5},{2,10},{6,14},... | collective-permute-start | bytes 196616 | tf_op jit(solution)/shard_map/ppermute | solution.py:37
  30.6 6.2 %collective-permute-start.9 = (bf16[8,4096]{1,0:T(8,128)(2,1)S(1)}, bf16[8,4096]{1,0:T(8,128)(2,1)S(1)}, u32[]{:S(2)}, u32[]{:S(2)}) collective-permute-start(bf16[8,4096]{1,0:T(8,128)(2,1)S(1)} %join.1.refs_0_), channel_id=1, source_target_pairs={{0,12},{4,8},{8,4},{12,0},{1,13},{5,9},{9,5},{13,1},{2,14},{6,10},... | collective-permute-start | bytes 196616 | tf_op jit(solution)/shard_map/ppermute | solution.py:37
  40.4 0.9 %copy-start = (bf16[8,4,2048]{2,1,0:T(4,128)(2,1)S(1)}, bf16[8,4,2048]{2,1,0:T(4,128)(2,1)}, u32[]{:S(2)}) copy-start(bf16[8,4,2048]{2,1,0:T(4,128)(2,1)} %project.1.refs_1_) | copy-start | bytes 393220

commit v4 on v3

--- a/solution.py
+++ b/solution.py
@@ -12,9 +12,6 @@
 REQ_GRP = 8
 CAP = 2
 HIDDEN = -1e30
-SPLIT_LIMIT = 8
-PACK_LIMIT = 48
-FETCH_LIMIT = 36
 
 ANY = pl.BlockSpec(memory_space=pl.ANY)
 HBM = pl.BlockSpec(memory_space=pltpu.HBM)
@@ -47,137 +44,114 @@
         source[target * CAP + order] = i
 
 
-def split_kernel(section_count, query_ref, *refs):
-    out_refs, sem = refs[:section_count], refs[section_count]
-    section = lax.axis_index("sec")
-    copies = []
-    for offset in range(section_count):
-        part = query_ref.at[0, pl.ds((section ^ offset) * CAP, CAP)]
-        copies.append(pltpu.make_async_copy(part, out_refs[offset], sem.at[offset]))
-        copies[-1].start()
-    for copy in copies:
-        copy.wait()
-
-
-def split(queries, section_count):
-    part = jax.ShapeDtypeStruct((CAP,) + queries.shape[2:], queries.dtype)
-    return pl.pallas_call(
-        functools.partial(split_kernel, section_count),
-        out_shape=[part] * section_count,
-        in_specs=[HBM],
-        out_specs=[VMEM] * section_count,
-        scratch_shapes=[pltpu.SemaphoreType.DMA((section_count,))],
-        compiler_params=limit(SPLIT_LIMIT),
-        cost_estimate=cost(0, 4 * queries.size),
-        name="split",
-    )(queries)
-
-
-def pack_kernel(section_count, routing_ref, cache_ref, *refs):
-    cache_out, (source, used, sem) = refs[-3 - section_count : -3], refs[-3:]
+def pack_kernel(pieces, section_count, routing_ref, cache_ref, *refs):
+    refs, (source, used, sem, query_sem) = refs[:-4], refs[-4:]
+    query_ref, refs = (refs[0], refs[1:]) if len(refs) > len(pieces) else (None, refs)
+    cache_out, query_out = refs[: len(pieces)], refs[len(pieces) :]
     section = lax.axis_index("sec")
     full = section_count * CAP == REQ_GRP
+    query_copies = []
+    for offset, out_ref in enumerate(query_out):
+        part = query_ref.at[0, pl.ds((section ^ offset) * CAP, CAP)]
+        query_copies.append(pltpu.make_async_copy(part, out_ref, query_sem.at[offset]))
+        query_copies[-1].start()
     own_slots(routing_ref, section, used, source)
-    slots = [(offset, order) for offset in reversed(range(section_count)) for order in range(CAP)]
-
-    def copy(offset, order, row):
-        return pltpu.make_async_copy(
-            cache_ref.at[row], cache_out[offset].at[order], sem.at[offset * CAP + order]
-        )
-
-    for offset, order in slots:
+
+    def copy(n, spot, row):
+        offset, order, place = spot
+        return pltpu.make_async_copy(cache_ref.at[row], cache_out[n].at[place], sem.at[offset * CAP + order])
+
+    spots = [
+        (n, (offset, first + place, place))
+        for n, (offset, first, count) in enumerate(pieces)
+        for place in range(count)
+    ]
+    for n, spot in spots:
+        offset, order, place = spot
         target = section ^ offset
         if full:
-            copy(offset, order, source[target * CAP + order]).start()
+            copy(n, spot, source[target * CAP + order]).start()
         else:
 
             @pl.when(order < used[target])
             def _():
-                copy(offset, order, source[target * CAP + order]).start()
+                copy(n, spot, source[target * CAP + order]).start()
 
             @pl.when(order >= used[target])
             def _():
-                cache_out[offset][order] = jnp.zeros_like(cache_out[offset][order])
-
-    for offset, order in slots:
+                cache_out[n][place] = jnp.zeros_like(cache_out[n][place])
+
+    for n, spot in spots:
         if full:
-            copy(offset, order, 0).wait()
+            copy(n, spot, 0).wait()
         else:
 
-            @pl.when(order < used[section ^ offset])
+            @pl.when(spot[1] < used[section ^ spot[0]])
             def _():
-                copy(offset, order, 0).wait()
-
-
-def pack(routing, cache, others, section_count):
+                copy(n, spot, 0).wait()
+
+    for query_copy in query_copies:
+        query_copy.wait()
+
+
+def in_hbm(value):
+    return pltpu.with_memory_space_constraint(value, pltpu.HBM)
+
+
+def pack(routing, cache, queries, pieces, section_count):
     slots = section_count * CAP
-    cache_part = jax.ShapeDtypeStruct((CAP,) + cache.shape[1:], cache.dtype)
-    return pl.pallas_call(
-        functools.partial(pack_kernel, section_count),
-        out_shape=[cache_part] * section_count,
-        in_specs=[SMEM, HBM] + [ANY] * len(others),
-        out_specs=[VMEM] * section_count,
+    shapes = [jax.ShapeDtypeStruct((count,) + cache.shape[1:], cache.dtype) for _, _, count in pieces]
+    moved = sum(shape.size for shape in shapes)
+    for query in queries:
+        shapes += [jax.ShapeDtypeStruct((CAP,) + query.shape[2:], query.dtype)] * section_count
+        moved += query.size
+    return pl.pallas_call(
+        functools.partial(pack_kernel, pieces, section_count),
+        out_shape=shapes,
+        in_specs=[SMEM, HBM] + [HBM] * len(queries),
+        out_specs=[VMEM] * len(shapes),
         scratch_shapes=[
             pltpu.SMEM((slots,), jnp.int32),
             pltpu.SMEM((section_count,), jnp.int32),
             pltpu.SemaphoreType.DMA((slots,)),
+            pltpu.SemaphoreType.DMA((section_count,)),
         ],
-        compiler_params=limit(PACK_LIMIT),
-        cost_estimate=cost(0, 4 * cache.size),
+        compiler_params=limit(16),
+        cost_estimate=cost(0, 4 * moved),
         name="pack",
-    )(routing, cache, *others)
-
-
-def gate_kernel(*refs):
-    pass
-
-
-def gate(values, others):
-    count = len(values)
-    return pl.pallas_call(
-        gate_kernel,
-        out_shape=[jax.ShapeDtypeStruct(value.shape, value.dtype) for value in values],
-        in_specs=[ANY] * (count + len(others)),
-        out_specs=[ANY] * count,
-        input_output_aliases={n: n for n in range(count)},
-        compiler_params=limit(1),
-        cost_estimate=cost(0, 0),
-        name="gate",
-    )(*values, *others)
-
-
-def place_kernel(offsets, *refs):
-    count = len(offsets)
+    )(in_hbm(routing), in_hbm(cache), *[in_hbm(query) for query in queries])
+
+
+def place_kernel(pieces, *refs):
+    count = len(pieces)
     part_refs, out_ref, sem = refs[-2 - count : -2], refs[-2], refs[-1]
     section = lax.axis_index("sec")
     copies = []
-    for n, offset in enumerate(offsets):
-        for order in range(CAP):
-            slot = out_ref.at[0, (section ^ offset) * CAP + order]
-            copy = pltpu.make_async_copy(part_refs[n].at[order], slot, sem.at[n * CAP + order])
-            copy.start()
-            copies.append(copy)
+    for n, (offset, first, size) in enumerate(pieces):
+        slots = out_ref.at[0, pl.ds((section ^ offset) * CAP + first, size)]
+        copies.append(pltpu.make_async_copy(part_refs[n], slots, sem.at[n]))
+        copies[-1].start()
     for copy in copies:
         copy.wait()
 
 
-def place(given, parts, offsets, slot_count):
+def place(given, parts, pieces, slot_count):
     part = parts[0]
     return pl.pallas_call(
-        functools.partial(place_kernel, offsets),
+        functools.partial(place_kernel, pieces),
         out_shape=jax.ShapeDtypeStruct((1, slot_count) + part.shape[1:], part.dtype),
         in_specs=[HBM] * len(given) + [VMEM] * len(parts),
         out_specs=HBM,
-        scratch_shapes=[pltpu.SemaphoreType.DMA((len(parts) * CAP,))],
-        input_output_aliases={0: 0} if given else {},
+        scratch_shapes=[pltpu.SemaphoreType.DMA((len(parts),))],
+        input_output_aliases={1: 0} if len(given) > 1 else {},
         compiler_params=limit(8),
-        cost_estimate=cost(0, 4 * len(parts) * part.size),
+        cost_estimate=cost(0, 4 * sum(piece.size for piece in parts)),
         name="place",
-    )(*given, *parts)
-
-
-def attend_kernel(section_count, tp_count, routing_ref, lengths_ref, *refs):
-    cache_refs, query_refs = refs[:section_count], refs[section_count : 2 * section_count]
+    )(*[in_hbm(value) for value in given], *parts)
+
+
+def attend_kernel(pieces, section_count, tp_count, routing_ref, lengths_ref, *refs):
+    cache_refs, query_refs = refs[: len(pieces)], refs[len(pieces) : len(pieces) + section_count]
     message_refs = refs[-5 - tp_count : -5]
     source, used, messages, stats, stacked = refs[-5:]
     section = lax.axis_index("sec")
@@ -191,7 +165,7 @@
     position = lax.broadcasted_iota(jnp.int32, (local, span), 0) + tp_index * local
     owner = lax.broadcasted_iota(jnp.int32, (HEAD_SIZE, span), 1) // rows
 
-    def prompt(offset, order):
+    def prompt(cache_ref, place, offset, order):
         row = source[(section ^ offset) * CAP + order]
         visible = position < lengths_ref[section * REQ_GRP + row]
         values = query_refs[offset][order].astype(jnp.float32)
@@ -202,7 +176,7 @@
         query = stacked[slot].T.astype(jnp.bfloat16)
         query = [jnp.where(owner == k, query, jnp.zeros_like(query)) for k in range(KEY_VALUE_HEADS)]
         score = jnp.dot(
-            cache_refs[offset][order, 0], jnp.concatenate(query, axis=0), preferred_element_type=jnp.float32
+            cache_ref[place, 0], jnp.concatenate(query, axis=0), preferred_element_type=jnp.float32
         ) * HEAD_SIZE ** (-0.5)
         score = jnp.where(visible, score, HIDDEN)
         peak = jnp.max(score, axis=0, keepdims=True)
@@ -215,18 +189,19 @@
         for k in range(KEY_VALUE_HEADS):
             mixed = jnp.dot(
                 weight[k * rows : (k + 1) * rows],
-                cache_refs[offset][order, 1, :, k * HEAD_SIZE : (k + 1) * HEAD_SIZE],
+                cache_ref[place, 1, :, k * HEAD_SIZE : (k + 1) * HEAD_SIZE],
                 preferred_element_type=jnp.float32,
             )
             group = row * KEY_VALUE_HEADS + k
             messages[group // groups, group % groups] = mixed.astype(jnp.bfloat16)
 
-    for offset in range(section_count):
-        for order in range(CAP):
+    for cache_ref, (offset, first, size) in zip(cache_refs, pieces):
+        for place in range(size):
+            one = functools.partial(prompt, cache_ref, place, offset, first + place)
             if full:
-                prompt(offset, order)
+                one()
             else:
-                pl.when(order < used[section ^ offset])(functools.partial(prompt, offset, order))
+                pl.when(first + place < used[section ^ offset])(one)
 
     level = stats[...]
     high = level.astype(jnp.bfloat16).astype(jnp.float32)
@@ -255,17 +230,17 @@
                 )
 
 
-def attend(routing, lengths, caches, queries, others, tp_count):
-    section_count = len(caches)
+def attend(routing, lengths, caches, pieces, queries, tp_count):
+    section_count = len(queries)
     samples, width = queries[0].shape[1:]
     span = width // HEAD_SIZE * samples
     rows = span // KEY_VALUE_HEADS
     groups = REQ_GRP * KEY_VALUE_HEADS // tp_count
     multiplies = REQ_GRP * span * HEAD_SIZE * caches[0].shape[2]
     return pl.pallas_call(
-        functools.partial(attend_kernel, section_count, tp_count),
+        functools.partial(attend_kernel, pieces, section_count, tp_count),
         out_shape=[jax.ShapeDtypeStruct((groups + 2, rows, HEAD_SIZE), jnp.bfloat16)] * tp_count,
-        in_specs=[SMEM, SMEM] + [VMEM] * (2 * section_count) + [ANY] * len(others),
+        in_specs=[SMEM, SMEM] + [VMEM] * (len(caches) + section_count),
         out_specs=[VMEM] * tp_count,
         scratch_shapes=[
             pltpu.SMEM((section_count * CAP,), jnp.int32),
@@ -275,9 +250,9 @@
             pltpu.VMEM((section_count * CAP, span, HEAD_SIZE), jnp.float32),
         ],
         compiler_params=limit(12),
-        cost_estimate=cost(4 * multiplies, 2 * section_count * caches[0].size, multiplies // HEAD_SIZE),
+        cost_estimate=cost(2 * 10**10, 2 * sum(part.size for part in caches), multiplies // HEAD_SIZE),
         name="attend",
-    )(routing, lengths, *caches, *queries, *others)
+    )(routing, lengths, *caches, *queries)
 
 
 def join_kernel(count, samples, *refs):
@@ -362,10 +337,10 @@
         in_specs=[HBM] + [ANY] * len(others),
         out_specs=VMEM,
         scratch_shapes=[pltpu.SemaphoreType.DMA((8,))],
-        compiler_params=limit(FETCH_LIMIT),
+        compiler_params=limit(36),
         cost_estimate=cost(0, 4 * weight.size),
         name="fetch",
-    )(weight, *others)
+    )(in_hbm(weight), *others)
 
 
 def project_kernel(count, tile, *refs):
@@ -404,12 +379,15 @@
     slot_count, samples, query_width = queries.shape[1:]
     routing = routing.reshape(-1)
 
-    query_parts = split(queries, section_count)
+    far = [(offset, 0, CAP) for offset in range(2, section_count)]
+    near = [(offset, 0, CAP) for offset in range(2)]
+    parts = pack(routing, prompt_key_values, [queries], far, section_count)
+    far_caches, query_parts = parts[: len(far)], parts[len(far) :]
     own_queries = [swap(part, "sec", offset) for offset, part in enumerate(query_parts)]
-    caches = pack(routing, prompt_key_values, query_parts[:1], section_count)
-    caches = caches[:1] + gate(caches[1:], own_queries[1:])
-    arrived = [swap(part, "sec", offset) for offset, part in enumerate(caches)]
-    messages = attend(routing, lengths, caches, own_queries, arrived[1:2], tp_count)
+    arrived = [swap(part, "sec", piece[0]) for part, piece in zip(far_caches, far)]
+    near_caches = pack(routing, prompt_key_values, [], near, section_count)
+
+    messages = attend(routing, lengths, far_caches + near_caches, far + near, own_queries, tp_count)
     partials = [swap(part, "tp", offset) for offset, part in enumerate(messages)]
     held_weight = fetch(out_weight, messages[:1])
     share = join(partials, [held_weight], samples)
@@ -423,10 +401,13 @@
     else:
         layer_out = project(shares, held_weight, samples)
 
-    whole = place([], arrived[:2], [0, 1], slot_count)
-    for offset in range(2, section_count):
-        whole = place([whole, layer_out], arrived[offset : offset + 1], [offset], slot_count)
-    return (layer_out, whole)
+    near_parts = [swap(part, "sec", piece[0]) for part, piece in zip(near_caches, near)]
+    stages = [([part], [piece]) for part, piece in zip(arrived, far)]
+    stages.insert(-1, (near_parts, near))
+    given = [layer_out]
+    for parts, pieces in stages:
+        given = [layer_out, place(given, parts, pieces, slot_count)]
+    return (layer_out, given[1])
 
 
 def solution(mesh):

time: 57.7 us -> 57.5 us (level)
  local copies, waits for them, and re-layouts: 2.51 us -> 0.01 us
  Pallas kernels: 20.2 us -> 22 us
  starting transfers between devices: 13.9 us -> 14.7 us
    unnamed x8 -> x4, local copies, waits for them, and re-layouts: 2.51 us -> 0.01 us
    pallas_call x7 -> x6, Pallas kernels: 10.2 us -> 12 us  [the longest x2 4.92 us: pack(): pl.pallas_call(functools.partial(pack_kernel, pieces, section_count), out...]
    ppermute x12, starting transfers between devices: 13.9 us -> 14.7 us  [swap(): return lax.ppermute(value, axis, [(i, i ^ offset) for i in range(count)])]
  transfers between devices with their start and end apart: 12 -> 12, of which waited for: 6 -> 5; matrix products, arithmetic and copies ran while one was open for 0% -> 0% of each run, Pallas kernels for 33% -> 32%
where the time goes in v4:
time: 57.5 us; the launch traced here: 57.3 us
  Pallas kernels  22 us (38%)
  waiting for transfers between devices  19.8 us (34%)
  starting transfers between devices  14.7 us (26%)
  between operations  0.76 us (1%)
    ppermute x12, waiting for transfers between devices, swap(): return lax.ppermute(value, axis, [(i, i ^ offset) for i in range(count)])  19.8 us
    ppermute x12, starting transfers between devices, swap(): return lax.ppermute(value, axis, [(i, i ^ offset) for i in range(count)])  14.7 us
    pallas_call x1, Pallas kernels, fetch(): pl.pallas_call(fetch_kernel, out_shape=jax.ShapeDtypeStruct(weight.shape,...  5.92 us
    pallas_call x2, Pallas kernels, pack(): pl.pallas_call(functools.partial(pack_kernel, pieces, section_count), out...  4.92 us
    pallas_call x1, Pallas kernels, attend(): pl.pallas_call(functools.partial(attend_kernel, pieces, section_count, tp...  3.79 us
    pallas_call x1, Pallas kernels, project(): pl.pallas_call(functools.partial(project_kernel, count, min(256, width)),...  3.64 us
    pallas_call x3, Pallas kernels, place(): pl.pallas_call(functools.partial(place_kernel, pieces), out_shape=jax.Sha...  3.3 us
  transfers between devices with their start and end apart: 12, of which 5 were waited for; matrix products, arithmetic and copies ran while one was open for 0% of the time, Pallas kernels for 32%

profile of v4, /device:TPU:0, one launch (start us, length us, event | category | flops | bytes accessed | tf_op | source)
XLA Modules:
  0.0 57.3 jit_solution(6696777457963687820)
XLA Ops:
  0.6 0.0 copy-start
  0.7 2.6 %pack.2 = (bf16[2,2,256,512]{3,2,1,0:T(8,128)(2,1)S(1)}, bf16[2,2,256,512]{3,2,1,0:T(8,128)(2,1)S(1)}, bf16[2,4,4096]{2,1,0:T(4,128)(2,1)S(1)}, bf16[2,4,4096]{2...) custom-call(s32[32]{0:T(128)} %bitcast.1, bf16[8,2,256,512]{3,2,1,0:T(8,128)(2,1)} %cache_ref.3, ...), custom_call_target="tpu_custom_call" | custom-call | bytes 4718592 | tf_op jit(solution)/shard_map/pack/pallas_call | solution.py:108
  3.2 0.5 collective-permute-start
  3.8 2.6 %collective-permute-start.1 = (bf16[2,4,4096]{2,1,0:T(4,128)(2,1)S(1)}, bf16[2,4,4096]{2,1,0:T(4,128)(2,1)S(1)}, u32[]{:S(2)}, u32[]{:S(2)}) collective-permute-start(bf16[2,4,4096]{2,1,0:T(4,128)(2,1)S(1)} %get-tuple-element.20), channel_id=1, source_target_pairs={{0,2},{1,3},{2,0},{3,1},{4,6},{5,7},{6,4},{7,5},{8,10},{9,11},{10,... | collective-permute-start | bytes 196616 | tf_op jit(solution)/shard_map/ppermute | solution.py:34
  6.3 0.1 collective-permute-start.2
  6.4 2.3 %pack.3 = (bf16[2,2,256,512]{3,2,1,0:T(8,128)(2,1)S(1)}, bf16[2,2,256,512]{3,2,1,0:T(8,128)(2,1)S(1)}) custom-call(s32[32]{0:T(128)} %bitcast.2, bf16[8,2,256,512]{3,2,1,0:T(8,128)(2,1)} %cache_ref.3), custom_call_target="tpu_custom_call" | custom-call | bytes 4194304 | tf_op jit(solution)/shard_map/pack/pallas_call | solution.py:108
  8.7 0.2 collective-permute-start.10
  8.9 1.9 %collective-permute-start.9 = (bf16[2,2,256,512]{3,2,1,0:T(8,128)(2,1)S(1)}, bf16[2,2,256,512]{3,2,1,0:T(8,128)(2,1)S(1)}, u32[]{:S(2)}, u32[]{:S(2)}) collective-permute-start(bf16[2,2,256,512]{3,2,1,0:T(8,128)(2,1)S(1)} %get-tuple-element.14.refs_0_), channel_id=1, source_target_pairs={{0,2},{1,3},{2,0},{3,1},{4,6},{5,7},{6,4},{7,5},{8,10},{9,11},{10,... | collective-permute-start | bytes 3145736 | tf_op jit(solution)/shard_map/ppermute | solution.py:34
  10.9 0.0 collective-permute-done.refs_5_
  10.9 0.0 collective-permute-start.11
  10.9 0.0 collective-permute-done.1.refs_6_
  10.9 0.0 collective-permute-done.2.refs_7_
  10.9 3.8 %attend.1 = (bf16[10,32,128]{2,1,0:T(8,128)(2,1)S(1)}, bf16[10,32,128]{2,1,0:T(8,128)(2,1)S(1)}, bf16[10,32,128]{2,1,0:T(8,128)(2,1)S(1)}, bf16[10,32,128]{2,1,0:T(8,128)(2,1)S(1)}) custom-call(s32[32]{0:T(128)S(1)} %bitcast.3, s32[32]{0:T(128)S(1)} %copy-done.1, bf16[2,2,256,512]{3,2,1,0:T(8,128)(2,1)S(1)} %get-tuple-element.14.refs_0_, ...), custom_call_target="tpu_custom_call" | custom-call | flops 20000000000 | bytes 4194304 | tf_op jit(solution)/shard_map/attend/pallas_call | solution.py:240
  14.7 1.7 %collective-permute-start.3 = (bf16[10,32,128]{2,1,0:T(8,128)(2,1)S(1)}, bf16[10,32,128]{2,1,0:T(8,128)(2,1)S(1)}, u32[]{:S(2)}, u32[]{:S(2)}) collective-permute-start(bf16[10,32,128]{2,1,0:T(8,128)(2,1)S(1)} %get-tuple-element.23), channel_id=1, source_target_pairs={{0,4},{4,0},{8,12},{12,8},{1,5},{5,1},{9,13},{13,9},{2,6},{6,2},{1... | collective-permute-start | bytes 245768 | tf_op jit(solution)/shard_map/ppermute | solution.py:34
  16.4 2.6 %collective-permute-start.4 = (bf16[10,32,128]{2,1,0:T(8,128)(2,1)S(1)}, bf16[10,32,128]{2,1,0:T(8,128)(2,1)S(1)}, u32[]{:S(2)}, u32[]{:S(2)}) collective-permute-start(bf16[10,32,128]{2,1,0:T(8,128)(2,1)S(1)} %get-tuple-element.24), channel_id=1, source_target_pairs={{0,8},{4,12},{8,0},{12,4},{1,9},{5,13},{9,1},{13,5},{2,10},{6,14},... | collective-permute-start | bytes 245768 | tf_op jit(solution)/shard_map/ppermute | solution.py:34
  19.0 0.6 %collective-permute-done.3.refs_1_ = bf16[10,32,128]{2,1,0:T(8,128)(2,1)S(1)} collective-permute-done((bf16[10,32,128]{2,1,0:T(8,128)(2,1)S(1)}, bf16[10,32,128]{2,1,0:T(8,128)(2,1)S(1)}, u32[]{:S(2)}, u32[]{:S(2)}) %collective-permute-start.3) | collective-permute-done | bytes 81952 | tf_op jit(solution)/shard_map/ppermute | solution.py:34
  19.6 4.8 %collective-permute-start.5 = (bf16[10,32,128]{2,1,0:T(8,128)(2,1)S(1)}, bf16[10,32,128]{2,1,0:T(8,128)(2,1)S(1)}, u32[]{:S(2)}, u32[]{:S(2)}) collective-permute-start(bf16[10,32,128]{2,1,0:T(8,128)(2,1)S(1)} %get-tuple-element.25), channel_id=1, source_target_pairs={{0,12},{4,8},{8,4},{12,0},{1,13},{5,9},{9,5},{13,1},{2,14},{6,10},... | collective-permute-start | bytes 245768 | tf_op jit(solution)/shard_map/ppermute | solution.py:34
  24.4 5.9 %fetch.1.refs_4_ = bf16[4096,2048]{1,0:T(8,128)(2,1)S(1)} custom-call(bf16[4096,2048]{1,0:T(8,128)(2,1)} %weight_ref.1, bf16[10,32,128]{2,1,0:T(8,128)(2,1)S(1)} %get-tuple-element.22.refs_0_), custom_call_target="tpu_custom_call" | custom-call | bytes 33554432 | tf_op jit(solution)/shard_map/fetch/pallas_call | solution.py:334
  30.4 0.0 collective-permute-done.5.refs_3_
  30.4 0.4 join.1.refs_0_
  30.8 0.4 collective-permute-start.8
  31.1 0.0 collective-permute-start.7
  31.1 6.2 %collective-permute-done.8.refs_3_ = bf16[8,4096]{1,0:T(8,128)(2,1)S(1)} collective-permute-done((bf16[8,4096]{1,0:T(8,128)(2,1)S(1)}, bf16[8,4096]{1,0:T(8,128)(2,1)S(1)}, u32[]{:S(2)}, u32[]{:S(2)}) %collective-permute-start.8) | collective-permute-done | bytes 65568 | tf_op jit(solution)/shard_map/ppermute | solution.py:34
  37.4 0.0 collective-permute-start.6
  37.4 0.5 collective-permute-done.7.refs_2_
  37.9 3.8 %collective-permute-done.6.refs_1_ = bf16[8,4096]{1,0:T(8,128)(2,1)S(1)} collective-permute-done((bf16[8,4096]{1,0:T(8,128)(2,1)S(1)}, bf16[8,4096]{1,0:T(8,128)(2,1)S(1)}, u32[]{:S(2)}, u32[]{:S(2)}) %collective-permute-start.6) | collective-permute-done | bytes 65568 | tf_op jit(solution)/shard_map/ppermute | solution.py:34
  41.6 3.6 %project.1.refs_0_ = bf16[8,4,2048]{2,1,0:T(4,128)(2,1)} custom-call(bf16[8,4096]{1,0:T(8,128)(2,1)S(1)} %join.1.refs_0_, bf16[8,4096]{1,0:T(8,128)(2,1)S(1)} %collective-permute-done.6.refs_1_, bf16[8,4096]{1,0:T(8,128)(2,1)S(1)} %collective-permute-done.7.refs_2_, bf16[8,4096]{1,0:T(8,128)(2,1)S(1)} %collective-permute-done.8.refs_3_, ...), custom_call_target="tpu_custom_call" | custom-call | flops 536870912 | bytes 16777216 | tf_op jit(solution)/shard_map/project/pallas_call | solution.py:365
  45.3 0.0 collective-permute-done.9.refs_1_
  45.3 1.0 %place.3.refs_1_ = bf16[1,8,2,256,512]{4,3,2,1,0:T(8,128)(2,1)} custom-call(bf16[8,4,2048]{2,1,0:T(4,128)(2,1)} %project.1.refs_0_, bf16[2,2,256,512]{3,2,1,0:T(8,128)(2,1)S(1)} %collective-permute-done.9.refs_1_), custom_call_target="tpu_custom_call" | custom-call | bytes 2097152 | tf_op jit(solution)/shard_map/place/pallas_call | solution.py:140
  46.3 1.3 %place.4.refs_1_ = bf16[1,8,2,256,512]{4,3,2,1,0:T(8,128)(2,1)} custom-call(bf16[8,4,2048]{2,1,0:T(4,128)(2,1)} %project.1.refs_0_, bf16[1,8,2,256,512]{4,3,2,1,0:T(8,128)(2,1)} %place.3.refs_1_, bf16[2,2,256,512]{3,2,1,0:T(8,128)(2,1)S(1)} %get-tuple-element.16.refs_2_, ...), custom_call_target="tpu_custom_call", output_to_operand_aliasing={{}: (1, {})} | custom-call | bytes 4194304 | tf_op jit(solution)/shard_map/place/pallas_call | solution.py:140
  47.6 8.7 %collective-permute-done.11.refs_2_ = bf16[2,2,256,512]{3,2,1,0:T(8,128)(2,1)S(1)} collective-permute-done((bf16[2,2,256,512]{3,2,1,0:T(8,128)(2,1)S(1)}, bf16[2,2,256,512]{3,2,1,0:T(8,128)(2,1)S(1)}, u32[]{:S(2)}, u32[]{:S(2)}) %collective-permute-start.11) | collective-permute-done | bytes 1048608 | tf_op jit(solution)/shard_map/ppermute | solution.py:34
  56.3 1.0 %place.5 = bf16[1,8,2,256,512]{4,3,2,1,0:T(8,128)(2,1)} custom-call(bf16[8,4,2048]{2,1,0:T(4,128)(2,1)} %project.1.refs_0_, bf16[1,8,2,256,512]{4,3,2,1,0:T(8,128)(2,1)} %place.4.refs_1_, bf16[2,2,256,512]{3,2,1,0:T(8,128)(2,1)S(1)} %collective-permute-done.11.refs_2_), custom_call_target="tpu_custom_call", output_to_operand_aliasing={{}: (1, {})} | custom-call | bytes 2097152 | tf_op jit(solution)/shard_map/place/pallas_call | solution.py:140
  (5 shorter events, 0.0 us)
Async XLA Ops:
  0.6 10.3 %copy-start = (s32[32,1]{0,1:T(1,128)S(1)}, s32[32,1]{0,1:T(1,128)}, u32[]{:S(2)}) copy-start(s32[32,1]{0,1:T(1,128)} %param.7) | copy-start | bytes 388
  0.6 10.3 %copy-start.1 = (s32[32]{0:T(128)S(1)}, s32[32]{0:T(128)}, u32[]{:S(2)}) copy-start(s32[32]{0:T(128)} %lengths_ref.1) | copy-start | bytes 388
  3.2 7.6 %collective-permute-start = (bf16[2,4,4096]{2,1,0:T(4,128)(2,1)S(1)}, bf16[2,4,4096]{2,1,0:T(4,128)(2,1)S(1)}, u32[]{:S(2)}, u32[]{:S(2)}) collective-permute-start(bf16[2,4,4096]{2,1,0:T(4,128)(2,1)S(1)} %get-tuple-element.19), channel_id=1, source_target_pairs={{0,1},{1,0},{2,3},{3,2},{4,5},{5,4},{6,7},{7,6},{8,9},{9,8},{10,11... | collective-permute-start | bytes 196616 | tf_op jit(solution)/shard_map/ppermute | solution.py:34
  3.8 7.1 %collective-permute-start.1 = (bf16[2,4,4096]{2,1,0:T(4,128)(2,1)S(1)}, bf16[2,4,4096]{2,1,0:T(4,128)(2,1)S(1)}, u32[]{:S(2)}, u32[]{:S(2)}) collective-permute-start(bf16[2,4,4096]{2,1,0:T(4,128)(2,1)S(1)} %get-tuple-element.20), channel_id=1, source_target_pairs={{0,2},{1,3},{2,0},{3,1},{4,6},{5,7},{6,4},{7,5},{8,10},{9,11},{10,... | collective-permute-start | bytes 196616 | tf_op jit(solution)/shard_map/ppermute | solution.py:34
  6.3 4.6 %collective-permute-start.2 = (bf16[2,4,4096]{2,1,0:T(4,128)(2,1)S(1)}, bf16[2,4,4096]{2,1,0:T(4,128)(2,1)S(1)}, u32[]{:S(2)}, u32[]{:S(2)}) collective-permute-start(bf16[2,4,4096]{2,1,0:T(4,128)(2,1)S(1)} %get-tuple-element.21), channel_id=1, source_target_pairs={{0,3},{1,2},{2,1},{3,0},{4,7},{5,6},{6,5},{7,4},{8,11},{9,10},{10,... | collective-permute-start | bytes 196616 | tf_op jit(solution)/shard_map/ppermute | solution.py:34
  8.7 37.5 %collective-permute-start.10 = (bf16[2,2,256,512]{3,2,1,0:T(8,128)(2,1)S(1)}, bf16[2,2,256,512]{3,2,1,0:T(8,128)(2,1)S(1)}, u32[]{:S(2)}, u32[]{:S(2)}) collective-permute-start(bf16[2,2,256,512]{3,2,1,0:T(8,128)(2,1)S(1)} %get-tuple-element.17.refs_3_), channel_id=1, source_target_pairs={{0,1},{1,0},{2,3},{3,2},{4,5},{5,4},{6,7},{7,6},{8,9},{9,8},{10,11... | collective-permute-start | bytes 3145736 | tf_op jit(solution)/shard_map/ppermute | solution.py:34
  8.9 36.3 %collective-permute-start.9 = (bf16[2,2,256,512]{3,2,1,0:T(8,128)(2,1)S(1)}, bf16[2,2,256,512]{3,2,1,0:T(8,128)(2,1)S(1)}, u32[]{:S(2)}, u32[]{:S(2)}) collective-permute-start(bf16[2,2,256,512]{3,2,1,0:T(8,128)(2,1)S(1)} %get-tuple-element.14.refs_0_), channel_id=1, source_target_pairs={{0,2},{1,3},{2,0},{3,1},{4,6},{5,7},{6,4},{7,5},{8,10},{9,11},{10,... | collective-permute-start | bytes 3145736 | tf_op jit(solution)/shard_map/ppermute | solution.py:34
  10.9 45.4 %collective-permute-start.11 = (bf16[2,2,256,512]{3,2,1,0:T(8,128)(2,1)S(1)}, bf16[2,2,256,512]{3,2,1,0:T(8,128)(2,1)S(1)}, u32[]{:S(2)}, u32[]{:S(2)}) collective-permute-start(bf16[2,2,256,512]{3,2,1,0:T(8,128)(2,1)S(1)} %get-tuple-element.15.refs_1_), channel_id=1, source_target_pairs={{0,3},{1,2},{2,1},{3,0},{4,7},{5,6},{6,5},{7,4},{8,11},{9,10},{10,... | collective-permute-start | bytes 3145736 | tf_op jit(solution)/shard_map/ppermute | solution.py:34
  14.7 4.9 %collective-permute-start.3 = (bf16[10,32,128]{2,1,0:T(8,128)(2,1)S(1)}, bf16[10,32,128]{2,1,0:T(8,128)(2,1)S(1)}, u32[]{:S(2)}, u32[]{:S(2)}) collective-permute-start(bf16[10,32,128]{2,1,0:T(8,128)(2,1)S(1)} %get-tuple-element.23), channel_id=1, source_target_pairs={{0,4},{4,0},{8,12},{12,8},{1,5},{5,1},{9,13},{13,9},{2,6},{6,2},{1... | collective-permute-start | bytes 245768 | tf_op jit(solution)/shard_map/ppermute | solution.py:34
  16.4 14.0 %collective-permute-start.4 = (bf16[10,32,128]{2,1,0:T(8,128)(2,1)S(1)}, bf16[10,32,128]{2,1,0:T(8,128)(2,1)S(1)}, u32[]{:S(2)}, u32[]{:S(2)}) collective-permute-start(bf16[10,32,128]{2,1,0:T(8,128)(2,1)S(1)} %get-tuple-element.24), channel_id=1, source_target_pairs={{0,8},{4,12},{8,0},{12,4},{1,9},{5,13},{9,1},{13,5},{2,10},{6,14},... | collective-permute-start | bytes 245768 | tf_op jit(solution)/shard_map/ppermute | solution.py:34
  19.6 10.8 %collective-permute-start.5 = (bf16[10,32,128]{2,1,0:T(8,128)(2,1)S(1)}, bf16[10,32,128]{2,1,0:T(8,128)(2,1)S(1)}, u32[]{:S(2)}, u32[]{:S(2)}) collective-permute-start(bf16[10,32,128]{2,1,0:T(8,128)(2,1)S(1)} %get-tuple-element.25), channel_id=1, source_target_pairs={{0,12},{4,8},{8,4},{12,0},{1,13},{5,9},{9,5},{13,1},{2,14},{6,10},... | collective-permute-start | bytes 245768 | tf_op jit(solution)/shard_map/ppermute | solution.py:34
  30.8 6.6 %collective-permute-start.8 = (bf16[8,4096]{1,0:T(8,128)(2,1)S(1)}, bf16[8,4096]{1,0:T(8,128)(2,1)S(1)}, u32[]{:S(2)}, u32[]{:S(2)}) collective-permute-start(bf16[8,4096]{1,0:T(8,128)(2,1)S(1)} %join.1.refs_0_), channel_id=1, source_target_pairs={{0,12},{4,8},{8,4},{12,0},{1,13},{5,9},{9,5},{13,1},{2,14},{6,10},... | collective-permute-start | bytes 196616 | tf_op jit(solution)/shard_map/ppermute | solution.py:34
  31.1 6.7 %collective-permute-start.7 = (bf16[8,4096]{1,0:T(8,128)(2,1)S(1)}, bf16[8,4096]{1,0:T(8,128)(2,1)S(1)}, u32[]{:S(2)}, u32[]{:S(2)}) collective-permute-start(bf16[8,4096]{1,0:T(8,128)(2,1)S(1)} %join.1.refs_0_), channel_id=1, source_target_pairs={{0,8},{4,12},{8,0},{12,4},{1,9},{5,13},{9,1},{13,5},{2,10},{6,14},... | collective-permute-start | bytes 196616 | tf_op jit(solution)/shard_map/ppermute | solution.py:34
  37.4 4.3 %collective-permute-start.6 = (bf16[8,4096]{1,0:T(8,128)(2,1)S(1)}, bf16[8,4096]{1,0:T(8,128)(2,1)S(1)}, u32[]{:S(2)}, u32[]{:S(2)}) collective-permute-start(bf16[8,4096]{1,0:T(8,128)(2,1)S(1)} %join.1.refs_0_), channel_id=1, source_target_pairs={{0,4},{4,0},{8,12},{12,8},{1,5},{5,1},{9,13},{13,9},{2,6},{6,2},{1... | collective-permute-start | bytes 196616 | tf_op jit(solution)/shard_map/ppermute | solution.py:34

commit v5 on v4

--- a/solution.py
+++ b/solution.py
@@ -44,10 +44,8 @@
         source[target * CAP + order] = i
 
 
-def pack_kernel(pieces, section_count, routing_ref, cache_ref, *refs):
-    refs, (source, used, sem, query_sem) = refs[:-4], refs[-4:]
-    query_ref, refs = (refs[0], refs[1:]) if len(refs) > len(pieces) else (None, refs)
-    cache_out, query_out = refs[: len(pieces)], refs[len(pieces) :]
+def pack_kernel(pieces, section_count, routing_ref, cache_ref, query_ref, *refs):
+    cache_out, query_out, (source, used, sem, query_sem) = refs[: len(pieces)], refs[len(pieces) : -4], refs[-4:]
     section = lax.axis_index("sec")
     full = section_count * CAP == REQ_GRP
     query_copies = []
@@ -101,14 +99,12 @@
 def pack(routing, cache, queries, pieces, section_count):
     slots = section_count * CAP
     shapes = [jax.ShapeDtypeStruct((count,) + cache.shape[1:], cache.dtype) for _, _, count in pieces]
+    shapes += [jax.ShapeDtypeStruct((CAP,) + queries.shape[2:], queries.dtype)] * section_count
     moved = sum(shape.size for shape in shapes)
-    for query in queries:
-        shapes += [jax.ShapeDtypeStruct((CAP,) + query.shape[2:], query.dtype)] * section_count
-        moved += query.size
     return pl.pallas_call(
         functools.partial(pack_kernel, pieces, section_count),
         out_shape=shapes,
-        in_specs=[SMEM, HBM] + [HBM] * len(queries),
+        in_specs=[SMEM, HBM, HBM],
         out_specs=[VMEM] * len(shapes),
         scratch_shapes=[
             pltpu.SMEM((slots,), jnp.int32),
@@ -119,7 +115,7 @@
         compiler_params=limit(16),
         cost_estimate=cost(0, 4 * moved),
         name="pack",
-    )(in_hbm(routing), in_hbm(cache), *[in_hbm(query) for query in queries])
+    )(in_hbm(routing), in_hbm(cache), in_hbm(queries))
 
 
 def place_kernel(pieces, *refs):
@@ -143,7 +139,7 @@
         in_specs=[HBM] * len(given) + [VMEM] * len(parts),
         out_specs=HBM,
         scratch_shapes=[pltpu.SemaphoreType.DMA((len(parts),))],
-        input_output_aliases={1: 0} if len(given) > 1 else {},
+        input_output_aliases={0: 0} if given else {},
         compiler_params=limit(8),
         cost_estimate=cost(0, 4 * sum(piece.size for piece in parts)),
         name="place",
@@ -230,7 +226,7 @@
                 )
 
 
-def attend(routing, lengths, caches, pieces, queries, tp_count):
+def attend(routing, lengths, caches, pieces, queries, others, tp_count):
     section_count = len(queries)
     samples, width = queries[0].shape[1:]
     span = width // HEAD_SIZE * samples
@@ -240,7 +236,7 @@
     return pl.pallas_call(
         functools.partial(attend_kernel, pieces, section_count, tp_count),
         out_shape=[jax.ShapeDtypeStruct((groups + 2, rows, HEAD_SIZE), jnp.bfloat16)] * tp_count,
-        in_specs=[SMEM, SMEM] + [VMEM] * (len(caches) + section_count),
+        in_specs=[SMEM, SMEM] + [VMEM] * (len(caches) + section_count) + [ANY] * len(others),
         out_specs=[VMEM] * tp_count,
         scratch_shapes=[
             pltpu.SMEM((section_count * CAP,), jnp.int32),
@@ -252,7 +248,7 @@
         compiler_params=limit(12),
         cost_estimate=cost(2 * 10**10, 2 * sum(part.size for part in caches), multiplies // HEAD_SIZE),
         name="attend",
-    )(routing, lengths, *caches, *queries)
+    )(routing, lengths, *caches, *queries, *others)
 
 
 def join_kernel(count, samples, *refs):
@@ -379,15 +375,16 @@
     slot_count, samples, query_width = queries.shape[1:]
     routing = routing.reshape(-1)
 
+    near = [(offset, 0, CAP) for offset in range(2)]
     far = [(offset, 0, CAP) for offset in range(2, section_count)]
-    near = [(offset, 0, CAP) for offset in range(2)]
-    parts = pack(routing, prompt_key_values, [queries], far, section_count)
-    far_caches, query_parts = parts[: len(far)], parts[len(far) :]
+    pieces = far + near
+    parts = pack(routing, prompt_key_values, queries, pieces, section_count)
+    caches, query_parts = parts[: len(pieces)], parts[len(pieces) :]
     own_queries = [swap(part, "sec", offset) for offset, part in enumerate(query_parts)]
-    arrived = [swap(part, "sec", piece[0]) for part, piece in zip(far_caches, far)]
-    near_caches = pack(routing, prompt_key_values, [], near, section_count)
-
-    messages = attend(routing, lengths, far_caches + near_caches, far + near, own_queries, tp_count)
+    arrived = [swap(part, "sec", piece[0]) for part, piece in zip(caches, pieces)]
+    far_parts, near_parts = arrived[: len(far)], arrived[len(far) :]
+
+    messages = attend(routing, lengths, caches, pieces, own_queries, near_parts[1:], tp_count)
     partials = [swap(part, "tp", offset) for offset, part in enumerate(messages)]
     held_weight = fetch(out_weight, messages[:1])
     share = join(partials, [held_weight], samples)
@@ -401,13 +398,10 @@
     else:
         layer_out = project(shares, held_weight, samples)
 
-    near_parts = [swap(part, "sec", piece[0]) for part, piece in zip(near_caches, near)]
-    stages = [([part], [piece]) for part, piece in zip(arrived, far)]
-    stages.insert(-1, (near_parts, near))
-    given = [layer_out]
-    for parts, pieces in stages:
-        given = [layer_out, place(given, parts, pieces, slot_count)]
-    return (layer_out, given[1])
+    whole = place([], near_parts, near, slot_count)
+    for part, piece in zip(far_parts, far):
+        whole = place([whole, layer_out], [part], [piece], slot_count)
+    return (layer_out, whole)
 
 
 def solution(mesh):

time: 57.5 us -> 57.8 us (level)
  waiting for transfers between devices: 19.8 us -> 22.3 us
  Pallas kernels: 22 us -> 20.3 us
    ppermute x12, waiting for transfers between devices: 19.8 us -> 22.3 us  [swap(): return lax.ppermute(value, axis, [(i, i ^ offset) for i in range(count)])]
    pallas_call x2 -> x1, Pallas kernels: 4.92 us -> 3.22 us  [pack(): pl.pallas_call(functools.partial(pack_kernel, pieces, section_count), out...]
  transfers between devices with their start and end apart: 12 -> 12, of which waited for: 5 -> 6; matrix products, arithmetic and copies ran while one was open for 0% -> 0% of each run, Pallas kernels for 32% -> 28%
where the time goes in v5:
time: 57.8 us; the launch traced here: 57.7 us
  waiting for transfers between devices  22.3 us (39%)
  Pallas kernels  20.3 us (35%)
  starting transfers between devices  14.4 us (25%)
  between operations  0.72 us (1%)
    ppermute x12, waiting for transfers between devices, swap(): return lax.ppermute(value, axis, [(i, i ^ offset) for i in range(count)])  22.3 us
    ppermute x12, starting transfers between devices, swap(): return lax.ppermute(value, axis, [(i, i ^ offset) for i in range(count)])  14.4 us
    pallas_call x1, Pallas kernels, fetch(): pl.pallas_call(fetch_kernel, out_shape=jax.ShapeDtypeStruct(weight.shape,...  5.92 us
    pallas_call x1, Pallas kernels, attend(): pl.pallas_call(functools.partial(attend_kernel, pieces, section_count, tp...  3.79 us
    pallas_call x1, Pallas kernels, project(): pl.pallas_call(functools.partial(project_kernel, count, min(256, width)),...  3.64 us
    pallas_call x3, Pallas kernels, place(): pl.pallas_call(functools.partial(place_kernel, pieces), out_shape=jax.Sha...  3.29 us
    pallas_call x1, Pallas kernels, pack(): pl.pallas_call(functools.partial(pack_kernel, pieces, section_count), out...  3.22 us
  transfers between devices with their start and end apart: 12, of which 6 were waited for; matrix products, arithmetic and copies ran while one was open for 0% of the time, Pallas kernels for 28%

profile of v5, /device:TPU:0, one launch (start us, length us, event | category | flops | bytes accessed | tf_op | source)
XLA Modules:
  0.0 57.7 jit_solution(8556240978995025100)
XLA Ops:
  0.7 3.2 %pack.1 = (bf16[2,2,256,512]{3,2,1,0:T(8,128)(2,1)S(1)}, bf16[2,2,256,512]{3,2,1,0:T(8,128)(2,1)S(1)}, bf16[2,2,256,512]{3,2,1,0:T(8,128)(2,1)S(1)}, bf16[2,2,25...) custom-call(s32[32]{0:T(128)} %bitcast.1, ...), custom_call_target="tpu_custom_call" | custom-call | bytes 8912896 | tf_op jit(solution)/shard_map/pack/pallas_call | solution.py:104
  3.9 0.5 collective-permute-start.3
  4.4 0.1 collective-permute-start
  4.5 2.9 %collective-permute-start.1 = (bf16[2,4,4096]{2,1,0:T(4,128)(2,1)S(1)}, bf16[2,4,4096]{2,1,0:T(4,128)(2,1)S(1)}, u32[]{:S(2)}, u32[]{:S(2)}) collective-permute-start(bf16[2,4,4096]{2,1,0:T(4,128)(2,1)S(1)} %get-tuple-element.20), channel_id=1, source_target_pairs={{0,2},{1,3},{2,0},{3,1},{4,6},{5,7},{6,4},{7,5},{8,10},{9,11},{10,... | collective-permute-start | bytes 196616 | tf_op jit(solution)/shard_map/ppermute | solution.py:34
  7.4 0.0 collective-permute-start.2
  7.4 1.4 %collective-permute-start.10 = (bf16[2,2,256,512]{3,2,1,0:T(8,128)(2,1)S(1)}, bf16[2,2,256,512]{3,2,1,0:T(8,128)(2,1)S(1)}, u32[]{:S(2)}, u32[]{:S(2)}) collective-permute-start(bf16[2,2,256,512]{3,2,1,0:T(8,128)(2,1)S(1)} %get-tuple-element.14.refs_0_), channel_id=1, source_target_pairs={{0,2},{1,3},{2,0},{3,1},{4,6},{5,7},{6,4},{7,5},{8,10},{9,11},{10,... | collective-permute-start | bytes 3145736 | tf_op jit(solution)/shard_map/ppermute | solution.py:34
  8.8 0.0 collective-permute-done.refs_5_
  8.8 0.6 collective-permute-start.11
  9.4 0.3 collective-permute-done.1.refs_6_
  9.7 2.1 %collective-permute-done.2.refs_7_ = bf16[2,4,4096]{2,1,0:T(4,128)(2,1)S(1)} collective-permute-done((bf16[2,4,4096]{2,1,0:T(4,128)(2,1)S(1)}, bf16[2,4,4096]{2,1,0:T(4,128)(2,1)S(1)}, u32[]{:S(2)}, u32[]{:S(2)}) %collective-permute-start.2) | collective-permute-done | bytes 65568 | tf_op jit(solution)/shard_map/ppermute | solution.py:34
  11.8 0.0 collective-permute-done.3.refs_8_.refs_1_
  11.8 3.8 %attend.1 = (bf16[10,32,128]{2,1,0:T(8,128)(2,1)S(1)}, bf16[10,32,128]{2,1,0:T(8,128)(2,1)S(1)}, bf16[10,32,128]{2,1,0:T(8,128)(2,1)S(1)}, bf16[10,32,128]{2,1,0:T(8,128)(2,1)S(1)}) custom-call(s32[32]{0:T(128)S(1)} %bitcast.2, s32[32]{0:T(128)S(1)} %copy-done.1, bf16[2,2,256,512]{3,2,1,0:T(8,128)(2,1)S(1)} %get-tuple-element.14.refs_0_, ...), custom_call_target="tpu_custom_call" | custom-call | flops 20000000000 | bytes 4194304 | tf_op jit(solution)/shard_map/attend/pallas_call | solution.py:236
  15.6 1.6 %collective-permute-start.4 = (bf16[10,32,128]{2,1,0:T(8,128)(2,1)S(1)}, bf16[10,32,128]{2,1,0:T(8,128)(2,1)S(1)}, u32[]{:S(2)}, u32[]{:S(2)}) collective-permute-start(bf16[10,32,128]{2,1,0:T(8,128)(2,1)S(1)} %get-tuple-element.23), channel_id=1, source_target_pairs={{0,4},{4,0},{8,12},{12,8},{1,5},{5,1},{9,13},{13,9},{2,6},{6,2},{1... | collective-permute-start | bytes 245768 | tf_op jit(solution)/shard_map/ppermute | solution.py:34
  17.2 2.6 %collective-permute-start.5 = (bf16[10,32,128]{2,1,0:T(8,128)(2,1)S(1)}, bf16[10,32,128]{2,1,0:T(8,128)(2,1)S(1)}, u32[]{:S(2)}, u32[]{:S(2)}) collective-permute-start(bf16[10,32,128]{2,1,0:T(8,128)(2,1)S(1)} %get-tuple-element.24), channel_id=1, source_target_pairs={{0,8},{4,12},{8,0},{12,4},{1,9},{5,13},{9,1},{13,5},{2,10},{6,14},... | collective-permute-start | bytes 245768 | tf_op jit(solution)/shard_map/ppermute | solution.py:34
  19.8 0.2 collective-permute-start.6
  20.1 5.9 %fetch.1.refs_4_ = bf16[4096,2048]{1,0:T(8,128)(2,1)S(1)} custom-call(bf16[4096,2048]{1,0:T(8,128)(2,1)} %weight_ref.1, bf16[10,32,128]{2,1,0:T(8,128)(2,1)S(1)} %get-tuple-element.22.refs_0_), custom_call_target="tpu_custom_call" | custom-call | bytes 33554432 | tf_op jit(solution)/shard_map/fetch/pallas_call | solution.py:330
  26.0 0.0 collective-permute-done.4.refs_1_
  26.0 0.7 %collective-permute-done.5.refs_2_ = bf16[10,32,128]{2,1,0:T(8,128)(2,1)S(1)} collective-permute-done((bf16[10,32,128]{2,1,0:T(8,128)(2,1)S(1)}, bf16[10,32,128]{2,1,0:T(8,128)(2,1)S(1)}, u32[]{:S(2)}, u32[]{:S(2)}) %collective-permute-start.5) | collective-permute-done | bytes 81952 | tf_op jit(solution)/shard_map/ppermute | solution.py:34
  26.7 0.0 collective-permute-done.6.refs_3_
  26.7 0.4 join.1.refs_0_
  27.1 1.6 %collective-permute-start.7 = (bf16[8,4096]{1,0:T(8,128)(2,1)S(1)}, bf16[8,4096]{1,0:T(8,128)(2,1)S(1)}, u32[]{:S(2)}, u32[]{:S(2)}) collective-permute-start(bf16[8,4096]{1,0:T(8,128)(2,1)S(1)} %join.1.refs_0_), channel_id=1, source_target_pairs={{0,4},{4,0},{8,12},{12,8},{1,5},{5,1},{9,13},{13,9},{2,6},{6,2},{1... | collective-permute-start | bytes 196616 | tf_op jit(solution)/shard_map/ppermute | solution.py:34
  28.6 2.0 %collective-permute-start.8 = (bf16[8,4096]{1,0:T(8,128)(2,1)S(1)}, bf16[8,4096]{1,0:T(8,128)(2,1)S(1)}, u32[]{:S(2)}, u32[]{:S(2)}) collective-permute-start(bf16[8,4096]{1,0:T(8,128)(2,1)S(1)} %join.1.refs_0_), channel_id=1, source_target_pairs={{0,8},{4,12},{8,0},{12,4},{1,9},{5,13},{9,1},{13,5},{2,10},{6,14},... | collective-permute-start | bytes 196616 | tf_op jit(solution)/shard_map/ppermute | solution.py:34
  30.6 0.9 %collective-permute-start.9 = (bf16[8,4096]{1,0:T(8,128)(2,1)S(1)}, bf16[8,4096]{1,0:T(8,128)(2,1)S(1)}, u32[]{:S(2)}, u32[]{:S(2)}) collective-permute-start(bf16[8,4096]{1,0:T(8,128)(2,1)S(1)} %join.1.refs_0_), channel_id=1, source_target_pairs={{0,12},{4,8},{8,4},{12,0},{1,13},{5,9},{9,5},{13,1},{2,14},{6,10},... | collective-permute-start | bytes 196616 | tf_op jit(solution)/shard_map/ppermute | solution.py:34
  31.5 1.3 %place.3.refs_0_ = bf16[1,8,2,256,512]{4,3,2,1,0:T(8,128)(2,1)} custom-call(bf16[2,2,256,512]{3,2,1,0:T(8,128)(2,1)S(1)} %get-tuple-element.16.refs_2_.refs_0_, bf16[2,2,256,512]{3,2,1,0:T(8,128)(2,1)S(1)} %collective-permute-done.3.refs_8_.refs_1_), custom_call_target="tpu_custom_call" | custom-call | bytes 4194304 | tf_op jit(solution)/shard_map/place/pallas_call | solution.py:136
  32.9 0.0 collective-permute-done.7.refs_1_
  32.9 2.5 %collective-permute-done.8.refs_2_ = bf16[8,4096]{1,0:T(8,128)(2,1)S(1)} collective-permute-done((bf16[8,4096]{1,0:T(8,128)(2,1)S(1)}, bf16[8,4096]{1,0:T(8,128)(2,1)S(1)}, u32[]{:S(2)}, u32[]{:S(2)}) %collective-permute-start.8) | collective-permute-done | bytes 65568 | tf_op jit(solution)/shard_map/ppermute | solution.py:34
  35.4 1.4 %collective-permute-done.9.refs_3_ = bf16[8,4096]{1,0:T(8,128)(2,1)S(1)} collective-permute-done((bf16[8,4096]{1,0:T(8,128)(2,1)S(1)}, bf16[8,4096]{1,0:T(8,128)(2,1)S(1)}, u32[]{:S(2)}, u32[]{:S(2)}) %collective-permute-start.9) | collective-permute-done | bytes 65568 | tf_op jit(solution)/shard_map/ppermute | solution.py:34
  36.8 3.6 %project.1.refs_1_ = bf16[8,4,2048]{2,1,0:T(4,128)(2,1)} custom-call(bf16[8,4096]{1,0:T(8,128)(2,1)S(1)} %join.1.refs_0_, bf16[8,4096]{1,0:T(8,128)(2,1)S(1)} %collective-permute-done.7.refs_1_, bf16[8,4096]{1,0:T(8,128)(2,1)S(1)} %collective-permute-done.8.refs_2_, bf16[8,4096]{1,0:T(8,128)(2,1)S(1)} %collective-permute-done.9.refs_3_, ...), custom_call_target="tpu_custom_call" | custom-call | flops 536870912 | bytes 16777216 | tf_op jit(solution)/shard_map/project/pallas_call | solution.py:361
  40.4 0.0 collective-permute-done.10.refs_2_
  40.4 1.0 %place.4.refs_0_ = bf16[1,8,2,256,512]{4,3,2,1,0:T(8,128)(2,1)} custom-call(bf16[1,8,2,256,512]{4,3,2,1,0:T(8,128)(2,1)} %place.3.refs_0_, bf16[8,4,2048]{2,1,0:T(4,128)(2,1)} %project.1.refs_1_, bf16[2,2,256,512]{3,2,1,0:T(8,128)(2,1)S(1)} %collective-permute-done.10.refs_2_), custom_call_target="tpu_custom_call", output_to_operand_aliasing={{}: (0, {})} | custom-call | bytes 2097152 | tf_op jit(solution)/shard_map/place/pallas_call | solution.py:136
  41.4 15.3 %collective-permute-done.11.refs_2_ = bf16[2,2,256,512]{3,2,1,0:T(8,128)(2,1)S(1)} collective-permute-done((bf16[2,2,256,512]{3,2,1,0:T(8,128)(2,1)S(1)}, bf16[2,2,256,512]{3,2,1,0:T(8,128)(2,1)S(1)}, u32[]{:S(2)}, u32[]{:S(2)}) %collective-permute-start.11) | collective-permute-done | bytes 1048608 | tf_op jit(solution)/shard_map/ppermute | solution.py:34
  56.7 1.0 %place.5 = bf16[1,8,2,256,512]{4,3,2,1,0:T(8,128)(2,1)} custom-call(bf16[1,8,2,256,512]{4,3,2,1,0:T(8,128)(2,1)} %place.4.refs_0_, bf16[8,4,2048]{2,1,0:T(4,128)(2,1)} %project.1.refs_1_, bf16[2,2,256,512]{3,2,1,0:T(8,128)(2,1)S(1)} %collective-permute-done.11.refs_2_), custom_call_target="tpu_custom_call", output_to_operand_aliasing={{}: (0, {})} | custom-call | bytes 2097152 | tf_op jit(solution)/shard_map/place/pallas_call | solution.py:136
  (4 shorter events, 0.0 us)
Async XLA Ops:
  0.6 11.2 %copy-start = (s32[32,1]{0,1:T(1,128)S(1)}, s32[32,1]{0,1:T(1,128)}, u32[]{:S(2)}) copy-start(s32[32,1]{0,1:T(1,128)} %param.7) | copy-start | bytes 388
  0.6 11.2 %copy-start.1 = (s32[32]{0:T(128)S(1)}, s32[32]{0:T(128)}, u32[]{:S(2)}) copy-start(s32[32]{0:T(128)} %lengths_ref.1) | copy-start | bytes 388
  3.9 7.9 %collective-permute-start.3 = (bf16[2,2,256,512]{3,2,1,0:T(8,128)(2,1)S(1)}, bf16[2,2,256,512]{3,2,1,0:T(8,128)(2,1)S(1)}, u32[]{:S(2)}, u32[]{:S(2)}) collective-permute-start(bf16[2,2,256,512]{3,2,1,0:T(8,128)(2,1)S(1)} %get-tuple-element.17.refs_3_), channel_id=1, source_target_pairs={{0,1},{1,0},{2,3},{3,2},{4,5},{5,4},{6,7},{7,6},{8,9},{9,8},{10,11... | collective-permute-start | bytes 3145736 | tf_op jit(solution)/shard_map/ppermute | solution.py:34
  4.4 4.4 %collective-permute-start = (bf16[2,4,4096]{2,1,0:T(4,128)(2,1)S(1)}, bf16[2,4,4096]{2,1,0:T(4,128)(2,1)S(1)}, u32[]{:S(2)}, u32[]{:S(2)}) collective-permute-start(bf16[2,4,4096]{2,1,0:T(4,128)(2,1)S(1)} %get-tuple-element.19), channel_id=1, source_target_pairs={{0,1},{1,0},{2,3},{3,2},{4,5},{5,4},{6,7},{7,6},{8,9},{9,8},{10,11... | collective-permute-start | bytes 196616 | tf_op jit(solution)/shard_map/ppermute | solution.py:34
  4.5 5.3 %collective-permute-start.1 = (bf16[2,4,4096]{2,1,0:T(4,128)(2,1)S(1)}, bf16[2,4,4096]{2,1,0:T(4,128)(2,1)S(1)}, u32[]{:S(2)}, u32[]{:S(2)}) collective-permute-start(bf16[2,4,4096]{2,1,0:T(4,128)(2,1)S(1)} %get-tuple-element.20), channel_id=1, source_target_pairs={{0,2},{1,3},{2,0},{3,1},{4,6},{5,7},{6,4},{7,5},{8,10},{9,11},{10,... | collective-permute-start | bytes 196616 | tf_op jit(solution)/shard_map/ppermute | solution.py:34
  7.4 4.4 %collective-permute-start.2 = (bf16[2,4,4096]{2,1,0:T(4,128)(2,1)S(1)}, bf16[2,4,4096]{2,1,0:T(4,128)(2,1)S(1)}, u32[]{:S(2)}, u32[]{:S(2)}) collective-permute-start(bf16[2,4,4096]{2,1,0:T(4,128)(2,1)S(1)} %get-tuple-element.21), channel_id=1, source_target_pairs={{0,3},{1,2},{2,1},{3,0},{4,7},{5,6},{6,5},{7,4},{8,11},{9,10},{10,... | collective-permute-start | bytes 196616 | tf_op jit(solution)/shard_map/ppermute | solution.py:34
  7.4 33.0 %collective-permute-start.10 = (bf16[2,2,256,512]{3,2,1,0:T(8,128)(2,1)S(1)}, bf16[2,2,256,512]{3,2,1,0:T(8,128)(2,1)S(1)}, u32[]{:S(2)}, u32[]{:S(2)}) collective-permute-start(bf16[2,2,256,512]{3,2,1,0:T(8,128)(2,1)S(1)} %get-tuple-element.14.refs_0_), channel_id=1, source_target_pairs={{0,2},{1,3},{2,0},{3,1},{4,6},{5,7},{6,4},{7,5},{8,10},{9,11},{10,... | collective-permute-start | bytes 3145736 | tf_op jit(solution)/shard_map/ppermute | solution.py:34
  8.8 47.9 %collective-permute-start.11 = (bf16[2,2,256,512]{3,2,1,0:T(8,128)(2,1)S(1)}, bf16[2,2,256,512]{3,2,1,0:T(8,128)(2,1)S(1)}, u32[]{:S(2)}, u32[]{:S(2)}) collective-permute-start(bf16[2,2,256,512]{3,2,1,0:T(8,128)(2,1)S(1)} %get-tuple-element.15.refs_1_), channel_id=1, source_target_pairs={{0,3},{1,2},{2,1},{3,0},{4,7},{5,6},{6,5},{7,4},{8,11},{9,10},{10,... | collective-permute-start | bytes 3145736 | tf_op jit(solution)/shard_map/ppermute | solution.py:34
  15.6 10.4 %collective-permute-start.4 = (bf16[10,32,128]{2,1,0:T(8,128)(2,1)S(1)}, bf16[10,32,128]{2,1,0:T(8,128)(2,1)S(1)}, u32[]{:S(2)}, u32[]{:S(2)}) collective-permute-start(bf16[10,32,128]{2,1,0:T(8,128)(2,1)S(1)} %get-tuple-element.23), channel_id=1, source_target_pairs={{0,4},{4,0},{8,12},{12,8},{1,5},{5,1},{9,13},{13,9},{2,6},{6,2},{1... | collective-permute-start | bytes 245768 | tf_op jit(solution)/shard_map/ppermute | solution.py:34
  17.2 9.4 %collective-permute-start.5 = (bf16[10,32,128]{2,1,0:T(8,128)(2,1)S(1)}, bf16[10,32,128]{2,1,0:T(8,128)(2,1)S(1)}, u32[]{:S(2)}, u32[]{:S(2)}) collective-permute-start(bf16[10,32,128]{2,1,0:T(8,128)(2,1)S(1)} %get-tuple-element.24), channel_id=1, source_target_pairs={{0,8},{4,12},{8,0},{12,4},{1,9},{5,13},{9,1},{13,5},{2,10},{6,14},... | collective-permute-start | bytes 245768 | tf_op jit(solution)/shard_map/ppermute | solution.py:34
  19.8 6.8 %collective-permute-start.6 = (bf16[10,32,128]{2,1,0:T(8,128)(2,1)S(1)}, bf16[10,32,128]{2,1,0:T(8,128)(2,1)S(1)}, u32[]{:S(2)}, u32[]{:S(2)}) collective-permute-start(bf16[10,32,128]{2,1,0:T(8,128)(2,1)S(1)} %get-tuple-element.25), channel_id=1, source_target_pairs={{0,12},{4,8},{8,4},{12,0},{1,13},{5,9},{9,5},{13,1},{2,14},{6,10},... | collective-permute-start | bytes 245768 | tf_op jit(solution)/shard_map/ppermute | solution.py:34
  27.1 5.8 %collective-permute-start.7 = (bf16[8,4096]{1,0:T(8,128)(2,1)S(1)}, bf16[8,4096]{1,0:T(8,128)(2,1)S(1)}, u32[]{:S(2)}, u32[]{:S(2)}) collective-permute-start(bf16[8,4096]{1,0:T(8,128)(2,1)S(1)} %join.1.refs_0_), channel_id=1, source_target_pairs={{0,4},{4,0},{8,12},{12,8},{1,5},{5,1},{9,13},{13,9},{2,6},{6,2},{1... | collective-permute-start | bytes 196616 | tf_op jit(solution)/shard_map/ppermute | solution.py:34
  28.6 6.7 %collective-permute-start.8 = (bf16[8,4096]{1,0:T(8,128)(2,1)S(1)}, bf16[8,4096]{1,0:T(8,128)(2,1)S(1)}, u32[]{:S(2)}, u32[]{:S(2)}) collective-permute-start(bf16[8,4096]{1,0:T(8,128)(2,1)S(1)} %join.1.refs_0_), channel_id=1, source_target_pairs={{0,8},{4,12},{8,0},{12,4},{1,9},{5,13},{9,1},{13,5},{2,10},{6,14},... | collective-permute-start | bytes 196616 | tf_op jit(solution)/shard_map/ppermute | solution.py:34
  30.6 6.1 %collective-permute-start.9 = (bf16[8,4096]{1,0:T(8,128)(2,1)S(1)}, bf16[8,4096]{1,0:T(8,128)(2,1)S(1)}, u32[]{:S(2)}, u32[]{:S(2)}) collective-permute-start(bf16[8,4096]{1,0:T(8,128)(2,1)S(1)} %join.1.refs_0_), channel_id=1, source_target_pairs={{0,12},{4,8},{8,4},{12,0},{1,13},{5,9},{9,5},{13,1},{2,14},{6,10},... | collective-permute-start | bytes 196616 | tf_op jit(solution)/shard_map/ppermute | solution.py:34

commit v6 on v5

--- a/solution.py
+++ b/solution.py
@@ -44,8 +44,10 @@
         source[target * CAP + order] = i
 
 
-def pack_kernel(pieces, section_count, routing_ref, cache_ref, query_ref, *refs):
-    cache_out, query_out, (source, used, sem, query_sem) = refs[: len(pieces)], refs[len(pieces) : -4], refs[-4:]
+def pack_kernel(pieces, shown, section_count, routing_ref, cache_ref, *refs):
+    refs, (source, used, sem, query_sem) = refs[:-4], refs[-4:]
+    cache_out = refs[len(refs) - shown :][: len(pieces)]
+    query_ref, query_out = refs[0], refs[len(refs) - shown + len(pieces) :]
     section = lax.axis_index("sec")
     full = section_count * CAP == REQ_GRP
     query_copies = []
@@ -96,15 +98,16 @@
     return pltpu.with_memory_space_constraint(value, pltpu.HBM)
 
 
-def pack(routing, cache, queries, pieces, section_count):
+def pack(routing, cache, queries, others, pieces, section_count):
     slots = section_count * CAP
     shapes = [jax.ShapeDtypeStruct((count,) + cache.shape[1:], cache.dtype) for _, _, count in pieces]
-    shapes += [jax.ShapeDtypeStruct((CAP,) + queries.shape[2:], queries.dtype)] * section_count
+    for query in queries:
+        shapes += [jax.ShapeDtypeStruct((CAP,) + query.shape[2:], query.dtype)] * section_count
     moved = sum(shape.size for shape in shapes)
     return pl.pallas_call(
-        functools.partial(pack_kernel, pieces, section_count),
+        functools.partial(pack_kernel, pieces, len(shapes), section_count),
         out_shape=shapes,
-        in_specs=[SMEM, HBM, HBM],
+        in_specs=[SMEM, HBM] + [HBM] * len(queries) + [ANY] * len(others),
         out_specs=[VMEM] * len(shapes),
         scratch_shapes=[
             pltpu.SMEM((slots,), jnp.int32),
@@ -115,7 +118,7 @@
         compiler_params=limit(16),
         cost_estimate=cost(0, 4 * moved),
         name="pack",
-    )(in_hbm(routing), in_hbm(cache), in_hbm(queries))
+    )(in_hbm(routing), in_hbm(cache), *[in_hbm(query) for query in queries], *others)
 
 
 def place_kernel(pieces, *refs):
@@ -226,7 +229,7 @@
                 )
 
 
-def attend(routing, lengths, caches, pieces, queries, others, tp_count):
+def attend(routing, lengths, caches, pieces, queries, tp_count):
     section_count = len(queries)
     samples, width = queries[0].shape[1:]
     span = width // HEAD_SIZE * samples
@@ -236,7 +239,7 @@
     return pl.pallas_call(
         functools.partial(attend_kernel, pieces, section_count, tp_count),
         out_shape=[jax.ShapeDtypeStruct((groups + 2, rows, HEAD_SIZE), jnp.bfloat16)] * tp_count,
-        in_specs=[SMEM, SMEM] + [VMEM] * (len(caches) + section_count) + [ANY] * len(others),
+        in_specs=[SMEM, SMEM] + [VMEM] * (len(caches) + section_count),
         out_specs=[VMEM] * tp_count,
         scratch_shapes=[
             pltpu.SMEM((section_count * CAP,), jnp.int32),
@@ -248,7 +251,7 @@
         compiler_params=limit(12),
         cost_estimate=cost(2 * 10**10, 2 * sum(part.size for part in caches), multiplies // HEAD_SIZE),
         name="attend",
-    )(routing, lengths, *caches, *queries, *others)
+    )(routing, lengths, *caches, *queries)
 
 
 def join_kernel(count, samples, *refs):
@@ -377,16 +380,16 @@
 
     near = [(offset, 0, CAP) for offset in range(2)]
     far = [(offset, 0, CAP) for offset in range(2, section_count)]
-    pieces = far + near
-    parts = pack(routing, prompt_key_values, queries, pieces, section_count)
-    caches, query_parts = parts[: len(pieces)], parts[len(pieces) :]
-    own_queries = [swap(part, "sec", offset) for offset, part in enumerate(query_parts)]
-    arrived = [swap(part, "sec", piece[0]) for part, piece in zip(caches, pieces)]
-    far_parts, near_parts = arrived[: len(far)], arrived[len(far) :]
-
-    messages = attend(routing, lengths, caches, pieces, own_queries, near_parts[1:], tp_count)
+    parts = pack(routing, prompt_key_values, [queries], [], far, section_count)
+    far_caches, query_parts = parts[: len(far)], parts[len(far) :]
+    own_queries = [swap(query_parts[offset], "sec", offset) for offset in reversed(range(section_count))][::-1]
+    far_parts = [swap(part, "sec", piece[0]) for part, piece in zip(far_caches, far)]
+    near_caches = pack(routing, prompt_key_values, [], own_queries[1:2], near, section_count)
+    near_parts = [swap(part, "sec", piece[0]) for part, piece in zip(near_caches, near)]
+
+    messages = attend(routing, lengths, [*far_caches, *near_caches], far + near, own_queries, tp_count)
     partials = [swap(part, "tp", offset) for offset, part in enumerate(messages)]
-    held_weight = fetch(out_weight, messages[:1])
+    held_weight = fetch(out_weight, [messages[0], *near_parts[1:]])
     share = join(partials, [held_weight], samples)
     shares = [swap(share, "tp", offset) for offset in range(tp_count)]
     if share.ndim == 3:

time: 57.8 us -> 56.5 us (0.978)
  waiting for transfers between devices: 22.3 us -> 19.3 us
  Pallas kernels: 20.3 us -> 21.9 us
    ppermute x12, waiting for transfers between devices: 22.3 us -> 19.3 us  [swap(): return lax.ppermute(value, axis, [(i, i ^ offset) for i in range(count)])]
    pallas_call x1 -> x2, Pallas kernels: 3.22 us -> 4.92 us  [pack(): pl.pallas_call(functools.partial(pack_kernel, pieces, len(shapes), sectio...]
  transfers between devices with their start and end apart: 12 -> 12, of which waited for: 6 -> 4; matrix products, arithmetic and copies ran while one was open for 0% -> 0% of each run, Pallas kernels for 28% -> 33%
where the time goes in v6:
time: 56.5 us; the launch traced here: 56.3 us
  Pallas kernels  21.9 us (39%)
  waiting for transfers between devices  19.3 us (34%)
  starting transfers between devices  14.3 us (25%)
  between operations  0.74 us (1%)
    ppermute x12, waiting for transfers between devices, swap(): return lax.ppermute(value, axis, [(i, i ^ offset) for i in range(count)])  19.3 us
    ppermute x12, starting transfers between devices, swap(): return lax.ppermute(value, axis, [(i, i ^ offset) for i in range(count)])  14.3 us
    pallas_call x1, Pallas kernels, fetch(): pl.pallas_call(fetch_kernel, out_shape=jax.ShapeDtypeStruct(weight.shape,...  5.92 us
    pallas_call x2, Pallas kernels, pack(): pl.pallas_call(functools.partial(pack_kernel, pieces, len(shapes), sectio...  4.92 us
    pallas_call x1, Pallas kernels, attend(): pl.pallas_call(functools.partial(attend_kernel, pieces, section_count, tp...  3.78 us
    pallas_call x1, Pallas kernels, project(): pl.pallas_call(functools.partial(project_kernel, count, min(256, width)),...  3.64 us
    pallas_call x3, Pallas kernels, place(): pl.pallas_call(functools.partial(place_kernel, pieces), out_shape=jax.Sha...  3.29 us
  transfers between devices with their start and end apart: 12, of which 4 were waited for; matrix products, arithmetic and copies ran while one was open for 0% of the time, Pallas kernels for 33%

profile of v6, /device:TPU:0, one launch (start us, length us, event | category | flops | bytes accessed | tf_op | source)
XLA Modules:
  0.0 56.3 jit_solution(9558190220158730371)
XLA Ops:
  0.6 0.0 copy-start
  0.7 2.6 %pack.2 = (bf16[2,2,256,512]{3,2,1,0:T(8,128)(2,1)S(1)}, bf16[2,2,256,512]{3,2,1,0:T(8,128)(2,1)S(1)}, bf16[2,4,4096]{2,1,0:T(4,128)(2,1)S(1)}, bf16[2,4,4096]{2...) custom-call(s32[32]{0:T(128)} %bitcast.1, bf16[8,2,256,512]{3,2,1,0:T(8,128)(2,1)} %cache_ref.3, ...), custom_call_target="tpu_custom_call" | custom-call | bytes 4718592 | tf_op jit(solution)/shard_map/pack/pallas_call | solution.py:107
  3.2 0.5 collective-permute-start
  3.8 2.6 %collective-permute-start.1 = (bf16[2,4,4096]{2,1,0:T(4,128)(2,1)S(1)}, bf16[2,4,4096]{2,1,0:T(4,128)(2,1)S(1)}, u32[]{:S(2)}, u32[]{:S(2)}) collective-permute-start(bf16[2,4,4096]{2,1,0:T(4,128)(2,1)S(1)} %get-tuple-element.20), channel_id=1, source_target_pairs={{0,2},{1,3},{2,0},{3,1},{4,6},{5,7},{6,4},{7,5},{8,10},{9,11},{10,... | collective-permute-start | bytes 196616 | tf_op jit(solution)/shard_map/ppermute | solution.py:34
  6.3 0.1 collective-permute-start.2
  6.4 1.7 %collective-permute-start.10 = (bf16[2,2,256,512]{3,2,1,0:T(8,128)(2,1)S(1)}, bf16[2,2,256,512]{3,2,1,0:T(8,128)(2,1)S(1)}, u32[]{:S(2)}, u32[]{:S(2)}) collective-permute-start(bf16[2,2,256,512]{3,2,1,0:T(8,128)(2,1)S(1)} %get-tuple-element.14.refs_0_), channel_id=1, source_target_pairs={{0,2},{1,3},{2,0},{3,1},{4,6},{5,7},{6,4},{7,5},{8,10},{9,11},{10,... | collective-permute-start | bytes 3145736 | tf_op jit(solution)/shard_map/ppermute | solution.py:34
  8.1 0.0 collective-permute-start.11
  8.1 0.0 collective-permute-done.refs_0_.refs_5_
  8.1 2.3 %pack.3 = (bf16[2,2,256,512]{3,2,1,0:T(8,128)(2,1)S(1)}, bf16[2,2,256,512]{3,2,1,0:T(8,128)(2,1)S(1)}) custom-call(s32[32]{0:T(128)} %bitcast.2, bf16[8,2,256,512]{3,2,1,0:T(8,128)(2,1)} %cache_ref.3, bf16[2,4,4096]{2,1,0:T(4,128)(2,1)S(1)} %collective-permute-done.refs_0_.refs_5_), custom_call_target="tpu_custom_call" | custom-call | bytes 4194304 | tf_op jit(solution)/shard_map/pack/pallas_call | solution.py:107
  10.5 0.5 collective-permute-start.6
  11.0 0.0 collective-permute-done.1.refs_6_
  11.0 0.0 collective-permute-done.2.refs_7_
  11.0 3.8 %attend.1 = (bf16[10,32,128]{2,1,0:T(8,128)(2,1)S(1)}, bf16[10,32,128]{2,1,0:T(8,128)(2,1)S(1)}, bf16[10,32,128]{2,1,0:T(8,128)(2,1)S(1)}, bf16[10,32,128]{2,1,0:T(8,128)(2,1)S(1)}) custom-call(s32[32]{0:T(128)S(1)} %bitcast.3, s32[32]{0:T(128)S(1)} %copy-done.1, bf16[2,2,256,512]{3,2,1,0:T(8,128)(2,1)S(1)} %get-tuple-element.14.refs_0_, ...), custom_call_target="tpu_custom_call" | custom-call | flops 20000000000 | bytes 4194304 | tf_op jit(solution)/shard_map/attend/pallas_call | solution.py:239
  14.8 1.9 %collective-permute-start.3 = (bf16[10,32,128]{2,1,0:T(8,128)(2,1)S(1)}, bf16[10,32,128]{2,1,0:T(8,128)(2,1)S(1)}, u32[]{:S(2)}, u32[]{:S(2)}) collective-permute-start(bf16[10,32,128]{2,1,0:T(8,128)(2,1)S(1)} %get-tuple-element.23), channel_id=1, source_target_pairs={{0,4},{4,0},{8,12},{12,8},{1,5},{5,1},{9,13},{13,9},{2,6},{6,2},{1... | collective-permute-start | bytes 245768 | tf_op jit(solution)/shard_map/ppermute | solution.py:34
  16.6 2.6 %collective-permute-start.4 = (bf16[10,32,128]{2,1,0:T(8,128)(2,1)S(1)}, bf16[10,32,128]{2,1,0:T(8,128)(2,1)S(1)}, u32[]{:S(2)}, u32[]{:S(2)}) collective-permute-start(bf16[10,32,128]{2,1,0:T(8,128)(2,1)S(1)} %get-tuple-element.24), channel_id=1, source_target_pairs={{0,8},{4,12},{8,0},{12,4},{1,9},{5,13},{9,1},{13,5},{2,10},{6,14},... | collective-permute-start | bytes 245768 | tf_op jit(solution)/shard_map/ppermute | solution.py:34
  19.2 0.0 collective-permute-done.6.refs_1_
  19.2 0.0 collective-permute-start.5
  19.2 5.9 %fetch.1.refs_4_ = bf16[4096,2048]{1,0:T(8,128)(2,1)S(1)} custom-call(bf16[4096,2048]{1,0:T(8,128)(2,1)} %weight_ref.1, bf16[10,32,128]{2,1,0:T(8,128)(2,1)S(1)} %get-tuple-element.22.refs_0_, bf16[2,2,256,512]{3,2,1,0:T(8,128)(2,1)S(1)} %collective-permute-done.6.refs_1_), custom_call_target="tpu_custom_call" | custom-call | bytes 33554432 | tf_op jit(solution)/shard_map/fetch/pallas_call | solution.py:333
  25.2 0.9 %collective-permute-done.4.refs_2_ = bf16[10,32,128]{2,1,0:T(8,128)(2,1)S(1)} collective-permute-done((bf16[10,32,128]{2,1,0:T(8,128)(2,1)S(1)}, bf16[10,32,128]{2,1,0:T(8,128)(2,1)S(1)}, u32[]{:S(2)}, u32[]{:S(2)}) %collective-permute-start.4) | collective-permute-done | bytes 81952 | tf_op jit(solution)/shard_map/ppermute | solution.py:34
  26.1 0.0 collective-permute-done.5.refs_3_
  26.1 0.4 join.1.refs_0_
  26.5 1.6 %collective-permute-start.7 = (bf16[8,4096]{1,0:T(8,128)(2,1)S(1)}, bf16[8,4096]{1,0:T(8,128)(2,1)S(1)}, u32[]{:S(2)}, u32[]{:S(2)}) collective-permute-start(bf16[8,4096]{1,0:T(8,128)(2,1)S(1)} %join.1.refs_0_), channel_id=1, source_target_pairs={{0,4},{4,0},{8,12},{12,8},{1,5},{5,1},{9,13},{13,9},{2,6},{6,2},{1... | collective-permute-start | bytes 196616 | tf_op jit(solution)/shard_map/ppermute | solution.py:34
  28.0 2.0 %collective-permute-start.8 = (bf16[8,4096]{1,0:T(8,128)(2,1)S(1)}, bf16[8,4096]{1,0:T(8,128)(2,1)S(1)}, u32[]{:S(2)}, u32[]{:S(2)}) collective-permute-start(bf16[8,4096]{1,0:T(8,128)(2,1)S(1)} %join.1.refs_0_), channel_id=1, source_target_pairs={{0,8},{4,12},{8,0},{12,4},{1,9},{5,13},{9,1},{13,5},{2,10},{6,14},... | collective-permute-start | bytes 196616 | tf_op jit(solution)/shard_map/ppermute | solution.py:34
  30.0 0.9 %collective-permute-start.9 = (bf16[8,4096]{1,0:T(8,128)(2,1)S(1)}, bf16[8,4096]{1,0:T(8,128)(2,1)S(1)}, u32[]{:S(2)}, u32[]{:S(2)}) collective-permute-start(bf16[8,4096]{1,0:T(8,128)(2,1)S(1)} %join.1.refs_0_), channel_id=1, source_target_pairs={{0,12},{4,8},{8,4},{12,0},{1,13},{5,9},{9,5},{13,1},{2,14},{6,10},... | collective-permute-start | bytes 196616 | tf_op jit(solution)/shard_map/ppermute | solution.py:34
  30.9 1.3 %place.3.refs_0_ = bf16[1,8,2,256,512]{4,3,2,1,0:T(8,128)(2,1)} custom-call(bf16[2,2,256,512]{3,2,1,0:T(8,128)(2,1)S(1)} %get-tuple-element.17.refs_2_.refs_0_, bf16[2,2,256,512]{3,2,1,0:T(8,128)(2,1)S(1)} %collective-permute-done.6.refs_1_), custom_call_target="tpu_custom_call" | custom-call | bytes 4194304 | tf_op jit(solution)/shard_map/place/pallas_call | solution.py:139
  32.3 0.0 collective-permute-done.7.refs_1_
  32.3 2.5 %collective-permute-done.8.refs_2_ = bf16[8,4096]{1,0:T(8,128)(2,1)S(1)} collective-permute-done((bf16[8,4096]{1,0:T(8,128)(2,1)S(1)}, bf16[8,4096]{1,0:T(8,128)(2,1)S(1)}, u32[]{:S(2)}, u32[]{:S(2)}) %collective-permute-start.8) | collective-permute-done | bytes 65568 | tf_op jit(solution)/shard_map/ppermute | solution.py:34
  34.7 1.4 %collective-permute-done.9.refs_3_ = bf16[8,4096]{1,0:T(8,128)(2,1)S(1)} collective-permute-done((bf16[8,4096]{1,0:T(8,128)(2,1)S(1)}, bf16[8,4096]{1,0:T(8,128)(2,1)S(1)}, u32[]{:S(2)}, u32[]{:S(2)}) %collective-permute-start.9) | collective-permute-done | bytes 65568 | tf_op jit(solution)/shard_map/ppermute | solution.py:34
  36.2 3.6 %project.1.refs_1_ = bf16[8,4,2048]{2,1,0:T(4,128)(2,1)} custom-call(bf16[8,4096]{1,0:T(8,128)(2,1)S(1)} %join.1.refs_0_, bf16[8,4096]{1,0:T(8,128)(2,1)S(1)} %collective-permute-done.7.refs_1_, bf16[8,4096]{1,0:T(8,128)(2,1)S(1)} %collective-permute-done.8.refs_2_, bf16[8,4096]{1,0:T(8,128)(2,1)S(1)} %collective-permute-done.9.refs_3_, ...), custom_call_target="tpu_custom_call" | custom-call | flops 536870912 | bytes 16777216 | tf_op jit(solution)/shard_map/project/pallas_call | solution.py:364
  39.8 1.0 %place.4.refs_0_ = bf16[1,8,2,256,512]{4,3,2,1,0:T(8,128)(2,1)} custom-call(bf16[1,8,2,256,512]{4,3,2,1,0:T(8,128)(2,1)} %place.3.refs_0_, bf16[8,4,2048]{2,1,0:T(4,128)(2,1)} %project.1.refs_1_, bf16[2,2,256,512]{3,2,1,0:T(8,128)(2,1)S(1)} %collective-permute-done.10.refs_2_), custom_call_target="tpu_custom_call", output_to_operand_aliasing={{}: (0, {})} | custom-call | bytes 2097152 | tf_op jit(solution)/shard_map/place/pallas_call | solution.py:139
  40.8 14.5 %collective-permute-done.11.refs_2_ = bf16[2,2,256,512]{3,2,1,0:T(8,128)(2,1)S(1)} collective-permute-done((bf16[2,2,256,512]{3,2,1,0:T(8,128)(2,1)S(1)}, bf16[2,2,256,512]{3,2,1,0:T(8,128)(2,1)S(1)}, u32[]{:S(2)}, u32[]{:S(2)}) %collective-permute-start.11) | collective-permute-done | bytes 1048608 | tf_op jit(solution)/shard_map/ppermute | solution.py:34
  55.3 1.0 %place.5 = bf16[1,8,2,256,512]{4,3,2,1,0:T(8,128)(2,1)} custom-call(bf16[1,8,2,256,512]{4,3,2,1,0:T(8,128)(2,1)} %place.4.refs_0_, bf16[8,4,2048]{2,1,0:T(4,128)(2,1)} %project.1.refs_1_, bf16[2,2,256,512]{3,2,1,0:T(8,128)(2,1)S(1)} %collective-permute-done.11.refs_2_), custom_call_target="tpu_custom_call", output_to_operand_aliasing={{}: (0, {})} | custom-call | bytes 2097152 | tf_op jit(solution)/shard_map/place/pallas_call | solution.py:139
  (5 shorter events, 0.0 us)
Async XLA Ops:
  0.6 10.3 %copy-start = (s32[32,1]{0,1:T(1,128)S(1)}, s32[32,1]{0,1:T(1,128)}, u32[]{:S(2)}) copy-start(s32[32,1]{0,1:T(1,128)} %param.7) | copy-start | bytes 388
  0.6 10.3 %copy-start.1 = (s32[32]{0:T(128)S(1)}, s32[32]{0:T(128)}, u32[]{:S(2)}) copy-start(s32[32]{0:T(128)} %lengths_ref.1) | copy-start | bytes 388
  3.2 4.9 %collective-permute-start = (bf16[2,4,4096]{2,1,0:T(4,128)(2,1)S(1)}, bf16[2,4,4096]{2,1,0:T(4,128)(2,1)S(1)}, u32[]{:S(2)}, u32[]{:S(2)}) collective-permute-start(bf16[2,4,4096]{2,1,0:T(4,128)(2,1)S(1)} %get-tuple-element.16), channel_id=1, source_target_pairs={{0,1},{1,0},{2,3},{3,2},{4,5},{5,4},{6,7},{7,6},{8,9},{9,8},{10,11... | collective-permute-start | bytes 196616 | tf_op jit(solution)/shard_map/ppermute | solution.py:34
  3.8 7.2 %collective-permute-start.1 = (bf16[2,4,4096]{2,1,0:T(4,128)(2,1)S(1)}, bf16[2,4,4096]{2,1,0:T(4,128)(2,1)S(1)}, u32[]{:S(2)}, u32[]{:S(2)}) collective-permute-start(bf16[2,4,4096]{2,1,0:T(4,128)(2,1)S(1)} %get-tuple-element.20), channel_id=1, source_target_pairs={{0,2},{1,3},{2,0},{3,1},{4,6},{5,7},{6,4},{7,5},{8,10},{9,11},{10,... | collective-permute-start | bytes 196616 | tf_op jit(solution)/shard_map/ppermute | solution.py:34
  6.3 4.6 %collective-permute-start.2 = (bf16[2,4,4096]{2,1,0:T(4,128)(2,1)S(1)}, bf16[2,4,4096]{2,1,0:T(4,128)(2,1)S(1)}, u32[]{:S(2)}, u32[]{:S(2)}) collective-permute-start(bf16[2,4,4096]{2,1,0:T(4,128)(2,1)S(1)} %get-tuple-element.21), channel_id=1, source_target_pairs={{0,3},{1,2},{2,1},{3,0},{4,7},{5,6},{6,5},{7,4},{8,11},{9,10},{10,... | collective-permute-start | bytes 196616 | tf_op jit(solution)/shard_map/ppermute | solution.py:34
  6.4 33.4 %collective-permute-start.10 = (bf16[2,2,256,512]{3,2,1,0:T(8,128)(2,1)S(1)}, bf16[2,2,256,512]{3,2,1,0:T(8,128)(2,1)S(1)}, u32[]{:S(2)}, u32[]{:S(2)}) collective-permute-start(bf16[2,2,256,512]{3,2,1,0:T(8,128)(2,1)S(1)} %get-tuple-element.14.refs_0_), channel_id=1, source_target_pairs={{0,2},{1,3},{2,0},{3,1},{4,6},{5,7},{6,4},{7,5},{8,10},{9,11},{10,... | collective-permute-start | bytes 3145736 | tf_op jit(solution)/shard_map/ppermute | solution.py:34
  8.1 47.2 %collective-permute-start.11 = (bf16[2,2,256,512]{3,2,1,0:T(8,128)(2,1)S(1)}, bf16[2,2,256,512]{3,2,1,0:T(8,128)(2,1)S(1)}, u32[]{:S(2)}, u32[]{:S(2)}) collective-permute-start(bf16[2,2,256,512]{3,2,1,0:T(8,128)(2,1)S(1)} %get-tuple-element.15.refs_1_), channel_id=1, source_target_pairs={{0,3},{1,2},{2,1},{3,0},{4,7},{5,6},{6,5},{7,4},{8,11},{9,10},{10,... | collective-permute-start | bytes 3145736 | tf_op jit(solution)/shard_map/ppermute | solution.py:34
  10.5 8.7 %collective-permute-start.6 = (bf16[2,2,256,512]{3,2,1,0:T(8,128)(2,1)S(1)}, bf16[2,2,256,512]{3,2,1,0:T(8,128)(2,1)S(1)}, u32[]{:S(2)}, u32[]{:S(2)}) collective-permute-start(bf16[2,2,256,512]{3,2,1,0:T(8,128)(2,1)S(1)} %get-tuple-element.18.refs_3_), channel_id=1, source_target_pairs={{0,1},{1,0},{2,3},{3,2},{4,5},{5,4},{6,7},{7,6},{8,9},{9,8},{10,11... | collective-permute-start | bytes 3145736 | tf_op jit(solution)/shard_map/ppermute | solution.py:34
  14.8 10.4 %collective-permute-start.3 = (bf16[10,32,128]{2,1,0:T(8,128)(2,1)S(1)}, bf16[10,32,128]{2,1,0:T(8,128)(2,1)S(1)}, u32[]{:S(2)}, u32[]{:S(2)}) collective-permute-start(bf16[10,32,128]{2,1,0:T(8,128)(2,1)S(1)} %get-tuple-element.23), channel_id=1, source_target_pairs={{0,4},{4,0},{8,12},{12,8},{1,5},{5,1},{9,13},{13,9},{2,6},{6,2},{1... | collective-permute-start | bytes 245768 | tf_op jit(solution)/shard_map/ppermute | solution.py:34
  16.6 9.4 %collective-permute-start.4 = (bf16[10,32,128]{2,1,0:T(8,128)(2,1)S(1)}, bf16[10,32,128]{2,1,0:T(8,128)(2,1)S(1)}, u32[]{:S(2)}, u32[]{:S(2)}) collective-permute-start(bf16[10,32,128]{2,1,0:T(8,128)(2,1)S(1)} %get-tuple-element.24), channel_id=1, source_target_pairs={{0,8},{4,12},{8,0},{12,4},{1,9},{5,13},{9,1},{13,5},{2,10},{6,14},... | collective-permute-start | bytes 245768 | tf_op jit(solution)/shard_map/ppermute | solution.py:34
  19.2 6.8 %collective-permute-start.5 = (bf16[10,32,128]{2,1,0:T(8,128)(2,1)S(1)}, bf16[10,32,128]{2,1,0:T(8,128)(2,1)S(1)}, u32[]{:S(2)}, u32[]{:S(2)}) collective-permute-start(bf16[10,32,128]{2,1,0:T(8,128)(2,1)S(1)} %get-tuple-element.25), channel_id=1, source_target_pairs={{0,12},{4,8},{8,4},{12,0},{1,13},{5,9},{9,5},{13,1},{2,14},{6,10},... | collective-permute-start | bytes 245768 | tf_op jit(solution)/shard_map/ppermute | solution.py:34
  26.5 5.8 %collective-permute-start.7 = (bf16[8,4096]{1,0:T(8,128)(2,1)S(1)}, bf16[8,4096]{1,0:T(8,128)(2,1)S(1)}, u32[]{:S(2)}, u32[]{:S(2)}) collective-permute-start(bf16[8,4096]{1,0:T(8,128)(2,1)S(1)} %join.1.refs_0_), channel_id=1, source_target_pairs={{0,4},{4,0},{8,12},{12,8},{1,5},{5,1},{9,13},{13,9},{2,6},{6,2},{1... | collective-permute-start | bytes 196616 | tf_op jit(solution)/shard_map/ppermute | solution.py:34
  28.0 6.7 %collective-permute-start.8 = (bf16[8,4096]{1,0:T(8,128)(2,1)S(1)}, bf16[8,4096]{1,0:T(8,128)(2,1)S(1)}, u32[]{:S(2)}, u32[]{:S(2)}) collective-permute-start(bf16[8,4096]{1,0:T(8,128)(2,1)S(1)} %join.1.refs_0_), channel_id=1, source_target_pairs={{0,8},{4,12},{8,0},{12,4},{1,9},{5,13},{9,1},{13,5},{2,10},{6,14},... | collective-permute-start | bytes 196616 | tf_op jit(solution)/shard_map/ppermute | solution.py:34
  30.0 6.1 %collective-permute-start.9 = (bf16[8,4096]{1,0:T(8,128)(2,1)S(1)}, bf16[8,4096]{1,0:T(8,128)(2,1)S(1)}, u32[]{:S(2)}, u32[]{:S(2)}) collective-permute-start(bf16[8,4096]{1,0:T(8,128)(2,1)S(1)} %join.1.refs_0_), channel_id=1, source_target_pairs={{0,12},{4,8},{8,4},{12,0},{1,13},{5,9},{9,5},{13,1},{2,14},{6,10},... | collective-permute-start | bytes 196616 | tf_op jit(solution)/shard_map/ppermute | solution.py:34

commit v7 on v5

--- a/solution.py
+++ b/solution.py
@@ -32,6 +32,13 @@
         return value
     count = lax.axis_size(axis)
     return lax.ppermute(value, axis, [(i, i ^ offset) for i in range(count)])
+
+
+def spread(value, axis):
+    values = [value]
+    while len(values) < lax.axis_size(axis):
+        values += [swap(one, axis, len(values)) for one in values]
+    return values
 
 
 def own_slots(routing_ref, section, used, source):
@@ -44,78 +51,121 @@
         source[target * CAP + order] = i
 
 
-def pack_kernel(pieces, section_count, routing_ref, cache_ref, query_ref, *refs):
-    cache_out, query_out, (source, used, sem, query_sem) = refs[: len(pieces)], refs[len(pieces) : -4], refs[-4:]
-    section = lax.axis_index("sec")
-    full = section_count * CAP == REQ_GRP
-    query_copies = []
-    for offset, out_ref in enumerate(query_out):
-        part = query_ref.at[0, pl.ds((section ^ offset) * CAP, CAP)]
-        query_copies.append(pltpu.make_async_copy(part, out_ref, query_sem.at[offset]))
-        query_copies[-1].start()
-    own_slots(routing_ref, section, used, source)
-
-    def copy(n, spot, row):
-        offset, order, place = spot
-        return pltpu.make_async_copy(cache_ref.at[row], cache_out[n].at[place], sem.at[offset * CAP + order])
-
-    spots = [
-        (n, (offset, first + place, place))
+def pack_slots(pieces, section_count):
+    return [
+        (n, place, offset, first + place)
         for n, (offset, first, count) in enumerate(pieces)
         for place in range(count)
     ]
-    for n, spot in spots:
-        offset, order, place = spot
+
+
+def start_packing(pieces, section_count, routing_ref, cache_ref, out_refs, source, used, sem):
+    section = lax.axis_index("sec")
+    full = section_count * CAP == REQ_GRP
+    own_slots(routing_ref, section, used, source)
+    spots = pack_slots(pieces, section_count)
+
+    def copy(n, place, offset, order, row):
+        return pltpu.make_async_copy(cache_ref.at[row], out_refs[n].at[place], sem.at[offset * CAP + order])
+
+    for n, place, offset, order in spots:
         target = section ^ offset
         if full:
-            copy(n, spot, source[target * CAP + order]).start()
+            copy(n, place, offset, order, source[target * CAP + order]).start()
         else:
 
             @pl.when(order < used[target])
             def _():
-                copy(n, spot, source[target * CAP + order]).start()
+                copy(n, place, offset, order, source[target * CAP + order]).start()
 
             @pl.when(order >= used[target])
             def _():
-                cache_out[n][place] = jnp.zeros_like(cache_out[n][place])
-
-    for n, spot in spots:
-        if full:
-            copy(n, spot, 0).wait()
-        else:
-
-            @pl.when(spot[1] < used[section ^ spot[0]])
-            def _():
-                copy(n, spot, 0).wait()
-
-    for query_copy in query_copies:
-        query_copy.wait()
+                out_refs[n][place] = jnp.zeros_like(out_refs[n][place])
+
+    def finish():
+        for n, place, offset, order in spots:
+            if full:
+                copy(n, place, offset, order, 0).wait()
+            else:
+
+                @pl.when(order < used[section ^ offset])
+                def _():
+                    copy(n, place, offset, order, 0).wait()
+
+    return finish
+
+
+def first_pack_kernel(pieces, section_count, routing_ref, cache_ref, query_ref, *refs):
+    cache_out, query_out = refs[: len(pieces)], refs[len(pieces) : -4]
+    source, used, sem, query_sem = refs[-4:]
+    section = lax.axis_index("sec")
+    query_copies = []
+    for offset, out_ref in enumerate(query_out):
+        width = out_ref.shape[2]
+        columns = pl.ds(pl.multiple_of(lax.axis_index("tp") * width, width) if offset > 1 else 0, width)
+        part = query_ref.at[0, pl.ds((section ^ offset) * CAP, CAP), :, columns]
+        query_copies.append(pltpu.make_async_copy(part, out_ref, query_sem.at[offset]))
+        query_copies[-1].start()
+    finish = start_packing(pieces, section_count, routing_ref, cache_ref, cache_out, source, used, sem)
+    finish()
+    for copy in query_copies:
+        copy.wait()
+
+
+def second_pack_kernel(pieces, section_count, routing_ref, cache_ref, *refs):
+    source, used, sem = refs[-3:]
+    cache_out, merged_ref, query_refs = refs[-4 - len(pieces) : -4], refs[-4], refs[: -4 - len(pieces)]
+    finish = start_packing(pieces, section_count, routing_ref, cache_ref, cache_out, source, used, sem)
+    for n, query_ref in enumerate(query_refs):
+        merged_ref[n] = query_ref[...]
+    finish()
 
 
 def in_hbm(value):
     return pltpu.with_memory_space_constraint(value, pltpu.HBM)
 
 
-def pack(routing, cache, queries, pieces, section_count):
-    slots = section_count * CAP
+def first_pack(routing, cache, queries, pieces, section_count, tp_count):
+    samples, width = queries.shape[2:]
+    widths = [width if offset < 2 else width // tp_count for offset in range(section_count)]
     shapes = [jax.ShapeDtypeStruct((count,) + cache.shape[1:], cache.dtype) for _, _, count in pieces]
-    shapes += [jax.ShapeDtypeStruct((CAP,) + queries.shape[2:], queries.dtype)] * section_count
-    moved = sum(shape.size for shape in shapes)
-    return pl.pallas_call(
-        functools.partial(pack_kernel, pieces, section_count),
+    shapes += [jax.ShapeDtypeStruct((CAP, samples, one), queries.dtype) for one in widths]
+    parts = pl.pallas_call(
+        functools.partial(first_pack_kernel, pieces, section_count),
         out_shape=shapes,
         in_specs=[SMEM, HBM, HBM],
         out_specs=[VMEM] * len(shapes),
         scratch_shapes=[
-            pltpu.SMEM((slots,), jnp.int32),
+            pltpu.SMEM((section_count * CAP,), jnp.int32),
             pltpu.SMEM((section_count,), jnp.int32),
-            pltpu.SemaphoreType.DMA((slots,)),
+            pltpu.SemaphoreType.DMA((section_count * CAP,)),
             pltpu.SemaphoreType.DMA((section_count,)),
         ],
         compiler_params=limit(16),
-        cost_estimate=cost(0, 4 * moved),
-        name="pack",
+        cost_estimate=cost(0, 4 * sum(shape.size for shape in shapes)),
+        name="first_pack",
     )(in_hbm(routing), in_hbm(cache), in_hbm(queries))
+    return parts[: len(pieces)], parts[len(pieces) :]
+
+
+def second_pack(routing, cache, queries, pieces, section_count):
+    shapes = [jax.ShapeDtypeStruct((count,) + cache.shape[1:], cache.dtype) for _, _, count in pieces]
+    merged = jax.ShapeDtypeStruct((len(queries),) + queries[0].shape, queries[0].dtype)
+    *parts, merged = pl.pallas_call(
+        functools.partial(second_pack_kernel, pieces, section_count),
+        out_shape=shapes + [merged],
+        in_specs=[SMEM, HBM] + [VMEM] * len(queries),
+        out_specs=[VMEM] * (len(shapes) + 1),
+        scratch_shapes=[
+            pltpu.SMEM((section_count * CAP,), jnp.int32),
+            pltpu.SMEM((section_count,), jnp.int32),
+            pltpu.SemaphoreType.DMA((section_count * CAP,)),
+        ],
+        compiler_params=limit(16),
+        cost_estimate=cost(0, 10**8),
+        name="second_pack",
+    )(in_hbm(routing), in_hbm(cache), *queries)
+    return parts, merged
 
 
 def place_kernel(pieces, *refs):
@@ -139,7 +189,7 @@
         in_specs=[HBM] * len(given) + [VMEM] * len(parts),
         out_specs=HBM,
         scratch_shapes=[pltpu.SemaphoreType.DMA((len(parts),))],
-        input_output_aliases={0: 0} if given else {},
+        input_output_aliases={0: 0} if len(given) > 1 else {},
         compiler_params=limit(8),
         cost_estimate=cost(0, 4 * sum(piece.size for piece in parts)),
         name="place",
@@ -147,9 +197,10 @@
 
 
 def attend_kernel(pieces, section_count, tp_count, routing_ref, lengths_ref, *refs):
-    cache_refs, query_refs = refs[: len(pieces)], refs[len(pieces) : len(pieces) + section_count]
-    message_refs = refs[-5 - tp_count : -5]
-    source, used, messages, stats, stacked = refs[-5:]
+    cache_refs, refs = refs[: len(pieces)], refs[len(pieces) :]
+    query_refs, far_refs = refs[:2], refs[2 : 2 + tp_count]
+    message_refs = refs[2 + tp_count : 2 + 2 * tp_count]
+    source, used, messages, stats, stacked, far_queries = refs[2 + 2 * tp_count :]
     section = lax.axis_index("sec")
     tp_index = lax.axis_index("tp")
     local = cache_refs[0].shape[2]
@@ -158,17 +209,24 @@
     prompts = max(1, groups // KEY_VALUE_HEADS)
     full = section_count * CAP == REQ_GRP
     own_slots(routing_ref, section, used, source)
+    samples = query_refs[0].shape[1]
+    for offset, far_ref in enumerate(far_refs):
+        far_queries[tp_index ^ offset] = far_ref[...]
     position = lax.broadcasted_iota(jnp.int32, (local, span), 0) + tp_index * local
     owner = lax.broadcasted_iota(jnp.int32, (HEAD_SIZE, span), 1) // rows
 
     def prompt(cache_ref, place, offset, order):
         row = source[(section ^ offset) * CAP + order]
         visible = position < lengths_ref[section * REQ_GRP + row]
-        values = query_refs[offset][order].astype(jnp.float32)
-        samples = values.shape[0]
         slot = offset * CAP + order
         for head in range(span // samples):
-            stacked[slot, head * samples : (head + 1) * samples] = values[:, head * HEAD_SIZE : (head + 1) * HEAD_SIZE]
+            first, part = head * HEAD_SIZE, far_queries.shape[-1]
+            if offset < 2:
+                values = query_refs[offset][order, :, first : first + HEAD_SIZE]
+            else:
+                inner = first % part
+                values = far_queries[first // part, offset - 2, order, :, inner : inner + HEAD_SIZE]
+            stacked[slot, head * samples : (head + 1) * samples] = values.astype(jnp.float32)
         query = stacked[slot].T.astype(jnp.bfloat16)
         query = [jnp.where(owner == k, query, jnp.zeros_like(query)) for k in range(KEY_VALUE_HEADS)]
         score = jnp.dot(
@@ -226,8 +284,9 @@
                 )
 
 
-def attend(routing, lengths, caches, pieces, queries, others, tp_count):
-    section_count = len(queries)
+def attend(routing, lengths, caches, pieces, queries, far_queries):
+    section_count = len(far_queries[0]) + 2
+    tp_count = len(far_queries)
     samples, width = queries[0].shape[1:]
     span = width // HEAD_SIZE * samples
     rows = span // KEY_VALUE_HEADS
@@ -236,7 +295,7 @@
     return pl.pallas_call(
         functools.partial(attend_kernel, pieces, section_count, tp_count),
         out_shape=[jax.ShapeDtypeStruct((groups + 2, rows, HEAD_SIZE), jnp.bfloat16)] * tp_count,
-        in_specs=[SMEM, SMEM] + [VMEM] * (len(caches) + section_count) + [ANY] * len(others),
+        in_specs=[SMEM, SMEM] + [VMEM] * (len(caches) + len(queries) + tp_count),
         out_specs=[VMEM] * tp_count,
         scratch_shapes=[
             pltpu.SMEM((section_count * CAP,), jnp.int32),
@@ -244,11 +303,12 @@
             pltpu.VMEM((tp_count, groups, rows, HEAD_SIZE), jnp.bfloat16),
             pltpu.VMEM((REQ_GRP, span), jnp.float32),
             pltpu.VMEM((section_count * CAP, span, HEAD_SIZE), jnp.float32),
+            pltpu.VMEM((tp_count,) + far_queries[0].shape, far_queries[0].dtype),
         ],
         compiler_params=limit(12),
-        cost_estimate=cost(2 * 10**10, 2 * sum(part.size for part in caches), multiplies // HEAD_SIZE),
+        cost_estimate=cost(4 * multiplies, 2 * sum(part.size for part in caches), multiplies // HEAD_SIZE),
         name="attend",
-    )(routing, lengths, *caches, *queries, *others)
+    )(routing, lengths, *caches, *queries, *far_queries)
 
 
 def join_kernel(count, samples, *refs):
@@ -377,18 +437,22 @@
 
     near = [(offset, 0, CAP) for offset in range(2)]
     far = [(offset, 0, CAP) for offset in range(2, section_count)]
-    pieces = far + near
-    parts = pack(routing, prompt_key_values, queries, pieces, section_count)
-    caches, query_parts = parts[: len(pieces)], parts[len(pieces) :]
-    own_queries = [swap(part, "sec", offset) for offset, part in enumerate(query_parts)]
+    early, late = far[:1], far[1:] + near
+    early_caches, query_parts = first_pack(
+        routing, prompt_key_values, queries, early, section_count, tp_count
+    )
+    query_parts = [swap(part, "sec", offset) for offset, part in enumerate(query_parts)]
+    late_caches, merged = second_pack(routing, prompt_key_values, query_parts[2:], late, section_count)
+    far_queries = spread(merged, "tp")
+    caches, pieces = [*early_caches, *late_caches], early + late
     arrived = [swap(part, "sec", piece[0]) for part, piece in zip(caches, pieces)]
     far_parts, near_parts = arrived[: len(far)], arrived[len(far) :]
 
-    messages = attend(routing, lengths, caches, pieces, own_queries, near_parts[1:], tp_count)
+    messages = attend(routing, lengths, caches, pieces, query_parts[:2], far_queries)
     partials = [swap(part, "tp", offset) for offset, part in enumerate(messages)]
     held_weight = fetch(out_weight, messages[:1])
     share = join(partials, [held_weight], samples)
-    shares = [swap(share, "tp", offset) for offset in range(tp_count)]
+    shares = spread(share, "tp")
     if share.ndim == 3:
         attended = jnp.stack(shares)[jnp.arange(tp_count) ^ lax.axis_index("tp")]
         attended = attended.reshape(REQ_GRP, KEY_VALUE_HEADS, samples, -1).transpose(0, 2, 1, 3)
@@ -398,10 +462,12 @@
     else:
         layer_out = project(shares, held_weight, samples)
 
-    whole = place([], near_parts, near, slot_count)
-    for part, piece in zip(far_parts, far):
-        whole = place([whole, layer_out], [part], [piece], slot_count)
-    return (layer_out, whole)
+    stages = [([part], [piece]) for part, piece in zip(far_parts, far)]
+    stages.insert(-1, (near_parts, near))
+    whole = []
+    for parts, pieces in stages:
+        whole = [place(whole + [layer_out], parts, pieces, slot_count)]
+    return (layer_out, *whole)
 
 
 def solution(mesh):

time: 57.8 us -> 61.6 us (1.066)
  starting transfers between devices: 14.4 us -> 21.6 us
  waiting for transfers between devices: 22.3 us -> 17.2 us
  Pallas kernels: 20.3 us -> 21.9 us
    ppermute x12 -> x15, starting transfers between devices: 14.4 us -> 21.6 us  [swap(): return lax.ppermute(value, axis, [(i, i ^ offset) for i in range(count)])]
    ppermute x12 -> x15, waiting for transfers between devices: 22.3 us -> 17.2 us  [swap(): return lax.ppermute(value, axis, [(i, i ^ offset) for i in range(count)])]
    pallas_call x1 -> x2, Pallas kernels: 3.22 us -> 4.84 us  [the longest x1 2.61 us: second_pack(): pl.pallas_call(functools.partial(second_pack_kernel, pieces, section_coun...]
  transfers between devices with their start and end apart: 12 -> 15, of which waited for: 6 -> 9; matrix products, arithmetic and copies ran while one was open for 0% -> 0% of each run, Pallas kernels for 28% -> 30%
where the time goes in v7:
time: 61.6 us; the launch traced here: 61.4 us
  Pallas kernels  21.9 us (36%)
  starting transfers between devices  21.6 us (35%)
  waiting for transfers between devices  17.2 us (28%)
  between operations  0.76 us (1%)
    ppermute x15, starting transfers between devices, swap(): return lax.ppermute(value, axis, [(i, i ^ offset) for i in range(count)])  21.6 us
    ppermute x15, waiting for transfers between devices, swap(): return lax.ppermute(value, axis, [(i, i ^ offset) for i in range(count)])  17.2 us
    pallas_call x1, Pallas kernels, fetch(): pl.pallas_call(fetch_kernel, out_shape=jax.ShapeDtypeStruct(weight.shape,...  5.92 us
    pallas_call x1, Pallas kernels, attend(): pl.pallas_call(functools.partial(attend_kernel, pieces, section_count, tp...  3.77 us
    pallas_call x1, Pallas kernels, project(): pl.pallas_call(functools.partial(project_kernel, count, min(256, width)),...  3.64 us
    pallas_call x3, Pallas kernels, place(): pl.pallas_call(functools.partial(place_kernel, pieces), out_shape=jax.Sha...  3.31 us
    pallas_call x1, Pallas kernels, second_pack(): pl.pallas_call(functools.partial(second_pack_kernel, pieces, section_coun...  2.61 us
    pallas_call x1, Pallas kernels, first_pack(): pl.pallas_call(functools.partial(first_pack_kernel, pieces, section_count...  2.23 us
  transfers between devices with their start and end apart: 15, of which 9 were waited for; matrix products, arithmetic and copies ran while one was open for 0% of the time, Pallas kernels for 30%

profile of v7, /device:TPU:0, one launch (start us, length us, event | category | flops | bytes accessed | tf_op | source)
XLA Modules:
  0.0 61.4 jit_solution(482485523074434396)
XLA Ops:
  0.6 0.0 copy-start
  0.7 2.2 %first_pack.1 = (bf16[2,2,256,512]{3,2,1,0:T(8,128)(2,1)S(1)}, bf16[2,4,4096]{2,1,0:T(4,128)(2,1)S(1)}, bf16[2,4,4096]{2,1,0:T(4,128)(2,1)S(1)}, bf16[2,4,1024]{2,1,0:T(4,128)(2,1)S(1)}, bf16[2,4,1024]{2,1,0:T(4,128)(2,1)S(1)}) custom-call(s32[32]{0:T(128)} %bitcast.1, bf16[8,2,256,512]{3,2,1,0:T(8,128)(2,1)} %cache_ref.3, bf16[1,8,4,4096]{3,2,1,0:T(4,128)(2,1)} %query_ref.1), custom_call_target="tpu_custom_call" | custom-call | bytes 2424832 | tf_op jit(solution)/shard_map/first_pack/pallas_call | solution.py:133
  2.9 3.0 %collective-permute-start = (bf16[2,4,1024]{2,1,0:T(4,128)(2,1)S(1)}, bf16[2,4,1024]{2,1,0:T(4,128)(2,1)S(1)}, u32[]{:S(2)}, u32[]{:S(2)}) collective-permute-start(bf16[2,4,1024]{2,1,0:T(4,128)(2,1)S(1)} %get-tuple-element.16), channel_id=1, source_target_pairs={{0,2},{1,3},{2,0},{3,1},{4,6},{5,7},{6,4},{7,5},{8,10},{9,11},{10,... | collective-permute-start | bytes 49160 | tf_op jit(solution)/shard_map/ppermute | solution.py:34
  5.9 0.0 collective-permute-start.1
  5.9 1.2 %collective-permute-start.12 = (bf16[2,2,256,512]{3,2,1,0:T(8,128)(2,1)S(1)}, bf16[2,2,256,512]{3,2,1,0:T(8,128)(2,1)S(1)}, u32[]{:S(2)}, u32[]{:S(2)}) collective-permute-start(bf16[2,2,256,512]{3,2,1,0:T(8,128)(2,1)S(1)} %get-tuple-element.15.refs_0_), channel_id=1, source_target_pairs={{0,2},{1,3},{2,0},{3,1},{4,6},{5,7},{6,4},{7,5},{8,10},{9,11},{10,... | collective-permute-start | bytes 3145736 | tf_op jit(solution)/shard_map/ppermute | solution.py:34
  7.1 0.5 collective-permute-done.refs_0_
  7.6 1.4 %collective-permute-done.1.refs_1_ = bf16[2,4,1024]{2,1,0:T(4,128)(2,1)S(1)} collective-permute-done((bf16[2,4,1024]{2,1,0:T(4,128)(2,1)S(1)}, bf16[2,4,1024]{2,1,0:T(4,128)(2,1)S(1)}, u32[]{:S(2)}, u32[]{:S(2)}) %collective-permute-start.1) | collective-permute-done | bytes 16416 | tf_op jit(solution)/shard_map/ppermute | solution.py:34
  9.1 2.6 %second_pack.1 = (bf16[2,2,256,512]{3,2,1,0:T(8,128)(2,1)S(1)}, bf16[2,2,256,512]{3,2,1,0:T(8,128)(2,1)S(1)}, bf16[2,2,256,512]{3,2,1,0:T(8,128)(2,1)S(1)}, bf16[2,2,4,1024]{3,2,1,0:T(4,128)(2,1)S(1)}) custom-call(s32[32]{0:T(128)} %bitcast.2, bf16[8,2,256,512]{3,2,1,0:T(8,128)(2,1)} %cache_ref.3, bf16[2,4,1024]{2,1,0:T(4,128)(2,1)S(1)} %collective-permute-done.refs_0_, ...), custom_call_target="tpu_custom_call" | custom-call | bytes 100000000 | tf_op jit(solution)/shard_map/second_pack/pallas_call | solution.py:154
  11.7 0.1 collective-permute-start.13
  11.8 0.7 %collective-permute-start.14 = (bf16[2,2,256,512]{3,2,1,0:T(8,128)(2,1)S(1)}, bf16[2,2,256,512]{3,2,1,0:T(8,128)(2,1)S(1)}, u32[]{:S(2)}, u32[]{:S(2)}) collective-permute-start(bf16[2,2,256,512]{3,2,1,0:T(8,128)(2,1)S(1)} %get-tuple-element.18.refs_1_), channel_id=1, source_target_pairs={{0,3},{1,2},{2,1},{3,0},{4,7},{5,6},{6,5},{7,4},{8,11},{9,10},{10,... | collective-permute-start | bytes 3145736 | tf_op jit(solution)/shard_map/ppermute | solution.py:34
  12.5 2.7 %collective-permute-start.4 = (bf16[2,2,4,1024]{3,2,1,0:T(4,128)(2,1)S(1)}, bf16[2,2,4,1024]{3,2,1,0:T(4,128)(2,1)S(1)}, u32[]{:S(2)}, u32[]{:S(2)}) collective-permute-start(bf16[2,2,4,1024]{3,2,1,0:T(4,128)(2,1)S(1)} %get-tuple-element.23.refs_6_), channel_id=1, source_target_pairs={{0,8},{4,12},{8,0},{12,4},{1,9},{5,13},{9,1},{13,5},{2,10},{6,14},... | collective-permute-start | bytes 98312 | tf_op jit(solution)/shard_map/ppermute | solution.py:34
  15.2 2.1 %collective-permute-done.4.refs_8_ = bf16[2,2,4,1024]{3,2,1,0:T(4,128)(2,1)S(1)} collective-permute-done((bf16[2,2,4,1024]{3,2,1,0:T(4,128)(2,1)S(1)}, bf16[2,2,4,1024]{3,2,1,0:T(4,128)(2,1)S(1)}, u32[]{:S(2)}, u32[]{:S(2)}) %collective-permute-start.4) | collective-permute-done | bytes 32800 | tf_op jit(solution)/shard_map/ppermute | solution.py:34
  17.3 1.7 %collective-permute-start.3 = (bf16[2,2,4,1024]{3,2,1,0:T(4,128)(2,1)S(1)}, bf16[2,2,4,1024]{3,2,1,0:T(4,128)(2,1)S(1)}, u32[]{:S(2)}, u32[]{:S(2)}) collective-permute-start(bf16[2,2,4,1024]{3,2,1,0:T(4,128)(2,1)S(1)} %get-tuple-element.23.refs_6_), channel_id=1, source_target_pairs={{0,4},{4,0},{8,12},{12,8},{1,5},{5,1},{9,13},{13,9},{2,6},{6,2},{1... | collective-permute-start | bytes 98312 | tf_op jit(solution)/shard_map/ppermute | solution.py:34
  19.0 2.2 %collective-permute-done.3.refs_7_ = bf16[2,2,4,1024]{3,2,1,0:T(4,128)(2,1)S(1)} collective-permute-done((bf16[2,2,4,1024]{3,2,1,0:T(4,128)(2,1)S(1)}, bf16[2,2,4,1024]{3,2,1,0:T(4,128)(2,1)S(1)}, u32[]{:S(2)}, u32[]{:S(2)}) %collective-permute-start.3) | collective-permute-done | bytes 32800 | tf_op jit(solution)/shard_map/ppermute | solution.py:34
  21.2 2.7 %collective-permute-start.5 = (bf16[2,2,4,1024]{3,2,1,0:T(4,128)(2,1)S(1)}, bf16[2,2,4,1024]{3,2,1,0:T(4,128)(2,1)S(1)}, u32[]{:S(2)}, u32[]{:S(2)}) collective-permute-start(bf16[2,2,4,1024]{3,2,1,0:T(4,128)(2,1)S(1)} %collective-permute-done.3.refs_7_), channel_id=1, source_target_pairs={{0,8},{4,12},{8,0},{12,4},{1,9},{5,13},{9,1},{13,5},{2,10},{6,14},... | collective-permute-start | bytes 98312 | tf_op jit(solution)/shard_map/ppermute | solution.py:34
  23.9 2.1 %collective-permute-done.5.refs_9_ = bf16[2,2,4,1024]{3,2,1,0:T(4,128)(2,1)S(1)} collective-permute-done((bf16[2,2,4,1024]{3,2,1,0:T(4,128)(2,1)S(1)}, bf16[2,2,4,1024]{3,2,1,0:T(4,128)(2,1)S(1)}, u32[]{:S(2)}, u32[]{:S(2)}) %collective-permute-start.5) | collective-permute-done | bytes 32800 | tf_op jit(solution)/shard_map/ppermute | solution.py:34
  26.0 3.8 %attend.1 = (bf16[10,32,128]{2,1,0:T(8,128)(2,1)S(1)}, bf16[10,32,128]{2,1,0:T(8,128)(2,1)S(1)}, bf16[10,32,128]{2,1,0:T(8,128)(2,1)S(1)}, bf16[10,32,128]{2,1,0:T(8,128)(2,1)S(1)}) custom-call(s32[32]{0:T(128)S(1)} %bitcast.3, s32[32]{0:T(128)S(1)} %copy-done.1, bf16[2,2,256,512]{3,2,1,0:T(8,128)(2,1)S(1)} %get-tuple-element.15.refs_0_, ...), custom_call_target="tpu_custom_call" | custom-call | flops 134217728 | bytes 4194304 | tf_op jit(solution)/shard_map/attend/pallas_call | solution.py:295
  29.8 1.8 %collective-permute-start.6 = (bf16[10,32,128]{2,1,0:T(8,128)(2,1)S(1)}, bf16[10,32,128]{2,1,0:T(8,128)(2,1)S(1)}, u32[]{:S(2)}, u32[]{:S(2)}) collective-permute-start(bf16[10,32,128]{2,1,0:T(8,128)(2,1)S(1)} %get-tuple-element.25), channel_id=1, source_target_pairs={{0,4},{4,0},{8,12},{12,8},{1,5},{5,1},{9,13},{13,9},{2,6},{6,2},{1... | collective-permute-start | bytes 245768 | tf_op jit(solution)/shard_map/ppermute | solution.py:34
  31.6 2.9 %collective-permute-start.7 = (bf16[10,32,128]{2,1,0:T(8,128)(2,1)S(1)}, bf16[10,32,128]{2,1,0:T(8,128)(2,1)S(1)}, u32[]{:S(2)}, u32[]{:S(2)}) collective-permute-start(bf16[10,32,128]{2,1,0:T(8,128)(2,1)S(1)} %get-tuple-element.26), channel_id=1, source_target_pairs={{0,8},{4,12},{8,0},{12,4},{1,9},{5,13},{9,1},{13,5},{2,10},{6,14},... | collective-permute-start | bytes 245768 | tf_op jit(solution)/shard_map/ppermute | solution.py:34
  34.4 0.1 collective-permute-done.6.refs_1_
  34.5 3.8 %collective-permute-start.8 = (bf16[10,32,128]{2,1,0:T(8,128)(2,1)S(1)}, bf16[10,32,128]{2,1,0:T(8,128)(2,1)S(1)}, u32[]{:S(2)}, u32[]{:S(2)}) collective-permute-start(bf16[10,32,128]{2,1,0:T(8,128)(2,1)S(1)} %get-tuple-element.27), channel_id=1, source_target_pairs={{0,12},{4,8},{8,4},{12,0},{1,13},{5,9},{9,5},{13,1},{2,14},{6,10},... | collective-permute-start | bytes 245768 | tf_op jit(solution)/shard_map/ppermute | solution.py:34
  38.3 5.9 %fetch.1.refs_4_ = bf16[4096,2048]{1,0:T(8,128)(2,1)S(1)} custom-call(bf16[4096,2048]{1,0:T(8,128)(2,1)} %weight_ref.1, bf16[10,32,128]{2,1,0:T(8,128)(2,1)S(1)} %get-tuple-element.24.refs_0_), custom_call_target="tpu_custom_call" | custom-call | bytes 33554432 | tf_op jit(solution)/shard_map/fetch/pallas_call | solution.py:390
  44.3 0.4 join.1.refs_0_
  44.6 0.1 collective-permute-start.9
  44.7 0.9 %collective-permute-start.10 = (bf16[8,4096]{1,0:T(8,128)(2,1)S(1)}, bf16[8,4096]{1,0:T(8,128)(2,1)S(1)}, u32[]{:S(2)}, u32[]{:S(2)}) collective-permute-start(bf16[8,4096]{1,0:T(8,128)(2,1)S(1)} %join.1.refs_0_), channel_id=1, source_target_pairs={{0,8},{4,12},{8,0},{12,4},{1,9},{5,13},{9,1},{13,5},{2,10},{6,14},... | collective-permute-start | bytes 196616 | tf_op jit(solution)/shard_map/ppermute | solution.py:34
  45.7 3.6 %collective-permute-done.9.refs_1_ = bf16[8,4096]{1,0:T(8,128)(2,1)S(1)} collective-permute-done((bf16[8,4096]{1,0:T(8,128)(2,1)S(1)}, bf16[8,4096]{1,0:T(8,128)(2,1)S(1)}, u32[]{:S(2)}, u32[]{:S(2)}) %collective-permute-start.9) | collective-permute-done | bytes 65568 | tf_op jit(solution)/shard_map/ppermute | solution.py:34
  49.3 0.7 %collective-permute-done.10.refs_2_ = bf16[8,4096]{1,0:T(8,128)(2,1)S(1)} collective-permute-done((bf16[8,4096]{1,0:T(8,128)(2,1)S(1)}, bf16[8,4096]{1,0:T(8,128)(2,1)S(1)}, u32[]{:S(2)}, u32[]{:S(2)}) %collective-permute-start.10) | collective-permute-done | bytes 65568 | tf_op jit(solution)/shard_map/ppermute | solution.py:34
  50.0 4.5 %collective-permute-done.11.refs_3_ = bf16[8,4096]{1,0:T(8,128)(2,1)S(1)} collective-permute-done((bf16[8,4096]{1,0:T(8,128)(2,1)S(1)}, bf16[8,4096]{1,0:T(8,128)(2,1)S(1)}, u32[]{:S(2)}, u32[]{:S(2)}) %collective-permute-start.11) | collective-permute-done | bytes 65568 | tf_op jit(solution)/shard_map/ppermute | solution.py:34
  54.4 3.6 %project.1.refs_0_.refs_1_ = bf16[8,4,2048]{2,1,0:T(4,128)(2,1)} custom-call(bf16[8,4096]{1,0:T(8,128)(2,1)S(1)} %join.1.refs_0_, bf16[8,4096]{1,0:T(8,128)(2,1)S(1)} %collective-permute-done.9.refs_1_, bf16[8,4096]{1,0:T(8,128)(2,1)S(1)} %collective-permute-done.10.refs_2_, bf16[8,4096]{1,0:T(8,128)(2,1)S(1)} %collective-permute-done.11.refs_3_, ...), custom_call_target="tpu_custom_call" | custom-call | flops 536870912 | bytes 16777216 | tf_op jit(solution)/shard_map/project/pallas_call | solution.py:421
  58.1 1.0 %place.3.refs_0_ = bf16[1,8,2,256,512]{4,3,2,1,0:T(8,128)(2,1)} custom-call(bf16[8,4,2048]{2,1,0:T(4,128)(2,1)} %project.1.refs_0_.refs_1_, bf16[2,2,256,512]{3,2,1,0:T(8,128)(2,1)S(1)} %collective-permute-done.12.refs_1_), custom_call_target="tpu_custom_call" | custom-call | bytes 2097152 | tf_op jit(solution)/shard_map/place/pallas_call | solution.py:186
  59.1 1.3 %place.4.refs_0_ = bf16[1,8,2,256,512]{4,3,2,1,0:T(8,128)(2,1)} custom-call(bf16[1,8,2,256,512]{4,3,2,1,0:T(8,128)(2,1)} %place.3.refs_0_, bf16[8,4,2048]{2,1,0:T(4,128)(2,1)} %project.1.refs_0_.refs_1_, bf16[2,2,256,512]{3,2,1,0:T(8,128)(2,1)S(1)} %get-tuple-element.19.refs_2_, ...), custom_call_target="tpu_custom_call", output_to_operand_aliasing={{}: (0, {})} | custom-call | bytes 4194304 | tf_op jit(solution)/shard_map/place/pallas_call | solution.py:186
  60.4 1.0 %place.5 = bf16[1,8,2,256,512]{4,3,2,1,0:T(8,128)(2,1)} custom-call(bf16[1,8,2,256,512]{4,3,2,1,0:T(8,128)(2,1)} %place.4.refs_0_, bf16[8,4,2048]{2,1,0:T(4,128)(2,1)} %project.1.refs_0_.refs_1_, bf16[2,2,256,512]{3,2,1,0:T(8,128)(2,1)S(1)} %collective-permute-done.14.refs_2_), custom_call_target="tpu_custom_call", output_to_operand_aliasing={{}: (0, {})} | custom-call | bytes 2097152 | tf_op jit(solution)/shard_map/place/pallas_call | solution.py:186
  (11 shorter events, 0.0 us)
Async XLA Ops:
  0.6 25.4 %copy-start = (s32[32,1]{0,1:T(1,128)S(1)}, s32[32,1]{0,1:T(1,128)}, u32[]{:S(2)}) copy-start(s32[32,1]{0,1:T(1,128)} %param.7) | copy-start | bytes 388
  0.6 25.4 %copy-start.1 = (s32[32]{0:T(128)S(1)}, s32[32]{0:T(128)}, u32[]{:S(2)}) copy-start(s32[32]{0:T(128)} %lengths_ref.1) | copy-start | bytes 388
  2.9 4.7 %collective-permute-start = (bf16[2,4,1024]{2,1,0:T(4,128)(2,1)S(1)}, bf16[2,4,1024]{2,1,0:T(4,128)(2,1)S(1)}, u32[]{:S(2)}, u32[]{:S(2)}) collective-permute-start(bf16[2,4,1024]{2,1,0:T(4,128)(2,1)S(1)} %get-tuple-element.16), channel_id=1, source_target_pairs={{0,2},{1,3},{2,0},{3,1},{4,6},{5,7},{6,4},{7,5},{8,10},{9,11},{10,... | collective-permute-start | bytes 49160 | tf_op jit(solution)/shard_map/ppermute | solution.py:34
  5.9 3.2 %collective-permute-start.1 = (bf16[2,4,1024]{2,1,0:T(4,128)(2,1)S(1)}, bf16[2,4,1024]{2,1,0:T(4,128)(2,1)S(1)}, u32[]{:S(2)}, u32[]{:S(2)}) collective-permute-start(bf16[2,4,1024]{2,1,0:T(4,128)(2,1)S(1)} %get-tuple-element.17), channel_id=1, source_target_pairs={{0,3},{1,2},{2,1},{3,0},{4,7},{5,6},{6,5},{7,4},{8,11},{9,10},{10,... | collective-permute-start | bytes 49160 | tf_op jit(solution)/shard_map/ppermute | solution.py:34
  5.9 52.2 %collective-permute-start.12 = (bf16[2,2,256,512]{3,2,1,0:T(8,128)(2,1)S(1)}, bf16[2,2,256,512]{3,2,1,0:T(8,128)(2,1)S(1)}, u32[]{:S(2)}, u32[]{:S(2)}) collective-permute-start(bf16[2,2,256,512]{3,2,1,0:T(8,128)(2,1)S(1)} %get-tuple-element.15.refs_0_), channel_id=1, source_target_pairs={{0,2},{1,3},{2,0},{3,1},{4,6},{5,7},{6,4},{7,5},{8,10},{9,11},{10,... | collective-permute-start | bytes 3145736 | tf_op jit(solution)/shard_map/ppermute | solution.py:34
  11.7 47.4 %collective-permute-start.13 = (bf16[2,2,256,512]{3,2,1,0:T(8,128)(2,1)S(1)}, bf16[2,2,256,512]{3,2,1,0:T(8,128)(2,1)S(1)}, u32[]{:S(2)}, u32[]{:S(2)}) collective-permute-start(bf16[2,2,256,512]{3,2,1,0:T(8,128)(2,1)S(1)} %get-tuple-element.20.refs_3_), channel_id=1, source_target_pairs={{0,1},{1,0},{2,3},{3,2},{4,5},{5,4},{6,7},{7,6},{8,9},{9,8},{10,11... | collective-permute-start | bytes 3145736 | tf_op jit(solution)/shard_map/ppermute | solution.py:34
  11.8 48.7 %collective-permute-start.14 = (bf16[2,2,256,512]{3,2,1,0:T(8,128)(2,1)S(1)}, bf16[2,2,256,512]{3,2,1,0:T(8,128)(2,1)S(1)}, u32[]{:S(2)}, u32[]{:S(2)}) collective-permute-start(bf16[2,2,256,512]{3,2,1,0:T(8,128)(2,1)S(1)} %get-tuple-element.18.refs_1_), channel_id=1, source_target_pairs={{0,3},{1,2},{2,1},{3,0},{4,7},{5,6},{6,5},{7,4},{8,11},{9,10},{10,... | collective-permute-start | bytes 3145736 | tf_op jit(solution)/shard_map/ppermute | solution.py:34
  12.5 4.8 %collective-permute-start.4 = (bf16[2,2,4,1024]{3,2,1,0:T(4,128)(2,1)S(1)}, bf16[2,2,4,1024]{3,2,1,0:T(4,128)(2,1)S(1)}, u32[]{:S(2)}, u32[]{:S(2)}) collective-permute-start(bf16[2,2,4,1024]{3,2,1,0:T(4,128)(2,1)S(1)} %get-tuple-element.23.refs_6_), channel_id=1, source_target_pairs={{0,8},{4,12},{8,0},{12,4},{1,9},{5,13},{9,1},{13,5},{2,10},{6,14},... | collective-permute-start | bytes 98312 | tf_op jit(solution)/shard_map/ppermute | solution.py:34
  15.2 8.8 %collective-permute-start.2 = (bf16[2,4,4096]{2,1,0:T(4,128)(2,1)S(1)}, bf16[2,4,4096]{2,1,0:T(4,128)(2,1)S(1)}, u32[]{:S(2)}, u32[]{:S(2)}) collective-permute-start(bf16[2,4,4096]{2,1,0:T(4,128)(2,1)S(1)} %get-tuple-element.22), channel_id=1, source_target_pairs={{0,1},{1,0},{2,3},{3,2},{4,5},{5,4},{6,7},{7,6},{8,9},{9,8},{10,11... | collective-permute-start | bytes 196616 | tf_op jit(solution)/shard_map/ppermute | solution.py:34
  17.3 3.9 %collective-permute-start.3 = (bf16[2,2,4,1024]{3,2,1,0:T(4,128)(2,1)S(1)}, bf16[2,2,4,1024]{3,2,1,0:T(4,128)(2,1)S(1)}, u32[]{:S(2)}, u32[]{:S(2)}) collective-permute-start(bf16[2,2,4,1024]{3,2,1,0:T(4,128)(2,1)S(1)} %get-tuple-element.23.refs_6_), channel_id=1, source_target_pairs={{0,4},{4,0},{8,12},{12,8},{1,5},{5,1},{9,13},{13,9},{2,6},{6,2},{1... | collective-permute-start | bytes 98312 | tf_op jit(solution)/shard_map/ppermute | solution.py:34
  21.2 4.8 %collective-permute-start.5 = (bf16[2,2,4,1024]{3,2,1,0:T(4,128)(2,1)S(1)}, bf16[2,2,4,1024]{3,2,1,0:T(4,128)(2,1)S(1)}, u32[]{:S(2)}, u32[]{:S(2)}) collective-permute-start(bf16[2,2,4,1024]{3,2,1,0:T(4,128)(2,1)S(1)} %collective-permute-done.3.refs_7_), channel_id=1, source_target_pairs={{0,8},{4,12},{8,0},{12,4},{1,9},{5,13},{9,1},{13,5},{2,10},{6,14},... | collective-permute-start | bytes 98312 | tf_op jit(solution)/shard_map/ppermute | solution.py:34
  29.8 4.7 %collective-permute-start.6 = (bf16[10,32,128]{2,1,0:T(8,128)(2,1)S(1)}, bf16[10,32,128]{2,1,0:T(8,128)(2,1)S(1)}, u32[]{:S(2)}, u32[]{:S(2)}) collective-permute-start(bf16[10,32,128]{2,1,0:T(8,128)(2,1)S(1)} %get-tuple-element.25), channel_id=1, source_target_pairs={{0,4},{4,0},{8,12},{12,8},{1,5},{5,1},{9,13},{13,9},{2,6},{6,2},{1... | collective-permute-start | bytes 245768 | tf_op jit(solution)/shard_map/ppermute | solution.py:34
  31.6 12.7 %collective-permute-start.7 = (bf16[10,32,128]{2,1,0:T(8,128)(2,1)S(1)}, bf16[10,32,128]{2,1,0:T(8,128)(2,1)S(1)}, u32[]{:S(2)}, u32[]{:S(2)}) collective-permute-start(bf16[10,32,128]{2,1,0:T(8,128)(2,1)S(1)} %get-tuple-element.26), channel_id=1, source_target_pairs={{0,8},{4,12},{8,0},{12,4},{1,9},{5,13},{9,1},{13,5},{2,10},{6,14},... | collective-permute-start | bytes 245768 | tf_op jit(solution)/shard_map/ppermute | solution.py:34
  34.5 9.8 %collective-permute-start.8 = (bf16[10,32,128]{2,1,0:T(8,128)(2,1)S(1)}, bf16[10,32,128]{2,1,0:T(8,128)(2,1)S(1)}, u32[]{:S(2)}, u32[]{:S(2)}) collective-permute-start(bf16[10,32,128]{2,1,0:T(8,128)(2,1)S(1)} %get-tuple-element.27), channel_id=1, source_target_pairs={{0,12},{4,8},{8,4},{12,0},{1,13},{5,9},{9,5},{13,1},{2,14},{6,10},... | collective-permute-start | bytes 245768 | tf_op jit(solution)/shard_map/ppermute | solution.py:34
  44.6 4.6 %collective-permute-start.9 = (bf16[8,4096]{1,0:T(8,128)(2,1)S(1)}, bf16[8,4096]{1,0:T(8,128)(2,1)S(1)}, u32[]{:S(2)}, u32[]{:S(2)}) collective-permute-start(bf16[8,4096]{1,0:T(8,128)(2,1)S(1)} %join.1.refs_0_), channel_id=1, source_target_pairs={{0,4},{4,0},{8,12},{12,8},{1,5},{5,1},{9,13},{13,9},{2,6},{6,2},{1... | collective-permute-start | bytes 196616 | tf_op jit(solution)/shard_map/ppermute | solution.py:34
  44.7 5.2 %collective-permute-start.10 = (bf16[8,4096]{1,0:T(8,128)(2,1)S(1)}, bf16[8,4096]{1,0:T(8,128)(2,1)S(1)}, u32[]{:S(2)}, u32[]{:S(2)}) collective-permute-start(bf16[8,4096]{1,0:T(8,128)(2,1)S(1)} %join.1.refs_0_), channel_id=1, source_target_pairs={{0,8},{4,12},{8,0},{12,4},{1,9},{5,13},{9,1},{13,5},{2,10},{6,14},... | collective-permute-start | bytes 196616 | tf_op jit(solution)/shard_map/ppermute | solution.py:34
  49.3 5.2 %collective-permute-start.11 = (bf16[8,4096]{1,0:T(8,128)(2,1)S(1)}, bf16[8,4096]{1,0:T(8,128)(2,1)S(1)}, u32[]{:S(2)}, u32[]{:S(2)}) collective-permute-start(bf16[8,4096]{1,0:T(8,128)(2,1)S(1)} %collective-permute-done.9.refs_1_), channel_id=1, source_target_pairs={{0,8},{4,12},{8,0},{12,4},{1,9},{5,13},{9,1},{13,5},{2,10},{6,14},... | collective-permute-start | bytes 196616 | tf_op jit(solution)/shard_map/ppermute | solution.py:34

commit v8 on v7

--- a/solution.py
+++ b/solution.py
@@ -35,10 +35,7 @@
 
 
 def spread(value, axis):
-    values = [value]
-    while len(values) < lax.axis_size(axis):
-        values += [swap(one, axis, len(values)) for one in values]
-    return values
+    return [swap(value, axis, offset) for offset in range(lax.axis_size(axis))]
 
 
 def own_slots(routing_ref, section, used, source):
@@ -113,12 +110,26 @@
 
 
 def second_pack_kernel(pieces, section_count, routing_ref, cache_ref, *refs):
-    source, used, sem = refs[-3:]
-    cache_out, merged_ref, query_refs = refs[-4 - len(pieces) : -4], refs[-4], refs[: -4 - len(pieces)]
-    finish = start_packing(pieces, section_count, routing_ref, cache_ref, cache_out, source, used, sem)
-    for n, query_ref in enumerate(query_refs):
-        merged_ref[n] = query_ref[...]
-    finish()
+    cache_out, (source, used, sem) = refs[-3 - len(pieces) : -3], refs[-3:]
+    start_packing(pieces, section_count, routing_ref, cache_ref, cache_out, source, used, sem)()
+
+
+def merge_kernel(count, *refs):
+    for n in range(count):
+        refs[-1][n] = refs[n][...]
+
+
+def merge(parts, others):
+    shape = (len(parts),) + parts[0].shape
+    return pl.pallas_call(
+        functools.partial(merge_kernel, len(parts)),
+        out_shape=jax.ShapeDtypeStruct(shape, parts[0].dtype),
+        in_specs=[VMEM] * len(parts) + [ANY] * len(others),
+        out_specs=VMEM,
+        compiler_params=limit(8),
+        cost_estimate=cost(0, 8 * len(parts) * parts[0].size),
+        name="merge",
+    )(*parts, *others)
 
 
 def in_hbm(value):
@@ -148,24 +159,22 @@
     return parts[: len(pieces)], parts[len(pieces) :]
 
 
-def second_pack(routing, cache, queries, pieces, section_count):
+def second_pack(routing, cache, others, pieces, section_count):
     shapes = [jax.ShapeDtypeStruct((count,) + cache.shape[1:], cache.dtype) for _, _, count in pieces]
-    merged = jax.ShapeDtypeStruct((len(queries),) + queries[0].shape, queries[0].dtype)
-    *parts, merged = pl.pallas_call(
+    return pl.pallas_call(
         functools.partial(second_pack_kernel, pieces, section_count),
-        out_shape=shapes + [merged],
-        in_specs=[SMEM, HBM] + [VMEM] * len(queries),
-        out_specs=[VMEM] * (len(shapes) + 1),
+        out_shape=shapes,
+        in_specs=[SMEM, HBM] + [ANY] * len(others),
+        out_specs=[VMEM] * len(shapes),
         scratch_shapes=[
             pltpu.SMEM((section_count * CAP,), jnp.int32),
             pltpu.SMEM((section_count,), jnp.int32),
             pltpu.SemaphoreType.DMA((section_count * CAP,)),
         ],
         compiler_params=limit(16),
-        cost_estimate=cost(0, 10**8),
+        cost_estimate=cost(10**10, 4 * sum(shape.size for shape in shapes)),
         name="second_pack",
-    )(in_hbm(routing), in_hbm(cache), *queries)
-    return parts, merged
+    )(in_hbm(routing), in_hbm(cache), *others)
 
 
 def place_kernel(pieces, *refs):
@@ -189,7 +198,7 @@
         in_specs=[HBM] * len(given) + [VMEM] * len(parts),
         out_specs=HBM,
         scratch_shapes=[pltpu.SemaphoreType.DMA((len(parts),))],
-        input_output_aliases={0: 0} if len(given) > 1 else {},
+        input_output_aliases={0: 0} if given else {},
         compiler_params=limit(8),
         cost_estimate=cost(0, 4 * sum(piece.size for piece in parts)),
         name="place",
@@ -306,7 +315,7 @@
             pltpu.VMEM((tp_count,) + far_queries[0].shape, far_queries[0].dtype),
         ],
         compiler_params=limit(12),
-        cost_estimate=cost(4 * multiplies, 2 * sum(part.size for part in caches), multiplies // HEAD_SIZE),
+        cost_estimate=cost(2 * 10**10, 2 * sum(part.size for part in caches), multiplies // HEAD_SIZE),
         name="attend",
     )(routing, lengths, *caches, *queries, *far_queries)
 
@@ -437,20 +446,18 @@
 
     near = [(offset, 0, CAP) for offset in range(2)]
     far = [(offset, 0, CAP) for offset in range(2, section_count)]
-    early, late = far[:1], far[1:] + near
-    early_caches, query_parts = first_pack(
-        routing, prompt_key_values, queries, early, section_count, tp_count
-    )
+    far_caches, query_parts = first_pack(routing, prompt_key_values, queries, far, section_count, tp_count)
     query_parts = [swap(part, "sec", offset) for offset, part in enumerate(query_parts)]
-    late_caches, merged = second_pack(routing, prompt_key_values, query_parts[2:], late, section_count)
+    far_parts = [swap(part, "sec", piece[0]) for part, piece in zip(far_caches, far)]
+    merged = merge(query_parts[2:], query_parts[1:2])
     far_queries = spread(merged, "tp")
-    caches, pieces = [*early_caches, *late_caches], early + late
-    arrived = [swap(part, "sec", piece[0]) for part, piece in zip(caches, pieces)]
-    far_parts, near_parts = arrived[: len(far)], arrived[len(far) :]
+    near_caches = second_pack(routing, prompt_key_values, [merged], near, section_count)
+    near_parts = [swap(part, "sec", piece[0]) for part, piece in zip(near_caches, near)]
+    caches, pieces = [*far_caches, *near_caches], far + near
 
     messages = attend(routing, lengths, caches, pieces, query_parts[:2], far_queries)
     partials = [swap(part, "tp", offset) for offset, part in enumerate(messages)]
-    held_weight = fetch(out_weight, messages[:1])
+    held_weight = fetch(out_weight, [messages[0], *near_parts[1:]])
     share = join(partials, [held_weight], samples)
     shares = spread(share, "tp")
     if share.ndim == 3:
@@ -462,12 +469,10 @@
     else:
         layer_out = project(shares, held_weight, samples)
 
-    stages = [([part], [piece]) for part, piece in zip(far_parts, far)]
-    stages.insert(-1, (near_parts, near))
-    whole = []
-    for parts, pieces in stages:
-        whole = [place(whole + [layer_out], parts, pieces, slot_count)]
-    return (layer_out, *whole)
+    whole = place([], near_parts, near, slot_count)
+    for part, piece in zip(far_parts, far):
+        whole = place([whole, layer_out], [part], [piece], slot_count)
+    return (layer_out, whole)
 
 
 def solution(mesh):

time: 61.6 us -> 55.2 us (0.90)
  starting transfers between devices: 21.6 us -> 18.3 us
  waiting for transfers between devices: 17.2 us -> 14.2 us
    ppermute x15, starting transfers between devices: 21.6 us -> 18.3 us  [swap(): return lax.ppermute(value, axis, [(i, i ^ offset) for i in range(count)])]
    ppermute x15, waiting for transfers between devices: 17.2 us -> 14.2 us  [swap(): return lax.ppermute(value, axis, [(i, i ^ offset) for i in range(count)])]
  transfers between devices with their start and end apart: 15 -> 15, of which waited for: 9 -> 6; matrix products, arithmetic and copies ran while one was open for 0% -> 0% of each run, Pallas kernels for 30% -> 33%
where the time goes in v8:
time: 55.2 us; the launch traced here: 55 us
  Pallas kernels  21.7 us (39%)
  starting transfers between devices  18.3 us (33%)
  waiting for transfers between devices  14.2 us (26%)
  between operations  0.77 us (1%)
    ppermute x15, starting transfers between devices, swap(): return lax.ppermute(value, axis, [(i, i ^ offset) for i in range(count)])  18.3 us
    ppermute x15, waiting for transfers between devices, swap(): return lax.ppermute(value, axis, [(i, i ^ offset) for i in range(count)])  14.2 us
    pallas_call x1, Pallas kernels, fetch(): pl.pallas_call(fetch_kernel, out_shape=jax.ShapeDtypeStruct(weight.shape,...  5.92 us
    pallas_call x1, Pallas kernels, attend(): pl.pallas_call(functools.partial(attend_kernel, pieces, section_count, tp...  3.76 us
    pallas_call x1, Pallas kernels, project(): pl.pallas_call(functools.partial(project_kernel, count, min(256, width)),...  3.64 us
    pallas_call x3, Pallas kernels, place(): pl.pallas_call(functools.partial(place_kernel, pieces), out_shape=jax.Sha...  3.29 us
    pallas_call x1, Pallas kernels, first_pack(): pl.pallas_call(functools.partial(first_pack_kernel, pieces, section_count...  2.41 us
    pallas_call x1, Pallas kernels, second_pack(): pl.pallas_call(functools.partial(second_pack_kernel, pieces, section_coun...  2.3 us
  transfers between devices with their start and end apart: 15, of which 6 were waited for; matrix products, arithmetic and copies ran while one was open for 0% of the time, Pallas kernels for 33%

profile of v8, /device:TPU:0, one launch (start us, length us, event | category | flops | bytes accessed | tf_op | source)
XLA Modules:
  0.0 55.0 jit_solution(12705731924882350317)
XLA Ops:
  0.6 2.4 %first_pack.1 = (bf16[2,2,256,512]{3,2,1,0:T(8,128)(2,1)S(1)}, bf16[2,2,256,512]{3,2,1,0:T(8,128)(2,1)S(1)}, bf16[2,4,4096]{2,1,0:T(4,128)(2,1)S(1)}, bf16[2,4,4...) custom-call(s32[32]{0:T(128)} %bitcast.1, ...), custom_call_target="tpu_custom_call" | custom-call | bytes 4521984 | tf_op jit(solution)/shard_map/first_pack/pallas_call | solution.py:144
  3.0 0.5 collective-permute-start.2
  3.6 2.6 %collective-permute-start = (bf16[2,4,1024]{2,1,0:T(4,128)(2,1)S(1)}, bf16[2,4,1024]{2,1,0:T(4,128)(2,1)S(1)}, u32[]{:S(2)}, u32[]{:S(2)}) collective-permute-start(bf16[2,4,1024]{2,1,0:T(4,128)(2,1)S(1)} %get-tuple-element.16), channel_id=1, source_target_pairs={{0,2},{1,3},{2,0},{3,1},{4,6},{5,7},{6,4},{7,5},{8,10},{9,11},{10,... | collective-permute-start | bytes 49160 | tf_op jit(solution)/shard_map/ppermute | solution.py:34
  6.1 0.1 collective-permute-start.1
  6.2 1.7 %collective-permute-start.13 = (bf16[2,2,256,512]{3,2,1,0:T(8,128)(2,1)S(1)}, bf16[2,2,256,512]{3,2,1,0:T(8,128)(2,1)S(1)}, u32[]{:S(2)}, u32[]{:S(2)}) collective-permute-start(bf16[2,2,256,512]{3,2,1,0:T(8,128)(2,1)S(1)} %get-tuple-element.14.refs_0_), channel_id=1, source_target_pairs={{0,2},{1,3},{2,0},{3,1},{4,6},{5,7},{6,4},{7,5},{8,10},{9,11},{10,... | collective-permute-start | bytes 3145736 | tf_op jit(solution)/shard_map/ppermute | solution.py:34
  8.0 1.3 %collective-permute-done.1.refs_1_ = bf16[2,4,1024]{2,1,0:T(4,128)(2,1)S(1)} collective-permute-done((bf16[2,4,1024]{2,1,0:T(4,128)(2,1)S(1)}, bf16[2,4,1024]{2,1,0:T(4,128)(2,1)S(1)}, u32[]{:S(2)}, u32[]{:S(2)}) %collective-permute-start.1) | collective-permute-done | bytes 16416 | tf_op jit(solution)/shard_map/ppermute | solution.py:34
  9.3 0.0 copy-start.1
  9.3 1.6 %collective-permute-start.3 = (bf16[2,2,4,1024]{3,2,1,0:T(4,128)(2,1)S(1)}, bf16[2,2,4,1024]{3,2,1,0:T(4,128)(2,1)S(1)}, u32[]{:S(2)}, u32[]{:S(2)}) collective-permute-start(bf16[2,2,4,1024]{3,2,1,0:T(4,128)(2,1)S(1)} %merge.1.refs_0_.refs_6_), channel_id=1, source_target_pairs={{0,4},{4,0},{8,12},{12,8},{1,5},{5,1},{9,13},{13,9},{2,6},{6,2},{1... | collective-permute-start | bytes 98312 | tf_op jit(solution)/shard_map/ppermute | solution.py:34
  11.0 2.6 %collective-permute-start.4 = (bf16[2,2,4,1024]{3,2,1,0:T(4,128)(2,1)S(1)}, bf16[2,2,4,1024]{3,2,1,0:T(4,128)(2,1)S(1)}, u32[]{:S(2)}, u32[]{:S(2)}) collective-permute-start(bf16[2,2,4,1024]{3,2,1,0:T(4,128)(2,1)S(1)} %merge.1.refs_0_.refs_6_), channel_id=1, source_target_pairs={{0,8},{4,12},{8,0},{12,4},{1,9},{5,13},{9,1},{13,5},{2,10},{6,14},... | collective-permute-start | bytes 98312 | tf_op jit(solution)/shard_map/ppermute | solution.py:34
  13.6 0.2 collective-permute-start.5
  13.8 2.3 %second_pack.1 = (bf16[2,2,256,512]{3,2,1,0:T(8,128)(2,1)S(1)}, bf16[2,2,256,512]{3,2,1,0:T(8,128)(2,1)S(1)}) custom-call(s32[32]{0:T(128)} %bitcast.2, bf16[8,2,256,512]{3,2,1,0:T(8,128)(2,1)} %cache_ref.3, bf16[2,2,4,1024]{3,2,1,0:T(4,128)(2,1)S(1)} %merge.1.refs_0_.refs_6_), custom_call_target="tpu_custom_call" | custom-call | flops 10000000000 | bytes 4194304 | tf_op jit(solution)/shard_map/second_pack/pallas_call | solution.py:164
  16.1 0.1 collective-permute-start.9
  16.2 0.2 collective-permute-done.4.refs_8_
  16.4 2.9 %collective-permute-done.5.refs_9_ = bf16[2,2,4,1024]{3,2,1,0:T(4,128)(2,1)S(1)} collective-permute-done((bf16[2,2,4,1024]{3,2,1,0:T(4,128)(2,1)S(1)}, bf16[2,2,4,1024]{3,2,1,0:T(4,128)(2,1)S(1)}, u32[]{:S(2)}, u32[]{:S(2)}) %collective-permute-start.5) | collective-permute-done | bytes 32800 | tf_op jit(solution)/shard_map/ppermute | solution.py:34
  19.3 3.8 %attend.1 = (bf16[10,32,128]{2,1,0:T(8,128)(2,1)S(1)}, bf16[10,32,128]{2,1,0:T(8,128)(2,1)S(1)}, bf16[10,32,128]{2,1,0:T(8,128)(2,1)S(1)}, bf16[10,32,128]{2,1,0:T(8,128)(2,1)S(1)}) custom-call(s32[32]{0:T(128)S(1)} %bitcast.3, s32[32]{0:T(128)S(1)} %copy-done.1, bf16[2,2,256,512]{3,2,1,0:T(8,128)(2,1)S(1)} %get-tuple-element.14.refs_0_, ...), custom_call_target="tpu_custom_call" | custom-call | flops 20000000000 | bytes 4194304 | tf_op jit(solution)/shard_map/attend/pallas_call | solution.py:304
  23.0 0.1 collective-permute-start.6
  23.1 1.1 %collective-permute-start.7 = (bf16[10,32,128]{2,1,0:T(8,128)(2,1)S(1)}, bf16[10,32,128]{2,1,0:T(8,128)(2,1)S(1)}, u32[]{:S(2)}, u32[]{:S(2)}) collective-permute-start(bf16[10,32,128]{2,1,0:T(8,128)(2,1)S(1)} %get-tuple-element.24), channel_id=1, source_target_pairs={{0,8},{4,12},{8,0},{12,4},{1,9},{5,13},{9,1},{13,5},{2,10},{6,14},... | collective-permute-start | bytes 245768 | tf_op jit(solution)/shard_map/ppermute | solution.py:34
  24.2 0.0 collective-permute-done.9.refs_1_
  24.2 3.3 %collective-permute-start.8 = (bf16[10,32,128]{2,1,0:T(8,128)(2,1)S(1)}, bf16[10,32,128]{2,1,0:T(8,128)(2,1)S(1)}, u32[]{:S(2)}, u32[]{:S(2)}) collective-permute-start(bf16[10,32,128]{2,1,0:T(8,128)(2,1)S(1)} %get-tuple-element.25), channel_id=1, source_target_pairs={{0,12},{4,8},{8,4},{12,0},{1,13},{5,9},{9,5},{13,1},{2,14},{6,10},... | collective-permute-start | bytes 245768 | tf_op jit(solution)/shard_map/ppermute | solution.py:34
  27.5 5.9 %fetch.1.refs_4_ = bf16[4096,2048]{1,0:T(8,128)(2,1)S(1)} custom-call(bf16[4096,2048]{1,0:T(8,128)(2,1)} %weight_ref.1, bf16[10,32,128]{2,1,0:T(8,128)(2,1)S(1)} %get-tuple-element.22.refs_0_, bf16[2,2,256,512]{3,2,1,0:T(8,128)(2,1)S(1)} %collective-permute-done.9.refs_1_), custom_call_target="tpu_custom_call" | custom-call | bytes 33554432 | tf_op jit(solution)/shard_map/fetch/pallas_call | solution.py:399
  33.4 0.0 collective-permute-done.6.refs_1_
  33.5 0.4 join.1.refs_0_
  33.9 0.1 collective-permute-start.10
  33.9 1.1 %collective-permute-start.11 = (bf16[8,4096]{1,0:T(8,128)(2,1)S(1)}, bf16[8,4096]{1,0:T(8,128)(2,1)S(1)}, u32[]{:S(2)}, u32[]{:S(2)}) collective-permute-start(bf16[8,4096]{1,0:T(8,128)(2,1)S(1)} %join.1.refs_0_), channel_id=1, source_target_pairs={{0,8},{4,12},{8,0},{12,4},{1,9},{5,13},{9,1},{13,5},{2,10},{6,14},... | collective-permute-start | bytes 196616 | tf_op jit(solution)/shard_map/ppermute | solution.py:34
  35.0 3.3 %collective-permute-start.12 = (bf16[8,4096]{1,0:T(8,128)(2,1)S(1)}, bf16[8,4096]{1,0:T(8,128)(2,1)S(1)}, u32[]{:S(2)}, u32[]{:S(2)}) collective-permute-start(bf16[8,4096]{1,0:T(8,128)(2,1)S(1)} %join.1.refs_0_), channel_id=1, source_target_pairs={{0,12},{4,8},{8,4},{12,0},{1,13},{5,9},{9,5},{13,1},{2,14},{6,10},... | collective-permute-start | bytes 196616 | tf_op jit(solution)/shard_map/ppermute | solution.py:34
  38.3 1.3 %place.3.refs_0_ = bf16[1,8,2,256,512]{4,3,2,1,0:T(8,128)(2,1)} custom-call(bf16[2,2,256,512]{3,2,1,0:T(8,128)(2,1)S(1)} %get-tuple-element.19.refs_2_.refs_0_, bf16[2,2,256,512]{3,2,1,0:T(8,128)(2,1)S(1)} %collective-permute-done.9.refs_1_), custom_call_target="tpu_custom_call" | custom-call | bytes 4194304 | tf_op jit(solution)/shard_map/place/pallas_call | solution.py:195
  39.7 0.2 collective-permute-done.11.refs_2_
  39.9 1.5 %collective-permute-done.12.refs_3_ = bf16[8,4096]{1,0:T(8,128)(2,1)S(1)} collective-permute-done((bf16[8,4096]{1,0:T(8,128)(2,1)S(1)}, bf16[8,4096]{1,0:T(8,128)(2,1)S(1)}, u32[]{:S(2)}, u32[]{:S(2)}) %collective-permute-start.12) | collective-permute-done | bytes 65568 | tf_op jit(solution)/shard_map/ppermute | solution.py:34
  41.4 3.6 %project.1.refs_1_ = bf16[8,4,2048]{2,1,0:T(4,128)(2,1)} custom-call(bf16[8,4096]{1,0:T(8,128)(2,1)S(1)} %join.1.refs_0_, bf16[8,4096]{1,0:T(8,128)(2,1)S(1)} %collective-permute-done.10.refs_1_, bf16[8,4096]{1,0:T(8,128)(2,1)S(1)} %collective-permute-done.11.refs_2_, bf16[8,4096]{1,0:T(8,128)(2,1)S(1)} %collective-permute-done.12.refs_3_, ...), custom_call_target="tpu_custom_call" | custom-call | flops 536870912 | bytes 16777216 | tf_op jit(solution)/shard_map/project/pallas_call | solution.py:430
  45.0 1.0 %place.4.refs_0_ = bf16[1,8,2,256,512]{4,3,2,1,0:T(8,128)(2,1)} custom-call(bf16[1,8,2,256,512]{4,3,2,1,0:T(8,128)(2,1)} %place.3.refs_0_, bf16[8,4,2048]{2,1,0:T(4,128)(2,1)} %project.1.refs_1_, bf16[2,2,256,512]{3,2,1,0:T(8,128)(2,1)S(1)} %collective-permute-done.13.refs_2_), custom_call_target="tpu_custom_call", output_to_operand_aliasing={{}: (0, {})} | custom-call | bytes 2097152 | tf_op jit(solution)/shard_map/place/pallas_call | solution.py:195
  46.0 8.1 %collective-permute-done.14.refs_2_ = bf16[2,2,256,512]{3,2,1,0:T(8,128)(2,1)S(1)} collective-permute-done((bf16[2,2,256,512]{3,2,1,0:T(8,128)(2,1)S(1)}, bf16[2,2,256,512]{3,2,1,0:T(8,128)(2,1)S(1)}, u32[]{:S(2)}, u32[]{:S(2)}) %collective-permute-start.14) | collective-permute-done | bytes 1048608 | tf_op jit(solution)/shard_map/ppermute | solution.py:34
  54.1 1.0 %place.5 = bf16[1,8,2,256,512]{4,3,2,1,0:T(8,128)(2,1)} custom-call(bf16[1,8,2,256,512]{4,3,2,1,0:T(8,128)(2,1)} %place.4.refs_0_, bf16[8,4,2048]{2,1,0:T(4,128)(2,1)} %project.1.refs_1_, bf16[2,2,256,512]{3,2,1,0:T(8,128)(2,1)S(1)} %collective-permute-done.14.refs_2_), custom_call_target="tpu_custom_call", output_to_operand_aliasing={{}: (0, {})} | custom-call | bytes 2097152 | tf_op jit(solution)/shard_map/place/pallas_call | solution.py:195
  (12 shorter events, 0.0 us)
Async XLA Ops:
  3.0 6.3 %collective-permute-start.2 = (bf16[2,4,4096]{2,1,0:T(4,128)(2,1)S(1)}, bf16[2,4,4096]{2,1,0:T(4,128)(2,1)S(1)}, u32[]{:S(2)}, u32[]{:S(2)}) collective-permute-start(bf16[2,4,4096]{2,1,0:T(4,128)(2,1)S(1)} %get-tuple-element.18), channel_id=1, source_target_pairs={{0,1},{1,0},{2,3},{3,2},{4,5},{5,4},{6,7},{7,6},{8,9},{9,8},{10,11... | collective-permute-start | bytes 196616 | tf_op jit(solution)/shard_map/ppermute | solution.py:34
  3.6 4.4 %collective-permute-start = (bf16[2,4,1024]{2,1,0:T(4,128)(2,1)S(1)}, bf16[2,4,1024]{2,1,0:T(4,128)(2,1)S(1)}, u32[]{:S(2)}, u32[]{:S(2)}) collective-permute-start(bf16[2,4,1024]{2,1,0:T(4,128)(2,1)S(1)} %get-tuple-element.16), channel_id=1, source_target_pairs={{0,2},{1,3},{2,0},{3,1},{4,6},{5,7},{6,4},{7,5},{8,10},{9,11},{10,... | collective-permute-start | bytes 49160 | tf_op jit(solution)/shard_map/ppermute | solution.py:34
  6.1 3.2 %collective-permute-start.1 = (bf16[2,4,1024]{2,1,0:T(4,128)(2,1)S(1)}, bf16[2,4,1024]{2,1,0:T(4,128)(2,1)S(1)}, u32[]{:S(2)}, u32[]{:S(2)}) collective-permute-start(bf16[2,4,1024]{2,1,0:T(4,128)(2,1)S(1)} %get-tuple-element.17), channel_id=1, source_target_pairs={{0,3},{1,2},{2,1},{3,0},{4,7},{5,6},{6,5},{7,4},{8,11},{9,10},{10,... | collective-permute-start | bytes 49160 | tf_op jit(solution)/shard_map/ppermute | solution.py:34
  6.2 38.8 %collective-permute-start.13 = (bf16[2,2,256,512]{3,2,1,0:T(8,128)(2,1)S(1)}, bf16[2,2,256,512]{3,2,1,0:T(8,128)(2,1)S(1)}, u32[]{:S(2)}, u32[]{:S(2)}) collective-permute-start(bf16[2,2,256,512]{3,2,1,0:T(8,128)(2,1)S(1)} %get-tuple-element.14.refs_0_), channel_id=1, source_target_pairs={{0,2},{1,3},{2,0},{3,1},{4,6},{5,7},{6,4},{7,5},{8,10},{9,11},{10,... | collective-permute-start | bytes 3145736 | tf_op jit(solution)/shard_map/ppermute | solution.py:34
  7.9 46.1 %collective-permute-start.14 = (bf16[2,2,256,512]{3,2,1,0:T(8,128)(2,1)S(1)}, bf16[2,2,256,512]{3,2,1,0:T(8,128)(2,1)S(1)}, u32[]{:S(2)}, u32[]{:S(2)}) collective-permute-start(bf16[2,2,256,512]{3,2,1,0:T(8,128)(2,1)S(1)} %get-tuple-element.15.refs_1_), channel_id=1, source_target_pairs={{0,3},{1,2},{2,1},{3,0},{4,7},{5,6},{6,5},{7,4},{8,11},{9,10},{10,... | collective-permute-start | bytes 3145736 | tf_op jit(solution)/shard_map/ppermute | solution.py:34
  9.3 10.0 %copy-start = (s32[32,1]{0,1:T(1,128)S(1)}, s32[32,1]{0,1:T(1,128)}, u32[]{:S(2)}) copy-start(s32[32,1]{0,1:T(1,128)} %param.7) | copy-start | bytes 388
  9.3 10.0 %copy-start.1 = (s32[32]{0:T(128)S(1)}, s32[32]{0:T(128)}, u32[]{:S(2)}) copy-start(s32[32]{0:T(128)} %lengths_ref.1) | copy-start | bytes 388
  9.3 6.8 %collective-permute-start.3 = (bf16[2,2,4,1024]{3,2,1,0:T(4,128)(2,1)S(1)}, bf16[2,2,4,1024]{3,2,1,0:T(4,128)(2,1)S(1)}, u32[]{:S(2)}, u32[]{:S(2)}) collective-permute-start(bf16[2,2,4,1024]{3,2,1,0:T(4,128)(2,1)S(1)} %merge.1.refs_0_.refs_6_), channel_id=1, source_target_pairs={{0,4},{4,0},{8,12},{12,8},{1,5},{5,1},{9,13},{13,9},{2,6},{6,2},{1... | collective-permute-start | bytes 98312 | tf_op jit(solution)/shard_map/ppermute | solution.py:34
  11.0 5.4 %collective-permute-start.4 = (bf16[2,2,4,1024]{3,2,1,0:T(4,128)(2,1)S(1)}, bf16[2,2,4,1024]{3,2,1,0:T(4,128)(2,1)S(1)}, u32[]{:S(2)}, u32[]{:S(2)}) collective-permute-start(bf16[2,2,4,1024]{3,2,1,0:T(4,128)(2,1)S(1)} %merge.1.refs_0_.refs_6_), channel_id=1, source_target_pairs={{0,8},{4,12},{8,0},{12,4},{1,9},{5,13},{9,1},{13,5},{2,10},{6,14},... | collective-permute-start | bytes 98312 | tf_op jit(solution)/shard_map/ppermute | solution.py:34
  13.6 5.7 %collective-permute-start.5 = (bf16[2,2,4,1024]{3,2,1,0:T(4,128)(2,1)S(1)}, bf16[2,2,4,1024]{3,2,1,0:T(4,128)(2,1)S(1)}, u32[]{:S(2)}, u32[]{:S(2)}) collective-permute-start(bf16[2,2,4,1024]{3,2,1,0:T(4,128)(2,1)S(1)} %merge.1.refs_0_.refs_6_), channel_id=1, source_target_pairs={{0,12},{4,8},{8,4},{12,0},{1,13},{5,9},{9,5},{13,1},{2,14},{6,10},... | collective-permute-start | bytes 98312 | tf_op jit(solution)/shard_map/ppermute | solution.py:34
  16.1 8.1 %collective-permute-start.9 = (bf16[2,2,256,512]{3,2,1,0:T(8,128)(2,1)S(1)}, bf16[2,2,256,512]{3,2,1,0:T(8,128)(2,1)S(1)}, u32[]{:S(2)}, u32[]{:S(2)}) collective-permute-start(bf16[2,2,256,512]{3,2,1,0:T(8,128)(2,1)S(1)} %get-tuple-element.20.refs_3_), channel_id=1, source_target_pairs={{0,1},{1,0},{2,3},{3,2},{4,5},{5,4},{6,7},{7,6},{8,9},{9,8},{10,11... | collective-permute-start | bytes 3145736 | tf_op jit(solution)/shard_map/ppermute | solution.py:34
  23.0 10.4 %collective-permute-start.6 = (bf16[10,32,128]{2,1,0:T(8,128)(2,1)S(1)}, bf16[10,32,128]{2,1,0:T(8,128)(2,1)S(1)}, u32[]{:S(2)}, u32[]{:S(2)}) collective-permute-start(bf16[10,32,128]{2,1,0:T(8,128)(2,1)S(1)} %get-tuple-element.23), channel_id=1, source_target_pairs={{0,4},{4,0},{8,12},{12,8},{1,5},{5,1},{9,13},{13,9},{2,6},{6,2},{1... | collective-permute-start | bytes 245768 | tf_op jit(solution)/shard_map/ppermute | solution.py:34
  23.1 10.3 %collective-permute-start.7 = (bf16[10,32,128]{2,1,0:T(8,128)(2,1)S(1)}, bf16[10,32,128]{2,1,0:T(8,128)(2,1)S(1)}, u32[]{:S(2)}, u32[]{:S(2)}) collective-permute-start(bf16[10,32,128]{2,1,0:T(8,128)(2,1)S(1)} %get-tuple-element.24), channel_id=1, source_target_pairs={{0,8},{4,12},{8,0},{12,4},{1,9},{5,13},{9,1},{13,5},{2,10},{6,14},... | collective-permute-start | bytes 245768 | tf_op jit(solution)/shard_map/ppermute | solution.py:34
  24.2 9.2 %collective-permute-start.8 = (bf16[10,32,128]{2,1,0:T(8,128)(2,1)S(1)}, bf16[10,32,128]{2,1,0:T(8,128)(2,1)S(1)}, u32[]{:S(2)}, u32[]{:S(2)}) collective-permute-start(bf16[10,32,128]{2,1,0:T(8,128)(2,1)S(1)} %get-tuple-element.25), channel_id=1, source_target_pairs={{0,12},{4,8},{8,4},{12,0},{1,13},{5,9},{9,5},{13,1},{2,14},{6,10},... | collective-permute-start | bytes 245768 | tf_op jit(solution)/shard_map/ppermute | solution.py:34
  33.9 5.8 %collective-permute-start.10 = (bf16[8,4096]{1,0:T(8,128)(2,1)S(1)}, bf16[8,4096]{1,0:T(8,128)(2,1)S(1)}, u32[]{:S(2)}, u32[]{:S(2)}) collective-permute-start(bf16[8,4096]{1,0:T(8,128)(2,1)S(1)} %join.1.refs_0_), channel_id=1, source_target_pairs={{0,4},{4,0},{8,12},{12,8},{1,5},{5,1},{9,13},{13,9},{2,6},{6,2},{1... | collective-permute-start | bytes 196616 | tf_op jit(solution)/shard_map/ppermute | solution.py:34
  33.9 5.9 %collective-permute-start.11 = (bf16[8,4096]{1,0:T(8,128)(2,1)S(1)}, bf16[8,4096]{1,0:T(8,128)(2,1)S(1)}, u32[]{:S(2)}, u32[]{:S(2)}) collective-permute-start(bf16[8,4096]{1,0:T(8,128)(2,1)S(1)} %join.1.refs_0_), channel_id=1, source_target_pairs={{0,8},{4,12},{8,0},{12,4},{1,9},{5,13},{9,1},{13,5},{2,10},{6,14},... | collective-permute-start | bytes 196616 | tf_op jit(solution)/shard_map/ppermute | solution.py:34
  35.0 6.3 %collective-permute-start.12 = (bf16[8,4096]{1,0:T(8,128)(2,1)S(1)}, bf16[8,4096]{1,0:T(8,128)(2,1)S(1)}, u32[]{:S(2)}, u32[]{:S(2)}) collective-permute-start(bf16[8,4096]{1,0:T(8,128)(2,1)S(1)} %join.1.refs_0_), channel_id=1, source_target_pairs={{0,12},{4,8},{8,4},{12,0},{1,13},{5,9},{9,5},{13,1},{2,14},{6,10},... | collective-permute-start | bytes 196616 | tf_op jit(solution)/shard_map/ppermute | solution.py:34

commit v9 on v8

--- a/solution.py
+++ b/solution.py
@@ -48,7 +48,7 @@
         source[target * CAP + order] = i
 
 
-def pack_slots(pieces, section_count):
+def halves_of(pieces):
     return [
         (n, place, offset, first + place)
         for n, (offset, first, count) in enumerate(pieces)
@@ -60,41 +60,43 @@
     section = lax.axis_index("sec")
     full = section_count * CAP == REQ_GRP
     own_slots(routing_ref, section, used, source)
-    spots = pack_slots(pieces, section_count)
-
-    def copy(n, place, offset, order, row):
-        return pltpu.make_async_copy(cache_ref.at[row], out_refs[n].at[place], sem.at[offset * CAP + order])
-
-    for n, place, offset, order in spots:
-        target = section ^ offset
+    halves = halves_of(pieces)
+
+    def copy(n, place, offset, half, row):
+        return pltpu.make_async_copy(
+            cache_ref.at[row, half % 2], out_refs[n].at[place], sem.at[offset * 2 * CAP + half]
+        )
+
+    for n, place, offset, half in halves:
+        target, order = section ^ offset, half // 2
         if full:
-            copy(n, place, offset, order, source[target * CAP + order]).start()
+            copy(n, place, offset, half, source[target * CAP + order]).start()
         else:
 
             @pl.when(order < used[target])
             def _():
-                copy(n, place, offset, order, source[target * CAP + order]).start()
+                copy(n, place, offset, half, source[target * CAP + order]).start()
 
             @pl.when(order >= used[target])
             def _():
                 out_refs[n][place] = jnp.zeros_like(out_refs[n][place])
 
     def finish():
-        for n, place, offset, order in spots:
+        for n, place, offset, half in halves:
             if full:
-                copy(n, place, offset, order, 0).wait()
+                copy(n, place, offset, half, 0).wait()
             else:
 
-                @pl.when(order < used[section ^ offset])
+                @pl.when(half // 2 < used[section ^ offset])
                 def _():
-                    copy(n, place, offset, order, 0).wait()
+                    copy(n, place, offset, half, 0).wait()
 
     return finish
 
 
 def first_pack_kernel(pieces, section_count, routing_ref, cache_ref, query_ref, *refs):
-    cache_out, query_out = refs[: len(pieces)], refs[len(pieces) : -4]
-    source, used, sem, query_sem = refs[-4:]
+    refs, (source, used, sem, query_sem) = refs[:-4], refs[-4:]
+    query_out, cache_out = refs[-section_count:], refs[-section_count - len(pieces) : -section_count]
     section = lax.axis_index("sec")
     query_copies = []
     for offset, out_ref in enumerate(query_out):
@@ -109,7 +111,7 @@
         copy.wait()
 
 
-def second_pack_kernel(pieces, section_count, routing_ref, cache_ref, *refs):
+def pack_kernel(pieces, section_count, routing_ref, cache_ref, *refs):
     cache_out, (source, used, sem) = refs[-3 - len(pieces) : -3], refs[-3:]
     start_packing(pieces, section_count, routing_ref, cache_ref, cache_out, source, used, sem)()
 
@@ -136,44 +138,44 @@
     return pltpu.with_memory_space_constraint(value, pltpu.HBM)
 
 
-def first_pack(routing, cache, queries, pieces, section_count, tp_count):
+def first_pack(routing, cache, queries, others, pieces, section_count, tp_count):
     samples, width = queries.shape[2:]
     widths = [width if offset < 2 else width // tp_count for offset in range(section_count)]
-    shapes = [jax.ShapeDtypeStruct((count,) + cache.shape[1:], cache.dtype) for _, _, count in pieces]
+    shapes = [jax.ShapeDtypeStruct((count,) + cache.shape[2:], cache.dtype) for _, _, count in pieces]
     shapes += [jax.ShapeDtypeStruct((CAP, samples, one), queries.dtype) for one in widths]
     parts = pl.pallas_call(
         functools.partial(first_pack_kernel, pieces, section_count),
         out_shape=shapes,
-        in_specs=[SMEM, HBM, HBM],
+        in_specs=[SMEM, HBM, HBM] + [ANY] * len(others),
         out_specs=[VMEM] * len(shapes),
         scratch_shapes=[
             pltpu.SMEM((section_count * CAP,), jnp.int32),
             pltpu.SMEM((section_count,), jnp.int32),
-            pltpu.SemaphoreType.DMA((section_count * CAP,)),
+            pltpu.SemaphoreType.DMA((section_count * CAP * 2,)),
             pltpu.SemaphoreType.DMA((section_count,)),
         ],
         compiler_params=limit(16),
         cost_estimate=cost(0, 4 * sum(shape.size for shape in shapes)),
         name="first_pack",
-    )(in_hbm(routing), in_hbm(cache), in_hbm(queries))
+    )(in_hbm(routing), in_hbm(cache), in_hbm(queries), *others)
     return parts[: len(pieces)], parts[len(pieces) :]
 
 
-def second_pack(routing, cache, others, pieces, section_count):
-    shapes = [jax.ShapeDtypeStruct((count,) + cache.shape[1:], cache.dtype) for _, _, count in pieces]
-    return pl.pallas_call(
-        functools.partial(second_pack_kernel, pieces, section_count),
+def pack(routing, cache, others, pieces, section_count, flops=0):
+    shapes = [jax.ShapeDtypeStruct((count,) + cache.shape[2:], cache.dtype) for _, _, count in pieces]
+    return pl.pallas_call(
+        functools.partial(pack_kernel, pieces, section_count),
         out_shape=shapes,
         in_specs=[SMEM, HBM] + [ANY] * len(others),
         out_specs=[VMEM] * len(shapes),
         scratch_shapes=[
             pltpu.SMEM((section_count * CAP,), jnp.int32),
             pltpu.SMEM((section_count,), jnp.int32),
-            pltpu.SemaphoreType.DMA((section_count * CAP,)),
+            pltpu.SemaphoreType.DMA((section_count * CAP * 2,)),
         ],
         compiler_params=limit(16),
-        cost_estimate=cost(10**10, 4 * sum(shape.size for shape in shapes)),
-        name="second_pack",
+        cost_estimate=cost(flops, 4 * sum(shape.size for shape in shapes)),
+        name="pack",
     )(in_hbm(routing), in_hbm(cache), *others)
 
 
@@ -183,8 +185,8 @@
     section = lax.axis_index("sec")
     copies = []
     for n, (offset, first, size) in enumerate(pieces):
-        slots = out_ref.at[0, pl.ds((section ^ offset) * CAP + first, size)]
-        copies.append(pltpu.make_async_copy(part_refs[n], slots, sem.at[n]))
+        halves = out_ref.at[0, pl.ds((section ^ offset) * 2 * CAP + first, size)]
+        copies.append(pltpu.make_async_copy(part_refs[n], halves, sem.at[n]))
         copies[-1].start()
     for copy in copies:
         copy.wait()
@@ -194,7 +196,7 @@
     part = parts[0]
     return pl.pallas_call(
         functools.partial(place_kernel, pieces),
-        out_shape=jax.ShapeDtypeStruct((1, slot_count) + part.shape[1:], part.dtype),
+        out_shape=jax.ShapeDtypeStruct((1, 2 * slot_count) + part.shape[1:], part.dtype),
         in_specs=[HBM] * len(given) + [VMEM] * len(parts),
         out_specs=HBM,
         scratch_shapes=[pltpu.SemaphoreType.DMA((len(parts),))],
@@ -212,7 +214,7 @@
     source, used, messages, stats, stacked, far_queries = refs[2 + 2 * tp_count :]
     section = lax.axis_index("sec")
     tp_index = lax.axis_index("tp")
-    local = cache_refs[0].shape[2]
+    local = cache_refs[0].shape[1]
     groups, rows, _ = messages.shape[1:]
     span = KEY_VALUE_HEADS * rows
     prompts = max(1, groups // KEY_VALUE_HEADS)
@@ -224,7 +226,10 @@
     position = lax.broadcasted_iota(jnp.int32, (local, span), 0) + tp_index * local
     owner = lax.broadcasted_iota(jnp.int32, (HEAD_SIZE, span), 1) // rows
 
-    def prompt(cache_ref, place, offset, order):
+    held = {(offset, half): cache_refs[n].at[place] for n, place, offset, half in halves_of(pieces)}
+
+    def prompt(offset, order):
+        keys_ref, values_ref = held[offset, 2 * order], held[offset, 2 * order + 1]
         row = source[(section ^ offset) * CAP + order]
         visible = position < lengths_ref[section * REQ_GRP + row]
         slot = offset * CAP + order
@@ -239,7 +244,7 @@
         query = stacked[slot].T.astype(jnp.bfloat16)
         query = [jnp.where(owner == k, query, jnp.zeros_like(query)) for k in range(KEY_VALUE_HEADS)]
         score = jnp.dot(
-            cache_ref[place, 0], jnp.concatenate(query, axis=0), preferred_element_type=jnp.float32
+            keys_ref[...], jnp.concatenate(query, axis=0), preferred_element_type=jnp.float32
         ) * HEAD_SIZE ** (-0.5)
         score = jnp.where(visible, score, HIDDEN)
         peak = jnp.max(score, axis=0, keepdims=True)
@@ -252,19 +257,19 @@
         for k in range(KEY_VALUE_HEADS):
             mixed = jnp.dot(
                 weight[k * rows : (k + 1) * rows],
-                cache_ref[place, 1, :, k * HEAD_SIZE : (k + 1) * HEAD_SIZE],
+                values_ref[:, k * HEAD_SIZE : (k + 1) * HEAD_SIZE],
                 preferred_element_type=jnp.float32,
             )
             group = row * KEY_VALUE_HEADS + k
             messages[group // groups, group % groups] = mixed.astype(jnp.bfloat16)
 
-    for cache_ref, (offset, first, size) in zip(cache_refs, pieces):
-        for place in range(size):
-            one = functools.partial(prompt, cache_ref, place, offset, first + place)
+    for offset, half in held:
+        if half % 2 == 0:
+            one = functools.partial(prompt, offset, half // 2)
             if full:
                 one()
             else:
-                pl.when(first + place < used[section ^ offset])(one)
+                pl.when(half // 2 < used[section ^ offset])(one)
 
     level = stats[...]
     high = level.astype(jnp.bfloat16).astype(jnp.float32)
@@ -300,7 +305,7 @@
     span = width // HEAD_SIZE * samples
     rows = span // KEY_VALUE_HEADS
     groups = REQ_GRP * KEY_VALUE_HEADS // tp_count
-    multiplies = REQ_GRP * span * HEAD_SIZE * caches[0].shape[2]
+    multiplies = REQ_GRP * span * HEAD_SIZE * caches[0].shape[1]
     return pl.pallas_call(
         functools.partial(attend_kernel, pieces, section_count, tp_count),
         out_shape=[jax.ShapeDtypeStruct((groups + 2, rows, HEAD_SIZE), jnp.bfloat16)] * tp_count,
@@ -444,16 +449,26 @@
     slot_count, samples, query_width = queries.shape[1:]
     routing = routing.reshape(-1)
 
-    near = [(offset, 0, CAP) for offset in range(2)]
-    far = [(offset, 0, CAP) for offset in range(2, section_count)]
-    far_caches, query_parts = first_pack(routing, prompt_key_values, queries, far, section_count, tp_count)
+    whole = 2 * CAP
+    near = [(offset, 0, whole) for offset in range(2)]
+    head, tail = [(2, 0, 1)], [(2, 1, whole - 1)]
+    far = tail + [(offset, 0, whole) for offset in range(3, section_count)]
+
+    def across(parts, pieces):
+        return [swap(part, "sec", piece[0]) for part, piece in zip(parts, pieces)]
+
+    head_caches = pack(routing, prompt_key_values, [], head, section_count)
+    head_parts = across(head_caches, head)
+    far_caches, query_parts = first_pack(
+        routing, prompt_key_values, queries, head_caches, far, section_count, tp_count
+    )
     query_parts = [swap(part, "sec", offset) for offset, part in enumerate(query_parts)]
-    far_parts = [swap(part, "sec", piece[0]) for part, piece in zip(far_caches, far)]
-    merged = merge(query_parts[2:], query_parts[1:2])
+    far_parts = across(far_caches, far)
+    merged = merge(query_parts[2:], head_parts)
     far_queries = spread(merged, "tp")
-    near_caches = second_pack(routing, prompt_key_values, [merged], near, section_count)
-    near_parts = [swap(part, "sec", piece[0]) for part, piece in zip(near_caches, near)]
-    caches, pieces = [*far_caches, *near_caches], far + near
+    near_caches = pack(routing, prompt_key_values, [merged, query_parts[1]], near, section_count, 10**10)
+    near_parts = across(near_caches, near)
+    caches, pieces = [*head_caches, *far_caches, *near_caches], head + far + near
 
     messages = attend(routing, lengths, caches, pieces, query_parts[:2], far_queries)
     partials = [swap(part, "tp", offset) for offset, part in enumerate(messages)]
@@ -469,10 +484,11 @@
     else:
         layer_out = project(shares, held_weight, samples)
 
-    whole = place([], near_parts, near, slot_count)
+    held_cache = place([], near_parts + head_parts, near + head, slot_count)
     for part, piece in zip(far_parts, far):
-        whole = place([whole, layer_out], [part], [piece], slot_count)
-    return (layer_out, whole)
+        held_cache = place([held_cache, layer_out], [part], [piece], slot_count)
+    held_cache = held_cache.reshape((1, slot_count) + prompt_key_values.shape[1:])
+    return (layer_out, held_cache)
 
 
 def solution(mesh):

time: 55.2 us -> 52.7 us (0.955)
  waiting for transfers between devices: 14.2 us -> 7.86 us
  starting transfers between devices: 18.3 us -> 20.3 us
  Pallas kernels: 21.7 us -> 23.6 us
    ppermute x15 -> x16, waiting for transfers between devices: 14.2 us -> 7.86 us  [swap(): return lax.ppermute(value, axis, [(i, i ^ offset) for i in range(count)])]
    ppermute x15 -> x16, starting transfers between devices: 18.3 us -> 20.3 us  [swap(): return lax.ppermute(value, axis, [(i, i ^ offset) for i in range(count)])]
    pallas_call x1 -> x2, Pallas kernels: 2.3 us -> 4.17 us  [pack(): pl.pallas_call(functools.partial(pack_kernel, pieces, section_count), out...]
  transfers between devices with their start and end apart: 15 -> 16, of which waited for: 6 -> 5; matrix products, arithmetic and copies ran while one was open for 0% -> 0% of each run, Pallas kernels for 33% -> 40%
where the time goes in v9:
time: 52.7 us; the launch traced here: 52.5 us
  Pallas kernels  23.6 us (45%)
  starting transfers between devices  20.3 us (39%)
  waiting for transfers between devices  7.86 us (15%)
  between operations  0.77 us (1%)
    ppermute x16, starting transfers between devices, swap(): return lax.ppermute(value, axis, [(i, i ^ offset) for i in range(count)])  20.3 us
    ppermute x16, waiting for transfers between devices, swap(): return lax.ppermute(value, axis, [(i, i ^ offset) for i in range(count)])  7.86 us
    pallas_call x1, Pallas kernels, fetch(): pl.pallas_call(fetch_kernel, out_shape=jax.ShapeDtypeStruct(weight.shape,...  5.92 us
    pallas_call x2, Pallas kernels, pack(): pl.pallas_call(functools.partial(pack_kernel, pieces, section_count), out...  4.17 us
    pallas_call x1, Pallas kernels, attend(): pl.pallas_call(functools.partial(attend_kernel, pieces, section_count, tp...  3.76 us
    pallas_call x1, Pallas kernels, project(): pl.pallas_call(functools.partial(project_kernel, count, min(256, width)),...  3.64 us
    pallas_call x3, Pallas kernels, place(): pl.pallas_call(functools.partial(place_kernel, pieces), out_shape=jax.Sha...  3.28 us
    pallas_call x1, Pallas kernels, first_pack(): pl.pallas_call(functools.partial(first_pack_kernel, pieces, section_count...  2.4 us
  transfers between devices with their start and end apart: 16, of which 5 were waited for; matrix products, arithmetic and copies ran while one was open for 0% of the time, Pallas kernels for 40%

profile of v9, /device:TPU:0, one launch (start us, length us, event | category | flops | bytes accessed | tf_op | source)
XLA Modules:
  0.0 52.5 jit_solution(17852935676062192727)
XLA Ops:
  0.6 1.8 %pack.2.refs_0_ = bf16[1,256,512]{2,1,0:T(8,128)(2,1)S(1)} custom-call(s32[32]{0:T(128)} %bitcast.2, bf16[8,2,256,512]{3,2,1,0:T(8,128)(2,1)} %cache_ref.5), custom_call_target="tpu_custom_call" | custom-call | bytes 524288 | tf_op jit(solution)/shard_map/pack/pallas_call | solution.py:166
  2.4 3.0 %collective-permute-start.2 = (bf16[1,256,512]{2,1,0:T(8,128)(2,1)S(1)}, bf16[1,256,512]{2,1,0:T(8,128)(2,1)S(1)}, u32[]{:S(2)}, u32[]{:S(2)}) collective-permute-start(bf16[1,256,512]{2,1,0:T(8,128)(2,1)S(1)} %pack.2.refs_0_), channel_id=1, source_target_pairs={{0,2},{1,3},{2,0},{3,1},{4,6},{5,7},{6,4},{7,5},{8,10},{9,11},{10,... | collective-permute-start | bytes 786440 | tf_op jit(solution)/shard_map/ppermute | solution.py:34
  5.5 2.4 %first_pack.1 = (bf16[3,256,512]{2,1,0:T(8,128)(2,1)S(1)}, bf16[4,256,512]{2,1,0:T(8,128)(2,1)S(1)}, bf16[2,4,4096]{2,1,0:T(4,128)(2,1)S(1)}, bf16[2,4,4096]{2,1...) custom-call(s32[32]{0:T(128)} %bitcast.3, bf16[8,2,256,512]{3,2,1,0:T(8,128)(2,1)} %cache_ref.5, ...), custom_call_target="tpu_custom_call" | custom-call | bytes 3997696 | tf_op jit(solution)/shard_map/first_pack/pallas_call | solution.py:146
  7.9 0.1 collective-permute-start.3
  7.9 0.1 collective-permute-start
  8.0 1.8 %collective-permute-start.1 = (bf16[2,4,1024]{2,1,0:T(4,128)(2,1)S(1)}, bf16[2,4,1024]{2,1,0:T(4,128)(2,1)S(1)}, u32[]{:S(2)}, u32[]{:S(2)}) collective-permute-start(bf16[2,4,1024]{2,1,0:T(4,128)(2,1)S(1)} %get-tuple-element.17), channel_id=1, source_target_pairs={{0,3},{1,2},{2,1},{3,0},{4,7},{5,6},{6,5},{7,4},{8,11},{9,10},{10,... | collective-permute-start | bytes 49160 | tf_op jit(solution)/shard_map/ppermute | solution.py:34
  9.8 0.3 collective-permute-start.14
  10.1 2.2 %collective-permute-done.refs_0_ = bf16[2,4,1024]{2,1,0:T(4,128)(2,1)S(1)} collective-permute-done((bf16[2,4,1024]{2,1,0:T(4,128)(2,1)S(1)}, bf16[2,4,1024]{2,1,0:T(4,128)(2,1)S(1)}, u32[]{:S(2)}, u32[]{:S(2)}) %collective-permute-start) | collective-permute-done | bytes 16416 | tf_op jit(solution)/shard_map/ppermute | solution.py:34
  12.3 0.1 collective-permute-start.15
  12.4 0.1 collective-permute-done.1.refs_1_
  12.5 0.0 copy-start.1
  12.5 1.7 %collective-permute-start.4 = (bf16[2,2,4,1024]{3,2,1,0:T(4,128)(2,1)S(1)}, bf16[2,2,4,1024]{3,2,1,0:T(4,128)(2,1)S(1)}, u32[]{:S(2)}, u32[]{:S(2)}) collective-permute-start(bf16[2,2,4,1024]{3,2,1,0:T(4,128)(2,1)S(1)} %merge.1.refs_0_.refs_7_), channel_id=1, source_target_pairs={{0,4},{4,0},{8,12},{12,8},{1,5},{5,1},{9,13},{13,9},{2,6},{6,2},{1... | collective-permute-start | bytes 98312 | tf_op jit(solution)/shard_map/ppermute | solution.py:34
  14.2 2.6 %collective-permute-start.5 = (bf16[2,2,4,1024]{3,2,1,0:T(4,128)(2,1)S(1)}, bf16[2,2,4,1024]{3,2,1,0:T(4,128)(2,1)S(1)}, u32[]{:S(2)}, u32[]{:S(2)}) collective-permute-start(bf16[2,2,4,1024]{3,2,1,0:T(4,128)(2,1)S(1)} %merge.1.refs_0_.refs_7_), channel_id=1, source_target_pairs={{0,8},{4,12},{8,0},{12,4},{1,9},{5,13},{9,1},{13,5},{2,10},{6,14},... | collective-permute-start | bytes 98312 | tf_op jit(solution)/shard_map/ppermute | solution.py:34
  16.8 0.1 collective-permute-start.6
  17.0 2.4 %pack.3 = (bf16[4,256,512]{2,1,0:T(8,128)(2,1)S(1)}, bf16[4,256,512]{2,1,0:T(8,128)(2,1)S(1)}) custom-call(s32[32]{0:T(128)} %bitcast.4, bf16[8,2,256,512]{3,2,1,0:T(8,128)(2,1)} %cache_ref.5, bf16[2,2,4,1024]{3,2,1,0:T(4,128)(2,1)S(1)} %merge.1.refs_0_.refs_7_, bf16[2,4,4096]{2,1,0:T(4,128)(2,1)S(1)} %collective-permute-done.3.refs_1_.refs_6_), custom_call_target="tpu_custom_call" | custom-call | flops 10000000000 | bytes 4194304 | tf_op jit(solution)/shard_map/pack/pallas_call | solution.py:166
  19.3 1.5 %collective-permute-start.10 = (bf16[4,256,512]{2,1,0:T(8,128)(2,1)S(1)}, bf16[4,256,512]{2,1,0:T(8,128)(2,1)S(1)}, u32[]{:S(2)}, u32[]{:S(2)}) collective-permute-start(bf16[4,256,512]{2,1,0:T(8,128)(2,1)S(1)} %get-tuple-element.20.refs_4_), channel_id=1, source_target_pairs={{0,1},{1,0},{2,3},{3,2},{4,5},{5,4},{6,7},{7,6},{8,9},{9,8},{10,11... | collective-permute-start | bytes 3145736 | tf_op jit(solution)/shard_map/ppermute | solution.py:34
  20.9 1.6 %collective-permute-done.6.refs_10_ = bf16[2,2,4,1024]{3,2,1,0:T(4,128)(2,1)S(1)} collective-permute-done((bf16[2,2,4,1024]{3,2,1,0:T(4,128)(2,1)S(1)}, bf16[2,2,4,1024]{3,2,1,0:T(4,128)(2,1)S(1)}, u32[]{:S(2)}, u32[]{:S(2)}) %collective-permute-start.6) | collective-permute-done | bytes 32800 | tf_op jit(solution)/shard_map/ppermute | solution.py:34
  22.5 3.8 %attend.1 = (bf16[10,32,128]{2,1,0:T(8,128)(2,1)S(1)}, bf16[10,32,128]{2,1,0:T(8,128)(2,1)S(1)}, bf16[10,32,128]{2,1,0:T(8,128)(2,1)S(1)}, bf16[10,32,128]{2,1,0:T(8,128)(2,1)S(1)}) custom-call(s32[32]{0:T(128)S(1)} %bitcast.5, s32[32]{0:T(128)S(1)} %copy-done.1, bf16[1,256,512]{2,1,0:T(8,128)(2,1)S(1)} %pack.2.refs_0_, ...), custom_call_target="tpu_custom_call" | custom-call | flops 20000000000 | bytes 4194304 | tf_op jit(solution)/shard_map/attend/pallas_call | solution.py:309
  26.3 0.1 collective-permute-start.7
  26.4 2.5 %collective-permute-start.8 = (bf16[10,32,128]{2,1,0:T(8,128)(2,1)S(1)}, bf16[10,32,128]{2,1,0:T(8,128)(2,1)S(1)}, u32[]{:S(2)}, u32[]{:S(2)}) collective-permute-start(bf16[10,32,128]{2,1,0:T(8,128)(2,1)S(1)} %get-tuple-element.24), channel_id=1, source_target_pairs={{0,8},{4,12},{8,0},{12,4},{1,9},{5,13},{9,1},{13,5},{2,10},{6,14},... | collective-permute-start | bytes 245768 | tf_op jit(solution)/shard_map/ppermute | solution.py:34
  28.9 1.9 %collective-permute-start.9 = (bf16[10,32,128]{2,1,0:T(8,128)(2,1)S(1)}, bf16[10,32,128]{2,1,0:T(8,128)(2,1)S(1)}, u32[]{:S(2)}, u32[]{:S(2)}) collective-permute-start(bf16[10,32,128]{2,1,0:T(8,128)(2,1)S(1)} %get-tuple-element.25), channel_id=1, source_target_pairs={{0,12},{4,8},{8,4},{12,0},{1,13},{5,9},{9,5},{13,1},{2,14},{6,10},... | collective-permute-start | bytes 245768 | tf_op jit(solution)/shard_map/ppermute | solution.py:34
  30.8 5.9 %fetch.1.refs_4_ = bf16[4096,2048]{1,0:T(8,128)(2,1)S(1)} custom-call(bf16[4096,2048]{1,0:T(8,128)(2,1)} %weight_ref.1, bf16[10,32,128]{2,1,0:T(8,128)(2,1)S(1)} %get-tuple-element.22.refs_0_, bf16[4,256,512]{2,1,0:T(8,128)(2,1)S(1)} %collective-permute-done.10.refs_1_), custom_call_target="tpu_custom_call" | custom-call | bytes 33554432 | tf_op jit(solution)/shard_map/fetch/pallas_call | solution.py:404
  36.7 0.4 join.1.refs_0_
  37.1 1.4 %collective-permute-start.11 = (bf16[8,4096]{1,0:T(8,128)(2,1)S(1)}, bf16[8,4096]{1,0:T(8,128)(2,1)S(1)}, u32[]{:S(2)}, u32[]{:S(2)}) collective-permute-start(bf16[8,4096]{1,0:T(8,128)(2,1)S(1)} %join.1.refs_0_), channel_id=1, source_target_pairs={{0,4},{4,0},{8,12},{12,8},{1,5},{5,1},{9,13},{13,9},{2,6},{6,2},{1... | collective-permute-start | bytes 196616 | tf_op jit(solution)/shard_map/ppermute | solution.py:34
  38.5 1.2 %collective-permute-start.12 = (bf16[8,4096]{1,0:T(8,128)(2,1)S(1)}, bf16[8,4096]{1,0:T(8,128)(2,1)S(1)}, u32[]{:S(2)}, u32[]{:S(2)}) collective-permute-start(bf16[8,4096]{1,0:T(8,128)(2,1)S(1)} %join.1.refs_0_), channel_id=1, source_target_pairs={{0,8},{4,12},{8,0},{12,4},{1,9},{5,13},{9,1},{13,5},{2,10},{6,14},... | collective-permute-start | bytes 196616 | tf_op jit(solution)/shard_map/ppermute | solution.py:34
  39.7 1.9 %collective-permute-start.13 = (bf16[8,4096]{1,0:T(8,128)(2,1)S(1)}, bf16[8,4096]{1,0:T(8,128)(2,1)S(1)}, u32[]{:S(2)}, u32[]{:S(2)}) collective-permute-start(bf16[8,4096]{1,0:T(8,128)(2,1)S(1)} %join.1.refs_0_), channel_id=1, source_target_pairs={{0,12},{4,8},{8,4},{12,0},{1,13},{5,9},{9,5},{13,1},{2,14},{6,10},... | collective-permute-start | bytes 196616 | tf_op jit(solution)/shard_map/ppermute | solution.py:34
  41.6 1.4 %place.3.refs_0_ = bf16[1,16,256,512]{3,2,1,0:T(8,128)(2,1)} custom-call(bf16[4,256,512]{2,1,0:T(8,128)(2,1)S(1)} %get-tuple-element.19.refs_3_.refs_0_, bf16[4,256,512]{2,1,0:T(8,128)(2,1)S(1)} %collective-permute-done.10.refs_1_, bf16[1,256,512]{2,1,0:T(8,128)(2,1)S(1)} %collective-permute-done.2.refs_2_), custom_call_target="tpu_custom_call" | custom-call | bytes 4718592 | tf_op jit(solution)/shard_map/place/pallas_call | solution.py:197
  43.0 3.3 %collective-permute-done.12.refs_2_ = bf16[8,4096]{1,0:T(8,128)(2,1)S(1)} collective-permute-done((bf16[8,4096]{1,0:T(8,128)(2,1)S(1)}, bf16[8,4096]{1,0:T(8,128)(2,1)S(1)}, u32[]{:S(2)}, u32[]{:S(2)}) %collective-permute-start.12) | collective-permute-done | bytes 65568 | tf_op jit(solution)/shard_map/ppermute | solution.py:34
  46.3 3.6 %project.1.refs_1_ = bf16[8,4,2048]{2,1,0:T(4,128)(2,1)} custom-call(bf16[8,4096]{1,0:T(8,128)(2,1)S(1)} %join.1.refs_0_, bf16[8,4096]{1,0:T(8,128)(2,1)S(1)} %collective-permute-done.11.refs_1_, bf16[8,4096]{1,0:T(8,128)(2,1)S(1)} %collective-permute-done.12.refs_2_, bf16[8,4096]{1,0:T(8,128)(2,1)S(1)} %collective-permute-done.13.refs_3_, ...), custom_call_target="tpu_custom_call" | custom-call | flops 536870912 | bytes 16777216 | tf_op jit(solution)/shard_map/project/pallas_call | solution.py:435
  50.0 0.9 %place.4.refs_0_ = bf16[1,16,256,512]{3,2,1,0:T(8,128)(2,1)} custom-call(bf16[1,16,256,512]{3,2,1,0:T(8,128)(2,1)} %place.3.refs_0_, bf16[8,4,2048]{2,1,0:T(4,128)(2,1)} %project.1.refs_1_, bf16[3,256,512]{2,1,0:T(8,128)(2,1)S(1)} %collective-permute-done.14.refs_2_), custom_call_target="tpu_custom_call", output_to_operand_aliasing={{}: (0, {})} | custom-call | bytes 1572864 | tf_op jit(solution)/shard_map/place/pallas_call | solution.py:197
  50.8 0.6 %collective-permute-done.15.refs_2_ = bf16[4,256,512]{2,1,0:T(8,128)(2,1)S(1)} collective-permute-done((bf16[4,256,512]{2,1,0:T(8,128)(2,1)S(1)}, bf16[4,256,512]{2,1,0:T(8,128)(2,1)S(1)}, u32[]{:S(2)}, u32[]{:S(2)}) %collective-permute-start.15) | collective-permute-done | bytes 1048608 | tf_op jit(solution)/shard_map/ppermute | solution.py:34
  51.5 1.0 %place.5 = bf16[1,16,256,512]{3,2,1,0:T(8,128)(2,1)} custom-call(bf16[1,16,256,512]{3,2,1,0:T(8,128)(2,1)} %place.4.refs_0_, bf16[8,4,2048]{2,1,0:T(4,128)(2,1)} %project.1.refs_1_, bf16[4,256,512]{2,1,0:T(8,128)(2,1)S(1)} %collective-permute-done.15.refs_2_), custom_call_target="tpu_custom_call", output_to_operand_aliasing={{}: (0, {})} | custom-call | bytes 2097152 | tf_op jit(solution)/shard_map/place/pallas_call | solution.py:197
  (15 shorter events, 0.0 us)
Async XLA Ops:
  2.4 10.0 %collective-permute-start.2 = (bf16[1,256,512]{2,1,0:T(8,128)(2,1)S(1)}, bf16[1,256,512]{2,1,0:T(8,128)(2,1)S(1)}, u32[]{:S(2)}, u32[]{:S(2)}) collective-permute-start(bf16[1,256,512]{2,1,0:T(8,128)(2,1)S(1)} %pack.2.refs_0_), channel_id=1, source_target_pairs={{0,2},{1,3},{2,0},{3,1},{4,6},{5,7},{6,4},{7,5},{8,10},{9,11},{10,... | collective-permute-start | bytes 786440 | tf_op jit(solution)/shard_map/ppermute | solution.py:34
  7.9 9.0 %collective-permute-start.3 = (bf16[2,4,4096]{2,1,0:T(4,128)(2,1)S(1)}, bf16[2,4,4096]{2,1,0:T(4,128)(2,1)S(1)}, u32[]{:S(2)}, u32[]{:S(2)}) collective-permute-start(bf16[2,4,4096]{2,1,0:T(4,128)(2,1)S(1)} %get-tuple-element.18), channel_id=1, source_target_pairs={{0,1},{1,0},{2,3},{3,2},{4,5},{5,4},{6,7},{7,6},{8,9},{9,8},{10,11... | collective-permute-start | bytes 196616 | tf_op jit(solution)/shard_map/ppermute | solution.py:34
  7.9 4.3 %collective-permute-start = (bf16[2,4,1024]{2,1,0:T(4,128)(2,1)S(1)}, bf16[2,4,1024]{2,1,0:T(4,128)(2,1)S(1)}, u32[]{:S(2)}, u32[]{:S(2)}) collective-permute-start(bf16[2,4,1024]{2,1,0:T(4,128)(2,1)S(1)} %get-tuple-element.16), channel_id=1, source_target_pairs={{0,2},{1,3},{2,0},{3,1},{4,6},{5,7},{6,4},{7,5},{8,10},{9,11},{10,... | collective-permute-start | bytes 49160 | tf_op jit(solution)/shard_map/ppermute | solution.py:34
  8.0 4.5 %collective-permute-start.1 = (bf16[2,4,1024]{2,1,0:T(4,128)(2,1)S(1)}, bf16[2,4,1024]{2,1,0:T(4,128)(2,1)S(1)}, u32[]{:S(2)}, u32[]{:S(2)}) collective-permute-start(bf16[2,4,1024]{2,1,0:T(4,128)(2,1)S(1)} %get-tuple-element.17), channel_id=1, source_target_pairs={{0,3},{1,2},{2,1},{3,0},{4,7},{5,6},{6,5},{7,4},{8,11},{9,10},{10,... | collective-permute-start | bytes 49160 | tf_op jit(solution)/shard_map/ppermute | solution.py:34
  9.8 40.2 %collective-permute-start.14 = (bf16[3,256,512]{2,1,0:T(8,128)(2,1)S(1)}, bf16[3,256,512]{2,1,0:T(8,128)(2,1)S(1)}, u32[]{:S(2)}, u32[]{:S(2)}) collective-permute-start(bf16[3,256,512]{2,1,0:T(8,128)(2,1)S(1)} %get-tuple-element.14.refs_1_), channel_id=1, source_target_pairs={{0,2},{1,3},{2,0},{3,1},{4,6},{5,7},{6,4},{7,5},{8,10},{9,11},{10,... | collective-permute-start | bytes 2359304 | tf_op jit(solution)/shard_map/ppermute | solution.py:34
  12.3 39.2 %collective-permute-start.15 = (bf16[4,256,512]{2,1,0:T(8,128)(2,1)S(1)}, bf16[4,256,512]{2,1,0:T(8,128)(2,1)S(1)}, u32[]{:S(2)}, u32[]{:S(2)}) collective-permute-start(bf16[4,256,512]{2,1,0:T(8,128)(2,1)S(1)} %get-tuple-element.15.refs_2_), channel_id=1, source_target_pairs={{0,3},{1,2},{2,1},{3,0},{4,7},{5,6},{6,5},{7,4},{8,11},{9,10},{10,... | collective-permute-start | bytes 3145736 | tf_op jit(solution)/shard_map/ppermute | solution.py:34
  12.5 10.0 %copy-start = (s32[32,1]{0,1:T(1,128)S(1)}, s32[32,1]{0,1:T(1,128)}, u32[]{:S(2)}) copy-start(s32[32,1]{0,1:T(1,128)} %param.7) | copy-start | bytes 388
  12.5 10.0 %copy-start.1 = (s32[32]{0:T(128)S(1)}, s32[32]{0:T(128)}, u32[]{:S(2)}) copy-start(s32[32]{0:T(128)} %lengths_ref.1) | copy-start | bytes 388
  12.5 6.8 %collective-permute-start.4 = (bf16[2,2,4,1024]{3,2,1,0:T(4,128)(2,1)S(1)}, bf16[2,2,4,1024]{3,2,1,0:T(4,128)(2,1)S(1)}, u32[]{:S(2)}, u32[]{:S(2)}) collective-permute-start(bf16[2,2,4,1024]{3,2,1,0:T(4,128)(2,1)S(1)} %merge.1.refs_0_.refs_7_), channel_id=1, source_target_pairs={{0,4},{4,0},{8,12},{12,8},{1,5},{5,1},{9,13},{13,9},{2,6},{6,2},{1... | collective-permute-start | bytes 98312 | tf_op jit(solution)/shard_map/ppermute | solution.py:34
  14.2 6.7 %collective-permute-start.5 = (bf16[2,2,4,1024]{3,2,1,0:T(4,128)(2,1)S(1)}, bf16[2,2,4,1024]{3,2,1,0:T(4,128)(2,1)S(1)}, u32[]{:S(2)}, u32[]{:S(2)}) collective-permute-start(bf16[2,2,4,1024]{3,2,1,0:T(4,128)(2,1)S(1)} %merge.1.refs_0_.refs_7_), channel_id=1, source_target_pairs={{0,8},{4,12},{8,0},{12,4},{1,9},{5,13},{9,1},{13,5},{2,10},{6,14},... | collective-permute-start | bytes 98312 | tf_op jit(solution)/shard_map/ppermute | solution.py:34
  16.8 5.7 %collective-permute-start.6 = (bf16[2,2,4,1024]{3,2,1,0:T(4,128)(2,1)S(1)}, bf16[2,2,4,1024]{3,2,1,0:T(4,128)(2,1)S(1)}, u32[]{:S(2)}, u32[]{:S(2)}) collective-permute-start(bf16[2,2,4,1024]{3,2,1,0:T(4,128)(2,1)S(1)} %merge.1.refs_0_.refs_7_), channel_id=1, source_target_pairs={{0,12},{4,8},{8,4},{12,0},{1,13},{5,9},{9,5},{13,1},{2,14},{6,10},... | collective-permute-start | bytes 98312 | tf_op jit(solution)/shard_map/ppermute | solution.py:34
  19.3 9.5 %collective-permute-start.10 = (bf16[4,256,512]{2,1,0:T(8,128)(2,1)S(1)}, bf16[4,256,512]{2,1,0:T(8,128)(2,1)S(1)}, u32[]{:S(2)}, u32[]{:S(2)}) collective-permute-start(bf16[4,256,512]{2,1,0:T(8,128)(2,1)S(1)} %get-tuple-element.20.refs_4_), channel_id=1, source_target_pairs={{0,1},{1,0},{2,3},{3,2},{4,5},{5,4},{6,7},{7,6},{8,9},{9,8},{10,11... | collective-permute-start | bytes 3145736 | tf_op jit(solution)/shard_map/ppermute | solution.py:34
  26.3 10.4 %collective-permute-start.7 = (bf16[10,32,128]{2,1,0:T(8,128)(2,1)S(1)}, bf16[10,32,128]{2,1,0:T(8,128)(2,1)S(1)}, u32[]{:S(2)}, u32[]{:S(2)}) collective-permute-start(bf16[10,32,128]{2,1,0:T(8,128)(2,1)S(1)} %get-tuple-element.23), channel_id=1, source_target_pairs={{0,4},{4,0},{8,12},{12,8},{1,5},{5,1},{9,13},{13,9},{2,6},{6,2},{1... | collective-permute-start | bytes 245768 | tf_op jit(solution)/shard_map/ppermute | solution.py:34
  26.4 10.3 %collective-permute-start.8 = (bf16[10,32,128]{2,1,0:T(8,128)(2,1)S(1)}, bf16[10,32,128]{2,1,0:T(8,128)(2,1)S(1)}, u32[]{:S(2)}, u32[]{:S(2)}) collective-permute-start(bf16[10,32,128]{2,1,0:T(8,128)(2,1)S(1)} %get-tuple-element.24), channel_id=1, source_target_pairs={{0,8},{4,12},{8,0},{12,4},{1,9},{5,13},{9,1},{13,5},{2,10},{6,14},... | collective-permute-start | bytes 245768 | tf_op jit(solution)/shard_map/ppermute | solution.py:34
  28.9 7.9 %collective-permute-start.9 = (bf16[10,32,128]{2,1,0:T(8,128)(2,1)S(1)}, bf16[10,32,128]{2,1,0:T(8,128)(2,1)S(1)}, u32[]{:S(2)}, u32[]{:S(2)}) collective-permute-start(bf16[10,32,128]{2,1,0:T(8,128)(2,1)S(1)} %get-tuple-element.25), channel_id=1, source_target_pairs={{0,12},{4,8},{8,4},{12,0},{1,13},{5,9},{9,5},{13,1},{2,14},{6,10},... | collective-permute-start | bytes 245768 | tf_op jit(solution)/shard_map/ppermute | solution.py:34
  37.1 5.9 %collective-permute-start.11 = (bf16[8,4096]{1,0:T(8,128)(2,1)S(1)}, bf16[8,4096]{1,0:T(8,128)(2,1)S(1)}, u32[]{:S(2)}, u32[]{:S(2)}) collective-permute-start(bf16[8,4096]{1,0:T(8,128)(2,1)S(1)} %join.1.refs_0_), channel_id=1, source_target_pairs={{0,4},{4,0},{8,12},{12,8},{1,5},{5,1},{9,13},{13,9},{2,6},{6,2},{1... | collective-permute-start | bytes 196616 | tf_op jit(solution)/shard_map/ppermute | solution.py:34
  38.5 7.8 %collective-permute-start.12 = (bf16[8,4096]{1,0:T(8,128)(2,1)S(1)}, bf16[8,4096]{1,0:T(8,128)(2,1)S(1)}, u32[]{:S(2)}, u32[]{:S(2)}) collective-permute-start(bf16[8,4096]{1,0:T(8,128)(2,1)S(1)} %join.1.refs_0_), channel_id=1, source_target_pairs={{0,8},{4,12},{8,0},{12,4},{1,9},{5,13},{9,1},{13,5},{2,10},{6,14},... | collective-permute-start | bytes 196616 | tf_op jit(solution)/shard_map/ppermute | solution.py:34
  39.7 6.6 %collective-permute-start.13 = (bf16[8,4096]{1,0:T(8,128)(2,1)S(1)}, bf16[8,4096]{1,0:T(8,128)(2,1)S(1)}, u32[]{:S(2)}, u32[]{:S(2)}) collective-permute-start(bf16[8,4096]{1,0:T(8,128)(2,1)S(1)} %join.1.refs_0_), channel_id=1, source_target_pairs={{0,12},{4,8},{8,4},{12,0},{1,13},{5,9},{9,5},{13,1},{2,14},{6,10},... | collective-permute-start | bytes 196616 | tf_op jit(solution)/shard_map/ppermute | solution.py:34

commit v10 on v9

--- a/solution.py
+++ b/solution.py
@@ -12,6 +12,7 @@
 REQ_GRP = 8
 CAP = 2
 HIDDEN = -1e30
+STAT_ROWS = 16
 
 ANY = pl.BlockSpec(memory_space=pl.ANY)
 HBM = pl.BlockSpec(memory_space=pltpu.HBM)
@@ -38,14 +39,17 @@
     return [swap(value, axis, offset) for offset in range(lax.axis_size(axis))]
 
 
-def own_slots(routing_ref, section, used, source):
-    for t in range(used.shape[0]):
-        used[t] = 0
-    for i in range(REQ_GRP):
-        target = routing_ref[section * REQ_GRP + i]
-        order = used[target]
-        used[target] = order + 1
-        source[target * CAP + order] = i
+def own_targets(routing_ref, section):
+    return [routing_ref[section * REQ_GRP + i] for i in range(REQ_GRP)]
+
+
+def slot_row(targets, group, order):
+    row, before = jnp.int32(0), jnp.int32(0)
+    for i, target in enumerate(targets):
+        here = target == group
+        row = jnp.where(here & (before == order), i, row)
+        before = before + here.astype(jnp.int32)
+    return row, before > order
 
 
 def halves_of(pieces):
@@ -56,46 +60,46 @@
     ]
 
 
-def start_packing(pieces, section_count, routing_ref, cache_ref, out_refs, source, used, sem):
+def start_packing(pieces, section_count, routing_ref, cache_ref, out_refs, sem):
     section = lax.axis_index("sec")
     full = section_count * CAP == REQ_GRP
-    own_slots(routing_ref, section, used, source)
+    targets = own_targets(routing_ref, section)
     halves = halves_of(pieces)
-
-    def copy(n, place, offset, half, row):
+    slots = {(offset, half // 2) for _, _, offset, half in halves}
+    rows = {slot: slot_row(targets, section ^ slot[0], slot[1]) for slot in sorted(slots)}
+
+    def copy(n, place, offset, half):
+        row, _ = rows[offset, half // 2]
         return pltpu.make_async_copy(
             cache_ref.at[row, half % 2], out_refs[n].at[place], sem.at[offset * 2 * CAP + half]
         )
 
     for n, place, offset, half in halves:
-        target, order = section ^ offset, half // 2
         if full:
-            copy(n, place, offset, half, source[target * CAP + order]).start()
+            copy(n, place, offset, half).start()
         else:
-
-            @pl.when(order < used[target])
+            _, filled = rows[offset, half // 2]
+
+            @pl.when(filled)
             def _():
-                copy(n, place, offset, half, source[target * CAP + order]).start()
-
-            @pl.when(order >= used[target])
+                copy(n, place, offset, half).start()
+
+            @pl.when(jnp.logical_not(filled))
             def _():
                 out_refs[n][place] = jnp.zeros_like(out_refs[n][place])
 
     def finish():
         for n, place, offset, half in halves:
             if full:
-                copy(n, place, offset, half, 0).wait()
+                copy(n, place, offset, half).wait()
             else:
-
-                @pl.when(half // 2 < used[section ^ offset])
-                def _():
-                    copy(n, place, offset, half, 0).wait()
+                pl.when(rows[offset, half // 2][1])(copy(n, place, offset, half).wait)
 
     return finish
 
 
 def first_pack_kernel(pieces, section_count, routing_ref, cache_ref, query_ref, *refs):
-    refs, (source, used, sem, query_sem) = refs[:-4], refs[-4:]
+    refs, (sem, query_sem) = refs[:-2], refs[-2:]
     query_out, cache_out = refs[-section_count:], refs[-section_count - len(pieces) : -section_count]
     section = lax.axis_index("sec")
     query_copies = []
@@ -105,15 +109,15 @@
         part = query_ref.at[0, pl.ds((section ^ offset) * CAP, CAP), :, columns]
         query_copies.append(pltpu.make_async_copy(part, out_ref, query_sem.at[offset]))
         query_copies[-1].start()
-    finish = start_packing(pieces, section_count, routing_ref, cache_ref, cache_out, source, used, sem)
+    finish = start_packing(pieces, section_count, routing_ref, cache_ref, cache_out, sem)
     finish()
     for copy in query_copies:
         copy.wait()
 
 
 def pack_kernel(pieces, section_count, routing_ref, cache_ref, *refs):
-    cache_out, (source, used, sem) = refs[-3 - len(pieces) : -3], refs[-3:]
-    start_packing(pieces, section_count, routing_ref, cache_ref, cache_out, source, used, sem)()
+    cache_out, sem = refs[-1 - len(pieces) : -1], refs[-1]
+    start_packing(pieces, section_count, routing_ref, cache_ref, cache_out, sem)()
 
 
 def merge_kernel(count, *refs):
@@ -149,8 +153,6 @@
         in_specs=[SMEM, HBM, HBM] + [ANY] * len(others),
         out_specs=[VMEM] * len(shapes),
         scratch_shapes=[
-            pltpu.SMEM((section_count * CAP,), jnp.int32),
-            pltpu.SMEM((section_count,), jnp.int32),
             pltpu.SemaphoreType.DMA((section_count * CAP * 2,)),
             pltpu.SemaphoreType.DMA((section_count,)),
         ],
@@ -169,8 +171,6 @@
         in_specs=[SMEM, HBM] + [ANY] * len(others),
         out_specs=[VMEM] * len(shapes),
         scratch_shapes=[
-            pltpu.SMEM((section_count * CAP,), jnp.int32),
-            pltpu.SMEM((section_count,), jnp.int32),
             pltpu.SemaphoreType.DMA((section_count * CAP * 2,)),
         ],
         compiler_params=limit(16),
@@ -185,9 +185,10 @@
     section = lax.axis_index("sec")
     copies = []
     for n, (offset, first, size) in enumerate(pieces):
-        halves = out_ref.at[0, pl.ds((section ^ offset) * 2 * CAP + first, size)]
-        copies.append(pltpu.make_async_copy(part_refs[n], halves, sem.at[n]))
-        copies[-1].start()
+        for place in range(size):
+            half = out_ref.at[0, (section ^ offset) * 2 * CAP + first + place]
+            copies.append(pltpu.make_async_copy(part_refs[n].at[place], half, sem.at[len(copies)]))
+            copies[-1].start()
     for copy in copies:
         copy.wait()
 
@@ -199,7 +200,7 @@
         out_shape=jax.ShapeDtypeStruct((1, 2 * slot_count) + part.shape[1:], part.dtype),
         in_specs=[HBM] * len(given) + [VMEM] * len(parts),
         out_specs=HBM,
-        scratch_shapes=[pltpu.SemaphoreType.DMA((len(parts),))],
+        scratch_shapes=[pltpu.SemaphoreType.DMA((sum(len(part) for part in parts),))],
         input_output_aliases={0: 0} if given else {},
         compiler_params=limit(8),
         cost_estimate=cost(0, 4 * sum(piece.size for piece in parts)),
@@ -211,7 +212,7 @@
     cache_refs, refs = refs[: len(pieces)], refs[len(pieces) :]
     query_refs, far_refs = refs[:2], refs[2 : 2 + tp_count]
     message_refs = refs[2 + tp_count : 2 + 2 * tp_count]
-    source, used, messages, stats, stacked, far_queries = refs[2 + 2 * tp_count :]
+    messages, stats, stacked, far_queries = refs[2 + 2 * tp_count :]
     section = lax.axis_index("sec")
     tp_index = lax.axis_index("tp")
     local = cache_refs[0].shape[1]
@@ -219,7 +220,7 @@
     span = KEY_VALUE_HEADS * rows
     prompts = max(1, groups // KEY_VALUE_HEADS)
     full = section_count * CAP == REQ_GRP
-    own_slots(routing_ref, section, used, source)
+    targets = own_targets(routing_ref, section)
     samples = query_refs[0].shape[1]
     for offset, far_ref in enumerate(far_refs):
         far_queries[tp_index ^ offset] = far_ref[...]
@@ -230,7 +231,7 @@
 
     def prompt(offset, order):
         keys_ref, values_ref = held[offset, 2 * order], held[offset, 2 * order + 1]
-        row = source[(section ^ offset) * CAP + order]
+        row, _ = slot_row(targets, section ^ offset, order)
         visible = position < lengths_ref[section * REQ_GRP + row]
         slot = offset * CAP + order
         for head in range(span // samples):
@@ -252,7 +253,7 @@
         total = jnp.sum(weight, axis=0, keepdims=True)
         some = total > 0.0
         safe = jnp.where(some, total, 1.0)
-        stats[pl.ds(row, 1)] = jnp.where(some, peak + jnp.log(safe), HIDDEN)
+        stats[0, pl.ds(row, 1)] = jnp.where(some, peak + jnp.log(safe), HIDDEN)
         weight = (weight * (1.0 / safe)).T.astype(jnp.bfloat16)
         for k in range(KEY_VALUE_HEADS):
             mixed = jnp.dot(
@@ -269,33 +270,21 @@
             if full:
                 one()
             else:
-                pl.when(half // 2 < used[section ^ offset])(one)
-
-    level = stats[...]
+                pl.when(slot_row(targets, section ^ offset, half // 2)[1])(one)
+
+    level = stats[0]
     high = level.astype(jnp.bfloat16).astype(jnp.float32)
     rest = level - high
     middle = rest.astype(jnp.bfloat16).astype(jnp.float32)
-    stats[...] = high
-    stats_middle, stats_low = middle, rest - middle
-    for offset in range(tp_count):
+    stats[0], stats[1], stats[2] = high, middle, rest - middle
+    for offset, message_ref in enumerate(message_refs):
         device = tp_index ^ offset
-        message_refs[offset][0:groups] = messages[device]
-        message_refs[offset][groups] = jnp.zeros((rows, HEAD_SIZE), jnp.bfloat16)
-    for part, values in enumerate((high, stats_middle, stats_low)):
-        stats[...] = values
-        for offset in range(tp_count):
-            first = (tp_index ^ offset) * groups // KEY_VALUE_HEADS
-            block = jnp.concatenate(
-                [stats[pl.ds(first + n, 1)] for n in range(prompts)]
-                + [jnp.zeros((16 - prompts, span), jnp.float32)],
-                axis=0,
-            )
-            if part < 2:
-                message_refs[offset][groups, part * 16 : part * 16 + 16] = block.astype(jnp.bfloat16)
-            else:
-                message_refs[offset][groups + 1] = jnp.concatenate([block, jnp.zeros_like(block)], axis=0).astype(
-                    jnp.bfloat16
-                )
+        for inner in range(groups):
+            message_ref[inner * rows : (inner + 1) * rows] = messages[device, inner]
+        first = device * groups // KEY_VALUE_HEADS
+        lines = [stats[part, pl.ds(first + n, 1)] for part in range(3) for n in range(prompts)]
+        lines.append(jnp.zeros((STAT_ROWS - 3 * prompts, span), jnp.float32))
+        message_ref[groups * rows :] = jnp.concatenate(lines, axis=0).astype(jnp.bfloat16)
 
 
 def attend(routing, lengths, caches, pieces, queries, far_queries):
@@ -308,14 +297,12 @@
     multiplies = REQ_GRP * span * HEAD_SIZE * caches[0].shape[1]
     return pl.pallas_call(
         functools.partial(attend_kernel, pieces, section_count, tp_count),
-        out_shape=[jax.ShapeDtypeStruct((groups + 2, rows, HEAD_SIZE), jnp.bfloat16)] * tp_count,
+        out_shape=[jax.ShapeDtypeStruct((groups * rows + STAT_ROWS, HEAD_SIZE), jnp.bfloat16)] * tp_count,
         in_specs=[SMEM, SMEM] + [VMEM] * (len(caches) + len(queries) + tp_count),
         out_specs=[VMEM] * tp_count,
         scratch_shapes=[
-            pltpu.SMEM((section_count * CAP,), jnp.int32),
-            pltpu.SMEM((section_count,), jnp.int32),
             pltpu.VMEM((tp_count, groups, rows, HEAD_SIZE), jnp.bfloat16),
-            pltpu.VMEM((REQ_GRP, span), jnp.float32),
+            pltpu.VMEM((3, REQ_GRP, span), jnp.float32),
             pltpu.VMEM((section_count * CAP, span, HEAD_SIZE), jnp.float32),
             pltpu.VMEM((tp_count,) + far_queries[0].shape, far_queries[0].dtype),
         ],
@@ -325,17 +312,16 @@
     )(routing, lengths, *caches, *queries, *far_queries)
 
 
-def join_kernel(count, samples, *refs):
+def join_kernel(count, samples, rows, *refs):
     message_refs, (out_ref, scaling, flat) = refs[:count], refs[-3:]
-    groups, rows, _ = message_refs[0].shape
-    groups -= 2
+    groups = (message_refs[0].shape[0] - STAT_ROWS) // rows
+    prompts = max(1, groups // KEY_VALUE_HEADS)
     heads = rows // samples
     tp_index = lax.axis_index("tp")
     levels = []
     for ref in message_refs:
-        upper = ref[groups].astype(jnp.float32)
-        lower = ref[groups + 1].astype(jnp.float32)
-        levels.append(upper[0:8] + upper[16:24] + lower[0:8])
+        lines = ref[groups * rows :].astype(jnp.float32)[0:8]
+        levels.append(lines + pltpu.roll(lines, 8 - prompts, 0) + pltpu.roll(lines, 8 - 2 * prompts, 0))
     summit = functools.reduce(jnp.maximum, levels)
     scales = [jnp.exp(level - summit) for level in levels]
     total = functools.reduce(jnp.add, scales)
@@ -349,7 +335,7 @@
             part = pl.ds(inner % KEY_VALUE_HEADS * rows, rows)
         prompt = inner // KEY_VALUE_HEADS
         terms = [
-            ref[inner].astype(jnp.float32) * scaling[n, part, prompt : prompt + 1]
+            ref[inner * rows : (inner + 1) * rows].astype(jnp.float32) * scaling[n, part, prompt : prompt + 1]
             for n, ref in enumerate(message_refs)
         ]
         joined = functools.reduce(jnp.add, terms)
@@ -364,9 +350,9 @@
     out_ref[...] = flat[...].astype(jnp.bfloat16)
 
 
-def join(messages, others, samples):
-    groups, rows, _ = messages[0].shape
-    groups -= 2
+def join(messages, others, samples, heads):
+    rows = heads * samples
+    groups = (messages[0].shape[0] - STAT_ROWS) // rows
     width = rows // samples * HEAD_SIZE
     if groups % KEY_VALUE_HEADS == 0:
         shape = (groups // KEY_VALUE_HEADS * samples, KEY_VALUE_HEADS * width)
@@ -374,7 +360,7 @@
         shape = (groups, samples, width)
     count = len(messages)
     return pl.pallas_call(
-        functools.partial(join_kernel, count, samples),
+        functools.partial(join_kernel, count, samples, rows),
         out_shape=jax.ShapeDtypeStruct(shape, jnp.bfloat16),
         in_specs=[VMEM] * count + [ANY] * len(others),
         out_specs=VMEM,
@@ -388,39 +374,51 @@
     )(*messages, *others)
 
 
-def fetch_kernel(weight_ref, *refs):
+def fetch_kernel(first, weight_ref, *refs):
     out_ref, sem = refs[-2:]
     copies = []
-    step = weight_ref.shape[0] // sem.shape[0]
+    step = out_ref.shape[0] // sem.shape[0]
     for n in range(sem.shape[0]):
-        part = pl.ds(n * step, step)
-        copies.append(pltpu.make_async_copy(weight_ref.at[part], out_ref.at[part], sem.at[n]))
+        rows = weight_ref.at[pl.ds(first + n * step, step)]
+        copies.append(pltpu.make_async_copy(rows, out_ref.at[pl.ds(n * step, step)], sem.at[n]))
         copies[-1].start()
     for copy in copies:
         copy.wait()
 
 
-def fetch(weight, others):
-    return pl.pallas_call(
-        fetch_kernel,
-        out_shape=jax.ShapeDtypeStruct(weight.shape, weight.dtype),
+def fetch(weight, others, number, count):
+    size = weight.shape[0] // count
+    return pl.pallas_call(
+        functools.partial(fetch_kernel, number * size),
+        out_shape=jax.ShapeDtypeStruct((size,) + weight.shape[1:], weight.dtype),
         in_specs=[HBM] + [ANY] * len(others),
         out_specs=VMEM,
         scratch_shapes=[pltpu.SemaphoreType.DMA((8,))],
-        compiler_params=limit(36),
-        cost_estimate=cost(0, 4 * weight.size),
+        compiler_params=limit(24),
+        cost_estimate=cost(0, 4 * weight.size // count),
         name="fetch",
     )(in_hbm(weight), *others)
 
 
 def project_kernel(count, tile, *refs):
-    part_refs, weight_ref, out_ref = refs[:count], refs[count], refs[count + 1]
+    part_refs, weight_refs, out_ref = refs[:count], refs[count:-1], refs[-1]
     tp_index = lax.axis_index("tp")
     prompts, samples, width = out_ref.shape
     share = prompts // count
     left = jnp.concatenate([ref[...].astype(jnp.float32) for ref in part_refs], axis=0).astype(jnp.bfloat16)
+    size = weight_refs[0].shape[0]
     for first in range(0, width, tile):
-        result = jnp.dot(left, weight_ref[:, first : first + tile], preferred_element_type=jnp.float32)
+        result = functools.reduce(
+            jnp.add,
+            [
+                jnp.dot(
+                    left[:, n * size : (n + 1) * size],
+                    ref[:, first : first + tile],
+                    preferred_element_type=jnp.float32,
+                )
+                for n, ref in enumerate(weight_refs)
+            ],
+        )
         for offset in range(count):
             for n in range(share):
                 row = (offset * share + n) * samples
@@ -428,19 +426,20 @@
                 out_ref[(tp_index ^ offset) * share + n, :, first : first + tile] = block
 
 
-def project(parts, weight, samples):
+def project(parts, weights, samples):
     count = len(parts)
-    depth, width = weight.shape
+    depth, width = weights[0].shape
+    depth *= len(weights)
     total = count * parts[0].shape[0]
     return pl.pallas_call(
         functools.partial(project_kernel, count, min(256, width)),
         out_shape=jax.ShapeDtypeStruct((total // samples, samples, width), jnp.bfloat16),
-        in_specs=[VMEM] * (count + 1),
+        in_specs=[VMEM] * (count + len(weights)),
         out_specs=VMEM,
         compiler_params=limit(24),
         cost_estimate=cost(2 * total * depth * width, 2 * depth * width),
         name="project",
-    )(*parts, weight)
+    )(*parts, *weights)
 
 
 def body(prompt_key_values, queries, routing, lengths, out_weight):
@@ -452,7 +451,7 @@
     whole = 2 * CAP
     near = [(offset, 0, whole) for offset in range(2)]
     head, tail = [(2, 0, 1)], [(2, 1, whole - 1)]
-    far = tail + [(offset, 0, whole) for offset in range(3, section_count)]
+    far = [(offset, 0, whole) for offset in range(3, section_count)] + tail
 
     def across(parts, pieces):
         return [swap(part, "sec", piece[0]) for part, piece in zip(parts, pieces)]
@@ -472,9 +471,10 @@
 
     messages = attend(routing, lengths, caches, pieces, query_parts[:2], far_queries)
     partials = [swap(part, "tp", offset) for offset, part in enumerate(messages)]
-    held_weight = fetch(out_weight, [messages[0], *near_parts[1:]])
-    share = join(partials, [held_weight], samples)
+    held_weight = [fetch(out_weight, [messages[0], *near_parts[1:]], 0, 2)]
+    share = join(partials, held_weight, samples, query_width // HEAD_SIZE // KEY_VALUE_HEADS)
     shares = spread(share, "tp")
+    held_weight.append(fetch(out_weight, [share], 1, 2))
     if share.ndim == 3:
         attended = jnp.stack(shares)[jnp.arange(tp_count) ^ lax.axis_index("tp")]
         attended = attended.reshape(REQ_GRP, KEY_VALUE_HEADS, samples, -1).transpose(0, 2, 1, 3)

time: 52.7 us -> 53.2 us (level)
  waiting for transfers between devices: 7.86 us -> 6.77 us
  Pallas kernels: 23.6 us -> 24.6 us
    ppermute x16, waiting for transfers between devices: 7.86 us -> 6.77 us  [swap(): return lax.ppermute(value, axis, [(i, i ^ offset) for i in range(count)])]
    pallas_call x2 -> x3, Pallas kernels: 6.31 us -> 7.34 us  [the longest x2 6.94 us: fetch(): pl.pallas_call(functools.partial(fetch_kernel, number * size), out_shape=...]
  transfers between devices with their start and end apart: 16 -> 16, of which waited for: 5 -> 4; matrix products, arithmetic and copies ran while one was open for 0% -> 0% of each run, Pallas kernels for 40% -> 41%
where the time goes in v10:
time: 53.2 us; the launch traced here: 53 us
  Pallas kernels  24.6 us (46%)
  starting transfers between devices  20.8 us (39%)
  waiting for transfers between devices  6.77 us (13%)
  between operations  0.81 us (2%)
    ppermute x16, starting transfers between devices, swap(): return lax.ppermute(value, axis, [(i, i ^ offset) for i in range(count)])  20.8 us
    pallas_call x2, Pallas kernels, fetch(): pl.pallas_call(functools.partial(fetch_kernel, number * size), out_shape=...  6.94 us
    ppermute x16, waiting for transfers between devices, swap(): return lax.ppermute(value, axis, [(i, i ^ offset) for i in range(count)])  6.77 us
    pallas_call x2, Pallas kernels, pack(): pl.pallas_call(functools.partial(pack_kernel, pieces, section_count), out...  4.12 us
    pallas_call x1, Pallas kernels, attend(): pl.pallas_call(functools.partial(attend_kernel, pieces, section_count, tp...  3.76 us
    pallas_call x1, Pallas kernels, project(): pl.pallas_call(functools.partial(project_kernel, count, min(256, width)),...  3.64 us
    pallas_call x3, Pallas kernels, place(): pl.pallas_call(functools.partial(place_kernel, pieces), out_shape=jax.Sha...  3.37 us
    pallas_call x1, Pallas kernels, first_pack(): pl.pallas_call(functools.partial(first_pack_kernel, pieces, section_count...  2.37 us
  transfers between devices with their start and end apart: 16, of which 4 were waited for; matrix products, arithmetic and copies ran while one was open for 0% of the time, Pallas kernels for 41%

profile of v10, /device:TPU:0, one launch (start us, length us, event | category | flops | bytes accessed | tf_op | source)
XLA Modules:
  0.0 53.0 jit_solution(10268031897827238265)
XLA Ops:
  0.6 1.8 %pack.2.refs_0_ = bf16[1,256,512]{2,1,0:T(8,128)(2,1)S(1)} custom-call(s32[32]{0:T(128)} %bitcast.2, bf16[8,2,256,512]{3,2,1,0:T(8,128)(2,1)} %cache_ref.5), custom_call_target="tpu_custom_call" | custom-call | bytes 524288 | tf_op jit(solution)/shard_map/pack/pallas_call | solution.py:168
  2.4 3.0 %collective-permute-start.2 = (bf16[1,256,512]{2,1,0:T(8,128)(2,1)S(1)}, bf16[1,256,512]{2,1,0:T(8,128)(2,1)S(1)}, u32[]{:S(2)}, u32[]{:S(2)}) collective-permute-start(bf16[1,256,512]{2,1,0:T(8,128)(2,1)S(1)} %pack.2.refs_0_), channel_id=1, source_target_pairs={{0,2},{1,3},{2,0},{3,1},{4,6},{5,7},{6,4},{7,5},{8,10},{9,11},{10,... | collective-permute-start | bytes 786440 | tf_op jit(solution)/shard_map/ppermute | solution.py:35
  5.4 2.4 %first_pack.1 = (bf16[4,256,512]{2,1,0:T(8,128)(2,1)S(1)}, bf16[3,256,512]{2,1,0:T(8,128)(2,1)S(1)}, bf16[2,4,4096]{2,1,0:T(4,128)(2,1)S(1)}, bf16[2,4,4096]{2,1...) custom-call(s32[32]{0:T(128)} %bitcast.3, bf16[8,2,256,512]{3,2,1,0:T(8,128)(2,1)} %cache_ref.5, ...), custom_call_target="tpu_custom_call" | custom-call | bytes 3997696 | tf_op jit(solution)/shard_map/first_pack/pallas_call | solution.py:150
  7.8 0.1 collective-permute-start.3
  7.9 0.1 collective-permute-start
  8.0 1.8 %collective-permute-start.1 = (bf16[2,4,1024]{2,1,0:T(4,128)(2,1)S(1)}, bf16[2,4,1024]{2,1,0:T(4,128)(2,1)S(1)}, u32[]{:S(2)}, u32[]{:S(2)}) collective-permute-start(bf16[2,4,1024]{2,1,0:T(4,128)(2,1)S(1)} %get-tuple-element.17), channel_id=1, source_target_pairs={{0,3},{1,2},{2,1},{3,0},{4,7},{5,6},{6,5},{7,4},{8,11},{9,10},{10,... | collective-permute-start | bytes 49160 | tf_op jit(solution)/shard_map/ppermute | solution.py:35
  9.7 0.0 collective-permute-start.14
  9.8 2.5 %collective-permute-done.refs_0_ = bf16[2,4,1024]{2,1,0:T(4,128)(2,1)S(1)} collective-permute-done((bf16[2,4,1024]{2,1,0:T(4,128)(2,1)S(1)}, bf16[2,4,1024]{2,1,0:T(4,128)(2,1)S(1)}, u32[]{:S(2)}, u32[]{:S(2)}) %collective-permute-start) | collective-permute-done | bytes 16416 | tf_op jit(solution)/shard_map/ppermute | solution.py:35
  12.3 2.4 %collective-permute-start.15 = (bf16[3,256,512]{2,1,0:T(8,128)(2,1)S(1)}, bf16[3,256,512]{2,1,0:T(8,128)(2,1)S(1)}, u32[]{:S(2)}, u32[]{:S(2)}) collective-permute-start(bf16[3,256,512]{2,1,0:T(8,128)(2,1)S(1)} %get-tuple-element.15.refs_2_), channel_id=1, source_target_pairs={{0,2},{1,3},{2,0},{3,1},{4,6},{5,7},{6,4},{7,5},{8,10},{9,11},{10,... | collective-permute-start | bytes 2359304 | tf_op jit(solution)/shard_map/ppermute | solution.py:35
  14.6 0.0 copy-start
  14.7 1.6 %collective-permute-start.4 = (bf16[2,2,4,1024]{3,2,1,0:T(4,128)(2,1)S(1)}, bf16[2,2,4,1024]{3,2,1,0:T(4,128)(2,1)S(1)}, u32[]{:S(2)}, u32[]{:S(2)}) collective-permute-start(bf16[2,2,4,1024]{3,2,1,0:T(4,128)(2,1)S(1)} %merge.1.refs_0_.refs_7_), channel_id=1, source_target_pairs={{0,4},{4,0},{8,12},{12,8},{1,5},{5,1},{9,13},{13,9},{2,6},{6,2},{1... | collective-permute-start | bytes 98312 | tf_op jit(solution)/shard_map/ppermute | solution.py:35
  16.3 2.6 %collective-permute-start.5 = (bf16[2,2,4,1024]{3,2,1,0:T(4,128)(2,1)S(1)}, bf16[2,2,4,1024]{3,2,1,0:T(4,128)(2,1)S(1)}, u32[]{:S(2)}, u32[]{:S(2)}) collective-permute-start(bf16[2,2,4,1024]{3,2,1,0:T(4,128)(2,1)S(1)} %merge.1.refs_0_.refs_7_), channel_id=1, source_target_pairs={{0,8},{4,12},{8,0},{12,4},{1,9},{5,13},{9,1},{13,5},{2,10},{6,14},... | collective-permute-start | bytes 98312 | tf_op jit(solution)/shard_map/ppermute | solution.py:35
  18.9 0.2 collective-permute-start.6
  19.1 2.3 %pack.3 = (bf16[4,256,512]{2,1,0:T(8,128)(2,1)S(1)}, bf16[4,256,512]{2,1,0:T(8,128)(2,1)S(1)}) custom-call(s32[32]{0:T(128)} %bitcast.4, bf16[8,2,256,512]{3,2,1,0:T(8,128)(2,1)} %cache_ref.5, bf16[2,2,4,1024]{3,2,1,0:T(4,128)(2,1)S(1)} %merge.1.refs_0_.refs_7_, bf16[2,4,4096]{2,1,0:T(4,128)(2,1)S(1)} %collective-permute-done.3.refs_1_.refs_6_), custom_call_target="tpu_custom_call" | custom-call | flops 10000000000 | bytes 4194304 | tf_op jit(solution)/shard_map/pack/pallas_call | solution.py:168
  21.5 0.1 collective-permute-start.10
  21.6 0.2 collective-permute-done.5.refs_9_
  21.7 2.9 %collective-permute-done.6.refs_10_ = bf16[2,2,4,1024]{3,2,1,0:T(4,128)(2,1)S(1)} collective-permute-done((bf16[2,2,4,1024]{3,2,1,0:T(4,128)(2,1)S(1)}, bf16[2,2,4,1024]{3,2,1,0:T(4,128)(2,1)S(1)}, u32[]{:S(2)}, u32[]{:S(2)}) %collective-permute-start.6) | collective-permute-done | bytes 32800 | tf_op jit(solution)/shard_map/ppermute | solution.py:35
  24.6 3.8 %attend.1 = (bf16[272,128]{1,0:T(8,128)(2,1)S(1)}, bf16[272,128]{1,0:T(8,128)(2,1)S(1)}, bf16[272,128]{1,0:T(8,128)(2,1)S(1)}, bf16[272,128]{1,0:T(8,128)(2,1)S(1)}) custom-call(s32[32]{0:T(128)S(1)} %bitcast.5, s32[32]{0:T(128)S(1)} %copy-done.1, bf16[1,256,512]{2,1,0:T(8,128)(2,1)S(1)} %pack.2.refs_0_, bf16[4,256,512]{2,1,0:T(8,128)(2,1)S(1)} %get-tuple-element.14.refs_1_, ...), custom_call_target="tpu_custom_call" | custom-call | flops 20000000000 | bytes 4194304 | tf_op jit(solution)/shard_map/attend/pallas_call | solution.py:298
  28.4 0.1 collective-permute-start.7
  28.5 1.2 %collective-permute-start.8 = (bf16[272,128]{1,0:T(8,128)(2,1)S(1)}, bf16[272,128]{1,0:T(8,128)(2,1)S(1)}, u32[]{:S(2)}, u32[]{:S(2)}) collective-permute-start(bf16[272,128]{1,0:T(8,128)(2,1)S(1)} %get-tuple-element.24), channel_id=1, source_target_pairs={{0,8},{4,12},{8,0},{12,4},{1,9},{5,13},{9,1},{13,5},{2,10},{6,14},... | collective-permute-start | bytes 208904 | tf_op jit(solution)/shard_map/ppermute | solution.py:35
  29.6 3.2 %collective-permute-start.9 = (bf16[272,128]{1,0:T(8,128)(2,1)S(1)}, bf16[272,128]{1,0:T(8,128)(2,1)S(1)}, u32[]{:S(2)}, u32[]{:S(2)}) collective-permute-start(bf16[272,128]{1,0:T(8,128)(2,1)S(1)} %get-tuple-element.25), channel_id=1, source_target_pairs={{0,12},{4,8},{8,4},{12,0},{1,13},{5,9},{9,5},{13,1},{2,14},{6,10},... | collective-permute-start | bytes 208904 | tf_op jit(solution)/shard_map/ppermute | solution.py:35
  32.8 3.5 %fetch.2.refs_4_ = bf16[2048,2048]{1,0:T(8,128)(2,1)S(1)} custom-call(bf16[4096,2048]{1,0:T(8,128)(2,1)} %weight_ref.3, bf16[272,128]{1,0:T(8,128)(2,1)S(1)} %get-tuple-element.22.refs_0_, bf16[4,256,512]{2,1,0:T(8,128)(2,1)S(1)} %collective-permute-done.10.refs_1_), custom_call_target="tpu_custom_call" | custom-call | bytes 16777216 | tf_op jit(solution)/shard_map/fetch/pallas_call | solution.py:391
  36.3 0.4 join.1.refs_0_
  36.7 1.3 %collective-permute-start.11 = (bf16[8,4096]{1,0:T(8,128)(2,1)S(1)}, bf16[8,4096]{1,0:T(8,128)(2,1)S(1)}, u32[]{:S(2)}, u32[]{:S(2)}) collective-permute-start(bf16[8,4096]{1,0:T(8,128)(2,1)S(1)} %join.1.refs_0_), channel_id=1, source_target_pairs={{0,4},{4,0},{8,12},{12,8},{1,5},{5,1},{9,13},{13,9},{2,6},{6,2},{1... | collective-permute-start | bytes 196616 | tf_op jit(solution)/shard_map/ppermute | solution.py:35
  38.0 2.1 %collective-permute-start.12 = (bf16[8,4096]{1,0:T(8,128)(2,1)S(1)}, bf16[8,4096]{1,0:T(8,128)(2,1)S(1)}, u32[]{:S(2)}, u32[]{:S(2)}) collective-permute-start(bf16[8,4096]{1,0:T(8,128)(2,1)S(1)} %join.1.refs_0_), channel_id=1, source_target_pairs={{0,8},{4,12},{8,0},{12,4},{1,9},{5,13},{9,1},{13,5},{2,10},{6,14},... | collective-permute-start | bytes 196616 | tf_op jit(solution)/shard_map/ppermute | solution.py:35
  40.1 1.1 %collective-permute-start.13 = (bf16[8,4096]{1,0:T(8,128)(2,1)S(1)}, bf16[8,4096]{1,0:T(8,128)(2,1)S(1)}, u32[]{:S(2)}, u32[]{:S(2)}) collective-permute-start(bf16[8,4096]{1,0:T(8,128)(2,1)S(1)} %join.1.refs_0_), channel_id=1, source_target_pairs={{0,12},{4,8},{8,4},{12,0},{1,13},{5,9},{9,5},{13,1},{2,14},{6,10},... | collective-permute-start | bytes 196616 | tf_op jit(solution)/shard_map/ppermute | solution.py:35
  41.2 3.5 %fetch.3.refs_5_ = bf16[2048,2048]{1,0:T(8,128)(2,1)S(1)} custom-call(bf16[4096,2048]{1,0:T(8,128)(2,1)} %weight_ref.3, bf16[8,4096]{1,0:T(8,128)(2,1)S(1)} %join.1.refs_0_), custom_call_target="tpu_custom_call" | custom-call | bytes 16777216 | tf_op jit(solution)/shard_map/fetch/pallas_call | solution.py:391
  44.7 1.5 %place.3.refs_0_ = bf16[1,16,256,512]{3,2,1,0:T(8,128)(2,1)} custom-call(bf16[4,256,512]{2,1,0:T(8,128)(2,1)S(1)} %get-tuple-element.19.refs_3_.refs_0_, bf16[4,256,512]{2,1,0:T(8,128)(2,1)S(1)} %collective-permute-done.10.refs_1_, bf16[1,256,512]{2,1,0:T(8,128)(2,1)S(1)} %collective-permute-done.2.refs_2_), custom_call_target="tpu_custom_call" | custom-call | bytes 4718592 | tf_op jit(solution)/shard_map/place/pallas_call | solution.py:198
  46.2 3.6 %project.1.refs_1_ = bf16[8,4,2048]{2,1,0:T(4,128)(2,1)} custom-call(bf16[8,4096]{1,0:T(8,128)(2,1)S(1)} %join.1.refs_0_, bf16[8,4096]{1,0:T(8,128)(2,1)S(1)} %collective-permute-done.11.refs_1_, bf16[8,4096]{1,0:T(8,128)(2,1)S(1)} %collective-permute-done.12.refs_2_, bf16[8,4096]{1,0:T(8,128)(2,1)S(1)} %collective-permute-done.13.refs_3_, ...), custom_call_target="tpu_custom_call" | custom-call | flops 536870912 | bytes 16777216 | tf_op jit(solution)/shard_map/project/pallas_call | solution.py:434
  49.8 1.0 %place.4.refs_0_ = bf16[1,16,256,512]{3,2,1,0:T(8,128)(2,1)} custom-call(bf16[1,16,256,512]{3,2,1,0:T(8,128)(2,1)} %place.3.refs_0_, bf16[8,4,2048]{2,1,0:T(4,128)(2,1)} %project.1.refs_1_, bf16[4,256,512]{2,1,0:T(8,128)(2,1)S(1)} %collective-permute-done.14.refs_2_), custom_call_target="tpu_custom_call", output_to_operand_aliasing={{}: (0, {})} | custom-call | bytes 2097152 | tf_op jit(solution)/shard_map/place/pallas_call | solution.py:198
  50.8 1.2 %collective-permute-done.15.refs_2_ = bf16[3,256,512]{2,1,0:T(8,128)(2,1)S(1)} collective-permute-done((bf16[3,256,512]{2,1,0:T(8,128)(2,1)S(1)}, bf16[3,256,512]{2,1,0:T(8,128)(2,1)S(1)}, u32[]{:S(2)}, u32[]{:S(2)}) %collective-permute-start.15) | collective-permute-done | bytes 786464 | tf_op jit(solution)/shard_map/ppermute | solution.py:35
  52.1 0.9 %place.5 = bf16[1,16,256,512]{3,2,1,0:T(8,128)(2,1)} custom-call(bf16[1,16,256,512]{3,2,1,0:T(8,128)(2,1)} %place.4.refs_0_, bf16[8,4,2048]{2,1,0:T(4,128)(2,1)} %project.1.refs_1_, bf16[3,256,512]{2,1,0:T(8,128)(2,1)S(1)} %collective-permute-done.15.refs_2_), custom_call_target="tpu_custom_call", output_to_operand_aliasing={{}: (0, {})} | custom-call | bytes 1572864 | tf_op jit(solution)/shard_map/place/pallas_call | solution.py:198
  (16 shorter events, 0.0 us)
Async XLA Ops:
  2.4 12.2 %collective-permute-start.2 = (bf16[1,256,512]{2,1,0:T(8,128)(2,1)S(1)}, bf16[1,256,512]{2,1,0:T(8,128)(2,1)S(1)}, u32[]{:S(2)}, u32[]{:S(2)}) collective-permute-start(bf16[1,256,512]{2,1,0:T(8,128)(2,1)S(1)} %pack.2.refs_0_), channel_id=1, source_target_pairs={{0,2},{1,3},{2,0},{3,1},{4,6},{5,7},{6,4},{7,5},{8,10},{9,11},{10,... | collective-permute-start | bytes 786440 | tf_op jit(solution)/shard_map/ppermute | solution.py:35
  7.8 11.1 %collective-permute-start.3 = (bf16[2,4,4096]{2,1,0:T(4,128)(2,1)S(1)}, bf16[2,4,4096]{2,1,0:T(4,128)(2,1)S(1)}, u32[]{:S(2)}, u32[]{:S(2)}) collective-permute-start(bf16[2,4,4096]{2,1,0:T(4,128)(2,1)S(1)} %get-tuple-element.18), channel_id=1, source_target_pairs={{0,1},{1,0},{2,3},{3,2},{4,5},{5,4},{6,7},{7,6},{8,9},{9,8},{10,11... | collective-permute-start | bytes 196616 | tf_op jit(solution)/shard_map/ppermute | solution.py:35
  7.9 4.4 %collective-permute-start = (bf16[2,4,1024]{2,1,0:T(4,128)(2,1)S(1)}, bf16[2,4,1024]{2,1,0:T(4,128)(2,1)S(1)}, u32[]{:S(2)}, u32[]{:S(2)}) collective-permute-start(bf16[2,4,1024]{2,1,0:T(4,128)(2,1)S(1)} %get-tuple-element.16), channel_id=1, source_target_pairs={{0,2},{1,3},{2,0},{3,1},{4,6},{5,7},{6,4},{7,5},{8,10},{9,11},{10,... | collective-permute-start | bytes 49160 | tf_op jit(solution)/shard_map/ppermute | solution.py:35
  8.0 6.7 %collective-permute-start.1 = (bf16[2,4,1024]{2,1,0:T(4,128)(2,1)S(1)}, bf16[2,4,1024]{2,1,0:T(4,128)(2,1)S(1)}, u32[]{:S(2)}, u32[]{:S(2)}) collective-permute-start(bf16[2,4,1024]{2,1,0:T(4,128)(2,1)S(1)} %get-tuple-element.17), channel_id=1, source_target_pairs={{0,3},{1,2},{2,1},{3,0},{4,7},{5,6},{6,5},{7,4},{8,11},{9,10},{10,... | collective-permute-start | bytes 49160 | tf_op jit(solution)/shard_map/ppermute | solution.py:35
  9.7 40.1 %collective-permute-start.14 = (bf16[4,256,512]{2,1,0:T(8,128)(2,1)S(1)}, bf16[4,256,512]{2,1,0:T(8,128)(2,1)S(1)}, u32[]{:S(2)}, u32[]{:S(2)}) collective-permute-start(bf16[4,256,512]{2,1,0:T(8,128)(2,1)S(1)} %get-tuple-element.14.refs_1_), channel_id=1, source_target_pairs={{0,3},{1,2},{2,1},{3,0},{4,7},{5,6},{6,5},{7,4},{8,11},{9,10},{10,... | collective-permute-start | bytes 3145736 | tf_op jit(solution)/shard_map/ppermute | solution.py:35
  12.3 39.8 %collective-permute-start.15 = (bf16[3,256,512]{2,1,0:T(8,128)(2,1)S(1)}, bf16[3,256,512]{2,1,0:T(8,128)(2,1)S(1)}, u32[]{:S(2)}, u32[]{:S(2)}) collective-permute-start(bf16[3,256,512]{2,1,0:T(8,128)(2,1)S(1)} %get-tuple-element.15.refs_2_), channel_id=1, source_target_pairs={{0,2},{1,3},{2,0},{3,1},{4,6},{5,7},{6,4},{7,5},{8,10},{9,11},{10,... | collective-permute-start | bytes 2359304 | tf_op jit(solution)/shard_map/ppermute | solution.py:35
  14.6 10.0 %copy-start = (s32[32,1]{0,1:T(1,128)S(1)}, s32[32,1]{0,1:T(1,128)}, u32[]{:S(2)}) copy-start(s32[32,1]{0,1:T(1,128)} %param.7) | copy-start | bytes 388
  14.6 10.0 %copy-start.1 = (s32[32]{0:T(128)S(1)}, s32[32]{0:T(128)}, u32[]{:S(2)}) copy-start(s32[32]{0:T(128)} %lengths_ref.1) | copy-start | bytes 388
  14.7 6.8 %collective-permute-start.4 = (bf16[2,2,4,1024]{3,2,1,0:T(4,128)(2,1)S(1)}, bf16[2,2,4,1024]{3,2,1,0:T(4,128)(2,1)S(1)}, u32[]{:S(2)}, u32[]{:S(2)}) collective-permute-start(bf16[2,2,4,1024]{3,2,1,0:T(4,128)(2,1)S(1)} %merge.1.refs_0_.refs_7_), channel_id=1, source_target_pairs={{0,4},{4,0},{8,12},{12,8},{1,5},{5,1},{9,13},{13,9},{2,6},{6,2},{1... | collective-permute-start | bytes 98312 | tf_op jit(solution)/shard_map/ppermute | solution.py:35
  16.3 5.4 %collective-permute-start.5 = (bf16[2,2,4,1024]{3,2,1,0:T(4,128)(2,1)S(1)}, bf16[2,2,4,1024]{3,2,1,0:T(4,128)(2,1)S(1)}, u32[]{:S(2)}, u32[]{:S(2)}) collective-permute-start(bf16[2,2,4,1024]{3,2,1,0:T(4,128)(2,1)S(1)} %merge.1.refs_0_.refs_7_), channel_id=1, source_target_pairs={{0,8},{4,12},{8,0},{12,4},{1,9},{5,13},{9,1},{13,5},{2,10},{6,14},... | collective-permute-start | bytes 98312 | tf_op jit(solution)/shard_map/ppermute | solution.py:35
  18.9 5.7 %collective-permute-start.6 = (bf16[2,2,4,1024]{3,2,1,0:T(4,128)(2,1)S(1)}, bf16[2,2,4,1024]{3,2,1,0:T(4,128)(2,1)S(1)}, u32[]{:S(2)}, u32[]{:S(2)}) collective-permute-start(bf16[2,2,4,1024]{3,2,1,0:T(4,128)(2,1)S(1)} %merge.1.refs_0_.refs_7_), channel_id=1, source_target_pairs={{0,12},{4,8},{8,4},{12,0},{1,13},{5,9},{9,5},{13,1},{2,14},{6,10},... | collective-permute-start | bytes 98312 | tf_op jit(solution)/shard_map/ppermute | solution.py:35
  21.5 8.1 %collective-permute-start.10 = (bf16[4,256,512]{2,1,0:T(8,128)(2,1)S(1)}, bf16[4,256,512]{2,1,0:T(8,128)(2,1)S(1)}, u32[]{:S(2)}, u32[]{:S(2)}) collective-permute-start(bf16[4,256,512]{2,1,0:T(8,128)(2,1)S(1)} %get-tuple-element.20.refs_4_), channel_id=1, source_target_pairs={{0,1},{1,0},{2,3},{3,2},{4,5},{5,4},{6,7},{7,6},{8,9},{9,8},{10,11... | collective-permute-start | bytes 3145736 | tf_op jit(solution)/shard_map/ppermute | solution.py:35
  28.4 7.9 %collective-permute-start.7 = (bf16[272,128]{1,0:T(8,128)(2,1)S(1)}, bf16[272,128]{1,0:T(8,128)(2,1)S(1)}, u32[]{:S(2)}, u32[]{:S(2)}) collective-permute-start(bf16[272,128]{1,0:T(8,128)(2,1)S(1)} %get-tuple-element.23), channel_id=1, source_target_pairs={{0,4},{4,0},{8,12},{12,8},{1,5},{5,1},{9,13},{13,9},{2,6},{6,2},{1... | collective-permute-start | bytes 208904 | tf_op jit(solution)/shard_map/ppermute | solution.py:35
  28.5 7.9 %collective-permute-start.8 = (bf16[272,128]{1,0:T(8,128)(2,1)S(1)}, bf16[272,128]{1,0:T(8,128)(2,1)S(1)}, u32[]{:S(2)}, u32[]{:S(2)}) collective-permute-start(bf16[272,128]{1,0:T(8,128)(2,1)S(1)} %get-tuple-element.24), channel_id=1, source_target_pairs={{0,8},{4,12},{8,0},{12,4},{1,9},{5,13},{9,1},{13,5},{2,10},{6,14},... | collective-permute-start | bytes 208904 | tf_op jit(solution)/shard_map/ppermute | solution.py:35
  29.6 6.7 %collective-permute-start.9 = (bf16[272,128]{1,0:T(8,128)(2,1)S(1)}, bf16[272,128]{1,0:T(8,128)(2,1)S(1)}, u32[]{:S(2)}, u32[]{:S(2)}) collective-permute-start(bf16[272,128]{1,0:T(8,128)(2,1)S(1)} %get-tuple-element.25), channel_id=1, source_target_pairs={{0,12},{4,8},{8,4},{12,0},{1,13},{5,9},{9,5},{13,1},{2,14},{6,10},... | collective-permute-start | bytes 208904 | tf_op jit(solution)/shard_map/ppermute | solution.py:35
  36.7 9.4 %collective-permute-start.11 = (bf16[8,4096]{1,0:T(8,128)(2,1)S(1)}, bf16[8,4096]{1,0:T(8,128)(2,1)S(1)}, u32[]{:S(2)}, u32[]{:S(2)}) collective-permute-start(bf16[8,4096]{1,0:T(8,128)(2,1)S(1)} %join.1.refs_0_), channel_id=1, source_target_pairs={{0,4},{4,0},{8,12},{12,8},{1,5},{5,1},{9,13},{13,9},{2,6},{6,2},{1... | collective-permute-start | bytes 196616 | tf_op jit(solution)/shard_map/ppermute | solution.py:35
  38.0 8.2 %collective-permute-start.12 = (bf16[8,4096]{1,0:T(8,128)(2,1)S(1)}, bf16[8,4096]{1,0:T(8,128)(2,1)S(1)}, u32[]{:S(2)}, u32[]{:S(2)}) collective-permute-start(bf16[8,4096]{1,0:T(8,128)(2,1)S(1)} %join.1.refs_0_), channel_id=1, source_target_pairs={{0,8},{4,12},{8,0},{12,4},{1,9},{5,13},{9,1},{13,5},{2,10},{6,14},... | collective-permute-start | bytes 196616 | tf_op jit(solution)/shard_map/ppermute | solution.py:35
  40.1 6.1 %collective-permute-start.13 = (bf16[8,4096]{1,0:T(8,128)(2,1)S(1)}, bf16[8,4096]{1,0:T(8,128)(2,1)S(1)}, u32[]{:S(2)}, u32[]{:S(2)}) collective-permute-start(bf16[8,4096]{1,0:T(8,128)(2,1)S(1)} %join.1.refs_0_), channel_id=1, source_target_pairs={{0,12},{4,8},{8,4},{12,0},{1,13},{5,9},{9,5},{13,1},{2,14},{6,10},... | collective-permute-start | bytes 196616 | tf_op jit(solution)/shard_map/ppermute | solution.py:35

commit v11 on v10

--- a/solution.py
+++ b/solution.py
@@ -451,7 +451,7 @@
     whole = 2 * CAP
     near = [(offset, 0, whole) for offset in range(2)]
     head, tail = [(2, 0, 1)], [(2, 1, whole - 1)]
-    far = [(offset, 0, whole) for offset in range(3, section_count)] + tail
+    far = tail + [(offset, 0, whole) for offset in range(3, section_count)]
 
     def across(parts, pieces):
         return [swap(part, "sec", piece[0]) for part, piece in zip(parts, pieces)]

time: 53.2 us -> 52.7 us (level)
  transfers between devices with their start and end apart: 16 -> 16, of which waited for: 4 -> 5; matrix products, arithmetic and copies ran while one was open for 0% -> 0% of each run, Pallas kernels for 41% -> 42%
where the time goes in v11:
time: 52.7 us; the launch traced here: 52.4 us
  Pallas kernels  24.6 us (47%)
  starting transfers between devices  20.3 us (39%)
  waiting for transfers between devices  6.77 us (13%)
  between operations  0.78 us (1%)
    ppermute x16, starting transfers between devices, swap(): return lax.ppermute(value, axis, [(i, i ^ offset) for i in range(count)])  20.3 us
    pallas_call x2, Pallas kernels, fetch(): pl.pallas_call(functools.partial(fetch_kernel, number * size), out_shape=...  6.94 us
    ppermute x16, waiting for transfers between devices, swap(): return lax.ppermute(value, axis, [(i, i ^ offset) for i in range(count)])  6.77 us
    pallas_call x2, Pallas kernels, pack(): pl.pallas_call(functools.partial(pack_kernel, pieces, section_count), out...  4.12 us
    pallas_call x1, Pallas kernels, attend(): pl.pallas_call(functools.partial(attend_kernel, pieces, section_count, tp...  3.76 us
    pallas_call x1, Pallas kernels, project(): pl.pallas_call(functools.partial(project_kernel, count, min(256, width)),...  3.65 us
    pallas_call x3, Pallas kernels, place(): pl.pallas_call(functools.partial(place_kernel, pieces), out_shape=jax.Sha...  3.37 us
    pallas_call x1, Pallas kernels, first_pack(): pl.pallas_call(functools.partial(first_pack_kernel, pieces, section_count...  2.38 us
  transfers between devices with their start and end apart: 16, of which 5 were waited for; matrix products, arithmetic and copies ran while one was open for 0% of the time, Pallas kernels for 42%

profile of v11, /device:TPU:0, one launch (start us, length us, event | category | flops | bytes accessed | tf_op | source)
XLA Modules:
  0.0 52.4 jit_solution(9776385899008507129)
XLA Ops:
  0.6 1.8 %pack.2.refs_0_ = bf16[1,256,512]{2,1,0:T(8,128)(2,1)S(1)} custom-call(s32[32]{0:T(128)} %bitcast.2, bf16[8,2,256,512]{3,2,1,0:T(8,128)(2,1)} %cache_ref.5), custom_call_target="tpu_custom_call" | custom-call | bytes 524288 | tf_op jit(solution)/shard_map/pack/pallas_call | solution.py:168
  2.4 3.0 %collective-permute-start.2 = (bf16[1,256,512]{2,1,0:T(8,128)(2,1)S(1)}, bf16[1,256,512]{2,1,0:T(8,128)(2,1)S(1)}, u32[]{:S(2)}, u32[]{:S(2)}) collective-permute-start(bf16[1,256,512]{2,1,0:T(8,128)(2,1)S(1)} %pack.2.refs_0_), channel_id=1, source_target_pairs={{0,2},{1,3},{2,0},{3,1},{4,6},{5,7},{6,4},{7,5},{8,10},{9,11},{10,... | collective-permute-start | bytes 786440 | tf_op jit(solution)/shard_map/ppermute | solution.py:35
  5.4 2.4 %first_pack.1 = (bf16[3,256,512]{2,1,0:T(8,128)(2,1)S(1)}, bf16[4,256,512]{2,1,0:T(8,128)(2,1)S(1)}, bf16[2,4,4096]{2,1,0:T(4,128)(2,1)S(1)}, bf16[2,4,4096]{2,1...) custom-call(s32[32]{0:T(128)} %bitcast.3, bf16[8,2,256,512]{3,2,1,0:T(8,128)(2,1)} %cache_ref.5, ...), custom_call_target="tpu_custom_call" | custom-call | bytes 3997696 | tf_op jit(solution)/shard_map/first_pack/pallas_call | solution.py:150
  7.8 0.1 collective-permute-start.3
  7.9 0.1 collective-permute-start
  8.0 1.8 %collective-permute-start.1 = (bf16[2,4,1024]{2,1,0:T(4,128)(2,1)S(1)}, bf16[2,4,1024]{2,1,0:T(4,128)(2,1)S(1)}, u32[]{:S(2)}, u32[]{:S(2)}) collective-permute-start(bf16[2,4,1024]{2,1,0:T(4,128)(2,1)S(1)} %get-tuple-element.17), channel_id=1, source_target_pairs={{0,3},{1,2},{2,1},{3,0},{4,7},{5,6},{6,5},{7,4},{8,11},{9,10},{10,... | collective-permute-start | bytes 49160 | tf_op jit(solution)/shard_map/ppermute | solution.py:35
  9.8 0.3 collective-permute-start.14
  10.1 2.2 %collective-permute-done.refs_0_ = bf16[2,4,1024]{2,1,0:T(4,128)(2,1)S(1)} collective-permute-done((bf16[2,4,1024]{2,1,0:T(4,128)(2,1)S(1)}, bf16[2,4,1024]{2,1,0:T(4,128)(2,1)S(1)}, u32[]{:S(2)}, u32[]{:S(2)}) %collective-permute-start) | collective-permute-done | bytes 16416 | tf_op jit(solution)/shard_map/ppermute | solution.py:35
  12.3 0.1 collective-permute-start.15
  12.4 0.1 collective-permute-done.1.refs_1_
  12.5 1.7 %collective-permute-start.4 = (bf16[2,2,4,1024]{3,2,1,0:T(4,128)(2,1)S(1)}, bf16[2,2,4,1024]{3,2,1,0:T(4,128)(2,1)S(1)}, u32[]{:S(2)}, u32[]{:S(2)}) collective-permute-start(bf16[2,2,4,1024]{3,2,1,0:T(4,128)(2,1)S(1)} %merge.1.refs_0_.refs_7_), channel_id=1, source_target_pairs={{0,4},{4,0},{8,12},{12,8},{1,5},{5,1},{9,13},{13,9},{2,6},{6,2},{1... | collective-permute-start | bytes 98312 | tf_op jit(solution)/shard_map/ppermute | solution.py:35
  14.2 2.6 %collective-permute-start.5 = (bf16[2,2,4,1024]{3,2,1,0:T(4,128)(2,1)S(1)}, bf16[2,2,4,1024]{3,2,1,0:T(4,128)(2,1)S(1)}, u32[]{:S(2)}, u32[]{:S(2)}) collective-permute-start(bf16[2,2,4,1024]{3,2,1,0:T(4,128)(2,1)S(1)} %merge.1.refs_0_.refs_7_), channel_id=1, source_target_pairs={{0,8},{4,12},{8,0},{12,4},{1,9},{5,13},{9,1},{13,5},{2,10},{6,14},... | collective-permute-start | bytes 98312 | tf_op jit(solution)/shard_map/ppermute | solution.py:35
  16.8 0.2 collective-permute-start.6
  16.9 2.3 %pack.3 = (bf16[4,256,512]{2,1,0:T(8,128)(2,1)S(1)}, bf16[4,256,512]{2,1,0:T(8,128)(2,1)S(1)}) custom-call(s32[32]{0:T(128)} %bitcast.4, bf16[8,2,256,512]{3,2,1,0:T(8,128)(2,1)} %cache_ref.5, bf16[2,2,4,1024]{3,2,1,0:T(4,128)(2,1)S(1)} %merge.1.refs_0_.refs_7_, bf16[2,4,4096]{2,1,0:T(4,128)(2,1)S(1)} %collective-permute-done.3.refs_1_.refs_6_), custom_call_target="tpu_custom_call" | custom-call | flops 10000000000 | bytes 4194304 | tf_op jit(solution)/shard_map/pack/pallas_call | solution.py:168
  19.3 1.5 %collective-permute-start.10 = (bf16[4,256,512]{2,1,0:T(8,128)(2,1)S(1)}, bf16[4,256,512]{2,1,0:T(8,128)(2,1)S(1)}, u32[]{:S(2)}, u32[]{:S(2)}) collective-permute-start(bf16[4,256,512]{2,1,0:T(8,128)(2,1)S(1)} %get-tuple-element.20.refs_4_), channel_id=1, source_target_pairs={{0,1},{1,0},{2,3},{3,2},{4,5},{5,4},{6,7},{7,6},{8,9},{9,8},{10,11... | collective-permute-start | bytes 3145736 | tf_op jit(solution)/shard_map/ppermute | solution.py:35
  20.9 1.6 %collective-permute-done.6.refs_10_ = bf16[2,2,4,1024]{3,2,1,0:T(4,128)(2,1)S(1)} collective-permute-done((bf16[2,2,4,1024]{3,2,1,0:T(4,128)(2,1)S(1)}, bf16[2,2,4,1024]{3,2,1,0:T(4,128)(2,1)S(1)}, u32[]{:S(2)}, u32[]{:S(2)}) %collective-permute-start.6) | collective-permute-done | bytes 32800 | tf_op jit(solution)/shard_map/ppermute | solution.py:35
  22.5 3.8 %attend.1 = (bf16[272,128]{1,0:T(8,128)(2,1)S(1)}, bf16[272,128]{1,0:T(8,128)(2,1)S(1)}, bf16[272,128]{1,0:T(8,128)(2,1)S(1)}, bf16[272,128]{1,0:T(8,128)(2,1)S(1)}) custom-call(s32[32]{0:T(128)S(1)} %bitcast.5, s32[32]{0:T(128)S(1)} %copy-done.1, bf16[1,256,512]{2,1,0:T(8,128)(2,1)S(1)} %pack.2.refs_0_, bf16[3,256,512]{2,1,0:T(8,128)(2,1)S(1)} %get-tuple-element.14.refs_1_, ...), custom_call_target="tpu_custom_call" | custom-call | flops 20000000000 | bytes 4194304 | tf_op jit(solution)/shard_map/attend/pallas_call | solution.py:298
  26.3 0.1 collective-permute-start.7
  26.4 2.5 %collective-permute-start.8 = (bf16[272,128]{1,0:T(8,128)(2,1)S(1)}, bf16[272,128]{1,0:T(8,128)(2,1)S(1)}, u32[]{:S(2)}, u32[]{:S(2)}) collective-permute-start(bf16[272,128]{1,0:T(8,128)(2,1)S(1)} %get-tuple-element.24), channel_id=1, source_target_pairs={{0,8},{4,12},{8,0},{12,4},{1,9},{5,13},{9,1},{13,5},{2,10},{6,14},... | collective-permute-start | bytes 208904 | tf_op jit(solution)/shard_map/ppermute | solution.py:35
  28.8 1.9 %collective-permute-start.9 = (bf16[272,128]{1,0:T(8,128)(2,1)S(1)}, bf16[272,128]{1,0:T(8,128)(2,1)S(1)}, u32[]{:S(2)}, u32[]{:S(2)}) collective-permute-start(bf16[272,128]{1,0:T(8,128)(2,1)S(1)} %get-tuple-element.25), channel_id=1, source_target_pairs={{0,12},{4,8},{8,4},{12,0},{1,13},{5,9},{9,5},{13,1},{2,14},{6,10},... | collective-permute-start | bytes 208904 | tf_op jit(solution)/shard_map/ppermute | solution.py:35
  30.7 3.5 %fetch.2.refs_4_ = bf16[2048,2048]{1,0:T(8,128)(2,1)S(1)} custom-call(bf16[4096,2048]{1,0:T(8,128)(2,1)} %weight_ref.3, bf16[272,128]{1,0:T(8,128)(2,1)S(1)} %get-tuple-element.22.refs_0_, bf16[4,256,512]{2,1,0:T(8,128)(2,1)S(1)} %collective-permute-done.10.refs_1_), custom_call_target="tpu_custom_call" | custom-call | bytes 16777216 | tf_op jit(solution)/shard_map/fetch/pallas_call | solution.py:391
  34.2 1.1 %collective-permute-done.8.refs_2_ = bf16[272,128]{1,0:T(8,128)(2,1)S(1)} collective-permute-done((bf16[272,128]{1,0:T(8,128)(2,1)S(1)}, bf16[272,128]{1,0:T(8,128)(2,1)S(1)}, u32[]{:S(2)}, u32[]{:S(2)}) %collective-permute-start.8) | collective-permute-done | bytes 69664 | tf_op jit(solution)/shard_map/ppermute | solution.py:35
  35.3 0.4 join.1.refs_0_
  35.7 1.7 %collective-permute-start.11 = (bf16[8,4096]{1,0:T(8,128)(2,1)S(1)}, bf16[8,4096]{1,0:T(8,128)(2,1)S(1)}, u32[]{:S(2)}, u32[]{:S(2)}) collective-permute-start(bf16[8,4096]{1,0:T(8,128)(2,1)S(1)} %join.1.refs_0_), channel_id=1, source_target_pairs={{0,4},{4,0},{8,12},{12,8},{1,5},{5,1},{9,13},{13,9},{2,6},{6,2},{1... | collective-permute-start | bytes 196616 | tf_op jit(solution)/shard_map/ppermute | solution.py:35
  37.4 0.6 %collective-permute-start.12 = (bf16[8,4096]{1,0:T(8,128)(2,1)S(1)}, bf16[8,4096]{1,0:T(8,128)(2,1)S(1)}, u32[]{:S(2)}, u32[]{:S(2)}) collective-permute-start(bf16[8,4096]{1,0:T(8,128)(2,1)S(1)} %join.1.refs_0_), channel_id=1, source_target_pairs={{0,8},{4,12},{8,0},{12,4},{1,9},{5,13},{9,1},{13,5},{2,10},{6,14},... | collective-permute-start | bytes 196616 | tf_op jit(solution)/shard_map/ppermute | solution.py:35
  38.1 2.1 %collective-permute-start.13 = (bf16[8,4096]{1,0:T(8,128)(2,1)S(1)}, bf16[8,4096]{1,0:T(8,128)(2,1)S(1)}, u32[]{:S(2)}, u32[]{:S(2)}) collective-permute-start(bf16[8,4096]{1,0:T(8,128)(2,1)S(1)} %join.1.refs_0_), channel_id=1, source_target_pairs={{0,12},{4,8},{8,4},{12,0},{1,13},{5,9},{9,5},{13,1},{2,14},{6,10},... | collective-permute-start | bytes 196616 | tf_op jit(solution)/shard_map/ppermute | solution.py:35
  40.2 3.5 %fetch.3.refs_5_ = bf16[2048,2048]{1,0:T(8,128)(2,1)S(1)} custom-call(bf16[4096,2048]{1,0:T(8,128)(2,1)} %weight_ref.3, bf16[8,4096]{1,0:T(8,128)(2,1)S(1)} %join.1.refs_0_), custom_call_target="tpu_custom_call" | custom-call | bytes 16777216 | tf_op jit(solution)/shard_map/fetch/pallas_call | solution.py:391
  43.7 1.5 %place.3.refs_0_ = bf16[1,16,256,512]{3,2,1,0:T(8,128)(2,1)} custom-call(bf16[4,256,512]{2,1,0:T(8,128)(2,1)S(1)} %get-tuple-element.19.refs_3_.refs_0_, bf16[4,256,512]{2,1,0:T(8,128)(2,1)S(1)} %collective-permute-done.10.refs_1_, bf16[1,256,512]{2,1,0:T(8,128)(2,1)S(1)} %collective-permute-done.2.refs_2_), custom_call_target="tpu_custom_call" | custom-call | bytes 4718592 | tf_op jit(solution)/shard_map/place/pallas_call | solution.py:198
  45.2 3.6 %project.1.refs_1_ = bf16[8,4,2048]{2,1,0:T(4,128)(2,1)} custom-call(bf16[8,4096]{1,0:T(8,128)(2,1)S(1)} %join.1.refs_0_, bf16[8,4096]{1,0:T(8,128)(2,1)S(1)} %collective-permute-done.11.refs_1_, bf16[8,4096]{1,0:T(8,128)(2,1)S(1)} %collective-permute-done.12.refs_2_, bf16[8,4096]{1,0:T(8,128)(2,1)S(1)} %collective-permute-done.13.refs_3_, ...), custom_call_target="tpu_custom_call" | custom-call | flops 536870912 | bytes 16777216 | tf_op jit(solution)/shard_map/project/pallas_call | solution.py:434
  48.8 0.9 %place.4.refs_0_ = bf16[1,16,256,512]{3,2,1,0:T(8,128)(2,1)} custom-call(bf16[1,16,256,512]{3,2,1,0:T(8,128)(2,1)} %place.3.refs_0_, bf16[8,4,2048]{2,1,0:T(4,128)(2,1)} %project.1.refs_1_, bf16[3,256,512]{2,1,0:T(8,128)(2,1)S(1)} %collective-permute-done.14.refs_2_), custom_call_target="tpu_custom_call", output_to_operand_aliasing={{}: (0, {})} | custom-call | bytes 1572864 | tf_op jit(solution)/shard_map/place/pallas_call | solution.py:198
  49.7 1.7 %collective-permute-done.15.refs_2_ = bf16[4,256,512]{2,1,0:T(8,128)(2,1)S(1)} collective-permute-done((bf16[4,256,512]{2,1,0:T(8,128)(2,1)S(1)}, bf16[4,256,512]{2,1,0:T(8,128)(2,1)S(1)}, u32[]{:S(2)}, u32[]{:S(2)}) %collective-permute-start.15) | collective-permute-done | bytes 1048608 | tf_op jit(solution)/shard_map/ppermute | solution.py:35
  51.5 1.0 %place.5 = bf16[1,16,256,512]{3,2,1,0:T(8,128)(2,1)} custom-call(bf16[1,16,256,512]{3,2,1,0:T(8,128)(2,1)} %place.4.refs_0_, bf16[8,4,2048]{2,1,0:T(4,128)(2,1)} %project.1.refs_1_, bf16[4,256,512]{2,1,0:T(8,128)(2,1)S(1)} %collective-permute-done.15.refs_2_), custom_call_target="tpu_custom_call", output_to_operand_aliasing={{}: (0, {})} | custom-call | bytes 2097152 | tf_op jit(solution)/shard_map/place/pallas_call | solution.py:198
  (16 shorter events, 0.0 us)
Async XLA Ops:
  2.4 10.0 %collective-permute-start.2 = (bf16[1,256,512]{2,1,0:T(8,128)(2,1)S(1)}, bf16[1,256,512]{2,1,0:T(8,128)(2,1)S(1)}, u32[]{:S(2)}, u32[]{:S(2)}) collective-permute-start(bf16[1,256,512]{2,1,0:T(8,128)(2,1)S(1)} %pack.2.refs_0_), channel_id=1, source_target_pairs={{0,2},{1,3},{2,0},{3,1},{4,6},{5,7},{6,4},{7,5},{8,10},{9,11},{10,... | collective-permute-start | bytes 786440 | tf_op jit(solution)/shard_map/ppermute | solution.py:35
  7.8 9.0 %collective-permute-start.3 = (bf16[2,4,4096]{2,1,0:T(4,128)(2,1)S(1)}, bf16[2,4,4096]{2,1,0:T(4,128)(2,1)S(1)}, u32[]{:S(2)}, u32[]{:S(2)}) collective-permute-start(bf16[2,4,4096]{2,1,0:T(4,128)(2,1)S(1)} %get-tuple-element.18), channel_id=1, source_target_pairs={{0,1},{1,0},{2,3},{3,2},{4,5},{5,4},{6,7},{7,6},{8,9},{9,8},{10,11... | collective-permute-start | bytes 196616 | tf_op jit(solution)/shard_map/ppermute | solution.py:35
  7.9 4.4 %collective-permute-start = (bf16[2,4,1024]{2,1,0:T(4,128)(2,1)S(1)}, bf16[2,4,1024]{2,1,0:T(4,128)(2,1)S(1)}, u32[]{:S(2)}, u32[]{:S(2)}) collective-permute-start(bf16[2,4,1024]{2,1,0:T(4,128)(2,1)S(1)} %get-tuple-element.16), channel_id=1, source_target_pairs={{0,2},{1,3},{2,0},{3,1},{4,6},{5,7},{6,4},{7,5},{8,10},{9,11},{10,... | collective-permute-start | bytes 49160 | tf_op jit(solution)/shard_map/ppermute | solution.py:35
  8.0 4.5 %collective-permute-start.1 = (bf16[2,4,1024]{2,1,0:T(4,128)(2,1)S(1)}, bf16[2,4,1024]{2,1,0:T(4,128)(2,1)S(1)}, u32[]{:S(2)}, u32[]{:S(2)}) collective-permute-start(bf16[2,4,1024]{2,1,0:T(4,128)(2,1)S(1)} %get-tuple-element.17), channel_id=1, source_target_pairs={{0,3},{1,2},{2,1},{3,0},{4,7},{5,6},{6,5},{7,4},{8,11},{9,10},{10,... | collective-permute-start | bytes 49160 | tf_op jit(solution)/shard_map/ppermute | solution.py:35
  9.8 39.1 %collective-permute-start.14 = (bf16[3,256,512]{2,1,0:T(8,128)(2,1)S(1)}, bf16[3,256,512]{2,1,0:T(8,128)(2,1)S(1)}, u32[]{:S(2)}, u32[]{:S(2)}) collective-permute-start(bf16[3,256,512]{2,1,0:T(8,128)(2,1)S(1)} %get-tuple-element.14.refs_1_), channel_id=1, source_target_pairs={{0,2},{1,3},{2,0},{3,1},{4,6},{5,7},{6,4},{7,5},{8,10},{9,11},{10,... | collective-permute-start | bytes 2359304 | tf_op jit(solution)/shard_map/ppermute | solution.py:35
  12.3 39.2 %collective-permute-start.15 = (bf16[4,256,512]{2,1,0:T(8,128)(2,1)S(1)}, bf16[4,256,512]{2,1,0:T(8,128)(2,1)S(1)}, u32[]{:S(2)}, u32[]{:S(2)}) collective-permute-start(bf16[4,256,512]{2,1,0:T(8,128)(2,1)S(1)} %get-tuple-element.15.refs_2_), channel_id=1, source_target_pairs={{0,3},{1,2},{2,1},{3,0},{4,7},{5,6},{6,5},{7,4},{8,11},{9,10},{10,... | collective-permute-start | bytes 3145736 | tf_op jit(solution)/shard_map/ppermute | solution.py:35
  12.5 10.0 %copy-start = (s32[32,1]{0,1:T(1,128)S(1)}, s32[32,1]{0,1:T(1,128)}, u32[]{:S(2)}) copy-start(s32[32,1]{0,1:T(1,128)} %param.7) | copy-start | bytes 388
  12.5 10.0 %copy-start.1 = (s32[32]{0:T(128)S(1)}, s32[32]{0:T(128)}, u32[]{:S(2)}) copy-start(s32[32]{0:T(128)} %lengths_ref.1) | copy-start | bytes 388
  12.5 6.8 %collective-permute-start.4 = (bf16[2,2,4,1024]{3,2,1,0:T(4,128)(2,1)S(1)}, bf16[2,2,4,1024]{3,2,1,0:T(4,128)(2,1)S(1)}, u32[]{:S(2)}, u32[]{:S(2)}) collective-permute-start(bf16[2,2,4,1024]{3,2,1,0:T(4,128)(2,1)S(1)} %merge.1.refs_0_.refs_7_), channel_id=1, source_target_pairs={{0,4},{4,0},{8,12},{12,8},{1,5},{5,1},{9,13},{13,9},{2,6},{6,2},{1... | collective-permute-start | bytes 98312 | tf_op jit(solution)/shard_map/ppermute | solution.py:35
  14.2 6.7 %collective-permute-start.5 = (bf16[2,2,4,1024]{3,2,1,0:T(4,128)(2,1)S(1)}, bf16[2,2,4,1024]{3,2,1,0:T(4,128)(2,1)S(1)}, u32[]{:S(2)}, u32[]{:S(2)}) collective-permute-start(bf16[2,2,4,1024]{3,2,1,0:T(4,128)(2,1)S(1)} %merge.1.refs_0_.refs_7_), channel_id=1, source_target_pairs={{0,8},{4,12},{8,0},{12,4},{1,9},{5,13},{9,1},{13,5},{2,10},{6,14},... | collective-permute-start | bytes 98312 | tf_op jit(solution)/shard_map/ppermute | solution.py:35
  16.8 5.7 %collective-permute-start.6 = (bf16[2,2,4,1024]{3,2,1,0:T(4,128)(2,1)S(1)}, bf16[2,2,4,1024]{3,2,1,0:T(4,128)(2,1)S(1)}, u32[]{:S(2)}, u32[]{:S(2)}) collective-permute-start(bf16[2,2,4,1024]{3,2,1,0:T(4,128)(2,1)S(1)} %merge.1.refs_0_.refs_7_), channel_id=1, source_target_pairs={{0,12},{4,8},{8,4},{12,0},{1,13},{5,9},{9,5},{13,1},{2,14},{6,10},... | collective-permute-start | bytes 98312 | tf_op jit(solution)/shard_map/ppermute | solution.py:35
  19.3 9.5 %collective-permute-start.10 = (bf16[4,256,512]{2,1,0:T(8,128)(2,1)S(1)}, bf16[4,256,512]{2,1,0:T(8,128)(2,1)S(1)}, u32[]{:S(2)}, u32[]{:S(2)}) collective-permute-start(bf16[4,256,512]{2,1,0:T(8,128)(2,1)S(1)} %get-tuple-element.20.refs_4_), channel_id=1, source_target_pairs={{0,1},{1,0},{2,3},{3,2},{4,5},{5,4},{6,7},{7,6},{8,9},{9,8},{10,11... | collective-permute-start | bytes 3145736 | tf_op jit(solution)/shard_map/ppermute | solution.py:35
  26.3 7.9 %collective-permute-start.7 = (bf16[272,128]{1,0:T(8,128)(2,1)S(1)}, bf16[272,128]{1,0:T(8,128)(2,1)S(1)}, u32[]{:S(2)}, u32[]{:S(2)}) collective-permute-start(bf16[272,128]{1,0:T(8,128)(2,1)S(1)} %get-tuple-element.23), channel_id=1, source_target_pairs={{0,4},{4,0},{8,12},{12,8},{1,5},{5,1},{9,13},{13,9},{2,6},{6,2},{1... | collective-permute-start | bytes 208904 | tf_op jit(solution)/shard_map/ppermute | solution.py:35
  26.4 9.0 %collective-permute-start.8 = (bf16[272,128]{1,0:T(8,128)(2,1)S(1)}, bf16[272,128]{1,0:T(8,128)(2,1)S(1)}, u32[]{:S(2)}, u32[]{:S(2)}) collective-permute-start(bf16[272,128]{1,0:T(8,128)(2,1)S(1)} %get-tuple-element.24), channel_id=1, source_target_pairs={{0,8},{4,12},{8,0},{12,4},{1,9},{5,13},{9,1},{13,5},{2,10},{6,14},... | collective-permute-start | bytes 208904 | tf_op jit(solution)/shard_map/ppermute | solution.py:35
  28.8 6.5 %collective-permute-start.9 = (bf16[272,128]{1,0:T(8,128)(2,1)S(1)}, bf16[272,128]{1,0:T(8,128)(2,1)S(1)}, u32[]{:S(2)}, u32[]{:S(2)}) collective-permute-start(bf16[272,128]{1,0:T(8,128)(2,1)S(1)} %get-tuple-element.25), channel_id=1, source_target_pairs={{0,12},{4,8},{8,4},{12,0},{1,13},{5,9},{9,5},{13,1},{2,14},{6,10},... | collective-permute-start | bytes 208904 | tf_op jit(solution)/shard_map/ppermute | solution.py:35
  35.7 9.4 %collective-permute-start.11 = (bf16[8,4096]{1,0:T(8,128)(2,1)S(1)}, bf16[8,4096]{1,0:T(8,128)(2,1)S(1)}, u32[]{:S(2)}, u32[]{:S(2)}) collective-permute-start(bf16[8,4096]{1,0:T(8,128)(2,1)S(1)} %join.1.refs_0_), channel_id=1, source_target_pairs={{0,4},{4,0},{8,12},{12,8},{1,5},{5,1},{9,13},{13,9},{2,6},{6,2},{1... | collective-permute-start | bytes 196616 | tf_op jit(solution)/shard_map/ppermute | solution.py:35
  37.4 7.7 %collective-permute-start.12 = (bf16[8,4096]{1,0:T(8,128)(2,1)S(1)}, bf16[8,4096]{1,0:T(8,128)(2,1)S(1)}, u32[]{:S(2)}, u32[]{:S(2)}) collective-permute-start(bf16[8,4096]{1,0:T(8,128)(2,1)S(1)} %join.1.refs_0_), channel_id=1, source_target_pairs={{0,8},{4,12},{8,0},{12,4},{1,9},{5,13},{9,1},{13,5},{2,10},{6,14},... | collective-permute-start | bytes 196616 | tf_op jit(solution)/shard_map/ppermute | solution.py:35
  38.1 7.1 %collective-permute-start.13 = (bf16[8,4096]{1,0:T(8,128)(2,1)S(1)}, bf16[8,4096]{1,0:T(8,128)(2,1)S(1)}, u32[]{:S(2)}, u32[]{:S(2)}) collective-permute-start(bf16[8,4096]{1,0:T(8,128)(2,1)S(1)} %join.1.refs_0_), channel_id=1, source_target_pairs={{0,12},{4,8},{8,4},{12,0},{1,13},{5,9},{9,5},{13,1},{2,14},{6,10},... | collective-permute-start | bytes 196616 | tf_op jit(solution)/shard_map/ppermute | solution.py:35

commit v12 on v11

--- a/solution.py
+++ b/solution.py
@@ -96,6 +96,41 @@
                 pl.when(rows[offset, half // 2][1])(copy(n, place, offset, half).wait)
 
     return finish
+
+
+def head_kernel(piece, full, routing_ref, cache_ref, out_ref, routed, held, routing_sem, sem):
+    offset, half, _ = piece
+    section = lax.axis_index("sec")
+    copies = [pltpu.make_async_copy(routing_ref, routed, routing_sem)]
+    for i in range(REQ_GRP):
+        copies.append(pltpu.make_async_copy(cache_ref.at[i, half % 2], held.at[i], sem.at[i]))
+    for copy in copies:
+        copy.start()
+    copies[0].wait()
+    row, filled = slot_row(own_targets(routed, section), section ^ offset, half // 2)
+    for copy in copies[1:]:
+        copy.wait()
+    chosen = held[row]
+    out_ref[0] = chosen if full else jnp.where(filled, chosen, jnp.zeros_like(chosen))
+
+
+def pack_head(routing, cache, piece, section_count):
+    shape = cache.shape[2:]
+    return pl.pallas_call(
+        functools.partial(head_kernel, piece, section_count * CAP == REQ_GRP),
+        out_shape=jax.ShapeDtypeStruct((1,) + shape, cache.dtype),
+        in_specs=[HBM, HBM],
+        out_specs=VMEM,
+        scratch_shapes=[
+            pltpu.SMEM(routing.shape, jnp.int32),
+            pltpu.VMEM((REQ_GRP,) + shape, cache.dtype),
+            pltpu.SemaphoreType.DMA,
+            pltpu.SemaphoreType.DMA((REQ_GRP,)),
+        ],
+        compiler_params=limit(16),
+        cost_estimate=cost(0, cache.size),
+        name="pack_head",
+    )(in_hbm(routing), in_hbm(cache))
 
 
 def first_pack_kernel(pieces, section_count, routing_ref, cache_ref, query_ref, *refs):
@@ -456,7 +491,7 @@
     def across(parts, pieces):
         return [swap(part, "sec", piece[0]) for part, piece in zip(parts, pieces)]
 
-    head_caches = pack(routing, prompt_key_values, [], head, section_count)
+    head_caches = [pack_head(routing, prompt_key_values, head[0], section_count)]
     head_parts = across(head_caches, head)
     far_caches, query_parts = first_pack(
         routing, prompt_key_values, queries, head_caches, far, section_count, tp_count

time: 52.7 us -> 52.5 us (level)
    pallas_call x2 -> x1, Pallas kernels: 4.12 us -> 2.34 us  [pack(): pl.pallas_call(functools.partial(pack_kernel, pieces, section_count), out...]
    pallas_call x0 -> x1, Pallas kernels: none -> 1.6 us  [pack_head(): pl.pallas_call(functools.partial(head_kernel, piece, section_count * CAP...]
where the time goes in v12:
time: 52.5 us; the launch traced here: 52.3 us
  Pallas kernels  24.4 us (46%)
  starting transfers between devices  20.3 us (39%)
  waiting for transfers between devices  6.77 us (13%)
  between operations  0.78 us (1%)
    ppermute x16, starting transfers between devices, swap(): return lax.ppermute(value, axis, [(i, i ^ offset) for i in range(count)])  20.3 us
    pallas_call x2, Pallas kernels, fetch(): pl.pallas_call(functools.partial(fetch_kernel, number * size), out_shape=...  6.94 us
    ppermute x16, waiting for transfers between devices, swap(): return lax.ppermute(value, axis, [(i, i ^ offset) for i in range(count)])  6.77 us
    pallas_call x1, Pallas kernels, attend(): pl.pallas_call(functools.partial(attend_kernel, pieces, section_count, tp...  3.76 us
    pallas_call x1, Pallas kernels, project(): pl.pallas_call(functools.partial(project_kernel, count, min(256, width)),...  3.65 us
    pallas_call x3, Pallas kernels, place(): pl.pallas_call(functools.partial(place_kernel, pieces), out_shape=jax.Sha...  3.37 us
    pallas_call x1, Pallas kernels, first_pack(): pl.pallas_call(functools.partial(first_pack_kernel, pieces, section_count...  2.38 us
    pallas_call x1, Pallas kernels, pack(): pl.pallas_call(functools.partial(pack_kernel, pieces, section_count), out...  2.34 us
  transfers between devices with their start and end apart: 16, of which 5 were waited for; matrix products, arithmetic and copies ran while one was open for 0% of the time, Pallas kernels for 42%

profile of v12, /device:TPU:0, one launch (start us, length us, event | category | flops | bytes accessed | tf_op | source)
XLA Modules:
  0.0 52.3 jit_solution(10155207308083164765)
XLA Ops:
  0.6 1.6 %pack_head.1.refs_0_ = bf16[1,256,512]{2,1,0:T(8,128)(2,1)S(1)} custom-call(s32[32]{0:T(128)} %bitcast.2, bf16[8,2,256,512]{3,2,1,0:T(8,128)(2,1)} %cache_ref.5), custom_call_target="tpu_custom_call" | custom-call | bytes 2097152 | tf_op jit(solution)/shard_map/pack_head/pallas_call | solution.py:119
  2.2 3.0 %collective-permute-start.2 = (bf16[1,256,512]{2,1,0:T(8,128)(2,1)S(1)}, bf16[1,256,512]{2,1,0:T(8,128)(2,1)S(1)}, u32[]{:S(2)}, u32[]{:S(2)}) collective-permute-start(bf16[1,256,512]{2,1,0:T(8,128)(2,1)S(1)} %pack_head.1.refs_0_), channel_id=1, source_target_pairs={{0,2},{1,3},{2,0},{3,1},{4,6},{5,7},{6,4},{7,5},{8,10},{9,11},{10,... | collective-permute-start | bytes 786440 | tf_op jit(solution)/shard_map/ppermute | solution.py:35
  5.2 2.4 %first_pack.1 = (bf16[3,256,512]{2,1,0:T(8,128)(2,1)S(1)}, bf16[4,256,512]{2,1,0:T(8,128)(2,1)S(1)}, bf16[2,4,4096]{2,1,0:T(4,128)(2,1)S(1)}, bf16[2,4,4096]{2,1...) custom-call(s32[32]{0:T(128)} %bitcast.3, bf16[8,2,256,512]{3,2,1,0:T(8,128)(2,1)} %cache_ref.5, ...), custom_call_target="tpu_custom_call" | custom-call | bytes 3997696 | tf_op jit(solution)/shard_map/first_pack/pallas_call | solution.py:185
  7.6 0.1 collective-permute-start.3
  7.7 0.1 collective-permute-start
  7.8 1.8 %collective-permute-start.1 = (bf16[2,4,1024]{2,1,0:T(4,128)(2,1)S(1)}, bf16[2,4,1024]{2,1,0:T(4,128)(2,1)S(1)}, u32[]{:S(2)}, u32[]{:S(2)}) collective-permute-start(bf16[2,4,1024]{2,1,0:T(4,128)(2,1)S(1)} %get-tuple-element.17), channel_id=1, source_target_pairs={{0,3},{1,2},{2,1},{3,0},{4,7},{5,6},{6,5},{7,4},{8,11},{9,10},{10,... | collective-permute-start | bytes 49160 | tf_op jit(solution)/shard_map/ppermute | solution.py:35
  9.6 0.3 collective-permute-start.14
  9.9 2.2 %collective-permute-done.refs_0_ = bf16[2,4,1024]{2,1,0:T(4,128)(2,1)S(1)} collective-permute-done((bf16[2,4,1024]{2,1,0:T(4,128)(2,1)S(1)}, bf16[2,4,1024]{2,1,0:T(4,128)(2,1)S(1)}, u32[]{:S(2)}, u32[]{:S(2)}) %collective-permute-start) | collective-permute-done | bytes 16416 | tf_op jit(solution)/shard_map/ppermute | solution.py:35
  12.1 0.1 collective-permute-start.15
  12.2 0.1 collective-permute-done.1.refs_1_
  12.3 1.7 %collective-permute-start.4 = (bf16[2,2,4,1024]{3,2,1,0:T(4,128)(2,1)S(1)}, bf16[2,2,4,1024]{3,2,1,0:T(4,128)(2,1)S(1)}, u32[]{:S(2)}, u32[]{:S(2)}) collective-permute-start(bf16[2,2,4,1024]{3,2,1,0:T(4,128)(2,1)S(1)} %merge.1.refs_0_.refs_7_), channel_id=1, source_target_pairs={{0,4},{4,0},{8,12},{12,8},{1,5},{5,1},{9,13},{13,9},{2,6},{6,2},{1... | collective-permute-start | bytes 98312 | tf_op jit(solution)/shard_map/ppermute | solution.py:35
  14.0 2.6 %collective-permute-start.5 = (bf16[2,2,4,1024]{3,2,1,0:T(4,128)(2,1)S(1)}, bf16[2,2,4,1024]{3,2,1,0:T(4,128)(2,1)S(1)}, u32[]{:S(2)}, u32[]{:S(2)}) collective-permute-start(bf16[2,2,4,1024]{3,2,1,0:T(4,128)(2,1)S(1)} %merge.1.refs_0_.refs_7_), channel_id=1, source_target_pairs={{0,8},{4,12},{8,0},{12,4},{1,9},{5,13},{9,1},{13,5},{2,10},{6,14},... | collective-permute-start | bytes 98312 | tf_op jit(solution)/shard_map/ppermute | solution.py:35
  16.6 0.2 collective-permute-start.6
  16.8 2.3 %pack.1 = (bf16[4,256,512]{2,1,0:T(8,128)(2,1)S(1)}, bf16[4,256,512]{2,1,0:T(8,128)(2,1)S(1)}) custom-call(s32[32]{0:T(128)} %bitcast.4, bf16[8,2,256,512]{3,2,1,0:T(8,128)(2,1)} %cache_ref.5, bf16[2,2,4,1024]{3,2,1,0:T(4,128)(2,1)S(1)} %merge.1.refs_0_.refs_7_, bf16[2,4,4096]{2,1,0:T(4,128)(2,1)S(1)} %collective-permute-done.3.refs_1_.refs_6_), custom_call_target="tpu_custom_call" | custom-call | flops 10000000000 | bytes 4194304 | tf_op jit(solution)/shard_map/pack/pallas_call | solution.py:203
  19.1 1.5 %collective-permute-start.10 = (bf16[4,256,512]{2,1,0:T(8,128)(2,1)S(1)}, bf16[4,256,512]{2,1,0:T(8,128)(2,1)S(1)}, u32[]{:S(2)}, u32[]{:S(2)}) collective-permute-start(bf16[4,256,512]{2,1,0:T(8,128)(2,1)S(1)} %get-tuple-element.20.refs_4_), channel_id=1, source_target_pairs={{0,1},{1,0},{2,3},{3,2},{4,5},{5,4},{6,7},{7,6},{8,9},{9,8},{10,11... | collective-permute-start | bytes 3145736 | tf_op jit(solution)/shard_map/ppermute | solution.py:35
  20.7 1.6 %collective-permute-done.6.refs_10_ = bf16[2,2,4,1024]{3,2,1,0:T(4,128)(2,1)S(1)} collective-permute-done((bf16[2,2,4,1024]{3,2,1,0:T(4,128)(2,1)S(1)}, bf16[2,2,4,1024]{3,2,1,0:T(4,128)(2,1)S(1)}, u32[]{:S(2)}, u32[]{:S(2)}) %collective-permute-start.6) | collective-permute-done | bytes 32800 | tf_op jit(solution)/shard_map/ppermute | solution.py:35
  22.3 3.8 %attend.1 = (bf16[272,128]{1,0:T(8,128)(2,1)S(1)}, bf16[272,128]{1,0:T(8,128)(2,1)S(1)}, bf16[272,128]{1,0:T(8,128)(2,1)S(1)}, bf16[272,128]{1,0:T(8,128)(2,1)S(1)}) custom-call(s32[32]{0:T(128)S(1)} %bitcast.5, s32[32]{0:T(128)S(1)} %copy-done.1, bf16[1,256,512]{2,1,0:T(8,128)(2,1)S(1)} %pack_head.1.refs_0_, ...), custom_call_target="tpu_custom_call" | custom-call | flops 20000000000 | bytes 4194304 | tf_op jit(solution)/shard_map/attend/pallas_call | solution.py:333
  26.1 0.1 collective-permute-start.7
  26.2 2.5 %collective-permute-start.8 = (bf16[272,128]{1,0:T(8,128)(2,1)S(1)}, bf16[272,128]{1,0:T(8,128)(2,1)S(1)}, u32[]{:S(2)}, u32[]{:S(2)}) collective-permute-start(bf16[272,128]{1,0:T(8,128)(2,1)S(1)} %get-tuple-element.24), channel_id=1, source_target_pairs={{0,8},{4,12},{8,0},{12,4},{1,9},{5,13},{9,1},{13,5},{2,10},{6,14},... | collective-permute-start | bytes 208904 | tf_op jit(solution)/shard_map/ppermute | solution.py:35
  28.6 1.9 %collective-permute-start.9 = (bf16[272,128]{1,0:T(8,128)(2,1)S(1)}, bf16[272,128]{1,0:T(8,128)(2,1)S(1)}, u32[]{:S(2)}, u32[]{:S(2)}) collective-permute-start(bf16[272,128]{1,0:T(8,128)(2,1)S(1)} %get-tuple-element.25), channel_id=1, source_target_pairs={{0,12},{4,8},{8,4},{12,0},{1,13},{5,9},{9,5},{13,1},{2,14},{6,10},... | collective-permute-start | bytes 208904 | tf_op jit(solution)/shard_map/ppermute | solution.py:35
  30.5 3.5 %fetch.2.refs_4_ = bf16[2048,2048]{1,0:T(8,128)(2,1)S(1)} custom-call(bf16[4096,2048]{1,0:T(8,128)(2,1)} %weight_ref.3, bf16[272,128]{1,0:T(8,128)(2,1)S(1)} %get-tuple-element.22.refs_0_, bf16[4,256,512]{2,1,0:T(8,128)(2,1)S(1)} %collective-permute-done.10.refs_1_), custom_call_target="tpu_custom_call" | custom-call | bytes 16777216 | tf_op jit(solution)/shard_map/fetch/pallas_call | solution.py:426
  34.0 1.1 %collective-permute-done.8.refs_2_ = bf16[272,128]{1,0:T(8,128)(2,1)S(1)} collective-permute-done((bf16[272,128]{1,0:T(8,128)(2,1)S(1)}, bf16[272,128]{1,0:T(8,128)(2,1)S(1)}, u32[]{:S(2)}, u32[]{:S(2)}) %collective-permute-start.8) | collective-permute-done | bytes 69664 | tf_op jit(solution)/shard_map/ppermute | solution.py:35
  35.1 0.4 join.1.refs_0_
  35.5 1.7 %collective-permute-start.11 = (bf16[8,4096]{1,0:T(8,128)(2,1)S(1)}, bf16[8,4096]{1,0:T(8,128)(2,1)S(1)}, u32[]{:S(2)}, u32[]{:S(2)}) collective-permute-start(bf16[8,4096]{1,0:T(8,128)(2,1)S(1)} %join.1.refs_0_), channel_id=1, source_target_pairs={{0,4},{4,0},{8,12},{12,8},{1,5},{5,1},{9,13},{13,9},{2,6},{6,2},{1... | collective-permute-start | bytes 196616 | tf_op jit(solution)/shard_map/ppermute | solution.py:35
  37.3 0.6 %collective-permute-start.12 = (bf16[8,4096]{1,0:T(8,128)(2,1)S(1)}, bf16[8,4096]{1,0:T(8,128)(2,1)S(1)}, u32[]{:S(2)}, u32[]{:S(2)}) collective-permute-start(bf16[8,4096]{1,0:T(8,128)(2,1)S(1)} %join.1.refs_0_), channel_id=1, source_target_pairs={{0,8},{4,12},{8,0},{12,4},{1,9},{5,13},{9,1},{13,5},{2,10},{6,14},... | collective-permute-start | bytes 196616 | tf_op jit(solution)/shard_map/ppermute | solution.py:35
  37.9 2.1 %collective-permute-start.13 = (bf16[8,4096]{1,0:T(8,128)(2,1)S(1)}, bf16[8,4096]{1,0:T(8,128)(2,1)S(1)}, u32[]{:S(2)}, u32[]{:S(2)}) collective-permute-start(bf16[8,4096]{1,0:T(8,128)(2,1)S(1)} %join.1.refs_0_), channel_id=1, source_target_pairs={{0,12},{4,8},{8,4},{12,0},{1,13},{5,9},{9,5},{13,1},{2,14},{6,10},... | collective-permute-start | bytes 196616 | tf_op jit(solution)/shard_map/ppermute | solution.py:35
  40.0 3.5 %fetch.3.refs_5_ = bf16[2048,2048]{1,0:T(8,128)(2,1)S(1)} custom-call(bf16[4096,2048]{1,0:T(8,128)(2,1)} %weight_ref.3, bf16[8,4096]{1,0:T(8,128)(2,1)S(1)} %join.1.refs_0_), custom_call_target="tpu_custom_call" | custom-call | bytes 16777216 | tf_op jit(solution)/shard_map/fetch/pallas_call | solution.py:426
  43.5 1.5 %place.3.refs_0_ = bf16[1,16,256,512]{3,2,1,0:T(8,128)(2,1)} custom-call(bf16[4,256,512]{2,1,0:T(8,128)(2,1)S(1)} %get-tuple-element.19.refs_3_.refs_0_, bf16[4,256,512]{2,1,0:T(8,128)(2,1)S(1)} %collective-permute-done.10.refs_1_, bf16[1,256,512]{2,1,0:T(8,128)(2,1)S(1)} %collective-permute-done.2.refs_2_), custom_call_target="tpu_custom_call" | custom-call | bytes 4718592 | tf_op jit(solution)/shard_map/place/pallas_call | solution.py:233
  45.0 3.6 %project.1.refs_1_ = bf16[8,4,2048]{2,1,0:T(4,128)(2,1)} custom-call(bf16[8,4096]{1,0:T(8,128)(2,1)S(1)} %join.1.refs_0_, bf16[8,4096]{1,0:T(8,128)(2,1)S(1)} %collective-permute-done.11.refs_1_, bf16[8,4096]{1,0:T(8,128)(2,1)S(1)} %collective-permute-done.12.refs_2_, bf16[8,4096]{1,0:T(8,128)(2,1)S(1)} %collective-permute-done.13.refs_3_, ...), custom_call_target="tpu_custom_call" | custom-call | flops 536870912 | bytes 16777216 | tf_op jit(solution)/shard_map/project/pallas_call | solution.py:469
  48.6 0.9 %place.4.refs_0_ = bf16[1,16,256,512]{3,2,1,0:T(8,128)(2,1)} custom-call(bf16[1,16,256,512]{3,2,1,0:T(8,128)(2,1)} %place.3.refs_0_, bf16[8,4,2048]{2,1,0:T(4,128)(2,1)} %project.1.refs_1_, bf16[3,256,512]{2,1,0:T(8,128)(2,1)S(1)} %collective-permute-done.14.refs_2_), custom_call_target="tpu_custom_call", output_to_operand_aliasing={{}: (0, {})} | custom-call | bytes 1572864 | tf_op jit(solution)/shard_map/place/pallas_call | solution.py:233
  49.6 1.7 %collective-permute-done.15.refs_2_ = bf16[4,256,512]{2,1,0:T(8,128)(2,1)S(1)} collective-permute-done((bf16[4,256,512]{2,1,0:T(8,128)(2,1)S(1)}, bf16[4,256,512]{2,1,0:T(8,128)(2,1)S(1)}, u32[]{:S(2)}, u32[]{:S(2)}) %collective-permute-start.15) | collective-permute-done | bytes 1048608 | tf_op jit(solution)/shard_map/ppermute | solution.py:35
  51.3 1.0 %place.5 = bf16[1,16,256,512]{3,2,1,0:T(8,128)(2,1)} custom-call(bf16[1,16,256,512]{3,2,1,0:T(8,128)(2,1)} %place.4.refs_0_, bf16[8,4,2048]{2,1,0:T(4,128)(2,1)} %project.1.refs_1_, bf16[4,256,512]{2,1,0:T(8,128)(2,1)S(1)} %collective-permute-done.15.refs_2_), custom_call_target="tpu_custom_call", output_to_operand_aliasing={{}: (0, {})} | custom-call | bytes 2097152 | tf_op jit(solution)/shard_map/place/pallas_call | solution.py:233
  (16 shorter events, 0.0 us)
Async XLA Ops:
  2.2 10.0 %collective-permute-start.2 = (bf16[1,256,512]{2,1,0:T(8,128)(2,1)S(1)}, bf16[1,256,512]{2,1,0:T(8,128)(2,1)S(1)}, u32[]{:S(2)}, u32[]{:S(2)}) collective-permute-start(bf16[1,256,512]{2,1,0:T(8,128)(2,1)S(1)} %pack_head.1.refs_0_), channel_id=1, source_target_pairs={{0,2},{1,3},{2,0},{3,1},{4,6},{5,7},{6,4},{7,5},{8,10},{9,11},{10,... | collective-permute-start | bytes 786440 | tf_op jit(solution)/shard_map/ppermute | solution.py:35
  7.6 9.0 %collective-permute-start.3 = (bf16[2,4,4096]{2,1,0:T(4,128)(2,1)S(1)}, bf16[2,4,4096]{2,1,0:T(4,128)(2,1)S(1)}, u32[]{:S(2)}, u32[]{:S(2)}) collective-permute-start(bf16[2,4,4096]{2,1,0:T(4,128)(2,1)S(1)} %get-tuple-element.18), channel_id=1, source_target_pairs={{0,1},{1,0},{2,3},{3,2},{4,5},{5,4},{6,7},{7,6},{8,9},{9,8},{10,11... | collective-permute-start | bytes 196616 | tf_op jit(solution)/shard_map/ppermute | solution.py:35
  7.7 4.4 %collective-permute-start = (bf16[2,4,1024]{2,1,0:T(4,128)(2,1)S(1)}, bf16[2,4,1024]{2,1,0:T(4,128)(2,1)S(1)}, u32[]{:S(2)}, u32[]{:S(2)}) collective-permute-start(bf16[2,4,1024]{2,1,0:T(4,128)(2,1)S(1)} %get-tuple-element.16), channel_id=1, source_target_pairs={{0,2},{1,3},{2,0},{3,1},{4,6},{5,7},{6,4},{7,5},{8,10},{9,11},{10,... | collective-permute-start | bytes 49160 | tf_op jit(solution)/shard_map/ppermute | solution.py:35
  7.8 4.5 %collective-permute-start.1 = (bf16[2,4,1024]{2,1,0:T(4,128)(2,1)S(1)}, bf16[2,4,1024]{2,1,0:T(4,128)(2,1)S(1)}, u32[]{:S(2)}, u32[]{:S(2)}) collective-permute-start(bf16[2,4,1024]{2,1,0:T(4,128)(2,1)S(1)} %get-tuple-element.17), channel_id=1, source_target_pairs={{0,3},{1,2},{2,1},{3,0},{4,7},{5,6},{6,5},{7,4},{8,11},{9,10},{10,... | collective-permute-start | bytes 49160 | tf_op jit(solution)/shard_map/ppermute | solution.py:35
  9.6 39.1 %collective-permute-start.14 = (bf16[3,256,512]{2,1,0:T(8,128)(2,1)S(1)}, bf16[3,256,512]{2,1,0:T(8,128)(2,1)S(1)}, u32[]{:S(2)}, u32[]{:S(2)}) collective-permute-start(bf16[3,256,512]{2,1,0:T(8,128)(2,1)S(1)} %get-tuple-element.14.refs_1_), channel_id=1, source_target_pairs={{0,2},{1,3},{2,0},{3,1},{4,6},{5,7},{6,4},{7,5},{8,10},{9,11},{10,... | collective-permute-start | bytes 2359304 | tf_op jit(solution)/shard_map/ppermute | solution.py:35
  12.1 39.2 %collective-permute-start.15 = (bf16[4,256,512]{2,1,0:T(8,128)(2,1)S(1)}, bf16[4,256,512]{2,1,0:T(8,128)(2,1)S(1)}, u32[]{:S(2)}, u32[]{:S(2)}) collective-permute-start(bf16[4,256,512]{2,1,0:T(8,128)(2,1)S(1)} %get-tuple-element.15.refs_2_), channel_id=1, source_target_pairs={{0,3},{1,2},{2,1},{3,0},{4,7},{5,6},{6,5},{7,4},{8,11},{9,10},{10,... | collective-permute-start | bytes 3145736 | tf_op jit(solution)/shard_map/ppermute | solution.py:35
  12.3 10.0 %copy-start = (s32[32,1]{0,1:T(1,128)S(1)}, s32[32,1]{0,1:T(1,128)}, u32[]{:S(2)}) copy-start(s32[32,1]{0,1:T(1,128)} %param.7) | copy-start | bytes 388
  12.3 10.0 %copy-start.1 = (s32[32]{0:T(128)S(1)}, s32[32]{0:T(128)}, u32[]{:S(2)}) copy-start(s32[32]{0:T(128)} %lengths_ref.1) | copy-start | bytes 388
  12.3 6.8 %collective-permute-start.4 = (bf16[2,2,4,1024]{3,2,1,0:T(4,128)(2,1)S(1)}, bf16[2,2,4,1024]{3,2,1,0:T(4,128)(2,1)S(1)}, u32[]{:S(2)}, u32[]{:S(2)}) collective-permute-start(bf16[2,2,4,1024]{3,2,1,0:T(4,128)(2,1)S(1)} %merge.1.refs_0_.refs_7_), channel_id=1, source_target_pairs={{0,4},{4,0},{8,12},{12,8},{1,5},{5,1},{9,13},{13,9},{2,6},{6,2},{1... | collective-permute-start | bytes 98312 | tf_op jit(solution)/shard_map/ppermute | solution.py:35
  14.0 6.7 %collective-permute-start.5 = (bf16[2,2,4,1024]{3,2,1,0:T(4,128)(2,1)S(1)}, bf16[2,2,4,1024]{3,2,1,0:T(4,128)(2,1)S(1)}, u32[]{:S(2)}, u32[]{:S(2)}) collective-permute-start(bf16[2,2,4,1024]{3,2,1,0:T(4,128)(2,1)S(1)} %merge.1.refs_0_.refs_7_), channel_id=1, source_target_pairs={{0,8},{4,12},{8,0},{12,4},{1,9},{5,13},{9,1},{13,5},{2,10},{6,14},... | collective-permute-start | bytes 98312 | tf_op jit(solution)/shard_map/ppermute | solution.py:35
  16.6 5.7 %collective-permute-start.6 = (bf16[2,2,4,1024]{3,2,1,0:T(4,128)(2,1)S(1)}, bf16[2,2,4,1024]{3,2,1,0:T(4,128)(2,1)S(1)}, u32[]{:S(2)}, u32[]{:S(2)}) collective-permute-start(bf16[2,2,4,1024]{3,2,1,0:T(4,128)(2,1)S(1)} %merge.1.refs_0_.refs_7_), channel_id=1, source_target_pairs={{0,12},{4,8},{8,4},{12,0},{1,13},{5,9},{9,5},{13,1},{2,14},{6,10},... | collective-permute-start | bytes 98312 | tf_op jit(solution)/shard_map/ppermute | solution.py:35
  19.1 9.5 %collective-permute-start.10 = (bf16[4,256,512]{2,1,0:T(8,128)(2,1)S(1)}, bf16[4,256,512]{2,1,0:T(8,128)(2,1)S(1)}, u32[]{:S(2)}, u32[]{:S(2)}) collective-permute-start(bf16[4,256,512]{2,1,0:T(8,128)(2,1)S(1)} %get-tuple-element.20.refs_4_), channel_id=1, source_target_pairs={{0,1},{1,0},{2,3},{3,2},{4,5},{5,4},{6,7},{7,6},{8,9},{9,8},{10,11... | collective-permute-start | bytes 3145736 | tf_op jit(solution)/shard_map/ppermute | solution.py:35
  26.1 7.9 %collective-permute-start.7 = (bf16[272,128]{1,0:T(8,128)(2,1)S(1)}, bf16[272,128]{1,0:T(8,128)(2,1)S(1)}, u32[]{:S(2)}, u32[]{:S(2)}) collective-permute-start(bf16[272,128]{1,0:T(8,128)(2,1)S(1)} %get-tuple-element.23), channel_id=1, source_target_pairs={{0,4},{4,0},{8,12},{12,8},{1,5},{5,1},{9,13},{13,9},{2,6},{6,2},{1... | collective-permute-start | bytes 208904 | tf_op jit(solution)/shard_map/ppermute | solution.py:35
  26.2 9.0 %collective-permute-start.8 = (bf16[272,128]{1,0:T(8,128)(2,1)S(1)}, bf16[272,128]{1,0:T(8,128)(2,1)S(1)}, u32[]{:S(2)}, u32[]{:S(2)}) collective-permute-start(bf16[272,128]{1,0:T(8,128)(2,1)S(1)} %get-tuple-element.24), channel_id=1, source_target_pairs={{0,8},{4,12},{8,0},{12,4},{1,9},{5,13},{9,1},{13,5},{2,10},{6,14},... | collective-permute-start | bytes 208904 | tf_op jit(solution)/shard_map/ppermute | solution.py:35
  28.6 6.5 %collective-permute-start.9 = (bf16[272,128]{1,0:T(8,128)(2,1)S(1)}, bf16[272,128]{1,0:T(8,128)(2,1)S(1)}, u32[]{:S(2)}, u32[]{:S(2)}) collective-permute-start(bf16[272,128]{1,0:T(8,128)(2,1)S(1)} %get-tuple-element.25), channel_id=1, source_target_pairs={{0,12},{4,8},{8,4},{12,0},{1,13},{5,9},{9,5},{13,1},{2,14},{6,10},... | collective-permute-start | bytes 208904 | tf_op jit(solution)/shard_map/ppermute | solution.py:35
  35.5 9.4 %collective-permute-start.11 = (bf16[8,4096]{1,0:T(8,128)(2,1)S(1)}, bf16[8,4096]{1,0:T(8,128)(2,1)S(1)}, u32[]{:S(2)}, u32[]{:S(2)}) collective-permute-start(bf16[8,4096]{1,0:T(8,128)(2,1)S(1)} %join.1.refs_0_), channel_id=1, source_target_pairs={{0,4},{4,0},{8,12},{12,8},{1,5},{5,1},{9,13},{13,9},{2,6},{6,2},{1... | collective-permute-start | bytes 196616 | tf_op jit(solution)/shard_map/ppermute | solution.py:35
  37.3 7.7 %collective-permute-start.12 = (bf16[8,4096]{1,0:T(8,128)(2,1)S(1)}, bf16[8,4096]{1,0:T(8,128)(2,1)S(1)}, u32[]{:S(2)}, u32[]{:S(2)}) collective-permute-start(bf16[8,4096]{1,0:T(8,128)(2,1)S(1)} %join.1.refs_0_), channel_id=1, source_target_pairs={{0,8},{4,12},{8,0},{12,4},{1,9},{5,13},{9,1},{13,5},{2,10},{6,14},... | collective-permute-start | bytes 196616 | tf_op jit(solution)/shard_map/ppermute | solution.py:35
  37.9 7.1 %collective-permute-start.13 = (bf16[8,4096]{1,0:T(8,128)(2,1)S(1)}, bf16[8,4096]{1,0:T(8,128)(2,1)S(1)}, u32[]{:S(2)}, u32[]{:S(2)}) collective-permute-start(bf16[8,4096]{1,0:T(8,128)(2,1)S(1)} %join.1.refs_0_), channel_id=1, source_target_pairs={{0,12},{4,8},{8,4},{12,0},{1,13},{5,9},{9,5},{13,1},{2,14},{6,10},... | collective-permute-start | bytes 196616 | tf_op jit(solution)/shard_map/ppermute | solution.py:35

commit v13 on v12

--- a/solution.py
+++ b/solution.py
@@ -520,8 +520,10 @@
         layer_out = project(shares, held_weight, samples)
 
     held_cache = place([], near_parts + head_parts, near + head, slot_count)
-    for part, piece in zip(far_parts, far):
+    for part, piece in zip(far_parts[:-1], far[:-1]):
         held_cache = place([held_cache, layer_out], [part], [piece], slot_count)
+    first = (lax.axis_index("sec") ^ far[-1][0]) * whole + far[-1][1]
+    held_cache = lax.dynamic_update_slice(held_cache, far_parts[-1][None], (0, first, 0, 0))
     held_cache = held_cache.reshape((1, slot_count) + prompt_key_values.shape[1:])
     return (layer_out, held_cache)
 

time: 52.5 us -> 58.8 us (1.12)
  local copies, waits for them, and re-layouts: 0.01 us -> 8.44 us
  waiting for transfers between devices: 6.77 us -> 4.8 us
  starting transfers between devices: 20.3 us -> 18.7 us
  Pallas kernels: 24.4 us -> 25.7 us
    unnamed x4 -> x8, local copies, waits for them, and re-layouts: 0.01 us -> 6.17 us
    dynamic_update_slice x0 -> x1, local copies, waits for them, and re-layouts: none -> 2.27 us  [body(): lax.dynamic_update_slice(held_cache, far_parts[-1][None], (0, first, 0, 0))]
    ppermute x16, waiting for transfers between devices: 6.77 us -> 4.8 us  [swap(): return lax.ppermute(value, axis, [(i, i ^ offset) for i in range(count)])]
    ppermute x16, starting transfers between devices: 20.3 us -> 18.7 us  [swap(): return lax.ppermute(value, axis, [(i, i ^ offset) for i in range(count)])]
    pallas_call x1, Pallas kernels: 2.38 us -> 3.7 us  [first_pack(): pl.pallas_call(functools.partial(first_pack_kernel, pieces, section_count...]
    pallas_call x3 -> x2, Pallas kernels: 3.37 us -> 2.38 us  [place(): pl.pallas_call(functools.partial(place_kernel, pieces), out_shape=jax.Sha...]
    pallas_call x1, Pallas kernels: 3.76 us -> 4.69 us  [attend(): pl.pallas_call(functools.partial(attend_kernel, pieces, section_count, tp...]
  transfers between devices with their start and end apart: 16 -> 16, of which waited for: 5 -> 4; matrix products, arithmetic and copies ran while one was open for 0% -> 0% of each run, Pallas kernels for 42% -> 41%
where the time goes in v13:
time: 58.8 us; the launch traced here: 58.5 us
  Pallas kernels  25.7 us (44%)
  starting transfers between devices  18.7 us (32%)
  local copies, waits for them, and re-layouts  8.44 us (14%)
  waiting for transfers between devices  4.8 us (8%)
  between operations  0.82 us (1%)
    ppermute x16, starting transfers between devices, swap(): return lax.ppermute(value, axis, [(i, i ^ offset) for i in range(count)])  18.7 us
    pallas_call x2, Pallas kernels, fetch(): pl.pallas_call(functools.partial(fetch_kernel, number * size), out_shape=...  6.94 us
    unnamed x8, local copies, waits for them, and re-layouts  6.17 us
    ppermute x16, waiting for transfers between devices, swap(): return lax.ppermute(value, axis, [(i, i ^ offset) for i in range(count)])  4.8 us
    pallas_call x1, Pallas kernels, attend(): pl.pallas_call(functools.partial(attend_kernel, pieces, section_count, tp...  4.69 us
    pallas_call x1, Pallas kernels, first_pack(): pl.pallas_call(functools.partial(first_pack_kernel, pieces, section_count...  3.7 us
    pallas_call x1, Pallas kernels, project(): pl.pallas_call(functools.partial(project_kernel, count, min(256, width)),...  3.64 us
    pallas_call x2, Pallas kernels, place(): pl.pallas_call(functools.partial(place_kernel, pieces), out_shape=jax.Sha...  2.38 us
  transfers between devices with their start and end apart: 16, of which 4 were waited for; matrix products, arithmetic and copies ran while one was open for 0% of the time, Pallas kernels for 41%

profile of v13, /device:TPU:0, one launch (start us, length us, event | category | flops | bytes accessed | tf_op | source)
XLA Modules:
  0.0 58.5 jit_solution(9051909608463955252)
XLA Ops:
  0.6 1.6 %pack_head.1.refs_0_ = bf16[1,256,512]{2,1,0:T(8,128)(2,1)S(1)} custom-call(s32[32]{0:T(128)} %bitcast.4, bf16[8,2,256,512]{3,2,1,0:T(8,128)(2,1)} %cache_ref.5), custom_call_target="tpu_custom_call" | custom-call | bytes 2097152 | tf_op jit(solution)/shard_map/pack_head/pallas_call | solution.py:119
  2.2 3.0 %collective-permute-start.2 = (bf16[1,256,512]{2,1,0:T(8,128)(2,1)S(1)}, bf16[1,256,512]{2,1,0:T(8,128)(2,1)S(1)}, u32[]{:S(2)}, u32[]{:S(2)}) collective-permute-start(bf16[1,256,512]{2,1,0:T(8,128)(2,1)S(1)} %pack_head.1.refs_0_), channel_id=1, source_target_pairs={{0,2},{1,3},{2,0},{3,1},{4,6},{5,7},{6,4},{7,5},{8,10},{9,11},{10,... | collective-permute-start | bytes 786440 | tf_op jit(solution)/shard_map/ppermute | solution.py:35
  5.2 3.7 %first_pack.1 = (bf16[3,256,512]{2,1,0:T(8,128)(2,1)}, bf16[4,256,512]{2,1,0:T(8,128)(2,1)}, bf16[2,4,4096]{2,1,0:T(4,128)(2,1)S(1)}, bf16[2,4,4096]{2,1,0:T(4,1...) custom-call(s32[32]{0:T(128)} %bitcast.5, bf16[8,2,256,512]{3,2,1,0:T(8,128)(2,1)} %cache_ref.5, ...), custom_call_target="tpu_custom_call" | custom-call | bytes 3997696 | tf_op jit(solution)/shard_map/first_pack/pallas_call | solution.py:185
  9.0 0.1 collective-permute-start.3
  9.0 0.1 collective-permute-start
  9.1 1.8 %collective-permute-start.1 = (bf16[2,4,1024]{2,1,0:T(4,128)(2,1)S(1)}, bf16[2,4,1024]{2,1,0:T(4,128)(2,1)S(1)}, u32[]{:S(2)}, u32[]{:S(2)}) collective-permute-start(bf16[2,4,1024]{2,1,0:T(4,128)(2,1)S(1)} %get-tuple-element.17), channel_id=1, source_target_pairs={{0,3},{1,2},{2,1},{3,0},{4,7},{5,6},{6,5},{7,4},{8,11},{9,10},{10,... | collective-permute-start | bytes 49160 | tf_op jit(solution)/shard_map/ppermute | solution.py:35
  10.9 0.3 collective-permute-start.14
  11.2 1.6 %collective-permute-done.refs_0_ = bf16[2,4,1024]{2,1,0:T(4,128)(2,1)S(1)} collective-permute-done((bf16[2,4,1024]{2,1,0:T(4,128)(2,1)S(1)}, bf16[2,4,1024]{2,1,0:T(4,128)(2,1)S(1)}, u32[]{:S(2)}, u32[]{:S(2)}) %collective-permute-start) | collective-permute-done | bytes 16416 | tf_op jit(solution)/shard_map/ppermute | solution.py:35
  12.9 0.0 copy-start.2
  12.9 1.8 %collective-permute-start.4 = (bf16[2,2,4,1024]{3,2,1,0:T(4,128)(2,1)S(1)}, bf16[2,2,4,1024]{3,2,1,0:T(4,128)(2,1)S(1)}, u32[]{:S(2)}, u32[]{:S(2)}) collective-permute-start(bf16[2,2,4,1024]{3,2,1,0:T(4,128)(2,1)S(1)} %merge.1.refs_0_.refs_7_), channel_id=1, source_target_pairs={{0,4},{4,0},{8,12},{12,8},{1,5},{5,1},{9,13},{13,9},{2,6},{6,2},{1... | collective-permute-start | bytes 98312 | tf_op jit(solution)/shard_map/ppermute | solution.py:35
  14.7 2.6 %collective-permute-start.5 = (bf16[2,2,4,1024]{3,2,1,0:T(4,128)(2,1)S(1)}, bf16[2,2,4,1024]{3,2,1,0:T(4,128)(2,1)S(1)}, u32[]{:S(2)}, u32[]{:S(2)}) collective-permute-start(bf16[2,2,4,1024]{3,2,1,0:T(4,128)(2,1)S(1)} %merge.1.refs_0_.refs_7_), channel_id=1, source_target_pairs={{0,8},{4,12},{8,0},{12,4},{1,9},{5,13},{9,1},{13,5},{2,10},{6,14},... | collective-permute-start | bytes 98312 | tf_op jit(solution)/shard_map/ppermute | solution.py:35
  17.3 0.1 collective-permute-start.6
  17.3 2.3 %pack.1 = (bf16[4,256,512]{2,1,0:T(8,128)(2,1)S(1)}, bf16[4,256,512]{2,1,0:T(8,128)(2,1)S(1)}) custom-call(s32[32]{0:T(128)} %bitcast.6, bf16[8,2,256,512]{3,2,1,0:T(8,128)(2,1)} %cache_ref.5, bf16[2,2,4,1024]{3,2,1,0:T(4,128)(2,1)S(1)} %merge.1.refs_0_.refs_7_, bf16[2,4,4096]{2,1,0:T(4,128)(2,1)S(1)} %collective-permute-done.3.refs_1_.refs_6_), custom_call_target="tpu_custom_call" | custom-call | flops 10000000000 | bytes 4194304 | tf_op jit(solution)/shard_map/pack/pallas_call | solution.py:203
  19.7 0.2 collective-permute-start.10
  19.9 0.3 collective-permute-done.5.refs_9_
  20.2 2.7 %collective-permute-done.6.refs_10_ = bf16[2,2,4,1024]{3,2,1,0:T(4,128)(2,1)S(1)} collective-permute-done((bf16[2,2,4,1024]{3,2,1,0:T(4,128)(2,1)S(1)}, bf16[2,2,4,1024]{3,2,1,0:T(4,128)(2,1)S(1)}, u32[]{:S(2)}, u32[]{:S(2)}) %collective-permute-start.6) | collective-permute-done | bytes 32800 | tf_op jit(solution)/shard_map/ppermute | solution.py:35
  23.0 4.7 %attend.1 = (bf16[272,128]{1,0:T(8,128)(2,1)S(1)}, bf16[272,128]{1,0:T(8,128)(2,1)S(1)}, bf16[272,128]{1,0:T(8,128)(2,1)S(1)}, bf16[272,128]{1,0:T(8,128)(2,1)S(1)}) custom-call(s32[32]{0:T(128)S(1)} %bitcast.7, s32[32]{0:T(128)S(1)} %copy-done.3, bf16[1,256,512]{2,1,0:T(8,128)(2,1)S(1)} %pack_head.1.refs_0_, ...), custom_call_target="tpu_custom_call" | custom-call | flops 20000000000 | bytes 4194304 | tf_op jit(solution)/shard_map/attend/pallas_call | solution.py:333
  27.7 0.1 collective-permute-start.7
  27.8 1.2 %collective-permute-start.8 = (bf16[272,128]{1,0:T(8,128)(2,1)S(1)}, bf16[272,128]{1,0:T(8,128)(2,1)S(1)}, u32[]{:S(2)}, u32[]{:S(2)}) collective-permute-start(bf16[272,128]{1,0:T(8,128)(2,1)S(1)} %get-tuple-element.24), channel_id=1, source_target_pairs={{0,8},{4,12},{8,0},{12,4},{1,9},{5,13},{9,1},{13,5},{2,10},{6,14},... | collective-permute-start | bytes 208904 | tf_op jit(solution)/shard_map/ppermute | solution.py:35
  29.0 3.1 %collective-permute-start.9 = (bf16[272,128]{1,0:T(8,128)(2,1)S(1)}, bf16[272,128]{1,0:T(8,128)(2,1)S(1)}, u32[]{:S(2)}, u32[]{:S(2)}) collective-permute-start(bf16[272,128]{1,0:T(8,128)(2,1)S(1)} %get-tuple-element.25), channel_id=1, source_target_pairs={{0,12},{4,8},{8,4},{12,0},{1,13},{5,9},{9,5},{13,1},{2,14},{6,10},... | collective-permute-start | bytes 208904 | tf_op jit(solution)/shard_map/ppermute | solution.py:35
  32.1 3.5 %fetch.2.refs_4_ = bf16[2048,2048]{1,0:T(8,128)(2,1)S(1)} custom-call(bf16[4096,2048]{1,0:T(8,128)(2,1)} %weight_ref.3, bf16[272,128]{1,0:T(8,128)(2,1)S(1)} %get-tuple-element.22.refs_0_, bf16[4,256,512]{2,1,0:T(8,128)(2,1)S(1)} %collective-permute-done.10.refs_1_), custom_call_target="tpu_custom_call" | custom-call | bytes 16777216 | tf_op jit(solution)/shard_map/fetch/pallas_call | solution.py:426
  35.6 0.1 collective-permute-done.8.refs_2_
  35.7 0.4 join.1.refs_0_
  36.1 2.8 %copy-done = bf16[2048,2048]{1,0:T(8,128)(2,1)} copy-done((bf16[2048,2048]{1,0:T(8,128)(2,1)}, bf16[2048,2048]{1,0:T(8,128)(2,1)S(1)}, u32[]{:S(2)}) %copy-start) | copy-done | bytes 8388632
  38.9 1.2 %collective-permute-start.12 = (bf16[8,4096]{1,0:T(8,128)(2,1)S(1)}, bf16[8,4096]{1,0:T(8,128)(2,1)S(1)}, u32[]{:S(2)}, u32[]{:S(2)}) collective-permute-start(bf16[8,4096]{1,0:T(8,128)(2,1)S(1)} %join.1.refs_0_), channel_id=1, source_target_pairs={{0,8},{4,12},{8,0},{12,4},{1,9},{5,13},{9,1},{13,5},{2,10},{6,14},... | collective-permute-start | bytes 196616 | tf_op jit(solution)/shard_map/ppermute | solution.py:35
  40.1 3.1 %collective-permute-start.13 = (bf16[8,4096]{1,0:T(8,128)(2,1)S(1)}, bf16[8,4096]{1,0:T(8,128)(2,1)S(1)}, u32[]{:S(2)}, u32[]{:S(2)}) collective-permute-start(bf16[8,4096]{1,0:T(8,128)(2,1)S(1)} %join.1.refs_0_), channel_id=1, source_target_pairs={{0,12},{4,8},{8,4},{12,0},{1,13},{5,9},{9,5},{13,1},{2,14},{6,10},... | collective-permute-start | bytes 196616 | tf_op jit(solution)/shard_map/ppermute | solution.py:35
  43.3 3.5 %fetch.3.refs_5_ = bf16[2048,2048]{1,0:T(8,128)(2,1)S(1)} custom-call(bf16[4096,2048]{1,0:T(8,128)(2,1)} %weight_ref.3, bf16[8,4096]{1,0:T(8,128)(2,1)S(1)} %join.1.refs_0_), custom_call_target="tpu_custom_call" | custom-call | bytes 16777216 | tf_op jit(solution)/shard_map/fetch/pallas_call | solution.py:426
  46.7 1.5 %place.2.refs_0_ = bf16[1,16,256,512]{3,2,1,0:T(8,128)(2,1)} custom-call(bf16[4,256,512]{2,1,0:T(8,128)(2,1)S(1)} %get-tuple-element.19.refs_3_.refs_0_, bf16[4,256,512]{2,1,0:T(8,128)(2,1)S(1)} %collective-permute-done.10.refs_1_, bf16[1,256,512]{2,1,0:T(8,128)(2,1)S(1)} %collective-permute-done.2.refs_2_), custom_call_target="tpu_custom_call" | custom-call | bytes 4718592 | tf_op jit(solution)/shard_map/place/pallas_call | solution.py:233
  48.3 3.4 %copy-done.1 = bf16[2048,2048]{1,0:T(8,128)(2,1)S(1)} copy-done((bf16[2048,2048]{1,0:T(8,128)(2,1)S(1)}, bf16[2048,2048]{1,0:T(8,128)(2,1)}, u32[]{:S(2)}) %copy-start.1) | copy-done | bytes 8388632
  51.6 3.6 %project.1.refs_1_ = bf16[8,4,2048]{2,1,0:T(4,128)(2,1)} custom-call(bf16[8,4096]{1,0:T(8,128)(2,1)S(1)} %join.1.refs_0_, bf16[8,4096]{1,0:T(8,128)(2,1)S(1)} %collective-permute-done.11.refs_1_, bf16[8,4096]{1,0:T(8,128)(2,1)S(1)} %collective-permute-done.12.refs_2_, bf16[8,4096]{1,0:T(8,128)(2,1)S(1)} %collective-permute-done.13.refs_3_, ...), custom_call_target="tpu_custom_call" | custom-call | flops 536870912 | bytes 16777216 | tf_op jit(solution)/shard_map/project/pallas_call | solution.py:469
  55.3 0.9 %place.3 = bf16[1,16,256,512]{3,2,1,0:T(8,128)(2,1)} custom-call(bf16[1,16,256,512]{3,2,1,0:T(8,128)(2,1)} %place.2.refs_0_, bf16[8,4,2048]{2,1,0:T(4,128)(2,1)} %project.1.refs_1_, bf16[3,256,512]{2,1,0:T(8,128)(2,1)S(1)} %collective-permute-done.14.refs_2_), custom_call_target="tpu_custom_call", output_to_operand_aliasing={{}: (0, {})} | custom-call | bytes 1572864 | tf_op jit(solution)/shard_map/place/pallas_call | solution.py:233
  56.2 2.3 %bitcast_dynamic-update-slice_fusion = bf16[1,16,256,512]{3,2,1,0:T(8,128)(2,1)} fusion(bf16[1,16,256,512]{3,2,1,0:T(8,128)(2,1)} %place.3, s32[]{:T(128)S(6)} %select_n.3, bf16[4,256,512]{2,1,0:T(8,128)(2,1)} %collective-permute-done.15), kind=kLoop, calls=%fused_computation | loop fusion | bytes 2097156 | tf_op jit(solution)/shard_map/dynamic_update_slice | solution.py:526
  (20 shorter events, 0.1 us)
Async XLA Ops:
  2.2 10.6 %collective-permute-start.2 = (bf16[1,256,512]{2,1,0:T(8,128)(2,1)S(1)}, bf16[1,256,512]{2,1,0:T(8,128)(2,1)S(1)}, u32[]{:S(2)}, u32[]{:S(2)}) collective-permute-start(bf16[1,256,512]{2,1,0:T(8,128)(2,1)S(1)} %pack_head.1.refs_0_), channel_id=1, source_target_pairs={{0,2},{1,3},{2,0},{3,1},{4,6},{5,7},{6,4},{7,5},{8,10},{9,11},{10,... | collective-permute-start | bytes 786440 | tf_op jit(solution)/shard_map/ppermute | solution.py:35
  9.0 8.3 %collective-permute-start.3 = (bf16[2,4,4096]{2,1,0:T(4,128)(2,1)S(1)}, bf16[2,4,4096]{2,1,0:T(4,128)(2,1)S(1)}, u32[]{:S(2)}, u32[]{:S(2)}) collective-permute-start(bf16[2,4,4096]{2,1,0:T(4,128)(2,1)S(1)} %get-tuple-element.18), channel_id=1, source_target_pairs={{0,1},{1,0},{2,3},{3,2},{4,5},{5,4},{6,7},{7,6},{8,9},{9,8},{10,11... | collective-permute-start | bytes 196616 | tf_op jit(solution)/shard_map/ppermute | solution.py:35
  9.0 3.8 %collective-permute-start = (bf16[2,4,1024]{2,1,0:T(4,128)(2,1)S(1)}, bf16[2,4,1024]{2,1,0:T(4,128)(2,1)S(1)}, u32[]{:S(2)}, u32[]{:S(2)}) collective-permute-start(bf16[2,4,1024]{2,1,0:T(4,128)(2,1)S(1)} %get-tuple-element.16), channel_id=1, source_target_pairs={{0,2},{1,3},{2,0},{3,1},{4,6},{5,7},{6,4},{7,5},{8,10},{9,11},{10,... | collective-permute-start | bytes 49160 | tf_op jit(solution)/shard_map/ppermute | solution.py:35
  9.1 3.7 %collective-permute-start.1 = (bf16[2,4,1024]{2,1,0:T(4,128)(2,1)S(1)}, bf16[2,4,1024]{2,1,0:T(4,128)(2,1)S(1)}, u32[]{:S(2)}, u32[]{:S(2)}) collective-permute-start(bf16[2,4,1024]{2,1,0:T(4,128)(2,1)S(1)} %get-tuple-element.17), channel_id=1, source_target_pairs={{0,3},{1,2},{2,1},{3,0},{4,7},{5,6},{6,5},{7,4},{8,11},{9,10},{10,... | collective-permute-start | bytes 49160 | tf_op jit(solution)/shard_map/ppermute | solution.py:35
  10.9 44.4 %collective-permute-start.14 = (bf16[3,256,512]{2,1,0:T(8,128)(2,1)}, bf16[3,256,512]{2,1,0:T(8,128)(2,1)S(1)}, u32[]{:S(2)}, u32[]{:S(2)}) collective-permute-start(bf16[3,256,512]{2,1,0:T(8,128)(2,1)} %get-tuple-element.14.refs_1_), channel_id=1, source_target_pairs={{0,2},{1,3},{2,0},{3,1},{4,6},{5,7},{6,4},{7,5},{8,10},{9,11},{10,... | collective-permute-start | bytes 2359304 | tf_op jit(solution)/shard_map/ppermute | solution.py:35
  12.8 43.4 %collective-permute-start.15 = (bf16[4,256,512]{2,1,0:T(8,128)(2,1)}, bf16[4,256,512]{2,1,0:T(8,128)(2,1)}, u32[]{:S(2)}, u32[]{:S(2)}) collective-permute-start(bf16[4,256,512]{2,1,0:T(8,128)(2,1)} %get-tuple-element.15.refs_2_), channel_id=1, source_target_pairs={{0,3},{1,2},{2,1},{3,0},{4,7},{5,6},{6,5},{7,4},{8,11},{9,10},{10,... | collective-permute-start | bytes 3145736 | tf_op jit(solution)/shard_map/ppermute | solution.py:35
  12.9 10.1 %copy-start.2 = (s32[32,1]{0,1:T(1,128)S(1)}, s32[32,1]{0,1:T(1,128)}, u32[]{:S(2)}) copy-start(s32[32,1]{0,1:T(1,128)} %param.7) | copy-start | bytes 388
  12.9 10.1 %copy-start.3 = (s32[32]{0:T(128)S(1)}, s32[32]{0:T(128)}, u32[]{:S(2)}) copy-start(s32[32]{0:T(128)} %lengths_ref.1) | copy-start | bytes 388
  12.9 6.8 %collective-permute-start.4 = (bf16[2,2,4,1024]{3,2,1,0:T(4,128)(2,1)S(1)}, bf16[2,2,4,1024]{3,2,1,0:T(4,128)(2,1)S(1)}, u32[]{:S(2)}, u32[]{:S(2)}) collective-permute-start(bf16[2,2,4,1024]{3,2,1,0:T(4,128)(2,1)S(1)} %merge.1.refs_0_.refs_7_), channel_id=1, source_target_pairs={{0,4},{4,0},{8,12},{12,8},{1,5},{5,1},{9,13},{13,9},{2,6},{6,2},{1... | collective-permute-start | bytes 98312 | tf_op jit(solution)/shard_map/ppermute | solution.py:35
  14.7 5.6 %collective-permute-start.5 = (bf16[2,2,4,1024]{3,2,1,0:T(4,128)(2,1)S(1)}, bf16[2,2,4,1024]{3,2,1,0:T(4,128)(2,1)S(1)}, u32[]{:S(2)}, u32[]{:S(2)}) collective-permute-start(bf16[2,2,4,1024]{3,2,1,0:T(4,128)(2,1)S(1)} %merge.1.refs_0_.refs_7_), channel_id=1, source_target_pairs={{0,8},{4,12},{8,0},{12,4},{1,9},{5,13},{9,1},{13,5},{2,10},{6,14},... | collective-permute-start | bytes 98312 | tf_op jit(solution)/shard_map/ppermute | solution.py:35
  17.3 5.7 %collective-permute-start.6 = (bf16[2,2,4,1024]{3,2,1,0:T(4,128)(2,1)S(1)}, bf16[2,2,4,1024]{3,2,1,0:T(4,128)(2,1)S(1)}, u32[]{:S(2)}, u32[]{:S(2)}) collective-permute-start(bf16[2,2,4,1024]{3,2,1,0:T(4,128)(2,1)S(1)} %merge.1.refs_0_.refs_7_), channel_id=1, source_target_pairs={{0,12},{4,8},{8,4},{12,0},{1,13},{5,9},{9,5},{13,1},{2,14},{6,10},... | collective-permute-start | bytes 98312 | tf_op jit(solution)/shard_map/ppermute | solution.py:35
  19.7 9.3 %collective-permute-start.10 = (bf16[4,256,512]{2,1,0:T(8,128)(2,1)S(1)}, bf16[4,256,512]{2,1,0:T(8,128)(2,1)S(1)}, u32[]{:S(2)}, u32[]{:S(2)}) collective-permute-start(bf16[4,256,512]{2,1,0:T(8,128)(2,1)S(1)} %get-tuple-element.20.refs_4_), channel_id=1, source_target_pairs={{0,1},{1,0},{2,3},{3,2},{4,5},{5,4},{6,7},{7,6},{8,9},{9,8},{10,11... | collective-permute-start | bytes 3145736 | tf_op jit(solution)/shard_map/ppermute | solution.py:35
  27.7 7.9 %collective-permute-start.7 = (bf16[272,128]{1,0:T(8,128)(2,1)S(1)}, bf16[272,128]{1,0:T(8,128)(2,1)S(1)}, u32[]{:S(2)}, u32[]{:S(2)}) collective-permute-start(bf16[272,128]{1,0:T(8,128)(2,1)S(1)} %get-tuple-element.23), channel_id=1, source_target_pairs={{0,4},{4,0},{8,12},{12,8},{1,5},{5,1},{9,13},{13,9},{2,6},{6,2},{1... | collective-permute-start | bytes 208904 | tf_op jit(solution)/shard_map/ppermute | solution.py:35
  27.8 7.9 %collective-permute-start.8 = (bf16[272,128]{1,0:T(8,128)(2,1)S(1)}, bf16[272,128]{1,0:T(8,128)(2,1)S(1)}, u32[]{:S(2)}, u32[]{:S(2)}) collective-permute-start(bf16[272,128]{1,0:T(8,128)(2,1)S(1)} %get-tuple-element.24), channel_id=1, source_target_pairs={{0,8},{4,12},{8,0},{12,4},{1,9},{5,13},{9,1},{13,5},{2,10},{6,14},... | collective-permute-start | bytes 208904 | tf_op jit(solution)/shard_map/ppermute | solution.py:35
  29.0 6.7 %collective-permute-start.9 = (bf16[272,128]{1,0:T(8,128)(2,1)S(1)}, bf16[272,128]{1,0:T(8,128)(2,1)S(1)}, u32[]{:S(2)}, u32[]{:S(2)}) collective-permute-start(bf16[272,128]{1,0:T(8,128)(2,1)S(1)} %get-tuple-element.25), channel_id=1, source_target_pairs={{0,12},{4,8},{8,4},{12,0},{1,13},{5,9},{9,5},{13,1},{2,14},{6,10},... | collective-permute-start | bytes 208904 | tf_op jit(solution)/shard_map/ppermute | solution.py:35
  35.6 3.3 %copy-start = (bf16[2048,2048]{1,0:T(8,128)(2,1)}, bf16[2048,2048]{1,0:T(8,128)(2,1)S(1)}, u32[]{:S(2)}) copy-start(bf16[2048,2048]{1,0:T(8,128)(2,1)S(1)} %fetch.2.refs_4_) | copy-start | bytes 25165828
  38.9 9.4 %collective-permute-start.11 = (bf16[8,4096]{1,0:T(8,128)(2,1)S(1)}, bf16[8,4096]{1,0:T(8,128)(2,1)S(1)}, u32[]{:S(2)}, u32[]{:S(2)}) collective-permute-start(bf16[8,4096]{1,0:T(8,128)(2,1)S(1)} %join.1.refs_0_), channel_id=1, source_target_pairs={{0,4},{4,0},{8,12},{12,8},{1,5},{5,1},{9,13},{13,9},{2,6},{6,2},{1... | collective-permute-start | bytes 196616 | tf_op jit(solution)/shard_map/ppermute | solution.py:35
  38.9 9.4 %collective-permute-start.12 = (bf16[8,4096]{1,0:T(8,128)(2,1)S(1)}, bf16[8,4096]{1,0:T(8,128)(2,1)S(1)}, u32[]{:S(2)}, u32[]{:S(2)}) collective-permute-start(bf16[8,4096]{1,0:T(8,128)(2,1)S(1)} %join.1.refs_0_), channel_id=1, source_target_pairs={{0,8},{4,12},{8,0},{12,4},{1,9},{5,13},{9,1},{13,5},{2,10},{6,14},... | collective-permute-start | bytes 196616 | tf_op jit(solution)/shard_map/ppermute | solution.py:35
  40.1 8.1 %collective-permute-start.13 = (bf16[8,4096]{1,0:T(8,128)(2,1)S(1)}, bf16[8,4096]{1,0:T(8,128)(2,1)S(1)}, u32[]{:S(2)}, u32[]{:S(2)}) collective-permute-start(bf16[8,4096]{1,0:T(8,128)(2,1)S(1)} %join.1.refs_0_), channel_id=1, source_target_pairs={{0,12},{4,8},{8,4},{12,0},{1,13},{5,9},{9,5},{13,1},{2,14},{6,10},... | collective-permute-start | bytes 196616 | tf_op jit(solution)/shard_map/ppermute | solution.py:35
  48.3 3.4 %copy-start.1 = (bf16[2048,2048]{1,0:T(8,128)(2,1)S(1)}, bf16[2048,2048]{1,0:T(8,128)(2,1)}, u32[]{:S(2)}) copy-start(bf16[2048,2048]{1,0:T(8,128)(2,1)} %copy-done) | copy-start | bytes 25165828

commit v14 on v12

--- a/solution.py
+++ b/solution.py
@@ -98,7 +98,26 @@
     return finish
 
 
-def head_kernel(piece, full, routing_ref, cache_ref, out_ref, routed, held, routing_sem, sem):
+def start_queries(query_ref, out_refs, offsets, sem):
+    section = lax.axis_index("sec")
+    copies = []
+    for n, (offset, out_ref) in enumerate(zip(offsets, out_refs)):
+        width = out_ref.shape[2]
+        columns = pl.ds(pl.multiple_of(lax.axis_index("tp") * width, width) if offset > 1 else 0, width)
+        part = query_ref.at[0, pl.ds((section ^ offset) * CAP, CAP), :, columns]
+        copies.append(pltpu.make_async_copy(part, out_ref, sem.at[n]))
+        copies[-1].start()
+    return copies
+
+
+def query_shapes(queries, offsets, tp_count):
+    samples, width = queries.shape[2:]
+    widths = [width if offset < 2 else width // tp_count for offset in offsets]
+    return [jax.ShapeDtypeStruct((CAP, samples, one), queries.dtype) for one in widths]
+
+
+def head_kernel(piece, offsets, full, routing_ref, cache_ref, query_ref, *refs):
+    out_ref, query_out, (routed, held, routing_sem, sem, query_sem) = refs[0], refs[1:-5], refs[-5:]
     offset, half, _ = piece
     section = lax.axis_index("sec")
     copies = [pltpu.make_async_copy(routing_ref, routed, routing_sem)]
@@ -106,46 +125,43 @@
         copies.append(pltpu.make_async_copy(cache_ref.at[i, half % 2], held.at[i], sem.at[i]))
     for copy in copies:
         copy.start()
+    query_copies = start_queries(query_ref, query_out, offsets, query_sem)
     copies[0].wait()
     row, filled = slot_row(own_targets(routed, section), section ^ offset, half // 2)
-    for copy in copies[1:]:
+    for copy in copies[1:] + query_copies:
         copy.wait()
     chosen = held[row]
     out_ref[0] = chosen if full else jnp.where(filled, chosen, jnp.zeros_like(chosen))
 
 
-def pack_head(routing, cache, piece, section_count):
+def pack_head(routing, cache, queries, piece, section_count, tp_count):
     shape = cache.shape[2:]
-    return pl.pallas_call(
-        functools.partial(head_kernel, piece, section_count * CAP == REQ_GRP),
-        out_shape=jax.ShapeDtypeStruct((1,) + shape, cache.dtype),
-        in_specs=[HBM, HBM],
-        out_specs=VMEM,
+    offsets = range(2, section_count)
+    shapes = [jax.ShapeDtypeStruct((1,) + shape, cache.dtype)] + query_shapes(queries, offsets, tp_count)
+    head, *parts = pl.pallas_call(
+        functools.partial(head_kernel, piece, offsets, section_count * CAP == REQ_GRP),
+        out_shape=shapes,
+        in_specs=[HBM, HBM, HBM],
+        out_specs=[VMEM] * len(shapes),
         scratch_shapes=[
             pltpu.SMEM(routing.shape, jnp.int32),
             pltpu.VMEM((REQ_GRP,) + shape, cache.dtype),
             pltpu.SemaphoreType.DMA,
             pltpu.SemaphoreType.DMA((REQ_GRP,)),
+            pltpu.SemaphoreType.DMA((section_count,)),
         ],
         compiler_params=limit(16),
         cost_estimate=cost(0, cache.size),
         name="pack_head",
-    )(in_hbm(routing), in_hbm(cache))
+    )(in_hbm(routing), in_hbm(cache), in_hbm(queries))
+    return [head], parts
 
 
 def first_pack_kernel(pieces, section_count, routing_ref, cache_ref, query_ref, *refs):
     refs, (sem, query_sem) = refs[:-2], refs[-2:]
-    query_out, cache_out = refs[-section_count:], refs[-section_count - len(pieces) : -section_count]
-    section = lax.axis_index("sec")
-    query_copies = []
-    for offset, out_ref in enumerate(query_out):
-        width = out_ref.shape[2]
-        columns = pl.ds(pl.multiple_of(lax.axis_index("tp") * width, width) if offset > 1 else 0, width)
-        part = query_ref.at[0, pl.ds((section ^ offset) * CAP, CAP), :, columns]
-        query_copies.append(pltpu.make_async_copy(part, out_ref, query_sem.at[offset]))
-        query_copies[-1].start()
-    finish = start_packing(pieces, section_count, routing_ref, cache_ref, cache_out, sem)
-    finish()
+    query_out, cache_out = refs[-2:], refs[-2 - len(pieces) : -2]
+    query_copies = start_queries(query_ref, query_out, range(2), query_sem)
+    start_packing(pieces, section_count, routing_ref, cache_ref, cache_out, sem)()
     for copy in query_copies:
         copy.wait()
 
@@ -168,7 +184,7 @@
         in_specs=[VMEM] * len(parts) + [ANY] * len(others),
         out_specs=VMEM,
         compiler_params=limit(8),
-        cost_estimate=cost(0, 8 * len(parts) * parts[0].size),
+        cost_estimate=cost(3 * 10**9, 8 * len(parts) * parts[0].size),
         name="merge",
     )(*parts, *others)
 
@@ -177,11 +193,9 @@
     return pltpu.with_memory_space_constraint(value, pltpu.HBM)
 
 
-def first_pack(routing, cache, queries, others, pieces, section_count, tp_count):
-    samples, width = queries.shape[2:]
-    widths = [width if offset < 2 else width // tp_count for offset in range(section_count)]
+def first_pack(routing, cache, queries, others, pieces, section_count):
     shapes = [jax.ShapeDtypeStruct((count,) + cache.shape[2:], cache.dtype) for _, _, count in pieces]
-    shapes += [jax.ShapeDtypeStruct((CAP, samples, one), queries.dtype) for one in widths]
+    shapes += query_shapes(queries, range(2), 1)
     parts = pl.pallas_call(
         functools.partial(first_pack_kernel, pieces, section_count),
         out_shape=shapes,
@@ -189,12 +203,12 @@
         out_specs=[VMEM] * len(shapes),
         scratch_shapes=[
             pltpu.SemaphoreType.DMA((section_count * CAP * 2,)),
-            pltpu.SemaphoreType.DMA((section_count,)),
+            pltpu.SemaphoreType.DMA((2,)),
         ],
         compiler_params=limit(16),
         cost_estimate=cost(0, 4 * sum(shape.size for shape in shapes)),
         name="first_pack",
-    )(in_hbm(routing), in_hbm(cache), in_hbm(queries), *others)
+    )(routing, in_hbm(cache), in_hbm(queries), *others)
     return parts[: len(pieces)], parts[len(pieces) :]
 
 
@@ -211,7 +225,7 @@
         compiler_params=limit(16),
         cost_estimate=cost(flops, 4 * sum(shape.size for shape in shapes)),
         name="pack",
-    )(in_hbm(routing), in_hbm(cache), *others)
+    )(routing, in_hbm(cache), *others)
 
 
 def place_kernel(pieces, *refs):
@@ -491,20 +505,23 @@
     def across(parts, pieces):
         return [swap(part, "sec", piece[0]) for part, piece in zip(parts, pieces)]
 
-    head_caches = [pack_head(routing, prompt_key_values, head[0], section_count)]
+    head_caches, far_queries = pack_head(
+        routing, prompt_key_values, queries, head[0], section_count, tp_count
+    )
     head_parts = across(head_caches, head)
+    far_queries = [swap(part, "sec", n + 2) for n, part in enumerate(far_queries)]
     far_caches, query_parts = first_pack(
-        routing, prompt_key_values, queries, head_caches, far, section_count, tp_count
+        routing, prompt_key_values, queries, head_caches, far, section_count
     )
+    far_parts = across(far_caches, far)
     query_parts = [swap(part, "sec", offset) for offset, part in enumerate(query_parts)]
-    far_parts = across(far_caches, far)
-    merged = merge(query_parts[2:], head_parts)
+    merged = merge(far_queries, head_parts)
     far_queries = spread(merged, "tp")
     near_caches = pack(routing, prompt_key_values, [merged, query_parts[1]], near, section_count, 10**10)
     near_parts = across(near_caches, near)
     caches, pieces = [*head_caches, *far_caches, *near_caches], head + far + near
 
-    messages = attend(routing, lengths, caches, pieces, query_parts[:2], far_queries)
+    messages = attend(routing, lengths, caches, pieces, query_parts, far_queries)
     partials = [swap(part, "tp", offset) for offset, part in enumerate(messages)]
     held_weight = [fetch(out_weight, [messages[0], *near_parts[1:]], 0, 2)]
     share = join(partials, held_weight, samples, query_width // HEAD_SIZE // KEY_VALUE_HEADS)

time: 52.5 us -> 52.3 us (level)
  transfers between devices with their start and end apart: 16 -> 16, of which waited for: 5 -> 6; matrix products, arithmetic and copies ran while one was open for 0% -> 0% of each run, Pallas kernels for 42% -> 41%
where the time goes in v14:
time: 52.3 us; the launch traced here: 51.9 us
  Pallas kernels  24.2 us (46%)
  starting transfers between devices  20.1 us (38%)
  waiting for transfers between devices  6.82 us (13%)
  between operations  0.76 us (1%)
    ppermute x16, starting transfers between devices, swap(): return lax.ppermute(value, axis, [(i, i ^ offset) for i in range(count)])  20.1 us
    pallas_call x2, Pallas kernels, fetch(): pl.pallas_call(functools.partial(fetch_kernel, number * size), out_shape=...  6.94 us
    ppermute x16, waiting for transfers between devices, swap(): return lax.ppermute(value, axis, [(i, i ^ offset) for i in range(count)])  6.82 us
    pallas_call x1, Pallas kernels, attend(): pl.pallas_call(functools.partial(attend_kernel, pieces, section_count, tp...  3.76 us
    pallas_call x1, Pallas kernels, project(): pl.pallas_call(functools.partial(project_kernel, count, min(256, width)),...  3.64 us
    pallas_call x3, Pallas kernels, place(): pl.pallas_call(functools.partial(place_kernel, pieces), out_shape=jax.Sha...  3.37 us
    pallas_call x1, Pallas kernels, pack(): pl.pallas_call(functools.partial(pack_kernel, pieces, section_count), out...  2.22 us
    pallas_call x1, Pallas kernels, first_pack(): pl.pallas_call(functools.partial(first_pack_kernel, pieces, section_count...  2.2 us
  transfers between devices with their start and end apart: 16, of which 6 were waited for; matrix products, arithmetic and copies ran while one was open for 0% of the time, Pallas kernels for 41%

profile of v14, /device:TPU:0, one launch (start us, length us, event | category | flops | bytes accessed | tf_op | source)
XLA Modules:
  0.0 51.9 jit_solution(6090684918938669121)
XLA Ops:
  0.6 1.7 %pack_head.1 = (bf16[1,256,512]{2,1,0:T(8,128)(2,1)S(1)}, bf16[2,4,1024]{2,1,0:T(4,128)(2,1)S(1)}, bf16[2,4,1024]{2,1,0:T(4,128)(2,1)S(1)}) custom-call(s32[32]{0:T(128)} %bitcast.2, bf16[8,2,256,512]{3,2,1,0:T(8,128)(2,1)} %cache_ref.5, bf16[1,8,4,4096]{3,2,1,0:T(4,128)(2,1)} %query_ref.3), custom_call_target="tpu_custom_call" | custom-call | bytes 2097152 | tf_op jit(solution)/shard_map/pack_head/pallas_call | solution.py:141
  2.3 3.0 %collective-permute-start.2 = (bf16[1,256,512]{2,1,0:T(8,128)(2,1)S(1)}, bf16[1,256,512]{2,1,0:T(8,128)(2,1)S(1)}, u32[]{:S(2)}, u32[]{:S(2)}) collective-permute-start(bf16[1,256,512]{2,1,0:T(8,128)(2,1)S(1)} %get-tuple-element.15.refs_0_), channel_id=1, source_target_pairs={{0,2},{1,3},{2,0},{3,1},{4,6},{5,7},{6,4},{7,5},{8,10},{9,11},{10,... | collective-permute-start | bytes 786440 | tf_op jit(solution)/shard_map/ppermute | solution.py:35
  5.3 0.1 collective-permute-start
  5.4 0.8 %collective-permute-start.1 = (bf16[2,4,1024]{2,1,0:T(4,128)(2,1)S(1)}, bf16[2,4,1024]{2,1,0:T(4,128)(2,1)S(1)}, u32[]{:S(2)}, u32[]{:S(2)}) collective-permute-start(bf16[2,4,1024]{2,1,0:T(4,128)(2,1)S(1)} %get-tuple-element.19), channel_id=1, source_target_pairs={{0,3},{1,2},{2,1},{3,0},{4,7},{5,6},{6,5},{7,4},{8,11},{9,10},{10,... | collective-permute-start | bytes 49160 | tf_op jit(solution)/shard_map/ppermute | solution.py:35
  6.2 2.2 %first_pack.1 = (bf16[3,256,512]{2,1,0:T(8,128)(2,1)S(1)}, bf16[4,256,512]{2,1,0:T(8,128)(2,1)S(1)}, bf16[2,4,4096]{2,1,0:T(4,128)(2,1)S(1)}, bf16[2,4,4096]{2,1,0:T(4,128)(2,1)S(1)}) custom-call(s32[32]{0:T(128)S(1)} %bitcast.3, bf16[8,2,256,512]{3,2,1,0:T(8,128)(2,1)} %cache_ref.5, bf16[1,8,4,4096]{3,2,1,0:T(4,128)(2,1)} %query_ref.3, ...), custom_call_target="tpu_custom_call" | custom-call | bytes 3932160 | tf_op jit(solution)/shard_map/first_pack/pallas_call | solution.py:199
  8.4 1.3 %collective-permute-start.3 = (bf16[2,4,4096]{2,1,0:T(4,128)(2,1)S(1)}, bf16[2,4,4096]{2,1,0:T(4,128)(2,1)S(1)}, u32[]{:S(2)}, u32[]{:S(2)}) collective-permute-start(bf16[2,4,4096]{2,1,0:T(4,128)(2,1)S(1)} %get-tuple-element.20), channel_id=1, source_target_pairs={{0,1},{1,0},{2,3},{3,2},{4,5},{5,4},{6,7},{7,6},{8,9},{9,8},{10,11... | collective-permute-start | bytes 196616 | tf_op jit(solution)/shard_map/ppermute | solution.py:35
  9.7 0.1 collective-permute-start.14
  9.8 2.6 %collective-permute-done.refs_0_ = bf16[2,4,1024]{2,1,0:T(4,128)(2,1)S(1)} collective-permute-done((bf16[2,4,1024]{2,1,0:T(4,128)(2,1)S(1)}, bf16[2,4,1024]{2,1,0:T(4,128)(2,1)S(1)}, u32[]{:S(2)}, u32[]{:S(2)}) %collective-permute-start) | collective-permute-done | bytes 16416 | tf_op jit(solution)/shard_map/ppermute | solution.py:35
  12.4 0.3 collective-permute-done.1.refs_1_
  12.7 1.5 %collective-permute-start.4 = (bf16[2,2,4,1024]{3,2,1,0:T(4,128)(2,1)S(1)}, bf16[2,2,4,1024]{3,2,1,0:T(4,128)(2,1)S(1)}, u32[]{:S(2)}, u32[]{:S(2)}) collective-permute-start(bf16[2,2,4,1024]{3,2,1,0:T(4,128)(2,1)S(1)} %merge.1.refs_0_.refs_7_), channel_id=1, source_target_pairs={{0,4},{4,0},{8,12},{12,8},{1,5},{5,1},{9,13},{13,9},{2,6},{6,2},{1... | collective-permute-start | bytes 98312 | tf_op jit(solution)/shard_map/ppermute | solution.py:35
  14.3 2.6 %collective-permute-start.5 = (bf16[2,2,4,1024]{3,2,1,0:T(4,128)(2,1)S(1)}, bf16[2,2,4,1024]{3,2,1,0:T(4,128)(2,1)S(1)}, u32[]{:S(2)}, u32[]{:S(2)}) collective-permute-start(bf16[2,2,4,1024]{3,2,1,0:T(4,128)(2,1)S(1)} %merge.1.refs_0_.refs_7_), channel_id=1, source_target_pairs={{0,8},{4,12},{8,0},{12,4},{1,9},{5,13},{9,1},{13,5},{2,10},{6,14},... | collective-permute-start | bytes 98312 | tf_op jit(solution)/shard_map/ppermute | solution.py:35
  16.9 0.3 collective-permute-start.6
  17.2 2.2 %pack.1 = (bf16[4,256,512]{2,1,0:T(8,128)(2,1)S(1)}, bf16[4,256,512]{2,1,0:T(8,128)(2,1)S(1)}) custom-call(s32[32]{0:T(128)S(1)} %bitcast.4, bf16[8,2,256,512]{3,2,1,0:T(8,128)(2,1)} %cache_ref.5, bf16[2,2,4,1024]{3,2,1,0:T(4,128)(2,1)S(1)} %merge.1.refs_0_.refs_7_, bf16[2,4,4096]{2,1,0:T(4,128)(2,1)S(1)} %collective-permute-done.3.refs_1_.refs_6_), custom_call_target="tpu_custom_call" | custom-call | flops 10000000000 | bytes 4194304 | tf_op jit(solution)/shard_map/pack/pallas_call | solution.py:217
  19.4 1.5 %collective-permute-start.10 = (bf16[4,256,512]{2,1,0:T(8,128)(2,1)S(1)}, bf16[4,256,512]{2,1,0:T(8,128)(2,1)S(1)}, u32[]{:S(2)}, u32[]{:S(2)}) collective-permute-start(bf16[4,256,512]{2,1,0:T(8,128)(2,1)S(1)} %get-tuple-element.22.refs_4_), channel_id=1, source_target_pairs={{0,1},{1,0},{2,3},{3,2},{4,5},{5,4},{6,7},{7,6},{8,9},{9,8},{10,11... | collective-permute-start | bytes 3145736 | tf_op jit(solution)/shard_map/ppermute | solution.py:35
  20.9 1.7 %collective-permute-done.6.refs_10_ = bf16[2,2,4,1024]{3,2,1,0:T(4,128)(2,1)S(1)} collective-permute-done((bf16[2,2,4,1024]{3,2,1,0:T(4,128)(2,1)S(1)}, bf16[2,2,4,1024]{3,2,1,0:T(4,128)(2,1)S(1)}, u32[]{:S(2)}, u32[]{:S(2)}) %collective-permute-start.6) | collective-permute-done | bytes 32800 | tf_op jit(solution)/shard_map/ppermute | solution.py:35
  22.6 3.8 %attend.1 = (bf16[272,128]{1,0:T(8,128)(2,1)S(1)}, bf16[272,128]{1,0:T(8,128)(2,1)S(1)}, bf16[272,128]{1,0:T(8,128)(2,1)S(1)}, bf16[272,128]{1,0:T(8,128)(2,1)S(1)}) custom-call(s32[32]{0:T(128)S(1)} %bitcast.5, s32[32]{0:T(128)S(1)} %copy-done.1, bf16[1,256,512]{2,1,0:T(8,128)(2,1)S(1)} %get-tuple-element.15.refs_0_, ...), custom_call_target="tpu_custom_call" | custom-call | flops 20000000000 | bytes 4194304 | tf_op jit(solution)/shard_map/attend/pallas_call | solution.py:347
  26.4 0.1 collective-permute-start.7
  26.4 2.4 %collective-permute-start.8 = (bf16[272,128]{1,0:T(8,128)(2,1)S(1)}, bf16[272,128]{1,0:T(8,128)(2,1)S(1)}, u32[]{:S(2)}, u32[]{:S(2)}) collective-permute-start(bf16[272,128]{1,0:T(8,128)(2,1)S(1)} %get-tuple-element.26), channel_id=1, source_target_pairs={{0,8},{4,12},{8,0},{12,4},{1,9},{5,13},{9,1},{13,5},{2,10},{6,14},... | collective-permute-start | bytes 208904 | tf_op jit(solution)/shard_map/ppermute | solution.py:35
  28.8 2.0 %collective-permute-start.9 = (bf16[272,128]{1,0:T(8,128)(2,1)S(1)}, bf16[272,128]{1,0:T(8,128)(2,1)S(1)}, u32[]{:S(2)}, u32[]{:S(2)}) collective-permute-start(bf16[272,128]{1,0:T(8,128)(2,1)S(1)} %get-tuple-element.27), channel_id=1, source_target_pairs={{0,12},{4,8},{8,4},{12,0},{1,13},{5,9},{9,5},{13,1},{2,14},{6,10},... | collective-permute-start | bytes 208904 | tf_op jit(solution)/shard_map/ppermute | solution.py:35
  30.8 3.5 %fetch.2.refs_4_ = bf16[2048,2048]{1,0:T(8,128)(2,1)S(1)} custom-call(bf16[4096,2048]{1,0:T(8,128)(2,1)} %weight_ref.3, bf16[272,128]{1,0:T(8,128)(2,1)S(1)} %get-tuple-element.24.refs_0_, bf16[4,256,512]{2,1,0:T(8,128)(2,1)S(1)} %collective-permute-done.10.refs_1_), custom_call_target="tpu_custom_call" | custom-call | bytes 16777216 | tf_op jit(solution)/shard_map/fetch/pallas_call | solution.py:440
  34.3 1.1 %collective-permute-done.8.refs_2_ = bf16[272,128]{1,0:T(8,128)(2,1)S(1)} collective-permute-done((bf16[272,128]{1,0:T(8,128)(2,1)S(1)}, bf16[272,128]{1,0:T(8,128)(2,1)S(1)}, u32[]{:S(2)}, u32[]{:S(2)}) %collective-permute-start.8) | collective-permute-done | bytes 69664 | tf_op jit(solution)/shard_map/ppermute | solution.py:35
  35.4 0.4 join.1.refs_0_
  35.8 1.8 %collective-permute-start.11 = (bf16[8,4096]{1,0:T(8,128)(2,1)S(1)}, bf16[8,4096]{1,0:T(8,128)(2,1)S(1)}, u32[]{:S(2)}, u32[]{:S(2)}) collective-permute-start(bf16[8,4096]{1,0:T(8,128)(2,1)S(1)} %join.1.refs_0_), channel_id=1, source_target_pairs={{0,4},{4,0},{8,12},{12,8},{1,5},{5,1},{9,13},{13,9},{2,6},{6,2},{1... | collective-permute-start | bytes 196616 | tf_op jit(solution)/shard_map/ppermute | solution.py:35
  37.6 0.4 collective-permute-start.12
  38.0 2.2 %collective-permute-start.13 = (bf16[8,4096]{1,0:T(8,128)(2,1)S(1)}, bf16[8,4096]{1,0:T(8,128)(2,1)S(1)}, u32[]{:S(2)}, u32[]{:S(2)}) collective-permute-start(bf16[8,4096]{1,0:T(8,128)(2,1)S(1)} %join.1.refs_0_), channel_id=1, source_target_pairs={{0,12},{4,8},{8,4},{12,0},{1,13},{5,9},{9,5},{13,1},{2,14},{6,10},... | collective-permute-start | bytes 196616 | tf_op jit(solution)/shard_map/ppermute | solution.py:35
  40.3 3.5 %fetch.3.refs_5_ = bf16[2048,2048]{1,0:T(8,128)(2,1)S(1)} custom-call(bf16[4096,2048]{1,0:T(8,128)(2,1)} %weight_ref.3, bf16[8,4096]{1,0:T(8,128)(2,1)S(1)} %join.1.refs_0_), custom_call_target="tpu_custom_call" | custom-call | bytes 16777216 | tf_op jit(solution)/shard_map/fetch/pallas_call | solution.py:440
  43.7 1.5 %place.3.refs_0_ = bf16[1,16,256,512]{3,2,1,0:T(8,128)(2,1)} custom-call(bf16[4,256,512]{2,1,0:T(8,128)(2,1)S(1)} %get-tuple-element.21.refs_3_.refs_0_, bf16[4,256,512]{2,1,0:T(8,128)(2,1)S(1)} %collective-permute-done.10.refs_1_, bf16[1,256,512]{2,1,0:T(8,128)(2,1)S(1)} %collective-permute-done.2.refs_2_), custom_call_target="tpu_custom_call" | custom-call | bytes 4718592 | tf_op jit(solution)/shard_map/place/pallas_call | solution.py:247
  45.2 0.1 collective-permute-done.12.refs_2_
  45.3 3.6 %project.1.refs_1_ = bf16[8,4,2048]{2,1,0:T(4,128)(2,1)} custom-call(bf16[8,4096]{1,0:T(8,128)(2,1)S(1)} %join.1.refs_0_, bf16[8,4096]{1,0:T(8,128)(2,1)S(1)} %collective-permute-done.11.refs_1_, bf16[8,4096]{1,0:T(8,128)(2,1)S(1)} %collective-permute-done.12.refs_2_, bf16[8,4096]{1,0:T(8,128)(2,1)S(1)} %collective-permute-done.13.refs_3_, ...), custom_call_target="tpu_custom_call" | custom-call | flops 536870912 | bytes 16777216 | tf_op jit(solution)/shard_map/project/pallas_call | solution.py:483
  49.0 0.9 %place.4.refs_0_ = bf16[1,16,256,512]{3,2,1,0:T(8,128)(2,1)} custom-call(bf16[1,16,256,512]{3,2,1,0:T(8,128)(2,1)} %place.3.refs_0_, bf16[8,4,2048]{2,1,0:T(4,128)(2,1)} %project.1.refs_1_, bf16[3,256,512]{2,1,0:T(8,128)(2,1)S(1)} %collective-permute-done.14.refs_2_), custom_call_target="tpu_custom_call", output_to_operand_aliasing={{}: (0, {})} | custom-call | bytes 1572864 | tf_op jit(solution)/shard_map/place/pallas_call | solution.py:247
  49.9 1.0 %collective-permute-done.15.refs_2_ = bf16[4,256,512]{2,1,0:T(8,128)(2,1)S(1)} collective-permute-done((bf16[4,256,512]{2,1,0:T(8,128)(2,1)S(1)}, bf16[4,256,512]{2,1,0:T(8,128)(2,1)S(1)}, u32[]{:S(2)}, u32[]{:S(2)}) %collective-permute-start.15) | collective-permute-done | bytes 1048608 | tf_op jit(solution)/shard_map/ppermute | solution.py:35
  50.9 1.0 %place.5 = bf16[1,16,256,512]{3,2,1,0:T(8,128)(2,1)} custom-call(bf16[1,16,256,512]{3,2,1,0:T(8,128)(2,1)} %place.4.refs_0_, bf16[8,4,2048]{2,1,0:T(4,128)(2,1)} %project.1.refs_1_, bf16[4,256,512]{2,1,0:T(8,128)(2,1)S(1)} %collective-permute-done.15.refs_2_), custom_call_target="tpu_custom_call", output_to_operand_aliasing={{}: (0, {})} | custom-call | bytes 2097152 | tf_op jit(solution)/shard_map/place/pallas_call | solution.py:247
  (16 shorter events, 0.0 us)
Async XLA Ops:
  0.6 5.6 %copy-start = (s32[32,1]{0,1:T(1,128)S(1)}, s32[32,1]{0,1:T(1,128)}, u32[]{:S(2)}) copy-start(s32[32,1]{0,1:T(1,128)} %param.7) | copy-start | bytes 388
  2.3 10.4 %collective-permute-start.2 = (bf16[1,256,512]{2,1,0:T(8,128)(2,1)S(1)}, bf16[1,256,512]{2,1,0:T(8,128)(2,1)S(1)}, u32[]{:S(2)}, u32[]{:S(2)}) collective-permute-start(bf16[1,256,512]{2,1,0:T(8,128)(2,1)S(1)} %get-tuple-element.15.refs_0_), channel_id=1, source_target_pairs={{0,2},{1,3},{2,0},{3,1},{4,6},{5,7},{6,4},{7,5},{8,10},{9,11},{10,... | collective-permute-start | bytes 786440 | tf_op jit(solution)/shard_map/ppermute | solution.py:35
  5.3 7.1 %collective-permute-start = (bf16[2,4,1024]{2,1,0:T(4,128)(2,1)S(1)}, bf16[2,4,1024]{2,1,0:T(4,128)(2,1)S(1)}, u32[]{:S(2)}, u32[]{:S(2)}) collective-permute-start(bf16[2,4,1024]{2,1,0:T(4,128)(2,1)S(1)} %get-tuple-element.18), channel_id=1, source_target_pairs={{0,2},{1,3},{2,0},{3,1},{4,6},{5,7},{6,4},{7,5},{8,10},{9,11},{10,... | collective-permute-start | bytes 49160 | tf_op jit(solution)/shard_map/ppermute | solution.py:35
  5.4 7.3 %collective-permute-start.1 = (bf16[2,4,1024]{2,1,0:T(4,128)(2,1)S(1)}, bf16[2,4,1024]{2,1,0:T(4,128)(2,1)S(1)}, u32[]{:S(2)}, u32[]{:S(2)}) collective-permute-start(bf16[2,4,1024]{2,1,0:T(4,128)(2,1)S(1)} %get-tuple-element.19), channel_id=1, source_target_pairs={{0,3},{1,2},{2,1},{3,0},{4,7},{5,6},{6,5},{7,4},{8,11},{9,10},{10,... | collective-permute-start | bytes 49160 | tf_op jit(solution)/shard_map/ppermute | solution.py:35
  8.4 8.4 %collective-permute-start.3 = (bf16[2,4,4096]{2,1,0:T(4,128)(2,1)S(1)}, bf16[2,4,4096]{2,1,0:T(4,128)(2,1)S(1)}, u32[]{:S(2)}, u32[]{:S(2)}) collective-permute-start(bf16[2,4,4096]{2,1,0:T(4,128)(2,1)S(1)} %get-tuple-element.20), channel_id=1, source_target_pairs={{0,1},{1,0},{2,3},{3,2},{4,5},{5,4},{6,7},{7,6},{8,9},{9,8},{10,11... | collective-permute-start | bytes 196616 | tf_op jit(solution)/shard_map/ppermute | solution.py:35
  9.7 39.2 %collective-permute-start.14 = (bf16[3,256,512]{2,1,0:T(8,128)(2,1)S(1)}, bf16[3,256,512]{2,1,0:T(8,128)(2,1)S(1)}, u32[]{:S(2)}, u32[]{:S(2)}) collective-permute-start(bf16[3,256,512]{2,1,0:T(8,128)(2,1)S(1)} %get-tuple-element.16.refs_1_), channel_id=1, source_target_pairs={{0,2},{1,3},{2,0},{3,1},{4,6},{5,7},{6,4},{7,5},{8,10},{9,11},{10,... | collective-permute-start | bytes 2359304 | tf_op jit(solution)/shard_map/ppermute | solution.py:35
  12.4 38.5 %collective-permute-start.15 = (bf16[4,256,512]{2,1,0:T(8,128)(2,1)S(1)}, bf16[4,256,512]{2,1,0:T(8,128)(2,1)S(1)}, u32[]{:S(2)}, u32[]{:S(2)}) collective-permute-start(bf16[4,256,512]{2,1,0:T(8,128)(2,1)S(1)} %get-tuple-element.17.refs_2_), channel_id=1, source_target_pairs={{0,3},{1,2},{2,1},{3,0},{4,7},{5,6},{6,5},{7,4},{8,11},{9,10},{10,... | collective-permute-start | bytes 3145736 | tf_op jit(solution)/shard_map/ppermute | solution.py:35
  12.7 9.9 %copy-start.1 = (s32[32]{0:T(128)S(1)}, s32[32]{0:T(128)}, u32[]{:S(2)}) copy-start(s32[32]{0:T(128)} %lengths_ref.1) | copy-start | bytes 388
  12.7 6.7 %collective-permute-start.4 = (bf16[2,2,4,1024]{3,2,1,0:T(4,128)(2,1)S(1)}, bf16[2,2,4,1024]{3,2,1,0:T(4,128)(2,1)S(1)}, u32[]{:S(2)}, u32[]{:S(2)}) collective-permute-start(bf16[2,2,4,1024]{3,2,1,0:T(4,128)(2,1)S(1)} %merge.1.refs_0_.refs_7_), channel_id=1, source_target_pairs={{0,4},{4,0},{8,12},{12,8},{1,5},{5,1},{9,13},{13,9},{2,6},{6,2},{1... | collective-permute-start | bytes 98312 | tf_op jit(solution)/shard_map/ppermute | solution.py:35
  14.3 6.6 %collective-permute-start.5 = (bf16[2,2,4,1024]{3,2,1,0:T(4,128)(2,1)S(1)}, bf16[2,2,4,1024]{3,2,1,0:T(4,128)(2,1)S(1)}, u32[]{:S(2)}, u32[]{:S(2)}) collective-permute-start(bf16[2,2,4,1024]{3,2,1,0:T(4,128)(2,1)S(1)} %merge.1.refs_0_.refs_7_), channel_id=1, source_target_pairs={{0,8},{4,12},{8,0},{12,4},{1,9},{5,13},{9,1},{13,5},{2,10},{6,14},... | collective-permute-start | bytes 98312 | tf_op jit(solution)/shard_map/ppermute | solution.py:35
  16.9 5.7 %collective-permute-start.6 = (bf16[2,2,4,1024]{3,2,1,0:T(4,128)(2,1)S(1)}, bf16[2,2,4,1024]{3,2,1,0:T(4,128)(2,1)S(1)}, u32[]{:S(2)}, u32[]{:S(2)}) collective-permute-start(bf16[2,2,4,1024]{3,2,1,0:T(4,128)(2,1)S(1)} %merge.1.refs_0_.refs_7_), channel_id=1, source_target_pairs={{0,12},{4,8},{8,4},{12,0},{1,13},{5,9},{9,5},{13,1},{2,14},{6,10},... | collective-permute-start | bytes 98312 | tf_op jit(solution)/shard_map/ppermute | solution.py:35
  19.4 9.4 %collective-permute-start.10 = (bf16[4,256,512]{2,1,0:T(8,128)(2,1)S(1)}, bf16[4,256,512]{2,1,0:T(8,128)(2,1)S(1)}, u32[]{:S(2)}, u32[]{:S(2)}) collective-permute-start(bf16[4,256,512]{2,1,0:T(8,128)(2,1)S(1)} %get-tuple-element.22.refs_4_), channel_id=1, source_target_pairs={{0,1},{1,0},{2,3},{3,2},{4,5},{5,4},{6,7},{7,6},{8,9},{9,8},{10,11... | collective-permute-start | bytes 3145736 | tf_op jit(solution)/shard_map/ppermute | solution.py:35
  26.4 7.9 %collective-permute-start.7 = (bf16[272,128]{1,0:T(8,128)(2,1)S(1)}, bf16[272,128]{1,0:T(8,128)(2,1)S(1)}, u32[]{:S(2)}, u32[]{:S(2)}) collective-permute-start(bf16[272,128]{1,0:T(8,128)(2,1)S(1)} %get-tuple-element.25), channel_id=1, source_target_pairs={{0,4},{4,0},{8,12},{12,8},{1,5},{5,1},{9,13},{13,9},{2,6},{6,2},{1... | collective-permute-start | bytes 208904 | tf_op jit(solution)/shard_map/ppermute | solution.py:35
  26.4 9.0 %collective-permute-start.8 = (bf16[272,128]{1,0:T(8,128)(2,1)S(1)}, bf16[272,128]{1,0:T(8,128)(2,1)S(1)}, u32[]{:S(2)}, u32[]{:S(2)}) collective-permute-start(bf16[272,128]{1,0:T(8,128)(2,1)S(1)} %get-tuple-element.26), channel_id=1, source_target_pairs={{0,8},{4,12},{8,0},{12,4},{1,9},{5,13},{9,1},{13,5},{2,10},{6,14},... | collective-permute-start | bytes 208904 | tf_op jit(solution)/shard_map/ppermute | solution.py:35
  28.8 6.6 %collective-permute-start.9 = (bf16[272,128]{1,0:T(8,128)(2,1)S(1)}, bf16[272,128]{1,0:T(8,128)(2,1)S(1)}, u32[]{:S(2)}, u32[]{:S(2)}) collective-permute-start(bf16[272,128]{1,0:T(8,128)(2,1)S(1)} %get-tuple-element.27), channel_id=1, source_target_pairs={{0,12},{4,8},{8,4},{12,0},{1,13},{5,9},{9,5},{13,1},{2,14},{6,10},... | collective-permute-start | bytes 208904 | tf_op jit(solution)/shard_map/ppermute | solution.py:35
  35.8 9.4 %collective-permute-start.11 = (bf16[8,4096]{1,0:T(8,128)(2,1)S(1)}, bf16[8,4096]{1,0:T(8,128)(2,1)S(1)}, u32[]{:S(2)}, u32[]{:S(2)}) collective-permute-start(bf16[8,4096]{1,0:T(8,128)(2,1)S(1)} %join.1.refs_0_), channel_id=1, source_target_pairs={{0,4},{4,0},{8,12},{12,8},{1,5},{5,1},{9,13},{13,9},{2,6},{6,2},{1... | collective-permute-start | bytes 196616 | tf_op jit(solution)/shard_map/ppermute | solution.py:35
  37.6 7.7 %collective-permute-start.12 = (bf16[8,4096]{1,0:T(8,128)(2,1)S(1)}, bf16[8,4096]{1,0:T(8,128)(2,1)S(1)}, u32[]{:S(2)}, u32[]{:S(2)}) collective-permute-start(bf16[8,4096]{1,0:T(8,128)(2,1)S(1)} %join.1.refs_0_), channel_id=1, source_target_pairs={{0,8},{4,12},{8,0},{12,4},{1,9},{5,13},{9,1},{13,5},{2,10},{6,14},... | collective-permute-start | bytes 196616 | tf_op jit(solution)/shard_map/ppermute | solution.py:35
  38.0 7.3 %collective-permute-start.13 = (bf16[8,4096]{1,0:T(8,128)(2,1)S(1)}, bf16[8,4096]{1,0:T(8,128)(2,1)S(1)}, u32[]{:S(2)}, u32[]{:S(2)}) collective-permute-start(bf16[8,4096]{1,0:T(8,128)(2,1)S(1)} %join.1.refs_0_), channel_id=1, source_target_pairs={{0,12},{4,8},{8,4},{12,0},{1,13},{5,9},{9,5},{13,1},{2,14},{6,10},... | collective-permute-start | bytes 196616 | tf_op jit(solution)/shard_map/ppermute | solution.py:35

commit v15 on v14

--- a/solution.py
+++ b/solution.py
@@ -449,7 +449,8 @@
     )(in_hbm(weight), *others)
 
 
-def project_kernel(count, tile, *refs):
+def project_kernel(count, tile, skipped, *refs):
+    refs = refs[skipped:]
     part_refs, weight_refs, out_ref = refs[:count], refs[count:-1], refs[-1]
     tp_index = lax.axis_index("tp")
     prompts, samples, width = out_ref.shape
@@ -475,20 +476,20 @@
                 out_ref[(tp_index ^ offset) * share + n, :, first : first + tile] = block
 
 
-def project(parts, weights, samples):
+def project(parts, weights, others, samples):
     count = len(parts)
     depth, width = weights[0].shape
     depth *= len(weights)
     total = count * parts[0].shape[0]
     return pl.pallas_call(
-        functools.partial(project_kernel, count, min(256, width)),
+        functools.partial(project_kernel, count, min(256, width), len(others)),
         out_shape=jax.ShapeDtypeStruct((total // samples, samples, width), jnp.bfloat16),
-        in_specs=[VMEM] * (count + len(weights)),
+        in_specs=[ANY] * len(others) + [VMEM] * (count + len(weights)),
         out_specs=VMEM,
         compiler_params=limit(24),
         cost_estimate=cost(2 * total * depth * width, 2 * depth * width),
         name="project",
-    )(*parts, *weights)
+    )(*others, *parts, *weights)
 
 
 def body(prompt_key_values, queries, routing, lengths, out_weight):
@@ -534,11 +535,11 @@
         layer_out = jnp.dot(attended, out_weight, preferred_element_type=jnp.float32)
         layer_out = layer_out.astype(jnp.bfloat16).reshape(REQ_GRP, samples, -1)
     else:
-        layer_out = project(shares, held_weight, samples)
+        layer_out = project(shares, held_weight, far_parts[:-1], samples)
 
     held_cache = place([], near_parts + head_parts, near + head, slot_count)
-    for part, piece in zip(far_parts, far):
-        held_cache = place([held_cache, layer_out], [part], [piece], slot_count)
+    held_cache = place([held_cache, share], far_parts[:-1], far[:-1], slot_count)
+    held_cache = place([held_cache, layer_out], far_parts[-1:], far[-1:], slot_count)
     held_cache = held_cache.reshape((1, slot_count) + prompt_key_values.shape[1:])
     return (layer_out, held_cache)
 

time: 52.3 us -> 52.8 us (level)
  waiting for transfers between devices: 6.82 us -> 7.41 us
    ppermute x16, waiting for transfers between devices: 6.82 us -> 7.41 us  [swap(): return lax.ppermute(value, axis, [(i, i ^ offset) for i in range(count)])]
  transfers between devices with their start and end apart: 16 -> 16, of which waited for: 6 -> 5; matrix products, arithmetic and copies ran while one was open for 0% -> 0% of each run, Pallas kernels for 41% -> 41%
where the time goes in v15:
time: 52.8 us; the launch traced here: 52.6 us
  Pallas kernels  24.2 us (46%)
  starting transfers between devices  20.2 us (38%)
  waiting for transfers between devices  7.41 us (14%)
  between operations  0.81 us (2%)
    ppermute x16, starting transfers between devices, swap(): return lax.ppermute(value, axis, [(i, i ^ offset) for i in range(count)])  20.2 us
    ppermute x16, waiting for transfers between devices, swap(): return lax.ppermute(value, axis, [(i, i ^ offset) for i in range(count)])  7.41 us
    pallas_call x2, Pallas kernels, fetch(): pl.pallas_call(functools.partial(fetch_kernel, number * size), out_shape=...  6.94 us
    pallas_call x1, Pallas kernels, attend(): pl.pallas_call(functools.partial(attend_kernel, pieces, section_count, tp...  3.77 us
    pallas_call x1, Pallas kernels, project(): pl.pallas_call(functools.partial(project_kernel, count, min(256, width),...  3.65 us
    pallas_call x3, Pallas kernels, place(): pl.pallas_call(functools.partial(place_kernel, pieces), out_shape=jax.Sha...  3.38 us
    pallas_call x1, Pallas kernels, pack(): pl.pallas_call(functools.partial(pack_kernel, pieces, section_count), out...  2.22 us
    pallas_call x1, Pallas kernels, first_pack(): pl.pallas_call(functools.partial(first_pack_kernel, pieces, section_count...  2.2 us
  transfers between devices with their start and end apart: 16, of which 5 were waited for; matrix products, arithmetic and copies ran while one was open for 0% of the time, Pallas kernels for 41%

profile of v15, /device:TPU:0, one launch (start us, length us, event | category | flops | bytes accessed | tf_op | source)
XLA Modules:
  0.0 52.6 jit_solution(7636655800738071805)
XLA Ops:
  0.6 1.7 %pack_head.1 = (bf16[1,256,512]{2,1,0:T(8,128)(2,1)S(1)}, bf16[2,4,1024]{2,1,0:T(4,128)(2,1)S(1)}, bf16[2,4,1024]{2,1,0:T(4,128)(2,1)S(1)}) custom-call(s32[32]{0:T(128)} %bitcast.2, bf16[8,2,256,512]{3,2,1,0:T(8,128)(2,1)} %cache_ref.5, bf16[1,8,4,4096]{3,2,1,0:T(4,128)(2,1)} %query_ref.3), custom_call_target="tpu_custom_call" | custom-call | bytes 2097152 | tf_op jit(solution)/shard_map/pack_head/pallas_call | solution.py:141
  2.3 3.0 %collective-permute-start.3 = (bf16[1,256,512]{2,1,0:T(8,128)(2,1)S(1)}, bf16[1,256,512]{2,1,0:T(8,128)(2,1)S(1)}, u32[]{:S(2)}, u32[]{:S(2)}) collective-permute-start(bf16[1,256,512]{2,1,0:T(8,128)(2,1)S(1)} %get-tuple-element.15.refs_0_), channel_id=1, source_target_pairs={{0,2},{1,3},{2,0},{3,1},{4,6},{5,7},{6,4},{7,5},{8,10},{9,11},{10,... | collective-permute-start | bytes 786440 | tf_op jit(solution)/shard_map/ppermute | solution.py:35
  5.3 0.1 collective-permute-start.1
  5.4 0.8 %collective-permute-start.2 = (bf16[2,4,1024]{2,1,0:T(4,128)(2,1)S(1)}, bf16[2,4,1024]{2,1,0:T(4,128)(2,1)S(1)}, u32[]{:S(2)}, u32[]{:S(2)}) collective-permute-start(bf16[2,4,1024]{2,1,0:T(4,128)(2,1)S(1)} %get-tuple-element.19), channel_id=1, source_target_pairs={{0,3},{1,2},{2,1},{3,0},{4,7},{5,6},{6,5},{7,4},{8,11},{9,10},{10,... | collective-permute-start | bytes 49160 | tf_op jit(solution)/shard_map/ppermute | solution.py:35
  6.2 2.2 %first_pack.1 = (bf16[3,256,512]{2,1,0:T(8,128)(2,1)S(1)}, bf16[4,256,512]{2,1,0:T(8,128)(2,1)S(1)}, bf16[2,4,4096]{2,1,0:T(4,128)(2,1)S(1)}, bf16[2,4,4096]{2,1,0:T(4,128)(2,1)S(1)}) custom-call(s32[32]{0:T(128)S(1)} %bitcast.3, bf16[8,2,256,512]{3,2,1,0:T(8,128)(2,1)} %cache_ref.5, bf16[1,8,4,4096]{3,2,1,0:T(4,128)(2,1)} %query_ref.3, ...), custom_call_target="tpu_custom_call" | custom-call | bytes 3932160 | tf_op jit(solution)/shard_map/first_pack/pallas_call | solution.py:199
  8.4 1.2 %collective-permute-start = (bf16[3,256,512]{2,1,0:T(8,128)(2,1)S(1)}, bf16[3,256,512]{2,1,0:T(8,128)(2,1)S(1)}, u32[]{:S(2)}, u32[]{:S(2)}) collective-permute-start(bf16[3,256,512]{2,1,0:T(8,128)(2,1)S(1)} %get-tuple-element.16.refs_1_), channel_id=1, source_target_pairs={{0,2},{1,3},{2,0},{3,1},{4,6},{5,7},{6,4},{7,5},{8,10},{9,11},{10,... | collective-permute-start | bytes 2359304 | tf_op jit(solution)/shard_map/ppermute | solution.py:35
  9.6 0.2 collective-permute-start.4
  9.8 2.6 %collective-permute-done.1.refs_0_ = bf16[2,4,1024]{2,1,0:T(4,128)(2,1)S(1)} collective-permute-done((bf16[2,4,1024]{2,1,0:T(4,128)(2,1)S(1)}, bf16[2,4,1024]{2,1,0:T(4,128)(2,1)S(1)}, u32[]{:S(2)}, u32[]{:S(2)}) %collective-permute-start.1) | collective-permute-done | bytes 16416 | tf_op jit(solution)/shard_map/ppermute | solution.py:35
  12.4 0.3 collective-permute-done.2.refs_1_
  12.7 1.6 %collective-permute-start.5 = (bf16[2,2,4,1024]{3,2,1,0:T(4,128)(2,1)S(1)}, bf16[2,2,4,1024]{3,2,1,0:T(4,128)(2,1)S(1)}, u32[]{:S(2)}, u32[]{:S(2)}) collective-permute-start(bf16[2,2,4,1024]{3,2,1,0:T(4,128)(2,1)S(1)} %merge.1.refs_0_.refs_7_), channel_id=1, source_target_pairs={{0,4},{4,0},{8,12},{12,8},{1,5},{5,1},{9,13},{13,9},{2,6},{6,2},{1... | collective-permute-start | bytes 98312 | tf_op jit(solution)/shard_map/ppermute | solution.py:35
  14.4 2.6 %collective-permute-start.6 = (bf16[2,2,4,1024]{3,2,1,0:T(4,128)(2,1)S(1)}, bf16[2,2,4,1024]{3,2,1,0:T(4,128)(2,1)S(1)}, u32[]{:S(2)}, u32[]{:S(2)}) collective-permute-start(bf16[2,2,4,1024]{3,2,1,0:T(4,128)(2,1)S(1)} %merge.1.refs_0_.refs_7_), channel_id=1, source_target_pairs={{0,8},{4,12},{8,0},{12,4},{1,9},{5,13},{9,1},{13,5},{2,10},{6,14},... | collective-permute-start | bytes 98312 | tf_op jit(solution)/shard_map/ppermute | solution.py:35
  17.0 0.2 collective-permute-start.7
  17.2 2.2 %pack.1 = (bf16[4,256,512]{2,1,0:T(8,128)(2,1)S(1)}, bf16[4,256,512]{2,1,0:T(8,128)(2,1)S(1)}) custom-call(s32[32]{0:T(128)S(1)} %bitcast.4, bf16[8,2,256,512]{3,2,1,0:T(8,128)(2,1)} %cache_ref.5, bf16[2,2,4,1024]{3,2,1,0:T(4,128)(2,1)S(1)} %merge.1.refs_0_.refs_7_, bf16[2,4,4096]{2,1,0:T(4,128)(2,1)S(1)} %collective-permute-done.4.refs_1_.refs_6_), custom_call_target="tpu_custom_call" | custom-call | flops 10000000000 | bytes 4194304 | tf_op jit(solution)/shard_map/pack/pallas_call | solution.py:217
  19.4 1.5 %collective-permute-start.11 = (bf16[4,256,512]{2,1,0:T(8,128)(2,1)S(1)}, bf16[4,256,512]{2,1,0:T(8,128)(2,1)S(1)}, u32[]{:S(2)}, u32[]{:S(2)}) collective-permute-start(bf16[4,256,512]{2,1,0:T(8,128)(2,1)S(1)} %get-tuple-element.22.refs_4_), channel_id=1, source_target_pairs={{0,1},{1,0},{2,3},{3,2},{4,5},{5,4},{6,7},{7,6},{8,9},{9,8},{10,11... | collective-permute-start | bytes 3145736 | tf_op jit(solution)/shard_map/ppermute | solution.py:35
  21.0 1.7 %collective-permute-done.7.refs_10_ = bf16[2,2,4,1024]{3,2,1,0:T(4,128)(2,1)S(1)} collective-permute-done((bf16[2,2,4,1024]{3,2,1,0:T(4,128)(2,1)S(1)}, bf16[2,2,4,1024]{3,2,1,0:T(4,128)(2,1)S(1)}, u32[]{:S(2)}, u32[]{:S(2)}) %collective-permute-start.7) | collective-permute-done | bytes 32800 | tf_op jit(solution)/shard_map/ppermute | solution.py:35
  22.7 3.8 %attend.1 = (bf16[272,128]{1,0:T(8,128)(2,1)S(1)}, bf16[272,128]{1,0:T(8,128)(2,1)S(1)}, bf16[272,128]{1,0:T(8,128)(2,1)S(1)}, bf16[272,128]{1,0:T(8,128)(2,1)S(1)}) custom-call(s32[32]{0:T(128)S(1)} %bitcast.5, s32[32]{0:T(128)S(1)} %copy-done.3, bf16[1,256,512]{2,1,0:T(8,128)(2,1)S(1)} %get-tuple-element.15.refs_0_, ...), custom_call_target="tpu_custom_call" | custom-call | flops 20000000000 | bytes 4194304 | tf_op jit(solution)/shard_map/attend/pallas_call | solution.py:347
  26.5 0.1 collective-permute-start.8
  26.5 2.4 %collective-permute-start.9 = (bf16[272,128]{1,0:T(8,128)(2,1)S(1)}, bf16[272,128]{1,0:T(8,128)(2,1)S(1)}, u32[]{:S(2)}, u32[]{:S(2)}) collective-permute-start(bf16[272,128]{1,0:T(8,128)(2,1)S(1)} %get-tuple-element.26), channel_id=1, source_target_pairs={{0,8},{4,12},{8,0},{12,4},{1,9},{5,13},{9,1},{13,5},{2,10},{6,14},... | collective-permute-start | bytes 208904 | tf_op jit(solution)/shard_map/ppermute | solution.py:35
  28.9 2.0 %collective-permute-start.10 = (bf16[272,128]{1,0:T(8,128)(2,1)S(1)}, bf16[272,128]{1,0:T(8,128)(2,1)S(1)}, u32[]{:S(2)}, u32[]{:S(2)}) collective-permute-start(bf16[272,128]{1,0:T(8,128)(2,1)S(1)} %get-tuple-element.27), channel_id=1, source_target_pairs={{0,12},{4,8},{8,4},{12,0},{1,13},{5,9},{9,5},{13,1},{2,14},{6,10},... | collective-permute-start | bytes 208904 | tf_op jit(solution)/shard_map/ppermute | solution.py:35
  30.9 3.5 %fetch.2.refs_4_.refs_5_ = bf16[2048,2048]{1,0:T(8,128)(2,1)S(1)} custom-call(bf16[4096,2048]{1,0:T(8,128)(2,1)} %weight_ref.3, bf16[272,128]{1,0:T(8,128)(2,1)S(1)} %get-tuple-element.24.refs_0_, bf16[4,256,512]{2,1,0:T(8,128)(2,1)S(1)} %collective-permute-done.11.refs_1_), custom_call_target="tpu_custom_call" | custom-call | bytes 16777216 | tf_op jit(solution)/shard_map/fetch/pallas_call | solution.py:440
  34.4 1.1 %collective-permute-done.9.refs_2_ = bf16[272,128]{1,0:T(8,128)(2,1)S(1)} collective-permute-done((bf16[272,128]{1,0:T(8,128)(2,1)S(1)}, bf16[272,128]{1,0:T(8,128)(2,1)S(1)}, u32[]{:S(2)}, u32[]{:S(2)}) %collective-permute-start.9) | collective-permute-done | bytes 69664 | tf_op jit(solution)/shard_map/ppermute | solution.py:35
  35.5 0.4 join.1.refs_0_.refs_1_
  35.9 0.0 copy-start
  35.9 1.8 %collective-permute-start.12 = (bf16[8,4096]{1,0:T(8,128)(2,1)S(1)}, bf16[8,4096]{1,0:T(8,128)(2,1)S(1)}, u32[]{:S(2)}, u32[]{:S(2)}) collective-permute-start(bf16[8,4096]{1,0:T(8,128)(2,1)S(1)} %join.1.refs_0_.refs_1_), channel_id=1, source_target_pairs={{0,4},{4,0},{8,12},{12,8},{1,5},{5,1},{9,13},{13,9},{2,6},{6,2},{1... | collective-permute-start | bytes 196616 | tf_op jit(solution)/shard_map/ppermute | solution.py:35
  37.7 0.4 collective-permute-start.13
  38.1 2.2 %collective-permute-start.14 = (bf16[8,4096]{1,0:T(8,128)(2,1)S(1)}, bf16[8,4096]{1,0:T(8,128)(2,1)S(1)}, u32[]{:S(2)}, u32[]{:S(2)}) collective-permute-start(bf16[8,4096]{1,0:T(8,128)(2,1)S(1)} %join.1.refs_0_.refs_1_), channel_id=1, source_target_pairs={{0,12},{4,8},{8,4},{12,0},{1,13},{5,9},{9,5},{13,1},{2,14},{6,10},... | collective-permute-start | bytes 196616 | tf_op jit(solution)/shard_map/ppermute | solution.py:35
  40.4 3.5 %fetch.3.refs_6_ = bf16[2048,2048]{1,0:T(8,128)(2,1)S(1)} custom-call(bf16[4096,2048]{1,0:T(8,128)(2,1)} %weight_ref.3, bf16[8,4096]{1,0:T(8,128)(2,1)S(1)} %join.1.refs_0_.refs_1_), custom_call_target="tpu_custom_call" | custom-call | bytes 16777216 | tf_op jit(solution)/shard_map/fetch/pallas_call | solution.py:440
  43.9 1.5 %place.3.refs_0_ = bf16[1,16,256,512]{3,2,1,0:T(8,128)(2,1)} custom-call(bf16[4,256,512]{2,1,0:T(8,128)(2,1)S(1)} %get-tuple-element.21.refs_3_.refs_0_, bf16[4,256,512]{2,1,0:T(8,128)(2,1)S(1)} %collective-permute-done.11.refs_1_, bf16[1,256,512]{2,1,0:T(8,128)(2,1)S(1)} %collective-permute-done.3.refs_2_), custom_call_target="tpu_custom_call" | custom-call | bytes 4718592 | tf_op jit(solution)/shard_map/place/pallas_call | solution.py:247
  45.4 0.9 %place.4.refs_0_ = bf16[1,16,256,512]{3,2,1,0:T(8,128)(2,1)} custom-call(bf16[1,16,256,512]{3,2,1,0:T(8,128)(2,1)} %place.3.refs_0_, bf16[8,4096]{1,0:T(8,128)(2,1)} %copy-done, bf16[3,256,512]{2,1,0:T(8,128)(2,1)S(1)} %collective-permute-done.refs_0_.refs_2_), custom_call_target="tpu_custom_call", output_to_operand_aliasing={{}: (0, {})} | custom-call | bytes 1572864 | tf_op jit(solution)/shard_map/place/pallas_call | solution.py:247
  46.3 3.6 %project.1.refs_1_ = bf16[8,4,2048]{2,1,0:T(4,128)(2,1)} custom-call(bf16[3,256,512]{2,1,0:T(8,128)(2,1)S(1)} %collective-permute-done.refs_0_.refs_2_, bf16[8,4096]{1,0:T(8,128)(2,1)S(1)} %copy-done.1, bf16[8,4096]{1,0:T(8,128)(2,1)S(1)} %collective-permute-done.12.refs_2_, bf16[8,4096]{1,0:T(8,128)(2,1)S(1)} %collective-permute-done.13.refs_3_, ...), custom_call_target="tpu_custom_call" | custom-call | flops 536870912 | bytes 16777216 | tf_op jit(solution)/shard_map/project/pallas_call | solution.py:484
  50.0 1.7 %collective-permute-done.15.refs_2_ = bf16[4,256,512]{2,1,0:T(8,128)(2,1)S(1)} collective-permute-done((bf16[4,256,512]{2,1,0:T(8,128)(2,1)S(1)}, bf16[4,256,512]{2,1,0:T(8,128)(2,1)S(1)}, u32[]{:S(2)}, u32[]{:S(2)}) %collective-permute-start.15) | collective-permute-done | bytes 1048608 | tf_op jit(solution)/shard_map/ppermute | solution.py:35
  51.6 1.0 %place.5 = bf16[1,16,256,512]{3,2,1,0:T(8,128)(2,1)} custom-call(bf16[1,16,256,512]{3,2,1,0:T(8,128)(2,1)} %place.4.refs_0_, bf16[8,4,2048]{2,1,0:T(4,128)(2,1)} %project.1.refs_1_, bf16[4,256,512]{2,1,0:T(8,128)(2,1)S(1)} %collective-permute-done.15.refs_2_), custom_call_target="tpu_custom_call", output_to_operand_aliasing={{}: (0, {})} | custom-call | bytes 2097152 | tf_op jit(solution)/shard_map/place/pallas_call | solution.py:247
  (20 shorter events, 0.1 us)
Async XLA Ops:
  0.6 5.6 %copy-start.2 = (s32[32,1]{0,1:T(1,128)S(1)}, s32[32,1]{0,1:T(1,128)}, u32[]{:S(2)}) copy-start(s32[32,1]{0,1:T(1,128)} %param.7) | copy-start | bytes 388
  2.3 10.4 %collective-permute-start.3 = (bf16[1,256,512]{2,1,0:T(8,128)(2,1)S(1)}, bf16[1,256,512]{2,1,0:T(8,128)(2,1)S(1)}, u32[]{:S(2)}, u32[]{:S(2)}) collective-permute-start(bf16[1,256,512]{2,1,0:T(8,128)(2,1)S(1)} %get-tuple-element.15.refs_0_), channel_id=1, source_target_pairs={{0,2},{1,3},{2,0},{3,1},{4,6},{5,7},{6,4},{7,5},{8,10},{9,11},{10,... | collective-permute-start | bytes 786440 | tf_op jit(solution)/shard_map/ppermute | solution.py:35
  5.3 7.1 %collective-permute-start.1 = (bf16[2,4,1024]{2,1,0:T(4,128)(2,1)S(1)}, bf16[2,4,1024]{2,1,0:T(4,128)(2,1)S(1)}, u32[]{:S(2)}, u32[]{:S(2)}) collective-permute-start(bf16[2,4,1024]{2,1,0:T(4,128)(2,1)S(1)} %get-tuple-element.18), channel_id=1, source_target_pairs={{0,2},{1,3},{2,0},{3,1},{4,6},{5,7},{6,4},{7,5},{8,10},{9,11},{10,... | collective-permute-start | bytes 49160 | tf_op jit(solution)/shard_map/ppermute | solution.py:35
  5.4 7.3 %collective-permute-start.2 = (bf16[2,4,1024]{2,1,0:T(4,128)(2,1)S(1)}, bf16[2,4,1024]{2,1,0:T(4,128)(2,1)S(1)}, u32[]{:S(2)}, u32[]{:S(2)}) collective-permute-start(bf16[2,4,1024]{2,1,0:T(4,128)(2,1)S(1)} %get-tuple-element.19), channel_id=1, source_target_pairs={{0,3},{1,2},{2,1},{3,0},{4,7},{5,6},{6,5},{7,4},{8,11},{9,10},{10,... | collective-permute-start | bytes 49160 | tf_op jit(solution)/shard_map/ppermute | solution.py:35
  8.4 36.9 %collective-permute-start = (bf16[3,256,512]{2,1,0:T(8,128)(2,1)S(1)}, bf16[3,256,512]{2,1,0:T(8,128)(2,1)S(1)}, u32[]{:S(2)}, u32[]{:S(2)}) collective-permute-start(bf16[3,256,512]{2,1,0:T(8,128)(2,1)S(1)} %get-tuple-element.16.refs_1_), channel_id=1, source_target_pairs={{0,2},{1,3},{2,0},{3,1},{4,6},{5,7},{6,4},{7,5},{8,10},{9,11},{10,... | collective-permute-start | bytes 2359304 | tf_op jit(solution)/shard_map/ppermute | solution.py:35
  9.6 7.4 %collective-permute-start.4 = (bf16[2,4,4096]{2,1,0:T(4,128)(2,1)S(1)}, bf16[2,4,4096]{2,1,0:T(4,128)(2,1)S(1)}, u32[]{:S(2)}, u32[]{:S(2)}) collective-permute-start(bf16[2,4,4096]{2,1,0:T(4,128)(2,1)S(1)} %get-tuple-element.20), channel_id=1, source_target_pairs={{0,1},{1,0},{2,3},{3,2},{4,5},{5,4},{6,7},{7,6},{8,9},{9,8},{10,11... | collective-permute-start | bytes 196616 | tf_op jit(solution)/shard_map/ppermute | solution.py:35
  12.4 39.3 %collective-permute-start.15 = (bf16[4,256,512]{2,1,0:T(8,128)(2,1)S(1)}, bf16[4,256,512]{2,1,0:T(8,128)(2,1)S(1)}, u32[]{:S(2)}, u32[]{:S(2)}) collective-permute-start(bf16[4,256,512]{2,1,0:T(8,128)(2,1)S(1)} %get-tuple-element.17.refs_2_), channel_id=1, source_target_pairs={{0,3},{1,2},{2,1},{3,0},{4,7},{5,6},{6,5},{7,4},{8,11},{9,10},{10,... | collective-permute-start | bytes 3145736 | tf_op jit(solution)/shard_map/ppermute | solution.py:35
  12.7 10.0 %copy-start.3 = (s32[32]{0:T(128)S(1)}, s32[32]{0:T(128)}, u32[]{:S(2)}) copy-start(s32[32]{0:T(128)} %lengths_ref.1) | copy-start | bytes 388
  12.7 6.7 %collective-permute-start.5 = (bf16[2,2,4,1024]{3,2,1,0:T(4,128)(2,1)S(1)}, bf16[2,2,4,1024]{3,2,1,0:T(4,128)(2,1)S(1)}, u32[]{:S(2)}, u32[]{:S(2)}) collective-permute-start(bf16[2,2,4,1024]{3,2,1,0:T(4,128)(2,1)S(1)} %merge.1.refs_0_.refs_7_), channel_id=1, source_target_pairs={{0,4},{4,0},{8,12},{12,8},{1,5},{5,1},{9,13},{13,9},{2,6},{6,2},{1... | collective-permute-start | bytes 98312 | tf_op jit(solution)/shard_map/ppermute | solution.py:35
  14.4 6.6 %collective-permute-start.6 = (bf16[2,2,4,1024]{3,2,1,0:T(4,128)(2,1)S(1)}, bf16[2,2,4,1024]{3,2,1,0:T(4,128)(2,1)S(1)}, u32[]{:S(2)}, u32[]{:S(2)}) collective-permute-start(bf16[2,2,4,1024]{3,2,1,0:T(4,128)(2,1)S(1)} %merge.1.refs_0_.refs_7_), channel_id=1, source_target_pairs={{0,8},{4,12},{8,0},{12,4},{1,9},{5,13},{9,1},{13,5},{2,10},{6,14},... | collective-permute-start | bytes 98312 | tf_op jit(solution)/shard_map/ppermute | solution.py:35
  17.0 5.7 %collective-permute-start.7 = (bf16[2,2,4,1024]{3,2,1,0:T(4,128)(2,1)S(1)}, bf16[2,2,4,1024]{3,2,1,0:T(4,128)(2,1)S(1)}, u32[]{:S(2)}, u32[]{:S(2)}) collective-permute-start(bf16[2,2,4,1024]{3,2,1,0:T(4,128)(2,1)S(1)} %merge.1.refs_0_.refs_7_), channel_id=1, source_target_pairs={{0,12},{4,8},{8,4},{12,0},{1,13},{5,9},{9,5},{13,1},{2,14},{6,10},... | collective-permute-start | bytes 98312 | tf_op jit(solution)/shard_map/ppermute | solution.py:35
  19.4 9.5 %collective-permute-start.11 = (bf16[4,256,512]{2,1,0:T(8,128)(2,1)S(1)}, bf16[4,256,512]{2,1,0:T(8,128)(2,1)S(1)}, u32[]{:S(2)}, u32[]{:S(2)}) collective-permute-start(bf16[4,256,512]{2,1,0:T(8,128)(2,1)S(1)} %get-tuple-element.22.refs_4_), channel_id=1, source_target_pairs={{0,1},{1,0},{2,3},{3,2},{4,5},{5,4},{6,7},{7,6},{8,9},{9,8},{10,11... | collective-permute-start | bytes 3145736 | tf_op jit(solution)/shard_map/ppermute | solution.py:35
  26.5 7.9 %collective-permute-start.8 = (bf16[272,128]{1,0:T(8,128)(2,1)S(1)}, bf16[272,128]{1,0:T(8,128)(2,1)S(1)}, u32[]{:S(2)}, u32[]{:S(2)}) collective-permute-start(bf16[272,128]{1,0:T(8,128)(2,1)S(1)} %get-tuple-element.25), channel_id=1, source_target_pairs={{0,4},{4,0},{8,12},{12,8},{1,5},{5,1},{9,13},{13,9},{2,6},{6,2},{1... | collective-permute-start | bytes 208904 | tf_op jit(solution)/shard_map/ppermute | solution.py:35
  26.5 9.0 %collective-permute-start.9 = (bf16[272,128]{1,0:T(8,128)(2,1)S(1)}, bf16[272,128]{1,0:T(8,128)(2,1)S(1)}, u32[]{:S(2)}, u32[]{:S(2)}) collective-permute-start(bf16[272,128]{1,0:T(8,128)(2,1)S(1)} %get-tuple-element.26), channel_id=1, source_target_pairs={{0,8},{4,12},{8,0},{12,4},{1,9},{5,13},{9,1},{13,5},{2,10},{6,14},... | collective-permute-start | bytes 208904 | tf_op jit(solution)/shard_map/ppermute | solution.py:35
  28.9 6.6 %collective-permute-start.10 = (bf16[272,128]{1,0:T(8,128)(2,1)S(1)}, bf16[272,128]{1,0:T(8,128)(2,1)S(1)}, u32[]{:S(2)}, u32[]{:S(2)}) collective-permute-start(bf16[272,128]{1,0:T(8,128)(2,1)S(1)} %get-tuple-element.27), channel_id=1, source_target_pairs={{0,12},{4,8},{8,4},{12,0},{1,13},{5,9},{9,5},{13,1},{2,14},{6,10},... | collective-permute-start | bytes 208904 | tf_op jit(solution)/shard_map/ppermute | solution.py:35
  35.9 7.9 %copy-start = (bf16[8,4096]{1,0:T(8,128)(2,1)}, bf16[8,4096]{1,0:T(8,128)(2,1)S(1)}, u32[]{:S(2)}) copy-start(bf16[8,4096]{1,0:T(8,128)(2,1)S(1)} %join.1.refs_0_.refs_1_) | copy-start | bytes 196612
  35.9 10.4 %collective-permute-start.12 = (bf16[8,4096]{1,0:T(8,128)(2,1)S(1)}, bf16[8,4096]{1,0:T(8,128)(2,1)S(1)}, u32[]{:S(2)}, u32[]{:S(2)}) collective-permute-start(bf16[8,4096]{1,0:T(8,128)(2,1)S(1)} %join.1.refs_0_.refs_1_), channel_id=1, source_target_pairs={{0,4},{4,0},{8,12},{12,8},{1,5},{5,1},{9,13},{13,9},{2,6},{6,2},{1... | collective-permute-start | bytes 196616 | tf_op jit(solution)/shard_map/ppermute | solution.py:35
  37.7 8.6 %collective-permute-start.13 = (bf16[8,4096]{1,0:T(8,128)(2,1)S(1)}, bf16[8,4096]{1,0:T(8,128)(2,1)S(1)}, u32[]{:S(2)}, u32[]{:S(2)}) collective-permute-start(bf16[8,4096]{1,0:T(8,128)(2,1)S(1)} %join.1.refs_0_.refs_1_), channel_id=1, source_target_pairs={{0,8},{4,12},{8,0},{12,4},{1,9},{5,13},{9,1},{13,5},{2,10},{6,14},... | collective-permute-start | bytes 196616 | tf_op jit(solution)/shard_map/ppermute | solution.py:35
  38.1 8.2 %collective-permute-start.14 = (bf16[8,4096]{1,0:T(8,128)(2,1)S(1)}, bf16[8,4096]{1,0:T(8,128)(2,1)S(1)}, u32[]{:S(2)}, u32[]{:S(2)}) collective-permute-start(bf16[8,4096]{1,0:T(8,128)(2,1)S(1)} %join.1.refs_0_.refs_1_), channel_id=1, source_target_pairs={{0,12},{4,8},{8,4},{12,0},{1,13},{5,9},{9,5},{13,1},{2,14},{6,10},... | collective-permute-start | bytes 196616 | tf_op jit(solution)/shard_map/ppermute | solution.py:35
  45.3 1.0 %copy-start.1 = (bf16[8,4096]{1,0:T(8,128)(2,1)S(1)}, bf16[8,4096]{1,0:T(8,128)(2,1)}, u32[]{:S(2)}) copy-start(bf16[8,4096]{1,0:T(8,128)(2,1)} %copy-done) | copy-start | bytes 196612

commit v16 on v15

--- a/solution.py
+++ b/solution.py
@@ -525,7 +525,8 @@
     messages = attend(routing, lengths, caches, pieces, query_parts, far_queries)
     partials = [swap(part, "tp", offset) for offset, part in enumerate(messages)]
     held_weight = [fetch(out_weight, [messages[0], *near_parts[1:]], 0, 2)]
-    share = join(partials, held_weight, samples, query_width // HEAD_SIZE // KEY_VALUE_HEADS)
+    held_cache = place([], near_parts + head_parts, near + head, slot_count)
+    share = join(partials, [*held_weight, held_cache], samples, query_width // HEAD_SIZE // KEY_VALUE_HEADS)
     shares = spread(share, "tp")
     held_weight.append(fetch(out_weight, [share], 1, 2))
     if share.ndim == 3:
@@ -537,7 +538,6 @@
     else:
         layer_out = project(shares, held_weight, far_parts[:-1], samples)
 
-    held_cache = place([], near_parts + head_parts, near + head, slot_count)
     held_cache = place([held_cache, share], far_parts[:-1], far[:-1], slot_count)
     held_cache = place([held_cache, layer_out], far_parts[-1:], far[-1:], slot_count)
     held_cache = held_cache.reshape((1, slot_count) + prompt_key_values.shape[1:])

time: 52.8 us -> 52.3 us (level)
  waiting for transfers between devices: 7.41 us -> 5.62 us
  local copies, waits for them, and re-layouts: 0.02 us -> 0.92 us
    ppermute x16, waiting for transfers between devices: 7.41 us -> 5.62 us  [swap(): return lax.ppermute(value, axis, [(i, i ^ offset) for i in range(count)])]
    unnamed x8 -> x10, local copies, waits for them, and re-layouts: 0.02 us -> 0.92 us
  transfers between devices with their start and end apart: 16 -> 16, of which waited for: 5 -> 5; matrix products, arithmetic and copies ran while one was open for 0% -> 0% of each run, Pallas kernels for 41% -> 42%
where the time goes in v16:
time: 52.3 us; the launch traced here: 51.9 us
  Pallas kernels  24.4 us (47%)
  starting transfers between devices  20.2 us (39%)
  waiting for transfers between devices  5.62 us (11%)
  local copies, waits for them, and re-layouts  0.92 us (2%)
  between operations  0.82 us (2%)
    ppermute x16, starting transfers between devices, swap(): return lax.ppermute(value, axis, [(i, i ^ offset) for i in range(count)])  20.2 us
    pallas_call x2, Pallas kernels, fetch(): pl.pallas_call(functools.partial(fetch_kernel, number * size), out_shape=...  7.09 us
    ppermute x16, waiting for transfers between devices, swap(): return lax.ppermute(value, axis, [(i, i ^ offset) for i in range(count)])  5.62 us
    pallas_call x1, Pallas kernels, attend(): pl.pallas_call(functools.partial(attend_kernel, pieces, section_count, tp...  3.77 us
    pallas_call x1, Pallas kernels, project(): pl.pallas_call(functools.partial(project_kernel, count, min(256, width),...  3.64 us
    pallas_call x3, Pallas kernels, place(): pl.pallas_call(functools.partial(place_kernel, pieces), out_shape=jax.Sha...  3.37 us
    pallas_call x1, Pallas kernels, pack(): pl.pallas_call(functools.partial(pack_kernel, pieces, section_count), out...  2.22 us
    pallas_call x1, Pallas kernels, first_pack(): pl.pallas_call(functools.partial(first_pack_kernel, pieces, section_count...  2.2 us
  transfers between devices with their start and end apart: 16, of which 5 were waited for; matrix products, arithmetic and copies ran while one was open for 0% of the time, Pallas kernels for 42%

profile of v16, /device:TPU:0, one launch (start us, length us, event | category | flops | bytes accessed | tf_op | source)
XLA Modules:
  0.0 51.9 jit_solution(2715029223227232387)
XLA Ops:
  0.6 1.7 %pack_head.1 = (bf16[1,256,512]{2,1,0:T(8,128)(2,1)S(1)}, bf16[2,4,1024]{2,1,0:T(4,128)(2,1)S(1)}, bf16[2,4,1024]{2,1,0:T(4,128)(2,1)S(1)}) custom-call(s32[32]{0:T(128)} %bitcast.3, bf16[8,2,256,512]{3,2,1,0:T(8,128)(2,1)} %cache_ref.5, bf16[1,8,4,4096]{3,2,1,0:T(4,128)(2,1)} %query_ref.3), custom_call_target="tpu_custom_call" | custom-call | bytes 2097152 | tf_op jit(solution)/shard_map/pack_head/pallas_call | solution.py:141
  2.3 3.0 %collective-permute-start.3 = (bf16[1,256,512]{2,1,0:T(8,128)(2,1)S(1)}, bf16[1,256,512]{2,1,0:T(8,128)(2,1)S(1)}, u32[]{:S(2)}, u32[]{:S(2)}) collective-permute-start(bf16[1,256,512]{2,1,0:T(8,128)(2,1)S(1)} %get-tuple-element.15.refs_0_), channel_id=1, source_target_pairs={{0,2},{1,3},{2,0},{3,1},{4,6},{5,7},{6,4},{7,5},{8,10},{9,11},{10,... | collective-permute-start | bytes 786440 | tf_op jit(solution)/shard_map/ppermute | solution.py:35
  5.3 0.1 collective-permute-start.1
  5.4 0.8 %collective-permute-start.2 = (bf16[2,4,1024]{2,1,0:T(4,128)(2,1)S(1)}, bf16[2,4,1024]{2,1,0:T(4,128)(2,1)S(1)}, u32[]{:S(2)}, u32[]{:S(2)}) collective-permute-start(bf16[2,4,1024]{2,1,0:T(4,128)(2,1)S(1)} %get-tuple-element.19), channel_id=1, source_target_pairs={{0,3},{1,2},{2,1},{3,0},{4,7},{5,6},{6,5},{7,4},{8,11},{9,10},{10,... | collective-permute-start | bytes 49160 | tf_op jit(solution)/shard_map/ppermute | solution.py:35
  6.2 2.2 %first_pack.1 = (bf16[3,256,512]{2,1,0:T(8,128)(2,1)S(1)}, bf16[4,256,512]{2,1,0:T(8,128)(2,1)S(1)}, bf16[2,4,4096]{2,1,0:T(4,128)(2,1)S(1)}, bf16[2,4,4096]{2,1,0:T(4,128)(2,1)S(1)}) custom-call(s32[32]{0:T(128)S(1)} %bitcast.4, bf16[8,2,256,512]{3,2,1,0:T(8,128)(2,1)} %cache_ref.5, bf16[1,8,4,4096]{3,2,1,0:T(4,128)(2,1)} %query_ref.3, ...), custom_call_target="tpu_custom_call" | custom-call | bytes 3932160 | tf_op jit(solution)/shard_map/first_pack/pallas_call | solution.py:199
  8.4 1.3 %collective-permute-start.4 = (bf16[2,4,4096]{2,1,0:T(4,128)(2,1)S(1)}, bf16[2,4,4096]{2,1,0:T(4,128)(2,1)S(1)}, u32[]{:S(2)}, u32[]{:S(2)}) collective-permute-start(bf16[2,4,4096]{2,1,0:T(4,128)(2,1)S(1)} %get-tuple-element.20), channel_id=1, source_target_pairs={{0,1},{1,0},{2,3},{3,2},{4,5},{5,4},{6,7},{7,6},{8,9},{9,8},{10,11... | collective-permute-start | bytes 196616 | tf_op jit(solution)/shard_map/ppermute | solution.py:35
  9.7 0.1 collective-permute-start
  9.8 2.6 %collective-permute-done.1.refs_0_ = bf16[2,4,1024]{2,1,0:T(4,128)(2,1)S(1)} collective-permute-done((bf16[2,4,1024]{2,1,0:T(4,128)(2,1)S(1)}, bf16[2,4,1024]{2,1,0:T(4,128)(2,1)S(1)}, u32[]{:S(2)}, u32[]{:S(2)}) %collective-permute-start.1) | collective-permute-done | bytes 16416 | tf_op jit(solution)/shard_map/ppermute | solution.py:35
  12.4 0.3 collective-permute-done.2.refs_1_
  12.7 3.6 %collective-permute-start.7 = (bf16[2,2,4,1024]{3,2,1,0:T(4,128)(2,1)S(1)}, bf16[2,2,4,1024]{3,2,1,0:T(4,128)(2,1)S(1)}, u32[]{:S(2)}, u32[]{:S(2)}) collective-permute-start(bf16[2,2,4,1024]{3,2,1,0:T(4,128)(2,1)S(1)} %merge.1.refs_0_.refs_7_), channel_id=1, source_target_pairs={{0,12},{4,8},{8,4},{12,0},{1,13},{5,9},{9,5},{13,1},{2,14},{6,10},... | collective-permute-start | bytes 98312 | tf_op jit(solution)/shard_map/ppermute | solution.py:35
  16.3 0.9 %collective-permute-start.5 = (bf16[2,2,4,1024]{3,2,1,0:T(4,128)(2,1)S(1)}, bf16[2,2,4,1024]{3,2,1,0:T(4,128)(2,1)S(1)}, u32[]{:S(2)}, u32[]{:S(2)}) collective-permute-start(bf16[2,2,4,1024]{3,2,1,0:T(4,128)(2,1)S(1)} %merge.1.refs_0_.refs_7_), channel_id=1, source_target_pairs={{0,4},{4,0},{8,12},{12,8},{1,5},{5,1},{9,13},{13,9},{2,6},{6,2},{1... | collective-permute-start | bytes 98312 | tf_op jit(solution)/shard_map/ppermute | solution.py:35
  17.2 2.2 %pack.1 = (bf16[4,256,512]{2,1,0:T(8,128)(2,1)S(1)}, bf16[4,256,512]{2,1,0:T(8,128)(2,1)S(1)}) custom-call(s32[32]{0:T(128)S(1)} %bitcast.5, bf16[8,2,256,512]{3,2,1,0:T(8,128)(2,1)} %cache_ref.5, bf16[2,2,4,1024]{3,2,1,0:T(4,128)(2,1)S(1)} %merge.1.refs_0_.refs_7_, bf16[2,4,4096]{2,1,0:T(4,128)(2,1)S(1)} %collective-permute-done.4.refs_1_.refs_6_), custom_call_target="tpu_custom_call" | custom-call | flops 10000000000 | bytes 4194304 | tf_op jit(solution)/shard_map/pack/pallas_call | solution.py:217
  19.4 1.5 %collective-permute-start.11 = (bf16[4,256,512]{2,1,0:T(8,128)(2,1)S(1)}, bf16[4,256,512]{2,1,0:T(8,128)(2,1)S(1)}, u32[]{:S(2)}, u32[]{:S(2)}) collective-permute-start(bf16[4,256,512]{2,1,0:T(8,128)(2,1)S(1)} %get-tuple-element.22.refs_4_), channel_id=1, source_target_pairs={{0,1},{1,0},{2,3},{3,2},{4,5},{5,4},{6,7},{7,6},{8,9},{9,8},{10,11... | collective-permute-start | bytes 3145736 | tf_op jit(solution)/shard_map/ppermute | solution.py:35
  21.0 0.6 %collective-permute-done.6.refs_9_ = bf16[2,2,4,1024]{3,2,1,0:T(4,128)(2,1)S(1)} collective-permute-done((bf16[2,2,4,1024]{3,2,1,0:T(4,128)(2,1)S(1)}, bf16[2,2,4,1024]{3,2,1,0:T(4,128)(2,1)S(1)}, u32[]{:S(2)}, u32[]{:S(2)}) %collective-permute-start.6) | collective-permute-done | bytes 32800 | tf_op jit(solution)/shard_map/ppermute | solution.py:35
  21.6 3.8 %attend.1 = (bf16[272,128]{1,0:T(8,128)(2,1)S(1)}, bf16[272,128]{1,0:T(8,128)(2,1)S(1)}, bf16[272,128]{1,0:T(8,128)(2,1)S(1)}, bf16[272,128]{1,0:T(8,128)(2,1)S(1)}) custom-call(s32[32]{0:T(128)S(1)} %bitcast.6, s32[32]{0:T(128)S(1)} %copy-done.4, bf16[1,256,512]{2,1,0:T(8,128)(2,1)S(1)} %get-tuple-element.15.refs_0_, ...), custom_call_target="tpu_custom_call" | custom-call | flops 20000000000 | bytes 4194304 | tf_op jit(solution)/shard_map/attend/pallas_call | solution.py:347
  25.4 0.9 %collective-permute-start.8 = (bf16[272,128]{1,0:T(8,128)(2,1)S(1)}, bf16[272,128]{1,0:T(8,128)(2,1)S(1)}, u32[]{:S(2)}, u32[]{:S(2)}) collective-permute-start(bf16[272,128]{1,0:T(8,128)(2,1)S(1)} %get-tuple-element.25), channel_id=1, source_target_pairs={{0,4},{4,0},{8,12},{12,8},{1,5},{5,1},{9,13},{13,9},{2,6},{6,2},{1... | collective-permute-start | bytes 208904 | tf_op jit(solution)/shard_map/ppermute | solution.py:35
  26.2 2.6 %collective-permute-start.9 = (bf16[272,128]{1,0:T(8,128)(2,1)S(1)}, bf16[272,128]{1,0:T(8,128)(2,1)S(1)}, u32[]{:S(2)}, u32[]{:S(2)}) collective-permute-start(bf16[272,128]{1,0:T(8,128)(2,1)S(1)} %get-tuple-element.26), channel_id=1, source_target_pairs={{0,8},{4,12},{8,0},{12,4},{1,9},{5,13},{9,1},{13,5},{2,10},{6,14},... | collective-permute-start | bytes 208904 | tf_op jit(solution)/shard_map/ppermute | solution.py:35
  28.9 1.0 %collective-permute-start.10 = (bf16[272,128]{1,0:T(8,128)(2,1)S(1)}, bf16[272,128]{1,0:T(8,128)(2,1)S(1)}, u32[]{:S(2)}, u32[]{:S(2)}) collective-permute-start(bf16[272,128]{1,0:T(8,128)(2,1)S(1)} %get-tuple-element.27), channel_id=1, source_target_pairs={{0,12},{4,8},{8,4},{12,0},{1,13},{5,9},{9,5},{13,1},{2,14},{6,10},... | collective-permute-start | bytes 208904 | tf_op jit(solution)/shard_map/ppermute | solution.py:35
  29.8 1.5 %place.3.refs_5_.refs_0_ = bf16[1,16,256,512]{3,2,1,0:T(8,128)(2,1)} custom-call(bf16[4,256,512]{2,1,0:T(8,128)(2,1)S(1)} %get-tuple-element.21.refs_3_.refs_0_, bf16[4,256,512]{2,1,0:T(8,128)(2,1)S(1)} %collective-permute-done.11.refs_1_, bf16[1,256,512]{2,1,0:T(8,128)(2,1)S(1)} %collective-permute-done.3.refs_2_), custom_call_target="tpu_custom_call" | custom-call | bytes 4718592 | tf_op jit(solution)/shard_map/place/pallas_call | solution.py:247
  31.3 3.6 %fetch.2.refs_4_.refs_5_ = bf16[2048,2048]{1,0:T(8,128)(2,1)S(1)} custom-call(bf16[4096,2048]{1,0:T(8,128)(2,1)} %weight_ref.3, bf16[272,128]{1,0:T(8,128)(2,1)S(1)} %get-tuple-element.24.refs_0_, bf16[4,256,512]{2,1,0:T(8,128)(2,1)S(1)} %collective-permute-done.11.refs_1_), custom_call_target="tpu_custom_call" | custom-call | bytes 16777216 | tf_op jit(solution)/shard_map/fetch/pallas_call | solution.py:440
  35.0 0.1 collective-permute-done.10.refs_3_
  35.1 0.9 %copy-done = bf16[1,16,256,512]{3,2,1,0:T(8,128)(2,1)S(1)} copy-done((bf16[1,16,256,512]{3,2,1,0:T(8,128)(2,1)S(1)}, bf16[1,16,256,512]{3,2,1,0:T(8,128)(2,1)}, u32[]{:S(2)}) %copy-start) | copy-done | bytes 4194328
  36.0 0.4 join.1.refs_0_.refs_1_
  36.4 0.0 copy-start.1
  36.4 2.9 %collective-permute-start.14 = (bf16[8,4096]{1,0:T(8,128)(2,1)S(1)}, bf16[8,4096]{1,0:T(8,128)(2,1)S(1)}, u32[]{:S(2)}, u32[]{:S(2)}) collective-permute-start(bf16[8,4096]{1,0:T(8,128)(2,1)S(1)} %join.1.refs_0_.refs_1_), channel_id=1, source_target_pairs={{0,12},{4,8},{8,4},{12,0},{1,13},{5,9},{9,5},{13,1},{2,14},{6,10},... | collective-permute-start | bytes 196616 | tf_op jit(solution)/shard_map/ppermute | solution.py:35
  39.3 1.5 %collective-permute-start.12 = (bf16[8,4096]{1,0:T(8,128)(2,1)S(1)}, bf16[8,4096]{1,0:T(8,128)(2,1)S(1)}, u32[]{:S(2)}, u32[]{:S(2)}) collective-permute-start(bf16[8,4096]{1,0:T(8,128)(2,1)S(1)} %join.1.refs_0_.refs_1_), channel_id=1, source_target_pairs={{0,4},{4,0},{8,12},{12,8},{1,5},{5,1},{9,13},{13,9},{2,6},{6,2},{1... | collective-permute-start | bytes 196616 | tf_op jit(solution)/shard_map/ppermute | solution.py:35
  40.8 3.5 %fetch.3.refs_6_ = bf16[2048,2048]{1,0:T(8,128)(2,1)S(1)} custom-call(bf16[4096,2048]{1,0:T(8,128)(2,1)} %weight_ref.3, bf16[8,4096]{1,0:T(8,128)(2,1)S(1)} %join.1.refs_0_.refs_1_), custom_call_target="tpu_custom_call" | custom-call | bytes 16777216 | tf_op jit(solution)/shard_map/fetch/pallas_call | solution.py:440
  44.3 0.0 copy-start.2
  44.3 0.9 %place.4.refs_0_ = bf16[1,16,256,512]{3,2,1,0:T(8,128)(2,1)} custom-call(bf16[1,16,256,512]{3,2,1,0:T(8,128)(2,1)} %place.3.refs_5_.refs_0_, bf16[8,4096]{1,0:T(8,128)(2,1)} %copy-done.1, bf16[3,256,512]{2,1,0:T(8,128)(2,1)S(1)} %collective-permute-done.refs_0_.refs_2_), custom_call_target="tpu_custom_call", output_to_operand_aliasing={{}: (0, {})} | custom-call | bytes 1572864 | tf_op jit(solution)/shard_map/place/pallas_call | solution.py:247
  45.3 3.6 %project.1.refs_1_ = bf16[8,4,2048]{2,1,0:T(4,128)(2,1)} custom-call(bf16[3,256,512]{2,1,0:T(8,128)(2,1)S(1)} %collective-permute-done.refs_0_.refs_2_, bf16[8,4096]{1,0:T(8,128)(2,1)S(1)} %copy-done.2, bf16[8,4096]{1,0:T(8,128)(2,1)S(1)} %collective-permute-done.12.refs_2_, bf16[8,4096]{1,0:T(8,128)(2,1)S(1)} %collective-permute-done.13.refs_3_, ...), custom_call_target="tpu_custom_call" | custom-call | flops 536870912 | bytes 16777216 | tf_op jit(solution)/shard_map/project/pallas_call | solution.py:484
  48.9 2.0 %collective-permute-done.15.refs_2_ = bf16[4,256,512]{2,1,0:T(8,128)(2,1)S(1)} collective-permute-done((bf16[4,256,512]{2,1,0:T(8,128)(2,1)S(1)}, bf16[4,256,512]{2,1,0:T(8,128)(2,1)S(1)}, u32[]{:S(2)}, u32[]{:S(2)}) %collective-permute-start.15) | collective-permute-done | bytes 1048608 | tf_op jit(solution)/shard_map/ppermute | solution.py:35
  50.9 1.0 %place.5 = bf16[1,16,256,512]{3,2,1,0:T(8,128)(2,1)} custom-call(bf16[1,16,256,512]{3,2,1,0:T(8,128)(2,1)} %place.4.refs_0_, bf16[8,4,2048]{2,1,0:T(4,128)(2,1)} %project.1.refs_1_, bf16[4,256,512]{2,1,0:T(8,128)(2,1)S(1)} %collective-permute-done.15.refs_2_), custom_call_target="tpu_custom_call", output_to_operand_aliasing={{}: (0, {})} | custom-call | bytes 2097152 | tf_op jit(solution)/shard_map/place/pallas_call | solution.py:247
  (22 shorter events, 0.1 us)
Async XLA Ops:
  0.6 5.6 %copy-start.3 = (s32[32,1]{0,1:T(1,128)S(1)}, s32[32,1]{0,1:T(1,128)}, u32[]{:S(2)}) copy-start(s32[32,1]{0,1:T(1,128)} %param.7) | copy-start | bytes 388
  2.3 10.4 %collective-permute-start.3 = (bf16[1,256,512]{2,1,0:T(8,128)(2,1)S(1)}, bf16[1,256,512]{2,1,0:T(8,128)(2,1)S(1)}, u32[]{:S(2)}, u32[]{:S(2)}) collective-permute-start(bf16[1,256,512]{2,1,0:T(8,128)(2,1)S(1)} %get-tuple-element.15.refs_0_), channel_id=1, source_target_pairs={{0,2},{1,3},{2,0},{3,1},{4,6},{5,7},{6,4},{7,5},{8,10},{9,11},{10,... | collective-permute-start | bytes 786440 | tf_op jit(solution)/shard_map/ppermute | solution.py:35
  5.3 7.1 %collective-permute-start.1 = (bf16[2,4,1024]{2,1,0:T(4,128)(2,1)S(1)}, bf16[2,4,1024]{2,1,0:T(4,128)(2,1)S(1)}, u32[]{:S(2)}, u32[]{:S(2)}) collective-permute-start(bf16[2,4,1024]{2,1,0:T(4,128)(2,1)S(1)} %get-tuple-element.18), channel_id=1, source_target_pairs={{0,2},{1,3},{2,0},{3,1},{4,6},{5,7},{6,4},{7,5},{8,10},{9,11},{10,... | collective-permute-start | bytes 49160 | tf_op jit(solution)/shard_map/ppermute | solution.py:35
  5.4 7.3 %collective-permute-start.2 = (bf16[2,4,1024]{2,1,0:T(4,128)(2,1)S(1)}, bf16[2,4,1024]{2,1,0:T(4,128)(2,1)S(1)}, u32[]{:S(2)}, u32[]{:S(2)}) collective-permute-start(bf16[2,4,1024]{2,1,0:T(4,128)(2,1)S(1)} %get-tuple-element.19), channel_id=1, source_target_pairs={{0,3},{1,2},{2,1},{3,0},{4,7},{5,6},{6,5},{7,4},{8,11},{9,10},{10,... | collective-permute-start | bytes 49160 | tf_op jit(solution)/shard_map/ppermute | solution.py:35
  8.4 7.9 %collective-permute-start.4 = (bf16[2,4,4096]{2,1,0:T(4,128)(2,1)S(1)}, bf16[2,4,4096]{2,1,0:T(4,128)(2,1)S(1)}, u32[]{:S(2)}, u32[]{:S(2)}) collective-permute-start(bf16[2,4,4096]{2,1,0:T(4,128)(2,1)S(1)} %get-tuple-element.20), channel_id=1, source_target_pairs={{0,1},{1,0},{2,3},{3,2},{4,5},{5,4},{6,7},{7,6},{8,9},{9,8},{10,11... | collective-permute-start | bytes 196616 | tf_op jit(solution)/shard_map/ppermute | solution.py:35
  9.7 34.6 %collective-permute-start = (bf16[3,256,512]{2,1,0:T(8,128)(2,1)S(1)}, bf16[3,256,512]{2,1,0:T(8,128)(2,1)S(1)}, u32[]{:S(2)}, u32[]{:S(2)}) collective-permute-start(bf16[3,256,512]{2,1,0:T(8,128)(2,1)S(1)} %get-tuple-element.16.refs_1_), channel_id=1, source_target_pairs={{0,2},{1,3},{2,0},{3,1},{4,6},{5,7},{6,4},{7,5},{8,10},{9,11},{10,... | collective-permute-start | bytes 2359304 | tf_op jit(solution)/shard_map/ppermute | solution.py:35
  12.4 38.5 %collective-permute-start.15 = (bf16[4,256,512]{2,1,0:T(8,128)(2,1)S(1)}, bf16[4,256,512]{2,1,0:T(8,128)(2,1)S(1)}, u32[]{:S(2)}, u32[]{:S(2)}) collective-permute-start(bf16[4,256,512]{2,1,0:T(8,128)(2,1)S(1)} %get-tuple-element.17.refs_2_), channel_id=1, source_target_pairs={{0,3},{1,2},{2,1},{3,0},{4,7},{5,6},{6,5},{7,4},{8,11},{9,10},{10,... | collective-permute-start | bytes 3145736 | tf_op jit(solution)/shard_map/ppermute | solution.py:35
  12.7 8.8 %copy-start.4 = (s32[32]{0:T(128)S(1)}, s32[32]{0:T(128)}, u32[]{:S(2)}) copy-start(s32[32]{0:T(128)} %lengths_ref.1) | copy-start | bytes 388
  12.7 6.7 %collective-permute-start.7 = (bf16[2,2,4,1024]{3,2,1,0:T(4,128)(2,1)S(1)}, bf16[2,2,4,1024]{3,2,1,0:T(4,128)(2,1)S(1)}, u32[]{:S(2)}, u32[]{:S(2)}) collective-permute-start(bf16[2,2,4,1024]{3,2,1,0:T(4,128)(2,1)S(1)} %merge.1.refs_0_.refs_7_), channel_id=1, source_target_pairs={{0,12},{4,8},{8,4},{12,0},{1,13},{5,9},{9,5},{13,1},{2,14},{6,10},... | collective-permute-start | bytes 98312 | tf_op jit(solution)/shard_map/ppermute | solution.py:35
  16.3 5.3 %collective-permute-start.6 = (bf16[2,2,4,1024]{3,2,1,0:T(4,128)(2,1)S(1)}, bf16[2,2,4,1024]{3,2,1,0:T(4,128)(2,1)S(1)}, u32[]{:S(2)}, u32[]{:S(2)}) collective-permute-start(bf16[2,2,4,1024]{3,2,1,0:T(4,128)(2,1)S(1)} %merge.1.refs_0_.refs_7_), channel_id=1, source_target_pairs={{0,8},{4,12},{8,0},{12,4},{1,9},{5,13},{9,1},{13,5},{2,10},{6,14},... | collective-permute-start | bytes 98312 | tf_op jit(solution)/shard_map/ppermute | solution.py:35
  16.3 5.3 %collective-permute-start.5 = (bf16[2,2,4,1024]{3,2,1,0:T(4,128)(2,1)S(1)}, bf16[2,2,4,1024]{3,2,1,0:T(4,128)(2,1)S(1)}, u32[]{:S(2)}, u32[]{:S(2)}) collective-permute-start(bf16[2,2,4,1024]{3,2,1,0:T(4,128)(2,1)S(1)} %merge.1.refs_0_.refs_7_), channel_id=1, source_target_pairs={{0,4},{4,0},{8,12},{12,8},{1,5},{5,1},{9,13},{13,9},{2,6},{6,2},{1... | collective-permute-start | bytes 98312 | tf_op jit(solution)/shard_map/ppermute | solution.py:35
  19.4 9.4 %collective-permute-start.11 = (bf16[4,256,512]{2,1,0:T(8,128)(2,1)S(1)}, bf16[4,256,512]{2,1,0:T(8,128)(2,1)S(1)}, u32[]{:S(2)}, u32[]{:S(2)}) collective-permute-start(bf16[4,256,512]{2,1,0:T(8,128)(2,1)S(1)} %get-tuple-element.22.refs_4_), channel_id=1, source_target_pairs={{0,1},{1,0},{2,3},{3,2},{4,5},{5,4},{6,7},{7,6},{8,9},{9,8},{10,11... | collective-permute-start | bytes 3145736 | tf_op jit(solution)/shard_map/ppermute | solution.py:35
  25.4 9.6 %collective-permute-start.8 = (bf16[272,128]{1,0:T(8,128)(2,1)S(1)}, bf16[272,128]{1,0:T(8,128)(2,1)S(1)}, u32[]{:S(2)}, u32[]{:S(2)}) collective-permute-start(bf16[272,128]{1,0:T(8,128)(2,1)S(1)} %get-tuple-element.25), channel_id=1, source_target_pairs={{0,4},{4,0},{8,12},{12,8},{1,5},{5,1},{9,13},{13,9},{2,6},{6,2},{1... | collective-permute-start | bytes 208904 | tf_op jit(solution)/shard_map/ppermute | solution.py:35
  26.2 8.7 %collective-permute-start.9 = (bf16[272,128]{1,0:T(8,128)(2,1)S(1)}, bf16[272,128]{1,0:T(8,128)(2,1)S(1)}, u32[]{:S(2)}, u32[]{:S(2)}) collective-permute-start(bf16[272,128]{1,0:T(8,128)(2,1)S(1)} %get-tuple-element.26), channel_id=1, source_target_pairs={{0,8},{4,12},{8,0},{12,4},{1,9},{5,13},{9,1},{13,5},{2,10},{6,14},... | collective-permute-start | bytes 208904 | tf_op jit(solution)/shard_map/ppermute | solution.py:35
  28.9 6.2 %collective-permute-start.10 = (bf16[272,128]{1,0:T(8,128)(2,1)S(1)}, bf16[272,128]{1,0:T(8,128)(2,1)S(1)}, u32[]{:S(2)}, u32[]{:S(2)}) collective-permute-start(bf16[272,128]{1,0:T(8,128)(2,1)S(1)} %get-tuple-element.27), channel_id=1, source_target_pairs={{0,12},{4,8},{8,4},{12,0},{1,13},{5,9},{9,5},{13,1},{2,14},{6,10},... | collective-permute-start | bytes 208904 | tf_op jit(solution)/shard_map/ppermute | solution.py:35
  31.3 4.7 %copy-start = (bf16[1,16,256,512]{3,2,1,0:T(8,128)(2,1)S(1)}, bf16[1,16,256,512]{3,2,1,0:T(8,128)(2,1)}, u32[]{:S(2)}) copy-start(bf16[1,16,256,512]{3,2,1,0:T(8,128)(2,1)} %place.3.refs_5_.refs_0_) | copy-start | bytes 12582916
  36.4 7.9 %copy-start.1 = (bf16[8,4096]{1,0:T(8,128)(2,1)}, bf16[8,4096]{1,0:T(8,128)(2,1)S(1)}, u32[]{:S(2)}) copy-start(bf16[8,4096]{1,0:T(8,128)(2,1)S(1)} %join.1.refs_0_.refs_1_) | copy-start | bytes 196612
  36.4 8.9 %collective-permute-start.14 = (bf16[8,4096]{1,0:T(8,128)(2,1)S(1)}, bf16[8,4096]{1,0:T(8,128)(2,1)S(1)}, u32[]{:S(2)}, u32[]{:S(2)}) collective-permute-start(bf16[8,4096]{1,0:T(8,128)(2,1)S(1)} %join.1.refs_0_.refs_1_), channel_id=1, source_target_pairs={{0,12},{4,8},{8,4},{12,0},{1,13},{5,9},{9,5},{13,1},{2,14},{6,10},... | collective-permute-start | bytes 196616 | tf_op jit(solution)/shard_map/ppermute | solution.py:35
  39.3 6.0 %collective-permute-start.13 = (bf16[8,4096]{1,0:T(8,128)(2,1)S(1)}, bf16[8,4096]{1,0:T(8,128)(2,1)S(1)}, u32[]{:S(2)}, u32[]{:S(2)}) collective-permute-start(bf16[8,4096]{1,0:T(8,128)(2,1)S(1)} %join.1.refs_0_.refs_1_), channel_id=1, source_target_pairs={{0,8},{4,12},{8,0},{12,4},{1,9},{5,13},{9,1},{13,5},{2,10},{6,14},... | collective-permute-start | bytes 196616 | tf_op jit(solution)/shard_map/ppermute | solution.py:35
  39.3 6.0 %collective-permute-start.12 = (bf16[8,4096]{1,0:T(8,128)(2,1)S(1)}, bf16[8,4096]{1,0:T(8,128)(2,1)S(1)}, u32[]{:S(2)}, u32[]{:S(2)}) collective-permute-start(bf16[8,4096]{1,0:T(8,128)(2,1)S(1)} %join.1.refs_0_.refs_1_), channel_id=1, source_target_pairs={{0,4},{4,0},{8,12},{12,8},{1,5},{5,1},{9,13},{13,9},{2,6},{6,2},{1... | collective-permute-start | bytes 196616 | tf_op jit(solution)/shard_map/ppermute | solution.py:35
  44.3 1.0 %copy-start.2 = (bf16[8,4096]{1,0:T(8,128)(2,1)S(1)}, bf16[8,4096]{1,0:T(8,128)(2,1)}, u32[]{:S(2)}) copy-start(bf16[8,4096]{1,0:T(8,128)(2,1)} %copy-done.1) | copy-start | bytes 196612

commit v17 on v16

--- a/solution.py
+++ b/solution.py
@@ -226,6 +226,24 @@
         cost_estimate=cost(flops, 4 * sum(shape.size for shape in shapes)),
         name="pack",
     )(routing, in_hbm(cache), *others)
+
+
+def gate_kernel(*refs):
+    pass
+
+
+def gate(values, others):
+    count = len(values)
+    return pl.pallas_call(
+        gate_kernel,
+        out_shape=[jax.ShapeDtypeStruct(value.shape, value.dtype) for value in values],
+        in_specs=[ANY] * (count + len(others)),
+        out_specs=[ANY] * count,
+        input_output_aliases={n: n for n in range(count)},
+        compiler_params=limit(1),
+        cost_estimate=cost(0, 0),
+        name="gate",
+    )(*values, *others)
 
 
 def place_kernel(pieces, *refs):
@@ -501,7 +519,8 @@
     whole = 2 * CAP
     near = [(offset, 0, whole) for offset in range(2)]
     head, tail = [(2, 0, 1)], [(2, 1, whole - 1)]
-    far = tail + [(offset, 0, whole) for offset in range(3, section_count)]
+    far = tail + [(offset, 0, whole) for offset in range(3, section_count - 1)]
+    far += [(section_count - 1, 0, whole - 1), (section_count - 1, whole - 1, 1)]
 
     def across(parts, pieces):
         return [swap(part, "sec", piece[0]) for part, piece in zip(parts, pieces)]
@@ -514,7 +533,7 @@
     far_caches, query_parts = first_pack(
         routing, prompt_key_values, queries, head_caches, far, section_count
     )
-    far_parts = across(far_caches, far)
+    far_parts = across(far_caches[:-1], far[:-1])
     query_parts = [swap(part, "sec", offset) for offset, part in enumerate(query_parts)]
     merged = merge(far_queries, head_parts)
     far_queries = spread(merged, "tp")
@@ -526,7 +545,8 @@
     partials = [swap(part, "tp", offset) for offset, part in enumerate(messages)]
     held_weight = [fetch(out_weight, [messages[0], *near_parts[1:]], 0, 2)]
     held_cache = place([], near_parts + head_parts, near + head, slot_count)
-    share = join(partials, [*held_weight, held_cache], samples, query_width // HEAD_SIZE // KEY_VALUE_HEADS)
+    share = join(partials, [*held_weight, held_cache, *far_parts[:-1]], samples, query_width // HEAD_SIZE // KEY_VALUE_HEADS)
+    far_parts += across(gate(far_caches[-1:], [share]), far[-1:])
     shares = spread(share, "tp")
     held_weight.append(fetch(out_weight, [share], 1, 2))
     if share.ndim == 3:
@@ -536,10 +556,11 @@
         layer_out = jnp.dot(attended, out_weight, preferred_element_type=jnp.float32)
         layer_out = layer_out.astype(jnp.bfloat16).reshape(REQ_GRP, samples, -1)
     else:
-        layer_out = project(shares, held_weight, far_parts[:-1], samples)
-
-    held_cache = place([held_cache, share], far_parts[:-1], far[:-1], slot_count)
-    held_cache = place([held_cache, layer_out], far_parts[-1:], far[-1:], slot_count)
+        layer_out = project(shares, held_weight, far_parts[:-2], samples)
+
+    held_cache = place([held_cache, share], far_parts[:-2], far[:-2], slot_count)
+    for part, piece in zip(far_parts[-2:], far[-2:]):
+        held_cache = place([held_cache, layer_out], [part], [piece], slot_count)
     held_cache = held_cache.reshape((1, slot_count) + prompt_key_values.shape[1:])
     return (layer_out, held_cache)
 

time: 52.3 us -> 52.7 us (level)
  waiting for transfers between devices: 5.62 us -> 4.63 us
  local copies, waits for them, and re-layouts: 0.92 us -> 1.75 us
  Pallas kernels: 24.4 us -> 25 us
    ppermute x16 -> x17, waiting for transfers between devices: 5.62 us -> 4.63 us  [swap(): return lax.ppermute(value, axis, [(i, i ^ offset) for i in range(count)])]
    unnamed x10, local copies, waits for them, and re-layouts: 0.92 us -> 1.75 us
    pallas_call x3 -> x4, Pallas kernels: 3.37 us -> 4 us  [place(): pl.pallas_call(functools.partial(place_kernel, pieces), out_shape=jax.Sha...]
    ppermute x16 -> x17, starting transfers between devices: 20.2 us -> 20.3 us  [swap(): return lax.ppermute(value, axis, [(i, i ^ offset) for i in range(count)])]
  transfers between devices with their start and end apart: 16 -> 17, of which waited for: 5 -> 6; matrix products, arithmetic and copies ran while one was open for 0% -> 0% of each run, Pallas kernels for 42% -> 43%
where the time goes in v17:
time: 52.7 us; the launch traced here: 52.4 us
  Pallas kernels  25 us (47%)
  starting transfers between devices  20.3 us (39%)
  waiting for transfers between devices  4.63 us (9%)
  local copies, waits for them, and re-layouts  1.75 us (3%)
  between operations  0.81 us (2%)
    ppermute x17, starting transfers between devices, swap(): return lax.ppermute(value, axis, [(i, i ^ offset) for i in range(count)])  20.3 us
    pallas_call x2, Pallas kernels, fetch(): pl.pallas_call(functools.partial(fetch_kernel, number * size), out_shape=...  7.09 us
    ppermute x17, waiting for transfers between devices, swap(): return lax.ppermute(value, axis, [(i, i ^ offset) for i in range(count)])  4.63 us
    pallas_call x4, Pallas kernels, place(): pl.pallas_call(functools.partial(place_kernel, pieces), out_shape=jax.Sha...  4 us
    pallas_call x1, Pallas kernels, attend(): pl.pallas_call(functools.partial(attend_kernel, pieces, section_count, tp...  3.77 us
    pallas_call x1, Pallas kernels, project(): pl.pallas_call(functools.partial(project_kernel, count, min(256, width),...  3.64 us
    pallas_call x1, Pallas kernels, pack(): pl.pallas_call(functools.partial(pack_kernel, pieces, section_count), out...  2.22 us
    pallas_call x1, Pallas kernels, first_pack(): pl.pallas_call(functools.partial(first_pack_kernel, pieces, section_count...  2.2 us
  transfers between devices with their start and end apart: 17, of which 6 were waited for; matrix products, arithmetic and copies ran while one was open for 0% of the time, Pallas kernels for 43%

profile of v17, /device:TPU:0, one launch (start us, length us, event | category | flops | bytes accessed | tf_op | source)
XLA Modules:
  0.0 52.4 jit_solution(11906717047809858512)
XLA Ops:
  0.6 1.7 %pack_head.1 = (bf16[1,256,512]{2,1,0:T(8,128)(2,1)S(1)}, bf16[2,4,1024]{2,1,0:T(4,128)(2,1)S(1)}, bf16[2,4,1024]{2,1,0:T(4,128)(2,1)S(1)}) custom-call(s32[32]{0:T(128)} %bitcast.3, bf16[8,2,256,512]{3,2,1,0:T(8,128)(2,1)} %cache_ref.5, bf16[1,8,4,4096]{3,2,1,0:T(4,128)(2,1)} %query_ref.3), custom_call_target="tpu_custom_call" | custom-call | bytes 2097152 | tf_op jit(solution)/shard_map/pack_head/pallas_call | solution.py:141
  2.3 3.0 %collective-permute-start.3 = (bf16[1,256,512]{2,1,0:T(8,128)(2,1)S(1)}, bf16[1,256,512]{2,1,0:T(8,128)(2,1)S(1)}, u32[]{:S(2)}, u32[]{:S(2)}) collective-permute-start(bf16[1,256,512]{2,1,0:T(8,128)(2,1)S(1)} %get-tuple-element.16.refs_0_), channel_id=1, source_target_pairs={{0,2},{1,3},{2,0},{3,1},{4,6},{5,7},{6,4},{7,5},{8,10},{9,11},{10,... | collective-permute-start | bytes 786440 | tf_op jit(solution)/shard_map/ppermute | solution.py:35
  5.3 0.1 collective-permute-start.1
  5.4 0.8 %collective-permute-start.2 = (bf16[2,4,1024]{2,1,0:T(4,128)(2,1)S(1)}, bf16[2,4,1024]{2,1,0:T(4,128)(2,1)S(1)}, u32[]{:S(2)}, u32[]{:S(2)}) collective-permute-start(bf16[2,4,1024]{2,1,0:T(4,128)(2,1)S(1)} %get-tuple-element.21), channel_id=1, source_target_pairs={{0,3},{1,2},{2,1},{3,0},{4,7},{5,6},{6,5},{7,4},{8,11},{9,10},{10,... | collective-permute-start | bytes 49160 | tf_op jit(solution)/shard_map/ppermute | solution.py:35
  6.2 2.2 %first_pack.1 = (bf16[3,256,512]{2,1,0:T(8,128)(2,1)S(1)}, bf16[3,256,512]{2,1,0:T(8,128)(2,1)S(1)}, bf16[1,256,512]{2,1,0:T(8,128)(2,1)S(1)}, bf16[2,4,4096]{2,1,0:T(4,128)(2,1)S(1)}, bf16[2,4,4096]{2,1,0:T(4,128)(2,1)S(1)}) custom-call(s32[32]{0:T(128)S(1)} %bitcast.4, bf16[8,2,256,512]{3,2,1,0:T(8,128)(2,1)} %cache_ref.5, ...), custom_call_target="tpu_custom_call" | custom-call | bytes 3932160 | tf_op jit(solution)/shard_map/first_pack/pallas_call | solution.py:199
  8.4 1.3 %collective-permute-start.4 = (bf16[2,4,4096]{2,1,0:T(4,128)(2,1)S(1)}, bf16[2,4,4096]{2,1,0:T(4,128)(2,1)S(1)}, u32[]{:S(2)}, u32[]{:S(2)}) collective-permute-start(bf16[2,4,4096]{2,1,0:T(4,128)(2,1)S(1)} %get-tuple-element.22), channel_id=1, source_target_pairs={{0,1},{1,0},{2,3},{3,2},{4,5},{5,4},{6,7},{7,6},{8,9},{9,8},{10,11... | collective-permute-start | bytes 196616 | tf_op jit(solution)/shard_map/ppermute | solution.py:35
  9.8 2.6 %collective-permute-done.1.refs_0_ = bf16[2,4,1024]{2,1,0:T(4,128)(2,1)S(1)} collective-permute-done((bf16[2,4,1024]{2,1,0:T(4,128)(2,1)S(1)}, bf16[2,4,1024]{2,1,0:T(4,128)(2,1)S(1)}, u32[]{:S(2)}, u32[]{:S(2)}) %collective-permute-start.1) | collective-permute-done | bytes 16416 | tf_op jit(solution)/shard_map/ppermute | solution.py:35
  12.4 0.3 collective-permute-done.2.refs_1_
  12.7 3.6 %collective-permute-start.7 = (bf16[2,2,4,1024]{3,2,1,0:T(4,128)(2,1)S(1)}, bf16[2,2,4,1024]{3,2,1,0:T(4,128)(2,1)S(1)}, u32[]{:S(2)}, u32[]{:S(2)}) collective-permute-start(bf16[2,2,4,1024]{3,2,1,0:T(4,128)(2,1)S(1)} %merge.1.refs_0_.refs_8_), channel_id=1, source_target_pairs={{0,12},{4,8},{8,4},{12,0},{1,13},{5,9},{9,5},{13,1},{2,14},{6,10},... | collective-permute-start | bytes 98312 | tf_op jit(solution)/shard_map/ppermute | solution.py:35
  16.3 0.9 %collective-permute-start.5 = (bf16[2,2,4,1024]{3,2,1,0:T(4,128)(2,1)S(1)}, bf16[2,2,4,1024]{3,2,1,0:T(4,128)(2,1)S(1)}, u32[]{:S(2)}, u32[]{:S(2)}) collective-permute-start(bf16[2,2,4,1024]{3,2,1,0:T(4,128)(2,1)S(1)} %merge.1.refs_0_.refs_8_), channel_id=1, source_target_pairs={{0,4},{4,0},{8,12},{12,8},{1,5},{5,1},{9,13},{13,9},{2,6},{6,2},{1... | collective-permute-start | bytes 98312 | tf_op jit(solution)/shard_map/ppermute | solution.py:35
  17.2 2.2 %pack.1 = (bf16[4,256,512]{2,1,0:T(8,128)(2,1)S(1)}, bf16[4,256,512]{2,1,0:T(8,128)(2,1)S(1)}) custom-call(s32[32]{0:T(128)S(1)} %bitcast.5, bf16[8,2,256,512]{3,2,1,0:T(8,128)(2,1)} %cache_ref.5, bf16[2,2,4,1024]{3,2,1,0:T(4,128)(2,1)S(1)} %merge.1.refs_0_.refs_8_, bf16[2,4,4096]{2,1,0:T(4,128)(2,1)S(1)} %collective-permute-done.4.refs_1_.refs_7_), custom_call_target="tpu_custom_call" | custom-call | flops 10000000000 | bytes 4194304 | tf_op jit(solution)/shard_map/pack/pallas_call | solution.py:217
  19.4 1.5 %collective-permute-start.11 = (bf16[4,256,512]{2,1,0:T(8,128)(2,1)S(1)}, bf16[4,256,512]{2,1,0:T(8,128)(2,1)S(1)}, u32[]{:S(2)}, u32[]{:S(2)}) collective-permute-start(bf16[4,256,512]{2,1,0:T(8,128)(2,1)S(1)} %get-tuple-element.24.refs_5_), channel_id=1, source_target_pairs={{0,1},{1,0},{2,3},{3,2},{4,5},{5,4},{6,7},{7,6},{8,9},{9,8},{10,11... | collective-permute-start | bytes 3145736 | tf_op jit(solution)/shard_map/ppermute | solution.py:35
  21.0 0.6 %collective-permute-done.6.refs_10_ = bf16[2,2,4,1024]{3,2,1,0:T(4,128)(2,1)S(1)} collective-permute-done((bf16[2,2,4,1024]{3,2,1,0:T(4,128)(2,1)S(1)}, bf16[2,2,4,1024]{3,2,1,0:T(4,128)(2,1)S(1)}, u32[]{:S(2)}, u32[]{:S(2)}) %collective-permute-start.6) | collective-permute-done | bytes 32800 | tf_op jit(solution)/shard_map/ppermute | solution.py:35
  21.6 3.8 %attend.1 = (bf16[272,128]{1,0:T(8,128)(2,1)S(1)}, bf16[272,128]{1,0:T(8,128)(2,1)S(1)}, bf16[272,128]{1,0:T(8,128)(2,1)S(1)}, bf16[272,128]{1,0:T(8,128)(2,1)S(1)}) custom-call(s32[32]{0:T(128)S(1)} %bitcast.6, s32[32]{0:T(128)S(1)} %copy-done.4, bf16[1,256,512]{2,1,0:T(8,128)(2,1)S(1)} %get-tuple-element.16.refs_0_, ...), custom_call_target="tpu_custom_call" | custom-call | flops 20000000000 | bytes 4194304 | tf_op jit(solution)/shard_map/attend/pallas_call | solution.py:365
  25.4 0.9 %collective-permute-start.8 = (bf16[272,128]{1,0:T(8,128)(2,1)S(1)}, bf16[272,128]{1,0:T(8,128)(2,1)S(1)}, u32[]{:S(2)}, u32[]{:S(2)}) collective-permute-start(bf16[272,128]{1,0:T(8,128)(2,1)S(1)} %get-tuple-element.27), channel_id=1, source_target_pairs={{0,4},{4,0},{8,12},{12,8},{1,5},{5,1},{9,13},{13,9},{2,6},{6,2},{1... | collective-permute-start | bytes 208904 | tf_op jit(solution)/shard_map/ppermute | solution.py:35
  26.2 2.6 %collective-permute-start.9 = (bf16[272,128]{1,0:T(8,128)(2,1)S(1)}, bf16[272,128]{1,0:T(8,128)(2,1)S(1)}, u32[]{:S(2)}, u32[]{:S(2)}) collective-permute-start(bf16[272,128]{1,0:T(8,128)(2,1)S(1)} %get-tuple-element.28), channel_id=1, source_target_pairs={{0,8},{4,12},{8,0},{12,4},{1,9},{5,13},{9,1},{13,5},{2,10},{6,14},... | collective-permute-start | bytes 208904 | tf_op jit(solution)/shard_map/ppermute | solution.py:35
  28.9 1.0 %collective-permute-start.10 = (bf16[272,128]{1,0:T(8,128)(2,1)S(1)}, bf16[272,128]{1,0:T(8,128)(2,1)S(1)}, u32[]{:S(2)}, u32[]{:S(2)}) collective-permute-start(bf16[272,128]{1,0:T(8,128)(2,1)S(1)} %get-tuple-element.29), channel_id=1, source_target_pairs={{0,12},{4,8},{8,4},{12,0},{1,13},{5,9},{9,5},{13,1},{2,14},{6,10},... | collective-permute-start | bytes 208904 | tf_op jit(solution)/shard_map/ppermute | solution.py:35
  29.8 1.5 %place.4.refs_5_.refs_0_ = bf16[1,16,256,512]{3,2,1,0:T(8,128)(2,1)} custom-call(bf16[4,256,512]{2,1,0:T(8,128)(2,1)S(1)} %get-tuple-element.23.refs_4_.refs_0_, bf16[4,256,512]{2,1,0:T(8,128)(2,1)S(1)} %collective-permute-done.11.refs_1_, bf16[1,256,512]{2,1,0:T(8,128)(2,1)S(1)} %collective-permute-done.3.refs_2_), custom_call_target="tpu_custom_call" | custom-call | bytes 4718592 | tf_op jit(solution)/shard_map/place/pallas_call | solution.py:265
  31.3 3.6 %fetch.2.refs_4_.refs_5_ = bf16[2048,2048]{1,0:T(8,128)(2,1)S(1)} custom-call(bf16[4096,2048]{1,0:T(8,128)(2,1)} %weight_ref.3, bf16[272,128]{1,0:T(8,128)(2,1)S(1)} %get-tuple-element.26.refs_0_, bf16[4,256,512]{2,1,0:T(8,128)(2,1)S(1)} %collective-permute-done.11.refs_1_), custom_call_target="tpu_custom_call" | custom-call | bytes 16777216 | tf_op jit(solution)/shard_map/fetch/pallas_call | solution.py:458
  35.0 0.1 collective-permute-done.10.refs_3_
  35.1 0.9 %copy-done = bf16[1,16,256,512]{3,2,1,0:T(8,128)(2,1)S(1)} copy-done((bf16[1,16,256,512]{3,2,1,0:T(8,128)(2,1)S(1)}, bf16[1,16,256,512]{3,2,1,0:T(8,128)(2,1)}, u32[]{:S(2)}) %copy-start) | copy-done | bytes 4194328
  36.0 0.4 join.1.refs_0_.refs_1_
  36.5 2.9 %collective-permute-start.14 = (bf16[8,4096]{1,0:T(8,128)(2,1)S(1)}, bf16[8,4096]{1,0:T(8,128)(2,1)S(1)}, u32[]{:S(2)}, u32[]{:S(2)}) collective-permute-start(bf16[8,4096]{1,0:T(8,128)(2,1)S(1)} %join.1.refs_0_.refs_1_), channel_id=1, source_target_pairs={{0,12},{4,8},{8,4},{12,0},{1,13},{5,9},{9,5},{13,1},{2,14},{6,10},... | collective-permute-start | bytes 196616 | tf_op jit(solution)/shard_map/ppermute | solution.py:35
  39.4 1.5 %collective-permute-start.12 = (bf16[8,4096]{1,0:T(8,128)(2,1)S(1)}, bf16[8,4096]{1,0:T(8,128)(2,1)S(1)}, u32[]{:S(2)}, u32[]{:S(2)}) collective-permute-start(bf16[8,4096]{1,0:T(8,128)(2,1)S(1)} %join.1.refs_0_.refs_1_), channel_id=1, source_target_pairs={{0,4},{4,0},{8,12},{12,8},{1,5},{5,1},{9,13},{13,9},{2,6},{6,2},{1... | collective-permute-start | bytes 196616 | tf_op jit(solution)/shard_map/ppermute | solution.py:35
  40.9 3.5 %fetch.3.refs_6_ = bf16[2048,2048]{1,0:T(8,128)(2,1)S(1)} custom-call(bf16[4096,2048]{1,0:T(8,128)(2,1)} %weight_ref.3, bf16[8,4096]{1,0:T(8,128)(2,1)S(1)} %join.1.refs_0_.refs_1_), custom_call_target="tpu_custom_call" | custom-call | bytes 16777216 | tf_op jit(solution)/shard_map/fetch/pallas_call | solution.py:458
  44.4 0.9 %place.5.refs_0_ = bf16[1,16,256,512]{3,2,1,0:T(8,128)(2,1)} custom-call(bf16[1,16,256,512]{3,2,1,0:T(8,128)(2,1)} %place.4.refs_5_.refs_0_, bf16[8,4096]{1,0:T(8,128)(2,1)} %copy-done.1, bf16[3,256,512]{2,1,0:T(8,128)(2,1)S(1)} %collective-permute-done.refs_6_.refs_0_.refs_2_), custom_call_target="tpu_custom_call", output_to_operand_aliasing={{}: (0, {})} | custom-call | bytes 1572864 | tf_op jit(solution)/shard_map/place/pallas_call | solution.py:265
  45.3 0.9 %collective-permute-done.13.refs_3_ = bf16[8,4096]{1,0:T(8,128)(2,1)S(1)} collective-permute-done((bf16[8,4096]{1,0:T(8,128)(2,1)S(1)}, bf16[8,4096]{1,0:T(8,128)(2,1)S(1)}, u32[]{:S(2)}, u32[]{:S(2)}) %collective-permute-start.13) | collective-permute-done | bytes 65568 | tf_op jit(solution)/shard_map/ppermute | solution.py:35
  46.2 0.1 collective-permute-done.12.refs_2_
  46.3 0.8 %copy-done.2 = bf16[8,4096]{1,0:T(8,128)(2,1)S(1)} copy-done((bf16[8,4096]{1,0:T(8,128)(2,1)S(1)}, bf16[8,4096]{1,0:T(8,128)(2,1)}, u32[]{:S(2)}) %copy-start.2) | copy-done | bytes 65560
  47.1 3.6 %project.1.refs_1_ = bf16[8,4,2048]{2,1,0:T(4,128)(2,1)} custom-call(bf16[3,256,512]{2,1,0:T(8,128)(2,1)S(1)} %collective-permute-done.refs_6_.refs_0_.refs_2_, bf16[8,4096]{1,0:T(8,128)(2,1)S(1)} %copy-done.2, bf16[8,4096]{1,0:T(8,128)(2,1)S(1)} %collective-permute-done.12.refs_2_, bf16[8,4096]{1,0:T(8,128)(2,1)S(1)} %collective-permute-done.13.refs_3_, ...), custom_call_target="tpu_custom_call" | custom-call | flops 536870912 | bytes 16777216 | tf_op jit(solution)/shard_map/project/pallas_call | solution.py:502
  50.8 0.9 %place.6.refs_0_ = bf16[1,16,256,512]{3,2,1,0:T(8,128)(2,1)} custom-call(bf16[1,16,256,512]{3,2,1,0:T(8,128)(2,1)} %place.5.refs_0_, bf16[8,4,2048]{2,1,0:T(4,128)(2,1)} %project.1.refs_1_, bf16[3,256,512]{2,1,0:T(8,128)(2,1)S(1)} %collective-permute-done.15.refs_2_), custom_call_target="tpu_custom_call", output_to_operand_aliasing={{}: (0, {})} | custom-call | bytes 1572864 | tf_op jit(solution)/shard_map/place/pallas_call | solution.py:265
  51.7 0.7 %place.7 = bf16[1,16,256,512]{3,2,1,0:T(8,128)(2,1)} custom-call(bf16[1,16,256,512]{3,2,1,0:T(8,128)(2,1)} %place.6.refs_0_, bf16[8,4,2048]{2,1,0:T(4,128)(2,1)} %project.1.refs_1_, bf16[1,256,512]{2,1,0:T(8,128)(2,1)S(1)} %collective-permute-done.16.refs_2_), custom_call_target="tpu_custom_call", output_to_operand_aliasing={{}: (0, {})} | custom-call | bytes 524288 | tf_op jit(solution)/shard_map/place/pallas_call | solution.py:265
  (26 shorter events, 0.2 us)
Async XLA Ops:
  0.6 5.6 %copy-start.3 = (s32[32,1]{0,1:T(1,128)S(1)}, s32[32,1]{0,1:T(1,128)}, u32[]{:S(2)}) copy-start(s32[32,1]{0,1:T(1,128)} %param.7) | copy-start | bytes 388
  2.3 10.4 %collective-permute-start.3 = (bf16[1,256,512]{2,1,0:T(8,128)(2,1)S(1)}, bf16[1,256,512]{2,1,0:T(8,128)(2,1)S(1)}, u32[]{:S(2)}, u32[]{:S(2)}) collective-permute-start(bf16[1,256,512]{2,1,0:T(8,128)(2,1)S(1)} %get-tuple-element.16.refs_0_), channel_id=1, source_target_pairs={{0,2},{1,3},{2,0},{3,1},{4,6},{5,7},{6,4},{7,5},{8,10},{9,11},{10,... | collective-permute-start | bytes 786440 | tf_op jit(solution)/shard_map/ppermute | solution.py:35
  5.3 7.1 %collective-permute-start.1 = (bf16[2,4,1024]{2,1,0:T(4,128)(2,1)S(1)}, bf16[2,4,1024]{2,1,0:T(4,128)(2,1)S(1)}, u32[]{:S(2)}, u32[]{:S(2)}) collective-permute-start(bf16[2,4,1024]{2,1,0:T(4,128)(2,1)S(1)} %get-tuple-element.20), channel_id=1, source_target_pairs={{0,2},{1,3},{2,0},{3,1},{4,6},{5,7},{6,4},{7,5},{8,10},{9,11},{10,... | collective-permute-start | bytes 49160 | tf_op jit(solution)/shard_map/ppermute | solution.py:35
  5.4 7.3 %collective-permute-start.2 = (bf16[2,4,1024]{2,1,0:T(4,128)(2,1)S(1)}, bf16[2,4,1024]{2,1,0:T(4,128)(2,1)S(1)}, u32[]{:S(2)}, u32[]{:S(2)}) collective-permute-start(bf16[2,4,1024]{2,1,0:T(4,128)(2,1)S(1)} %get-tuple-element.21), channel_id=1, source_target_pairs={{0,3},{1,2},{2,1},{3,0},{4,7},{5,6},{6,5},{7,4},{8,11},{9,10},{10,... | collective-permute-start | bytes 49160 | tf_op jit(solution)/shard_map/ppermute | solution.py:35
  8.4 7.9 %collective-permute-start.4 = (bf16[2,4,4096]{2,1,0:T(4,128)(2,1)S(1)}, bf16[2,4,4096]{2,1,0:T(4,128)(2,1)S(1)}, u32[]{:S(2)}, u32[]{:S(2)}) collective-permute-start(bf16[2,4,4096]{2,1,0:T(4,128)(2,1)S(1)} %get-tuple-element.22), channel_id=1, source_target_pairs={{0,1},{1,0},{2,3},{3,2},{4,5},{5,4},{6,7},{7,6},{8,9},{9,8},{10,11... | collective-permute-start | bytes 196616 | tf_op jit(solution)/shard_map/ppermute | solution.py:35
  9.7 25.3 %collective-permute-start = (bf16[3,256,512]{2,1,0:T(8,128)(2,1)S(1)}, bf16[3,256,512]{2,1,0:T(8,128)(2,1)S(1)}, u32[]{:S(2)}, u32[]{:S(2)}) collective-permute-start(bf16[3,256,512]{2,1,0:T(8,128)(2,1)S(1)} %get-tuple-element.17.refs_1_), channel_id=1, source_target_pairs={{0,2},{1,3},{2,0},{3,1},{4,6},{5,7},{6,4},{7,5},{8,10},{9,11},{10,... | collective-permute-start | bytes 2359304 | tf_op jit(solution)/shard_map/ppermute | solution.py:35
  12.4 38.4 %collective-permute-start.15 = (bf16[3,256,512]{2,1,0:T(8,128)(2,1)S(1)}, bf16[3,256,512]{2,1,0:T(8,128)(2,1)S(1)}, u32[]{:S(2)}, u32[]{:S(2)}) collective-permute-start(bf16[3,256,512]{2,1,0:T(8,128)(2,1)S(1)} %get-tuple-element.18.refs_2_), channel_id=1, source_target_pairs={{0,3},{1,2},{2,1},{3,0},{4,7},{5,6},{6,5},{7,4},{8,11},{9,10},{10,... | collective-permute-start | bytes 2359304 | tf_op jit(solution)/shard_map/ppermute | solution.py:35
  12.7 8.8 %copy-start.4 = (s32[32]{0:T(128)S(1)}, s32[32]{0:T(128)}, u32[]{:S(2)}) copy-start(s32[32]{0:T(128)} %lengths_ref.1) | copy-start | bytes 388
  12.7 6.7 %collective-permute-start.7 = (bf16[2,2,4,1024]{3,2,1,0:T(4,128)(2,1)S(1)}, bf16[2,2,4,1024]{3,2,1,0:T(4,128)(2,1)S(1)}, u32[]{:S(2)}, u32[]{:S(2)}) collective-permute-start(bf16[2,2,4,1024]{3,2,1,0:T(4,128)(2,1)S(1)} %merge.1.refs_0_.refs_8_), channel_id=1, source_target_pairs={{0,12},{4,8},{8,4},{12,0},{1,13},{5,9},{9,5},{13,1},{2,14},{6,10},... | collective-permute-start | bytes 98312 | tf_op jit(solution)/shard_map/ppermute | solution.py:35
  16.3 5.3 %collective-permute-start.6 = (bf16[2,2,4,1024]{3,2,1,0:T(4,128)(2,1)S(1)}, bf16[2,2,4,1024]{3,2,1,0:T(4,128)(2,1)S(1)}, u32[]{:S(2)}, u32[]{:S(2)}) collective-permute-start(bf16[2,2,4,1024]{3,2,1,0:T(4,128)(2,1)S(1)} %merge.1.refs_0_.refs_8_), channel_id=1, source_target_pairs={{0,8},{4,12},{8,0},{12,4},{1,9},{5,13},{9,1},{13,5},{2,10},{6,14},... | collective-permute-start | bytes 98312 | tf_op jit(solution)/shard_map/ppermute | solution.py:35
  16.3 5.3 %collective-permute-start.5 = (bf16[2,2,4,1024]{3,2,1,0:T(4,128)(2,1)S(1)}, bf16[2,2,4,1024]{3,2,1,0:T(4,128)(2,1)S(1)}, u32[]{:S(2)}, u32[]{:S(2)}) collective-permute-start(bf16[2,2,4,1024]{3,2,1,0:T(4,128)(2,1)S(1)} %merge.1.refs_0_.refs_8_), channel_id=1, source_target_pairs={{0,4},{4,0},{8,12},{12,8},{1,5},{5,1},{9,13},{13,9},{2,6},{6,2},{1... | collective-permute-start | bytes 98312 | tf_op jit(solution)/shard_map/ppermute | solution.py:35
  19.4 9.4 %collective-permute-start.11 = (bf16[4,256,512]{2,1,0:T(8,128)(2,1)S(1)}, bf16[4,256,512]{2,1,0:T(8,128)(2,1)S(1)}, u32[]{:S(2)}, u32[]{:S(2)}) collective-permute-start(bf16[4,256,512]{2,1,0:T(8,128)(2,1)S(1)} %get-tuple-element.24.refs_5_), channel_id=1, source_target_pairs={{0,1},{1,0},{2,3},{3,2},{4,5},{5,4},{6,7},{7,6},{8,9},{9,8},{10,11... | collective-permute-start | bytes 3145736 | tf_op jit(solution)/shard_map/ppermute | solution.py:35
  25.4 9.6 %collective-permute-start.8 = (bf16[272,128]{1,0:T(8,128)(2,1)S(1)}, bf16[272,128]{1,0:T(8,128)(2,1)S(1)}, u32[]{:S(2)}, u32[]{:S(2)}) collective-permute-start(bf16[272,128]{1,0:T(8,128)(2,1)S(1)} %get-tuple-element.27), channel_id=1, source_target_pairs={{0,4},{4,0},{8,12},{12,8},{1,5},{5,1},{9,13},{13,9},{2,6},{6,2},{1... | collective-permute-start | bytes 208904 | tf_op jit(solution)/shard_map/ppermute | solution.py:35
  26.2 8.8 %collective-permute-start.9 = (bf16[272,128]{1,0:T(8,128)(2,1)S(1)}, bf16[272,128]{1,0:T(8,128)(2,1)S(1)}, u32[]{:S(2)}, u32[]{:S(2)}) collective-permute-start(bf16[272,128]{1,0:T(8,128)(2,1)S(1)} %get-tuple-element.28), channel_id=1, source_target_pairs={{0,8},{4,12},{8,0},{12,4},{1,9},{5,13},{9,1},{13,5},{2,10},{6,14},... | collective-permute-start | bytes 208904 | tf_op jit(solution)/shard_map/ppermute | solution.py:35
  28.9 6.2 %collective-permute-start.10 = (bf16[272,128]{1,0:T(8,128)(2,1)S(1)}, bf16[272,128]{1,0:T(8,128)(2,1)S(1)}, u32[]{:S(2)}, u32[]{:S(2)}) collective-permute-start(bf16[272,128]{1,0:T(8,128)(2,1)S(1)} %get-tuple-element.29), channel_id=1, source_target_pairs={{0,12},{4,8},{8,4},{12,0},{1,13},{5,9},{9,5},{13,1},{2,14},{6,10},... | collective-permute-start | bytes 208904 | tf_op jit(solution)/shard_map/ppermute | solution.py:35
  31.3 4.7 %copy-start = (bf16[1,16,256,512]{3,2,1,0:T(8,128)(2,1)S(1)}, bf16[1,16,256,512]{3,2,1,0:T(8,128)(2,1)}, u32[]{:S(2)}) copy-start(bf16[1,16,256,512]{3,2,1,0:T(8,128)(2,1)} %place.4.refs_5_.refs_0_) | copy-start | bytes 12582916
  36.4 8.0 %copy-start.1 = (bf16[8,4096]{1,0:T(8,128)(2,1)}, bf16[8,4096]{1,0:T(8,128)(2,1)S(1)}, u32[]{:S(2)}) copy-start(bf16[8,4096]{1,0:T(8,128)(2,1)S(1)} %join.1.refs_0_.refs_1_) | copy-start | bytes 196612
  36.4 15.3 %collective-permute-start.16 = (bf16[1,256,512]{2,1,0:T(8,128)(2,1)S(1)}, bf16[1,256,512]{2,1,0:T(8,128)(2,1)S(1)}, u32[]{:S(2)}, u32[]{:S(2)}) collective-permute-start(bf16[1,256,512]{2,1,0:T(8,128)(2,1)S(1)} %gate.1), channel_id=1, source_target_pairs={{0,3},{1,2},{2,1},{3,0},{4,7},{5,6},{6,5},{7,4},{8,11},{9,10},{10,... | collective-permute-start | bytes 786440 | tf_op jit(solution)/shard_map/ppermute | solution.py:35
  36.5 8.9 %collective-permute-start.14 = (bf16[8,4096]{1,0:T(8,128)(2,1)S(1)}, bf16[8,4096]{1,0:T(8,128)(2,1)S(1)}, u32[]{:S(2)}, u32[]{:S(2)}) collective-permute-start(bf16[8,4096]{1,0:T(8,128)(2,1)S(1)} %join.1.refs_0_.refs_1_), channel_id=1, source_target_pairs={{0,12},{4,8},{8,4},{12,0},{1,13},{5,9},{9,5},{13,1},{2,14},{6,10},... | collective-permute-start | bytes 196616 | tf_op jit(solution)/shard_map/ppermute | solution.py:35
  39.4 6.8 %collective-permute-start.13 = (bf16[8,4096]{1,0:T(8,128)(2,1)S(1)}, bf16[8,4096]{1,0:T(8,128)(2,1)S(1)}, u32[]{:S(2)}, u32[]{:S(2)}) collective-permute-start(bf16[8,4096]{1,0:T(8,128)(2,1)S(1)} %join.1.refs_0_.refs_1_), channel_id=1, source_target_pairs={{0,8},{4,12},{8,0},{12,4},{1,9},{5,13},{9,1},{13,5},{2,10},{6,14},... | collective-permute-start | bytes 196616 | tf_op jit(solution)/shard_map/ppermute | solution.py:35
  39.4 6.9 %collective-permute-start.12 = (bf16[8,4096]{1,0:T(8,128)(2,1)S(1)}, bf16[8,4096]{1,0:T(8,128)(2,1)S(1)}, u32[]{:S(2)}, u32[]{:S(2)}) collective-permute-start(bf16[8,4096]{1,0:T(8,128)(2,1)S(1)} %join.1.refs_0_.refs_1_), channel_id=1, source_target_pairs={{0,4},{4,0},{8,12},{12,8},{1,5},{5,1},{9,13},{13,9},{2,6},{6,2},{1... | collective-permute-start | bytes 196616 | tf_op jit(solution)/shard_map/ppermute | solution.py:35
  46.3 0.8 %copy-start.2 = (bf16[8,4096]{1,0:T(8,128)(2,1)S(1)}, bf16[8,4096]{1,0:T(8,128)(2,1)}, u32[]{:S(2)}) copy-start(bf16[8,4096]{1,0:T(8,128)(2,1)} %copy-done.1) | copy-start | bytes 196612

commit v18 on v17

--- a/solution.py
+++ b/solution.py
@@ -260,19 +260,19 @@
         copy.wait()
 
 
-def place(given, parts, pieces, slot_count):
+def place(given, others, parts, pieces, slot_count):
     part = parts[0]
     return pl.pallas_call(
         functools.partial(place_kernel, pieces),
         out_shape=jax.ShapeDtypeStruct((1, 2 * slot_count) + part.shape[1:], part.dtype),
-        in_specs=[HBM] * len(given) + [VMEM] * len(parts),
+        in_specs=[HBM] * len(given) + [ANY] * len(others) + [VMEM] * len(parts),
         out_specs=HBM,
         scratch_shapes=[pltpu.SemaphoreType.DMA((sum(len(part) for part in parts),))],
         input_output_aliases={0: 0} if given else {},
         compiler_params=limit(8),
         cost_estimate=cost(0, 4 * sum(piece.size for piece in parts)),
         name="place",
-    )(*[in_hbm(value) for value in given], *parts)
+    )(*[in_hbm(value) for value in given], *others, *parts)
 
 
 def attend_kernel(pieces, section_count, tp_count, routing_ref, lengths_ref, *refs):
@@ -544,8 +544,8 @@
     messages = attend(routing, lengths, caches, pieces, query_parts, far_queries)
     partials = [swap(part, "tp", offset) for offset, part in enumerate(messages)]
     held_weight = [fetch(out_weight, [messages[0], *near_parts[1:]], 0, 2)]
-    held_cache = place([], near_parts + head_parts, near + head, slot_count)
-    share = join(partials, [*held_weight, held_cache, *far_parts[:-1]], samples, query_width // HEAD_SIZE // KEY_VALUE_HEADS)
+    held_cache = place([], [], near_parts + head_parts, near + head, slot_count)
+    share = join(partials, [in_hbm(held_cache), *held_weight, *far_parts[:-1]], samples, query_width // HEAD_SIZE // KEY_VALUE_HEADS)
     far_parts += across(gate(far_caches[-1:], [share]), far[-1:])
     shares = spread(share, "tp")
     held_weight.append(fetch(out_weight, [share], 1, 2))
@@ -558,9 +558,9 @@
     else:
         layer_out = project(shares, held_weight, far_parts[:-2], samples)
 
-    held_cache = place([held_cache, share], far_parts[:-2], far[:-2], slot_count)
+    held_cache = place([held_cache], [share], far_parts[:-2], far[:-2], slot_count)
     for part, piece in zip(far_parts[-2:], far[-2:]):
-        held_cache = place([held_cache, layer_out], [part], [piece], slot_count)
+        held_cache = place([held_cache, layer_out], [], [part], [piece], slot_count)
     held_cache = held_cache.reshape((1, slot_count) + prompt_key_values.shape[1:])
     return (layer_out, held_cache)
 

time: 52.7 us -> 52 us (0.987)
  local copies, waits for them, and re-layouts: 1.75 us -> 0.01 us
  waiting for transfers between devices: 4.63 us -> 5.74 us
    unnamed x10 -> x4, local copies, waits for them, and re-layouts: 1.75 us -> 0.01 us
    ppermute x17, waiting for transfers between devices: 4.63 us -> 5.74 us  [swap(): return lax.ppermute(value, axis, [(i, i ^ offset) for i in range(count)])]
  transfers between devices with their start and end apart: 17 -> 17, of which waited for: 6 -> 6; matrix products, arithmetic and copies ran while one was open for 0% -> 0% of each run, Pallas kernels for 43% -> 44%
where the time goes in v18:
time: 52 us; the launch traced here: 51.6 us
  Pallas kernels  24.8 us (48%)
  starting transfers between devices  20.3 us (39%)
  waiting for transfers between devices  5.74 us (11%)
  between operations  0.78 us (2%)
    ppermute x17, starting transfers between devices, swap(): return lax.ppermute(value, axis, [(i, i ^ offset) for i in range(count)])  20.3 us
    pallas_call x2, Pallas kernels, fetch(): pl.pallas_call(functools.partial(fetch_kernel, number * size), out_shape=...  6.95 us
    ppermute x17, waiting for transfers between devices, swap(): return lax.ppermute(value, axis, [(i, i ^ offset) for i in range(count)])  5.74 us
    pallas_call x4, Pallas kernels, place(): pl.pallas_call(functools.partial(place_kernel, pieces), out_shape=jax.Sha...  3.99 us
    pallas_call x1, Pallas kernels, attend(): pl.pallas_call(functools.partial(attend_kernel, pieces, section_count, tp...  3.77 us
    pallas_call x1, Pallas kernels, project(): pl.pallas_call(functools.partial(project_kernel, count, min(256, width),...  3.64 us
    pallas_call x1, Pallas kernels, pack(): pl.pallas_call(functools.partial(pack_kernel, pieces, section_count), out...  2.22 us
    pallas_call x1, Pallas kernels, first_pack(): pl.pallas_call(functools.partial(first_pack_kernel, pieces, section_count...  2.2 us
  transfers between devices with their start and end apart: 17, of which 6 were waited for; matrix products, arithmetic and copies ran while one was open for 0% of the time, Pallas kernels for 44%

profile of v18, /device:TPU:0, one launch (start us, length us, event | category | flops | bytes accessed | tf_op | source)
XLA Modules:
  0.0 51.6 jit_solution(5122980094421546982)
XLA Ops:
  0.6 1.7 %pack_head.1 = (bf16[1,256,512]{2,1,0:T(8,128)(2,1)S(1)}, bf16[2,4,1024]{2,1,0:T(4,128)(2,1)S(1)}, bf16[2,4,1024]{2,1,0:T(4,128)(2,1)S(1)}) custom-call(s32[32]{0:T(128)} %bitcast.2, bf16[8,2,256,512]{3,2,1,0:T(8,128)(2,1)} %cache_ref.5, bf16[1,8,4,4096]{3,2,1,0:T(4,128)(2,1)} %query_ref.3), custom_call_target="tpu_custom_call" | custom-call | bytes 2097152 | tf_op jit(solution)/shard_map/pack_head/pallas_call | solution.py:141
  2.3 3.0 %collective-permute-start.3 = (bf16[1,256,512]{2,1,0:T(8,128)(2,1)S(1)}, bf16[1,256,512]{2,1,0:T(8,128)(2,1)S(1)}, u32[]{:S(2)}, u32[]{:S(2)}) collective-permute-start(bf16[1,256,512]{2,1,0:T(8,128)(2,1)S(1)} %get-tuple-element.16.refs_0_), channel_id=1, source_target_pairs={{0,2},{1,3},{2,0},{3,1},{4,6},{5,7},{6,4},{7,5},{8,10},{9,11},{10,... | collective-permute-start | bytes 786440 | tf_op jit(solution)/shard_map/ppermute | solution.py:35
  5.3 0.1 collective-permute-start.1
  5.4 0.8 %collective-permute-start.2 = (bf16[2,4,1024]{2,1,0:T(4,128)(2,1)S(1)}, bf16[2,4,1024]{2,1,0:T(4,128)(2,1)S(1)}, u32[]{:S(2)}, u32[]{:S(2)}) collective-permute-start(bf16[2,4,1024]{2,1,0:T(4,128)(2,1)S(1)} %get-tuple-element.21), channel_id=1, source_target_pairs={{0,3},{1,2},{2,1},{3,0},{4,7},{5,6},{6,5},{7,4},{8,11},{9,10},{10,... | collective-permute-start | bytes 49160 | tf_op jit(solution)/shard_map/ppermute | solution.py:35
  6.2 2.2 %first_pack.1 = (bf16[3,256,512]{2,1,0:T(8,128)(2,1)S(1)}, bf16[3,256,512]{2,1,0:T(8,128)(2,1)S(1)}, bf16[1,256,512]{2,1,0:T(8,128)(2,1)S(1)}, bf16[2,4,4096]{2,1,0:T(4,128)(2,1)S(1)}, bf16[2,4,4096]{2,1,0:T(4,128)(2,1)S(1)}) custom-call(s32[32]{0:T(128)S(1)} %bitcast.3, bf16[8,2,256,512]{3,2,1,0:T(8,128)(2,1)} %cache_ref.5, ...), custom_call_target="tpu_custom_call" | custom-call | bytes 3932160 | tf_op jit(solution)/shard_map/first_pack/pallas_call | solution.py:199
  8.4 1.3 %collective-permute-start.4 = (bf16[2,4,4096]{2,1,0:T(4,128)(2,1)S(1)}, bf16[2,4,4096]{2,1,0:T(4,128)(2,1)S(1)}, u32[]{:S(2)}, u32[]{:S(2)}) collective-permute-start(bf16[2,4,4096]{2,1,0:T(4,128)(2,1)S(1)} %get-tuple-element.22), channel_id=1, source_target_pairs={{0,1},{1,0},{2,3},{3,2},{4,5},{5,4},{6,7},{7,6},{8,9},{9,8},{10,11... | collective-permute-start | bytes 196616 | tf_op jit(solution)/shard_map/ppermute | solution.py:35
  9.7 0.1 collective-permute-start
  9.8 2.6 %collective-permute-done.1.refs_0_ = bf16[2,4,1024]{2,1,0:T(4,128)(2,1)S(1)} collective-permute-done((bf16[2,4,1024]{2,1,0:T(4,128)(2,1)S(1)}, bf16[2,4,1024]{2,1,0:T(4,128)(2,1)S(1)}, u32[]{:S(2)}, u32[]{:S(2)}) %collective-permute-start.1) | collective-permute-done | bytes 16416 | tf_op jit(solution)/shard_map/ppermute | solution.py:35
  12.4 0.3 collective-permute-done.2.refs_1_
  12.7 3.6 %collective-permute-start.7 = (bf16[2,2,4,1024]{3,2,1,0:T(4,128)(2,1)S(1)}, bf16[2,2,4,1024]{3,2,1,0:T(4,128)(2,1)S(1)}, u32[]{:S(2)}, u32[]{:S(2)}) collective-permute-start(bf16[2,2,4,1024]{3,2,1,0:T(4,128)(2,1)S(1)} %merge.1.refs_0_.refs_8_), channel_id=1, source_target_pairs={{0,12},{4,8},{8,4},{12,0},{1,13},{5,9},{9,5},{13,1},{2,14},{6,10},... | collective-permute-start | bytes 98312 | tf_op jit(solution)/shard_map/ppermute | solution.py:35
  16.3 0.9 %collective-permute-start.5 = (bf16[2,2,4,1024]{3,2,1,0:T(4,128)(2,1)S(1)}, bf16[2,2,4,1024]{3,2,1,0:T(4,128)(2,1)S(1)}, u32[]{:S(2)}, u32[]{:S(2)}) collective-permute-start(bf16[2,2,4,1024]{3,2,1,0:T(4,128)(2,1)S(1)} %merge.1.refs_0_.refs_8_), channel_id=1, source_target_pairs={{0,4},{4,0},{8,12},{12,8},{1,5},{5,1},{9,13},{13,9},{2,6},{6,2},{1... | collective-permute-start | bytes 98312 | tf_op jit(solution)/shard_map/ppermute | solution.py:35
  17.2 2.2 %pack.1 = (bf16[4,256,512]{2,1,0:T(8,128)(2,1)S(1)}, bf16[4,256,512]{2,1,0:T(8,128)(2,1)S(1)}) custom-call(s32[32]{0:T(128)S(1)} %bitcast.4, bf16[8,2,256,512]{3,2,1,0:T(8,128)(2,1)} %cache_ref.5, bf16[2,2,4,1024]{3,2,1,0:T(4,128)(2,1)S(1)} %merge.1.refs_0_.refs_8_, bf16[2,4,4096]{2,1,0:T(4,128)(2,1)S(1)} %collective-permute-done.4.refs_1_.refs_7_), custom_call_target="tpu_custom_call" | custom-call | flops 10000000000 | bytes 4194304 | tf_op jit(solution)/shard_map/pack/pallas_call | solution.py:217
  19.4 1.5 %collective-permute-start.11 = (bf16[4,256,512]{2,1,0:T(8,128)(2,1)S(1)}, bf16[4,256,512]{2,1,0:T(8,128)(2,1)S(1)}, u32[]{:S(2)}, u32[]{:S(2)}) collective-permute-start(bf16[4,256,512]{2,1,0:T(8,128)(2,1)S(1)} %get-tuple-element.24.refs_5_), channel_id=1, source_target_pairs={{0,1},{1,0},{2,3},{3,2},{4,5},{5,4},{6,7},{7,6},{8,9},{9,8},{10,11... | collective-permute-start | bytes 3145736 | tf_op jit(solution)/shard_map/ppermute | solution.py:35
  21.0 0.6 %collective-permute-done.6.refs_10_ = bf16[2,2,4,1024]{3,2,1,0:T(4,128)(2,1)S(1)} collective-permute-done((bf16[2,2,4,1024]{3,2,1,0:T(4,128)(2,1)S(1)}, bf16[2,2,4,1024]{3,2,1,0:T(4,128)(2,1)S(1)}, u32[]{:S(2)}, u32[]{:S(2)}) %collective-permute-start.6) | collective-permute-done | bytes 32800 | tf_op jit(solution)/shard_map/ppermute | solution.py:35
  21.6 3.8 %attend.1 = (bf16[272,128]{1,0:T(8,128)(2,1)S(1)}, bf16[272,128]{1,0:T(8,128)(2,1)S(1)}, bf16[272,128]{1,0:T(8,128)(2,1)S(1)}, bf16[272,128]{1,0:T(8,128)(2,1)S(1)}) custom-call(s32[32]{0:T(128)S(1)} %bitcast.5, s32[32]{0:T(128)S(1)} %copy-done.1, bf16[1,256,512]{2,1,0:T(8,128)(2,1)S(1)} %get-tuple-element.16.refs_0_, ...), custom_call_target="tpu_custom_call" | custom-call | flops 20000000000 | bytes 4194304 | tf_op jit(solution)/shard_map/attend/pallas_call | solution.py:365
  25.4 0.8 %collective-permute-start.8 = (bf16[272,128]{1,0:T(8,128)(2,1)S(1)}, bf16[272,128]{1,0:T(8,128)(2,1)S(1)}, u32[]{:S(2)}, u32[]{:S(2)}) collective-permute-start(bf16[272,128]{1,0:T(8,128)(2,1)S(1)} %get-tuple-element.27), channel_id=1, source_target_pairs={{0,4},{4,0},{8,12},{12,8},{1,5},{5,1},{9,13},{13,9},{2,6},{6,2},{1... | collective-permute-start | bytes 208904 | tf_op jit(solution)/shard_map/ppermute | solution.py:35
  26.2 2.6 %collective-permute-start.9 = (bf16[272,128]{1,0:T(8,128)(2,1)S(1)}, bf16[272,128]{1,0:T(8,128)(2,1)S(1)}, u32[]{:S(2)}, u32[]{:S(2)}) collective-permute-start(bf16[272,128]{1,0:T(8,128)(2,1)S(1)} %get-tuple-element.28), channel_id=1, source_target_pairs={{0,8},{4,12},{8,0},{12,4},{1,9},{5,13},{9,1},{13,5},{2,10},{6,14},... | collective-permute-start | bytes 208904 | tf_op jit(solution)/shard_map/ppermute | solution.py:35
  28.9 1.0 %collective-permute-start.10 = (bf16[272,128]{1,0:T(8,128)(2,1)S(1)}, bf16[272,128]{1,0:T(8,128)(2,1)S(1)}, u32[]{:S(2)}, u32[]{:S(2)}) collective-permute-start(bf16[272,128]{1,0:T(8,128)(2,1)S(1)} %get-tuple-element.29), channel_id=1, source_target_pairs={{0,12},{4,8},{8,4},{12,0},{1,13},{5,9},{9,5},{13,1},{2,14},{6,10},... | collective-permute-start | bytes 208904 | tf_op jit(solution)/shard_map/ppermute | solution.py:35
  29.8 1.5 %place.4.refs_4_.refs_0_ = bf16[1,16,256,512]{3,2,1,0:T(8,128)(2,1)} custom-call(bf16[4,256,512]{2,1,0:T(8,128)(2,1)S(1)} %get-tuple-element.23.refs_4_.refs_0_, bf16[4,256,512]{2,1,0:T(8,128)(2,1)S(1)} %collective-permute-done.11.refs_1_, bf16[1,256,512]{2,1,0:T(8,128)(2,1)S(1)} %collective-permute-done.3.refs_2_), custom_call_target="tpu_custom_call" | custom-call | bytes 4718592 | tf_op jit(solution)/shard_map/place/pallas_call | solution.py:265
  31.3 3.5 %fetch.2.refs_5_ = bf16[2048,2048]{1,0:T(8,128)(2,1)S(1)} custom-call(bf16[4096,2048]{1,0:T(8,128)(2,1)} %weight_ref.3, bf16[272,128]{1,0:T(8,128)(2,1)S(1)} %get-tuple-element.26.refs_0_, bf16[4,256,512]{2,1,0:T(8,128)(2,1)S(1)} %collective-permute-done.11.refs_1_), custom_call_target="tpu_custom_call" | custom-call | bytes 16777216 | tf_op jit(solution)/shard_map/fetch/pallas_call | solution.py:458
  34.8 0.3 collective-permute-done.10.refs_3_
  35.1 0.4 join.1.refs_0_.refs_1_
  35.6 2.7 %collective-permute-start.14 = (bf16[8,4096]{1,0:T(8,128)(2,1)S(1)}, bf16[8,4096]{1,0:T(8,128)(2,1)S(1)}, u32[]{:S(2)}, u32[]{:S(2)}) collective-permute-start(bf16[8,4096]{1,0:T(8,128)(2,1)S(1)} %join.1.refs_0_.refs_1_), channel_id=1, source_target_pairs={{0,12},{4,8},{8,4},{12,0},{1,13},{5,9},{9,5},{13,1},{2,14},{6,10},... | collective-permute-start | bytes 196616 | tf_op jit(solution)/shard_map/ppermute | solution.py:35
  38.2 0.2 collective-permute-start.13
  38.5 1.5 %collective-permute-start.12 = (bf16[8,4096]{1,0:T(8,128)(2,1)S(1)}, bf16[8,4096]{1,0:T(8,128)(2,1)S(1)}, u32[]{:S(2)}, u32[]{:S(2)}) collective-permute-start(bf16[8,4096]{1,0:T(8,128)(2,1)S(1)} %join.1.refs_0_.refs_1_), channel_id=1, source_target_pairs={{0,4},{4,0},{8,12},{12,8},{1,5},{5,1},{9,13},{13,9},{2,6},{6,2},{1... | collective-permute-start | bytes 196616 | tf_op jit(solution)/shard_map/ppermute | solution.py:35
  40.0 3.5 %fetch.3.refs_6_ = bf16[2048,2048]{1,0:T(8,128)(2,1)S(1)} custom-call(bf16[4096,2048]{1,0:T(8,128)(2,1)} %weight_ref.3, bf16[8,4096]{1,0:T(8,128)(2,1)S(1)} %join.1.refs_0_.refs_1_), custom_call_target="tpu_custom_call" | custom-call | bytes 16777216 | tf_op jit(solution)/shard_map/fetch/pallas_call | solution.py:458
  43.5 0.9 %place.5.refs_0_ = bf16[1,16,256,512]{3,2,1,0:T(8,128)(2,1)} custom-call(bf16[1,16,256,512]{3,2,1,0:T(8,128)(2,1)} %place.4.refs_4_.refs_0_, bf16[8,4096]{1,0:T(8,128)(2,1)S(1)} %join.1.refs_0_.refs_1_, bf16[3,256,512]{2,1,0:T(8,128)(2,1)S(1)} %collective-permute-done.refs_6_.refs_0_.refs_2_), custom_call_target="tpu_custom_call", output_to_operand_aliasing={{}: (0, {})} | custom-call | bytes 1572864 | tf_op jit(solution)/shard_map/place/pallas_call | solution.py:265
  44.4 1.0 %collective-permute-done.13.refs_3_ = bf16[8,4096]{1,0:T(8,128)(2,1)S(1)} collective-permute-done((bf16[8,4096]{1,0:T(8,128)(2,1)S(1)}, bf16[8,4096]{1,0:T(8,128)(2,1)S(1)}, u32[]{:S(2)}, u32[]{:S(2)}) %collective-permute-start.13) | collective-permute-done | bytes 65568 | tf_op jit(solution)/shard_map/ppermute | solution.py:35
  45.4 3.6 %project.1.refs_1_ = bf16[8,4,2048]{2,1,0:T(4,128)(2,1)} custom-call(bf16[3,256,512]{2,1,0:T(8,128)(2,1)S(1)} %collective-permute-done.refs_6_.refs_0_.refs_2_, bf16[8,4096]{1,0:T(8,128)(2,1)S(1)} %join.1.refs_0_.refs_1_, bf16[8,4096]{1,0:T(8,128)(2,1)S(1)} %collective-permute-done.12.refs_2_, bf16[8,4096]{1,0:T(8,128)(2,1)S(1)} %collective-permute-done.13.refs_3_, ...), custom_call_target="tpu_custom_call" | custom-call | flops 536870912 | bytes 16777216 | tf_op jit(solution)/shard_map/project/pallas_call | solution.py:502
  49.1 0.9 %place.6.refs_0_ = bf16[1,16,256,512]{3,2,1,0:T(8,128)(2,1)} custom-call(bf16[1,16,256,512]{3,2,1,0:T(8,128)(2,1)} %place.5.refs_0_, bf16[8,4,2048]{2,1,0:T(4,128)(2,1)} %project.1.refs_1_, bf16[3,256,512]{2,1,0:T(8,128)(2,1)S(1)} %collective-permute-done.15.refs_2_), custom_call_target="tpu_custom_call", output_to_operand_aliasing={{}: (0, {})} | custom-call | bytes 1572864 | tf_op jit(solution)/shard_map/place/pallas_call | solution.py:265
  50.0 0.9 %collective-permute-done.16.refs_2_ = bf16[1,256,512]{2,1,0:T(8,128)(2,1)S(1)} collective-permute-done((bf16[1,256,512]{2,1,0:T(8,128)(2,1)S(1)}, bf16[1,256,512]{2,1,0:T(8,128)(2,1)S(1)}, u32[]{:S(2)}, u32[]{:S(2)}) %collective-permute-start.16) | collective-permute-done | bytes 262176 | tf_op jit(solution)/shard_map/ppermute | solution.py:35
  50.9 0.7 %place.7 = bf16[1,16,256,512]{3,2,1,0:T(8,128)(2,1)} custom-call(bf16[1,16,256,512]{3,2,1,0:T(8,128)(2,1)} %place.6.refs_0_, bf16[8,4,2048]{2,1,0:T(4,128)(2,1)} %project.1.refs_1_, bf16[1,256,512]{2,1,0:T(8,128)(2,1)S(1)} %collective-permute-done.16.refs_2_), custom_call_target="tpu_custom_call", output_to_operand_aliasing={{}: (0, {})} | custom-call | bytes 524288 | tf_op jit(solution)/shard_map/place/pallas_call | solution.py:265
  (20 shorter events, 0.1 us)
Async XLA Ops:
  0.6 5.6 %copy-start = (s32[32,1]{0,1:T(1,128)S(1)}, s32[32,1]{0,1:T(1,128)}, u32[]{:S(2)}) copy-start(s32[32,1]{0,1:T(1,128)} %param.7) | copy-start | bytes 388
  2.3 10.4 %collective-permute-start.3 = (bf16[1,256,512]{2,1,0:T(8,128)(2,1)S(1)}, bf16[1,256,512]{2,1,0:T(8,128)(2,1)S(1)}, u32[]{:S(2)}, u32[]{:S(2)}) collective-permute-start(bf16[1,256,512]{2,1,0:T(8,128)(2,1)S(1)} %get-tuple-element.16.refs_0_), channel_id=1, source_target_pairs={{0,2},{1,3},{2,0},{3,1},{4,6},{5,7},{6,4},{7,5},{8,10},{9,11},{10,... | collective-permute-start | bytes 786440 | tf_op jit(solution)/shard_map/ppermute | solution.py:35
  5.3 7.1 %collective-permute-start.1 = (bf16[2,4,1024]{2,1,0:T(4,128)(2,1)S(1)}, bf16[2,4,1024]{2,1,0:T(4,128)(2,1)S(1)}, u32[]{:S(2)}, u32[]{:S(2)}) collective-permute-start(bf16[2,4,1024]{2,1,0:T(4,128)(2,1)S(1)} %get-tuple-element.20), channel_id=1, source_target_pairs={{0,2},{1,3},{2,0},{3,1},{4,6},{5,7},{6,4},{7,5},{8,10},{9,11},{10,... | collective-permute-start | bytes 49160 | tf_op jit(solution)/shard_map/ppermute | solution.py:35
  5.4 7.3 %collective-permute-start.2 = (bf16[2,4,1024]{2,1,0:T(4,128)(2,1)S(1)}, bf16[2,4,1024]{2,1,0:T(4,128)(2,1)S(1)}, u32[]{:S(2)}, u32[]{:S(2)}) collective-permute-start(bf16[2,4,1024]{2,1,0:T(4,128)(2,1)S(1)} %get-tuple-element.21), channel_id=1, source_target_pairs={{0,3},{1,2},{2,1},{3,0},{4,7},{5,6},{6,5},{7,4},{8,11},{9,10},{10,... | collective-permute-start | bytes 49160 | tf_op jit(solution)/shard_map/ppermute | solution.py:35
  8.4 7.9 %collective-permute-start.4 = (bf16[2,4,4096]{2,1,0:T(4,128)(2,1)S(1)}, bf16[2,4,4096]{2,1,0:T(4,128)(2,1)S(1)}, u32[]{:S(2)}, u32[]{:S(2)}) collective-permute-start(bf16[2,4,4096]{2,1,0:T(4,128)(2,1)S(1)} %get-tuple-element.22), channel_id=1, source_target_pairs={{0,1},{1,0},{2,3},{3,2},{4,5},{5,4},{6,7},{7,6},{8,9},{9,8},{10,11... | collective-permute-start | bytes 196616 | tf_op jit(solution)/shard_map/ppermute | solution.py:35
  9.7 25.3 %collective-permute-start = (bf16[3,256,512]{2,1,0:T(8,128)(2,1)S(1)}, bf16[3,256,512]{2,1,0:T(8,128)(2,1)S(1)}, u32[]{:S(2)}, u32[]{:S(2)}) collective-permute-start(bf16[3,256,512]{2,1,0:T(8,128)(2,1)S(1)} %get-tuple-element.17.refs_1_), channel_id=1, source_target_pairs={{0,2},{1,3},{2,0},{3,1},{4,6},{5,7},{6,4},{7,5},{8,10},{9,11},{10,... | collective-permute-start | bytes 2359304 | tf_op jit(solution)/shard_map/ppermute | solution.py:35
  12.4 36.7 %collective-permute-start.15 = (bf16[3,256,512]{2,1,0:T(8,128)(2,1)S(1)}, bf16[3,256,512]{2,1,0:T(8,128)(2,1)S(1)}, u32[]{:S(2)}, u32[]{:S(2)}) collective-permute-start(bf16[3,256,512]{2,1,0:T(8,128)(2,1)S(1)} %get-tuple-element.18.refs_2_), channel_id=1, source_target_pairs={{0,3},{1,2},{2,1},{3,0},{4,7},{5,6},{6,5},{7,4},{8,11},{9,10},{10,... | collective-permute-start | bytes 2359304 | tf_op jit(solution)/shard_map/ppermute | solution.py:35
  12.7 8.8 %copy-start.1 = (s32[32]{0:T(128)S(1)}, s32[32]{0:T(128)}, u32[]{:S(2)}) copy-start(s32[32]{0:T(128)} %lengths_ref.1) | copy-start | bytes 388
  12.7 6.7 %collective-permute-start.7 = (bf16[2,2,4,1024]{3,2,1,0:T(4,128)(2,1)S(1)}, bf16[2,2,4,1024]{3,2,1,0:T(4,128)(2,1)S(1)}, u32[]{:S(2)}, u32[]{:S(2)}) collective-permute-start(bf16[2,2,4,1024]{3,2,1,0:T(4,128)(2,1)S(1)} %merge.1.refs_0_.refs_8_), channel_id=1, source_target_pairs={{0,12},{4,8},{8,4},{12,0},{1,13},{5,9},{9,5},{13,1},{2,14},{6,10},... | collective-permute-start | bytes 98312 | tf_op jit(solution)/shard_map/ppermute | solution.py:35
  16.3 5.3 %collective-permute-start.6 = (bf16[2,2,4,1024]{3,2,1,0:T(4,128)(2,1)S(1)}, bf16[2,2,4,1024]{3,2,1,0:T(4,128)(2,1)S(1)}, u32[]{:S(2)}, u32[]{:S(2)}) collective-permute-start(bf16[2,2,4,1024]{3,2,1,0:T(4,128)(2,1)S(1)} %merge.1.refs_0_.refs_8_), channel_id=1, source_target_pairs={{0,8},{4,12},{8,0},{12,4},{1,9},{5,13},{9,1},{13,5},{2,10},{6,14},... | collective-permute-start | bytes 98312 | tf_op jit(solution)/shard_map/ppermute | solution.py:35
  16.3 5.3 %collective-permute-start.5 = (bf16[2,2,4,1024]{3,2,1,0:T(4,128)(2,1)S(1)}, bf16[2,2,4,1024]{3,2,1,0:T(4,128)(2,1)S(1)}, u32[]{:S(2)}, u32[]{:S(2)}) collective-permute-start(bf16[2,2,4,1024]{3,2,1,0:T(4,128)(2,1)S(1)} %merge.1.refs_0_.refs_8_), channel_id=1, source_target_pairs={{0,4},{4,0},{8,12},{12,8},{1,5},{5,1},{9,13},{13,9},{2,6},{6,2},{1... | collective-permute-start | bytes 98312 | tf_op jit(solution)/shard_map/ppermute | solution.py:35
  19.4 9.4 %collective-permute-start.11 = (bf16[4,256,512]{2,1,0:T(8,128)(2,1)S(1)}, bf16[4,256,512]{2,1,0:T(8,128)(2,1)S(1)}, u32[]{:S(2)}, u32[]{:S(2)}) collective-permute-start(bf16[4,256,512]{2,1,0:T(8,128)(2,1)S(1)} %get-tuple-element.24.refs_5_), channel_id=1, source_target_pairs={{0,1},{1,0},{2,3},{3,2},{4,5},{5,4},{6,7},{7,6},{8,9},{9,8},{10,11... | collective-permute-start | bytes 3145736 | tf_op jit(solution)/shard_map/ppermute | solution.py:35
  25.4 9.4 %collective-permute-start.8 = (bf16[272,128]{1,0:T(8,128)(2,1)S(1)}, bf16[272,128]{1,0:T(8,128)(2,1)S(1)}, u32[]{:S(2)}, u32[]{:S(2)}) collective-permute-start(bf16[272,128]{1,0:T(8,128)(2,1)S(1)} %get-tuple-element.27), channel_id=1, source_target_pairs={{0,4},{4,0},{8,12},{12,8},{1,5},{5,1},{9,13},{13,9},{2,6},{6,2},{1... | collective-permute-start | bytes 208904 | tf_op jit(solution)/shard_map/ppermute | solution.py:35
  26.2 8.6 %collective-permute-start.9 = (bf16[272,128]{1,0:T(8,128)(2,1)S(1)}, bf16[272,128]{1,0:T(8,128)(2,1)S(1)}, u32[]{:S(2)}, u32[]{:S(2)}) collective-permute-start(bf16[272,128]{1,0:T(8,128)(2,1)S(1)} %get-tuple-element.28), channel_id=1, source_target_pairs={{0,8},{4,12},{8,0},{12,4},{1,9},{5,13},{9,1},{13,5},{2,10},{6,14},... | collective-permute-start | bytes 208904 | tf_op jit(solution)/shard_map/ppermute | solution.py:35
  28.9 6.2 %collective-permute-start.10 = (bf16[272,128]{1,0:T(8,128)(2,1)S(1)}, bf16[272,128]{1,0:T(8,128)(2,1)S(1)}, u32[]{:S(2)}, u32[]{:S(2)}) collective-permute-start(bf16[272,128]{1,0:T(8,128)(2,1)S(1)} %get-tuple-element.29), channel_id=1, source_target_pairs={{0,12},{4,8},{8,4},{12,0},{1,13},{5,9},{9,5},{13,1},{2,14},{6,10},... | collective-permute-start | bytes 208904 | tf_op jit(solution)/shard_map/ppermute | solution.py:35
  35.5 15.4 %collective-permute-start.16 = (bf16[1,256,512]{2,1,0:T(8,128)(2,1)S(1)}, bf16[1,256,512]{2,1,0:T(8,128)(2,1)S(1)}, u32[]{:S(2)}, u32[]{:S(2)}) collective-permute-start(bf16[1,256,512]{2,1,0:T(8,128)(2,1)S(1)} %gate.1), channel_id=1, source_target_pairs={{0,3},{1,2},{2,1},{3,0},{4,7},{5,6},{6,5},{7,4},{8,11},{9,10},{10,... | collective-permute-start | bytes 786440 | tf_op jit(solution)/shard_map/ppermute | solution.py:35
  35.6 8.9 %collective-permute-start.14 = (bf16[8,4096]{1,0:T(8,128)(2,1)S(1)}, bf16[8,4096]{1,0:T(8,128)(2,1)S(1)}, u32[]{:S(2)}, u32[]{:S(2)}) collective-permute-start(bf16[8,4096]{1,0:T(8,128)(2,1)S(1)} %join.1.refs_0_.refs_1_), channel_id=1, source_target_pairs={{0,12},{4,8},{8,4},{12,0},{1,13},{5,9},{9,5},{13,1},{2,14},{6,10},... | collective-permute-start | bytes 196616 | tf_op jit(solution)/shard_map/ppermute | solution.py:35
  38.2 7.2 %collective-permute-start.13 = (bf16[8,4096]{1,0:T(8,128)(2,1)S(1)}, bf16[8,4096]{1,0:T(8,128)(2,1)S(1)}, u32[]{:S(2)}, u32[]{:S(2)}) collective-permute-start(bf16[8,4096]{1,0:T(8,128)(2,1)S(1)} %join.1.refs_0_.refs_1_), channel_id=1, source_target_pairs={{0,8},{4,12},{8,0},{12,4},{1,9},{5,13},{9,1},{13,5},{2,10},{6,14},... | collective-permute-start | bytes 196616 | tf_op jit(solution)/shard_map/ppermute | solution.py:35
  38.5 7.0 %collective-permute-start.12 = (bf16[8,4096]{1,0:T(8,128)(2,1)S(1)}, bf16[8,4096]{1,0:T(8,128)(2,1)S(1)}, u32[]{:S(2)}, u32[]{:S(2)}) collective-permute-start(bf16[8,4096]{1,0:T(8,128)(2,1)S(1)} %join.1.refs_0_.refs_1_), channel_id=1, source_target_pairs={{0,4},{4,0},{8,12},{12,8},{1,5},{5,1},{9,13},{13,9},{2,6},{6,2},{1... | collective-permute-start | bytes 196616 | tf_op jit(solution)/shard_map/ppermute | solution.py:35

commit v19 on v18

--- a/solution.py
+++ b/solution.py
@@ -121,7 +121,7 @@
     offset, half, _ = piece
     section = lax.axis_index("sec")
     copies = [pltpu.make_async_copy(routing_ref, routed, routing_sem)]
-    for i in range(REQ_GRP):
+    for i in range(REQ_GRP - CAP + 1 if full and half < 2 else REQ_GRP):
         copies.append(pltpu.make_async_copy(cache_ref.at[i, half % 2], held.at[i], sem.at[i]))
     for copy in copies:
         copy.start()
@@ -130,8 +130,10 @@
     row, filled = slot_row(own_targets(routed, section), section ^ offset, half // 2)
     for copy in copies[1:] + query_copies:
         copy.wait()
-    chosen = held[row]
-    out_ref[0] = chosen if full else jnp.where(filled, chosen, jnp.zeros_like(chosen))
+    block = min(32, held.shape[1])
+    for first in range(0, held.shape[1], block):
+        chosen = held[row, first : first + block]
+        out_ref[0, first : first + block] = chosen if full else jnp.where(filled, chosen, jnp.zeros_like(chosen))
 
 
 def pack_head(routing, cache, queries, piece, section_count, tp_count):

time: 52 us -> 51.9 us (level)
  no operation moved by 1% of the time
where the time goes in v19:
time: 51.9 us; the launch traced here: 51.5 us
  Pallas kernels  24.7 us (48%)
  starting transfers between devices  20.3 us (39%)
  waiting for transfers between devices  5.72 us (11%)
  between operations  0.78 us (2%)
    ppermute x17, starting transfers between devices, swap(): return lax.ppermute(value, axis, [(i, i ^ offset) for i in range(count)])  20.3 us
    pallas_call x2, Pallas kernels, fetch(): pl.pallas_call(functools.partial(fetch_kernel, number * size), out_shape=...  6.95 us
    ppermute x17, waiting for transfers between devices, swap(): return lax.ppermute(value, axis, [(i, i ^ offset) for i in range(count)])  5.72 us
    pallas_call x4, Pallas kernels, place(): pl.pallas_call(functools.partial(place_kernel, pieces), out_shape=jax.Sha...  3.99 us
    pallas_call x1, Pallas kernels, attend(): pl.pallas_call(functools.partial(attend_kernel, pieces, section_count, tp...  3.77 us
    pallas_call x1, Pallas kernels, project(): pl.pallas_call(functools.partial(project_kernel, count, min(256, width),...  3.64 us
    pallas_call x1, Pallas kernels, pack(): pl.pallas_call(functools.partial(pack_kernel, pieces, section_count), out...  2.22 us
    pallas_call x1, Pallas kernels, first_pack(): pl.pallas_call(functools.partial(first_pack_kernel, pieces, section_count...  2.2 us
  transfers between devices with their start and end apart: 17, of which 6 were waited for; matrix products, arithmetic and copies ran while one was open for 0% of the time, Pallas kernels for 44%

profile of v19, /device:TPU:0, one launch (start us, length us, event | category | flops | bytes accessed | tf_op | source)
XLA Modules:
  0.0 51.5 jit_solution(6688561420736473817)
XLA Ops:
  0.6 1.6 %pack_head.1 = (bf16[1,256,512]{2,1,0:T(8,128)(2,1)S(1)}, bf16[2,4,1024]{2,1,0:T(4,128)(2,1)S(1)}, bf16[2,4,1024]{2,1,0:T(4,128)(2,1)S(1)}) custom-call(s32[32]{0:T(128)} %bitcast.2, bf16[8,2,256,512]{3,2,1,0:T(8,128)(2,1)} %cache_ref.5, bf16[1,8,4,4096]{3,2,1,0:T(4,128)(2,1)} %query_ref.3), custom_call_target="tpu_custom_call" | custom-call | bytes 2097152 | tf_op jit(solution)/shard_map/pack_head/pallas_call | solution.py:143
  2.2 3.0 %collective-permute-start.3 = (bf16[1,256,512]{2,1,0:T(8,128)(2,1)S(1)}, bf16[1,256,512]{2,1,0:T(8,128)(2,1)S(1)}, u32[]{:S(2)}, u32[]{:S(2)}) collective-permute-start(bf16[1,256,512]{2,1,0:T(8,128)(2,1)S(1)} %get-tuple-element.16.refs_0_), channel_id=1, source_target_pairs={{0,2},{1,3},{2,0},{3,1},{4,6},{5,7},{6,4},{7,5},{8,10},{9,11},{10,... | collective-permute-start | bytes 786440 | tf_op jit(solution)/shard_map/ppermute | solution.py:35
  5.2 0.1 collective-permute-start.1
  5.3 0.8 %collective-permute-start.2 = (bf16[2,4,1024]{2,1,0:T(4,128)(2,1)S(1)}, bf16[2,4,1024]{2,1,0:T(4,128)(2,1)S(1)}, u32[]{:S(2)}, u32[]{:S(2)}) collective-permute-start(bf16[2,4,1024]{2,1,0:T(4,128)(2,1)S(1)} %get-tuple-element.21), channel_id=1, source_target_pairs={{0,3},{1,2},{2,1},{3,0},{4,7},{5,6},{6,5},{7,4},{8,11},{9,10},{10,... | collective-permute-start | bytes 49160 | tf_op jit(solution)/shard_map/ppermute | solution.py:35
  6.1 2.2 %first_pack.1 = (bf16[3,256,512]{2,1,0:T(8,128)(2,1)S(1)}, bf16[3,256,512]{2,1,0:T(8,128)(2,1)S(1)}, bf16[1,256,512]{2,1,0:T(8,128)(2,1)S(1)}, bf16[2,4,4096]{2,1,0:T(4,128)(2,1)S(1)}, bf16[2,4,4096]{2,1,0:T(4,128)(2,1)S(1)}) custom-call(s32[32]{0:T(128)S(1)} %bitcast.3, bf16[8,2,256,512]{3,2,1,0:T(8,128)(2,1)} %cache_ref.5, ...), custom_call_target="tpu_custom_call" | custom-call | bytes 3932160 | tf_op jit(solution)/shard_map/first_pack/pallas_call | solution.py:201
  8.3 1.3 %collective-permute-start.4 = (bf16[2,4,4096]{2,1,0:T(4,128)(2,1)S(1)}, bf16[2,4,4096]{2,1,0:T(4,128)(2,1)S(1)}, u32[]{:S(2)}, u32[]{:S(2)}) collective-permute-start(bf16[2,4,4096]{2,1,0:T(4,128)(2,1)S(1)} %get-tuple-element.22), channel_id=1, source_target_pairs={{0,1},{1,0},{2,3},{3,2},{4,5},{5,4},{6,7},{7,6},{8,9},{9,8},{10,11... | collective-permute-start | bytes 196616 | tf_op jit(solution)/shard_map/ppermute | solution.py:35
  9.6 0.1 collective-permute-start
  9.7 2.6 %collective-permute-done.1.refs_0_ = bf16[2,4,1024]{2,1,0:T(4,128)(2,1)S(1)} collective-permute-done((bf16[2,4,1024]{2,1,0:T(4,128)(2,1)S(1)}, bf16[2,4,1024]{2,1,0:T(4,128)(2,1)S(1)}, u32[]{:S(2)}, u32[]{:S(2)}) %collective-permute-start.1) | collective-permute-done | bytes 16416 | tf_op jit(solution)/shard_map/ppermute | solution.py:35
  12.3 0.3 collective-permute-done.2.refs_1_
  12.6 3.6 %collective-permute-start.7 = (bf16[2,2,4,1024]{3,2,1,0:T(4,128)(2,1)S(1)}, bf16[2,2,4,1024]{3,2,1,0:T(4,128)(2,1)S(1)}, u32[]{:S(2)}, u32[]{:S(2)}) collective-permute-start(bf16[2,2,4,1024]{3,2,1,0:T(4,128)(2,1)S(1)} %merge.1.refs_0_.refs_8_), channel_id=1, source_target_pairs={{0,12},{4,8},{8,4},{12,0},{1,13},{5,9},{9,5},{13,1},{2,14},{6,10},... | collective-permute-start | bytes 98312 | tf_op jit(solution)/shard_map/ppermute | solution.py:35
  16.2 0.9 %collective-permute-start.5 = (bf16[2,2,4,1024]{3,2,1,0:T(4,128)(2,1)S(1)}, bf16[2,2,4,1024]{3,2,1,0:T(4,128)(2,1)S(1)}, u32[]{:S(2)}, u32[]{:S(2)}) collective-permute-start(bf16[2,2,4,1024]{3,2,1,0:T(4,128)(2,1)S(1)} %merge.1.refs_0_.refs_8_), channel_id=1, source_target_pairs={{0,4},{4,0},{8,12},{12,8},{1,5},{5,1},{9,13},{13,9},{2,6},{6,2},{1... | collective-permute-start | bytes 98312 | tf_op jit(solution)/shard_map/ppermute | solution.py:35
  17.1 2.2 %pack.1 = (bf16[4,256,512]{2,1,0:T(8,128)(2,1)S(1)}, bf16[4,256,512]{2,1,0:T(8,128)(2,1)S(1)}) custom-call(s32[32]{0:T(128)S(1)} %bitcast.4, bf16[8,2,256,512]{3,2,1,0:T(8,128)(2,1)} %cache_ref.5, bf16[2,2,4,1024]{3,2,1,0:T(4,128)(2,1)S(1)} %merge.1.refs_0_.refs_8_, bf16[2,4,4096]{2,1,0:T(4,128)(2,1)S(1)} %collective-permute-done.4.refs_1_.refs_7_), custom_call_target="tpu_custom_call" | custom-call | flops 10000000000 | bytes 4194304 | tf_op jit(solution)/shard_map/pack/pallas_call | solution.py:219
  19.3 1.5 %collective-permute-start.11 = (bf16[4,256,512]{2,1,0:T(8,128)(2,1)S(1)}, bf16[4,256,512]{2,1,0:T(8,128)(2,1)S(1)}, u32[]{:S(2)}, u32[]{:S(2)}) collective-permute-start(bf16[4,256,512]{2,1,0:T(8,128)(2,1)S(1)} %get-tuple-element.24.refs_5_), channel_id=1, source_target_pairs={{0,1},{1,0},{2,3},{3,2},{4,5},{5,4},{6,7},{7,6},{8,9},{9,8},{10,11... | collective-permute-start | bytes 3145736 | tf_op jit(solution)/shard_map/ppermute | solution.py:35
  20.9 0.6 %collective-permute-done.6.refs_10_ = bf16[2,2,4,1024]{3,2,1,0:T(4,128)(2,1)S(1)} collective-permute-done((bf16[2,2,4,1024]{3,2,1,0:T(4,128)(2,1)S(1)}, bf16[2,2,4,1024]{3,2,1,0:T(4,128)(2,1)S(1)}, u32[]{:S(2)}, u32[]{:S(2)}) %collective-permute-start.6) | collective-permute-done | bytes 32800 | tf_op jit(solution)/shard_map/ppermute | solution.py:35
  21.5 3.8 %attend.1 = (bf16[272,128]{1,0:T(8,128)(2,1)S(1)}, bf16[272,128]{1,0:T(8,128)(2,1)S(1)}, bf16[272,128]{1,0:T(8,128)(2,1)S(1)}, bf16[272,128]{1,0:T(8,128)(2,1)S(1)}) custom-call(s32[32]{0:T(128)S(1)} %bitcast.5, s32[32]{0:T(128)S(1)} %copy-done.1, bf16[1,256,512]{2,1,0:T(8,128)(2,1)S(1)} %get-tuple-element.16.refs_0_, ...), custom_call_target="tpu_custom_call" | custom-call | flops 20000000000 | bytes 4194304 | tf_op jit(solution)/shard_map/attend/pallas_call | solution.py:367
  25.3 0.9 %collective-permute-start.8 = (bf16[272,128]{1,0:T(8,128)(2,1)S(1)}, bf16[272,128]{1,0:T(8,128)(2,1)S(1)}, u32[]{:S(2)}, u32[]{:S(2)}) collective-permute-start(bf16[272,128]{1,0:T(8,128)(2,1)S(1)} %get-tuple-element.27), channel_id=1, source_target_pairs={{0,4},{4,0},{8,12},{12,8},{1,5},{5,1},{9,13},{13,9},{2,6},{6,2},{1... | collective-permute-start | bytes 208904 | tf_op jit(solution)/shard_map/ppermute | solution.py:35
  26.1 2.6 %collective-permute-start.9 = (bf16[272,128]{1,0:T(8,128)(2,1)S(1)}, bf16[272,128]{1,0:T(8,128)(2,1)S(1)}, u32[]{:S(2)}, u32[]{:S(2)}) collective-permute-start(bf16[272,128]{1,0:T(8,128)(2,1)S(1)} %get-tuple-element.28), channel_id=1, source_target_pairs={{0,8},{4,12},{8,0},{12,4},{1,9},{5,13},{9,1},{13,5},{2,10},{6,14},... | collective-permute-start | bytes 208904 | tf_op jit(solution)/shard_map/ppermute | solution.py:35
  28.8 1.0 %collective-permute-start.10 = (bf16[272,128]{1,0:T(8,128)(2,1)S(1)}, bf16[272,128]{1,0:T(8,128)(2,1)S(1)}, u32[]{:S(2)}, u32[]{:S(2)}) collective-permute-start(bf16[272,128]{1,0:T(8,128)(2,1)S(1)} %get-tuple-element.29), channel_id=1, source_target_pairs={{0,12},{4,8},{8,4},{12,0},{1,13},{5,9},{9,5},{13,1},{2,14},{6,10},... | collective-permute-start | bytes 208904 | tf_op jit(solution)/shard_map/ppermute | solution.py:35
  29.7 1.5 %place.4.refs_4_.refs_0_ = bf16[1,16,256,512]{3,2,1,0:T(8,128)(2,1)} custom-call(bf16[4,256,512]{2,1,0:T(8,128)(2,1)S(1)} %get-tuple-element.23.refs_4_.refs_0_, bf16[4,256,512]{2,1,0:T(8,128)(2,1)S(1)} %collective-permute-done.11.refs_1_, bf16[1,256,512]{2,1,0:T(8,128)(2,1)S(1)} %collective-permute-done.3.refs_2_), custom_call_target="tpu_custom_call" | custom-call | bytes 4718592 | tf_op jit(solution)/shard_map/place/pallas_call | solution.py:267
  31.2 3.5 %fetch.2.refs_5_ = bf16[2048,2048]{1,0:T(8,128)(2,1)S(1)} custom-call(bf16[4096,2048]{1,0:T(8,128)(2,1)} %weight_ref.3, bf16[272,128]{1,0:T(8,128)(2,1)S(1)} %get-tuple-element.26.refs_0_, bf16[4,256,512]{2,1,0:T(8,128)(2,1)S(1)} %collective-permute-done.11.refs_1_), custom_call_target="tpu_custom_call" | custom-call | bytes 16777216 | tf_op jit(solution)/shard_map/fetch/pallas_call | solution.py:460
  34.7 0.3 collective-permute-done.10.refs_3_
  35.0 0.4 join.1.refs_0_.refs_1_
  35.5 2.7 %collective-permute-start.14 = (bf16[8,4096]{1,0:T(8,128)(2,1)S(1)}, bf16[8,4096]{1,0:T(8,128)(2,1)S(1)}, u32[]{:S(2)}, u32[]{:S(2)}) collective-permute-start(bf16[8,4096]{1,0:T(8,128)(2,1)S(1)} %join.1.refs_0_.refs_1_), channel_id=1, source_target_pairs={{0,12},{4,8},{8,4},{12,0},{1,13},{5,9},{9,5},{13,1},{2,14},{6,10},... | collective-permute-start | bytes 196616 | tf_op jit(solution)/shard_map/ppermute | solution.py:35
  38.2 0.2 collective-permute-start.13
  38.4 1.5 %collective-permute-start.12 = (bf16[8,4096]{1,0:T(8,128)(2,1)S(1)}, bf16[8,4096]{1,0:T(8,128)(2,1)S(1)}, u32[]{:S(2)}, u32[]{:S(2)}) collective-permute-start(bf16[8,4096]{1,0:T(8,128)(2,1)S(1)} %join.1.refs_0_.refs_1_), channel_id=1, source_target_pairs={{0,4},{4,0},{8,12},{12,8},{1,5},{5,1},{9,13},{13,9},{2,6},{6,2},{1... | collective-permute-start | bytes 196616 | tf_op jit(solution)/shard_map/ppermute | solution.py:35
  39.9 3.5 %fetch.3.refs_6_ = bf16[2048,2048]{1,0:T(8,128)(2,1)S(1)} custom-call(bf16[4096,2048]{1,0:T(8,128)(2,1)} %weight_ref.3, bf16[8,4096]{1,0:T(8,128)(2,1)S(1)} %join.1.refs_0_.refs_1_), custom_call_target="tpu_custom_call" | custom-call | bytes 16777216 | tf_op jit(solution)/shard_map/fetch/pallas_call | solution.py:460
  43.4 0.9 %place.5.refs_0_ = bf16[1,16,256,512]{3,2,1,0:T(8,128)(2,1)} custom-call(bf16[1,16,256,512]{3,2,1,0:T(8,128)(2,1)} %place.4.refs_4_.refs_0_, bf16[8,4096]{1,0:T(8,128)(2,1)S(1)} %join.1.refs_0_.refs_1_, bf16[3,256,512]{2,1,0:T(8,128)(2,1)S(1)} %collective-permute-done.refs_6_.refs_0_.refs_2_), custom_call_target="tpu_custom_call", output_to_operand_aliasing={{}: (0, {})} | custom-call | bytes 1572864 | tf_op jit(solution)/shard_map/place/pallas_call | solution.py:267
  44.3 1.0 %collective-permute-done.13.refs_3_ = bf16[8,4096]{1,0:T(8,128)(2,1)S(1)} collective-permute-done((bf16[8,4096]{1,0:T(8,128)(2,1)S(1)}, bf16[8,4096]{1,0:T(8,128)(2,1)S(1)}, u32[]{:S(2)}, u32[]{:S(2)}) %collective-permute-start.13) | collective-permute-done | bytes 65568 | tf_op jit(solution)/shard_map/ppermute | solution.py:35
  45.4 3.6 %project.1.refs_1_ = bf16[8,4,2048]{2,1,0:T(4,128)(2,1)} custom-call(bf16[3,256,512]{2,1,0:T(8,128)(2,1)S(1)} %collective-permute-done.refs_6_.refs_0_.refs_2_, bf16[8,4096]{1,0:T(8,128)(2,1)S(1)} %join.1.refs_0_.refs_1_, bf16[8,4096]{1,0:T(8,128)(2,1)S(1)} %collective-permute-done.12.refs_2_, bf16[8,4096]{1,0:T(8,128)(2,1)S(1)} %collective-permute-done.13.refs_3_, ...), custom_call_target="tpu_custom_call" | custom-call | flops 536870912 | bytes 16777216 | tf_op jit(solution)/shard_map/project/pallas_call | solution.py:504
  49.0 0.9 %place.6.refs_0_ = bf16[1,16,256,512]{3,2,1,0:T(8,128)(2,1)} custom-call(bf16[1,16,256,512]{3,2,1,0:T(8,128)(2,1)} %place.5.refs_0_, bf16[8,4,2048]{2,1,0:T(4,128)(2,1)} %project.1.refs_1_, bf16[3,256,512]{2,1,0:T(8,128)(2,1)S(1)} %collective-permute-done.15.refs_2_), custom_call_target="tpu_custom_call", output_to_operand_aliasing={{}: (0, {})} | custom-call | bytes 1572864 | tf_op jit(solution)/shard_map/place/pallas_call | solution.py:267
  49.9 0.9 %collective-permute-done.16.refs_2_ = bf16[1,256,512]{2,1,0:T(8,128)(2,1)S(1)} collective-permute-done((bf16[1,256,512]{2,1,0:T(8,128)(2,1)S(1)}, bf16[1,256,512]{2,1,0:T(8,128)(2,1)S(1)}, u32[]{:S(2)}, u32[]{:S(2)}) %collective-permute-start.16) | collective-permute-done | bytes 262176 | tf_op jit(solution)/shard_map/ppermute | solution.py:35
  50.8 0.7 %place.7 = bf16[1,16,256,512]{3,2,1,0:T(8,128)(2,1)} custom-call(bf16[1,16,256,512]{3,2,1,0:T(8,128)(2,1)} %place.6.refs_0_, bf16[8,4,2048]{2,1,0:T(4,128)(2,1)} %project.1.refs_1_, bf16[1,256,512]{2,1,0:T(8,128)(2,1)S(1)} %collective-permute-done.16.refs_2_), custom_call_target="tpu_custom_call", output_to_operand_aliasing={{}: (0, {})} | custom-call | bytes 524288 | tf_op jit(solution)/shard_map/place/pallas_call | solution.py:267
  (20 shorter events, 0.1 us)
Async XLA Ops:
  0.6 5.5 %copy-start = (s32[32,1]{0,1:T(1,128)S(1)}, s32[32,1]{0,1:T(1,128)}, u32[]{:S(2)}) copy-start(s32[32,1]{0,1:T(1,128)} %param.7) | copy-start | bytes 388
  2.2 10.4 %collective-permute-start.3 = (bf16[1,256,512]{2,1,0:T(8,128)(2,1)S(1)}, bf16[1,256,512]{2,1,0:T(8,128)(2,1)S(1)}, u32[]{:S(2)}, u32[]{:S(2)}) collective-permute-start(bf16[1,256,512]{2,1,0:T(8,128)(2,1)S(1)} %get-tuple-element.16.refs_0_), channel_id=1, source_target_pairs={{0,2},{1,3},{2,0},{3,1},{4,6},{5,7},{6,4},{7,5},{8,10},{9,11},{10,... | collective-permute-start | bytes 786440 | tf_op jit(solution)/shard_map/ppermute | solution.py:35
  5.2 7.1 %collective-permute-start.1 = (bf16[2,4,1024]{2,1,0:T(4,128)(2,1)S(1)}, bf16[2,4,1024]{2,1,0:T(4,128)(2,1)S(1)}, u32[]{:S(2)}, u32[]{:S(2)}) collective-permute-start(bf16[2,4,1024]{2,1,0:T(4,128)(2,1)S(1)} %get-tuple-element.20), channel_id=1, source_target_pairs={{0,2},{1,3},{2,0},{3,1},{4,6},{5,7},{6,4},{7,5},{8,10},{9,11},{10,... | collective-permute-start | bytes 49160 | tf_op jit(solution)/shard_map/ppermute | solution.py:35
  5.3 7.3 %collective-permute-start.2 = (bf16[2,4,1024]{2,1,0:T(4,128)(2,1)S(1)}, bf16[2,4,1024]{2,1,0:T(4,128)(2,1)S(1)}, u32[]{:S(2)}, u32[]{:S(2)}) collective-permute-start(bf16[2,4,1024]{2,1,0:T(4,128)(2,1)S(1)} %get-tuple-element.21), channel_id=1, source_target_pairs={{0,3},{1,2},{2,1},{3,0},{4,7},{5,6},{6,5},{7,4},{8,11},{9,10},{10,... | collective-permute-start | bytes 49160 | tf_op jit(solution)/shard_map/ppermute | solution.py:35
  8.3 7.9 %collective-permute-start.4 = (bf16[2,4,4096]{2,1,0:T(4,128)(2,1)S(1)}, bf16[2,4,4096]{2,1,0:T(4,128)(2,1)S(1)}, u32[]{:S(2)}, u32[]{:S(2)}) collective-permute-start(bf16[2,4,4096]{2,1,0:T(4,128)(2,1)S(1)} %get-tuple-element.22), channel_id=1, source_target_pairs={{0,1},{1,0},{2,3},{3,2},{4,5},{5,4},{6,7},{7,6},{8,9},{9,8},{10,11... | collective-permute-start | bytes 196616 | tf_op jit(solution)/shard_map/ppermute | solution.py:35
  9.6 25.4 %collective-permute-start = (bf16[3,256,512]{2,1,0:T(8,128)(2,1)S(1)}, bf16[3,256,512]{2,1,0:T(8,128)(2,1)S(1)}, u32[]{:S(2)}, u32[]{:S(2)}) collective-permute-start(bf16[3,256,512]{2,1,0:T(8,128)(2,1)S(1)} %get-tuple-element.17.refs_1_), channel_id=1, source_target_pairs={{0,2},{1,3},{2,0},{3,1},{4,6},{5,7},{6,4},{7,5},{8,10},{9,11},{10,... | collective-permute-start | bytes 2359304 | tf_op jit(solution)/shard_map/ppermute | solution.py:35
  12.3 36.7 %collective-permute-start.15 = (bf16[3,256,512]{2,1,0:T(8,128)(2,1)S(1)}, bf16[3,256,512]{2,1,0:T(8,128)(2,1)S(1)}, u32[]{:S(2)}, u32[]{:S(2)}) collective-permute-start(bf16[3,256,512]{2,1,0:T(8,128)(2,1)S(1)} %get-tuple-element.18.refs_2_), channel_id=1, source_target_pairs={{0,3},{1,2},{2,1},{3,0},{4,7},{5,6},{6,5},{7,4},{8,11},{9,10},{10,... | collective-permute-start | bytes 2359304 | tf_op jit(solution)/shard_map/ppermute | solution.py:35
  12.6 8.8 %copy-start.1 = (s32[32]{0:T(128)S(1)}, s32[32]{0:T(128)}, u32[]{:S(2)}) copy-start(s32[32]{0:T(128)} %lengths_ref.1) | copy-start | bytes 388
  12.6 6.7 %collective-permute-start.7 = (bf16[2,2,4,1024]{3,2,1,0:T(4,128)(2,1)S(1)}, bf16[2,2,4,1024]{3,2,1,0:T(4,128)(2,1)S(1)}, u32[]{:S(2)}, u32[]{:S(2)}) collective-permute-start(bf16[2,2,4,1024]{3,2,1,0:T(4,128)(2,1)S(1)} %merge.1.refs_0_.refs_8_), channel_id=1, source_target_pairs={{0,12},{4,8},{8,4},{12,0},{1,13},{5,9},{9,5},{13,1},{2,14},{6,10},... | collective-permute-start | bytes 98312 | tf_op jit(solution)/shard_map/ppermute | solution.py:35
  16.2 5.3 %collective-permute-start.6 = (bf16[2,2,4,1024]{3,2,1,0:T(4,128)(2,1)S(1)}, bf16[2,2,4,1024]{3,2,1,0:T(4,128)(2,1)S(1)}, u32[]{:S(2)}, u32[]{:S(2)}) collective-permute-start(bf16[2,2,4,1024]{3,2,1,0:T(4,128)(2,1)S(1)} %merge.1.refs_0_.refs_8_), channel_id=1, source_target_pairs={{0,8},{4,12},{8,0},{12,4},{1,9},{5,13},{9,1},{13,5},{2,10},{6,14},... | collective-permute-start | bytes 98312 | tf_op jit(solution)/shard_map/ppermute | solution.py:35
  16.2 5.3 %collective-permute-start.5 = (bf16[2,2,4,1024]{3,2,1,0:T(4,128)(2,1)S(1)}, bf16[2,2,4,1024]{3,2,1,0:T(4,128)(2,1)S(1)}, u32[]{:S(2)}, u32[]{:S(2)}) collective-permute-start(bf16[2,2,4,1024]{3,2,1,0:T(4,128)(2,1)S(1)} %merge.1.refs_0_.refs_8_), channel_id=1, source_target_pairs={{0,4},{4,0},{8,12},{12,8},{1,5},{5,1},{9,13},{13,9},{2,6},{6,2},{1... | collective-permute-start | bytes 98312 | tf_op jit(solution)/shard_map/ppermute | solution.py:35
  19.3 9.4 %collective-permute-start.11 = (bf16[4,256,512]{2,1,0:T(8,128)(2,1)S(1)}, bf16[4,256,512]{2,1,0:T(8,128)(2,1)S(1)}, u32[]{:S(2)}, u32[]{:S(2)}) collective-permute-start(bf16[4,256,512]{2,1,0:T(8,128)(2,1)S(1)} %get-tuple-element.24.refs_5_), channel_id=1, source_target_pairs={{0,1},{1,0},{2,3},{3,2},{4,5},{5,4},{6,7},{7,6},{8,9},{9,8},{10,11... | collective-permute-start | bytes 3145736 | tf_op jit(solution)/shard_map/ppermute | solution.py:35
  25.3 9.4 %collective-permute-start.8 = (bf16[272,128]{1,0:T(8,128)(2,1)S(1)}, bf16[272,128]{1,0:T(8,128)(2,1)S(1)}, u32[]{:S(2)}, u32[]{:S(2)}) collective-permute-start(bf16[272,128]{1,0:T(8,128)(2,1)S(1)} %get-tuple-element.27), channel_id=1, source_target_pairs={{0,4},{4,0},{8,12},{12,8},{1,5},{5,1},{9,13},{13,9},{2,6},{6,2},{1... | collective-permute-start | bytes 208904 | tf_op jit(solution)/shard_map/ppermute | solution.py:35
  26.1 8.6 %collective-permute-start.9 = (bf16[272,128]{1,0:T(8,128)(2,1)S(1)}, bf16[272,128]{1,0:T(8,128)(2,1)S(1)}, u32[]{:S(2)}, u32[]{:S(2)}) collective-permute-start(bf16[272,128]{1,0:T(8,128)(2,1)S(1)} %get-tuple-element.28), channel_id=1, source_target_pairs={{0,8},{4,12},{8,0},{12,4},{1,9},{5,13},{9,1},{13,5},{2,10},{6,14},... | collective-permute-start | bytes 208904 | tf_op jit(solution)/shard_map/ppermute | solution.py:35
  28.8 6.2 %collective-permute-start.10 = (bf16[272,128]{1,0:T(8,128)(2,1)S(1)}, bf16[272,128]{1,0:T(8,128)(2,1)S(1)}, u32[]{:S(2)}, u32[]{:S(2)}) collective-permute-start(bf16[272,128]{1,0:T(8,128)(2,1)S(1)} %get-tuple-element.29), channel_id=1, source_target_pairs={{0,12},{4,8},{8,4},{12,0},{1,13},{5,9},{9,5},{13,1},{2,14},{6,10},... | collective-permute-start | bytes 208904 | tf_op jit(solution)/shard_map/ppermute | solution.py:35
  35.4 15.4 %collective-permute-start.16 = (bf16[1,256,512]{2,1,0:T(8,128)(2,1)S(1)}, bf16[1,256,512]{2,1,0:T(8,128)(2,1)S(1)}, u32[]{:S(2)}, u32[]{:S(2)}) collective-permute-start(bf16[1,256,512]{2,1,0:T(8,128)(2,1)S(1)} %gate.1), channel_id=1, source_target_pairs={{0,3},{1,2},{2,1},{3,0},{4,7},{5,6},{6,5},{7,4},{8,11},{9,10},{10,... | collective-permute-start | bytes 786440 | tf_op jit(solution)/shard_map/ppermute | solution.py:35
  35.5 8.9 %collective-permute-start.14 = (bf16[8,4096]{1,0:T(8,128)(2,1)S(1)}, bf16[8,4096]{1,0:T(8,128)(2,1)S(1)}, u32[]{:S(2)}, u32[]{:S(2)}) collective-permute-start(bf16[8,4096]{1,0:T(8,128)(2,1)S(1)} %join.1.refs_0_.refs_1_), channel_id=1, source_target_pairs={{0,12},{4,8},{8,4},{12,0},{1,13},{5,9},{9,5},{13,1},{2,14},{6,10},... | collective-permute-start | bytes 196616 | tf_op jit(solution)/shard_map/ppermute | solution.py:35
  38.2 7.2 %collective-permute-start.13 = (bf16[8,4096]{1,0:T(8,128)(2,1)S(1)}, bf16[8,4096]{1,0:T(8,128)(2,1)S(1)}, u32[]{:S(2)}, u32[]{:S(2)}) collective-permute-start(bf16[8,4096]{1,0:T(8,128)(2,1)S(1)} %join.1.refs_0_.refs_1_), channel_id=1, source_target_pairs={{0,8},{4,12},{8,0},{12,4},{1,9},{5,13},{9,1},{13,5},{2,10},{6,14},... | collective-permute-start | bytes 196616 | tf_op jit(solution)/shard_map/ppermute | solution.py:35
  38.4 7.0 %collective-permute-start.12 = (bf16[8,4096]{1,0:T(8,128)(2,1)S(1)}, bf16[8,4096]{1,0:T(8,128)(2,1)S(1)}, u32[]{:S(2)}, u32[]{:S(2)}) collective-permute-start(bf16[8,4096]{1,0:T(8,128)(2,1)S(1)} %join.1.refs_0_.refs_1_), channel_id=1, source_target_pairs={{0,4},{4,0},{8,12},{12,8},{1,5},{5,1},{9,13},{13,9},{2,6},{6,2},{1... | collective-permute-start | bytes 196616 | tf_op jit(solution)/shard_map/ppermute | solution.py:35

commit v20 on v19

--- a/solution.py
+++ b/solution.py
@@ -76,7 +76,7 @@
 
     for n, place, offset, half in halves:
         if full:
-            copy(n, place, offset, half).start()
+            copy(n, place, offset, half).start(priority=half % 2)
         else:
             _, filled = rows[offset, half // 2]
 
@@ -123,17 +123,20 @@
     copies = [pltpu.make_async_copy(routing_ref, routed, routing_sem)]
     for i in range(REQ_GRP - CAP + 1 if full and half < 2 else REQ_GRP):
         copies.append(pltpu.make_async_copy(cache_ref.at[i, half % 2], held.at[i], sem.at[i]))
-    for copy in copies:
-        copy.start()
+    for n, copy in enumerate(copies):
+        copy.start(priority=n % 2)
     query_copies = start_queries(query_ref, query_out, offsets, query_sem)
     copies[0].wait()
     row, filled = slot_row(own_targets(routed, section), section ^ offset, half // 2)
-    for copy in copies[1:] + query_copies:
-        copy.wait()
+    pltpu.make_async_copy(cache_ref.at[row, half % 2], held.at[row], sem.at[row]).wait()
     block = min(32, held.shape[1])
     for first in range(0, held.shape[1], block):
         chosen = held[row, first : first + block]
         out_ref[0, first : first + block] = chosen if full else jnp.where(filled, chosen, jnp.zeros_like(chosen))
+    for i, copy in enumerate(copies[1:]):
+        pl.when(i != row)(copy.wait)
+    for copy in query_copies:
+        copy.wait()
 
 
 def pack_head(routing, cache, queries, piece, section_count, tp_count):
@@ -257,7 +260,7 @@
         for place in range(size):
             half = out_ref.at[0, (section ^ offset) * 2 * CAP + first + place]
             copies.append(pltpu.make_async_copy(part_refs[n].at[place], half, sem.at[len(copies)]))
-            copies[-1].start()
+            copies[-1].start(priority=len(copies) % 2)
     for copy in copies:
         copy.wait()
 
@@ -450,7 +453,7 @@
     for n in range(sem.shape[0]):
         rows = weight_ref.at[pl.ds(first + n * step, step)]
         copies.append(pltpu.make_async_copy(rows, out_ref.at[pl.ds(n * step, step)], sem.at[n]))
-        copies[-1].start()
+        copies[-1].start(priority=n % 2)
     for copy in copies:
         copy.wait()
 

time: 51.9 us -> 51.9 us (level)
  no operation moved by 1% of the time
where the time goes in v20:
time: 51.9 us; the launch traced here: 51.5 us
  Pallas kernels  24.8 us (48%)
  starting transfers between devices  20.3 us (39%)
  waiting for transfers between devices  5.69 us (11%)
  between operations  0.78 us (2%)
    ppermute x17, starting transfers between devices, swap(): return lax.ppermute(value, axis, [(i, i ^ offset) for i in range(count)])  20.3 us
    pallas_call x2, Pallas kernels, fetch(): pl.pallas_call(functools.partial(fetch_kernel, number * size), out_shape=...  7.01 us
    ppermute x17, waiting for transfers between devices, swap(): return lax.ppermute(value, axis, [(i, i ^ offset) for i in range(count)])  5.69 us
    pallas_call x4, Pallas kernels, place(): pl.pallas_call(functools.partial(place_kernel, pieces), out_shape=jax.Sha...  3.99 us
    pallas_call x1, Pallas kernels, attend(): pl.pallas_call(functools.partial(attend_kernel, pieces, section_count, tp...  3.77 us
    pallas_call x1, Pallas kernels, project(): pl.pallas_call(functools.partial(project_kernel, count, min(256, width),...  3.64 us
    pallas_call x1, Pallas kernels, pack(): pl.pallas_call(functools.partial(pack_kernel, pieces, section_count), out...  2.21 us
    pallas_call x1, Pallas kernels, first_pack(): pl.pallas_call(functools.partial(first_pack_kernel, pieces, section_count...  2.2 us
  transfers between devices with their start and end apart: 17, of which 6 were waited for; matrix products, arithmetic and copies ran while one was open for 0% of the time, Pallas kernels for 44%

profile of v20, /device:TPU:0, one launch (start us, length us, event | category | flops | bytes accessed | tf_op | source)
XLA Modules:
  0.0 51.5 jit_solution(10750464643293656297)
XLA Ops:
  0.6 1.6 %pack_head.1 = (bf16[1,256,512]{2,1,0:T(8,128)(2,1)S(1)}, bf16[2,4,1024]{2,1,0:T(4,128)(2,1)S(1)}, bf16[2,4,1024]{2,1,0:T(4,128)(2,1)S(1)}) custom-call(s32[32]{0:T(128)} %bitcast.2, bf16[8,2,256,512]{3,2,1,0:T(8,128)(2,1)} %cache_ref.5, bf16[1,8,4,4096]{3,2,1,0:T(4,128)(2,1)} %query_ref.3), custom_call_target="tpu_custom_call" | custom-call | bytes 2097152 | tf_op jit(solution)/shard_map/pack_head/pallas_call | solution.py:146
  2.2 3.0 %collective-permute-start.3 = (bf16[1,256,512]{2,1,0:T(8,128)(2,1)S(1)}, bf16[1,256,512]{2,1,0:T(8,128)(2,1)S(1)}, u32[]{:S(2)}, u32[]{:S(2)}) collective-permute-start(bf16[1,256,512]{2,1,0:T(8,128)(2,1)S(1)} %get-tuple-element.16.refs_0_), channel_id=1, source_target_pairs={{0,2},{1,3},{2,0},{3,1},{4,6},{5,7},{6,4},{7,5},{8,10},{9,11},{10,... | collective-permute-start | bytes 786440 | tf_op jit(solution)/shard_map/ppermute | solution.py:35
  5.2 0.1 collective-permute-start.1
  5.3 0.8 %collective-permute-start.2 = (bf16[2,4,1024]{2,1,0:T(4,128)(2,1)S(1)}, bf16[2,4,1024]{2,1,0:T(4,128)(2,1)S(1)}, u32[]{:S(2)}, u32[]{:S(2)}) collective-permute-start(bf16[2,4,1024]{2,1,0:T(4,128)(2,1)S(1)} %get-tuple-element.21), channel_id=1, source_target_pairs={{0,3},{1,2},{2,1},{3,0},{4,7},{5,6},{6,5},{7,4},{8,11},{9,10},{10,... | collective-permute-start | bytes 49160 | tf_op jit(solution)/shard_map/ppermute | solution.py:35
  6.1 2.2 %first_pack.1 = (bf16[3,256,512]{2,1,0:T(8,128)(2,1)S(1)}, bf16[3,256,512]{2,1,0:T(8,128)(2,1)S(1)}, bf16[1,256,512]{2,1,0:T(8,128)(2,1)S(1)}, bf16[2,4,4096]{2,1,0:T(4,128)(2,1)S(1)}, bf16[2,4,4096]{2,1,0:T(4,128)(2,1)S(1)}) custom-call(s32[32]{0:T(128)S(1)} %bitcast.3, bf16[8,2,256,512]{3,2,1,0:T(8,128)(2,1)} %cache_ref.5, ...), custom_call_target="tpu_custom_call" | custom-call | bytes 3932160 | tf_op jit(solution)/shard_map/first_pack/pallas_call | solution.py:204
  8.3 1.3 %collective-permute-start.4 = (bf16[2,4,4096]{2,1,0:T(4,128)(2,1)S(1)}, bf16[2,4,4096]{2,1,0:T(4,128)(2,1)S(1)}, u32[]{:S(2)}, u32[]{:S(2)}) collective-permute-start(bf16[2,4,4096]{2,1,0:T(4,128)(2,1)S(1)} %get-tuple-element.22), channel_id=1, source_target_pairs={{0,1},{1,0},{2,3},{3,2},{4,5},{5,4},{6,7},{7,6},{8,9},{9,8},{10,11... | collective-permute-start | bytes 196616 | tf_op jit(solution)/shard_map/ppermute | solution.py:35
  9.6 0.1 collective-permute-start
  9.7 2.6 %collective-permute-done.1.refs_0_ = bf16[2,4,1024]{2,1,0:T(4,128)(2,1)S(1)} collective-permute-done((bf16[2,4,1024]{2,1,0:T(4,128)(2,1)S(1)}, bf16[2,4,1024]{2,1,0:T(4,128)(2,1)S(1)}, u32[]{:S(2)}, u32[]{:S(2)}) %collective-permute-start.1) | collective-permute-done | bytes 16416 | tf_op jit(solution)/shard_map/ppermute | solution.py:35
  12.3 0.3 collective-permute-done.2.refs_1_
  12.6 3.6 %collective-permute-start.7 = (bf16[2,2,4,1024]{3,2,1,0:T(4,128)(2,1)S(1)}, bf16[2,2,4,1024]{3,2,1,0:T(4,128)(2,1)S(1)}, u32[]{:S(2)}, u32[]{:S(2)}) collective-permute-start(bf16[2,2,4,1024]{3,2,1,0:T(4,128)(2,1)S(1)} %merge.1.refs_0_.refs_8_), channel_id=1, source_target_pairs={{0,12},{4,8},{8,4},{12,0},{1,13},{5,9},{9,5},{13,1},{2,14},{6,10},... | collective-permute-start | bytes 98312 | tf_op jit(solution)/shard_map/ppermute | solution.py:35
  16.2 0.9 %collective-permute-start.5 = (bf16[2,2,4,1024]{3,2,1,0:T(4,128)(2,1)S(1)}, bf16[2,2,4,1024]{3,2,1,0:T(4,128)(2,1)S(1)}, u32[]{:S(2)}, u32[]{:S(2)}) collective-permute-start(bf16[2,2,4,1024]{3,2,1,0:T(4,128)(2,1)S(1)} %merge.1.refs_0_.refs_8_), channel_id=1, source_target_pairs={{0,4},{4,0},{8,12},{12,8},{1,5},{5,1},{9,13},{13,9},{2,6},{6,2},{1... | collective-permute-start | bytes 98312 | tf_op jit(solution)/shard_map/ppermute | solution.py:35
  17.1 2.2 %pack.1 = (bf16[4,256,512]{2,1,0:T(8,128)(2,1)S(1)}, bf16[4,256,512]{2,1,0:T(8,128)(2,1)S(1)}) custom-call(s32[32]{0:T(128)S(1)} %bitcast.4, bf16[8,2,256,512]{3,2,1,0:T(8,128)(2,1)} %cache_ref.5, bf16[2,2,4,1024]{3,2,1,0:T(4,128)(2,1)S(1)} %merge.1.refs_0_.refs_8_, bf16[2,4,4096]{2,1,0:T(4,128)(2,1)S(1)} %collective-permute-done.4.refs_1_.refs_7_), custom_call_target="tpu_custom_call" | custom-call | flops 10000000000 | bytes 4194304 | tf_op jit(solution)/shard_map/pack/pallas_call | solution.py:222
  19.3 1.5 %collective-permute-start.11 = (bf16[4,256,512]{2,1,0:T(8,128)(2,1)S(1)}, bf16[4,256,512]{2,1,0:T(8,128)(2,1)S(1)}, u32[]{:S(2)}, u32[]{:S(2)}) collective-permute-start(bf16[4,256,512]{2,1,0:T(8,128)(2,1)S(1)} %get-tuple-element.24.refs_5_), channel_id=1, source_target_pairs={{0,1},{1,0},{2,3},{3,2},{4,5},{5,4},{6,7},{7,6},{8,9},{9,8},{10,11... | collective-permute-start | bytes 3145736 | tf_op jit(solution)/shard_map/ppermute | solution.py:35
  20.9 0.6 %collective-permute-done.6.refs_10_ = bf16[2,2,4,1024]{3,2,1,0:T(4,128)(2,1)S(1)} collective-permute-done((bf16[2,2,4,1024]{3,2,1,0:T(4,128)(2,1)S(1)}, bf16[2,2,4,1024]{3,2,1,0:T(4,128)(2,1)S(1)}, u32[]{:S(2)}, u32[]{:S(2)}) %collective-permute-start.6) | collective-permute-done | bytes 32800 | tf_op jit(solution)/shard_map/ppermute | solution.py:35
  21.5 3.8 %attend.1 = (bf16[272,128]{1,0:T(8,128)(2,1)S(1)}, bf16[272,128]{1,0:T(8,128)(2,1)S(1)}, bf16[272,128]{1,0:T(8,128)(2,1)S(1)}, bf16[272,128]{1,0:T(8,128)(2,1)S(1)}) custom-call(s32[32]{0:T(128)S(1)} %bitcast.5, s32[32]{0:T(128)S(1)} %copy-done.1, bf16[1,256,512]{2,1,0:T(8,128)(2,1)S(1)} %get-tuple-element.16.refs_0_, ...), custom_call_target="tpu_custom_call" | custom-call | flops 20000000000 | bytes 4194304 | tf_op jit(solution)/shard_map/attend/pallas_call | solution.py:370
  25.3 0.9 %collective-permute-start.8 = (bf16[272,128]{1,0:T(8,128)(2,1)S(1)}, bf16[272,128]{1,0:T(8,128)(2,1)S(1)}, u32[]{:S(2)}, u32[]{:S(2)}) collective-permute-start(bf16[272,128]{1,0:T(8,128)(2,1)S(1)} %get-tuple-element.27), channel_id=1, source_target_pairs={{0,4},{4,0},{8,12},{12,8},{1,5},{5,1},{9,13},{13,9},{2,6},{6,2},{1... | collective-permute-start | bytes 208904 | tf_op jit(solution)/shard_map/ppermute | solution.py:35
  26.1 2.6 %collective-permute-start.9 = (bf16[272,128]{1,0:T(8,128)(2,1)S(1)}, bf16[272,128]{1,0:T(8,128)(2,1)S(1)}, u32[]{:S(2)}, u32[]{:S(2)}) collective-permute-start(bf16[272,128]{1,0:T(8,128)(2,1)S(1)} %get-tuple-element.28), channel_id=1, source_target_pairs={{0,8},{4,12},{8,0},{12,4},{1,9},{5,13},{9,1},{13,5},{2,10},{6,14},... | collective-permute-start | bytes 208904 | tf_op jit(solution)/shard_map/ppermute | solution.py:35
  28.8 1.0 %collective-permute-start.10 = (bf16[272,128]{1,0:T(8,128)(2,1)S(1)}, bf16[272,128]{1,0:T(8,128)(2,1)S(1)}, u32[]{:S(2)}, u32[]{:S(2)}) collective-permute-start(bf16[272,128]{1,0:T(8,128)(2,1)S(1)} %get-tuple-element.29), channel_id=1, source_target_pairs={{0,12},{4,8},{8,4},{12,0},{1,13},{5,9},{9,5},{13,1},{2,14},{6,10},... | collective-permute-start | bytes 208904 | tf_op jit(solution)/shard_map/ppermute | solution.py:35
  29.7 1.5 %place.4.refs_4_.refs_0_ = bf16[1,16,256,512]{3,2,1,0:T(8,128)(2,1)} custom-call(bf16[4,256,512]{2,1,0:T(8,128)(2,1)S(1)} %get-tuple-element.23.refs_4_.refs_0_, bf16[4,256,512]{2,1,0:T(8,128)(2,1)S(1)} %collective-permute-done.11.refs_1_, bf16[1,256,512]{2,1,0:T(8,128)(2,1)S(1)} %collective-permute-done.3.refs_2_), custom_call_target="tpu_custom_call" | custom-call | bytes 4718592 | tf_op jit(solution)/shard_map/place/pallas_call | solution.py:270
  31.2 3.5 %fetch.2.refs_5_ = bf16[2048,2048]{1,0:T(8,128)(2,1)S(1)} custom-call(bf16[4096,2048]{1,0:T(8,128)(2,1)} %weight_ref.3, bf16[272,128]{1,0:T(8,128)(2,1)S(1)} %get-tuple-element.26.refs_0_, bf16[4,256,512]{2,1,0:T(8,128)(2,1)S(1)} %collective-permute-done.11.refs_1_), custom_call_target="tpu_custom_call" | custom-call | bytes 16777216 | tf_op jit(solution)/shard_map/fetch/pallas_call | solution.py:463
  34.7 0.2 collective-permute-done.10.refs_3_
  35.0 0.4 join.1.refs_0_.refs_1_
  35.5 2.7 %collective-permute-start.14 = (bf16[8,4096]{1,0:T(8,128)(2,1)S(1)}, bf16[8,4096]{1,0:T(8,128)(2,1)S(1)}, u32[]{:S(2)}, u32[]{:S(2)}) collective-permute-start(bf16[8,4096]{1,0:T(8,128)(2,1)S(1)} %join.1.refs_0_.refs_1_), channel_id=1, source_target_pairs={{0,12},{4,8},{8,4},{12,0},{1,13},{5,9},{9,5},{13,1},{2,14},{6,10},... | collective-permute-start | bytes 196616 | tf_op jit(solution)/shard_map/ppermute | solution.py:35
  38.2 0.2 collective-permute-start.13
  38.4 1.5 %collective-permute-start.12 = (bf16[8,4096]{1,0:T(8,128)(2,1)S(1)}, bf16[8,4096]{1,0:T(8,128)(2,1)S(1)}, u32[]{:S(2)}, u32[]{:S(2)}) collective-permute-start(bf16[8,4096]{1,0:T(8,128)(2,1)S(1)} %join.1.refs_0_.refs_1_), channel_id=1, source_target_pairs={{0,4},{4,0},{8,12},{12,8},{1,5},{5,1},{9,13},{13,9},{2,6},{6,2},{1... | collective-permute-start | bytes 196616 | tf_op jit(solution)/shard_map/ppermute | solution.py:35
  39.9 3.5 %fetch.3.refs_6_ = bf16[2048,2048]{1,0:T(8,128)(2,1)S(1)} custom-call(bf16[4096,2048]{1,0:T(8,128)(2,1)} %weight_ref.3, bf16[8,4096]{1,0:T(8,128)(2,1)S(1)} %join.1.refs_0_.refs_1_), custom_call_target="tpu_custom_call" | custom-call | bytes 16777216 | tf_op jit(solution)/shard_map/fetch/pallas_call | solution.py:463
  43.4 0.9 %place.5.refs_0_ = bf16[1,16,256,512]{3,2,1,0:T(8,128)(2,1)} custom-call(bf16[1,16,256,512]{3,2,1,0:T(8,128)(2,1)} %place.4.refs_4_.refs_0_, bf16[8,4096]{1,0:T(8,128)(2,1)S(1)} %join.1.refs_0_.refs_1_, bf16[3,256,512]{2,1,0:T(8,128)(2,1)S(1)} %collective-permute-done.refs_6_.refs_0_.refs_2_), custom_call_target="tpu_custom_call", output_to_operand_aliasing={{}: (0, {})} | custom-call | bytes 1572864 | tf_op jit(solution)/shard_map/place/pallas_call | solution.py:270
  44.4 1.0 %collective-permute-done.13.refs_3_ = bf16[8,4096]{1,0:T(8,128)(2,1)S(1)} collective-permute-done((bf16[8,4096]{1,0:T(8,128)(2,1)S(1)}, bf16[8,4096]{1,0:T(8,128)(2,1)S(1)}, u32[]{:S(2)}, u32[]{:S(2)}) %collective-permute-start.13) | collective-permute-done | bytes 65568 | tf_op jit(solution)/shard_map/ppermute | solution.py:35
  45.3 3.6 %project.1.refs_1_ = bf16[8,4,2048]{2,1,0:T(4,128)(2,1)} custom-call(bf16[3,256,512]{2,1,0:T(8,128)(2,1)S(1)} %collective-permute-done.refs_6_.refs_0_.refs_2_, bf16[8,4096]{1,0:T(8,128)(2,1)S(1)} %join.1.refs_0_.refs_1_, bf16[8,4096]{1,0:T(8,128)(2,1)S(1)} %collective-permute-done.12.refs_2_, bf16[8,4096]{1,0:T(8,128)(2,1)S(1)} %collective-permute-done.13.refs_3_, ...), custom_call_target="tpu_custom_call" | custom-call | flops 536870912 | bytes 16777216 | tf_op jit(solution)/shard_map/project/pallas_call | solution.py:507
  49.0 0.9 %place.6.refs_0_ = bf16[1,16,256,512]{3,2,1,0:T(8,128)(2,1)} custom-call(bf16[1,16,256,512]{3,2,1,0:T(8,128)(2,1)} %place.5.refs_0_, bf16[8,4,2048]{2,1,0:T(4,128)(2,1)} %project.1.refs_1_, bf16[3,256,512]{2,1,0:T(8,128)(2,1)S(1)} %collective-permute-done.15.refs_2_), custom_call_target="tpu_custom_call", output_to_operand_aliasing={{}: (0, {})} | custom-call | bytes 1572864 | tf_op jit(solution)/shard_map/place/pallas_call | solution.py:270
  49.9 0.9 %collective-permute-done.16.refs_2_ = bf16[1,256,512]{2,1,0:T(8,128)(2,1)S(1)} collective-permute-done((bf16[1,256,512]{2,1,0:T(8,128)(2,1)S(1)}, bf16[1,256,512]{2,1,0:T(8,128)(2,1)S(1)}, u32[]{:S(2)}, u32[]{:S(2)}) %collective-permute-start.16) | collective-permute-done | bytes 262176 | tf_op jit(solution)/shard_map/ppermute | solution.py:35
  50.8 0.7 %place.7 = bf16[1,16,256,512]{3,2,1,0:T(8,128)(2,1)} custom-call(bf16[1,16,256,512]{3,2,1,0:T(8,128)(2,1)} %place.6.refs_0_, bf16[8,4,2048]{2,1,0:T(4,128)(2,1)} %project.1.refs_1_, bf16[1,256,512]{2,1,0:T(8,128)(2,1)S(1)} %collective-permute-done.16.refs_2_), custom_call_target="tpu_custom_call", output_to_operand_aliasing={{}: (0, {})} | custom-call | bytes 524288 | tf_op jit(solution)/shard_map/place/pallas_call | solution.py:270
  (20 shorter events, 0.1 us)
Async XLA Ops:
  0.6 5.5 %copy-start = (s32[32,1]{0,1:T(1,128)S(1)}, s32[32,1]{0,1:T(1,128)}, u32[]{:S(2)}) copy-start(s32[32,1]{0,1:T(1,128)} %param.7) | copy-start | bytes 388
  2.2 10.4 %collective-permute-start.3 = (bf16[1,256,512]{2,1,0:T(8,128)(2,1)S(1)}, bf16[1,256,512]{2,1,0:T(8,128)(2,1)S(1)}, u32[]{:S(2)}, u32[]{:S(2)}) collective-permute-start(bf16[1,256,512]{2,1,0:T(8,128)(2,1)S(1)} %get-tuple-element.16.refs_0_), channel_id=1, source_target_pairs={{0,2},{1,3},{2,0},{3,1},{4,6},{5,7},{6,4},{7,5},{8,10},{9,11},{10,... | collective-permute-start | bytes 786440 | tf_op jit(solution)/shard_map/ppermute | solution.py:35
  5.2 7.1 %collective-permute-start.1 = (bf16[2,4,1024]{2,1,0:T(4,128)(2,1)S(1)}, bf16[2,4,1024]{2,1,0:T(4,128)(2,1)S(1)}, u32[]{:S(2)}, u32[]{:S(2)}) collective-permute-start(bf16[2,4,1024]{2,1,0:T(4,128)(2,1)S(1)} %get-tuple-element.20), channel_id=1, source_target_pairs={{0,2},{1,3},{2,0},{3,1},{4,6},{5,7},{6,4},{7,5},{8,10},{9,11},{10,... | collective-permute-start | bytes 49160 | tf_op jit(solution)/shard_map/ppermute | solution.py:35
  5.3 7.3 %collective-permute-start.2 = (bf16[2,4,1024]{2,1,0:T(4,128)(2,1)S(1)}, bf16[2,4,1024]{2,1,0:T(4,128)(2,1)S(1)}, u32[]{:S(2)}, u32[]{:S(2)}) collective-permute-start(bf16[2,4,1024]{2,1,0:T(4,128)(2,1)S(1)} %get-tuple-element.21), channel_id=1, source_target_pairs={{0,3},{1,2},{2,1},{3,0},{4,7},{5,6},{6,5},{7,4},{8,11},{9,10},{10,... | collective-permute-start | bytes 49160 | tf_op jit(solution)/shard_map/ppermute | solution.py:35
  8.3 7.9 %collective-permute-start.4 = (bf16[2,4,4096]{2,1,0:T(4,128)(2,1)S(1)}, bf16[2,4,4096]{2,1,0:T(4,128)(2,1)S(1)}, u32[]{:S(2)}, u32[]{:S(2)}) collective-permute-start(bf16[2,4,4096]{2,1,0:T(4,128)(2,1)S(1)} %get-tuple-element.22), channel_id=1, source_target_pairs={{0,1},{1,0},{2,3},{3,2},{4,5},{5,4},{6,7},{7,6},{8,9},{9,8},{10,11... | collective-permute-start | bytes 196616 | tf_op jit(solution)/shard_map/ppermute | solution.py:35
  9.6 25.3 %collective-permute-start = (bf16[3,256,512]{2,1,0:T(8,128)(2,1)S(1)}, bf16[3,256,512]{2,1,0:T(8,128)(2,1)S(1)}, u32[]{:S(2)}, u32[]{:S(2)}) collective-permute-start(bf16[3,256,512]{2,1,0:T(8,128)(2,1)S(1)} %get-tuple-element.17.refs_1_), channel_id=1, source_target_pairs={{0,2},{1,3},{2,0},{3,1},{4,6},{5,7},{6,4},{7,5},{8,10},{9,11},{10,... | collective-permute-start | bytes 2359304 | tf_op jit(solution)/shard_map/ppermute | solution.py:35
  12.3 36.7 %collective-permute-start.15 = (bf16[3,256,512]{2,1,0:T(8,128)(2,1)S(1)}, bf16[3,256,512]{2,1,0:T(8,128)(2,1)S(1)}, u32[]{:S(2)}, u32[]{:S(2)}) collective-permute-start(bf16[3,256,512]{2,1,0:T(8,128)(2,1)S(1)} %get-tuple-element.18.refs_2_), channel_id=1, source_target_pairs={{0,3},{1,2},{2,1},{3,0},{4,7},{5,6},{6,5},{7,4},{8,11},{9,10},{10,... | collective-permute-start | bytes 2359304 | tf_op jit(solution)/shard_map/ppermute | solution.py:35
  12.6 8.8 %copy-start.1 = (s32[32]{0:T(128)S(1)}, s32[32]{0:T(128)}, u32[]{:S(2)}) copy-start(s32[32]{0:T(128)} %lengths_ref.1) | copy-start | bytes 388
  12.6 6.7 %collective-permute-start.7 = (bf16[2,2,4,1024]{3,2,1,0:T(4,128)(2,1)S(1)}, bf16[2,2,4,1024]{3,2,1,0:T(4,128)(2,1)S(1)}, u32[]{:S(2)}, u32[]{:S(2)}) collective-permute-start(bf16[2,2,4,1024]{3,2,1,0:T(4,128)(2,1)S(1)} %merge.1.refs_0_.refs_8_), channel_id=1, source_target_pairs={{0,12},{4,8},{8,4},{12,0},{1,13},{5,9},{9,5},{13,1},{2,14},{6,10},... | collective-permute-start | bytes 98312 | tf_op jit(solution)/shard_map/ppermute | solution.py:35
  16.2 5.3 %collective-permute-start.6 = (bf16[2,2,4,1024]{3,2,1,0:T(4,128)(2,1)S(1)}, bf16[2,2,4,1024]{3,2,1,0:T(4,128)(2,1)S(1)}, u32[]{:S(2)}, u32[]{:S(2)}) collective-permute-start(bf16[2,2,4,1024]{3,2,1,0:T(4,128)(2,1)S(1)} %merge.1.refs_0_.refs_8_), channel_id=1, source_target_pairs={{0,8},{4,12},{8,0},{12,4},{1,9},{5,13},{9,1},{13,5},{2,10},{6,14},... | collective-permute-start | bytes 98312 | tf_op jit(solution)/shard_map/ppermute | solution.py:35
  16.2 5.3 %collective-permute-start.5 = (bf16[2,2,4,1024]{3,2,1,0:T(4,128)(2,1)S(1)}, bf16[2,2,4,1024]{3,2,1,0:T(4,128)(2,1)S(1)}, u32[]{:S(2)}, u32[]{:S(2)}) collective-permute-start(bf16[2,2,4,1024]{3,2,1,0:T(4,128)(2,1)S(1)} %merge.1.refs_0_.refs_8_), channel_id=1, source_target_pairs={{0,4},{4,0},{8,12},{12,8},{1,5},{5,1},{9,13},{13,9},{2,6},{6,2},{1... | collective-permute-start | bytes 98312 | tf_op jit(solution)/shard_map/ppermute | solution.py:35
  19.3 9.4 %collective-permute-start.11 = (bf16[4,256,512]{2,1,0:T(8,128)(2,1)S(1)}, bf16[4,256,512]{2,1,0:T(8,128)(2,1)S(1)}, u32[]{:S(2)}, u32[]{:S(2)}) collective-permute-start(bf16[4,256,512]{2,1,0:T(8,128)(2,1)S(1)} %get-tuple-element.24.refs_5_), channel_id=1, source_target_pairs={{0,1},{1,0},{2,3},{3,2},{4,5},{5,4},{6,7},{7,6},{8,9},{9,8},{10,11... | collective-permute-start | bytes 3145736 | tf_op jit(solution)/shard_map/ppermute | solution.py:35
  25.3 9.5 %collective-permute-start.8 = (bf16[272,128]{1,0:T(8,128)(2,1)S(1)}, bf16[272,128]{1,0:T(8,128)(2,1)S(1)}, u32[]{:S(2)}, u32[]{:S(2)}) collective-permute-start(bf16[272,128]{1,0:T(8,128)(2,1)S(1)} %get-tuple-element.27), channel_id=1, source_target_pairs={{0,4},{4,0},{8,12},{12,8},{1,5},{5,1},{9,13},{13,9},{2,6},{6,2},{1... | collective-permute-start | bytes 208904 | tf_op jit(solution)/shard_map/ppermute | solution.py:35
  26.1 8.6 %collective-permute-start.9 = (bf16[272,128]{1,0:T(8,128)(2,1)S(1)}, bf16[272,128]{1,0:T(8,128)(2,1)S(1)}, u32[]{:S(2)}, u32[]{:S(2)}) collective-permute-start(bf16[272,128]{1,0:T(8,128)(2,1)S(1)} %get-tuple-element.28), channel_id=1, source_target_pairs={{0,8},{4,12},{8,0},{12,4},{1,9},{5,13},{9,1},{13,5},{2,10},{6,14},... | collective-permute-start | bytes 208904 | tf_op jit(solution)/shard_map/ppermute | solution.py:35
  28.8 6.2 %collective-permute-start.10 = (bf16[272,128]{1,0:T(8,128)(2,1)S(1)}, bf16[272,128]{1,0:T(8,128)(2,1)S(1)}, u32[]{:S(2)}, u32[]{:S(2)}) collective-permute-start(bf16[272,128]{1,0:T(8,128)(2,1)S(1)} %get-tuple-element.29), channel_id=1, source_target_pairs={{0,12},{4,8},{8,4},{12,0},{1,13},{5,9},{9,5},{13,1},{2,14},{6,10},... | collective-permute-start | bytes 208904 | tf_op jit(solution)/shard_map/ppermute | solution.py:35
  35.4 15.4 %collective-permute-start.16 = (bf16[1,256,512]{2,1,0:T(8,128)(2,1)S(1)}, bf16[1,256,512]{2,1,0:T(8,128)(2,1)S(1)}, u32[]{:S(2)}, u32[]{:S(2)}) collective-permute-start(bf16[1,256,512]{2,1,0:T(8,128)(2,1)S(1)} %gate.1), channel_id=1, source_target_pairs={{0,3},{1,2},{2,1},{3,0},{4,7},{5,6},{6,5},{7,4},{8,11},{9,10},{10,... | collective-permute-start | bytes 786440 | tf_op jit(solution)/shard_map/ppermute | solution.py:35
  35.5 8.9 %collective-permute-start.14 = (bf16[8,4096]{1,0:T(8,128)(2,1)S(1)}, bf16[8,4096]{1,0:T(8,128)(2,1)S(1)}, u32[]{:S(2)}, u32[]{:S(2)}) collective-permute-start(bf16[8,4096]{1,0:T(8,128)(2,1)S(1)} %join.1.refs_0_.refs_1_), channel_id=1, source_target_pairs={{0,12},{4,8},{8,4},{12,0},{1,13},{5,9},{9,5},{13,1},{2,14},{6,10},... | collective-permute-start | bytes 196616 | tf_op jit(solution)/shard_map/ppermute | solution.py:35
  38.2 7.2 %collective-permute-start.13 = (bf16[8,4096]{1,0:T(8,128)(2,1)S(1)}, bf16[8,4096]{1,0:T(8,128)(2,1)S(1)}, u32[]{:S(2)}, u32[]{:S(2)}) collective-permute-start(bf16[8,4096]{1,0:T(8,128)(2,1)S(1)} %join.1.refs_0_.refs_1_), channel_id=1, source_target_pairs={{0,8},{4,12},{8,0},{12,4},{1,9},{5,13},{9,1},{13,5},{2,10},{6,14},... | collective-permute-start | bytes 196616 | tf_op jit(solution)/shard_map/ppermute | solution.py:35
  38.4 7.0 %collective-permute-start.12 = (bf16[8,4096]{1,0:T(8,128)(2,1)S(1)}, bf16[8,4096]{1,0:T(8,128)(2,1)S(1)}, u32[]{:S(2)}, u32[]{:S(2)}) collective-permute-start(bf16[8,4096]{1,0:T(8,128)(2,1)S(1)} %join.1.refs_0_.refs_1_), channel_id=1, source_target_pairs={{0,4},{4,0},{8,12},{12,8},{1,5},{5,1},{9,13},{13,9},{2,6},{6,2},{1... | collective-permute-start | bytes 196616 | tf_op jit(solution)/shard_map/ppermute | solution.py:35

commit v21 on v19

--- a/solution.py
+++ b/solution.py
@@ -13,6 +13,7 @@
 CAP = 2
 HIDDEN = -1e30
 STAT_ROWS = 16
+EARLY_ROWS = 4
 
 ANY = pl.BlockSpec(memory_space=pl.ANY)
 HBM = pl.BlockSpec(memory_space=pltpu.HBM)
@@ -121,19 +122,24 @@
     offset, half, _ = piece
     section = lax.axis_index("sec")
     copies = [pltpu.make_async_copy(routing_ref, routed, routing_sem)]
-    for i in range(REQ_GRP - CAP + 1 if full and half < 2 else REQ_GRP):
+    for i in range(EARLY_ROWS):
         copies.append(pltpu.make_async_copy(cache_ref.at[i, half % 2], held.at[i], sem.at[i]))
     for copy in copies:
         copy.start()
     query_copies = start_queries(query_ref, query_out, offsets, query_sem)
     copies[0].wait()
     row, filled = slot_row(own_targets(routed, section), section ^ offset, half // 2)
-    for copy in copies[1:] + query_copies:
-        copy.wait()
+    wanted = pltpu.make_async_copy(cache_ref.at[row, half % 2], held.at[row], sem.at[row])
+    pl.when(row >= EARLY_ROWS)(wanted.start)
+    wanted.wait()
     block = min(32, held.shape[1])
     for first in range(0, held.shape[1], block):
         chosen = held[row, first : first + block]
         out_ref[0, first : first + block] = chosen if full else jnp.where(filled, chosen, jnp.zeros_like(chosen))
+    for i, copy in enumerate(copies[1:]):
+        pl.when(i != row)(copy.wait)
+    for copy in query_copies:
+        copy.wait()
 
 
 def pack_head(routing, cache, queries, piece, section_count, tp_count):

time: 51.9 us -> 51.7 us (level)
  no operation moved by 1% of the time
where the time goes in v21:
time: 51.7 us; the launch traced here: 51.3 us
  Pallas kernels  24.5 us (47%)
  starting transfers between devices  20.3 us (39%)
  waiting for transfers between devices  5.73 us (11%)
  between operations  0.78 us (2%)
    ppermute x17, starting transfers between devices, swap(): return lax.ppermute(value, axis, [(i, i ^ offset) for i in range(count)])  20.3 us
    pallas_call x2, Pallas kernels, fetch(): pl.pallas_call(functools.partial(fetch_kernel, number * size), out_shape=...  6.95 us
    ppermute x17, waiting for transfers between devices, swap(): return lax.ppermute(value, axis, [(i, i ^ offset) for i in range(count)])  5.73 us
    pallas_call x4, Pallas kernels, place(): pl.pallas_call(functools.partial(place_kernel, pieces), out_shape=jax.Sha...  3.99 us
    pallas_call x1, Pallas kernels, attend(): pl.pallas_call(functools.partial(attend_kernel, pieces, section_count, tp...  3.77 us
    pallas_call x1, Pallas kernels, project(): pl.pallas_call(functools.partial(project_kernel, count, min(256, width),...  3.64 us
    pallas_call x1, Pallas kernels, pack(): pl.pallas_call(functools.partial(pack_kernel, pieces, section_count), out...  2.22 us
    pallas_call x1, Pallas kernels, first_pack(): pl.pallas_call(functools.partial(first_pack_kernel, pieces, section_count...  2.2 us
  transfers between devices with their start and end apart: 17, of which 6 were waited for; matrix products, arithmetic and copies ran while one was open for 0% of the time, Pallas kernels for 44%

profile of v21, /device:TPU:0, one launch (start us, length us, event | category | flops | bytes accessed | tf_op | source)
XLA Modules:
  0.0 51.3 jit_solution(5213204726575546432)
XLA Ops:
  0.6 1.4 %pack_head.1 = (bf16[1,256,512]{2,1,0:T(8,128)(2,1)S(1)}, bf16[2,4,1024]{2,1,0:T(4,128)(2,1)S(1)}, bf16[2,4,1024]{2,1,0:T(4,128)(2,1)S(1)}) custom-call(s32[32]{0:T(128)} %bitcast.2, bf16[8,2,256,512]{3,2,1,0:T(8,128)(2,1)} %cache_ref.5, bf16[1,8,4,4096]{3,2,1,0:T(4,128)(2,1)} %query_ref.3), custom_call_target="tpu_custom_call" | custom-call | bytes 2097152 | tf_op jit(solution)/shard_map/pack_head/pallas_call | solution.py:149
  2.0 3.0 %collective-permute-start.3 = (bf16[1,256,512]{2,1,0:T(8,128)(2,1)S(1)}, bf16[1,256,512]{2,1,0:T(8,128)(2,1)S(1)}, u32[]{:S(2)}, u32[]{:S(2)}) collective-permute-start(bf16[1,256,512]{2,1,0:T(8,128)(2,1)S(1)} %get-tuple-element.16.refs_0_), channel_id=1, source_target_pairs={{0,2},{1,3},{2,0},{3,1},{4,6},{5,7},{6,4},{7,5},{8,10},{9,11},{10,... | collective-permute-start | bytes 786440 | tf_op jit(solution)/shard_map/ppermute | solution.py:36
  5.0 0.1 collective-permute-start.1
  5.1 0.8 %collective-permute-start.2 = (bf16[2,4,1024]{2,1,0:T(4,128)(2,1)S(1)}, bf16[2,4,1024]{2,1,0:T(4,128)(2,1)S(1)}, u32[]{:S(2)}, u32[]{:S(2)}) collective-permute-start(bf16[2,4,1024]{2,1,0:T(4,128)(2,1)S(1)} %get-tuple-element.21), channel_id=1, source_target_pairs={{0,3},{1,2},{2,1},{3,0},{4,7},{5,6},{6,5},{7,4},{8,11},{9,10},{10,... | collective-permute-start | bytes 49160 | tf_op jit(solution)/shard_map/ppermute | solution.py:36
  5.9 2.2 %first_pack.1 = (bf16[3,256,512]{2,1,0:T(8,128)(2,1)S(1)}, bf16[3,256,512]{2,1,0:T(8,128)(2,1)S(1)}, bf16[1,256,512]{2,1,0:T(8,128)(2,1)S(1)}, bf16[2,4,4096]{2,1,0:T(4,128)(2,1)S(1)}, bf16[2,4,4096]{2,1,0:T(4,128)(2,1)S(1)}) custom-call(s32[32]{0:T(128)S(1)} %bitcast.3, bf16[8,2,256,512]{3,2,1,0:T(8,128)(2,1)} %cache_ref.5, ...), custom_call_target="tpu_custom_call" | custom-call | bytes 3932160 | tf_op jit(solution)/shard_map/first_pack/pallas_call | solution.py:207
  8.1 1.3 %collective-permute-start.4 = (bf16[2,4,4096]{2,1,0:T(4,128)(2,1)S(1)}, bf16[2,4,4096]{2,1,0:T(4,128)(2,1)S(1)}, u32[]{:S(2)}, u32[]{:S(2)}) collective-permute-start(bf16[2,4,4096]{2,1,0:T(4,128)(2,1)S(1)} %get-tuple-element.22), channel_id=1, source_target_pairs={{0,1},{1,0},{2,3},{3,2},{4,5},{5,4},{6,7},{7,6},{8,9},{9,8},{10,11... | collective-permute-start | bytes 196616 | tf_op jit(solution)/shard_map/ppermute | solution.py:36
  9.4 0.1 collective-permute-start
  9.5 2.6 %collective-permute-done.1.refs_0_ = bf16[2,4,1024]{2,1,0:T(4,128)(2,1)S(1)} collective-permute-done((bf16[2,4,1024]{2,1,0:T(4,128)(2,1)S(1)}, bf16[2,4,1024]{2,1,0:T(4,128)(2,1)S(1)}, u32[]{:S(2)}, u32[]{:S(2)}) %collective-permute-start.1) | collective-permute-done | bytes 16416 | tf_op jit(solution)/shard_map/ppermute | solution.py:36
  12.0 0.3 collective-permute-done.2.refs_1_
  12.4 3.6 %collective-permute-start.7 = (bf16[2,2,4,1024]{3,2,1,0:T(4,128)(2,1)S(1)}, bf16[2,2,4,1024]{3,2,1,0:T(4,128)(2,1)S(1)}, u32[]{:S(2)}, u32[]{:S(2)}) collective-permute-start(bf16[2,2,4,1024]{3,2,1,0:T(4,128)(2,1)S(1)} %merge.1.refs_0_.refs_8_), channel_id=1, source_target_pairs={{0,12},{4,8},{8,4},{12,0},{1,13},{5,9},{9,5},{13,1},{2,14},{6,10},... | collective-permute-start | bytes 98312 | tf_op jit(solution)/shard_map/ppermute | solution.py:36
  16.0 0.9 %collective-permute-start.5 = (bf16[2,2,4,1024]{3,2,1,0:T(4,128)(2,1)S(1)}, bf16[2,2,4,1024]{3,2,1,0:T(4,128)(2,1)S(1)}, u32[]{:S(2)}, u32[]{:S(2)}) collective-permute-start(bf16[2,2,4,1024]{3,2,1,0:T(4,128)(2,1)S(1)} %merge.1.refs_0_.refs_8_), channel_id=1, source_target_pairs={{0,4},{4,0},{8,12},{12,8},{1,5},{5,1},{9,13},{13,9},{2,6},{6,2},{1... | collective-permute-start | bytes 98312 | tf_op jit(solution)/shard_map/ppermute | solution.py:36
  16.9 2.2 %pack.1 = (bf16[4,256,512]{2,1,0:T(8,128)(2,1)S(1)}, bf16[4,256,512]{2,1,0:T(8,128)(2,1)S(1)}) custom-call(s32[32]{0:T(128)S(1)} %bitcast.4, bf16[8,2,256,512]{3,2,1,0:T(8,128)(2,1)} %cache_ref.5, bf16[2,2,4,1024]{3,2,1,0:T(4,128)(2,1)S(1)} %merge.1.refs_0_.refs_8_, bf16[2,4,4096]{2,1,0:T(4,128)(2,1)S(1)} %collective-permute-done.4.refs_1_.refs_7_), custom_call_target="tpu_custom_call" | custom-call | flops 10000000000 | bytes 4194304 | tf_op jit(solution)/shard_map/pack/pallas_call | solution.py:225
  19.1 1.5 %collective-permute-start.11 = (bf16[4,256,512]{2,1,0:T(8,128)(2,1)S(1)}, bf16[4,256,512]{2,1,0:T(8,128)(2,1)S(1)}, u32[]{:S(2)}, u32[]{:S(2)}) collective-permute-start(bf16[4,256,512]{2,1,0:T(8,128)(2,1)S(1)} %get-tuple-element.24.refs_5_), channel_id=1, source_target_pairs={{0,1},{1,0},{2,3},{3,2},{4,5},{5,4},{6,7},{7,6},{8,9},{9,8},{10,11... | collective-permute-start | bytes 3145736 | tf_op jit(solution)/shard_map/ppermute | solution.py:36
  20.6 0.6 %collective-permute-done.6.refs_10_ = bf16[2,2,4,1024]{3,2,1,0:T(4,128)(2,1)S(1)} collective-permute-done((bf16[2,2,4,1024]{3,2,1,0:T(4,128)(2,1)S(1)}, bf16[2,2,4,1024]{3,2,1,0:T(4,128)(2,1)S(1)}, u32[]{:S(2)}, u32[]{:S(2)}) %collective-permute-start.6) | collective-permute-done | bytes 32800 | tf_op jit(solution)/shard_map/ppermute | solution.py:36
  21.3 3.8 %attend.1 = (bf16[272,128]{1,0:T(8,128)(2,1)S(1)}, bf16[272,128]{1,0:T(8,128)(2,1)S(1)}, bf16[272,128]{1,0:T(8,128)(2,1)S(1)}, bf16[272,128]{1,0:T(8,128)(2,1)S(1)}) custom-call(s32[32]{0:T(128)S(1)} %bitcast.5, s32[32]{0:T(128)S(1)} %copy-done.1, bf16[1,256,512]{2,1,0:T(8,128)(2,1)S(1)} %get-tuple-element.16.refs_0_, ...), custom_call_target="tpu_custom_call" | custom-call | flops 20000000000 | bytes 4194304 | tf_op jit(solution)/shard_map/attend/pallas_call | solution.py:373
  25.1 0.9 %collective-permute-start.8 = (bf16[272,128]{1,0:T(8,128)(2,1)S(1)}, bf16[272,128]{1,0:T(8,128)(2,1)S(1)}, u32[]{:S(2)}, u32[]{:S(2)}) collective-permute-start(bf16[272,128]{1,0:T(8,128)(2,1)S(1)} %get-tuple-element.27), channel_id=1, source_target_pairs={{0,4},{4,0},{8,12},{12,8},{1,5},{5,1},{9,13},{13,9},{2,6},{6,2},{1... | collective-permute-start | bytes 208904 | tf_op jit(solution)/shard_map/ppermute | solution.py:36
  25.9 2.6 %collective-permute-start.9 = (bf16[272,128]{1,0:T(8,128)(2,1)S(1)}, bf16[272,128]{1,0:T(8,128)(2,1)S(1)}, u32[]{:S(2)}, u32[]{:S(2)}) collective-permute-start(bf16[272,128]{1,0:T(8,128)(2,1)S(1)} %get-tuple-element.28), channel_id=1, source_target_pairs={{0,8},{4,12},{8,0},{12,4},{1,9},{5,13},{9,1},{13,5},{2,10},{6,14},... | collective-permute-start | bytes 208904 | tf_op jit(solution)/shard_map/ppermute | solution.py:36
  28.6 1.0 %collective-permute-start.10 = (bf16[272,128]{1,0:T(8,128)(2,1)S(1)}, bf16[272,128]{1,0:T(8,128)(2,1)S(1)}, u32[]{:S(2)}, u32[]{:S(2)}) collective-permute-start(bf16[272,128]{1,0:T(8,128)(2,1)S(1)} %get-tuple-element.29), channel_id=1, source_target_pairs={{0,12},{4,8},{8,4},{12,0},{1,13},{5,9},{9,5},{13,1},{2,14},{6,10},... | collective-permute-start | bytes 208904 | tf_op jit(solution)/shard_map/ppermute | solution.py:36
  29.5 1.5 %place.4.refs_4_.refs_0_ = bf16[1,16,256,512]{3,2,1,0:T(8,128)(2,1)} custom-call(bf16[4,256,512]{2,1,0:T(8,128)(2,1)S(1)} %get-tuple-element.23.refs_4_.refs_0_, bf16[4,256,512]{2,1,0:T(8,128)(2,1)S(1)} %collective-permute-done.11.refs_1_, bf16[1,256,512]{2,1,0:T(8,128)(2,1)S(1)} %collective-permute-done.3.refs_2_), custom_call_target="tpu_custom_call" | custom-call | bytes 4718592 | tf_op jit(solution)/shard_map/place/pallas_call | solution.py:273
  31.0 3.5 %fetch.2.refs_5_ = bf16[2048,2048]{1,0:T(8,128)(2,1)S(1)} custom-call(bf16[4096,2048]{1,0:T(8,128)(2,1)} %weight_ref.3, bf16[272,128]{1,0:T(8,128)(2,1)S(1)} %get-tuple-element.26.refs_0_, bf16[4,256,512]{2,1,0:T(8,128)(2,1)S(1)} %collective-permute-done.11.refs_1_), custom_call_target="tpu_custom_call" | custom-call | bytes 16777216 | tf_op jit(solution)/shard_map/fetch/pallas_call | solution.py:466
  34.5 0.3 collective-permute-done.10.refs_3_
  34.8 0.4 join.1.refs_0_.refs_1_
  35.3 2.7 %collective-permute-start.14 = (bf16[8,4096]{1,0:T(8,128)(2,1)S(1)}, bf16[8,4096]{1,0:T(8,128)(2,1)S(1)}, u32[]{:S(2)}, u32[]{:S(2)}) collective-permute-start(bf16[8,4096]{1,0:T(8,128)(2,1)S(1)} %join.1.refs_0_.refs_1_), channel_id=1, source_target_pairs={{0,12},{4,8},{8,4},{12,0},{1,13},{5,9},{9,5},{13,1},{2,14},{6,10},... | collective-permute-start | bytes 196616 | tf_op jit(solution)/shard_map/ppermute | solution.py:36
  37.9 0.2 collective-permute-start.13
  38.2 1.5 %collective-permute-start.12 = (bf16[8,4096]{1,0:T(8,128)(2,1)S(1)}, bf16[8,4096]{1,0:T(8,128)(2,1)S(1)}, u32[]{:S(2)}, u32[]{:S(2)}) collective-permute-start(bf16[8,4096]{1,0:T(8,128)(2,1)S(1)} %join.1.refs_0_.refs_1_), channel_id=1, source_target_pairs={{0,4},{4,0},{8,12},{12,8},{1,5},{5,1},{9,13},{13,9},{2,6},{6,2},{1... | collective-permute-start | bytes 196616 | tf_op jit(solution)/shard_map/ppermute | solution.py:36
  39.7 3.5 %fetch.3.refs_6_ = bf16[2048,2048]{1,0:T(8,128)(2,1)S(1)} custom-call(bf16[4096,2048]{1,0:T(8,128)(2,1)} %weight_ref.3, bf16[8,4096]{1,0:T(8,128)(2,1)S(1)} %join.1.refs_0_.refs_1_), custom_call_target="tpu_custom_call" | custom-call | bytes 16777216 | tf_op jit(solution)/shard_map/fetch/pallas_call | solution.py:466
  43.2 0.9 %place.5.refs_0_ = bf16[1,16,256,512]{3,2,1,0:T(8,128)(2,1)} custom-call(bf16[1,16,256,512]{3,2,1,0:T(8,128)(2,1)} %place.4.refs_4_.refs_0_, bf16[8,4096]{1,0:T(8,128)(2,1)S(1)} %join.1.refs_0_.refs_1_, bf16[3,256,512]{2,1,0:T(8,128)(2,1)S(1)} %collective-permute-done.refs_6_.refs_0_.refs_2_), custom_call_target="tpu_custom_call", output_to_operand_aliasing={{}: (0, {})} | custom-call | bytes 1572864 | tf_op jit(solution)/shard_map/place/pallas_call | solution.py:273
  44.1 1.0 %collective-permute-done.13.refs_3_ = bf16[8,4096]{1,0:T(8,128)(2,1)S(1)} collective-permute-done((bf16[8,4096]{1,0:T(8,128)(2,1)S(1)}, bf16[8,4096]{1,0:T(8,128)(2,1)S(1)}, u32[]{:S(2)}, u32[]{:S(2)}) %collective-permute-start.13) | collective-permute-done | bytes 65568 | tf_op jit(solution)/shard_map/ppermute | solution.py:36
  45.1 3.6 %project.1.refs_1_ = bf16[8,4,2048]{2,1,0:T(4,128)(2,1)} custom-call(bf16[3,256,512]{2,1,0:T(8,128)(2,1)S(1)} %collective-permute-done.refs_6_.refs_0_.refs_2_, bf16[8,4096]{1,0:T(8,128)(2,1)S(1)} %join.1.refs_0_.refs_1_, bf16[8,4096]{1,0:T(8,128)(2,1)S(1)} %collective-permute-done.12.refs_2_, bf16[8,4096]{1,0:T(8,128)(2,1)S(1)} %collective-permute-done.13.refs_3_, ...), custom_call_target="tpu_custom_call" | custom-call | flops 536870912 | bytes 16777216 | tf_op jit(solution)/shard_map/project/pallas_call | solution.py:510
  48.8 0.9 %place.6.refs_0_ = bf16[1,16,256,512]{3,2,1,0:T(8,128)(2,1)} custom-call(bf16[1,16,256,512]{3,2,1,0:T(8,128)(2,1)} %place.5.refs_0_, bf16[8,4,2048]{2,1,0:T(4,128)(2,1)} %project.1.refs_1_, bf16[3,256,512]{2,1,0:T(8,128)(2,1)S(1)} %collective-permute-done.15.refs_2_), custom_call_target="tpu_custom_call", output_to_operand_aliasing={{}: (0, {})} | custom-call | bytes 1572864 | tf_op jit(solution)/shard_map/place/pallas_call | solution.py:273
  49.7 0.9 %collective-permute-done.16.refs_2_ = bf16[1,256,512]{2,1,0:T(8,128)(2,1)S(1)} collective-permute-done((bf16[1,256,512]{2,1,0:T(8,128)(2,1)S(1)}, bf16[1,256,512]{2,1,0:T(8,128)(2,1)S(1)}, u32[]{:S(2)}, u32[]{:S(2)}) %collective-permute-start.16) | collective-permute-done | bytes 262176 | tf_op jit(solution)/shard_map/ppermute | solution.py:36
  50.6 0.7 %place.7 = bf16[1,16,256,512]{3,2,1,0:T(8,128)(2,1)} custom-call(bf16[1,16,256,512]{3,2,1,0:T(8,128)(2,1)} %place.6.refs_0_, bf16[8,4,2048]{2,1,0:T(4,128)(2,1)} %project.1.refs_1_, bf16[1,256,512]{2,1,0:T(8,128)(2,1)S(1)} %collective-permute-done.16.refs_2_), custom_call_target="tpu_custom_call", output_to_operand_aliasing={{}: (0, {})} | custom-call | bytes 524288 | tf_op jit(solution)/shard_map/place/pallas_call | solution.py:273
  (20 shorter events, 0.1 us)
Async XLA Ops:
  0.6 5.3 %copy-start = (s32[32,1]{0,1:T(1,128)S(1)}, s32[32,1]{0,1:T(1,128)}, u32[]{:S(2)}) copy-start(s32[32,1]{0,1:T(1,128)} %param.7) | copy-start | bytes 388
  2.0 10.4 %collective-permute-start.3 = (bf16[1,256,512]{2,1,0:T(8,128)(2,1)S(1)}, bf16[1,256,512]{2,1,0:T(8,128)(2,1)S(1)}, u32[]{:S(2)}, u32[]{:S(2)}) collective-permute-start(bf16[1,256,512]{2,1,0:T(8,128)(2,1)S(1)} %get-tuple-element.16.refs_0_), channel_id=1, source_target_pairs={{0,2},{1,3},{2,0},{3,1},{4,6},{5,7},{6,4},{7,5},{8,10},{9,11},{10,... | collective-permute-start | bytes 786440 | tf_op jit(solution)/shard_map/ppermute | solution.py:36
  5.0 7.1 %collective-permute-start.1 = (bf16[2,4,1024]{2,1,0:T(4,128)(2,1)S(1)}, bf16[2,4,1024]{2,1,0:T(4,128)(2,1)S(1)}, u32[]{:S(2)}, u32[]{:S(2)}) collective-permute-start(bf16[2,4,1024]{2,1,0:T(4,128)(2,1)S(1)} %get-tuple-element.20), channel_id=1, source_target_pairs={{0,2},{1,3},{2,0},{3,1},{4,6},{5,7},{6,4},{7,5},{8,10},{9,11},{10,... | collective-permute-start | bytes 49160 | tf_op jit(solution)/shard_map/ppermute | solution.py:36
  5.1 7.3 %collective-permute-start.2 = (bf16[2,4,1024]{2,1,0:T(4,128)(2,1)S(1)}, bf16[2,4,1024]{2,1,0:T(4,128)(2,1)S(1)}, u32[]{:S(2)}, u32[]{:S(2)}) collective-permute-start(bf16[2,4,1024]{2,1,0:T(4,128)(2,1)S(1)} %get-tuple-element.21), channel_id=1, source_target_pairs={{0,3},{1,2},{2,1},{3,0},{4,7},{5,6},{6,5},{7,4},{8,11},{9,10},{10,... | collective-permute-start | bytes 49160 | tf_op jit(solution)/shard_map/ppermute | solution.py:36
  8.1 7.9 %collective-permute-start.4 = (bf16[2,4,4096]{2,1,0:T(4,128)(2,1)S(1)}, bf16[2,4,4096]{2,1,0:T(4,128)(2,1)S(1)}, u32[]{:S(2)}, u32[]{:S(2)}) collective-permute-start(bf16[2,4,4096]{2,1,0:T(4,128)(2,1)S(1)} %get-tuple-element.22), channel_id=1, source_target_pairs={{0,1},{1,0},{2,3},{3,2},{4,5},{5,4},{6,7},{7,6},{8,9},{9,8},{10,11... | collective-permute-start | bytes 196616 | tf_op jit(solution)/shard_map/ppermute | solution.py:36
  9.4 25.4 %collective-permute-start = (bf16[3,256,512]{2,1,0:T(8,128)(2,1)S(1)}, bf16[3,256,512]{2,1,0:T(8,128)(2,1)S(1)}, u32[]{:S(2)}, u32[]{:S(2)}) collective-permute-start(bf16[3,256,512]{2,1,0:T(8,128)(2,1)S(1)} %get-tuple-element.17.refs_1_), channel_id=1, source_target_pairs={{0,2},{1,3},{2,0},{3,1},{4,6},{5,7},{6,4},{7,5},{8,10},{9,11},{10,... | collective-permute-start | bytes 2359304 | tf_op jit(solution)/shard_map/ppermute | solution.py:36
  12.0 36.7 %collective-permute-start.15 = (bf16[3,256,512]{2,1,0:T(8,128)(2,1)S(1)}, bf16[3,256,512]{2,1,0:T(8,128)(2,1)S(1)}, u32[]{:S(2)}, u32[]{:S(2)}) collective-permute-start(bf16[3,256,512]{2,1,0:T(8,128)(2,1)S(1)} %get-tuple-element.18.refs_2_), channel_id=1, source_target_pairs={{0,3},{1,2},{2,1},{3,0},{4,7},{5,6},{6,5},{7,4},{8,11},{9,10},{10,... | collective-permute-start | bytes 2359304 | tf_op jit(solution)/shard_map/ppermute | solution.py:36
  12.4 8.9 %copy-start.1 = (s32[32]{0:T(128)S(1)}, s32[32]{0:T(128)}, u32[]{:S(2)}) copy-start(s32[32]{0:T(128)} %lengths_ref.1) | copy-start | bytes 388
  12.4 6.7 %collective-permute-start.7 = (bf16[2,2,4,1024]{3,2,1,0:T(4,128)(2,1)S(1)}, bf16[2,2,4,1024]{3,2,1,0:T(4,128)(2,1)S(1)}, u32[]{:S(2)}, u32[]{:S(2)}) collective-permute-start(bf16[2,2,4,1024]{3,2,1,0:T(4,128)(2,1)S(1)} %merge.1.refs_0_.refs_8_), channel_id=1, source_target_pairs={{0,12},{4,8},{8,4},{12,0},{1,13},{5,9},{9,5},{13,1},{2,14},{6,10},... | collective-permute-start | bytes 98312 | tf_op jit(solution)/shard_map/ppermute | solution.py:36
  16.0 5.3 %collective-permute-start.6 = (bf16[2,2,4,1024]{3,2,1,0:T(4,128)(2,1)S(1)}, bf16[2,2,4,1024]{3,2,1,0:T(4,128)(2,1)S(1)}, u32[]{:S(2)}, u32[]{:S(2)}) collective-permute-start(bf16[2,2,4,1024]{3,2,1,0:T(4,128)(2,1)S(1)} %merge.1.refs_0_.refs_8_), channel_id=1, source_target_pairs={{0,8},{4,12},{8,0},{12,4},{1,9},{5,13},{9,1},{13,5},{2,10},{6,14},... | collective-permute-start | bytes 98312 | tf_op jit(solution)/shard_map/ppermute | solution.py:36
  16.0 5.3 %collective-permute-start.5 = (bf16[2,2,4,1024]{3,2,1,0:T(4,128)(2,1)S(1)}, bf16[2,2,4,1024]{3,2,1,0:T(4,128)(2,1)S(1)}, u32[]{:S(2)}, u32[]{:S(2)}) collective-permute-start(bf16[2,2,4,1024]{3,2,1,0:T(4,128)(2,1)S(1)} %merge.1.refs_0_.refs_8_), channel_id=1, source_target_pairs={{0,4},{4,0},{8,12},{12,8},{1,5},{5,1},{9,13},{13,9},{2,6},{6,2},{1... | collective-permute-start | bytes 98312 | tf_op jit(solution)/shard_map/ppermute | solution.py:36
  19.1 9.5 %collective-permute-start.11 = (bf16[4,256,512]{2,1,0:T(8,128)(2,1)S(1)}, bf16[4,256,512]{2,1,0:T(8,128)(2,1)S(1)}, u32[]{:S(2)}, u32[]{:S(2)}) collective-permute-start(bf16[4,256,512]{2,1,0:T(8,128)(2,1)S(1)} %get-tuple-element.24.refs_5_), channel_id=1, source_target_pairs={{0,1},{1,0},{2,3},{3,2},{4,5},{5,4},{6,7},{7,6},{8,9},{9,8},{10,11... | collective-permute-start | bytes 3145736 | tf_op jit(solution)/shard_map/ppermute | solution.py:36
  25.1 9.4 %collective-permute-start.8 = (bf16[272,128]{1,0:T(8,128)(2,1)S(1)}, bf16[272,128]{1,0:T(8,128)(2,1)S(1)}, u32[]{:S(2)}, u32[]{:S(2)}) collective-permute-start(bf16[272,128]{1,0:T(8,128)(2,1)S(1)} %get-tuple-element.27), channel_id=1, source_target_pairs={{0,4},{4,0},{8,12},{12,8},{1,5},{5,1},{9,13},{13,9},{2,6},{6,2},{1... | collective-permute-start | bytes 208904 | tf_op jit(solution)/shard_map/ppermute | solution.py:36
  25.9 8.6 %collective-permute-start.9 = (bf16[272,128]{1,0:T(8,128)(2,1)S(1)}, bf16[272,128]{1,0:T(8,128)(2,1)S(1)}, u32[]{:S(2)}, u32[]{:S(2)}) collective-permute-start(bf16[272,128]{1,0:T(8,128)(2,1)S(1)} %get-tuple-element.28), channel_id=1, source_target_pairs={{0,8},{4,12},{8,0},{12,4},{1,9},{5,13},{9,1},{13,5},{2,10},{6,14},... | collective-permute-start | bytes 208904 | tf_op jit(solution)/shard_map/ppermute | solution.py:36
  28.6 6.2 %collective-permute-start.10 = (bf16[272,128]{1,0:T(8,128)(2,1)S(1)}, bf16[272,128]{1,0:T(8,128)(2,1)S(1)}, u32[]{:S(2)}, u32[]{:S(2)}) collective-permute-start(bf16[272,128]{1,0:T(8,128)(2,1)S(1)} %get-tuple-element.29), channel_id=1, source_target_pairs={{0,12},{4,8},{8,4},{12,0},{1,13},{5,9},{9,5},{13,1},{2,14},{6,10},... | collective-permute-start | bytes 208904 | tf_op jit(solution)/shard_map/ppermute | solution.py:36
  35.2 15.4 %collective-permute-start.16 = (bf16[1,256,512]{2,1,0:T(8,128)(2,1)S(1)}, bf16[1,256,512]{2,1,0:T(8,128)(2,1)S(1)}, u32[]{:S(2)}, u32[]{:S(2)}) collective-permute-start(bf16[1,256,512]{2,1,0:T(8,128)(2,1)S(1)} %gate.1), channel_id=1, source_target_pairs={{0,3},{1,2},{2,1},{3,0},{4,7},{5,6},{6,5},{7,4},{8,11},{9,10},{10,... | collective-permute-start | bytes 786440 | tf_op jit(solution)/shard_map/ppermute | solution.py:36
  35.3 8.9 %collective-permute-start.14 = (bf16[8,4096]{1,0:T(8,128)(2,1)S(1)}, bf16[8,4096]{1,0:T(8,128)(2,1)S(1)}, u32[]{:S(2)}, u32[]{:S(2)}) collective-permute-start(bf16[8,4096]{1,0:T(8,128)(2,1)S(1)} %join.1.refs_0_.refs_1_), channel_id=1, source_target_pairs={{0,12},{4,8},{8,4},{12,0},{1,13},{5,9},{9,5},{13,1},{2,14},{6,10},... | collective-permute-start | bytes 196616 | tf_op jit(solution)/shard_map/ppermute | solution.py:36
  37.9 7.2 %collective-permute-start.13 = (bf16[8,4096]{1,0:T(8,128)(2,1)S(1)}, bf16[8,4096]{1,0:T(8,128)(2,1)S(1)}, u32[]{:S(2)}, u32[]{:S(2)}) collective-permute-start(bf16[8,4096]{1,0:T(8,128)(2,1)S(1)} %join.1.refs_0_.refs_1_), channel_id=1, source_target_pairs={{0,8},{4,12},{8,0},{12,4},{1,9},{5,13},{9,1},{13,5},{2,10},{6,14},... | collective-permute-start | bytes 196616 | tf_op jit(solution)/shard_map/ppermute | solution.py:36
  38.2 7.0 %collective-permute-start.12 = (bf16[8,4096]{1,0:T(8,128)(2,1)S(1)}, bf16[8,4096]{1,0:T(8,128)(2,1)S(1)}, u32[]{:S(2)}, u32[]{:S(2)}) collective-permute-start(bf16[8,4096]{1,0:T(8,128)(2,1)S(1)} %join.1.refs_0_.refs_1_), channel_id=1, source_target_pairs={{0,4},{4,0},{8,12},{12,8},{1,5},{5,1},{9,13},{13,9},{2,6},{6,2},{1... | collective-permute-start | bytes 196616 | tf_op jit(solution)/shard_map/ppermute | solution.py:36

commit v22 on v19

--- a/solution.py
+++ b/solution.py
@@ -138,7 +138,7 @@
 
 def pack_head(routing, cache, queries, piece, section_count, tp_count):
     shape = cache.shape[2:]
-    offsets = range(2, section_count)
+    offsets = range(1, section_count)
     shapes = [jax.ShapeDtypeStruct((1,) + shape, cache.dtype)] + query_shapes(queries, offsets, tp_count)
     head, *parts = pl.pallas_call(
         functools.partial(head_kernel, piece, offsets, section_count * CAP == REQ_GRP),
@@ -161,8 +161,8 @@
 
 def first_pack_kernel(pieces, section_count, routing_ref, cache_ref, query_ref, *refs):
     refs, (sem, query_sem) = refs[:-2], refs[-2:]
-    query_out, cache_out = refs[-2:], refs[-2 - len(pieces) : -2]
-    query_copies = start_queries(query_ref, query_out, range(2), query_sem)
+    query_out, cache_out = refs[-1:], refs[-1 - len(pieces) : -1]
+    query_copies = start_queries(query_ref, query_out, range(1), query_sem)
     start_packing(pieces, section_count, routing_ref, cache_ref, cache_out, sem)()
     for copy in query_copies:
         copy.wait()
@@ -197,7 +197,7 @@
 
 def first_pack(routing, cache, queries, others, pieces, section_count):
     shapes = [jax.ShapeDtypeStruct((count,) + cache.shape[2:], cache.dtype) for _, _, count in pieces]
-    shapes += query_shapes(queries, range(2), 1)
+    shapes += query_shapes(queries, range(1), 1)
     parts = pl.pallas_call(
         functools.partial(first_pack_kernel, pieces, section_count),
         out_shape=shapes,
@@ -527,19 +527,20 @@
     def across(parts, pieces):
         return [swap(part, "sec", piece[0]) for part, piece in zip(parts, pieces)]
 
-    head_caches, far_queries = pack_head(
+    head_caches, (near_query, *far_queries) = pack_head(
         routing, prompt_key_values, queries, head[0], section_count, tp_count
     )
     head_parts = across(head_caches, head)
+    near_query = swap(near_query, "sec", 1)
     far_queries = [swap(part, "sec", n + 2) for n, part in enumerate(far_queries)]
     far_caches, query_parts = first_pack(
         routing, prompt_key_values, queries, head_caches, far, section_count
     )
     far_parts = across(far_caches[:-1], far[:-1])
-    query_parts = [swap(part, "sec", offset) for offset, part in enumerate(query_parts)]
-    merged = merge(far_queries, head_parts)
+    query_parts = [*query_parts, near_query]
+    merged = merge(far_queries, [*head_parts, near_query])
     far_queries = spread(merged, "tp")
-    near_caches = pack(routing, prompt_key_values, [merged, query_parts[1]], near, section_count, 10**10)
+    near_caches = pack(routing, prompt_key_values, [merged], near, section_count, 10**10)
     near_parts = across(near_caches, near)
     caches, pieces = [*head_caches, *far_caches, *near_caches], head + far + near
 

time: 51.9 us -> 51.9 us (level)
  transfers between devices with their start and end apart: 17 -> 17, of which waited for: 6 -> 6; matrix products, arithmetic and copies ran while one was open for 0% -> 0% of each run, Pallas kernels for 44% -> 43%
where the time goes in v22:
time: 51.9 us; the launch traced here: 51.7 us
  Pallas kernels  24.8 us (48%)
  starting transfers between devices  20.3 us (39%)
  waiting for transfers between devices  5.8 us (11%)
  between operations  0.79 us (2%)
    ppermute x17, starting transfers between devices, swap(): return lax.ppermute(value, axis, [(i, i ^ offset) for i in range(count)])  20.3 us
    pallas_call x2, Pallas kernels, fetch(): pl.pallas_call(functools.partial(fetch_kernel, number * size), out_shape=...  6.95 us
    ppermute x17, waiting for transfers between devices, swap(): return lax.ppermute(value, axis, [(i, i ^ offset) for i in range(count)])  5.8 us
    pallas_call x4, Pallas kernels, place(): pl.pallas_call(functools.partial(place_kernel, pieces), out_shape=jax.Sha...  3.99 us
    pallas_call x1, Pallas kernels, attend(): pl.pallas_call(functools.partial(attend_kernel, pieces, section_count, tp...  3.78 us
    pallas_call x1, Pallas kernels, project(): pl.pallas_call(functools.partial(project_kernel, count, min(256, width),...  3.64 us
    pallas_call x1, Pallas kernels, pack(): pl.pallas_call(functools.partial(pack_kernel, pieces, section_count), out...  2.22 us
    pallas_call x1, Pallas kernels, first_pack(): pl.pallas_call(functools.partial(first_pack_kernel, pieces, section_count...  2.18 us
  transfers between devices with their start and end apart: 17, of which 6 were waited for; matrix products, arithmetic and copies ran while one was open for 0% of the time, Pallas kernels for 43%

profile of v22, /device:TPU:0, one launch (start us, length us, event | category | flops | bytes accessed | tf_op | source)
XLA Modules:
  0.0 51.7 jit_solution(4429489361206004970)
XLA Ops:
  0.6 1.6 %pack_head.1 = (bf16[1,256,512]{2,1,0:T(8,128)(2,1)S(1)}, bf16[2,4,4096]{2,1,0:T(4,128)(2,1)S(1)}, bf16[2,4,1024]{2,1,0:T(4,128)(2,1)S(1)}, bf16[2,4,1024]{2,1,0:T(4,128)(2,1)S(1)}) custom-call(s32[32]{0:T(128)} %bitcast.2, bf16[8,2,256,512]{3,2,1,0:T(8,128)(2,1)} %cache_ref.5, bf16[1,8,4,4096]{3,2,1,0:T(4,128)(2,1)} %query_ref.3), custom_call_target="tpu_custom_call" | custom-call | bytes 2097152 | tf_op jit(solution)/shard_map/pack_head/pallas_call | solution.py:143
  2.3 3.0 %collective-permute-start.3 = (bf16[1,256,512]{2,1,0:T(8,128)(2,1)S(1)}, bf16[1,256,512]{2,1,0:T(8,128)(2,1)S(1)}, u32[]{:S(2)}, u32[]{:S(2)}) collective-permute-start(bf16[1,256,512]{2,1,0:T(8,128)(2,1)S(1)} %get-tuple-element.16.refs_0_), channel_id=1, source_target_pairs={{0,2},{1,3},{2,0},{3,1},{4,6},{5,7},{6,4},{7,5},{8,10},{9,11},{10,... | collective-permute-start | bytes 786440 | tf_op jit(solution)/shard_map/ppermute | solution.py:35
  5.3 0.2 collective-permute-start.1
  5.4 1.7 %collective-permute-start.2 = (bf16[2,4,1024]{2,1,0:T(4,128)(2,1)S(1)}, bf16[2,4,1024]{2,1,0:T(4,128)(2,1)S(1)}, u32[]{:S(2)}, u32[]{:S(2)}) collective-permute-start(bf16[2,4,1024]{2,1,0:T(4,128)(2,1)S(1)} %get-tuple-element.21), channel_id=1, source_target_pairs={{0,3},{1,2},{2,1},{3,0},{4,7},{5,6},{6,5},{7,4},{8,11},{9,10},{10,... | collective-permute-start | bytes 49160 | tf_op jit(solution)/shard_map/ppermute | solution.py:35
  7.1 2.2 %first_pack.1 = (bf16[3,256,512]{2,1,0:T(8,128)(2,1)S(1)}, bf16[3,256,512]{2,1,0:T(8,128)(2,1)S(1)}, bf16[1,256,512]{2,1,0:T(8,128)(2,1)S(1)}, bf16[2,4,4096]{2,1,0:T(4,128)(2,1)S(1)}) custom-call(s32[32]{0:T(128)S(1)} %bitcast.3, bf16[8,2,256,512]{3,2,1,0:T(8,128)(2,1)} %cache_ref.5, bf16[1,8,4,4096]{3,2,1,0:T(4,128)(2,1)} %query_ref.3, ...), custom_call_target="tpu_custom_call" | custom-call | bytes 3801088 | tf_op jit(solution)/shard_map/first_pack/pallas_call | solution.py:201
  9.3 0.4 collective-permute-start
  9.7 2.6 %collective-permute-done.1.refs_0_ = bf16[2,4,1024]{2,1,0:T(4,128)(2,1)S(1)} collective-permute-done((bf16[2,4,1024]{2,1,0:T(4,128)(2,1)S(1)}, bf16[2,4,1024]{2,1,0:T(4,128)(2,1)S(1)}, u32[]{:S(2)}, u32[]{:S(2)}) %collective-permute-start.1) | collective-permute-done | bytes 16416 | tf_op jit(solution)/shard_map/ppermute | solution.py:35
  12.3 0.3 collective-permute-done.2.refs_1_
  12.7 3.7 %collective-permute-start.7 = (bf16[2,2,4,1024]{3,2,1,0:T(4,128)(2,1)S(1)}, bf16[2,2,4,1024]{3,2,1,0:T(4,128)(2,1)S(1)}, u32[]{:S(2)}, u32[]{:S(2)}) collective-permute-start(bf16[2,2,4,1024]{3,2,1,0:T(4,128)(2,1)S(1)} %merge.1.refs_0_.refs_8_), channel_id=1, source_target_pairs={{0,12},{4,8},{8,4},{12,0},{1,13},{5,9},{9,5},{13,1},{2,14},{6,10},... | collective-permute-start | bytes 98312 | tf_op jit(solution)/shard_map/ppermute | solution.py:35
  16.4 0.8 %collective-permute-start.5 = (bf16[2,2,4,1024]{3,2,1,0:T(4,128)(2,1)S(1)}, bf16[2,2,4,1024]{3,2,1,0:T(4,128)(2,1)S(1)}, u32[]{:S(2)}, u32[]{:S(2)}) collective-permute-start(bf16[2,2,4,1024]{3,2,1,0:T(4,128)(2,1)S(1)} %merge.1.refs_0_.refs_8_), channel_id=1, source_target_pairs={{0,4},{4,0},{8,12},{12,8},{1,5},{5,1},{9,13},{13,9},{2,6},{6,2},{1... | collective-permute-start | bytes 98312 | tf_op jit(solution)/shard_map/ppermute | solution.py:35
  17.1 2.2 %pack.1 = (bf16[4,256,512]{2,1,0:T(8,128)(2,1)S(1)}, bf16[4,256,512]{2,1,0:T(8,128)(2,1)S(1)}) custom-call(s32[32]{0:T(128)S(1)} %bitcast.4, bf16[8,2,256,512]{3,2,1,0:T(8,128)(2,1)} %cache_ref.5, bf16[2,2,4,1024]{3,2,1,0:T(4,128)(2,1)S(1)} %merge.1.refs_0_.refs_8_), custom_call_target="tpu_custom_call" | custom-call | flops 10000000000 | bytes 4194304 | tf_op jit(solution)/shard_map/pack/pallas_call | solution.py:219
  19.4 1.6 %collective-permute-start.11 = (bf16[4,256,512]{2,1,0:T(8,128)(2,1)S(1)}, bf16[4,256,512]{2,1,0:T(8,128)(2,1)S(1)}, u32[]{:S(2)}, u32[]{:S(2)}) collective-permute-start(bf16[4,256,512]{2,1,0:T(8,128)(2,1)S(1)} %get-tuple-element.24.refs_5_), channel_id=1, source_target_pairs={{0,1},{1,0},{2,3},{3,2},{4,5},{5,4},{6,7},{7,6},{8,9},{9,8},{10,11... | collective-permute-start | bytes 3145736 | tf_op jit(solution)/shard_map/ppermute | solution.py:35
  21.0 0.6 %collective-permute-done.6.refs_10_ = bf16[2,2,4,1024]{3,2,1,0:T(4,128)(2,1)S(1)} collective-permute-done((bf16[2,2,4,1024]{3,2,1,0:T(4,128)(2,1)S(1)}, bf16[2,2,4,1024]{3,2,1,0:T(4,128)(2,1)S(1)}, u32[]{:S(2)}, u32[]{:S(2)}) %collective-permute-start.6) | collective-permute-done | bytes 32800 | tf_op jit(solution)/shard_map/ppermute | solution.py:35
  21.6 3.8 %attend.1 = (bf16[272,128]{1,0:T(8,128)(2,1)S(1)}, bf16[272,128]{1,0:T(8,128)(2,1)S(1)}, bf16[272,128]{1,0:T(8,128)(2,1)S(1)}, bf16[272,128]{1,0:T(8,128)(2,1)S(1)}) custom-call(s32[32]{0:T(128)S(1)} %bitcast.5, s32[32]{0:T(128)S(1)} %copy-done.1, bf16[1,256,512]{2,1,0:T(8,128)(2,1)S(1)} %get-tuple-element.16.refs_0_, ...), custom_call_target="tpu_custom_call" | custom-call | flops 20000000000 | bytes 4194304 | tf_op jit(solution)/shard_map/attend/pallas_call | solution.py:367
  25.4 0.8 %collective-permute-start.8 = (bf16[272,128]{1,0:T(8,128)(2,1)S(1)}, bf16[272,128]{1,0:T(8,128)(2,1)S(1)}, u32[]{:S(2)}, u32[]{:S(2)}) collective-permute-start(bf16[272,128]{1,0:T(8,128)(2,1)S(1)} %get-tuple-element.27), channel_id=1, source_target_pairs={{0,4},{4,0},{8,12},{12,8},{1,5},{5,1},{9,13},{13,9},{2,6},{6,2},{1... | collective-permute-start | bytes 208904 | tf_op jit(solution)/shard_map/ppermute | solution.py:35
  26.3 2.6 %collective-permute-start.9 = (bf16[272,128]{1,0:T(8,128)(2,1)S(1)}, bf16[272,128]{1,0:T(8,128)(2,1)S(1)}, u32[]{:S(2)}, u32[]{:S(2)}) collective-permute-start(bf16[272,128]{1,0:T(8,128)(2,1)S(1)} %get-tuple-element.28), channel_id=1, source_target_pairs={{0,8},{4,12},{8,0},{12,4},{1,9},{5,13},{9,1},{13,5},{2,10},{6,14},... | collective-permute-start | bytes 208904 | tf_op jit(solution)/shard_map/ppermute | solution.py:35
  28.9 1.0 %collective-permute-start.10 = (bf16[272,128]{1,0:T(8,128)(2,1)S(1)}, bf16[272,128]{1,0:T(8,128)(2,1)S(1)}, u32[]{:S(2)}, u32[]{:S(2)}) collective-permute-start(bf16[272,128]{1,0:T(8,128)(2,1)S(1)} %get-tuple-element.29), channel_id=1, source_target_pairs={{0,12},{4,8},{8,4},{12,0},{1,13},{5,9},{9,5},{13,1},{2,14},{6,10},... | collective-permute-start | bytes 208904 | tf_op jit(solution)/shard_map/ppermute | solution.py:35
  29.9 1.5 %place.4.refs_4_.refs_0_ = bf16[1,16,256,512]{3,2,1,0:T(8,128)(2,1)} custom-call(bf16[4,256,512]{2,1,0:T(8,128)(2,1)S(1)} %get-tuple-element.23.refs_4_.refs_0_, bf16[4,256,512]{2,1,0:T(8,128)(2,1)S(1)} %collective-permute-done.11.refs_1_, bf16[1,256,512]{2,1,0:T(8,128)(2,1)S(1)} %collective-permute-done.3.refs_2_), custom_call_target="tpu_custom_call" | custom-call | bytes 4718592 | tf_op jit(solution)/shard_map/place/pallas_call | solution.py:267
  31.4 3.5 %fetch.2.refs_5_ = bf16[2048,2048]{1,0:T(8,128)(2,1)S(1)} custom-call(bf16[4096,2048]{1,0:T(8,128)(2,1)} %weight_ref.3, bf16[272,128]{1,0:T(8,128)(2,1)S(1)} %get-tuple-element.26.refs_0_, bf16[4,256,512]{2,1,0:T(8,128)(2,1)S(1)} %collective-permute-done.11.refs_1_), custom_call_target="tpu_custom_call" | custom-call | bytes 16777216 | tf_op jit(solution)/shard_map/fetch/pallas_call | solution.py:460
  34.9 0.3 collective-permute-done.10.refs_3_
  35.1 0.4 join.1.refs_0_.refs_1_
  35.5 0.1 collective-permute-start.16
  35.6 2.7 %collective-permute-start.14 = (bf16[8,4096]{1,0:T(8,128)(2,1)S(1)}, bf16[8,4096]{1,0:T(8,128)(2,1)S(1)}, u32[]{:S(2)}, u32[]{:S(2)}) collective-permute-start(bf16[8,4096]{1,0:T(8,128)(2,1)S(1)} %join.1.refs_0_.refs_1_), channel_id=1, source_target_pairs={{0,12},{4,8},{8,4},{12,0},{1,13},{5,9},{9,5},{13,1},{2,14},{6,10},... | collective-permute-start | bytes 196616 | tf_op jit(solution)/shard_map/ppermute | solution.py:35
  38.3 0.2 collective-permute-start.13
  38.5 1.5 %collective-permute-start.12 = (bf16[8,4096]{1,0:T(8,128)(2,1)S(1)}, bf16[8,4096]{1,0:T(8,128)(2,1)S(1)}, u32[]{:S(2)}, u32[]{:S(2)}) collective-permute-start(bf16[8,4096]{1,0:T(8,128)(2,1)S(1)} %join.1.refs_0_.refs_1_), channel_id=1, source_target_pairs={{0,4},{4,0},{8,12},{12,8},{1,5},{5,1},{9,13},{13,9},{2,6},{6,2},{1... | collective-permute-start | bytes 196616 | tf_op jit(solution)/shard_map/ppermute | solution.py:35
  40.1 3.5 %fetch.3.refs_6_ = bf16[2048,2048]{1,0:T(8,128)(2,1)S(1)} custom-call(bf16[4096,2048]{1,0:T(8,128)(2,1)} %weight_ref.3, bf16[8,4096]{1,0:T(8,128)(2,1)S(1)} %join.1.refs_0_.refs_1_), custom_call_target="tpu_custom_call" | custom-call | bytes 16777216 | tf_op jit(solution)/shard_map/fetch/pallas_call | solution.py:460
  43.6 0.9 %place.5.refs_0_ = bf16[1,16,256,512]{3,2,1,0:T(8,128)(2,1)} custom-call(bf16[1,16,256,512]{3,2,1,0:T(8,128)(2,1)} %place.4.refs_4_.refs_0_, bf16[8,4096]{1,0:T(8,128)(2,1)S(1)} %join.1.refs_0_.refs_1_, bf16[3,256,512]{2,1,0:T(8,128)(2,1)S(1)} %collective-permute-done.refs_6_.refs_0_.refs_2_), custom_call_target="tpu_custom_call", output_to_operand_aliasing={{}: (0, {})} | custom-call | bytes 1572864 | tf_op jit(solution)/shard_map/place/pallas_call | solution.py:267
  44.5 1.0 %collective-permute-done.13.refs_3_ = bf16[8,4096]{1,0:T(8,128)(2,1)S(1)} collective-permute-done((bf16[8,4096]{1,0:T(8,128)(2,1)S(1)}, bf16[8,4096]{1,0:T(8,128)(2,1)S(1)}, u32[]{:S(2)}, u32[]{:S(2)}) %collective-permute-start.13) | collective-permute-done | bytes 65568 | tf_op jit(solution)/shard_map/ppermute | solution.py:35
  45.5 3.6 %project.1.refs_1_ = bf16[8,4,2048]{2,1,0:T(4,128)(2,1)} custom-call(bf16[3,256,512]{2,1,0:T(8,128)(2,1)S(1)} %collective-permute-done.refs_6_.refs_0_.refs_2_, bf16[8,4096]{1,0:T(8,128)(2,1)S(1)} %join.1.refs_0_.refs_1_, bf16[8,4096]{1,0:T(8,128)(2,1)S(1)} %collective-permute-done.12.refs_2_, bf16[8,4096]{1,0:T(8,128)(2,1)S(1)} %collective-permute-done.13.refs_3_, ...), custom_call_target="tpu_custom_call" | custom-call | flops 536870912 | bytes 16777216 | tf_op jit(solution)/shard_map/project/pallas_call | solution.py:504
  49.1 0.9 %place.6.refs_0_ = bf16[1,16,256,512]{3,2,1,0:T(8,128)(2,1)} custom-call(bf16[1,16,256,512]{3,2,1,0:T(8,128)(2,1)} %place.5.refs_0_, bf16[8,4,2048]{2,1,0:T(4,128)(2,1)} %project.1.refs_1_, bf16[3,256,512]{2,1,0:T(8,128)(2,1)S(1)} %collective-permute-done.15.refs_2_), custom_call_target="tpu_custom_call", output_to_operand_aliasing={{}: (0, {})} | custom-call | bytes 1572864 | tf_op jit(solution)/shard_map/place/pallas_call | solution.py:267
  50.0 0.9 %collective-permute-done.16.refs_2_ = bf16[1,256,512]{2,1,0:T(8,128)(2,1)S(1)} collective-permute-done((bf16[1,256,512]{2,1,0:T(8,128)(2,1)S(1)}, bf16[1,256,512]{2,1,0:T(8,128)(2,1)S(1)}, u32[]{:S(2)}, u32[]{:S(2)}) %collective-permute-start.16) | collective-permute-done | bytes 262176 | tf_op jit(solution)/shard_map/ppermute | solution.py:35
  51.0 0.7 %place.7 = bf16[1,16,256,512]{3,2,1,0:T(8,128)(2,1)} custom-call(bf16[1,16,256,512]{3,2,1,0:T(8,128)(2,1)} %place.6.refs_0_, bf16[8,4,2048]{2,1,0:T(4,128)(2,1)} %project.1.refs_1_, bf16[1,256,512]{2,1,0:T(8,128)(2,1)S(1)} %collective-permute-done.16.refs_2_), custom_call_target="tpu_custom_call", output_to_operand_aliasing={{}: (0, {})} | custom-call | bytes 524288 | tf_op jit(solution)/shard_map/place/pallas_call | solution.py:267
  (20 shorter events, 0.1 us)
Async XLA Ops:
  0.6 6.5 %copy-start = (s32[32,1]{0,1:T(1,128)S(1)}, s32[32,1]{0,1:T(1,128)}, u32[]{:S(2)}) copy-start(s32[32,1]{0,1:T(1,128)} %param.7) | copy-start | bytes 388
  2.3 10.4 %collective-permute-start.3 = (bf16[1,256,512]{2,1,0:T(8,128)(2,1)S(1)}, bf16[1,256,512]{2,1,0:T(8,128)(2,1)S(1)}, u32[]{:S(2)}, u32[]{:S(2)}) collective-permute-start(bf16[1,256,512]{2,1,0:T(8,128)(2,1)S(1)} %get-tuple-element.16.refs_0_), channel_id=1, source_target_pairs={{0,2},{1,3},{2,0},{3,1},{4,6},{5,7},{6,4},{7,5},{8,10},{9,11},{10,... | collective-permute-start | bytes 786440 | tf_op jit(solution)/shard_map/ppermute | solution.py:35
  5.3 7.4 %collective-permute-start.4 = (bf16[2,4,4096]{2,1,0:T(4,128)(2,1)S(1)}, bf16[2,4,4096]{2,1,0:T(4,128)(2,1)S(1)}, u32[]{:S(2)}, u32[]{:S(2)}) collective-permute-start(bf16[2,4,4096]{2,1,0:T(4,128)(2,1)S(1)} %get-tuple-element.22), channel_id=1, source_target_pairs={{0,1},{1,0},{2,3},{3,2},{4,5},{5,4},{6,7},{7,6},{8,9},{9,8},{10,11... | collective-permute-start | bytes 196616 | tf_op jit(solution)/shard_map/ppermute | solution.py:35
  5.3 7.1 %collective-permute-start.1 = (bf16[2,4,1024]{2,1,0:T(4,128)(2,1)S(1)}, bf16[2,4,1024]{2,1,0:T(4,128)(2,1)S(1)}, u32[]{:S(2)}, u32[]{:S(2)}) collective-permute-start(bf16[2,4,1024]{2,1,0:T(4,128)(2,1)S(1)} %get-tuple-element.20), channel_id=1, source_target_pairs={{0,2},{1,3},{2,0},{3,1},{4,6},{5,7},{6,4},{7,5},{8,10},{9,11},{10,... | collective-permute-start | bytes 49160 | tf_op jit(solution)/shard_map/ppermute | solution.py:35
  5.4 7.3 %collective-permute-start.2 = (bf16[2,4,1024]{2,1,0:T(4,128)(2,1)S(1)}, bf16[2,4,1024]{2,1,0:T(4,128)(2,1)S(1)}, u32[]{:S(2)}, u32[]{:S(2)}) collective-permute-start(bf16[2,4,1024]{2,1,0:T(4,128)(2,1)S(1)} %get-tuple-element.21), channel_id=1, source_target_pairs={{0,3},{1,2},{2,1},{3,0},{4,7},{5,6},{6,5},{7,4},{8,11},{9,10},{10,... | collective-permute-start | bytes 49160 | tf_op jit(solution)/shard_map/ppermute | solution.py:35
  9.3 25.8 %collective-permute-start = (bf16[3,256,512]{2,1,0:T(8,128)(2,1)S(1)}, bf16[3,256,512]{2,1,0:T(8,128)(2,1)S(1)}, u32[]{:S(2)}, u32[]{:S(2)}) collective-permute-start(bf16[3,256,512]{2,1,0:T(8,128)(2,1)S(1)} %get-tuple-element.17.refs_1_), channel_id=1, source_target_pairs={{0,2},{1,3},{2,0},{3,1},{4,6},{5,7},{6,4},{7,5},{8,10},{9,11},{10,... | collective-permute-start | bytes 2359304 | tf_op jit(solution)/shard_map/ppermute | solution.py:35
  12.3 36.8 %collective-permute-start.15 = (bf16[3,256,512]{2,1,0:T(8,128)(2,1)S(1)}, bf16[3,256,512]{2,1,0:T(8,128)(2,1)S(1)}, u32[]{:S(2)}, u32[]{:S(2)}) collective-permute-start(bf16[3,256,512]{2,1,0:T(8,128)(2,1)S(1)} %get-tuple-element.18.refs_2_), channel_id=1, source_target_pairs={{0,3},{1,2},{2,1},{3,0},{4,7},{5,6},{6,5},{7,4},{8,11},{9,10},{10,... | collective-permute-start | bytes 2359304 | tf_op jit(solution)/shard_map/ppermute | solution.py:35
  12.7 8.9 %copy-start.1 = (s32[32]{0:T(128)S(1)}, s32[32]{0:T(128)}, u32[]{:S(2)}) copy-start(s32[32]{0:T(128)} %lengths_ref.1) | copy-start | bytes 388
  12.7 6.7 %collective-permute-start.7 = (bf16[2,2,4,1024]{3,2,1,0:T(4,128)(2,1)S(1)}, bf16[2,2,4,1024]{3,2,1,0:T(4,128)(2,1)S(1)}, u32[]{:S(2)}, u32[]{:S(2)}) collective-permute-start(bf16[2,2,4,1024]{3,2,1,0:T(4,128)(2,1)S(1)} %merge.1.refs_0_.refs_8_), channel_id=1, source_target_pairs={{0,12},{4,8},{8,4},{12,0},{1,13},{5,9},{9,5},{13,1},{2,14},{6,10},... | collective-permute-start | bytes 98312 | tf_op jit(solution)/shard_map/ppermute | solution.py:35
  16.4 5.3 %collective-permute-start.6 = (bf16[2,2,4,1024]{3,2,1,0:T(4,128)(2,1)S(1)}, bf16[2,2,4,1024]{3,2,1,0:T(4,128)(2,1)S(1)}, u32[]{:S(2)}, u32[]{:S(2)}) collective-permute-start(bf16[2,2,4,1024]{3,2,1,0:T(4,128)(2,1)S(1)} %merge.1.refs_0_.refs_8_), channel_id=1, source_target_pairs={{0,8},{4,12},{8,0},{12,4},{1,9},{5,13},{9,1},{13,5},{2,10},{6,14},... | collective-permute-start | bytes 98312 | tf_op jit(solution)/shard_map/ppermute | solution.py:35
  16.4 5.3 %collective-permute-start.5 = (bf16[2,2,4,1024]{3,2,1,0:T(4,128)(2,1)S(1)}, bf16[2,2,4,1024]{3,2,1,0:T(4,128)(2,1)S(1)}, u32[]{:S(2)}, u32[]{:S(2)}) collective-permute-start(bf16[2,2,4,1024]{3,2,1,0:T(4,128)(2,1)S(1)} %merge.1.refs_0_.refs_8_), channel_id=1, source_target_pairs={{0,4},{4,0},{8,12},{12,8},{1,5},{5,1},{9,13},{13,9},{2,6},{6,2},{1... | collective-permute-start | bytes 98312 | tf_op jit(solution)/shard_map/ppermute | solution.py:35
  19.4 9.5 %collective-permute-start.11 = (bf16[4,256,512]{2,1,0:T(8,128)(2,1)S(1)}, bf16[4,256,512]{2,1,0:T(8,128)(2,1)S(1)}, u32[]{:S(2)}, u32[]{:S(2)}) collective-permute-start(bf16[4,256,512]{2,1,0:T(8,128)(2,1)S(1)} %get-tuple-element.24.refs_5_), channel_id=1, source_target_pairs={{0,1},{1,0},{2,3},{3,2},{4,5},{5,4},{6,7},{7,6},{8,9},{9,8},{10,11... | collective-permute-start | bytes 3145736 | tf_op jit(solution)/shard_map/ppermute | solution.py:35
  25.4 9.4 %collective-permute-start.8 = (bf16[272,128]{1,0:T(8,128)(2,1)S(1)}, bf16[272,128]{1,0:T(8,128)(2,1)S(1)}, u32[]{:S(2)}, u32[]{:S(2)}) collective-permute-start(bf16[272,128]{1,0:T(8,128)(2,1)S(1)} %get-tuple-element.27), channel_id=1, source_target_pairs={{0,4},{4,0},{8,12},{12,8},{1,5},{5,1},{9,13},{13,9},{2,6},{6,2},{1... | collective-permute-start | bytes 208904 | tf_op jit(solution)/shard_map/ppermute | solution.py:35
  26.3 8.6 %collective-permute-start.9 = (bf16[272,128]{1,0:T(8,128)(2,1)S(1)}, bf16[272,128]{1,0:T(8,128)(2,1)S(1)}, u32[]{:S(2)}, u32[]{:S(2)}) collective-permute-start(bf16[272,128]{1,0:T(8,128)(2,1)S(1)} %get-tuple-element.28), channel_id=1, source_target_pairs={{0,8},{4,12},{8,0},{12,4},{1,9},{5,13},{9,1},{13,5},{2,10},{6,14},... | collective-permute-start | bytes 208904 | tf_op jit(solution)/shard_map/ppermute | solution.py:35
  28.9 6.2 %collective-permute-start.10 = (bf16[272,128]{1,0:T(8,128)(2,1)S(1)}, bf16[272,128]{1,0:T(8,128)(2,1)S(1)}, u32[]{:S(2)}, u32[]{:S(2)}) collective-permute-start(bf16[272,128]{1,0:T(8,128)(2,1)S(1)} %get-tuple-element.29), channel_id=1, source_target_pairs={{0,12},{4,8},{8,4},{12,0},{1,13},{5,9},{9,5},{13,1},{2,14},{6,10},... | collective-permute-start | bytes 208904 | tf_op jit(solution)/shard_map/ppermute | solution.py:35
  35.5 15.4 %collective-permute-start.16 = (bf16[1,256,512]{2,1,0:T(8,128)(2,1)S(1)}, bf16[1,256,512]{2,1,0:T(8,128)(2,1)S(1)}, u32[]{:S(2)}, u32[]{:S(2)}) collective-permute-start(bf16[1,256,512]{2,1,0:T(8,128)(2,1)S(1)} %gate.1), channel_id=1, source_target_pairs={{0,3},{1,2},{2,1},{3,0},{4,7},{5,6},{6,5},{7,4},{8,11},{9,10},{10,... | collective-permute-start | bytes 786440 | tf_op jit(solution)/shard_map/ppermute | solution.py:35
  35.6 8.9 %collective-permute-start.14 = (bf16[8,4096]{1,0:T(8,128)(2,1)S(1)}, bf16[8,4096]{1,0:T(8,128)(2,1)S(1)}, u32[]{:S(2)}, u32[]{:S(2)}) collective-permute-start(bf16[8,4096]{1,0:T(8,128)(2,1)S(1)} %join.1.refs_0_.refs_1_), channel_id=1, source_target_pairs={{0,12},{4,8},{8,4},{12,0},{1,13},{5,9},{9,5},{13,1},{2,14},{6,10},... | collective-permute-start | bytes 196616 | tf_op jit(solution)/shard_map/ppermute | solution.py:35
  38.3 7.2 %collective-permute-start.13 = (bf16[8,4096]{1,0:T(8,128)(2,1)S(1)}, bf16[8,4096]{1,0:T(8,128)(2,1)S(1)}, u32[]{:S(2)}, u32[]{:S(2)}) collective-permute-start(bf16[8,4096]{1,0:T(8,128)(2,1)S(1)} %join.1.refs_0_.refs_1_), channel_id=1, source_target_pairs={{0,8},{4,12},{8,0},{12,4},{1,9},{5,13},{9,1},{13,5},{2,10},{6,14},... | collective-permute-start | bytes 196616 | tf_op jit(solution)/shard_map/ppermute | solution.py:35
  38.5 7.0 %collective-permute-start.12 = (bf16[8,4096]{1,0:T(8,128)(2,1)S(1)}, bf16[8,4096]{1,0:T(8,128)(2,1)S(1)}, u32[]{:S(2)}, u32[]{:S(2)}) collective-permute-start(bf16[8,4096]{1,0:T(8,128)(2,1)S(1)} %join.1.refs_0_.refs_1_), channel_id=1, source_target_pairs={{0,4},{4,0},{8,12},{12,8},{1,5},{5,1},{9,13},{13,9},{2,6},{6,2},{1... | collective-permute-start | bytes 196616 | tf_op jit(solution)/shard_map/ppermute | solution.py:35

commit v23 on v19

--- a/solution.py
+++ b/solution.py
@@ -561,8 +561,8 @@
         layer_out = project(shares, held_weight, far_parts[:-2], samples)
 
     held_cache = place([held_cache], [share], far_parts[:-2], far[:-2], slot_count)
-    for part, piece in zip(far_parts[-2:], far[-2:]):
-        held_cache = place([held_cache, layer_out], [], [part], [piece], slot_count)
+    held_cache = place([held_cache, layer_out], [], far_parts[-2:-1], far[-2:-1], slot_count)
+    held_cache = place([held_cache], [], far_parts[-1:], far[-1:], slot_count)
     held_cache = held_cache.reshape((1, slot_count) + prompt_key_values.shape[1:])
     return (layer_out, held_cache)
 

time: 51.9 us -> 51.9 us (level)
  no operation moved by 1% of the time
where the time goes in v23:
time: 51.9 us; the launch traced here: 51.5 us
  Pallas kernels  24.7 us (48%)
  starting transfers between devices  20.3 us (39%)
  waiting for transfers between devices  5.72 us (11%)
  between operations  0.78 us (2%)
    ppermute x17, starting transfers between devices, swap(): return lax.ppermute(value, axis, [(i, i ^ offset) for i in range(count)])  20.3 us
    pallas_call x2, Pallas kernels, fetch(): pl.pallas_call(functools.partial(fetch_kernel, number * size), out_shape=...  6.95 us
    ppermute x17, waiting for transfers between devices, swap(): return lax.ppermute(value, axis, [(i, i ^ offset) for i in range(count)])  5.72 us
    pallas_call x4, Pallas kernels, place(): pl.pallas_call(functools.partial(place_kernel, pieces), out_shape=jax.Sha...  3.99 us
    pallas_call x1, Pallas kernels, attend(): pl.pallas_call(functools.partial(attend_kernel, pieces, section_count, tp...  3.77 us
    pallas_call x1, Pallas kernels, project(): pl.pallas_call(functools.partial(project_kernel, count, min(256, width),...  3.64 us
    pallas_call x1, Pallas kernels, pack(): pl.pallas_call(functools.partial(pack_kernel, pieces, section_count), out...  2.22 us
    pallas_call x1, Pallas kernels, first_pack(): pl.pallas_call(functools.partial(first_pack_kernel, pieces, section_count...  2.2 us
  transfers between devices with their start and end apart: 17, of which 6 were waited for; matrix products, arithmetic and copies ran while one was open for 0% of the time, Pallas kernels for 44%

profile of v23, /device:TPU:0, one launch (start us, length us, event | category | flops | bytes accessed | tf_op | source)
XLA Modules:
  0.0 51.5 jit_solution(13256508011358256142)
XLA Ops:
  0.6 1.6 %pack_head.1 = (bf16[1,256,512]{2,1,0:T(8,128)(2,1)S(1)}, bf16[2,4,1024]{2,1,0:T(4,128)(2,1)S(1)}, bf16[2,4,1024]{2,1,0:T(4,128)(2,1)S(1)}) custom-call(s32[32]{0:T(128)} %bitcast.2, bf16[8,2,256,512]{3,2,1,0:T(8,128)(2,1)} %cache_ref.5, bf16[1,8,4,4096]{3,2,1,0:T(4,128)(2,1)} %query_ref.3), custom_call_target="tpu_custom_call" | custom-call | bytes 2097152 | tf_op jit(solution)/shard_map/pack_head/pallas_call | solution.py:143
  2.2 3.0 %collective-permute-start.3 = (bf16[1,256,512]{2,1,0:T(8,128)(2,1)S(1)}, bf16[1,256,512]{2,1,0:T(8,128)(2,1)S(1)}, u32[]{:S(2)}, u32[]{:S(2)}) collective-permute-start(bf16[1,256,512]{2,1,0:T(8,128)(2,1)S(1)} %get-tuple-element.16.refs_0_), channel_id=1, source_target_pairs={{0,2},{1,3},{2,0},{3,1},{4,6},{5,7},{6,4},{7,5},{8,10},{9,11},{10,... | collective-permute-start | bytes 786440 | tf_op jit(solution)/shard_map/ppermute | solution.py:35
  5.2 0.1 collective-permute-start.1
  5.3 0.8 %collective-permute-start.2 = (bf16[2,4,1024]{2,1,0:T(4,128)(2,1)S(1)}, bf16[2,4,1024]{2,1,0:T(4,128)(2,1)S(1)}, u32[]{:S(2)}, u32[]{:S(2)}) collective-permute-start(bf16[2,4,1024]{2,1,0:T(4,128)(2,1)S(1)} %get-tuple-element.21), channel_id=1, source_target_pairs={{0,3},{1,2},{2,1},{3,0},{4,7},{5,6},{6,5},{7,4},{8,11},{9,10},{10,... | collective-permute-start | bytes 49160 | tf_op jit(solution)/shard_map/ppermute | solution.py:35
  6.1 2.2 %first_pack.1 = (bf16[3,256,512]{2,1,0:T(8,128)(2,1)S(1)}, bf16[3,256,512]{2,1,0:T(8,128)(2,1)S(1)}, bf16[1,256,512]{2,1,0:T(8,128)(2,1)S(1)}, bf16[2,4,4096]{2,1,0:T(4,128)(2,1)S(1)}, bf16[2,4,4096]{2,1,0:T(4,128)(2,1)S(1)}) custom-call(s32[32]{0:T(128)S(1)} %bitcast.3, bf16[8,2,256,512]{3,2,1,0:T(8,128)(2,1)} %cache_ref.5, ...), custom_call_target="tpu_custom_call" | custom-call | bytes 3932160 | tf_op jit(solution)/shard_map/first_pack/pallas_call | solution.py:201
  8.3 1.3 %collective-permute-start.4 = (bf16[2,4,4096]{2,1,0:T(4,128)(2,1)S(1)}, bf16[2,4,4096]{2,1,0:T(4,128)(2,1)S(1)}, u32[]{:S(2)}, u32[]{:S(2)}) collective-permute-start(bf16[2,4,4096]{2,1,0:T(4,128)(2,1)S(1)} %get-tuple-element.22), channel_id=1, source_target_pairs={{0,1},{1,0},{2,3},{3,2},{4,5},{5,4},{6,7},{7,6},{8,9},{9,8},{10,11... | collective-permute-start | bytes 196616 | tf_op jit(solution)/shard_map/ppermute | solution.py:35
  9.6 0.1 collective-permute-start
  9.7 2.6 %collective-permute-done.1.refs_0_ = bf16[2,4,1024]{2,1,0:T(4,128)(2,1)S(1)} collective-permute-done((bf16[2,4,1024]{2,1,0:T(4,128)(2,1)S(1)}, bf16[2,4,1024]{2,1,0:T(4,128)(2,1)S(1)}, u32[]{:S(2)}, u32[]{:S(2)}) %collective-permute-start.1) | collective-permute-done | bytes 16416 | tf_op jit(solution)/shard_map/ppermute | solution.py:35
  12.3 0.3 collective-permute-done.2.refs_1_
  12.6 3.6 %collective-permute-start.7 = (bf16[2,2,4,1024]{3,2,1,0:T(4,128)(2,1)S(1)}, bf16[2,2,4,1024]{3,2,1,0:T(4,128)(2,1)S(1)}, u32[]{:S(2)}, u32[]{:S(2)}) collective-permute-start(bf16[2,2,4,1024]{3,2,1,0:T(4,128)(2,1)S(1)} %merge.1.refs_0_.refs_8_), channel_id=1, source_target_pairs={{0,12},{4,8},{8,4},{12,0},{1,13},{5,9},{9,5},{13,1},{2,14},{6,10},... | collective-permute-start | bytes 98312 | tf_op jit(solution)/shard_map/ppermute | solution.py:35
  16.2 0.9 %collective-permute-start.5 = (bf16[2,2,4,1024]{3,2,1,0:T(4,128)(2,1)S(1)}, bf16[2,2,4,1024]{3,2,1,0:T(4,128)(2,1)S(1)}, u32[]{:S(2)}, u32[]{:S(2)}) collective-permute-start(bf16[2,2,4,1024]{3,2,1,0:T(4,128)(2,1)S(1)} %merge.1.refs_0_.refs_8_), channel_id=1, source_target_pairs={{0,4},{4,0},{8,12},{12,8},{1,5},{5,1},{9,13},{13,9},{2,6},{6,2},{1... | collective-permute-start | bytes 98312 | tf_op jit(solution)/shard_map/ppermute | solution.py:35
  17.1 2.2 %pack.1 = (bf16[4,256,512]{2,1,0:T(8,128)(2,1)S(1)}, bf16[4,256,512]{2,1,0:T(8,128)(2,1)S(1)}) custom-call(s32[32]{0:T(128)S(1)} %bitcast.4, bf16[8,2,256,512]{3,2,1,0:T(8,128)(2,1)} %cache_ref.5, bf16[2,2,4,1024]{3,2,1,0:T(4,128)(2,1)S(1)} %merge.1.refs_0_.refs_8_, bf16[2,4,4096]{2,1,0:T(4,128)(2,1)S(1)} %collective-permute-done.4.refs_1_.refs_7_), custom_call_target="tpu_custom_call" | custom-call | flops 10000000000 | bytes 4194304 | tf_op jit(solution)/shard_map/pack/pallas_call | solution.py:219
  19.3 1.5 %collective-permute-start.11 = (bf16[4,256,512]{2,1,0:T(8,128)(2,1)S(1)}, bf16[4,256,512]{2,1,0:T(8,128)(2,1)S(1)}, u32[]{:S(2)}, u32[]{:S(2)}) collective-permute-start(bf16[4,256,512]{2,1,0:T(8,128)(2,1)S(1)} %get-tuple-element.24.refs_5_), channel_id=1, source_target_pairs={{0,1},{1,0},{2,3},{3,2},{4,5},{5,4},{6,7},{7,6},{8,9},{9,8},{10,11... | collective-permute-start | bytes 3145736 | tf_op jit(solution)/shard_map/ppermute | solution.py:35
  20.9 0.6 %collective-permute-done.6.refs_10_ = bf16[2,2,4,1024]{3,2,1,0:T(4,128)(2,1)S(1)} collective-permute-done((bf16[2,2,4,1024]{3,2,1,0:T(4,128)(2,1)S(1)}, bf16[2,2,4,1024]{3,2,1,0:T(4,128)(2,1)S(1)}, u32[]{:S(2)}, u32[]{:S(2)}) %collective-permute-start.6) | collective-permute-done | bytes 32800 | tf_op jit(solution)/shard_map/ppermute | solution.py:35
  21.5 3.8 %attend.1 = (bf16[272,128]{1,0:T(8,128)(2,1)S(1)}, bf16[272,128]{1,0:T(8,128)(2,1)S(1)}, bf16[272,128]{1,0:T(8,128)(2,1)S(1)}, bf16[272,128]{1,0:T(8,128)(2,1)S(1)}) custom-call(s32[32]{0:T(128)S(1)} %bitcast.5, s32[32]{0:T(128)S(1)} %copy-done.1, bf16[1,256,512]{2,1,0:T(8,128)(2,1)S(1)} %get-tuple-element.16.refs_0_, ...), custom_call_target="tpu_custom_call" | custom-call | flops 20000000000 | bytes 4194304 | tf_op jit(solution)/shard_map/attend/pallas_call | solution.py:367
  25.3 0.9 %collective-permute-start.8 = (bf16[272,128]{1,0:T(8,128)(2,1)S(1)}, bf16[272,128]{1,0:T(8,128)(2,1)S(1)}, u32[]{:S(2)}, u32[]{:S(2)}) collective-permute-start(bf16[272,128]{1,0:T(8,128)(2,1)S(1)} %get-tuple-element.27), channel_id=1, source_target_pairs={{0,4},{4,0},{8,12},{12,8},{1,5},{5,1},{9,13},{13,9},{2,6},{6,2},{1... | collective-permute-start | bytes 208904 | tf_op jit(solution)/shard_map/ppermute | solution.py:35
  26.1 2.6 %collective-permute-start.9 = (bf16[272,128]{1,0:T(8,128)(2,1)S(1)}, bf16[272,128]{1,0:T(8,128)(2,1)S(1)}, u32[]{:S(2)}, u32[]{:S(2)}) collective-permute-start(bf16[272,128]{1,0:T(8,128)(2,1)S(1)} %get-tuple-element.28), channel_id=1, source_target_pairs={{0,8},{4,12},{8,0},{12,4},{1,9},{5,13},{9,1},{13,5},{2,10},{6,14},... | collective-permute-start | bytes 208904 | tf_op jit(solution)/shard_map/ppermute | solution.py:35
  28.8 1.0 %collective-permute-start.10 = (bf16[272,128]{1,0:T(8,128)(2,1)S(1)}, bf16[272,128]{1,0:T(8,128)(2,1)S(1)}, u32[]{:S(2)}, u32[]{:S(2)}) collective-permute-start(bf16[272,128]{1,0:T(8,128)(2,1)S(1)} %get-tuple-element.29), channel_id=1, source_target_pairs={{0,12},{4,8},{8,4},{12,0},{1,13},{5,9},{9,5},{13,1},{2,14},{6,10},... | collective-permute-start | bytes 208904 | tf_op jit(solution)/shard_map/ppermute | solution.py:35
  29.7 1.5 %place.4.refs_4_.refs_0_ = bf16[1,16,256,512]{3,2,1,0:T(8,128)(2,1)} custom-call(bf16[4,256,512]{2,1,0:T(8,128)(2,1)S(1)} %get-tuple-element.23.refs_4_.refs_0_, bf16[4,256,512]{2,1,0:T(8,128)(2,1)S(1)} %collective-permute-done.11.refs_1_, bf16[1,256,512]{2,1,0:T(8,128)(2,1)S(1)} %collective-permute-done.3.refs_2_), custom_call_target="tpu_custom_call" | custom-call | bytes 4718592 | tf_op jit(solution)/shard_map/place/pallas_call | solution.py:267
  31.2 3.5 %fetch.2.refs_5_ = bf16[2048,2048]{1,0:T(8,128)(2,1)S(1)} custom-call(bf16[4096,2048]{1,0:T(8,128)(2,1)} %weight_ref.3, bf16[272,128]{1,0:T(8,128)(2,1)S(1)} %get-tuple-element.26.refs_0_, bf16[4,256,512]{2,1,0:T(8,128)(2,1)S(1)} %collective-permute-done.11.refs_1_), custom_call_target="tpu_custom_call" | custom-call | bytes 16777216 | tf_op jit(solution)/shard_map/fetch/pallas_call | solution.py:460
  34.7 0.3 collective-permute-done.10.refs_3_
  35.0 0.4 join.1.refs_0_.refs_1_
  35.5 2.7 %collective-permute-start.14 = (bf16[8,4096]{1,0:T(8,128)(2,1)S(1)}, bf16[8,4096]{1,0:T(8,128)(2,1)S(1)}, u32[]{:S(2)}, u32[]{:S(2)}) collective-permute-start(bf16[8,4096]{1,0:T(8,128)(2,1)S(1)} %join.1.refs_0_.refs_1_), channel_id=1, source_target_pairs={{0,12},{4,8},{8,4},{12,0},{1,13},{5,9},{9,5},{13,1},{2,14},{6,10},... | collective-permute-start | bytes 196616 | tf_op jit(solution)/shard_map/ppermute | solution.py:35
  38.2 0.2 collective-permute-start.13
  38.4 1.5 %collective-permute-start.12 = (bf16[8,4096]{1,0:T(8,128)(2,1)S(1)}, bf16[8,4096]{1,0:T(8,128)(2,1)S(1)}, u32[]{:S(2)}, u32[]{:S(2)}) collective-permute-start(bf16[8,4096]{1,0:T(8,128)(2,1)S(1)} %join.1.refs_0_.refs_1_), channel_id=1, source_target_pairs={{0,4},{4,0},{8,12},{12,8},{1,5},{5,1},{9,13},{13,9},{2,6},{6,2},{1... | collective-permute-start | bytes 196616 | tf_op jit(solution)/shard_map/ppermute | solution.py:35
  39.9 3.5 %fetch.3.refs_6_ = bf16[2048,2048]{1,0:T(8,128)(2,1)S(1)} custom-call(bf16[4096,2048]{1,0:T(8,128)(2,1)} %weight_ref.3, bf16[8,4096]{1,0:T(8,128)(2,1)S(1)} %join.1.refs_0_.refs_1_), custom_call_target="tpu_custom_call" | custom-call | bytes 16777216 | tf_op jit(solution)/shard_map/fetch/pallas_call | solution.py:460
  43.4 0.9 %place.5.refs_0_ = bf16[1,16,256,512]{3,2,1,0:T(8,128)(2,1)} custom-call(bf16[1,16,256,512]{3,2,1,0:T(8,128)(2,1)} %place.4.refs_4_.refs_0_, bf16[8,4096]{1,0:T(8,128)(2,1)S(1)} %join.1.refs_0_.refs_1_, bf16[3,256,512]{2,1,0:T(8,128)(2,1)S(1)} %collective-permute-done.refs_6_.refs_0_.refs_2_), custom_call_target="tpu_custom_call", output_to_operand_aliasing={{}: (0, {})} | custom-call | bytes 1572864 | tf_op jit(solution)/shard_map/place/pallas_call | solution.py:267
  44.3 1.0 %collective-permute-done.13.refs_3_ = bf16[8,4096]{1,0:T(8,128)(2,1)S(1)} collective-permute-done((bf16[8,4096]{1,0:T(8,128)(2,1)S(1)}, bf16[8,4096]{1,0:T(8,128)(2,1)S(1)}, u32[]{:S(2)}, u32[]{:S(2)}) %collective-permute-start.13) | collective-permute-done | bytes 65568 | tf_op jit(solution)/shard_map/ppermute | solution.py:35
  45.4 3.6 %project.1.refs_1_ = bf16[8,4,2048]{2,1,0:T(4,128)(2,1)} custom-call(bf16[3,256,512]{2,1,0:T(8,128)(2,1)S(1)} %collective-permute-done.refs_6_.refs_0_.refs_2_, bf16[8,4096]{1,0:T(8,128)(2,1)S(1)} %join.1.refs_0_.refs_1_, bf16[8,4096]{1,0:T(8,128)(2,1)S(1)} %collective-permute-done.12.refs_2_, bf16[8,4096]{1,0:T(8,128)(2,1)S(1)} %collective-permute-done.13.refs_3_, ...), custom_call_target="tpu_custom_call" | custom-call | flops 536870912 | bytes 16777216 | tf_op jit(solution)/shard_map/project/pallas_call | solution.py:504
  49.0 0.9 %place.6.refs_0_ = bf16[1,16,256,512]{3,2,1,0:T(8,128)(2,1)} custom-call(bf16[1,16,256,512]{3,2,1,0:T(8,128)(2,1)} %place.5.refs_0_, bf16[8,4,2048]{2,1,0:T(4,128)(2,1)} %project.1.refs_1_, bf16[3,256,512]{2,1,0:T(8,128)(2,1)S(1)} %collective-permute-done.15.refs_2_), custom_call_target="tpu_custom_call", output_to_operand_aliasing={{}: (0, {})} | custom-call | bytes 1572864 | tf_op jit(solution)/shard_map/place/pallas_call | solution.py:267
  49.9 0.9 %collective-permute-done.16.refs_1_ = bf16[1,256,512]{2,1,0:T(8,128)(2,1)S(1)} collective-permute-done((bf16[1,256,512]{2,1,0:T(8,128)(2,1)S(1)}, bf16[1,256,512]{2,1,0:T(8,128)(2,1)S(1)}, u32[]{:S(2)}, u32[]{:S(2)}) %collective-permute-start.16) | collective-permute-done | bytes 262176 | tf_op jit(solution)/shard_map/ppermute | solution.py:35
  50.8 0.7 %place.7 = bf16[1,16,256,512]{3,2,1,0:T(8,128)(2,1)} custom-call(bf16[1,16,256,512]{3,2,1,0:T(8,128)(2,1)} %place.6.refs_0_, bf16[1,256,512]{2,1,0:T(8,128)(2,1)S(1)} %collective-permute-done.16.refs_1_), custom_call_target="tpu_custom_call", output_to_operand_aliasing={{}: (0, {})} | custom-call | bytes 524288 | tf_op jit(solution)/shard_map/place/pallas_call | solution.py:267
  (20 shorter events, 0.1 us)
Async XLA Ops:
  0.6 5.5 %copy-start = (s32[32,1]{0,1:T(1,128)S(1)}, s32[32,1]{0,1:T(1,128)}, u32[]{:S(2)}) copy-start(s32[32,1]{0,1:T(1,128)} %param.7) | copy-start | bytes 388
  2.2 10.4 %collective-permute-start.3 = (bf16[1,256,512]{2,1,0:T(8,128)(2,1)S(1)}, bf16[1,256,512]{2,1,0:T(8,128)(2,1)S(1)}, u32[]{:S(2)}, u32[]{:S(2)}) collective-permute-start(bf16[1,256,512]{2,1,0:T(8,128)(2,1)S(1)} %get-tuple-element.16.refs_0_), channel_id=1, source_target_pairs={{0,2},{1,3},{2,0},{3,1},{4,6},{5,7},{6,4},{7,5},{8,10},{9,11},{10,... | collective-permute-start | bytes 786440 | tf_op jit(solution)/shard_map/ppermute | solution.py:35
  5.2 7.1 %collective-permute-start.1 = (bf16[2,4,1024]{2,1,0:T(4,128)(2,1)S(1)}, bf16[2,4,1024]{2,1,0:T(4,128)(2,1)S(1)}, u32[]{:S(2)}, u32[]{:S(2)}) collective-permute-start(bf16[2,4,1024]{2,1,0:T(4,128)(2,1)S(1)} %get-tuple-element.20), channel_id=1, source_target_pairs={{0,2},{1,3},{2,0},{3,1},{4,6},{5,7},{6,4},{7,5},{8,10},{9,11},{10,... | collective-permute-start | bytes 49160 | tf_op jit(solution)/shard_map/ppermute | solution.py:35
  5.3 7.3 %collective-permute-start.2 = (bf16[2,4,1024]{2,1,0:T(4,128)(2,1)S(1)}, bf16[2,4,1024]{2,1,0:T(4,128)(2,1)S(1)}, u32[]{:S(2)}, u32[]{:S(2)}) collective-permute-start(bf16[2,4,1024]{2,1,0:T(4,128)(2,1)S(1)} %get-tuple-element.21), channel_id=1, source_target_pairs={{0,3},{1,2},{2,1},{3,0},{4,7},{5,6},{6,5},{7,4},{8,11},{9,10},{10,... | collective-permute-start | bytes 49160 | tf_op jit(solution)/shard_map/ppermute | solution.py:35
  8.3 7.9 %collective-permute-start.4 = (bf16[2,4,4096]{2,1,0:T(4,128)(2,1)S(1)}, bf16[2,4,4096]{2,1,0:T(4,128)(2,1)S(1)}, u32[]{:S(2)}, u32[]{:S(2)}) collective-permute-start(bf16[2,4,4096]{2,1,0:T(4,128)(2,1)S(1)} %get-tuple-element.22), channel_id=1, source_target_pairs={{0,1},{1,0},{2,3},{3,2},{4,5},{5,4},{6,7},{7,6},{8,9},{9,8},{10,11... | collective-permute-start | bytes 196616 | tf_op jit(solution)/shard_map/ppermute | solution.py:35
  9.6 25.4 %collective-permute-start = (bf16[3,256,512]{2,1,0:T(8,128)(2,1)S(1)}, bf16[3,256,512]{2,1,0:T(8,128)(2,1)S(1)}, u32[]{:S(2)}, u32[]{:S(2)}) collective-permute-start(bf16[3,256,512]{2,1,0:T(8,128)(2,1)S(1)} %get-tuple-element.17.refs_1_), channel_id=1, source_target_pairs={{0,2},{1,3},{2,0},{3,1},{4,6},{5,7},{6,4},{7,5},{8,10},{9,11},{10,... | collective-permute-start | bytes 2359304 | tf_op jit(solution)/shard_map/ppermute | solution.py:35
  12.3 36.7 %collective-permute-start.15 = (bf16[3,256,512]{2,1,0:T(8,128)(2,1)S(1)}, bf16[3,256,512]{2,1,0:T(8,128)(2,1)S(1)}, u32[]{:S(2)}, u32[]{:S(2)}) collective-permute-start(bf16[3,256,512]{2,1,0:T(8,128)(2,1)S(1)} %get-tuple-element.18.refs_2_), channel_id=1, source_target_pairs={{0,3},{1,2},{2,1},{3,0},{4,7},{5,6},{6,5},{7,4},{8,11},{9,10},{10,... | collective-permute-start | bytes 2359304 | tf_op jit(solution)/shard_map/ppermute | solution.py:35
  12.6 8.8 %copy-start.1 = (s32[32]{0:T(128)S(1)}, s32[32]{0:T(128)}, u32[]{:S(2)}) copy-start(s32[32]{0:T(128)} %lengths_ref.1) | copy-start | bytes 388
  12.6 6.7 %collective-permute-start.7 = (bf16[2,2,4,1024]{3,2,1,0:T(4,128)(2,1)S(1)}, bf16[2,2,4,1024]{3,2,1,0:T(4,128)(2,1)S(1)}, u32[]{:S(2)}, u32[]{:S(2)}) collective-permute-start(bf16[2,2,4,1024]{3,2,1,0:T(4,128)(2,1)S(1)} %merge.1.refs_0_.refs_8_), channel_id=1, source_target_pairs={{0,12},{4,8},{8,4},{12,0},{1,13},{5,9},{9,5},{13,1},{2,14},{6,10},... | collective-permute-start | bytes 98312 | tf_op jit(solution)/shard_map/ppermute | solution.py:35
  16.2 5.3 %collective-permute-start.6 = (bf16[2,2,4,1024]{3,2,1,0:T(4,128)(2,1)S(1)}, bf16[2,2,4,1024]{3,2,1,0:T(4,128)(2,1)S(1)}, u32[]{:S(2)}, u32[]{:S(2)}) collective-permute-start(bf16[2,2,4,1024]{3,2,1,0:T(4,128)(2,1)S(1)} %merge.1.refs_0_.refs_8_), channel_id=1, source_target_pairs={{0,8},{4,12},{8,0},{12,4},{1,9},{5,13},{9,1},{13,5},{2,10},{6,14},... | collective-permute-start | bytes 98312 | tf_op jit(solution)/shard_map/ppermute | solution.py:35
  16.2 5.3 %collective-permute-start.5 = (bf16[2,2,4,1024]{3,2,1,0:T(4,128)(2,1)S(1)}, bf16[2,2,4,1024]{3,2,1,0:T(4,128)(2,1)S(1)}, u32[]{:S(2)}, u32[]{:S(2)}) collective-permute-start(bf16[2,2,4,1024]{3,2,1,0:T(4,128)(2,1)S(1)} %merge.1.refs_0_.refs_8_), channel_id=1, source_target_pairs={{0,4},{4,0},{8,12},{12,8},{1,5},{5,1},{9,13},{13,9},{2,6},{6,2},{1... | collective-permute-start | bytes 98312 | tf_op jit(solution)/shard_map/ppermute | solution.py:35
  19.3 9.4 %collective-permute-start.11 = (bf16[4,256,512]{2,1,0:T(8,128)(2,1)S(1)}, bf16[4,256,512]{2,1,0:T(8,128)(2,1)S(1)}, u32[]{:S(2)}, u32[]{:S(2)}) collective-permute-start(bf16[4,256,512]{2,1,0:T(8,128)(2,1)S(1)} %get-tuple-element.24.refs_5_), channel_id=1, source_target_pairs={{0,1},{1,0},{2,3},{3,2},{4,5},{5,4},{6,7},{7,6},{8,9},{9,8},{10,11... | collective-permute-start | bytes 3145736 | tf_op jit(solution)/shard_map/ppermute | solution.py:35
  25.3 9.4 %collective-permute-start.8 = (bf16[272,128]{1,0:T(8,128)(2,1)S(1)}, bf16[272,128]{1,0:T(8,128)(2,1)S(1)}, u32[]{:S(2)}, u32[]{:S(2)}) collective-permute-start(bf16[272,128]{1,0:T(8,128)(2,1)S(1)} %get-tuple-element.27), channel_id=1, source_target_pairs={{0,4},{4,0},{8,12},{12,8},{1,5},{5,1},{9,13},{13,9},{2,6},{6,2},{1... | collective-permute-start | bytes 208904 | tf_op jit(solution)/shard_map/ppermute | solution.py:35
  26.1 8.6 %collective-permute-start.9 = (bf16[272,128]{1,0:T(8,128)(2,1)S(1)}, bf16[272,128]{1,0:T(8,128)(2,1)S(1)}, u32[]{:S(2)}, u32[]{:S(2)}) collective-permute-start(bf16[272,128]{1,0:T(8,128)(2,1)S(1)} %get-tuple-element.28), channel_id=1, source_target_pairs={{0,8},{4,12},{8,0},{12,4},{1,9},{5,13},{9,1},{13,5},{2,10},{6,14},... | collective-permute-start | bytes 208904 | tf_op jit(solution)/shard_map/ppermute | solution.py:35
  28.8 6.2 %collective-permute-start.10 = (bf16[272,128]{1,0:T(8,128)(2,1)S(1)}, bf16[272,128]{1,0:T(8,128)(2,1)S(1)}, u32[]{:S(2)}, u32[]{:S(2)}) collective-permute-start(bf16[272,128]{1,0:T(8,128)(2,1)S(1)} %get-tuple-element.29), channel_id=1, source_target_pairs={{0,12},{4,8},{8,4},{12,0},{1,13},{5,9},{9,5},{13,1},{2,14},{6,10},... | collective-permute-start | bytes 208904 | tf_op jit(solution)/shard_map/ppermute | solution.py:35
  35.4 15.4 %collective-permute-start.16 = (bf16[1,256,512]{2,1,0:T(8,128)(2,1)S(1)}, bf16[1,256,512]{2,1,0:T(8,128)(2,1)S(1)}, u32[]{:S(2)}, u32[]{:S(2)}) collective-permute-start(bf16[1,256,512]{2,1,0:T(8,128)(2,1)S(1)} %gate.1), channel_id=1, source_target_pairs={{0,3},{1,2},{2,1},{3,0},{4,7},{5,6},{6,5},{7,4},{8,11},{9,10},{10,... | collective-permute-start | bytes 786440 | tf_op jit(solution)/shard_map/ppermute | solution.py:35
  35.5 8.9 %collective-permute-start.14 = (bf16[8,4096]{1,0:T(8,128)(2,1)S(1)}, bf16[8,4096]{1,0:T(8,128)(2,1)S(1)}, u32[]{:S(2)}, u32[]{:S(2)}) collective-permute-start(bf16[8,4096]{1,0:T(8,128)(2,1)S(1)} %join.1.refs_0_.refs_1_), channel_id=1, source_target_pairs={{0,12},{4,8},{8,4},{12,0},{1,13},{5,9},{9,5},{13,1},{2,14},{6,10},... | collective-permute-start | bytes 196616 | tf_op jit(solution)/shard_map/ppermute | solution.py:35
  38.2 7.2 %collective-permute-start.13 = (bf16[8,4096]{1,0:T(8,128)(2,1)S(1)}, bf16[8,4096]{1,0:T(8,128)(2,1)S(1)}, u32[]{:S(2)}, u32[]{:S(2)}) collective-permute-start(bf16[8,4096]{1,0:T(8,128)(2,1)S(1)} %join.1.refs_0_.refs_1_), channel_id=1, source_target_pairs={{0,8},{4,12},{8,0},{12,4},{1,9},{5,13},{9,1},{13,5},{2,10},{6,14},... | collective-permute-start | bytes 196616 | tf_op jit(solution)/shard_map/ppermute | solution.py:35
  38.4 7.0 %collective-permute-start.12 = (bf16[8,4096]{1,0:T(8,128)(2,1)S(1)}, bf16[8,4096]{1,0:T(8,128)(2,1)S(1)}, u32[]{:S(2)}, u32[]{:S(2)}) collective-permute-start(bf16[8,4096]{1,0:T(8,128)(2,1)S(1)} %join.1.refs_0_.refs_1_), channel_id=1, source_target_pairs={{0,4},{4,0},{8,12},{12,8},{1,5},{5,1},{9,13},{13,9},{2,6},{6,2},{1... | collective-permute-start | bytes 196616 | tf_op jit(solution)/shard_map/ppermute | solution.py:35

commit v24 on v21

--- a/solution.py
+++ b/solution.py
@@ -13,7 +13,7 @@
 CAP = 2
 HIDDEN = -1e30
 STAT_ROWS = 16
-EARLY_ROWS = 4
+EARLY_ROWS = 6
 
 ANY = pl.BlockSpec(memory_space=pl.ANY)
 HBM = pl.BlockSpec(memory_space=pltpu.HBM)

time: 51.7 us -> 51.8 us (level)
  no operation moved by 1% of the time
where the time goes in v24:
time: 51.8 us; the launch traced here: 51.4 us
  Pallas kernels  24.7 us (48%)
  starting transfers between devices  20.3 us (39%)
  waiting for transfers between devices  5.73 us (11%)
  between operations  0.78 us (2%)
    ppermute x17, starting transfers between devices, swap(): return lax.ppermute(value, axis, [(i, i ^ offset) for i in range(count)])  20.3 us
    pallas_call x2, Pallas kernels, fetch(): pl.pallas_call(functools.partial(fetch_kernel, number * size), out_shape=...  6.95 us
    ppermute x17, waiting for transfers between devices, swap(): return lax.ppermute(value, axis, [(i, i ^ offset) for i in range(count)])  5.73 us
    pallas_call x4, Pallas kernels, place(): pl.pallas_call(functools.partial(place_kernel, pieces), out_shape=jax.Sha...  3.99 us
    pallas_call x1, Pallas kernels, attend(): pl.pallas_call(functools.partial(attend_kernel, pieces, section_count, tp...  3.77 us
    pallas_call x1, Pallas kernels, project(): pl.pallas_call(functools.partial(project_kernel, count, min(256, width),...  3.64 us
    pallas_call x1, Pallas kernels, pack(): pl.pallas_call(functools.partial(pack_kernel, pieces, section_count), out...  2.22 us
    pallas_call x1, Pallas kernels, first_pack(): pl.pallas_call(functools.partial(first_pack_kernel, pieces, section_count...  2.2 us
  transfers between devices with their start and end apart: 17, of which 6 were waited for; matrix products, arithmetic and copies ran while one was open for 0% of the time, Pallas kernels for 44%

profile of v24, /device:TPU:0, one launch (start us, length us, event | category | flops | bytes accessed | tf_op | source)
XLA Modules:
  0.0 51.4 jit_solution(15950410959465882843)
XLA Ops:
  0.6 1.5 %pack_head.1 = (bf16[1,256,512]{2,1,0:T(8,128)(2,1)S(1)}, bf16[2,4,1024]{2,1,0:T(4,128)(2,1)S(1)}, bf16[2,4,1024]{2,1,0:T(4,128)(2,1)S(1)}) custom-call(s32[32]{0:T(128)} %bitcast.2, bf16[8,2,256,512]{3,2,1,0:T(8,128)(2,1)} %cache_ref.5, bf16[1,8,4,4096]{3,2,1,0:T(4,128)(2,1)} %query_ref.3), custom_call_target="tpu_custom_call" | custom-call | bytes 2097152 | tf_op jit(solution)/shard_map/pack_head/pallas_call | solution.py:149
  2.1 3.0 %collective-permute-start.3 = (bf16[1,256,512]{2,1,0:T(8,128)(2,1)S(1)}, bf16[1,256,512]{2,1,0:T(8,128)(2,1)S(1)}, u32[]{:S(2)}, u32[]{:S(2)}) collective-permute-start(bf16[1,256,512]{2,1,0:T(8,128)(2,1)S(1)} %get-tuple-element.16.refs_0_), channel_id=1, source_target_pairs={{0,2},{1,3},{2,0},{3,1},{4,6},{5,7},{6,4},{7,5},{8,10},{9,11},{10,... | collective-permute-start | bytes 786440 | tf_op jit(solution)/shard_map/ppermute | solution.py:36
  5.1 0.1 collective-permute-start.1
  5.2 0.8 %collective-permute-start.2 = (bf16[2,4,1024]{2,1,0:T(4,128)(2,1)S(1)}, bf16[2,4,1024]{2,1,0:T(4,128)(2,1)S(1)}, u32[]{:S(2)}, u32[]{:S(2)}) collective-permute-start(bf16[2,4,1024]{2,1,0:T(4,128)(2,1)S(1)} %get-tuple-element.21), channel_id=1, source_target_pairs={{0,3},{1,2},{2,1},{3,0},{4,7},{5,6},{6,5},{7,4},{8,11},{9,10},{10,... | collective-permute-start | bytes 49160 | tf_op jit(solution)/shard_map/ppermute | solution.py:36
  6.0 2.2 %first_pack.1 = (bf16[3,256,512]{2,1,0:T(8,128)(2,1)S(1)}, bf16[3,256,512]{2,1,0:T(8,128)(2,1)S(1)}, bf16[1,256,512]{2,1,0:T(8,128)(2,1)S(1)}, bf16[2,4,4096]{2,1,0:T(4,128)(2,1)S(1)}, bf16[2,4,4096]{2,1,0:T(4,128)(2,1)S(1)}) custom-call(s32[32]{0:T(128)S(1)} %bitcast.3, bf16[8,2,256,512]{3,2,1,0:T(8,128)(2,1)} %cache_ref.5, ...), custom_call_target="tpu_custom_call" | custom-call | bytes 3932160 | tf_op jit(solution)/shard_map/first_pack/pallas_call | solution.py:207
  8.3 1.3 %collective-permute-start.4 = (bf16[2,4,4096]{2,1,0:T(4,128)(2,1)S(1)}, bf16[2,4,4096]{2,1,0:T(4,128)(2,1)S(1)}, u32[]{:S(2)}, u32[]{:S(2)}) collective-permute-start(bf16[2,4,4096]{2,1,0:T(4,128)(2,1)S(1)} %get-tuple-element.22), channel_id=1, source_target_pairs={{0,1},{1,0},{2,3},{3,2},{4,5},{5,4},{6,7},{7,6},{8,9},{9,8},{10,11... | collective-permute-start | bytes 196616 | tf_op jit(solution)/shard_map/ppermute | solution.py:36
  9.6 0.1 collective-permute-start
  9.6 2.6 %collective-permute-done.1.refs_0_ = bf16[2,4,1024]{2,1,0:T(4,128)(2,1)S(1)} collective-permute-done((bf16[2,4,1024]{2,1,0:T(4,128)(2,1)S(1)}, bf16[2,4,1024]{2,1,0:T(4,128)(2,1)S(1)}, u32[]{:S(2)}, u32[]{:S(2)}) %collective-permute-start.1) | collective-permute-done | bytes 16416 | tf_op jit(solution)/shard_map/ppermute | solution.py:36
  12.2 0.3 collective-permute-done.2.refs_1_
  12.6 3.6 %collective-permute-start.7 = (bf16[2,2,4,1024]{3,2,1,0:T(4,128)(2,1)S(1)}, bf16[2,2,4,1024]{3,2,1,0:T(4,128)(2,1)S(1)}, u32[]{:S(2)}, u32[]{:S(2)}) collective-permute-start(bf16[2,2,4,1024]{3,2,1,0:T(4,128)(2,1)S(1)} %merge.1.refs_0_.refs_8_), channel_id=1, source_target_pairs={{0,12},{4,8},{8,4},{12,0},{1,13},{5,9},{9,5},{13,1},{2,14},{6,10},... | collective-permute-start | bytes 98312 | tf_op jit(solution)/shard_map/ppermute | solution.py:36
  16.1 0.9 %collective-permute-start.5 = (bf16[2,2,4,1024]{3,2,1,0:T(4,128)(2,1)S(1)}, bf16[2,2,4,1024]{3,2,1,0:T(4,128)(2,1)S(1)}, u32[]{:S(2)}, u32[]{:S(2)}) collective-permute-start(bf16[2,2,4,1024]{3,2,1,0:T(4,128)(2,1)S(1)} %merge.1.refs_0_.refs_8_), channel_id=1, source_target_pairs={{0,4},{4,0},{8,12},{12,8},{1,5},{5,1},{9,13},{13,9},{2,6},{6,2},{1... | collective-permute-start | bytes 98312 | tf_op jit(solution)/shard_map/ppermute | solution.py:36
  17.0 2.2 %pack.1 = (bf16[4,256,512]{2,1,0:T(8,128)(2,1)S(1)}, bf16[4,256,512]{2,1,0:T(8,128)(2,1)S(1)}) custom-call(s32[32]{0:T(128)S(1)} %bitcast.4, bf16[8,2,256,512]{3,2,1,0:T(8,128)(2,1)} %cache_ref.5, bf16[2,2,4,1024]{3,2,1,0:T(4,128)(2,1)S(1)} %merge.1.refs_0_.refs_8_, bf16[2,4,4096]{2,1,0:T(4,128)(2,1)S(1)} %collective-permute-done.4.refs_1_.refs_7_), custom_call_target="tpu_custom_call" | custom-call | flops 10000000000 | bytes 4194304 | tf_op jit(solution)/shard_map/pack/pallas_call | solution.py:225
  19.3 1.5 %collective-permute-start.11 = (bf16[4,256,512]{2,1,0:T(8,128)(2,1)S(1)}, bf16[4,256,512]{2,1,0:T(8,128)(2,1)S(1)}, u32[]{:S(2)}, u32[]{:S(2)}) collective-permute-start(bf16[4,256,512]{2,1,0:T(8,128)(2,1)S(1)} %get-tuple-element.24.refs_5_), channel_id=1, source_target_pairs={{0,1},{1,0},{2,3},{3,2},{4,5},{5,4},{6,7},{7,6},{8,9},{9,8},{10,11... | collective-permute-start | bytes 3145736 | tf_op jit(solution)/shard_map/ppermute | solution.py:36
  20.8 0.6 %collective-permute-done.6.refs_10_ = bf16[2,2,4,1024]{3,2,1,0:T(4,128)(2,1)S(1)} collective-permute-done((bf16[2,2,4,1024]{3,2,1,0:T(4,128)(2,1)S(1)}, bf16[2,2,4,1024]{3,2,1,0:T(4,128)(2,1)S(1)}, u32[]{:S(2)}, u32[]{:S(2)}) %collective-permute-start.6) | collective-permute-done | bytes 32800 | tf_op jit(solution)/shard_map/ppermute | solution.py:36
  21.4 3.8 %attend.1 = (bf16[272,128]{1,0:T(8,128)(2,1)S(1)}, bf16[272,128]{1,0:T(8,128)(2,1)S(1)}, bf16[272,128]{1,0:T(8,128)(2,1)S(1)}, bf16[272,128]{1,0:T(8,128)(2,1)S(1)}) custom-call(s32[32]{0:T(128)S(1)} %bitcast.5, s32[32]{0:T(128)S(1)} %copy-done.1, bf16[1,256,512]{2,1,0:T(8,128)(2,1)S(1)} %get-tuple-element.16.refs_0_, ...), custom_call_target="tpu_custom_call" | custom-call | flops 20000000000 | bytes 4194304 | tf_op jit(solution)/shard_map/attend/pallas_call | solution.py:373
  25.2 0.9 %collective-permute-start.8 = (bf16[272,128]{1,0:T(8,128)(2,1)S(1)}, bf16[272,128]{1,0:T(8,128)(2,1)S(1)}, u32[]{:S(2)}, u32[]{:S(2)}) collective-permute-start(bf16[272,128]{1,0:T(8,128)(2,1)S(1)} %get-tuple-element.27), channel_id=1, source_target_pairs={{0,4},{4,0},{8,12},{12,8},{1,5},{5,1},{9,13},{13,9},{2,6},{6,2},{1... | collective-permute-start | bytes 208904 | tf_op jit(solution)/shard_map/ppermute | solution.py:36
  26.0 2.6 %collective-permute-start.9 = (bf16[272,128]{1,0:T(8,128)(2,1)S(1)}, bf16[272,128]{1,0:T(8,128)(2,1)S(1)}, u32[]{:S(2)}, u32[]{:S(2)}) collective-permute-start(bf16[272,128]{1,0:T(8,128)(2,1)S(1)} %get-tuple-element.28), channel_id=1, source_target_pairs={{0,8},{4,12},{8,0},{12,4},{1,9},{5,13},{9,1},{13,5},{2,10},{6,14},... | collective-permute-start | bytes 208904 | tf_op jit(solution)/shard_map/ppermute | solution.py:36
  28.7 1.0 %collective-permute-start.10 = (bf16[272,128]{1,0:T(8,128)(2,1)S(1)}, bf16[272,128]{1,0:T(8,128)(2,1)S(1)}, u32[]{:S(2)}, u32[]{:S(2)}) collective-permute-start(bf16[272,128]{1,0:T(8,128)(2,1)S(1)} %get-tuple-element.29), channel_id=1, source_target_pairs={{0,12},{4,8},{8,4},{12,0},{1,13},{5,9},{9,5},{13,1},{2,14},{6,10},... | collective-permute-start | bytes 208904 | tf_op jit(solution)/shard_map/ppermute | solution.py:36
  29.7 1.5 %place.4.refs_4_.refs_0_ = bf16[1,16,256,512]{3,2,1,0:T(8,128)(2,1)} custom-call(bf16[4,256,512]{2,1,0:T(8,128)(2,1)S(1)} %get-tuple-element.23.refs_4_.refs_0_, bf16[4,256,512]{2,1,0:T(8,128)(2,1)S(1)} %collective-permute-done.11.refs_1_, bf16[1,256,512]{2,1,0:T(8,128)(2,1)S(1)} %collective-permute-done.3.refs_2_), custom_call_target="tpu_custom_call" | custom-call | bytes 4718592 | tf_op jit(solution)/shard_map/place/pallas_call | solution.py:273
  31.1 3.5 %fetch.2.refs_5_ = bf16[2048,2048]{1,0:T(8,128)(2,1)S(1)} custom-call(bf16[4096,2048]{1,0:T(8,128)(2,1)} %weight_ref.3, bf16[272,128]{1,0:T(8,128)(2,1)S(1)} %get-tuple-element.26.refs_0_, bf16[4,256,512]{2,1,0:T(8,128)(2,1)S(1)} %collective-permute-done.11.refs_1_), custom_call_target="tpu_custom_call" | custom-call | bytes 16777216 | tf_op jit(solution)/shard_map/fetch/pallas_call | solution.py:466
  34.6 0.3 collective-permute-done.10.refs_3_
  34.9 0.4 join.1.refs_0_.refs_1_
  35.4 2.7 %collective-permute-start.14 = (bf16[8,4096]{1,0:T(8,128)(2,1)S(1)}, bf16[8,4096]{1,0:T(8,128)(2,1)S(1)}, u32[]{:S(2)}, u32[]{:S(2)}) collective-permute-start(bf16[8,4096]{1,0:T(8,128)(2,1)S(1)} %join.1.refs_0_.refs_1_), channel_id=1, source_target_pairs={{0,12},{4,8},{8,4},{12,0},{1,13},{5,9},{9,5},{13,1},{2,14},{6,10},... | collective-permute-start | bytes 196616 | tf_op jit(solution)/shard_map/ppermute | solution.py:36
  38.1 0.2 collective-permute-start.13
  38.3 1.5 %collective-permute-start.12 = (bf16[8,4096]{1,0:T(8,128)(2,1)S(1)}, bf16[8,4096]{1,0:T(8,128)(2,1)S(1)}, u32[]{:S(2)}, u32[]{:S(2)}) collective-permute-start(bf16[8,4096]{1,0:T(8,128)(2,1)S(1)} %join.1.refs_0_.refs_1_), channel_id=1, source_target_pairs={{0,4},{4,0},{8,12},{12,8},{1,5},{5,1},{9,13},{13,9},{2,6},{6,2},{1... | collective-permute-start | bytes 196616 | tf_op jit(solution)/shard_map/ppermute | solution.py:36
  39.9 3.5 %fetch.3.refs_6_ = bf16[2048,2048]{1,0:T(8,128)(2,1)S(1)} custom-call(bf16[4096,2048]{1,0:T(8,128)(2,1)} %weight_ref.3, bf16[8,4096]{1,0:T(8,128)(2,1)S(1)} %join.1.refs_0_.refs_1_), custom_call_target="tpu_custom_call" | custom-call | bytes 16777216 | tf_op jit(solution)/shard_map/fetch/pallas_call | solution.py:466
  43.3 0.9 %place.5.refs_0_ = bf16[1,16,256,512]{3,2,1,0:T(8,128)(2,1)} custom-call(bf16[1,16,256,512]{3,2,1,0:T(8,128)(2,1)} %place.4.refs_4_.refs_0_, bf16[8,4096]{1,0:T(8,128)(2,1)S(1)} %join.1.refs_0_.refs_1_, bf16[3,256,512]{2,1,0:T(8,128)(2,1)S(1)} %collective-permute-done.refs_6_.refs_0_.refs_2_), custom_call_target="tpu_custom_call", output_to_operand_aliasing={{}: (0, {})} | custom-call | bytes 1572864 | tf_op jit(solution)/shard_map/place/pallas_call | solution.py:273
  44.3 1.0 %collective-permute-done.13.refs_3_ = bf16[8,4096]{1,0:T(8,128)(2,1)S(1)} collective-permute-done((bf16[8,4096]{1,0:T(8,128)(2,1)S(1)}, bf16[8,4096]{1,0:T(8,128)(2,1)S(1)}, u32[]{:S(2)}, u32[]{:S(2)}) %collective-permute-start.13) | collective-permute-done | bytes 65568 | tf_op jit(solution)/shard_map/ppermute | solution.py:36
  45.3 3.6 %project.1.refs_1_ = bf16[8,4,2048]{2,1,0:T(4,128)(2,1)} custom-call(bf16[3,256,512]{2,1,0:T(8,128)(2,1)S(1)} %collective-permute-done.refs_6_.refs_0_.refs_2_, bf16[8,4096]{1,0:T(8,128)(2,1)S(1)} %join.1.refs_0_.refs_1_, bf16[8,4096]{1,0:T(8,128)(2,1)S(1)} %collective-permute-done.12.refs_2_, bf16[8,4096]{1,0:T(8,128)(2,1)S(1)} %collective-permute-done.13.refs_3_, ...), custom_call_target="tpu_custom_call" | custom-call | flops 536870912 | bytes 16777216 | tf_op jit(solution)/shard_map/project/pallas_call | solution.py:510
  48.9 0.9 %place.6.refs_0_ = bf16[1,16,256,512]{3,2,1,0:T(8,128)(2,1)} custom-call(bf16[1,16,256,512]{3,2,1,0:T(8,128)(2,1)} %place.5.refs_0_, bf16[8,4,2048]{2,1,0:T(4,128)(2,1)} %project.1.refs_1_, bf16[3,256,512]{2,1,0:T(8,128)(2,1)S(1)} %collective-permute-done.15.refs_2_), custom_call_target="tpu_custom_call", output_to_operand_aliasing={{}: (0, {})} | custom-call | bytes 1572864 | tf_op jit(solution)/shard_map/place/pallas_call | solution.py:273
  49.8 0.9 %collective-permute-done.16.refs_2_ = bf16[1,256,512]{2,1,0:T(8,128)(2,1)S(1)} collective-permute-done((bf16[1,256,512]{2,1,0:T(8,128)(2,1)S(1)}, bf16[1,256,512]{2,1,0:T(8,128)(2,1)S(1)}, u32[]{:S(2)}, u32[]{:S(2)}) %collective-permute-start.16) | collective-permute-done | bytes 262176 | tf_op jit(solution)/shard_map/ppermute | solution.py:36
  50.7 0.7 %place.7 = bf16[1,16,256,512]{3,2,1,0:T(8,128)(2,1)} custom-call(bf16[1,16,256,512]{3,2,1,0:T(8,128)(2,1)} %place.6.refs_0_, bf16[8,4,2048]{2,1,0:T(4,128)(2,1)} %project.1.refs_1_, bf16[1,256,512]{2,1,0:T(8,128)(2,1)S(1)} %collective-permute-done.16.refs_2_), custom_call_target="tpu_custom_call", output_to_operand_aliasing={{}: (0, {})} | custom-call | bytes 524288 | tf_op jit(solution)/shard_map/place/pallas_call | solution.py:273
  (20 shorter events, 0.1 us)
Async XLA Ops:
  0.6 5.4 %copy-start = (s32[32,1]{0,1:T(1,128)S(1)}, s32[32,1]{0,1:T(1,128)}, u32[]{:S(2)}) copy-start(s32[32,1]{0,1:T(1,128)} %param.7) | copy-start | bytes 388
  2.1 10.4 %collective-permute-start.3 = (bf16[1,256,512]{2,1,0:T(8,128)(2,1)S(1)}, bf16[1,256,512]{2,1,0:T(8,128)(2,1)S(1)}, u32[]{:S(2)}, u32[]{:S(2)}) collective-permute-start(bf16[1,256,512]{2,1,0:T(8,128)(2,1)S(1)} %get-tuple-element.16.refs_0_), channel_id=1, source_target_pairs={{0,2},{1,3},{2,0},{3,1},{4,6},{5,7},{6,4},{7,5},{8,10},{9,11},{10,... | collective-permute-start | bytes 786440 | tf_op jit(solution)/shard_map/ppermute | solution.py:36
  5.1 7.1 %collective-permute-start.1 = (bf16[2,4,1024]{2,1,0:T(4,128)(2,1)S(1)}, bf16[2,4,1024]{2,1,0:T(4,128)(2,1)S(1)}, u32[]{:S(2)}, u32[]{:S(2)}) collective-permute-start(bf16[2,4,1024]{2,1,0:T(4,128)(2,1)S(1)} %get-tuple-element.20), channel_id=1, source_target_pairs={{0,2},{1,3},{2,0},{3,1},{4,6},{5,7},{6,4},{7,5},{8,10},{9,11},{10,... | collective-permute-start | bytes 49160 | tf_op jit(solution)/shard_map/ppermute | solution.py:36
  5.2 7.3 %collective-permute-start.2 = (bf16[2,4,1024]{2,1,0:T(4,128)(2,1)S(1)}, bf16[2,4,1024]{2,1,0:T(4,128)(2,1)S(1)}, u32[]{:S(2)}, u32[]{:S(2)}) collective-permute-start(bf16[2,4,1024]{2,1,0:T(4,128)(2,1)S(1)} %get-tuple-element.21), channel_id=1, source_target_pairs={{0,3},{1,2},{2,1},{3,0},{4,7},{5,6},{6,5},{7,4},{8,11},{9,10},{10,... | collective-permute-start | bytes 49160 | tf_op jit(solution)/shard_map/ppermute | solution.py:36
  8.3 7.9 %collective-permute-start.4 = (bf16[2,4,4096]{2,1,0:T(4,128)(2,1)S(1)}, bf16[2,4,4096]{2,1,0:T(4,128)(2,1)S(1)}, u32[]{:S(2)}, u32[]{:S(2)}) collective-permute-start(bf16[2,4,4096]{2,1,0:T(4,128)(2,1)S(1)} %get-tuple-element.22), channel_id=1, source_target_pairs={{0,1},{1,0},{2,3},{3,2},{4,5},{5,4},{6,7},{7,6},{8,9},{9,8},{10,11... | collective-permute-start | bytes 196616 | tf_op jit(solution)/shard_map/ppermute | solution.py:36
  9.6 25.4 %collective-permute-start = (bf16[3,256,512]{2,1,0:T(8,128)(2,1)S(1)}, bf16[3,256,512]{2,1,0:T(8,128)(2,1)S(1)}, u32[]{:S(2)}, u32[]{:S(2)}) collective-permute-start(bf16[3,256,512]{2,1,0:T(8,128)(2,1)S(1)} %get-tuple-element.17.refs_1_), channel_id=1, source_target_pairs={{0,2},{1,3},{2,0},{3,1},{4,6},{5,7},{6,4},{7,5},{8,10},{9,11},{10,... | collective-permute-start | bytes 2359304 | tf_op jit(solution)/shard_map/ppermute | solution.py:36
  12.2 36.7 %collective-permute-start.15 = (bf16[3,256,512]{2,1,0:T(8,128)(2,1)S(1)}, bf16[3,256,512]{2,1,0:T(8,128)(2,1)S(1)}, u32[]{:S(2)}, u32[]{:S(2)}) collective-permute-start(bf16[3,256,512]{2,1,0:T(8,128)(2,1)S(1)} %get-tuple-element.18.refs_2_), channel_id=1, source_target_pairs={{0,3},{1,2},{2,1},{3,0},{4,7},{5,6},{6,5},{7,4},{8,11},{9,10},{10,... | collective-permute-start | bytes 2359304 | tf_op jit(solution)/shard_map/ppermute | solution.py:36
  12.6 8.8 %copy-start.1 = (s32[32]{0:T(128)S(1)}, s32[32]{0:T(128)}, u32[]{:S(2)}) copy-start(s32[32]{0:T(128)} %lengths_ref.1) | copy-start | bytes 388
  12.6 6.7 %collective-permute-start.7 = (bf16[2,2,4,1024]{3,2,1,0:T(4,128)(2,1)S(1)}, bf16[2,2,4,1024]{3,2,1,0:T(4,128)(2,1)S(1)}, u32[]{:S(2)}, u32[]{:S(2)}) collective-permute-start(bf16[2,2,4,1024]{3,2,1,0:T(4,128)(2,1)S(1)} %merge.1.refs_0_.refs_8_), channel_id=1, source_target_pairs={{0,12},{4,8},{8,4},{12,0},{1,13},{5,9},{9,5},{13,1},{2,14},{6,10},... | collective-permute-start | bytes 98312 | tf_op jit(solution)/shard_map/ppermute | solution.py:36
  16.1 5.3 %collective-permute-start.6 = (bf16[2,2,4,1024]{3,2,1,0:T(4,128)(2,1)S(1)}, bf16[2,2,4,1024]{3,2,1,0:T(4,128)(2,1)S(1)}, u32[]{:S(2)}, u32[]{:S(2)}) collective-permute-start(bf16[2,2,4,1024]{3,2,1,0:T(4,128)(2,1)S(1)} %merge.1.refs_0_.refs_8_), channel_id=1, source_target_pairs={{0,8},{4,12},{8,0},{12,4},{1,9},{5,13},{9,1},{13,5},{2,10},{6,14},... | collective-permute-start | bytes 98312 | tf_op jit(solution)/shard_map/ppermute | solution.py:36
  16.1 5.3 %collective-permute-start.5 = (bf16[2,2,4,1024]{3,2,1,0:T(4,128)(2,1)S(1)}, bf16[2,2,4,1024]{3,2,1,0:T(4,128)(2,1)S(1)}, u32[]{:S(2)}, u32[]{:S(2)}) collective-permute-start(bf16[2,2,4,1024]{3,2,1,0:T(4,128)(2,1)S(1)} %merge.1.refs_0_.refs_8_), channel_id=1, source_target_pairs={{0,4},{4,0},{8,12},{12,8},{1,5},{5,1},{9,13},{13,9},{2,6},{6,2},{1... | collective-permute-start | bytes 98312 | tf_op jit(solution)/shard_map/ppermute | solution.py:36
  19.3 9.4 %collective-permute-start.11 = (bf16[4,256,512]{2,1,0:T(8,128)(2,1)S(1)}, bf16[4,256,512]{2,1,0:T(8,128)(2,1)S(1)}, u32[]{:S(2)}, u32[]{:S(2)}) collective-permute-start(bf16[4,256,512]{2,1,0:T(8,128)(2,1)S(1)} %get-tuple-element.24.refs_5_), channel_id=1, source_target_pairs={{0,1},{1,0},{2,3},{3,2},{4,5},{5,4},{6,7},{7,6},{8,9},{9,8},{10,11... | collective-permute-start | bytes 3145736 | tf_op jit(solution)/shard_map/ppermute | solution.py:36
  25.2 9.4 %collective-permute-start.8 = (bf16[272,128]{1,0:T(8,128)(2,1)S(1)}, bf16[272,128]{1,0:T(8,128)(2,1)S(1)}, u32[]{:S(2)}, u32[]{:S(2)}) collective-permute-start(bf16[272,128]{1,0:T(8,128)(2,1)S(1)} %get-tuple-element.27), channel_id=1, source_target_pairs={{0,4},{4,0},{8,12},{12,8},{1,5},{5,1},{9,13},{13,9},{2,6},{6,2},{1... | collective-permute-start | bytes 208904 | tf_op jit(solution)/shard_map/ppermute | solution.py:36
  26.0 8.6 %collective-permute-start.9 = (bf16[272,128]{1,0:T(8,128)(2,1)S(1)}, bf16[272,128]{1,0:T(8,128)(2,1)S(1)}, u32[]{:S(2)}, u32[]{:S(2)}) collective-permute-start(bf16[272,128]{1,0:T(8,128)(2,1)S(1)} %get-tuple-element.28), channel_id=1, source_target_pairs={{0,8},{4,12},{8,0},{12,4},{1,9},{5,13},{9,1},{13,5},{2,10},{6,14},... | collective-permute-start | bytes 208904 | tf_op jit(solution)/shard_map/ppermute | solution.py:36
  28.7 6.2 %collective-permute-start.10 = (bf16[272,128]{1,0:T(8,128)(2,1)S(1)}, bf16[272,128]{1,0:T(8,128)(2,1)S(1)}, u32[]{:S(2)}, u32[]{:S(2)}) collective-permute-start(bf16[272,128]{1,0:T(8,128)(2,1)S(1)} %get-tuple-element.29), channel_id=1, source_target_pairs={{0,12},{4,8},{8,4},{12,0},{1,13},{5,9},{9,5},{13,1},{2,14},{6,10},... | collective-permute-start | bytes 208904 | tf_op jit(solution)/shard_map/ppermute | solution.py:36
  35.3 15.4 %collective-permute-start.16 = (bf16[1,256,512]{2,1,0:T(8,128)(2,1)S(1)}, bf16[1,256,512]{2,1,0:T(8,128)(2,1)S(1)}, u32[]{:S(2)}, u32[]{:S(2)}) collective-permute-start(bf16[1,256,512]{2,1,0:T(8,128)(2,1)S(1)} %gate.1), channel_id=1, source_target_pairs={{0,3},{1,2},{2,1},{3,0},{4,7},{5,6},{6,5},{7,4},{8,11},{9,10},{10,... | collective-permute-start | bytes 786440 | tf_op jit(solution)/shard_map/ppermute | solution.py:36
  35.4 8.9 %collective-permute-start.14 = (bf16[8,4096]{1,0:T(8,128)(2,1)S(1)}, bf16[8,4096]{1,0:T(8,128)(2,1)S(1)}, u32[]{:S(2)}, u32[]{:S(2)}) collective-permute-start(bf16[8,4096]{1,0:T(8,128)(2,1)S(1)} %join.1.refs_0_.refs_1_), channel_id=1, source_target_pairs={{0,12},{4,8},{8,4},{12,0},{1,13},{5,9},{9,5},{13,1},{2,14},{6,10},... | collective-permute-start | bytes 196616 | tf_op jit(solution)/shard_map/ppermute | solution.py:36
  38.1 7.2 %collective-permute-start.13 = (bf16[8,4096]{1,0:T(8,128)(2,1)S(1)}, bf16[8,4096]{1,0:T(8,128)(2,1)S(1)}, u32[]{:S(2)}, u32[]{:S(2)}) collective-permute-start(bf16[8,4096]{1,0:T(8,128)(2,1)S(1)} %join.1.refs_0_.refs_1_), channel_id=1, source_target_pairs={{0,8},{4,12},{8,0},{12,4},{1,9},{5,13},{9,1},{13,5},{2,10},{6,14},... | collective-permute-start | bytes 196616 | tf_op jit(solution)/shard_map/ppermute | solution.py:36
  38.3 7.0 %collective-permute-start.12 = (bf16[8,4096]{1,0:T(8,128)(2,1)S(1)}, bf16[8,4096]{1,0:T(8,128)(2,1)S(1)}, u32[]{:S(2)}, u32[]{:S(2)}) collective-permute-start(bf16[8,4096]{1,0:T(8,128)(2,1)S(1)} %join.1.refs_0_.refs_1_), channel_id=1, source_target_pairs={{0,4},{4,0},{8,12},{12,8},{1,5},{5,1},{9,13},{13,9},{2,6},{6,2},{1... | collective-permute-start | bytes 196616 | tf_op jit(solution)/shard_map/ppermute | solution.py:36
